TPU v7x, 32 devices: a whole 2x2x4 slice. The times are simulated.
32 devices in a mesh: tm: 8 (over y, x, core), rows: 4 (over z).
Axes of the slice: x: 2, y: 2, z: 4, core: 2. Of those that a mesh axis runs over, the one named last changes fastest.
Arguments:
- latents: bfloat16 [16, 16, 64, 512], P('tm', 'rows'), may hold values from -128 to 128
- conv_weight: bfloat16 [27, 512, 512], P(None, 'tm'), may hold values from -0.0546875 to 0.0546875
- query_weight: bfloat16 [512, 512], replicated, may hold values from -1 to 4
- key_weight: bfloat16 [512, 512], replicated, may hold values from -1 to 4
- value_weight: bfloat16 [512, 512], replicated, may hold values from -0.25 to 0.25
- out_weight: bfloat16 [512, 512], replicated, may hold values from -1.5 to 1.5
Outputs:
- output: bfloat16 [16, 16, 64, 512], P('tm', 'rows')
All inputs are finite; a program needn't handle non-finite values.
Results may differ from a plain program's by a relative error of at most 0.028.
Values may be sent and summed in bfloat16 or wider, within the bound.
No kernel may reach another device: no remote copies, remote signals or barrier semaphores. Data moves between devices by JAX's collectives and lax.ppermute only.
A program may use at most 128 MiB of HBM per device.

v0:
```python
import jax
import jax.numpy as jnp
from jax import lax
from jax.sharding import PartitionSpec as P

G = 32


epsilon = 1e-06


def with_halo(block, sides, width):
    for axis, dim in sides:
        count = lax.axis_size(axis)
        forward = [(i, i + 1) for i in range(count - 1)]
        backward = [(target, source) for source, target in forward]
        low = lax.ppermute(
            lax.slice_in_dim(block, block.shape[dim] - width, None, axis=dim), axis, forward
        )
        high = lax.ppermute(lax.slice_in_dim(block, 0, width, axis=dim), axis, backward)
        block = jnp.concatenate([low, block, high], axis=dim)
    return block


def from_behind(shard, axis, by):
    devices = lax.axis_size(axis)
    pairs = [(i, i + by) for i in range(devices) if 0 <= i + by < devices]
    return lax.ppermute(shard, axis, pairs)


def body(latents, conv_weight, query_weight, key_weight, value_weight, out_weight):
    frames, rows_here, columns, chans = latents.shape
    framed = with_halo(latents, (("rows", 1),), 1)
    earlier = from_behind(framed, "tm", 1)
    window = jnp.concatenate([earlier, framed], axis=0)
    window = jnp.pad(window, ((0, 0), (0, 0), (1, 1), (0, 0)))
    tokens_here = frames * rows_here * columns
    initial = jnp.zeros((tokens_here, chans), jnp.float32)
    totals = initial
    kernel_piece = lax.all_gather(conv_weight, "tm", axis=1, tiled=True)
    channels_in = kernel_piece.shape[1]
    for tap_index in range(27):
        frame_lag = tap_index // 9
        row_lag = tap_index // 3 % 3
        col_lag = tap_index % 3
        patches = window[
            frame_lag : frame_lag + frames,
            row_lag : row_lag + rows_here,
            col_lag : col_lag + columns,
            :,
        ]
        patches = patches.reshape(tokens_here, channels_in)
        totals = totals + jnp.dot(
            patches, kernel_piece[tap_index], preferred_element_type=jnp.float32
        )
    convolved = totals.astype(jnp.bfloat16)
    per_frame = rows_here * columns
    entries = rows_here * lax.axis_size("rows") * columns * (chans // G)
    grouped = convolved.astype(jnp.float32).reshape(frames, per_frame, G, chans // G)
    group_total, squares = lax.psum(
        (jnp.sum(grouped, axis=(1, 3)), jnp.sum(grouped * grouped, axis=(1, 3))), "rows"
    )
    average = group_total / entries
    variance = squares / entries - average * average
    centered = grouped - average[:, None, :, None]
    normed = (
        (centered * lax.rsqrt(variance + epsilon)[:, None, :, None])
        .reshape(tokens_here, chans)
        .astype(jnp.bfloat16)
    )
    queries = (
        jnp.dot(normed, query_weight, preferred_element_type=jnp.float32)
        .astype(jnp.bfloat16)
        .reshape(frames, per_frame, chans)
    )
    keys = (
        jnp.dot(normed, key_weight, preferred_element_type=jnp.float32)
        .astype(jnp.bfloat16)
        .reshape(frames, per_frame, chans)
    )
    values = (
        jnp.dot(normed, value_weight, preferred_element_type=jnp.float32)
        .astype(jnp.bfloat16)
        .reshape(frames, per_frame, chans)
    )
    score_scale = chans ** (-0.5)
    all_keys, all_values = (
        lax.all_gather(keys, "rows", axis=1, tiled=True),
        lax.all_gather(values, "rows", axis=1, tiled=True),
    )
    scores = (
        jnp.einsum("fqc,fkc->fqk", queries, all_keys, preferred_element_type=jnp.float32)
        * score_scale
    )
    row_max = jnp.max(scores, axis=2)
    exp_weights = jnp.exp(scores - row_max[:, :, None]).astype(jnp.bfloat16)
    denominator = jnp.sum(exp_weights.astype(jnp.float32), axis=2)
    numerator = jnp.einsum(
        "fqk,fkc->fqc", exp_weights, all_values, preferred_element_type=jnp.float32
    )
    attended = (
        (numerator / denominator[:, :, None]).astype(jnp.bfloat16).reshape(tokens_here, chans)
    )
    summed = convolved.astype(jnp.float32) + jnp.dot(
        attended, out_weight, preferred_element_type=jnp.float32
    )
    return summed.astype(jnp.bfloat16).reshape(frames, rows_here, columns, chans)


def solution(mesh):
    placed = (P("tm", "rows", None, None), P(None, "tm", None), P(), P(), P(), P())
    return jax.shard_map(
        body, mesh=mesh, in_specs=placed, out_specs=P("tm", "rows", None, None), check_vma=False
    )
```

profile of v0, /device:TPU:1, one launch (start us, length us, event | category | flops | bytes accessed | tf_op | source)
XLA Modules:
  0.0 257.3 jit_solution(7563346825033139236)
XLA Ops:
  6.5 0.7 all-gather.4.cloned.1.call-update
  7.3 1.0 fusion.25
  8.3 4.0 %collective-permute-start = (bf16[2,1,64,512]{3,2,1,0:T(8,128)(2,1)S(1)}, bf16[2,1,64,512]{3,2,1,0:T(8,128)(2,1)S(1)}, u32[]{:S(2)}, u32[]{:S(2)}) collective-permute-start(bf16[2,1,64,512]{3,2,1,0:T(8,128)(2,1)S(1)} %get-tuple-element.37), channel_id=1, source_target_pairs={{0,1},{1,2},{2,3},{4,5},{5,6},{6,7},{8,9},{9,10},{10,11},{12,13},{... | collective-permute-start | bytes 393224 | tf_op jit(solution)/shard_map/ppermute | solution.py:17
  12.3 1.3 collective-permute-start.1
  13.6 0.8 collective-permute-done
  14.5 3.6 %collective-permute-done.1 = bf16[2,1,64,512]{3,2,1,0:T(8,128)(2,1)S(1)} collective-permute-done((bf16[2,1,64,512]{3,2,1,0:T(8,128)(2,1)S(1)}, bf16[2,1,64,512]{3,2,1,0:T(8,128)(2,1)S(1)}, u32[]{:S(2)}, u32[]{:S(2)}) %collective-permute-start.1) | collective-permute-done | bytes 131104 | tf_op jit(solution)/shard_map/ppermute | solution.py:20
  18.1 1.1 pad_maximum_fusion.1
  19.2 5.1 %collective-permute-start.2 = (bf16[2,6,64,512]{3,2,1,0:T(8,128)(2,1)S(1)}, bf16[2,6,64,512]{3,2,1,0:T(8,128)(2,1)S(1)}, u32[]{:S(2)}, u32[]{:S(2)}) collective-permute-start(bf16[2,6,64,512]{3,2,1,0:T(8,128)(2,1)S(1)} %constant_dynamic-update-slice_fusion), channel_id=1, source_target_pairs={{0,4},{4,8},{8,12},{12,16},{16,20},{20,24},{24,28},{1,5},{5,9},{9,... | collective-permute-start | bytes 2359304 | tf_op jit(solution)/shard_map/ppermute | solution.py:28
  24.3 23.9 %collective-permute-done.2 = bf16[2,6,64,512]{3,2,1,0:T(8,128)(2,1)S(1)} collective-permute-done((bf16[2,6,64,512]{3,2,1,0:T(8,128)(2,1)S(1)}, bf16[2,6,64,512]{3,2,1,0:T(8,128)(2,1)S(1)}, u32[]{:S(2)}, u32[]{:S(2)}) %collective-permute-start.2) | collective-permute-done | bytes 786464 | tf_op jit(solution)/shard_map/ppermute | solution.py:28
  48.4 2.4 pad_slice_fusion.8
  50.7 2.8 %pad_slice_fusion.7 = (bf16[2,4,64,512]{3,2,1,0:T(8,128)(2,1)S(1)}, bf16[2,4,64,512]{3,2,1,0:T(8,128)(2,1)}, bf16[2,4,64,512]{3,2,1,0:T(8,128)(2,1)}, bf16[2,4,6...) fusion(bf16[4,6,64,512]{3,2,1,0:T(8,128)(2,1)S(1)} %pad_maximum, ...), kind=kLoop, calls=%fused_computation.94 | loop fusion | bytes 6291456 | tf_op jit(solution)/shard_map/slice | solution.py:46
  53.5 1.8 fusion.13
  55.3 43.3 %all-gather.4.cloned.1.call-done = bf16[27,512,512]{2,1,0:T(8,128)(2,1)} async-done(((bf16[27,64,512]{2,1,0:T(8,128)(2,1)}), bf16[27,512,512]{2,1,0:T(8,128)(2,1)}) %all-gather.4.cloned.1.call-update) | async-done | bytes 14155792 | tf_op jit(solution)/shard_map/all_gather | solution.py:40
  98.5 1.8 fusion.22
  100.3 2.0 fusion.21
  102.3 2.2 fusion.20
  104.5 1.6 fusion.19
  106.2 1.6 fusion.18
  107.8 1.7 fusion.17
  109.5 1.7 fusion.16
  111.2 0.4 fusion.15
  111.7 0.4 fusion.14
  112.3 0.4 convolution_add_fusion.18
  112.7 0.6 copy-done.10
  113.3 0.4 convolution_add_fusion.17
  113.8 0.4 fusion.6
  114.2 0.6 copy-done.7
  114.8 0.4 convolution_add_fusion.15
  115.3 0.4 fusion.5
  115.8 0.6 copy-done.6
  116.4 0.4 convolution_add_fusion.13
  116.8 0.4 fusion.4
  117.3 0.6 copy-done.5
  118.4 0.4 fusion.3
  118.8 0.6 copy-done.4
  119.9 0.4 fusion.2
  120.3 0.4 convolution_add_fusion.7
  120.8 0.6 copy-done.18
  121.4 0.4 fusion.1
  121.8 0.4 convolution_add_fusion.5
  122.3 0.4 convolution_add_fusion.4
  122.7 0.4 convolution_add_fusion.3
  123.2 0.4 convolution_add_fusion.2
  123.6 0.6 copy-done.17
  124.2 0.4 fusion.8
  124.6 1.3 copy.7
  126.0 1.9 reshape.133
  127.9 0.8 fusion.24
  128.7 15.2 %all-reduce.1 = (f32[2,32]{0,1:T(8,128)S(1)}, f32[2,32]{0,1:T(8,128)S(1)}) all-reduce(f32[2,32]{0,1:T(8,128)S(1)} %get-tuple-element.6, f32[2,32]{0,1:T(8,128)S(1)} %get-tuple-element.5), channel_id=1, replica_groups=mesh['tm'=8,'rows'=4] {'rows'}, use_global_device_ids=true, to_apply=%region_3.4 | all-reduce | flops 128 | bytes 1024 | tf_op jit(solution)/shard_map/psum | solution.py:60
  144.3 1.1 copy.10
  145.3 1.6 copy.8
  147.2 1.1 copy.11
  148.3 2.5 copy.9
  150.8 1.5 multiply_convert_fusion
  152.4 1.3 convolution_convert_fusion.1
  153.7 1.2 convolution_convert_fusion
  155.0 0.4 convolution_convert_fusion.2
  155.4 44.9 %all-gather.6.cloned.1.call-done = bf16[2,1024,512]{2,1,0:T(8,128)(2,1)} async-done(((bf16[2,256,512]{2,1,0:T(8,128)(2,1)}), bf16[2,1024,512]{2,1,0:T(8,128)(2,1)}) %all-gather.6.cloned.1.call-update) | async-done | bytes 2097168 | tf_op jit(solution)/shard_map/all_gather | solution.py:88
  200.3 2.4 multiply_reduce_fusion
  202.7 1.3 copy-done.2
  204.0 0.5 convert_reduce_fusion
  204.5 42.0 %all-gather.8.cloned.1.call-done = bf16[2,1024,512]{2,1,0:T(8,128)(2,1)} async-done(((bf16[2,256,512]{2,1,0:T(8,128)(2,1)}), bf16[2,1024,512]{2,1,0:T(8,128)(2,1)}) %all-gather.8.cloned.1.call-update) | async-done | bytes 2097168 | tf_op jit(solution)/shard_map/all_gather | solution.py:89
  246.6 3.0 %fusion.9 = bf16[2,256,512]{2,1,0:T(8,128)(2,1)S(1)} fusion(bf16[2,1024,512]{2,1,0:T(8,128)(2,1)} %all-gather.8.cloned.1.call-done, f32[2,256]{1,0:T(2,128)S(1)} %convert_reduce_fusion, f32[2,256,1024]{2,1,0:T(8,128)} %copy-done.2, f32[2,256]{1,0:T(2,128)S(1)} %get-tuple-element.40), kind=kOutput, calls=%fused_computation.42 | convolution fusion | flops 538968064 | bytes 4722688 | tf_op jit(solution)/shard_map/fqk,fkc->fqc/dot_general | solution.py:98
  249.6 1.2 fusion.10
  (49 shorter events, 2.2 us)
Async XLA Ops:
  6.5 145.8 %copy-start = (bf16[512,512]{1,0:T(8,128)(2,1)S(1)}, bf16[512,512]{1,0:T(8,128)(2,1)}, u32[]{:S(2)}) copy-start(bf16[512,512]{1,0:T(8,128)(2,1)} %param.9) | copy-start | bytes 1572868
  6.5 11.5 %copy-start.3 = (bf16[2,4,64,512]{3,2,1,0:T(8,128)(2,1)S(1)}, bf16[2,4,64,512]{3,2,1,0:T(8,128)(2,1)}, u32[]{:S(2)}) copy-start(bf16[2,4,64,512]{3,2,1,0:T(8,128)(2,1)} %param.6) | copy-start | bytes 1572868
  6.5 92.0 %all-gather.4.cloned.1.call-start = ((), (), s32[]{:S(2)}) async-start(), calls=%async_computation | async-start | bytes 15925248 | tf_op jit(solution)/shard_map/all_gather | solution.py:40
  7.3 193.0 %all-gather.6.cloned.1.call-start = ((), (), s32[]{:S(2)}) async-start(), calls=%async_computation.1 | async-start | bytes 2621440 | tf_op jit(solution)/shard_map/all_gather | solution.py:88
  8.3 6.2 %collective-permute-start = (bf16[2,1,64,512]{3,2,1,0:T(8,128)(2,1)S(1)}, bf16[2,1,64,512]{3,2,1,0:T(8,128)(2,1)S(1)}, u32[]{:S(2)}, u32[]{:S(2)}) collective-permute-start(bf16[2,1,64,512]{3,2,1,0:T(8,128)(2,1)S(1)} %get-tuple-element.37), channel_id=1, source_target_pairs={{0,1},{1,2},{2,3},{4,5},{5,6},{6,7},{8,9},{9,10},{10,11},{12,13},{... | collective-permute-start | bytes 393224 | tf_op jit(solution)/shard_map/ppermute | solution.py:17
  12.3 5.7 %collective-permute-start.1 = (bf16[2,1,64,512]{3,2,1,0:T(8,128)(2,1)S(1)}, bf16[2,1,64,512]{3,2,1,0:T(8,128)(2,1)S(1)}, u32[]{:S(2)}, u32[]{:S(2)}) collective-permute-start(bf16[2,1,64,512]{3,2,1,0:T(8,128)(2,1)S(1)} %get-tuple-element.36), channel_id=1, source_target_pairs={{1,0},{2,1},{3,2},{5,4},{6,5},{7,6},{9,8},{10,9},{11,10},{13,12},{... | collective-permute-start | bytes 393224 | tf_op jit(solution)/shard_map/ppermute | solution.py:20
  19.2 29.0 %collective-permute-start.2 = (bf16[2,6,64,512]{3,2,1,0:T(8,128)(2,1)S(1)}, bf16[2,6,64,512]{3,2,1,0:T(8,128)(2,1)S(1)}, u32[]{:S(2)}, u32[]{:S(2)}) collective-permute-start(bf16[2,6,64,512]{3,2,1,0:T(8,128)(2,1)S(1)} %constant_dynamic-update-slice_fusion), channel_id=1, source_target_pairs={{0,4},{4,8},{8,12},{12,16},{16,20},{20,24},{24,28},{1,5},{5,9},{9,... | collective-permute-start | bytes 2359304 | tf_op jit(solution)/shard_map/ppermute | solution.py:28
  98.5 12.7 %copy-start.1 = (bf16[27,512,512]{2,1,0:T(8,128)(2,1)S(1)}, bf16[27,512,512]{2,1,0:T(8,128)(2,1)}, u32[]{:S(2)}) copy-start(bf16[27,512,512]{2,1,0:T(8,128)(2,1)} %all-gather.4.cloned.1.call-done) | copy-start | bytes 42467332
  107.8 3.4 %copy-start.9 = (bf16[2,4,64,512]{3,2,1,0:T(8,128)(2,1)S(1)}, bf16[2,4,64,512]{3,2,1,0:T(8,128)(2,1)}, u32[]{:S(2)}) copy-start(bf16[2,4,64,512]{3,2,1,0:T(8,128)(2,1)} %get-tuple-element.23) | copy-start | bytes 1572868
  109.5 2.2 copy-start.8
  111.2 1.0 copy-start.15
  112.3 1.0 copy-start.10
  112.7 1.1 copy-start.16
  113.8 1.0 copy-start.7
  114.2 1.1 copy-start.14
  115.3 1.0 copy-start.6
  115.8 1.1 copy-start.13
  116.8 1.0 copy-start.5
  117.3 1.1 copy-start.12
  118.4 1.0 copy-start.4
  118.8 1.1 copy-start.11
  120.3 1.0 copy-start.18
  123.1 1.0 copy-start.17
  152.4 1.4 copy-start.19
  152.4 2.6 %copy-start.20 = (bf16[512,512]{1,0:T(8,128)(2,1)S(1)}, bf16[512,512]{1,0:T(8,128)(2,1)}, u32[]{:S(2)}) copy-start(bf16[512,512]{1,0:T(8,128)(2,1)} %param.8) | copy-start | bytes 1572868
  153.7 92.9 %all-gather.8.cloned.1.call-start = ((), (), s32[]{:S(2)}) async-start(), calls=%async_computation.2 | async-start | bytes 2621440 | tf_op jit(solution)/shard_map/all_gather | solution.py:89
  202.7 1.3 copy-start.2
  204.5 45.1 %copy-start.21 = (bf16[512,512]{1,0:T(8,128)(2,1)S(1)}, bf16[512,512]{1,0:T(8,128)(2,1)}, u32[]{:S(2)}) copy-start(bf16[512,512]{1,0:T(8,128)(2,1)} %param.11) | copy-start | bytes 1572868
Sparse Core Ops, SparseCore 0:
  9.3 89.2 all-gather.3
  153.8 46.4 all-gather.5
  201.9 44.6 all-gather.7
where the time goes:
time: 259 us; the launch traced here: 257 us
  waiting for transfers between devices  159 us (61%)
  matrix products  30.9 us (12%)
  local copies, waits for them, and re-layouts  22.1 us (9%)
  blocking collectives  15.2 us (6%)
  between operations  13.6 us (5%)
  starting transfers between devices  10.5 us (4%)
  other arithmetic  5.82 us (2%)
    all_gather x1, waiting for transfers between devices, body(): lax.all_gather(keys, 'rows', axis=1, tiled=True)  44.9 us
    all_gather x1, waiting for transfers between devices, body(): kernel_piece = lax.all_gather(conv_weight, 'tm', axis=1, tiled=True)  43.3 us
    all_gather x1, waiting for transfers between devices, body(): lax.all_gather(values, 'rows', axis=1, tiled=True)  42 us
    ppermute x1, waiting for transfers between devices, from_behind(): return lax.ppermute(shard, axis, pairs)  23.9 us
    dot_general x27, matrix products, body(): jnp.dot(patches, kernel_piece[tap_index], preferred_element_type=jnp.floa...  21.3 us
    psum x1, blocking collectives, body(): lax.psum((jnp.sum(grouped, axis=(1, 3)), jnp.sum(grouped * grouped, axis=...  15.2 us
    unnamed x47, local copies, waits for them, and re-layouts  8.02 us
  transfers between devices with their start and end apart: 6, of which 6 were waited for; matrix products, arithmetic and copies ran while one was open for 5% of the time, Pallas kernels for 0%

commit v1 on v0

v1 whole, which is shorter than its diff:
```python
import jax
import jax.numpy as jnp
from jax import lax
from jax.sharding import PartitionSpec as P

G = 32
LANES = 128
CORES = 2

epsilon = 1e-06

BOTH = ("tm", "rows")


def everywhere(sizes, target):
    devices, depth = sizes
    pairs = []
    for t in range(devices):
        for z in range(depth):
            to = target(t, z)
            if to is not None:
                pairs.append((t * depth + z, to[0] * depth + to[1]))
    return pairs


def body(latents, conv_weight, query_weight, key_weight, value_weight, out_weight):
    frames, rows_here, columns, chans = latents.shape
    taps, chans_here, _ = conv_weight.shape
    devices, depth = lax.axis_size("tm"), lax.axis_size("rows")
    sizes = (devices, depth)
    group = LANES // chans_here
    parts = devices // group
    width = group * chans_here
    t_index, z_index = lax.axis_index("tm"), lax.axis_index("rows")
    part, member = t_index // group, t_index % group

    def permute(block, target):
        return lax.ppermute(block, BOTH, everywhere(sizes, target))

    kernel_parts = [conv_weight]
    for step in range(1, group):
        kernel_parts.append(
            permute(
                conv_weight, lambda t, z: (t // group * group + (t + step) % group, z)
            )
        )
    order = (member - jnp.arange(group)) % group
    kernel = jnp.take(jnp.stack(kernel_parts), order, axis=0)
    kernel = jnp.moveaxis(kernel, 0, 1).reshape(taps, width, chans)

    above = permute(latents[:, -1:], lambda t, z: (t, z + 1) if z + 1 < depth else None)
    below = permute(latents[:, :1], lambda t, z: (t, z - 1) if z else None)
    framed = jnp.concatenate([above, latents, below], axis=1)

    held = []
    for s in range(parts):
        piece = lax.dynamic_slice_in_dim(framed, (part ^ s) * width, width, axis=3)
        if s:
            piece = permute(piece, lambda t, z: ((t // group ^ s) * group + t % group, z))
        held.append(piece)
    held = jnp.stack(held)

    earlier = permute(held, lambda t, z: (t // group * group + (t + 1) % group, z))
    place = jnp.arange(parts)
    wrapped = jnp.take(earlier, part ^ jnp.maximum((part ^ place) - 1, 0), axis=0)
    wrapped = jnp.where(((part ^ place) == 0)[:, None, None, None, None], 0, wrapped)
    earlier = jnp.where(member == 0, wrapped, earlier)

    window = jnp.concatenate([earlier, held], axis=1)
    side = round(taps ** (1 / 3))
    partial = lax.conv_general_dilated(
        window,
        kernel.reshape(side, side, side, width, chans),
        (1, 1, 1),
        ((0, 0), (0, 0), (1, 1)),
        dimension_numbers=("NDHWC", "DHWIO", "NDHWC"),
        preferred_element_type=jnp.float32,
    ).astype(jnp.bfloat16)
    total = partial[0].astype(jnp.float32)
    for s in range(1, parts):
        total = total + permute(
            partial[s], lambda t, z: ((t // group ^ s) * group + t % group, z)
        ).astype(jnp.float32)
    convolved = total.astype(jnp.bfloat16)

    share = depth // frames
    per_block = rows_here * columns

    def frame_home(t, z, p):
        frame = t % CORES * frames + (z + p) % frames
        m = z // frames
        slot = frame * share + m
        return (t // CORES * CORES + slot % CORES, slot // CORES)

    blocks = []
    for p in range(frames):
        mine = lax.dynamic_index_in_dim(convolved, (z_index + p) % frames, 0, keepdims=False)
        blocks.append(permute(mine, lambda t, z: frame_home(t, z, p)))
    own = jnp.stack(blocks).reshape(frames * per_block, chans)

    def next_in_frame(t, z, step):
        slot = z * CORES + t % CORES
        slot = slot // share * share + (slot + step) % share
        return (t // CORES * CORES + slot % CORES, slot // CORES)

    whole = [own]
    for step in range(1, share):
        whole.append(permute(own, lambda t, z: next_in_frame(t, z, step)))
    whole = jnp.concatenate(whole)
    tokens = whole.shape[0]

    per_group = chans // G
    spread = (jnp.arange(chans)[:, None] // per_group == jnp.arange(G)[None, :]).astype(jnp.float32)
    wide = whole.astype(jnp.float32)
    entries = tokens * per_group
    average = jnp.dot(jnp.sum(wide, axis=0), spread, precision="highest") / entries
    average = jnp.dot(average, spread.T, precision="highest")
    centered = wide - average
    variance = jnp.dot(jnp.sum(centered * centered, axis=0), spread, precision="highest") / entries
    scale = jnp.dot(lax.rsqrt(variance + epsilon), spread.T, precision="highest")
    normed = (centered * scale).astype(jnp.bfloat16)

    def project(x, w):
        return jnp.dot(x, w, preferred_element_type=jnp.float32).astype(jnp.bfloat16)

    queries = project(normed[: frames * per_block], query_weight)
    keys = project(normed, key_weight)
    values = project(normed, value_weight)
    scores = jnp.dot(queries, keys.T, preferred_element_type=jnp.float32) * chans ** (-0.5)
    row_max = jnp.max(scores, axis=1, keepdims=True)
    exp_weights = jnp.exp(scores - row_max).astype(jnp.bfloat16)
    denominator = jnp.sum(exp_weights.astype(jnp.float32), axis=1, keepdims=True)
    numerator = jnp.dot(exp_weights, values, preferred_element_type=jnp.float32)
    attended = (numerator / denominator).astype(jnp.bfloat16)
    summed = own.astype(jnp.float32) + jnp.dot(
        attended, out_weight, preferred_element_type=jnp.float32
    )
    summed = summed.astype(jnp.bfloat16).reshape(frames, rows_here, columns, chans)

    back = []
    for p in range(frames):
        pairs = [(b, a) for a, b in everywhere(sizes, lambda t, z: frame_home(t, z, p))]
        back.append(lax.ppermute(summed[p], BOTH, pairs))
    return jnp.take(jnp.stack(back), (jnp.arange(frames) - z_index) % frames, axis=0)


def solution(mesh):
    placed = (P("tm", "rows", None, None), P(None, "tm", None), P(), P(), P(), P())
    return jax.shard_map(
        body, mesh=mesh, in_specs=placed, out_specs=P("tm", "rows", None, None), check_vma=False
    )
```

time: 259 us -> 129 us (0.50)
  waiting for transfers between devices: 159 us -> 56 us
  blocking collectives: 15.2 us -> 0 us
  starting transfers between devices: 10.5 us -> 25.1 us
  between operations: 13.6 us -> 0.36 us
  matrix products: 30.9 us -> 18.7 us
  other arithmetic: 5.82 us -> 12.3 us
  local copies, waits for them, and re-layouts: 22.1 us -> 16.5 us
    all_gather x3 -> x0, waiting for transfers between devices: 130 us -> none  [the longest x1 44.9 us: body(): lax.all_gather(keys, 'rows', axis=1, tiled=True)]
    ppermute x3 -> x15, waiting for transfers between devices: 28.3 us -> 56 us  [the longest x13 46.1 us: permute(): return lax.ppermute(block, BOTH, everywhere(sizes, target))]
    dot_general x32 -> x7, matrix products: 29.6 us -> 6.5 us  [the longest x2 2.92 us: project(): jnp.dot(x, w, preferred_element_type=jnp.float32).astype(jnp.bfloat16)]
    psum x1 -> x0, blocking collectives: 15.2 us -> none  [body(): lax.psum((jnp.sum(grouped, axis=(1, 3)), jnp.sum(grouped * grouped, axis=...]
    ppermute x3 -> x15, starting transfers between devices: 10.4 us -> 25.1 us  [the longest x13 20.5 us: permute(): return lax.ppermute(block, BOTH, everywhere(sizes, target))]
    conv_general_dilated x0 -> x1, matrix products: none -> 8.99 us  [body(): lax.conv_general_dilated(window, kernel.reshape(side, side, side, width,...]
    gather x0 -> x3, local copies, waits for them, and re-layouts: none -> 5.85 us  [the longest x1 4.57 us: body(): kernel = jnp.take(jnp.stack(kernel_parts), order, axis=0)]
    unnamed x47 -> x13, local copies, waits for them, and re-layouts: 8.02 us -> 2.81 us
  transfers between devices with their start and end apart: 6 -> 15, of which waited for: 6 -> 11; matrix products, arithmetic and copies ran while one was open for 5% -> 5% of each run, Pallas kernels for 0% -> 0%
where the time goes in v1:
time: 129 us
  waiting for transfers between devices  56 us (43%)
  starting transfers between devices  25.1 us (19%)
  matrix products  18.7 us (14%)
  local copies, waits for them, and re-layouts  16.5 us (13%)
  other arithmetic  12.3 us (10%)
    ppermute x13, waiting for transfers between devices, permute(): return lax.ppermute(block, BOTH, everywhere(sizes, target))  46.1 us
    ppermute x13, starting transfers between devices, permute(): return lax.ppermute(block, BOTH, everywhere(sizes, target))  20.5 us
    ppermute x2, waiting for transfers between devices, body(): back.append(lax.ppermute(summed[p], BOTH, pairs))  9.96 us
    conv_general_dilated x1, matrix products, body(): lax.conv_general_dilated(window, kernel.reshape(side, side, side, width,...  8.99 us
    gather x1, local copies, waits for them, and re-layouts, body(): kernel = jnp.take(jnp.stack(kernel_parts), order, axis=0)  4.57 us
    ppermute x2, starting transfers between devices, body(): back.append(lax.ppermute(summed[p], BOTH, pairs))  4.55 us
    another operation x1, other arithmetic, body(): kernel = jnp.take(jnp.stack(kernel_parts), order, axis=0)  4.08 us
    dot_general x1, matrix products, body(): jnp.dot(attended, out_weight, preferred_element_type=jnp.float32)  3.19 us
  transfers between devices with their start and end apart: 15, of which 11 were waited for; matrix products, arithmetic and copies ran while one was open for 5% of the time, Pallas kernels for 0%

profile of v1, /device:TPU:1, one launch (start us, length us, event | category | flops | bytes accessed | tf_op | source)
XLA Modules:
  0.0 128.9 jit_solution(13495385107638832992)
XLA Ops:
  0.0 1.0 fusion.43
  1.1 4.0 %collective-permute-start = (bf16[2,1,64,512]{3,2,1,0:T(8,128)(2,1)S(1)}, bf16[2,1,64,512]{3,2,1,0:T(8,128)(2,1)S(1)}, u32[]{:S(2)}, u32[]{:S(2)}) collective-permute-start(bf16[2,1,64,512]{3,2,1,0:T(8,128)(2,1)S(1)} %get-tuple-element.17), channel_id=1, source_target_pairs={{0,1},{1,2},{2,3},{4,5},{5,6},{6,7},{8,9},{9,10},{10,11},{12,13},{... | collective-permute-start | bytes 393224 | tf_op jit(solution)/shard_map/ppermute | solution.py:38
  5.1 1.3 %collective-permute-start.1 = (bf16[2,1,64,512]{3,2,1,0:T(8,128)(2,1)S(1)}, bf16[2,1,64,512]{3,2,1,0:T(8,128)(2,1)S(1)}, u32[]{:S(2)}, u32[]{:S(2)}) collective-permute-start(bf16[2,1,64,512]{3,2,1,0:T(8,128)(2,1)S(1)} %get-tuple-element.16), channel_id=1, source_target_pairs={{1,0},{2,1},{3,2},{5,4},{6,5},{7,6},{9,8},{10,9},{11,10},{13,12},{... | collective-permute-start | bytes 393224 | tf_op jit(solution)/shard_map/ppermute | solution.py:38
  6.4 0.8 collective-permute-done
  7.2 1.1 constant_dynamic-update-slice_fusion.1
  8.3 2.5 %collective-permute-done.1 = bf16[2,1,64,512]{3,2,1,0:T(8,128)(2,1)S(1)} collective-permute-done((bf16[2,1,64,512]{3,2,1,0:T(8,128)(2,1)S(1)}, bf16[2,1,64,512]{3,2,1,0:T(8,128)(2,1)S(1)}, u32[]{:S(2)}, u32[]{:S(2)}) %collective-permute-start.1) | collective-permute-done | bytes 131104 | tf_op jit(solution)/shard_map/ppermute | solution.py:38
  10.8 0.2 dynamic-slice_bitcast_fusion
  11.0 2.2 %collective-permute-start.4 = (bf16[2,6,64,128]{3,2,1,0:T(8,128)(2,1)S(1)}, bf16[2,6,64,128]{3,2,1,0:T(8,128)(2,1)S(1)}, u32[]{:S(2)}, u32[]{:S(2)}) collective-permute-start(bf16[2,6,64,128]{3,2,1,0:T(8,128)(2,1)S(1)} %get-tuple-element.9), channel_id=1, source_target_pairs={{0,24},{1,25},{2,26},{3,27},{4,28},{5,29},{6,30},{7,31},{8,16},{9,... | collective-permute-start | bytes 589832 | tf_op jit(solution)/shard_map/ppermute | solution.py:38
  13.2 0.2 collective-permute-start.3
  13.4 0.3 collective-permute-start.2
  13.7 2.9 %collective-permute-start.6 = (bf16[27,64,512]{2,1,0:T(8,128)(2,1)}, bf16[27,64,512]{2,1,0:T(8,128)(2,1)}, u32[]{:S(2)}, u32[]{:S(2)}) collective-permute-start(bf16[27,64,512]{2,1,0:T(8,128)(2,1)} %param.7), channel_id=1, source_target_pairs={{0,4},{1,5},{2,6},{3,7},{4,0},{5,1},{6,2},{7,3},{8,12},{9,13},{10,... | collective-permute-start | bytes 5308424 | tf_op jit(solution)/shard_map/ppermute | solution.py:38
  16.6 5.1 %collective-permute-done.3 = bf16[2,6,64,128]{3,2,1,0:T(8,128)(2,1)S(1)} collective-permute-done((bf16[2,6,64,128]{3,2,1,0:T(8,128)(2,1)S(1)}, bf16[2,6,64,128]{3,2,1,0:T(8,128)(2,1)S(1)}, u32[]{:S(2)}, u32[]{:S(2)}) %collective-permute-start.3) | collective-permute-done | bytes 196640 | tf_op jit(solution)/shard_map/ppermute | solution.py:38
  21.8 0.1 pad_maximum_fusion.2
  21.9 1.9 %collective-permute-start.5 = (bf16[4,2,6,64,128]{4,3,2,1,0:T(8,128)(2,1)S(1)}, bf16[4,2,6,64,128]{4,3,2,1,0:T(8,128)(2,1)S(1)}, u32[]{:S(2)}, u32[]{:S(2)}) collective-permute-start(bf16[4,2,6,64,128]{4,3,2,1,0:T(8,128)(2,1)S(1)} %pad_maximum_fusion.2), channel_id=1, source_target_pairs={{0,4},{1,5},{2,6},{3,7},{4,0},{5,1},{6,2},{7,3},{8,12},{9,13},{10,... | collective-permute-start | bytes 2359304 | tf_op jit(solution)/shard_map/ppermute | solution.py:38
  23.8 1.8 %collective-permute-done.5 = bf16[4,2,6,64,128]{4,3,2,1,0:T(8,128)(2,1)S(1)} collective-permute-done((bf16[4,2,6,64,128]{4,3,2,1,0:T(8,128)(2,1)S(1)}, bf16[4,2,6,64,128]{4,3,2,1,0:T(8,128)(2,1)S(1)}, u32[]{:S(2)}, u32[]{:S(2)}) %collective-permute-start.5) | collective-permute-done | bytes 786464 | tf_op jit(solution)/shard_map/ppermute | solution.py:38
  25.7 0.7 gather_fusion
  26.4 0.2 select_select_fusion
  26.5 0.2 maximum_bitcast_fusion
  26.7 1.4 %copy.27 = bf16[4,6,4,64,128]{4,2,3,1,0:T(4,128)(2,1)S(1)} copy(bf16[4,6,4,64,128]{4,3,1,0,2:T(8,128)(2,1)S(1)} %maximum_bitcast_fusion) | data formatting | bytes 3145728
  28.2 0.7 pad.clone
  28.9 0.1 slice.46
  29.0 1.2 fusion.3
  30.2 4.1 %pad_maximum_fusion = bf16[2,27,64,512]{3,2,1,0:T(8,128)(2,1)} fusion(bf16[1,27,64,512]{3,2,1,0:T(8,128)(2,1)} %bitcast.9, bf16[1,27,64,512]{3,2,1,0:T(8,128)(2,1)} %bitcast.8), kind=kLoop, calls=%fused_computation.6 | loop fusion | flops 1769472 | bytes 7077888 | tf_op jit(solution)/shard_map/stack | solution.py:48
  34.3 4.6 %gather_fusion.1 = bf16[2,27,64,512]{3,2,1,0:T(8,128)(2,1)} fusion(bf16[2,27,64,512]{3,2,1,0:T(8,128)(2,1)} %pad_maximum_fusion, s32[1024]{0:T(1024)S(1)} %pad_clamp_fusion.1), kind=kCustom, calls=%fused_computation.1 | custom fusion | bytes 7077896 | tf_op jit(solution)/shard_map/jit(_take)/gather | solution.py:48
  38.8 2.4 %select_bitcast_fusion = bf16[27,2,64,512]{3,2,0,1:T(8,128)(2,1)S(1)} fusion(bf16[2,27,64,512]{3,2,1,0:T(8,128)(2,1)} %gather_fusion.1, pred[2]{0:T(512)(128)(4,1)S(1)} %compare_and_fusion), kind=kLoop, calls=%fused_computation.7 | loop fusion | flops 1769472 | bytes 7077890 | tf_op jit(solution)/shard_map/jit(_take)/select_n | solution.py:48
  41.3 0.4 copy.17
  41.7 0.3 copy-done.4
  41.9 9.0 %select_convert_fusion = bf16[2,4,32,9,512]{4,2,3,1,0:T(8,128)(2,1)S(1)} fusion(pred[32,9]{0,1:T(8,128)(4,1)S(1)} %copy-done.4, bf16[3,3,3,128,512]{4,3,2,1,0:T(8,128)(2,1)S(1)} %bitcast.102, bf16[4,6,4,8,11,128]{5,2,4,3,1,0:T(4,128)(2,1)S(1)} %fusion.3), kind=kOutput, calls=%fused_computation.3 | convolution fusion | flops 8156086272 | bytes 8061216 | tf_op jit(solution)/shard_map/conv_general_dilated | solution.py:71
  50.9 1.8 %copy.18 = bf16[2,4,32,9,512]{4,1,3,2,0:T(4,128)(2,1)S(1)} copy(bf16[2,4,32,9,512]{4,2,3,1,0:T(8,128)(2,1)S(1)} %select_convert_fusion) | data formatting | bytes 4718592 | tf_op jit(solution)/shard_map/convert_element_type | solution.py:78
  52.8 0.7 slice_bitcast_fusion
  53.5 1.5 %slice_bitcast_fusion.3 = (bf16[2,4,64,512]{3,1,2,0:T(4,128)(2,1)}, bf16[2,4,64,512]{3,1,2,0:T(4,128)(2,1)}, bf16[2,4,64,512]{3,1,2,0:T(4,128)(2,1)}) fusion(bf16[4,2,4,64,512]{4,2,3,0,1:T(4,128)(2,1)S(1)} %slice_bitcast_fusion), kind=kLoop, calls=%fused_computation.49 | loop fusion | bytes 3145728 | tf_op jit(solution)/shard_map/squeeze | solution.py:82
  55.0 1.4 %collective-permute-start.9 = (bf16[2,4,64,512]{3,1,2,0:T(4,128)(2,1)}, bf16[2,4,64,512]{3,1,2,0:T(4,128)(2,1)S(1)}, u32[]{:S(2)}, u32[]{:S(2)}) collective-permute-start(bf16[2,4,64,512]{3,1,2,0:T(4,128)(2,1)} %get-tuple-element.6), channel_id=1, source_target_pairs={{0,24},{1,25},{2,26},{3,27},{4,28},{5,29},{6,30},{7,31},{8,16},{9,... | collective-permute-start | bytes 1572872 | tf_op jit(solution)/shard_map/ppermute | solution.py:38
  56.4 1.0 collective-permute-start.8
  57.4 0.2 collective-permute-start.7
  57.6 11.6 %collective-permute-done.9 = bf16[2,4,64,512]{3,1,2,0:T(4,128)(2,1)S(1)} collective-permute-done((bf16[2,4,64,512]{3,1,2,0:T(4,128)(2,1)}, bf16[2,4,64,512]{3,1,2,0:T(4,128)(2,1)S(1)}, u32[]{:S(2)}, u32[]{:S(2)}) %collective-permute-start.9) | collective-permute-done | bytes 524320 | tf_op jit(solution)/shard_map/ppermute | solution.py:38
  69.3 12.0 %collective-permute-done.8 = bf16[2,4,64,512]{3,1,2,0:T(4,128)(2,1)} collective-permute-done((bf16[2,4,64,512]{3,1,2,0:T(4,128)(2,1)}, bf16[2,4,64,512]{3,1,2,0:T(4,128)(2,1)}, u32[]{:S(2)}, u32[]{:S(2)}) %collective-permute-start.8) | collective-permute-done | bytes 524320 | tf_op jit(solution)/shard_map/ppermute | solution.py:38
  81.3 1.7 %fusion.22 = bf16[2,4,64,512]{3,1,2,0:T(4,128)(2,1)S(1)} fusion(bf16[2,4,64,512]{3,1,2,0:T(4,128)(2,1)S(1)} %collective-permute-done.9, bf16[2,4,64,512]{3,1,2,0:T(4,128)(2,1)} %collective-permute-done.8, bf16[2,4,64,512]{3,1,2,0:T(4,128)(2,1)} %collective-permute-done.7, bf16[4,2,4,64,512]{4,2,3,0,1:T(4,128)(2,1)S(1)} %slice_bitcast_fusion), kind=kLoop, calls=%fused_computation.42 | loop fusion | flops 2097152 | bytes 2621440 | tf_op jit(solution)/shard_map/convert_element_type | solution.py:84
  83.0 0.2 constant_dynamic-slice_fusion.1
  83.3 2.2 %collective-permute-start.11 = (bf16[4,64,512]{2,1,0:T(8,128)(2,1)S(1)}, bf16[4,64,512]{2,1,0:T(8,128)(2,1)S(1)}, u32[]{:S(2)}, u32[]{:S(2)}) collective-permute-start(bf16[4,64,512]{2,1,0:T(8,128)(2,1)S(1)} %bitcast.109), channel_id=1, source_target_pairs={{0,1},{1,0},{2,5},{3,4},{4,3},{5,2},{6,7},{7,6},{8,9},{9,8},{10,13... | collective-permute-start | bytes 786440 | tf_op jit(solution)/shard_map/ppermute | solution.py:38
  85.6 2.7 %collective-permute-start.10 = (bf16[4,64,512]{2,1,0:T(8,128)(2,1)S(1)}, bf16[4,64,512]{2,1,0:T(8,128)(2,1)S(1)}, u32[]{:S(2)}, u32[]{:S(2)}) collective-permute-start(bf16[4,64,512]{2,1,0:T(8,128)(2,1)S(1)} %bitcast.110), channel_id=1, source_target_pairs={{0,0},{1,1},{2,4},{3,5},{4,2},{5,3},{6,6},{7,7},{8,8},{9,9},{10,12... | collective-permute-start | bytes 786440 | tf_op jit(solution)/shard_map/ppermute | solution.py:38
  88.3 5.1 %collective-permute-done.11 = bf16[4,64,512]{2,1,0:T(8,128)(2,1)S(1)} collective-permute-done((bf16[4,64,512]{2,1,0:T(8,128)(2,1)S(1)}, bf16[4,64,512]{2,1,0:T(8,128)(2,1)S(1)}, u32[]{:S(2)}, u32[]{:S(2)}) %collective-permute-start.11) | collective-permute-done | bytes 262176 | tf_op jit(solution)/shard_map/ppermute | solution.py:38
  93.4 5.2 %collective-permute-done.10 = bf16[4,64,512]{2,1,0:T(8,128)(2,1)S(1)} collective-permute-done((bf16[4,64,512]{2,1,0:T(8,128)(2,1)S(1)}, bf16[4,64,512]{2,1,0:T(8,128)(2,1)S(1)}, u32[]{:S(2)}, u32[]{:S(2)}) %collective-permute-start.10) | collective-permute-done | bytes 262176 | tf_op jit(solution)/shard_map/ppermute | solution.py:38
  98.6 0.1 pad_maximum_fusion.3
  98.6 0.1 collective-permute-start.12
  98.7 1.9 %collective-permute-done.12 = bf16[512,512]{1,0:T(8,128)(2,1)S(1)} collective-permute-done((bf16[512,512]{1,0:T(8,128)(2,1)S(1)}, bf16[512,512]{1,0:T(8,128)(2,1)S(1)}, u32[]{:S(2)}, u32[]{:S(2)}) %collective-permute-start.12) | collective-permute-done | bytes 524320 | tf_op jit(solution)/shard_map/ppermute | solution.py:38
  100.6 0.2 convert_reduce_fusion
  100.8 0.3 fusion.15
  101.1 0.1 fusion.28
  101.3 0.3 fusion.7
  101.6 0.3 fusion.19
  101.9 0.2 fusion.27
  102.1 0.3 fusion.8
  102.4 1.7 %convolution_convert_fusion = bf16[1024,512]{1,0:T(8,128)(2,1)} fusion(bf16[1024,512]{1,0:T(8,128)(2,1)S(1)} %fusion.8, bf16[512,512]{1,0:T(8,128)(2,1)S(1)} %copy-done.2), kind=kOutput, calls=%fused_computation.23 | convolution fusion | flops 537395200 | bytes 2621440 | tf_op jit(solution)/shard_map/dot_general | solution.py:124
  104.1 1.2 convolution_convert_fusion.2
  105.3 2.7 %multiply_reduce_fusion = (f32[512]{0:T(512)S(1)}, f32[512,1024]{1,0:T(8,128)S(1)}) fusion(bf16[512,512]{1,0:T(8,128)(2,1)} %convolution_convert_fusion.2, bf16[1024,512]{1,0:T(8,128)(2,1)} %copy-done.1, bf16[512,512]{1,0:T(8,128)(2,1)S(1)} %copy-done), kind=kOutput, calls=%fused_computation.21 | convolution fusion | flops 1075314176 | bytes 4196352 | tf_op jit(solution)/shard_map/dot_general | solution.py:129
  108.0 0.5 convert_reduce_fusion.1
  108.5 3.2 %add_convert_fusion = bf16[512,512]{1,0:T(8,128)(2,1)} fusion(bf16[512,512]{1,0:T(8,128)(2,1)S(1)} %bitcast.101, bf16[512,512]{1,0:T(8,128)(2,1)} %param.11, bf16[1024,512]{1,0:T(8,128)(2,1)} %convolution_convert_fusion, f32[512]{0:T(512)S(1)} %convert_reduce_fusion.1, f32[512,1024]{1,0:T(8,128)S(1)} %get-tuple-element.19, f32[512]{0:T(512)S(1)} %get-tuple-element.18), kind=kOutput, calls=%fused_computation.43 | convolution fusion | flops 808189952 | bytes 4722688 | tf_op jit(solution)/shard_map/dot_general | solution.py:135
  111.7 1.1 fusion.42
  112.8 2.6 %collective-permute-start.14 = (bf16[4,64,512]{2,1,0:T(8,128)(2,1)S(1)}, bf16[4,64,512]{2,1,0:T(8,128)(2,1)S(1)}, u32[]{:S(2)}, u32[]{:S(2)}) collective-permute-start(bf16[4,64,512]{2,1,0:T(8,128)(2,1)S(1)} %bitcast.114), channel_id=1, source_target_pairs={{1,0},{0,1},{5,2},{4,3},{3,4},{2,5},{7,6},{6,7},{9,8},{8,9},{13,10... | collective-permute-start | bytes 786440 | tf_op jit(solution)/shard_map/ppermute | solution.py:143
  115.4 1.9 %collective-permute-start.13 = (bf16[4,64,512]{2,1,0:T(8,128)(2,1)S(1)}, bf16[4,64,512]{2,1,0:T(8,128)(2,1)S(1)}, u32[]{:S(2)}, u32[]{:S(2)}) collective-permute-start(bf16[4,64,512]{2,1,0:T(8,128)(2,1)S(1)} %bitcast.111), channel_id=1, source_target_pairs={{0,0},{1,1},{4,2},{5,3},{2,4},{3,5},{6,6},{7,7},{8,8},{9,9},{12,10... | collective-permute-start | bytes 786440 | tf_op jit(solution)/shard_map/ppermute | solution.py:143
  117.4 4.4 %collective-permute-done.14 = bf16[4,64,512]{2,1,0:T(8,128)(2,1)S(1)} collective-permute-done((bf16[4,64,512]{2,1,0:T(8,128)(2,1)S(1)}, bf16[4,64,512]{2,1,0:T(8,128)(2,1)S(1)}, u32[]{:S(2)}, u32[]{:S(2)}) %collective-permute-start.14) | collective-permute-done | bytes 262176 | tf_op jit(solution)/shard_map/ppermute | solution.py:143
  121.8 5.6 %collective-permute-done.13 = bf16[4,64,512]{2,1,0:T(8,128)(2,1)S(1)} collective-permute-done((bf16[4,64,512]{2,1,0:T(8,128)(2,1)S(1)}, bf16[4,64,512]{2,1,0:T(8,128)(2,1)S(1)}, u32[]{:S(2)}, u32[]{:S(2)}) %collective-permute-start.13) | collective-permute-done | bytes 262176 | tf_op jit(solution)/shard_map/ppermute | solution.py:143
  127.4 0.6 gather_fusion.2
  128.0 0.9 broadcast_select_fusion
  (28 shorter events, 0.3 us)
Async XLA Ops:
  0.0 105.3 %copy-start = (bf16[512,512]{1,0:T(8,128)(2,1)S(1)}, bf16[512,512]{1,0:T(8,128)(2,1)}, u32[]{:S(2)}) copy-start(bf16[512,512]{1,0:T(8,128)(2,1)} %param.9) | copy-start | bytes 1572868
  1.1 6.2 %collective-permute-start = (bf16[2,1,64,512]{3,2,1,0:T(8,128)(2,1)S(1)}, bf16[2,1,64,512]{3,2,1,0:T(8,128)(2,1)S(1)}, u32[]{:S(2)}, u32[]{:S(2)}) collective-permute-start(bf16[2,1,64,512]{3,2,1,0:T(8,128)(2,1)S(1)} %get-tuple-element.17), channel_id=1, source_target_pairs={{0,1},{1,2},{2,3},{4,5},{5,6},{6,7},{8,9},{9,10},{10,11},{12,13},{... | collective-permute-start | bytes 393224 | tf_op jit(solution)/shard_map/ppermute | solution.py:38
  5.1 5.7 %collective-permute-start.1 = (bf16[2,1,64,512]{3,2,1,0:T(8,128)(2,1)S(1)}, bf16[2,1,64,512]{3,2,1,0:T(8,128)(2,1)S(1)}, u32[]{:S(2)}, u32[]{:S(2)}) collective-permute-start(bf16[2,1,64,512]{3,2,1,0:T(8,128)(2,1)S(1)} %get-tuple-element.16), channel_id=1, source_target_pairs={{1,0},{2,1},{3,2},{5,4},{6,5},{7,6},{9,8},{10,9},{11,10},{13,12},{... | collective-permute-start | bytes 393224 | tf_op jit(solution)/shard_map/ppermute | solution.py:38
  11.0 5.7 %collective-permute-start.4 = (bf16[2,6,64,128]{3,2,1,0:T(8,128)(2,1)S(1)}, bf16[2,6,64,128]{3,2,1,0:T(8,128)(2,1)S(1)}, u32[]{:S(2)}, u32[]{:S(2)}) collective-permute-start(bf16[2,6,64,128]{3,2,1,0:T(8,128)(2,1)S(1)} %get-tuple-element.9), channel_id=1, source_target_pairs={{0,24},{1,25},{2,26},{3,27},{4,28},{5,29},{6,30},{7,31},{8,16},{9,... | collective-permute-start | bytes 589832 | tf_op jit(solution)/shard_map/ppermute | solution.py:38
  13.2 8.6 %collective-permute-start.3 = (bf16[2,6,64,128]{3,2,1,0:T(8,128)(2,1)S(1)}, bf16[2,6,64,128]{3,2,1,0:T(8,128)(2,1)S(1)}, u32[]{:S(2)}, u32[]{:S(2)}) collective-permute-start(bf16[2,6,64,128]{3,2,1,0:T(8,128)(2,1)S(1)} %get-tuple-element.10), channel_id=1, source_target_pairs={{0,16},{1,17},{2,18},{3,19},{4,20},{5,21},{6,22},{7,23},{8,24},{9,... | collective-permute-start | bytes 589832 | tf_op jit(solution)/shard_map/ppermute | solution.py:38
  13.4 8.3 %collective-permute-start.2 = (bf16[2,6,64,128]{3,2,1,0:T(8,128)(2,1)S(1)}, bf16[2,6,64,128]{3,2,1,0:T(8,128)(2,1)S(1)}, u32[]{:S(2)}, u32[]{:S(2)}) collective-permute-start(bf16[2,6,64,128]{3,2,1,0:T(8,128)(2,1)S(1)} %get-tuple-element.11), channel_id=1, source_target_pairs={{0,8},{1,9},{2,10},{3,11},{4,12},{5,13},{6,14},{7,15},{8,0},{9,1},... | collective-permute-start | bytes 589832 | tf_op jit(solution)/shard_map/ppermute | solution.py:38
  13.7 16.5 %collective-permute-start.6 = (bf16[27,64,512]{2,1,0:T(8,128)(2,1)}, bf16[27,64,512]{2,1,0:T(8,128)(2,1)}, u32[]{:S(2)}, u32[]{:S(2)}) collective-permute-start(bf16[27,64,512]{2,1,0:T(8,128)(2,1)} %param.7), channel_id=1, source_target_pairs={{0,4},{1,5},{2,6},{3,7},{4,0},{5,1},{6,2},{7,3},{8,12},{9,13},{10,... | collective-permute-start | bytes 5308424 | tf_op jit(solution)/shard_map/ppermute | solution.py:38
  21.9 3.8 %collective-permute-start.5 = (bf16[4,2,6,64,128]{4,3,2,1,0:T(8,128)(2,1)S(1)}, bf16[4,2,6,64,128]{4,3,2,1,0:T(8,128)(2,1)S(1)}, u32[]{:S(2)}, u32[]{:S(2)}) collective-permute-start(bf16[4,2,6,64,128]{4,3,2,1,0:T(8,128)(2,1)S(1)} %pad_maximum_fusion.2), channel_id=1, source_target_pairs={{0,4},{1,5},{2,6},{3,7},{4,0},{5,1},{6,2},{7,3},{8,12},{9,13},{10,... | collective-permute-start | bytes 2359304 | tf_op jit(solution)/shard_map/ppermute | solution.py:38
  41.2 0.7 copy-start.4
  55.0 14.3 %collective-permute-start.9 = (bf16[2,4,64,512]{3,1,2,0:T(4,128)(2,1)}, bf16[2,4,64,512]{3,1,2,0:T(4,128)(2,1)S(1)}, u32[]{:S(2)}, u32[]{:S(2)}) collective-permute-start(bf16[2,4,64,512]{3,1,2,0:T(4,128)(2,1)} %get-tuple-element.6), channel_id=1, source_target_pairs={{0,24},{1,25},{2,26},{3,27},{4,28},{5,29},{6,30},{7,31},{8,16},{9,... | collective-permute-start | bytes 1572872 | tf_op jit(solution)/shard_map/ppermute | solution.py:38
  56.4 24.9 %collective-permute-start.8 = (bf16[2,4,64,512]{3,1,2,0:T(4,128)(2,1)}, bf16[2,4,64,512]{3,1,2,0:T(4,128)(2,1)}, u32[]{:S(2)}, u32[]{:S(2)}) collective-permute-start(bf16[2,4,64,512]{3,1,2,0:T(4,128)(2,1)} %get-tuple-element.7), channel_id=1, source_target_pairs={{0,16},{1,17},{2,18},{3,19},{4,20},{5,21},{6,22},{7,23},{8,24},{9,... | collective-permute-start | bytes 1572872 | tf_op jit(solution)/shard_map/ppermute | solution.py:38
  57.4 23.9 %collective-permute-start.7 = (bf16[2,4,64,512]{3,1,2,0:T(4,128)(2,1)}, bf16[2,4,64,512]{3,1,2,0:T(4,128)(2,1)}, u32[]{:S(2)}, u32[]{:S(2)}) collective-permute-start(bf16[2,4,64,512]{3,1,2,0:T(4,128)(2,1)} %get-tuple-element.5), channel_id=1, source_target_pairs={{0,8},{1,9},{2,10},{3,11},{4,12},{5,13},{6,14},{7,15},{8,0},{9,1},... | collective-permute-start | bytes 1572872 | tf_op jit(solution)/shard_map/ppermute | solution.py:38
  83.3 10.1 %collective-permute-start.11 = (bf16[4,64,512]{2,1,0:T(8,128)(2,1)S(1)}, bf16[4,64,512]{2,1,0:T(8,128)(2,1)S(1)}, u32[]{:S(2)}, u32[]{:S(2)}) collective-permute-start(bf16[4,64,512]{2,1,0:T(8,128)(2,1)S(1)} %bitcast.109), channel_id=1, source_target_pairs={{0,1},{1,0},{2,5},{3,4},{4,3},{5,2},{6,7},{7,6},{8,9},{9,8},{10,13... | collective-permute-start | bytes 786440 | tf_op jit(solution)/shard_map/ppermute | solution.py:38
  85.6 13.0 %collective-permute-start.10 = (bf16[4,64,512]{2,1,0:T(8,128)(2,1)S(1)}, bf16[4,64,512]{2,1,0:T(8,128)(2,1)S(1)}, u32[]{:S(2)}, u32[]{:S(2)}) collective-permute-start(bf16[4,64,512]{2,1,0:T(8,128)(2,1)S(1)} %bitcast.110), channel_id=1, source_target_pairs={{0,0},{1,1},{2,4},{3,5},{4,2},{5,3},{6,6},{7,7},{8,8},{9,9},{10,12... | collective-permute-start | bytes 786440 | tf_op jit(solution)/shard_map/ppermute | solution.py:38
  98.6 2.0 %collective-permute-start.12 = (bf16[512,512]{1,0:T(8,128)(2,1)S(1)}, bf16[512,512]{1,0:T(8,128)(2,1)S(1)}, u32[]{:S(2)}, u32[]{:S(2)}) collective-permute-start(bf16[512,512]{1,0:T(8,128)(2,1)S(1)} %bitcast.97), channel_id=1, source_target_pairs={{0,4},{1,5},{2,6},{3,7},{4,0},{5,1},{6,2},{7,3},{8,12},{9,13},{10,... | collective-permute-start | bytes 1572872 | tf_op jit(solution)/shard_map/ppermute | solution.py:38
  98.7 3.6 %copy-start.2 = (bf16[512,512]{1,0:T(8,128)(2,1)S(1)}, bf16[512,512]{1,0:T(8,128)(2,1)}, u32[]{:S(2)}) copy-start(bf16[512,512]{1,0:T(8,128)(2,1)} %param.10) | copy-start | bytes 1572868
  102.1 2.0 %copy-start.3 = (bf16[512,512]{1,0:T(8,128)(2,1)S(1)}, bf16[512,512]{1,0:T(8,128)(2,1)}, u32[]{:S(2)}) copy-start(bf16[512,512]{1,0:T(8,128)(2,1)} %param.8) | copy-start | bytes 1572868
  102.3 1.7 %copy-start.1 = (bf16[1024,512]{1,0:T(8,128)(2,1)}, bf16[1024,512]{1,0:T(8,128)(2,1)S(1)}, u32[]{:S(2)}) copy-start(bf16[1024,512]{1,0:T(8,128)(2,1)S(1)} %fusion.8) | copy-start | bytes 3145732
  112.8 9.0 %collective-permute-start.14 = (bf16[4,64,512]{2,1,0:T(8,128)(2,1)S(1)}, bf16[4,64,512]{2,1,0:T(8,128)(2,1)S(1)}, u32[]{:S(2)}, u32[]{:S(2)}) collective-permute-start(bf16[4,64,512]{2,1,0:T(8,128)(2,1)S(1)} %bitcast.114), channel_id=1, source_target_pairs={{1,0},{0,1},{5,2},{4,3},{3,4},{2,5},{7,6},{6,7},{9,8},{8,9},{13,10... | collective-permute-start | bytes 786440 | tf_op jit(solution)/shard_map/ppermute | solution.py:143
  115.4 11.9 %collective-permute-start.13 = (bf16[4,64,512]{2,1,0:T(8,128)(2,1)S(1)}, bf16[4,64,512]{2,1,0:T(8,128)(2,1)S(1)}, u32[]{:S(2)}, u32[]{:S(2)}) collective-permute-start(bf16[4,64,512]{2,1,0:T(8,128)(2,1)S(1)} %bitcast.111), channel_id=1, source_target_pairs={{0,0},{1,1},{4,2},{5,3},{2,4},{3,5},{6,6},{7,7},{8,8},{9,9},{12,10... | collective-permute-start | bytes 786440 | tf_op jit(solution)/shard_map/ppermute | solution.py:143

commit v2 on v1

v2 whole, which is shorter than its diff:
```python
import functools

import jax
import jax.numpy as jnp
from jax import lax
from jax.experimental import pallas as pl
from jax.experimental.pallas import tpu as pltpu
from jax.sharding import PartitionSpec as P

G = 32
LANES = 128
CORES = 2

epsilon = 1e-06

BOTH = ("tm", "rows")
VMEM_LIMIT = 48 * 1024 * 1024


def everywhere(sizes, target):
    devices, depth = sizes
    pairs = []
    for t in range(devices):
        for z in range(depth):
            to = target(t, z)
            if to is not None:
                pairs.append((t * depth + z, to[0] * depth + to[1]))
    return pairs


def in_vmem(count):
    return [pl.BlockSpec(memory_space=pltpu.VMEM)] * count


def conv_kernel(dests, parts, group, rim, out_type, frames, *refs):
    meta = refs[0]
    weight_refs = refs[1 : 1 + group]
    refs = refs[1 + group :]
    held, refs = refs[: len(dests)], refs[len(dests) :]
    before, refs = refs[:parts], refs[parts:]
    if rim:
        (above, below), refs = refs[:2], refs[2:]
    outs, (weights, raw, sems) = refs[: len(dests)], refs[len(dests) :]
    part, member, z = meta[0], meta[1], meta[2]
    lags = weights.shape[0]
    width, chans = weights.shape[2:]
    chans_here = width // group
    _, rows_here, columns, _ = held[0].shape

    copies = []
    for lag in range(lags):
        for step in range(group):
            owner = lax.rem(member - step + group, group)
            copies.append(
                pltpu.make_async_copy(
                    weight_refs[step].at[:, lag],
                    weights.at[lag, :, pl.ds(pl.multiple_of(owner * chans_here, 16), chans_here)],
                    sems.at[lag, step],
                )
            )
    for copy in copies:
        copy.start()

    skip = 1 if rim else 0
    for n, s in enumerate(dests):
        to = lax.bitwise_xor(part, s)
        wraps = member == 0
        place = jnp.where(wraps, lax.bitwise_xor(part, jnp.maximum(to - 1, 0)), s)
        valid = jnp.logical_or(jnp.logical_not(wraps), to > 0)
        raw[n, frames:, skip : skip + rows_here] = held[n][...]
        if rim:
            raw[n, frames:, 0] = above[s]
            raw[n, frames:, skip + rows_here] = below[s]
            raw[n, :frames, 0] = above[parts + place]
            raw[n, :frames, skip + rows_here] = below[parts + place]
        for i in range(parts):

            @pl.when(place == i)
            def _():
                raw[n, :frames, skip : skip + rows_here] = before[i][...]

        @pl.when(jnp.logical_not(valid))
        def _():
            raw[n, :frames] = jnp.zeros_like(raw[n, :frames])

    side = 3
    count = outs[0].shape[0]
    column = lax.broadcasted_iota(jnp.int32, (count, chans), 0) % columns

    def patches(n):
        whole = []
        for a in range(side):
            for b in range(side):
                pieces = []
                for p in range(frames):
                    f = lax.rem(z + p, frames) + a
                    if rim:
                        pieces.append(raw[n, f, b])
                        pieces.append(raw[n, f, rows_here - 1 + b])
                    else:
                        inner = raw[n, f, b : b + rows_here - 2]
                        pieces.append(inner.reshape(-1, width))
                whole.append(jnp.concatenate(pieces, axis=0))
        return jnp.concatenate(whole, axis=1)

    for n in range(len(dests)):
        lhs = patches(n)
        total = None
        for lag in (1, 0, 2):
            if n == 0:
                for step in range(group):
                    copies[lag * group + step].wait()
            product = jnp.dot(
                lhs,
                weights[lag].reshape(-1, chans),
                preferred_element_type=jnp.float32,
            )
            if lag == 1:
                total = product
            elif lag == 0:
                moved = pltpu.roll(product, 1, 0)
                total = total + jnp.where(column == 0, 0.0, moved)
            else:
                moved = pltpu.roll(product, count - 1, 0)
                total = total + jnp.where(column == columns - 1, 0.0, moved)
        outs[n][...] = total.astype(out_type)


def conv_call(dests, meta, weights, held, before, halos, frames, out_type):
    group, parts = len(weights), len(held)
    _, rows_here, columns, width = held[0].shape
    taps, _, _, chans = weights[0].shape
    lags = weights[0].shape[1]
    rim = halos is not None
    rows = 2 if rim else rows_here - 2
    count = frames * rows * columns
    out = jax.ShapeDtypeStruct((count, chans), out_type)
    operands = [meta, *weights, *[held[s] for s in dests], *before, *(halos or ())]
    specs = [pl.BlockSpec(memory_space=pltpu.SMEM)]
    specs += [pl.BlockSpec(memory_space=pl.ANY)] * group
    specs += in_vmem(len(operands) - 1 - group)
    return pl.pallas_call(
        functools.partial(conv_kernel, dests, parts, group, rim, out_type, frames),
        out_shape=[out] * len(dests),
        in_specs=specs,
        out_specs=in_vmem(len(dests)),
        scratch_shapes=[
            pltpu.VMEM((lags, taps, width, chans), jnp.bfloat16),
            pltpu.VMEM(
                (len(dests), 2 * frames, rows_here + (2 if rim else 0), columns, width),
                jnp.bfloat16,
            ),
            pltpu.SemaphoreType.DMA((lags, group)),
        ],
        compiler_params=pltpu.CompilerParams(vmem_limit_bytes=VMEM_LIMIT),
        cost_estimate=pl.CostEstimate(
            flops=2 * len(dests) * count * taps * lags * width * chans,
            bytes_accessed=2 * taps * lags * width * chans,
            transcendentals=0,
        ),
        name="conv_rim" if rim else "conv_inner",
    )(*operands)


def sum_call(pieces, frames):
    count, chans = pieces[0].shape
    out = jax.ShapeDtypeStruct((count // frames, chans), jnp.bfloat16)

    def kernel(*refs):
        ins, outs = refs[: len(pieces)], refs[len(pieces) :]
        for p, out_ref in enumerate(outs):
            size = out_ref.shape[0]
            total = ins[0][pl.ds(p * size, size)].astype(jnp.float32)
            for ref in ins[1:]:
                total = total + ref[pl.ds(p * size, size)].astype(jnp.float32)
            out_ref[...] = total.astype(out_ref.dtype)

    return pl.pallas_call(
        kernel,
        out_shape=[out] * frames,
        in_specs=in_vmem(len(pieces)),
        out_specs=in_vmem(frames),
        compiler_params=pltpu.CompilerParams(vmem_limit_bytes=VMEM_LIMIT),
        name="sum_parts",
    )(*pieces)


def attend_kernel(frames, share, chunks, *refs):
    own_count = frames * chunks
    all_count = own_count * share
    tokens, refs = refs[:all_count], refs[all_count:]
    (wq, wk, wv, wo), refs = refs[:4], refs[4:]
    outs, (normed, keys, values) = refs[:frames], refs[frames:]
    size, chans = normed.shape
    per_group = chans // G

    tile_row = lax.broadcasted_iota(jnp.int32, (LANES, LANES), 0) // per_group
    tile_col = lax.broadcasted_iota(jnp.int32, (LANES, LANES), 1) // per_group
    same = (tile_row == tile_col).astype(jnp.float32).astype(jnp.bfloat16)

    def group_mean(sums):
        first = sums.astype(jnp.bfloat16)
        rest = sums - first.astype(jnp.float32)
        second = rest.astype(jnp.bfloat16)
        third = rest - second.astype(jnp.float32)
        tiles = []
        for tile in range(chans // LANES):
            lanes = slice(tile * LANES, (tile + 1) * LANES)
            stacked = jnp.concatenate(
                [
                    first.astype(jnp.float32)[:, lanes],
                    second.astype(jnp.float32)[:, lanes],
                    third[:, lanes],
                ],
                axis=0,
            ).astype(jnp.bfloat16)
            spread = jnp.dot(stacked, same, preferred_element_type=jnp.float32)
            tiles.append(jnp.sum(spread, axis=0, keepdims=True))
        return jnp.concatenate(tiles, axis=1) / (size * per_group)

    def folded(x):
        return jnp.sum(x.reshape(-1, 8, chans), axis=0)

    average = group_mean(sum(folded(ref[...].astype(jnp.float32)) for ref in tokens))

    def spread_of(ref):
        centered = ref[...].astype(jnp.float32) - average
        return folded(centered * centered)

    scale = lax.rsqrt(group_mean(sum(spread_of(ref) for ref in tokens)) + epsilon)
    place = 0
    for ref in tokens:
        rows = ref.shape[0]
        normed[pl.ds(place, rows)] = (
            (ref[...].astype(jnp.float32) - average) * scale
        ).astype(jnp.bfloat16)
        place += rows

    step = min(256, size)
    for start in range(0, size, step):
        x = normed[pl.ds(start, step)]
        keys[pl.ds(start, step)] = jnp.dot(
            x, wk[...], preferred_element_type=jnp.float32
        ).astype(jnp.bfloat16)
        values[pl.ds(start, step)] = jnp.dot(
            x, wv[...], preferred_element_type=jnp.float32
        ).astype(jnp.bfloat16)

    place = 0
    for index in range(own_count):
        ref = tokens[index]
        rows = ref.shape[0]
        queries = jnp.dot(
            normed[pl.ds(place, rows)], wq[...], preferred_element_type=jnp.float32
        ).astype(jnp.bfloat16)
        place += rows
        scores = lax.dot_general(
            queries, keys[...], (((1,), (1,)), ((), ())), preferred_element_type=jnp.float32
        ) * chans ** (-0.5)
        row_max = jnp.max(scores, axis=1, keepdims=True)
        exp_weights = jnp.exp(scores - row_max).astype(jnp.bfloat16)
        denominator = jnp.sum(exp_weights.astype(jnp.float32), axis=1, keepdims=True)
        numerator = jnp.dot(exp_weights, values[...], preferred_element_type=jnp.float32)
        attended = (numerator / denominator).astype(jnp.bfloat16)
        summed = ref[...].astype(jnp.float32) + jnp.dot(
            attended, wo[...], preferred_element_type=jnp.float32
        )
        summed = summed.astype(jnp.bfloat16)
        out = outs[index // chunks]
        rows_here, columns, _ = out.shape
        if index % chunks == 0:
            out[1 : rows_here - 1] = summed.reshape(rows_here - 2, columns, chans)
        else:
            out[0] = summed[:columns]
            out[rows_here - 1] = summed[columns:]


def attend_call(own, others, weights, frames, rows_here, columns):
    chunks = len(own) // frames
    share = 1 + len(others) // len(own)
    chans = own[0].shape[1]
    size = sum(x.shape[0] for x in own) * share
    mine = size // share
    out = jax.ShapeDtypeStruct((rows_here, columns, chans), jnp.bfloat16)
    operands = [*own, *others, *weights]
    return pl.pallas_call(
        functools.partial(attend_kernel, frames, share, chunks),
        out_shape=[out] * frames,
        in_specs=in_vmem(len(operands)),
        out_specs=in_vmem(frames),
        scratch_shapes=[pltpu.VMEM((size, chans), jnp.bfloat16)] * 3,
        compiler_params=pltpu.CompilerParams(vmem_limit_bytes=VMEM_LIMIT),
        cost_estimate=pl.CostEstimate(
            flops=2 * (2 * size * chans * chans + 2 * mine * chans * (chans + size)),
            bytes_accessed=8 * chans * chans + 2 * size * chans,
            transcendentals=mine * size,
        ),
        name="attend",
    )(*operands)


def place_kernel(meta, *refs):
    parts, out, sems = refs[:-2], refs[-2], refs[-1]
    frames = len(parts)
    copies = [
        pltpu.make_async_copy(ref, out.at[lax.rem(meta[2] + p, frames)], sems.at[p])
        for p, ref in enumerate(parts)
    ]
    for copy in copies:
        copy.start()
    for copy in copies:
        copy.wait()


def place_call(meta, parts):
    frames = len(parts)
    anywhere = pl.BlockSpec(memory_space=pl.ANY)
    return pl.pallas_call(
        place_kernel,
        out_shape=jax.ShapeDtypeStruct((frames, *parts[0].shape), parts[0].dtype),
        in_specs=[pl.BlockSpec(memory_space=pltpu.SMEM)] + [anywhere] * frames,
        out_specs=anywhere,
        scratch_shapes=[pltpu.SemaphoreType.DMA((frames,))],
        name="place_frames",
    )(meta, *parts)


def body(latents, conv_weight, query_weight, key_weight, value_weight, out_weight):
    frames, rows_here, columns, chans = latents.shape
    taps, chans_here, _ = conv_weight.shape
    devices, depth = lax.axis_size("tm"), lax.axis_size("rows")
    sizes = (devices, depth)
    group = LANES // chans_here
    parts = devices // group
    width = group * chans_here
    t_index, z_index = lax.axis_index("tm"), lax.axis_index("rows")
    part, member = t_index // group, t_index % group
    meta = jnp.stack([part, member, z_index]).astype(jnp.int32)

    def permute(block, target):
        return lax.ppermute(block, BOTH, everywhere(sizes, target))

    def to_part(s):
        return lambda t, z: ((t // group ^ s) * group + t % group, z)

    def to_member(step):
        return lambda t, z: (t // group * group + (t + step) % group, z)

    held, before = [None] * parts, [None] * parts
    for s in reversed(range(parts)):
        piece = lax.dynamic_slice_in_dim(latents, (part ^ s) * width, width, axis=3)
        held[s] = permute(piece, to_part(s)) if s else piece
    for s in range(parts):
        before[s] = permute(held[s], to_member(1))

    split = conv_weight.reshape(taps // 3, 3, chans_here, chans)
    weights = [split] + [permute(split, to_member(step)) for step in range(1, group)]

    last = jnp.stack([x[:, rows_here - 1] for x in (*held, *before)])
    first = jnp.stack([x[:, 0] for x in (*held, *before)])
    halos = (
        permute(last, lambda t, z: (t, z + 1) if z + 1 < depth else None),
        permute(first, lambda t, z: (t, z - 1) if z else None),
    )

    away = list(reversed(range(1, parts)))
    sums = []
    for halo in (None, halos):
        call = functools.partial(conv_call, meta=meta, weights=weights, held=held, before=before)
        call = functools.partial(call, halos=halo, frames=frames)
        if halo is None:
            sent = call(away[:1], out_type=jnp.bfloat16) + call(away[1:], out_type=jnp.bfloat16)
        else:
            sent = call(away, out_type=jnp.bfloat16)
        got = [permute(x, to_part(s)) for s, x in zip(away, sent)]
        (mine,) = call([0], out_type=jnp.float32)
        sums.append(sum_call([mine, *got], frames))

    share = depth // frames

    def frame_home(t, z, p):
        frame = t % CORES * frames + (z + p) % frames
        slot = frame * share + z // frames
        return (t // CORES * CORES + slot % CORES, slot // CORES)

    def next_in_frame(t, z, step):
        slot = z * CORES + t % CORES
        slot = slot // share * share + (slot + step) % share
        return (t // CORES * CORES + slot % CORES, slot // CORES)

    own = []
    for p in range(frames):
        for chunk in sums:
            own.append(permute(chunk[p], lambda t, z: frame_home(t, z, p)))
    others = []
    for step in range(1, share):
        others += [permute(x, lambda t, z: next_in_frame(t, z, step)) for x in own]

    done = attend_call(
        own,
        others,
        (query_weight, key_weight, value_weight, out_weight),
        frames,
        rows_here,
        columns,
    )
    back = []
    for p in range(frames):
        pairs = [(b, a) for a, b in everywhere(sizes, lambda t, z: frame_home(t, z, p))]
        back.append(lax.ppermute(done[p], BOTH, pairs))
    return place_call(meta, back)


def solution(mesh):
    placed = (P("tm", "rows", None, None), P(None, "tm", None), P(), P(), P(), P())
    return jax.shard_map(
        body, mesh=mesh, in_specs=placed, out_specs=P("tm", "rows", None, None), check_vma=False
    )
```

time: 129 us -> 114 us (0.88)
  Pallas kernels: 0 us -> 39.7 us
  waiting for transfers between devices: 56 us -> 17.1 us
  matrix products: 18.7 us -> 0 us
  starting transfers between devices: 25.1 us -> 41.1 us
  other arithmetic: 12.3 us -> 0.08 us
  local copies, waits for them, and re-layouts: 16.5 us -> 14.3 us
    pallas_call x0 -> x9, Pallas kernels: none -> 39.7 us  [the longest x1 17.7 us: place_call(): pl.pallas_call(place_kernel, out_shape=jax.ShapeDtypeStruct((frames, *par...]
    ppermute x13 -> x24, waiting for transfers between devices: 46.1 us -> 7.68 us  [permute(): return lax.ppermute(block, BOTH, everywhere(sizes, target))]
    ppermute x13 -> x24, starting transfers between devices: 20.5 us -> 36 us  [permute(): return lax.ppermute(block, BOTH, everywhere(sizes, target))]
    dot_general x8 -> x0, matrix products: 9.69 us -> none  [the longest x1 3.19 us: body(): jnp.dot(attended, out_weight, preferred_element_type=jnp.float32)]
    conv_general_dilated x1 -> x0, matrix products: 8.99 us -> none  [body(): lax.conv_general_dilated(window, kernel.reshape(side, side, side, width,...]
    ppermute x0 -> x7, local copies, waits for them, and re-layouts: none -> 6.4 us  [permute(): return lax.ppermute(block, BOTH, everywhere(sizes, target))]
    gather x3 -> x0, local copies, waits for them, and re-layouts: 5.85 us -> none  [the longest x1 4.57 us: body(): kernel = jnp.take(jnp.stack(kernel_parts), order, axis=0)]
    another operation x4 -> x1, other arithmetic: 4.28 us -> 0.08 us  [body(): meta = jnp.stack([part, member, z_index]).astype(jnp.int32)]
  transfers between devices with their start and end apart: 15 -> 26, of which waited for: 11 -> 5; matrix products, arithmetic and copies ran while one was open for 5% -> 10% of each run, Pallas kernels for 0% -> 10%
where the time goes in v2:
time: 114 us; the launch traced here: 113 us
  starting transfers between devices  41.1 us (36%)
  Pallas kernels  39.7 us (35%)
  waiting for transfers between devices  17.1 us (15%)
  local copies, waits for them, and re-layouts  14.3 us (13%)
    ppermute x24, starting transfers between devices, permute(): return lax.ppermute(block, BOTH, everywhere(sizes, target))  36 us
    pallas_call x1, Pallas kernels, place_call(): pl.pallas_call(place_kernel, out_shape=jax.ShapeDtypeStruct((frames, *par...  17.7 us
    pallas_call x5, Pallas kernels, conv_call(): pl.pallas_call(functools.partial(conv_kernel, dests, parts, group, rim, o...  15.9 us
    ppermute x2, waiting for transfers between devices, body(): back.append(lax.ppermute(done[p], BOTH, pairs))  9.39 us
    ppermute x24, waiting for transfers between devices, permute(): return lax.ppermute(block, BOTH, everywhere(sizes, target))  7.68 us
    ppermute x7, local copies, waits for them, and re-layouts, permute(): return lax.ppermute(block, BOTH, everywhere(sizes, target))  6.4 us
    unnamed x45, local copies, waits for them, and re-layouts  6 us
    pallas_call x1, Pallas kernels, attend_call(): pl.pallas_call(functools.partial(attend_kernel, frames, share, chunks), o...  5.92 us
  transfers between devices with their start and end apart: 26, of which 5 were waited for; matrix products, arithmetic and copies ran while one was open for 10% of the time, Pallas kernels for 10%

profile of v2, /device:TPU:1, one launch (start us, length us, event | category | flops | bytes accessed | tf_op | source)
XLA Modules:
  0.0 112.8 jit_solution(16603772158208220522)
XLA Ops:
  0.0 1.3 %constant_dynamic-slice_fusion = (bf16[2,4,64,128]{3,2,1,0:T(8,128)(2,1)S(1)}, bf16[2,4,64,128]{3,2,1,0:T(8,128)(2,1)S(1)}, bf16[2,4,64,128]{3,2,1,0:T(8,128)(2,1)S(1)}, bf16[2,4,64,128]{3,2,1,0:T(8,128)(2,1)S(1)}) fusion(bf16[2,4,64,512]{3,2,1,0:T(8,128)(2,1)} %param.6, s32[]{:T(128)S(6)} %select_n.28, s32[]{:T(128)S(6)} %select_n.27, s32[]{:T(128)S(6)} %select_n.26, ...), kind=kLoop, calls=%fused_computation.32 | loop fusion | bytes 1048592 | tf_op jit(solution)/shard_map/dynamic_slice | solution.py:351
  1.3 2.1 %collective-permute-start.2 = (bf16[2,4,64,128]{3,2,0,1:T(8,128)(2,1)S(1)}, bf16[2,4,64,128]{3,2,0,1:T(8,128)(2,1)S(1)}, u32[]{:S(2)}, u32[]{:S(2)}) collective-permute-start(bf16[2,4,64,128]{3,2,0,1:T(8,128)(2,1)S(1)} %copy.40), channel_id=1, source_target_pairs={{0,8},{1,9},{2,10},{3,11},{4,12},{5,13},{6,14},{7,15},{8,0},{9,1},... | collective-permute-start | bytes 393224 | tf_op jit(solution)/shard_map/ppermute | solution.py:341
  3.4 1.3 %collective-permute-start.4 = (bf16[2,4,64,128]{3,2,0,1:T(8,128)(2,1)S(1)}, bf16[2,4,64,128]{3,2,0,1:T(8,128)(2,1)S(1)}, u32[]{:S(2)}, u32[]{:S(2)}) collective-permute-start(bf16[2,4,64,128]{3,2,0,1:T(8,128)(2,1)S(1)} %copy.41), channel_id=1, source_target_pairs={{0,16},{1,17},{2,18},{3,19},{4,20},{5,21},{6,22},{7,23},{8,24},{9,... | collective-permute-start | bytes 393224 | tf_op jit(solution)/shard_map/ppermute | solution.py:341
  4.8 0.1 collective-permute-start.6
  4.9 1.3 %collective-permute-start.1 = (bf16[2,4,64,128]{3,2,0,1:T(8,128)(2,1)S(1)}, bf16[2,4,64,128]{3,2,0,1:T(8,128)(2,1)S(1)}, u32[]{:S(2)}, u32[]{:S(2)}) collective-permute-start(bf16[2,4,64,128]{3,2,0,1:T(8,128)(2,1)S(1)} %copy.39), channel_id=1, source_target_pairs={{0,4},{1,5},{2,6},{3,7},{4,0},{5,1},{6,2},{7,3},{8,12},{9,13},{10,... | collective-permute-start | bytes 393224 | tf_op jit(solution)/shard_map/ppermute | solution.py:341
  6.2 0.1 collective-permute-start
  6.2 0.6 constant_dynamic-update-slice_fusion.15
  6.9 0.0 collective-permute-done.2
  6.9 1.4 %collective-permute-start.3 = (bf16[2,4,64,128]{3,2,0,1:T(8,128)(2,1)S(1)}, bf16[2,4,64,128]{3,2,0,1:T(8,128)(2,1)S(1)}, u32[]{:S(2)}, u32[]{:S(2)}) collective-permute-start(bf16[2,4,64,128]{3,2,0,1:T(8,128)(2,1)S(1)} %collective-permute-done.2), channel_id=1, source_target_pairs={{0,4},{1,5},{2,6},{3,7},{4,0},{5,1},{6,2},{7,3},{8,12},{9,13},{10,... | collective-permute-start | bytes 393224 | tf_op jit(solution)/shard_map/ppermute | solution.py:341
  8.3 0.0 collective-permute-done.4
  8.3 3.9 %collective-permute-start.5 = (bf16[2,4,64,128]{3,2,0,1:T(8,128)(2,1)S(1)}, bf16[2,4,64,128]{3,2,0,1:T(8,128)(2,1)S(1)}, u32[]{:S(2)}, u32[]{:S(2)}) collective-permute-start(bf16[2,4,64,128]{3,2,0,1:T(8,128)(2,1)S(1)} %collective-permute-done.4), channel_id=1, source_target_pairs={{0,4},{1,5},{2,6},{3,7},{4,0},{5,1},{6,2},{7,3},{8,12},{9,13},{10,... | collective-permute-start | bytes 393224 | tf_op jit(solution)/shard_map/ppermute | solution.py:341
  12.2 0.1 collective-permute-start.7
  12.3 0.6 constant_dynamic-update-slice_fusion.14
  13.0 0.6 constant_dynamic-update-slice_fusion.13
  13.6 0.6 constant_dynamic-update-slice_fusion.12
  14.2 0.0 collective-permute-done.1
  14.2 0.7 constant_dynamic-update-slice_fusion.11
  14.9 0.7 constant_dynamic-update-slice_fusion.10
  15.6 0.7 constant_dynamic-update-slice_fusion.9
  16.2 0.6 constant_dynamic-update-slice_fusion.8
  16.9 3.9 %collective-permute-start.12 = (bf16[8,2,64,128]{3,2,1,0:T(8,128)(2,1)}, bf16[8,2,64,128]{3,2,1,0:T(8,128)(2,1)}, u32[]{:S(2)}, u32[]{:S(2)}) collective-permute-start(bf16[8,2,64,128]{3,2,1,0:T(8,128)(2,1)} %get-tuple-element.32), channel_id=1, source_target_pairs={{0,1},{1,2},{2,3},{4,5},{5,6},{6,7},{8,9},{9,10},{10,11},{12,13},{... | collective-permute-start | bytes 786440 | tf_op jit(solution)/shard_map/ppermute | solution.py:341
  20.8 1.3 %collective-permute-start.13 = (bf16[8,2,64,128]{3,2,1,0:T(8,128)(2,1)}, bf16[8,2,64,128]{3,2,1,0:T(8,128)(2,1)}, u32[]{:S(2)}, u32[]{:S(2)}) collective-permute-start(bf16[8,2,64,128]{3,2,1,0:T(8,128)(2,1)} %get-tuple-element.31), channel_id=1, source_target_pairs={{1,0},{2,1},{3,2},{5,4},{6,5},{7,6},{9,8},{10,9},{11,10},{13,12},{... | collective-permute-start | bytes 786440 | tf_op jit(solution)/shard_map/ppermute | solution.py:341
  22.1 0.1 pad_add_fusion.refs_0_.meta
  22.2 0.9 copy.12.refs_4_.refs_5_.refs_6_
  23.1 0.9 copy.16.refs_3_
  24.0 0.9 copy.21.refs_3_.refs_4_
  24.9 0.9 copy.22.refs_4_.refs_5_
  25.8 0.9 copy.13.refs_5_.refs_6_.refs_7_
  26.8 0.9 copy.14.refs_6_.refs_7_.refs_8_
  27.7 0.9 copy.15.refs_7_.refs_8_.refs_9_
  28.6 1.5 %collective-permute-done.13.refs_9_.refs_11_ = bf16[8,2,64,128]{3,2,1,0:T(8,128)(2,1)} collective-permute-done((bf16[8,2,64,128]{3,2,1,0:T(8,128)(2,1)}, bf16[8,2,64,128]{3,2,1,0:T(8,128)(2,1)}, u32[]{:S(2)}, u32[]{:S(2)}) %collective-permute-start.13) | collective-permute-done | bytes 262176 | tf_op jit(solution)/shard_map/ppermute | solution.py:341
  30.1 5.0 %conv_rim.3 = (bf16[256,512]{1,0:T(8,128)(2,1)S(1)}, bf16[256,512]{1,0:T(8,128)(2,1)S(1)}, bf16[256,512]{1,0:T(8,128)(2,1)S(1)}) custom-call(s32[3]{0:T(128)S(1)} %pad_add_fusion.refs_0_.meta, bf16[9,3,64,512]{3,2,1,0:T(8,128)(2,1)S(1)} %bitcast.69, bf16[9,3,64,512]{3,2,1,0:T(8,128)(2,1)S(1)} %collective-permute-done.refs_2_, ...), custom_call_target="tpu_custom_call" | custom-call | flops 2717908992 | bytes 3538944 | tf_op jit(solution)/shard_map/conv_rim/pallas_call | solution.py:142
  35.1 1.3 %collective-permute-start.14 = (bf16[256,512]{1,0:T(8,128)(2,1)S(1)}, bf16[256,512]{1,0:T(8,128)(2,1)S(1)}, u32[]{:S(2)}, u32[]{:S(2)}) collective-permute-start(bf16[256,512]{1,0:T(8,128)(2,1)S(1)} %get-tuple-element.19), channel_id=1, source_target_pairs={{0,24},{1,25},{2,26},{3,27},{4,28},{5,29},{6,30},{7,31},{8,16},{9,... | collective-permute-start | bytes 786440 | tf_op jit(solution)/shard_map/ppermute | solution.py:341
  36.4 1.2 %collective-permute-start.15 = (bf16[256,512]{1,0:T(8,128)(2,1)S(1)}, bf16[256,512]{1,0:T(8,128)(2,1)S(1)}, u32[]{:S(2)}, u32[]{:S(2)}) collective-permute-start(bf16[256,512]{1,0:T(8,128)(2,1)S(1)} %get-tuple-element.20), channel_id=1, source_target_pairs={{0,16},{1,17},{2,18},{3,19},{4,20},{5,21},{6,22},{7,23},{8,24},{9,... | collective-permute-start | bytes 786440 | tf_op jit(solution)/shard_map/ppermute | solution.py:341
  37.6 0.2 collective-permute-start.16
  37.8 3.4 %conv_inner.5 = (bf16[256,512]{1,0:T(8,128)(2,1)S(1)}, bf16[256,512]{1,0:T(8,128)(2,1)S(1)}) custom-call(s32[3]{0:T(128)S(1)} %pad_add_fusion.refs_0_.meta, bf16[9,3,64,512]{3,2,1,0:T(8,128)(2,1)S(1)} %bitcast.70, bf16[9,3,64,512]{3,2,1,0:T(8,128)(2,1)S(1)} %collective-permute-done.refs_2_, bf16[2,4,64,128]{3,2,1,0:T(8,128)(2,1)S(1)} %copy.21.refs_3_.refs_4_, ...), custom_call_target="tpu_custom_call" | custom-call | flops 1811939328 | bytes 3538944 | tf_op jit(solution)/shard_map/conv_inner/pallas_call | solution.py:142
  41.2 1.3 %collective-permute-start.10 = (bf16[256,512]{1,0:T(8,128)(2,1)S(1)}, bf16[256,512]{1,0:T(8,128)(2,1)S(1)}, u32[]{:S(2)}, u32[]{:S(2)}) collective-permute-start(bf16[256,512]{1,0:T(8,128)(2,1)S(1)} %get-tuple-element.17), channel_id=1, source_target_pairs={{0,8},{1,9},{2,10},{3,11},{4,12},{5,13},{6,14},{7,15},{8,0},{9,1},... | collective-permute-start | bytes 786440 | tf_op jit(solution)/shard_map/ppermute | solution.py:341
  42.5 0.3 collective-permute-start.9
  42.8 2.3 %conv_inner.4 = bf16[256,512]{1,0:T(8,128)(2,1)S(1)} custom-call(s32[3]{0:T(128)S(1)} %pad_add_fusion.refs_0_.meta, bf16[9,3,64,512]{3,2,1,0:T(8,128)(2,1)S(1)} %bitcast.71, bf16[9,3,64,512]{3,2,1,0:T(8,128)(2,1)S(1)} %collective-permute-done.refs_2_, bf16[2,4,64,128]{3,2,1,0:T(8,128)(2,1)S(1)} %copy.16.refs_3_, ...), custom_call_target="tpu_custom_call" | custom-call | flops 905969664 | bytes 3538944 | tf_op jit(solution)/shard_map/conv_inner/pallas_call | solution.py:142
  45.1 1.2 %collective-permute-start.8 = (bf16[256,512]{1,0:T(8,128)(2,1)S(1)}, bf16[256,512]{1,0:T(8,128)(2,1)S(1)}, u32[]{:S(2)}, u32[]{:S(2)}) collective-permute-start(bf16[256,512]{1,0:T(8,128)(2,1)S(1)} %conv_inner.4), channel_id=1, source_target_pairs={{0,24},{1,25},{2,26},{3,27},{4,28},{5,29},{6,30},{7,31},{8,16},{9,... | collective-permute-start | bytes 786440 | tf_op jit(solution)/shard_map/ppermute | solution.py:341
  46.4 2.9 %conv_rim.2.refs_0_ = f32[256,512]{1,0:T(8,128)S(1)} custom-call(s32[3]{0:T(128)S(1)} %pad_add_fusion.refs_0_.meta, bf16[9,3,64,512]{3,2,1,0:T(8,128)(2,1)S(1)} %bitcast.72, bf16[9,3,64,512]{3,2,1,0:T(8,128)(2,1)S(1)} %collective-permute-done.refs_2_, bf16[2,4,64,128]{3,2,1,0:T(8,128)(2,1)S(1)} %copy-done.2, ...), custom_call_target="tpu_custom_call" | custom-call | flops 905969664 | bytes 3538944 | tf_op jit(solution)/shard_map/conv_rim/pallas_call | solution.py:142
  49.3 2.3 %conv_inner.3.refs_0_ = f32[256,512]{1,0:T(8,128)S(1)} custom-call(s32[3]{0:T(128)S(1)} %pad_add_fusion.refs_0_.meta, bf16[9,3,64,512]{3,2,1,0:T(8,128)(2,1)S(1)} %bitcast.73, bf16[9,3,64,512]{3,2,1,0:T(8,128)(2,1)S(1)} %collective-permute-done.refs_2_, bf16[2,4,64,128]{3,2,1,0:T(8,128)(2,1)S(1)} %copy-done.2, ...), custom_call_target="tpu_custom_call" | custom-call | flops 905969664 | bytes 3538944 | tf_op jit(solution)/shard_map/conv_inner/pallas_call | solution.py:142
  51.6 0.0 copy-start.4
  51.6 0.0 copy-start.5
  51.6 0.0 copy-start.6
  51.6 0.0 copy-start.7
  51.7 0.1 sum_parts.3
  51.8 6.9 %collective-permute-start.17 = (bf16[128,512]{1,0:T(8,128)(2,1)S(1)}, bf16[128,512]{1,0:T(8,128)(2,1)S(1)}, u32[]{:S(2)}, u32[]{:S(2)}) collective-permute-start(bf16[128,512]{1,0:T(8,128)(2,1)S(1)} %get-tuple-element.22), channel_id=1, source_target_pairs={{0,0},{1,1},{2,4},{3,5},{4,2},{5,3},{6,6},{7,7},{8,8},{9,9},{10,12... | collective-permute-start | bytes 393224 | tf_op jit(solution)/shard_map/ppermute | solution.py:341
  58.7 0.5 collective-permute-start.19
  59.2 0.0 collective-permute-done.8.refs_1_
  59.2 0.1 sum_parts.2
  59.3 6.1 %collective-permute-start.11 = (bf16[128,512]{1,0:T(8,128)(2,1)S(1)}, bf16[128,512]{1,0:T(8,128)(2,1)S(1)}, u32[]{:S(2)}, u32[]{:S(2)}) collective-permute-start(bf16[128,512]{1,0:T(8,128)(2,1)S(1)} %get-tuple-element.18), channel_id=1, source_target_pairs={{0,0},{1,1},{2,4},{3,5},{4,2},{5,3},{6,6},{7,7},{8,8},{9,9},{10,12... | collective-permute-start | bytes 393224 | tf_op jit(solution)/shard_map/ppermute | solution.py:341
  65.4 1.1 collective-permute-start.18
  66.5 0.5 collective-permute-start.23
  67.0 2.3 %collective-permute-done.11.refs_0_ = bf16[128,512]{1,0:T(8,128)(2,1)S(1)} collective-permute-done((bf16[128,512]{1,0:T(8,128)(2,1)S(1)}, bf16[128,512]{1,0:T(8,128)(2,1)S(1)}, u32[]{:S(2)}, u32[]{:S(2)}) %collective-permute-start.11) | collective-permute-done | bytes 131104 | tf_op jit(solution)/shard_map/ppermute | solution.py:341
  69.3 2.5 %collective-permute-done.18.refs_2_ = bf16[128,512]{1,0:T(8,128)(2,1)S(1)} collective-permute-done((bf16[128,512]{1,0:T(8,128)(2,1)S(1)}, bf16[128,512]{1,0:T(8,128)(2,1)S(1)}, u32[]{:S(2)}, u32[]{:S(2)}) %collective-permute-start.18) | collective-permute-done | bytes 131104 | tf_op jit(solution)/shard_map/ppermute | solution.py:341
  71.8 1.3 %collective-permute-done.22.refs_6_ = bf16[128,512]{1,0:T(8,128)(2,1)S(1)} collective-permute-done((bf16[128,512]{1,0:T(8,128)(2,1)S(1)}, bf16[128,512]{1,0:T(8,128)(2,1)S(1)}, u32[]{:S(2)}, u32[]{:S(2)}) %collective-permute-start.22) | collective-permute-done | bytes 131104 | tf_op jit(solution)/shard_map/ppermute | solution.py:341
  73.1 5.9 %attend.1 = (bf16[4,64,512]{2,1,0:T(8,128)(2,1)S(1)}, bf16[4,64,512]{2,1,0:T(8,128)(2,1)S(1)}) custom-call(bf16[128,512]{1,0:T(8,128)(2,1)S(1)} %collective-permute-done.11.refs_0_, bf16[128,512]{1,0:T(8,128)(2,1)S(1)} %collective-permute-done.17.refs_1_, bf16[128,512]{1,0:T(8,128)(2,1)S(1)} %collective-permute-done.18.refs_2_, ...), custom_call_target="tpu_custom_call" | custom-call | flops 2684354560 | bytes 3145728 | tf_op jit(solution)/shard_map/attend/pallas_call | solution.py:286
  79.1 4.8 %collective-permute-start.24 = (bf16[4,64,512]{2,1,0:T(8,128)(2,1)S(1)}, bf16[4,64,512]{2,1,0:T(8,128)(2,1)S(1)}, u32[]{:S(2)}, u32[]{:S(2)}) collective-permute-start(bf16[4,64,512]{2,1,0:T(8,128)(2,1)S(1)} %get-tuple-element.25), channel_id=1, source_target_pairs={{0,0},{1,1},{4,2},{5,3},{2,4},{3,5},{6,6},{7,7},{8,8},{9,9},{12,10... | collective-permute-start | bytes 786440 | tf_op jit(solution)/shard_map/ppermute | solution.py:410
  83.9 0.3 collective-permute-start.25
  84.2 9.4 %collective-permute-done.24.refs_0_ = bf16[4,64,512]{2,1,0:T(8,128)(2,1)S(1)} collective-permute-done((bf16[4,64,512]{2,1,0:T(8,128)(2,1)S(1)}, bf16[4,64,512]{2,1,0:T(8,128)(2,1)S(1)}, u32[]{:S(2)}, u32[]{:S(2)}) %collective-permute-start.24) | collective-permute-done | bytes 262176 | tf_op jit(solution)/shard_map/ppermute | solution.py:410
  93.6 0.7 copy-done.15
  94.3 0.7 copy-done.16
  95.0 17.7 %place_frames.1 = bf16[2,4,64,512]{3,2,1,0:T(8,128)(2,1)} custom-call(s32[3]{0:T(128)} %copy-done.3, bf16[4,64,512]{2,1,0:T(8,128)(2,1)} %copy-done.15, bf16[4,64,512]{2,1,0:T(8,128)(2,1)} %copy-done.16), custom_call_target="tpu_custom_call" | custom-call | tf_op jit(solution)/shard_map/place_frames/pallas_call | solution.py:318
  (52 shorter events, 0.1 us)
Async XLA Ops:
  0.0 6.2 %copy-start = (bf16[27,64,512]{2,1,0:T(8,128)(2,1)S(1)}, bf16[27,64,512]{2,1,0:T(8,128)(2,1)}, u32[]{:S(2)}) copy-start(bf16[27,64,512]{2,1,0:T(8,128)(2,1)} %param.7) | copy-start | bytes 5308420
  1.3 5.0 %copy-start.1 = (bf16[2,4,64,128]{3,2,1,0:T(8,128)(2,1)}, bf16[2,4,64,128]{3,2,1,0:T(8,128)(2,1)S(1)}, u32[]{:S(2)}) copy-start(bf16[2,4,64,128]{3,2,1,0:T(8,128)(2,1)S(1)} %get-tuple-element.30.refs_3_) | copy-start | bytes 393220
  1.3 5.6 %collective-permute-start.2 = (bf16[2,4,64,128]{3,2,0,1:T(8,128)(2,1)S(1)}, bf16[2,4,64,128]{3,2,0,1:T(8,128)(2,1)S(1)}, u32[]{:S(2)}, u32[]{:S(2)}) collective-permute-start(bf16[2,4,64,128]{3,2,0,1:T(8,128)(2,1)S(1)} %copy.40), channel_id=1, source_target_pairs={{0,8},{1,9},{2,10},{3,11},{4,12},{5,13},{6,14},{7,15},{8,0},{9,1},... | collective-permute-start | bytes 393224 | tf_op jit(solution)/shard_map/ppermute | solution.py:341
  3.4 4.9 %collective-permute-start.4 = (bf16[2,4,64,128]{3,2,0,1:T(8,128)(2,1)S(1)}, bf16[2,4,64,128]{3,2,0,1:T(8,128)(2,1)S(1)}, u32[]{:S(2)}, u32[]{:S(2)}) collective-permute-start(bf16[2,4,64,128]{3,2,0,1:T(8,128)(2,1)S(1)} %copy.41), channel_id=1, source_target_pairs={{0,16},{1,17},{2,18},{3,19},{4,20},{5,21},{6,22},{7,23},{8,24},{9,... | collective-permute-start | bytes 393224 | tf_op jit(solution)/shard_map/ppermute | solution.py:341
  4.8 7.5 %collective-permute-start.6 = (bf16[2,4,64,128]{3,2,0,1:T(8,128)(2,1)S(1)}, bf16[2,4,64,128]{3,2,0,1:T(8,128)(2,1)S(1)}, u32[]{:S(2)}, u32[]{:S(2)}) collective-permute-start(bf16[2,4,64,128]{3,2,0,1:T(8,128)(2,1)S(1)} %copy.42), channel_id=1, source_target_pairs={{0,24},{1,25},{2,26},{3,27},{4,28},{5,29},{6,30},{7,31},{8,16},{9,... | collective-permute-start | bytes 393224 | tf_op jit(solution)/shard_map/ppermute | solution.py:341
  4.9 9.4 %collective-permute-start.1 = (bf16[2,4,64,128]{3,2,0,1:T(8,128)(2,1)S(1)}, bf16[2,4,64,128]{3,2,0,1:T(8,128)(2,1)S(1)}, u32[]{:S(2)}, u32[]{:S(2)}) collective-permute-start(bf16[2,4,64,128]{3,2,0,1:T(8,128)(2,1)S(1)} %copy.39), channel_id=1, source_target_pairs={{0,4},{1,5},{2,6},{3,7},{4,0},{5,1},{6,2},{7,3},{8,12},{9,13},{10,... | collective-permute-start | bytes 393224 | tf_op jit(solution)/shard_map/ppermute | solution.py:341
  6.2 24.0 %collective-permute-start = (bf16[9,3,64,512]{3,2,1,0:T(8,128)(2,1)S(1)}, bf16[9,3,64,512]{3,2,1,0:T(8,128)(2,1)S(1)}, u32[]{:S(2)}, u32[]{:S(2)}) collective-permute-start(bf16[9,3,64,512]{3,2,1,0:T(8,128)(2,1)S(1)} %bitcast.68), channel_id=1, source_target_pairs={{0,4},{1,5},{2,6},{3,7},{4,0},{5,1},{6,2},{7,3},{8,12},{9,13},{10,... | collective-permute-start | bytes 5308424 | tf_op jit(solution)/shard_map/ppermute | solution.py:341
  6.9 5.4 %copy-start.8 = (bf16[2,4,64,128]{3,2,0,1:T(8,128)(2,1)}, bf16[2,4,64,128]{3,2,0,1:T(8,128)(2,1)S(1)}, u32[]{:S(2)}) copy-start(bf16[2,4,64,128]{3,2,0,1:T(8,128)(2,1)S(1)} %collective-permute-done.2) | copy-start | bytes 393220
  6.9 8.0 %collective-permute-start.3 = (bf16[2,4,64,128]{3,2,0,1:T(8,128)(2,1)S(1)}, bf16[2,4,64,128]{3,2,0,1:T(8,128)(2,1)S(1)}, u32[]{:S(2)}, u32[]{:S(2)}) collective-permute-start(bf16[2,4,64,128]{3,2,0,1:T(8,128)(2,1)S(1)} %collective-permute-done.2), channel_id=1, source_target_pairs={{0,4},{1,5},{2,6},{3,7},{4,0},{5,1},{6,2},{7,3},{8,12},{9,13},{10,... | collective-permute-start | bytes 393224 | tf_op jit(solution)/shard_map/ppermute | solution.py:341
  8.3 6.6 %copy-start.9 = (bf16[2,4,64,128]{3,2,0,1:T(8,128)(2,1)}, bf16[2,4,64,128]{3,2,0,1:T(8,128)(2,1)S(1)}, u32[]{:S(2)}) copy-start(bf16[2,4,64,128]{3,2,0,1:T(8,128)(2,1)S(1)} %collective-permute-done.4) | copy-start | bytes 393220
  8.3 7.3 %collective-permute-start.5 = (bf16[2,4,64,128]{3,2,0,1:T(8,128)(2,1)S(1)}, bf16[2,4,64,128]{3,2,0,1:T(8,128)(2,1)S(1)}, u32[]{:S(2)}, u32[]{:S(2)}) collective-permute-start(bf16[2,4,64,128]{3,2,0,1:T(8,128)(2,1)S(1)} %collective-permute-done.4), channel_id=1, source_target_pairs={{0,4},{1,5},{2,6},{3,7},{4,0},{5,1},{6,2},{7,3},{8,12},{9,13},{10,... | collective-permute-start | bytes 393224 | tf_op jit(solution)/shard_map/ppermute | solution.py:341
  12.2 3.3 %copy-start.10 = (bf16[2,4,64,128]{3,2,0,1:T(8,128)(2,1)}, bf16[2,4,64,128]{3,2,0,1:T(8,128)(2,1)S(1)}, u32[]{:S(2)}) copy-start(bf16[2,4,64,128]{3,2,0,1:T(8,128)(2,1)S(1)} %collective-permute-done.6) | copy-start | bytes 393220
  12.2 4.0 %collective-permute-start.7 = (bf16[2,4,64,128]{3,2,0,1:T(8,128)(2,1)S(1)}, bf16[2,4,64,128]{3,2,0,1:T(8,128)(2,1)S(1)}, u32[]{:S(2)}, u32[]{:S(2)}) collective-permute-start(bf16[2,4,64,128]{3,2,0,1:T(8,128)(2,1)S(1)} %collective-permute-done.6), channel_id=1, source_target_pairs={{0,4},{1,5},{2,6},{3,7},{4,0},{5,1},{6,2},{7,3},{8,12},{9,13},{10,... | collective-permute-start | bytes 393224 | tf_op jit(solution)/shard_map/ppermute | solution.py:341
  14.2 2.0 %copy-start.11 = (bf16[2,4,64,128]{3,2,0,1:T(8,128)(2,1)}, bf16[2,4,64,128]{3,2,0,1:T(8,128)(2,1)S(1)}, u32[]{:S(2)}) copy-start(bf16[2,4,64,128]{3,2,0,1:T(8,128)(2,1)S(1)} %collective-permute-done.1) | copy-start | bytes 393220
  14.9 1.4 %copy-start.12 = (bf16[2,4,64,128]{3,2,0,1:T(8,128)(2,1)}, bf16[2,4,64,128]{3,2,0,1:T(8,128)(2,1)S(1)}, u32[]{:S(2)}) copy-start(bf16[2,4,64,128]{3,2,0,1:T(8,128)(2,1)S(1)} %collective-permute-done.3) | copy-start | bytes 393220
  15.5 0.7 copy-start.13
  16.2 0.7 copy-start.14
  16.9 11.7 %collective-permute-start.12 = (bf16[8,2,64,128]{3,2,1,0:T(8,128)(2,1)}, bf16[8,2,64,128]{3,2,1,0:T(8,128)(2,1)}, u32[]{:S(2)}, u32[]{:S(2)}) collective-permute-start(bf16[8,2,64,128]{3,2,1,0:T(8,128)(2,1)} %get-tuple-element.32), channel_id=1, source_target_pairs={{0,1},{1,2},{2,3},{4,5},{5,6},{6,7},{8,9},{9,10},{10,11},{12,13},{... | collective-permute-start | bytes 786440 | tf_op jit(solution)/shard_map/ppermute | solution.py:341
  20.8 9.3 %collective-permute-start.13 = (bf16[8,2,64,128]{3,2,1,0:T(8,128)(2,1)}, bf16[8,2,64,128]{3,2,1,0:T(8,128)(2,1)}, u32[]{:S(2)}, u32[]{:S(2)}) collective-permute-start(bf16[8,2,64,128]{3,2,1,0:T(8,128)(2,1)} %get-tuple-element.31), channel_id=1, source_target_pairs={{1,0},{2,1},{3,2},{5,4},{6,5},{7,6},{9,8},{10,9},{11,10},{13,12},{... | collective-permute-start | bytes 786440 | tf_op jit(solution)/shard_map/ppermute | solution.py:341
  22.2 27.1 %copy-start.3 = (s32[3]{0:T(128)}, s32[3]{0:T(128)S(1)}, u32[]{:S(2)}) copy-start(s32[3]{0:T(128)S(1)} %pad_add_fusion.refs_0_.meta) | copy-start | bytes 40
  35.1 10.0 %collective-permute-start.14 = (bf16[256,512]{1,0:T(8,128)(2,1)S(1)}, bf16[256,512]{1,0:T(8,128)(2,1)S(1)}, u32[]{:S(2)}, u32[]{:S(2)}) collective-permute-start(bf16[256,512]{1,0:T(8,128)(2,1)S(1)} %get-tuple-element.19), channel_id=1, source_target_pairs={{0,24},{1,25},{2,26},{3,27},{4,28},{5,29},{6,30},{7,31},{8,16},{9,... | collective-permute-start | bytes 786440 | tf_op jit(solution)/shard_map/ppermute | solution.py:341
  36.4 15.3 %collective-permute-start.15 = (bf16[256,512]{1,0:T(8,128)(2,1)S(1)}, bf16[256,512]{1,0:T(8,128)(2,1)S(1)}, u32[]{:S(2)}, u32[]{:S(2)}) collective-permute-start(bf16[256,512]{1,0:T(8,128)(2,1)S(1)} %get-tuple-element.20), channel_id=1, source_target_pairs={{0,16},{1,17},{2,18},{3,19},{4,20},{5,21},{6,22},{7,23},{8,24},{9,... | collective-permute-start | bytes 786440 | tf_op jit(solution)/shard_map/ppermute | solution.py:341
  37.6 14.1 %collective-permute-start.16 = (bf16[256,512]{1,0:T(8,128)(2,1)S(1)}, bf16[256,512]{1,0:T(8,128)(2,1)S(1)}, u32[]{:S(2)}, u32[]{:S(2)}) collective-permute-start(bf16[256,512]{1,0:T(8,128)(2,1)S(1)} %get-tuple-element.21), channel_id=1, source_target_pairs={{0,8},{1,9},{2,10},{3,11},{4,12},{5,13},{6,14},{7,15},{8,0},{9,1},... | collective-permute-start | bytes 786440 | tf_op jit(solution)/shard_map/ppermute | solution.py:341
  41.2 17.9 %collective-permute-start.10 = (bf16[256,512]{1,0:T(8,128)(2,1)S(1)}, bf16[256,512]{1,0:T(8,128)(2,1)S(1)}, u32[]{:S(2)}, u32[]{:S(2)}) collective-permute-start(bf16[256,512]{1,0:T(8,128)(2,1)S(1)} %get-tuple-element.17), channel_id=1, source_target_pairs={{0,8},{1,9},{2,10},{3,11},{4,12},{5,13},{6,14},{7,15},{8,0},{9,1},... | collective-permute-start | bytes 786440 | tf_op jit(solution)/shard_map/ppermute | solution.py:341
  42.5 3.8 %copy-start.2 = (bf16[2,4,64,128]{3,2,1,0:T(8,128)(2,1)S(1)}, bf16[2,4,64,128]{3,2,1,0:T(8,128)(2,1)}, u32[]{:S(2)}) copy-start(bf16[2,4,64,128]{3,2,1,0:T(8,128)(2,1)} %copy-done.1) | copy-start | bytes 393220
  42.5 16.6 %collective-permute-start.9 = (bf16[256,512]{1,0:T(8,128)(2,1)S(1)}, bf16[256,512]{1,0:T(8,128)(2,1)S(1)}, u32[]{:S(2)}, u32[]{:S(2)}) collective-permute-start(bf16[256,512]{1,0:T(8,128)(2,1)S(1)} %get-tuple-element.16), channel_id=1, source_target_pairs={{0,16},{1,17},{2,18},{3,19},{4,20},{5,21},{6,22},{7,23},{8,24},{9,... | collective-permute-start | bytes 786440 | tf_op jit(solution)/shard_map/ppermute | solution.py:341
  45.1 14.1 %collective-permute-start.8 = (bf16[256,512]{1,0:T(8,128)(2,1)S(1)}, bf16[256,512]{1,0:T(8,128)(2,1)S(1)}, u32[]{:S(2)}, u32[]{:S(2)}) collective-permute-start(bf16[256,512]{1,0:T(8,128)(2,1)S(1)} %conv_inner.4), channel_id=1, source_target_pairs={{0,24},{1,25},{2,26},{3,27},{4,28},{5,29},{6,30},{7,31},{8,16},{9,... | collective-permute-start | bytes 786440 | tf_op jit(solution)/shard_map/ppermute | solution.py:341
  51.6 21.5 %copy-start.4 = (bf16[512,512]{1,0:T(8,128)(2,1)S(1)}, bf16[512,512]{1,0:T(8,128)(2,1)}, u32[]{:S(2)}) copy-start(bf16[512,512]{1,0:T(8,128)(2,1)} %refs_8_.1) | copy-start | bytes 1572868
  51.6 21.5 %copy-start.5 = (bf16[512,512]{1,0:T(8,128)(2,1)S(1)}, bf16[512,512]{1,0:T(8,128)(2,1)}, u32[]{:S(2)}) copy-start(bf16[512,512]{1,0:T(8,128)(2,1)} %refs_9_.1) | copy-start | bytes 1572868
  51.6 21.5 %copy-start.6 = (bf16[512,512]{1,0:T(8,128)(2,1)S(1)}, bf16[512,512]{1,0:T(8,128)(2,1)}, u32[]{:S(2)}) copy-start(bf16[512,512]{1,0:T(8,128)(2,1)} %refs_10_.1) | copy-start | bytes 1572868
  51.6 21.5 %copy-start.7 = (bf16[512,512]{1,0:T(8,128)(2,1)S(1)}, bf16[512,512]{1,0:T(8,128)(2,1)}, u32[]{:S(2)}) copy-start(bf16[512,512]{1,0:T(8,128)(2,1)} %refs_11_.1) | copy-start | bytes 1572868
  51.8 14.7 %collective-permute-start.17 = (bf16[128,512]{1,0:T(8,128)(2,1)S(1)}, bf16[128,512]{1,0:T(8,128)(2,1)S(1)}, u32[]{:S(2)}, u32[]{:S(2)}) collective-permute-start(bf16[128,512]{1,0:T(8,128)(2,1)S(1)} %get-tuple-element.22), channel_id=1, source_target_pairs={{0,0},{1,1},{2,4},{3,5},{4,2},{5,3},{6,6},{7,7},{8,8},{9,9},{10,12... | collective-permute-start | bytes 393224 | tf_op jit(solution)/shard_map/ppermute | solution.py:341
  58.7 7.8 %collective-permute-start.19 = (bf16[128,512]{1,0:T(8,128)(2,1)S(1)}, bf16[128,512]{1,0:T(8,128)(2,1)S(1)}, u32[]{:S(2)}, u32[]{:S(2)}) collective-permute-start(bf16[128,512]{1,0:T(8,128)(2,1)S(1)} %get-tuple-element.24), channel_id=1, source_target_pairs={{0,1},{1,0},{2,5},{3,4},{4,3},{5,2},{6,7},{7,6},{8,9},{9,8},{10,13... | collective-permute-start | bytes 393224 | tf_op jit(solution)/shard_map/ppermute | solution.py:341
  59.3 10.0 %collective-permute-start.11 = (bf16[128,512]{1,0:T(8,128)(2,1)S(1)}, bf16[128,512]{1,0:T(8,128)(2,1)S(1)}, u32[]{:S(2)}, u32[]{:S(2)}) collective-permute-start(bf16[128,512]{1,0:T(8,128)(2,1)S(1)} %get-tuple-element.18), channel_id=1, source_target_pairs={{0,0},{1,1},{2,4},{3,5},{4,2},{5,3},{6,6},{7,7},{8,8},{9,9},{10,12... | collective-permute-start | bytes 393224 | tf_op jit(solution)/shard_map/ppermute | solution.py:341
  65.4 6.4 %collective-permute-start.18 = (bf16[128,512]{1,0:T(8,128)(2,1)S(1)}, bf16[128,512]{1,0:T(8,128)(2,1)S(1)}, u32[]{:S(2)}, u32[]{:S(2)}) collective-permute-start(bf16[128,512]{1,0:T(8,128)(2,1)S(1)} %get-tuple-element.23), channel_id=1, source_target_pairs={{0,1},{1,0},{2,5},{3,4},{4,3},{5,2},{6,7},{7,6},{8,9},{9,8},{10,13... | collective-permute-start | bytes 393224 | tf_op jit(solution)/shard_map/ppermute | solution.py:341
  66.5 5.3 %collective-permute-start.21 = (bf16[128,512]{1,0:T(8,128)(2,1)S(1)}, bf16[128,512]{1,0:T(8,128)(2,1)S(1)}, u32[]{:S(2)}, u32[]{:S(2)}) collective-permute-start(bf16[128,512]{1,0:T(8,128)(2,1)S(1)} %collective-permute-done.17.refs_1_), channel_id=1, source_target_pairs={{0,4},{1,5},{2,6},{3,7},{4,0},{5,1},{6,2},{7,3},{8,12},{9,13},{10,... | collective-permute-start | bytes 393224 | tf_op jit(solution)/shard_map/ppermute | solution.py:341
  66.5 5.3 %collective-permute-start.23 = (bf16[128,512]{1,0:T(8,128)(2,1)S(1)}, bf16[128,512]{1,0:T(8,128)(2,1)S(1)}, u32[]{:S(2)}, u32[]{:S(2)}) collective-permute-start(bf16[128,512]{1,0:T(8,128)(2,1)S(1)} %collective-permute-done.19.refs_3_), channel_id=1, source_target_pairs={{0,4},{1,5},{2,6},{3,7},{4,0},{5,1},{6,2},{7,3},{8,12},{9,13},{10,... | collective-permute-start | bytes 393224 | tf_op jit(solution)/shard_map/ppermute | solution.py:341
  69.3 2.5 %collective-permute-start.20 = (bf16[128,512]{1,0:T(8,128)(2,1)S(1)}, bf16[128,512]{1,0:T(8,128)(2,1)S(1)}, u32[]{:S(2)}, u32[]{:S(2)}) collective-permute-start(bf16[128,512]{1,0:T(8,128)(2,1)S(1)} %collective-permute-done.11.refs_0_), channel_id=1, source_target_pairs={{0,4},{1,5},{2,6},{3,7},{4,0},{5,1},{6,2},{7,3},{8,12},{9,13},{10,... | collective-permute-start | bytes 393224 | tf_op jit(solution)/shard_map/ppermute | solution.py:341
  71.8 1.3 %collective-permute-start.22 = (bf16[128,512]{1,0:T(8,128)(2,1)S(1)}, bf16[128,512]{1,0:T(8,128)(2,1)S(1)}, u32[]{:S(2)}, u32[]{:S(2)}) collective-permute-start(bf16[128,512]{1,0:T(8,128)(2,1)S(1)} %collective-permute-done.18.refs_2_), channel_id=1, source_target_pairs={{0,4},{1,5},{2,6},{3,7},{4,0},{5,1},{6,2},{7,3},{8,12},{9,13},{10,... | collective-permute-start | bytes 393224 | tf_op jit(solution)/shard_map/ppermute | solution.py:341
  79.1 14.5 %collective-permute-start.24 = (bf16[4,64,512]{2,1,0:T(8,128)(2,1)S(1)}, bf16[4,64,512]{2,1,0:T(8,128)(2,1)S(1)}, u32[]{:S(2)}, u32[]{:S(2)}) collective-permute-start(bf16[4,64,512]{2,1,0:T(8,128)(2,1)S(1)} %get-tuple-element.25), channel_id=1, source_target_pairs={{0,0},{1,1},{4,2},{5,3},{2,4},{3,5},{6,6},{7,7},{8,8},{9,9},{12,10... | collective-permute-start | bytes 786440 | tf_op jit(solution)/shard_map/ppermute | solution.py:410
  83.9 9.7 %collective-permute-start.25 = (bf16[4,64,512]{2,1,0:T(8,128)(2,1)S(1)}, bf16[4,64,512]{2,1,0:T(8,128)(2,1)S(1)}, u32[]{:S(2)}, u32[]{:S(2)}) collective-permute-start(bf16[4,64,512]{2,1,0:T(8,128)(2,1)S(1)} %get-tuple-element.26), channel_id=1, source_target_pairs={{1,0},{0,1},{5,2},{4,3},{3,4},{2,5},{7,6},{6,7},{9,8},{8,9},{13,10... | collective-permute-start | bytes 786440 | tf_op jit(solution)/shard_map/ppermute | solution.py:410
  93.6 0.7 copy-start.15
  94.3 0.7 copy-start.16

commit v3 on v2

--- a/solution.py
+++ b/solution.py
@@ -14,7 +14,7 @@
 epsilon = 1e-06
 
 BOTH = ("tm", "rows")
-VMEM_LIMIT = 48 * 1024 * 1024
+VMEM_LIMIT = 32 * 1024 * 1024
 
 
 def everywhere(sizes, target):
@@ -32,134 +32,157 @@
     return [pl.BlockSpec(memory_space=pltpu.VMEM)] * count
 
 
-def conv_kernel(dests, parts, group, rim, out_type, frames, *refs):
-    meta = refs[0]
-    weight_refs = refs[1 : 1 + group]
-    refs = refs[1 + group :]
-    held, refs = refs[: len(dests)], refs[len(dests) :]
-    before, refs = refs[:parts], refs[parts:]
-    if rim:
-        (above, below), refs = refs[:2], refs[2:]
-    outs, (weights, raw, sems) = refs[: len(dests)], refs[len(dests) :]
-    part, member, z = meta[0], meta[1], meta[2]
-    lags = weights.shape[0]
-    width, chans = weights.shape[2:]
-    chans_here = width // group
-    _, rows_here, columns, _ = held[0].shape
-
+def merge_kernel(group, *refs):
+    meta, refs = refs[0], refs[1:]
+    slices, out, sems = refs[:group], refs[group], refs[group + 1]
+    chans_here = slices[0].shape[2]
     copies = []
-    for lag in range(lags):
+    for lag in range(out.shape[0]):
         for step in range(group):
-            owner = lax.rem(member - step + group, group)
+            owner = lax.rem(meta[1] - step + group, group)
+            rows = pl.ds(pl.multiple_of(owner * chans_here, 16), chans_here)
             copies.append(
                 pltpu.make_async_copy(
-                    weight_refs[step].at[:, lag],
-                    weights.at[lag, :, pl.ds(pl.multiple_of(owner * chans_here, 16), chans_here)],
-                    sems.at[lag, step],
+                    slices[step].at[:, lag], out.at[lag, :, rows], sems.at[lag, step]
                 )
             )
     for copy in copies:
         copy.start()
-
-    skip = 1 if rim else 0
+    for copy in copies:
+        copy.wait()
+
+
+def merge_call(meta, slices):
+    group = len(slices)
+    taps, lags, chans_here, chans = slices[0].shape
+    return pl.pallas_call(
+        functools.partial(merge_kernel, group),
+        out_shape=jax.ShapeDtypeStruct((lags, taps, group * chans_here, chans), jnp.bfloat16),
+        in_specs=[pl.BlockSpec(memory_space=pltpu.SMEM)]
+        + [pl.BlockSpec(memory_space=pl.ANY)] * group,
+        out_specs=pl.BlockSpec(memory_space=pltpu.VMEM),
+        scratch_shapes=[pltpu.SemaphoreType.DMA((lags, group))],
+        compiler_params=pltpu.CompilerParams(vmem_limit_bytes=VMEM_LIMIT),
+        name="merge_kernel_slices",
+    )(meta, *slices)
+
+
+def halo_call(pieces, after):
+    frames, rows_here, columns, width = pieces[0].shape
+    out = jax.ShapeDtypeStruct((len(pieces), frames, columns, width), jnp.bfloat16)
+
+    def kernel(*refs):
+        first, last = refs[-2:]
+        for i in range(len(pieces)):
+            first[i] = refs[i][:, 0]
+            last[i] = refs[i][:, rows_here - 1]
+
+    return pl.pallas_call(
+        kernel,
+        out_shape=[out] * 2,
+        in_specs=in_vmem(len(pieces)) + [pl.BlockSpec(memory_space=pl.ANY)],
+        out_specs=in_vmem(2),
+        compiler_params=pltpu.CompilerParams(vmem_limit_bytes=VMEM_LIMIT),
+        name="halo_rows",
+    )(*pieces, after)
+
+
+def conv_kernel(jobs, parts, frames, *refs):
+    meta, weights, refs = refs[0], refs[1], refs[2:]
+    dests = sorted({s for s, _ in jobs})
+    any_rim = any(rim for _, rim in jobs)
+    held, refs = refs[: len(dests)], refs[len(dests) :]
+    before, refs = refs[:parts], refs[parts:]
+    if any_rim:
+        (above, below), refs = refs[:2], refs[2:]
+    outs, raw = refs[-1 - len(jobs) : -1], refs[-1]
+    part, member, z = meta[0], meta[1], meta[2]
+    lags, _, width, chans = weights.shape
+    _, rows_here, columns, _ = held[0].shape
+
     for n, s in enumerate(dests):
         to = lax.bitwise_xor(part, s)
         wraps = member == 0
         place = jnp.where(wraps, lax.bitwise_xor(part, jnp.maximum(to - 1, 0)), s)
         valid = jnp.logical_or(jnp.logical_not(wraps), to > 0)
-        raw[n, frames:, skip : skip + rows_here] = held[n][...]
-        if rim:
+        raw[n, frames:, 1 : 1 + rows_here] = held[n][...]
+        if any_rim:
             raw[n, frames:, 0] = above[s]
-            raw[n, frames:, skip + rows_here] = below[s]
+            raw[n, frames:, 1 + rows_here] = below[s]
             raw[n, :frames, 0] = above[parts + place]
-            raw[n, :frames, skip + rows_here] = below[parts + place]
+            raw[n, :frames, 1 + rows_here] = below[parts + place]
         for i in range(parts):
 
             @pl.when(place == i)
             def _():
-                raw[n, :frames, skip : skip + rows_here] = before[i][...]
+                raw[n, :frames, 1 : 1 + rows_here] = before[i][...]
 
         @pl.when(jnp.logical_not(valid))
         def _():
             raw[n, :frames] = jnp.zeros_like(raw[n, :frames])
 
     side = 3
-    count = outs[0].shape[0]
+
+    def patches(a, b):
+        pieces = []
+        for s, rim in jobs:
+            n = dests.index(s)
+            for p in range(frames):
+                f = lax.rem(z + p, frames) + a
+                if rim:
+                    pieces.append(raw[n, f, b])
+                    pieces.append(raw[n, f, rows_here - 1 + b])
+                else:
+                    pieces.append(raw[n, f, 1 + b : b + rows_here - 1].reshape(-1, width))
+        return jnp.concatenate(pieces, axis=0)
+
+    lhs = jnp.concatenate([patches(a, b) for a in range(side) for b in range(side)], axis=1)
+    count = lhs.shape[0]
     column = lax.broadcasted_iota(jnp.int32, (count, chans), 0) % columns
-
-    def patches(n):
-        whole = []
-        for a in range(side):
-            for b in range(side):
-                pieces = []
-                for p in range(frames):
-                    f = lax.rem(z + p, frames) + a
-                    if rim:
-                        pieces.append(raw[n, f, b])
-                        pieces.append(raw[n, f, rows_here - 1 + b])
-                    else:
-                        inner = raw[n, f, b : b + rows_here - 2]
-                        pieces.append(inner.reshape(-1, width))
-                whole.append(jnp.concatenate(pieces, axis=0))
-        return jnp.concatenate(whole, axis=1)
-
-    for n in range(len(dests)):
-        lhs = patches(n)
-        total = None
-        for lag in (1, 0, 2):
-            if n == 0:
-                for step in range(group):
-                    copies[lag * group + step].wait()
-            product = jnp.dot(
-                lhs,
-                weights[lag].reshape(-1, chans),
-                preferred_element_type=jnp.float32,
-            )
-            if lag == 1:
-                total = product
-            elif lag == 0:
-                moved = pltpu.roll(product, 1, 0)
-                total = total + jnp.where(column == 0, 0.0, moved)
-            else:
-                moved = pltpu.roll(product, count - 1, 0)
-                total = total + jnp.where(column == columns - 1, 0.0, moved)
-        outs[n][...] = total.astype(out_type)
-
-
-def conv_call(dests, meta, weights, held, before, halos, frames, out_type):
-    group, parts = len(weights), len(held)
+    total = None
+    for lag in (1, 0, 2):
+        product = jnp.dot(
+            lhs, weights[lag].reshape(-1, chans), preferred_element_type=jnp.float32
+        )
+        if lag == 1:
+            total = product
+        elif lag == 0:
+            total = total + jnp.where(column == 0, 0.0, pltpu.roll(product, 1, 0))
+        else:
+            moved = pltpu.roll(product, count - 1, 0)
+            total = total + jnp.where(column == columns - 1, 0.0, moved)
+    place = 0
+    for out in outs:
+        out[...] = total[place : place + out.shape[0]].astype(out.dtype)
+        place += out.shape[0]
+
+
+def conv_call(jobs, meta, weights, held, before, halos, frames, out_type, after=()):
+    parts = len(held)
+    dests = sorted({s for s, _ in jobs})
     _, rows_here, columns, width = held[0].shape
-    taps, _, _, chans = weights[0].shape
-    lags = weights[0].shape[1]
-    rim = halos is not None
-    rows = 2 if rim else rows_here - 2
-    count = frames * rows * columns
-    out = jax.ShapeDtypeStruct((count, chans), out_type)
-    operands = [meta, *weights, *[held[s] for s in dests], *before, *(halos or ())]
-    specs = [pl.BlockSpec(memory_space=pltpu.SMEM)]
-    specs += [pl.BlockSpec(memory_space=pl.ANY)] * group
-    specs += in_vmem(len(operands) - 1 - group)
-    return pl.pallas_call(
-        functools.partial(conv_kernel, dests, parts, group, rim, out_type, frames),
-        out_shape=[out] * len(dests),
+    lags, taps, _, chans = weights.shape
+    any_rim = any(rim for _, rim in jobs)
+    counts = [frames * (2 if rim else rows_here - 2) * columns for _, rim in jobs]
+    operands = [weights, *[held[s] for s in dests], *before, *(halos if any_rim else ())]
+    specs = [pl.BlockSpec(memory_space=pltpu.SMEM)] + in_vmem(len(operands))
+    specs += [pl.BlockSpec(memory_space=pl.ANY)] * len(after)
+    return pl.pallas_call(
+        functools.partial(conv_kernel, tuple(jobs), parts, frames),
+        out_shape=[jax.ShapeDtypeStruct((count, chans), out_type) for count in counts],
         in_specs=specs,
-        out_specs=in_vmem(len(dests)),
+        out_specs=in_vmem(len(jobs)),
         scratch_shapes=[
-            pltpu.VMEM((lags, taps, width, chans), jnp.bfloat16),
-            pltpu.VMEM(
-                (len(dests), 2 * frames, rows_here + (2 if rim else 0), columns, width),
-                jnp.bfloat16,
-            ),
-            pltpu.SemaphoreType.DMA((lags, group)),
+            pltpu.VMEM((len(dests), 2 * frames, rows_here + 2, columns, width), jnp.bfloat16)
         ],
         compiler_params=pltpu.CompilerParams(vmem_limit_bytes=VMEM_LIMIT),
         cost_estimate=pl.CostEstimate(
-            flops=2 * len(dests) * count * taps * lags * width * chans,
+            flops=2 * sum(counts) * taps * lags * width * chans,
             bytes_accessed=2 * taps * lags * width * chans,
             transcendentals=0,
         ),
-        name="conv_rim" if rim else "conv_inner",
-    )(*operands)
+        name="conv_rim" if any_rim else "conv_inner",
+    )(meta, *operands, *after)
 
 
 def sum_call(pieces, frames):
@@ -314,12 +337,11 @@
 
 def place_call(meta, parts):
     frames = len(parts)
-    anywhere = pl.BlockSpec(memory_space=pl.ANY)
     return pl.pallas_call(
         place_kernel,
         out_shape=jax.ShapeDtypeStruct((frames, *parts[0].shape), parts[0].dtype),
-        in_specs=[pl.BlockSpec(memory_space=pltpu.SMEM)] + [anywhere] * frames,
-        out_specs=anywhere,
+        in_specs=[pl.BlockSpec(memory_space=pltpu.SMEM)] + in_vmem(frames),
+        out_specs=pl.BlockSpec(memory_space=pl.ANY),
         scratch_shapes=[pltpu.SemaphoreType.DMA((frames,))],
         name="place_frames",
     )(meta, *parts)
@@ -354,27 +376,26 @@
         before[s] = permute(held[s], to_member(1))
 
     split = conv_weight.reshape(taps // 3, 3, chans_here, chans)
-    weights = [split] + [permute(split, to_member(step)) for step in range(1, group)]
-
-    last = jnp.stack([x[:, rows_here - 1] for x in (*held, *before)])
-    first = jnp.stack([x[:, 0] for x in (*held, *before)])
+    slices = [split] + [permute(split, to_member(step)) for step in range(1, group)]
+    weights = merge_call(meta, slices)
+
+    away = list(reversed(range(1, parts)))
+    conv = functools.partial(
+        conv_call, meta=meta, weights=weights, held=held, before=before, frames=frames
+    )
+    inner = conv([(s, False) for s in away[:1]], halos=None, out_type=jnp.bfloat16)
+    first, last = halo_call([*held, *before], inner[0])
     halos = (
         permute(last, lambda t, z: (t, z + 1) if z + 1 < depth else None),
         permute(first, lambda t, z: (t, z - 1) if z else None),
     )
-
-    away = list(reversed(range(1, parts)))
+    inner += conv([(s, False) for s in away[1:]], halos=None, out_type=jnp.bfloat16)
+    rim = conv([(s, True) for s in away], halos=halos, out_type=jnp.bfloat16, after=inner[-1:])
+    mine = conv([(0, False), (0, True)], halos=halos, out_type=jnp.float32, after=rim[-1:])
     sums = []
-    for halo in (None, halos):
-        call = functools.partial(conv_call, meta=meta, weights=weights, held=held, before=before)
-        call = functools.partial(call, halos=halo, frames=frames)
-        if halo is None:
-            sent = call(away[:1], out_type=jnp.bfloat16) + call(away[1:], out_type=jnp.bfloat16)
-        else:
-            sent = call(away, out_type=jnp.bfloat16)
+    for sent, own_part in ((inner, mine[0]), (rim, mine[1])):
         got = [permute(x, to_part(s)) for s, x in zip(away, sent)]
-        (mine,) = call([0], out_type=jnp.float32)
-        sums.append(sum_call([mine, *got], frames))
+        sums.append(sum_call([own_part, *got], frames))
 
     share = depth // frames
 

time: 114 us -> 85.1 us (0.75)
  Pallas kernels: 39.7 us -> 20.3 us
  local copies, waits for them, and re-layouts: 14.3 us -> 4.05 us
  waiting for transfers between devices: 17.1 us -> 25.1 us
  starting transfers between devices: 41.1 us -> 34.8 us
    pallas_call x1, Pallas kernels: 17.7 us -> 1.85 us  [place_call(): pl.pallas_call(place_kernel, out_shape=jax.ShapeDtypeStruct((frames, *par...]
    ppermute x24, waiting for transfers between devices: 7.68 us -> 15.7 us  [permute(): return lax.ppermute(block, BOTH, everywhere(sizes, target))]
    ppermute x24, starting transfers between devices: 36 us -> 29.5 us  [permute(): return lax.ppermute(block, BOTH, everywhere(sizes, target))]
    ppermute x7 -> x0, local copies, waits for them, and re-layouts: 6.4 us -> none  [permute(): return lax.ppermute(block, BOTH, everywhere(sizes, target))]
    pallas_call x5 -> x6, Pallas kernels: 15.9 us -> 12.2 us  [the longest x4 11.3 us: conv_call(): pl.pallas_call(functools.partial(conv_kernel, tuple(jobs), parts, frames)...]
    unnamed x45 -> x16, local copies, waits for them, and re-layouts: 6 us -> 2.9 us
  transfers between devices with their start and end apart: 26 -> 26, of which waited for: 5 -> 8; matrix products, arithmetic and copies ran while one was open for 10% -> 1% of each run, Pallas kernels for 10% -> 13%
where the time goes in v3:
time: 85.1 us; the launch traced here: 84.5 us
  starting transfers between devices  34.8 us (41%)
  waiting for transfers between devices  25.1 us (29%)
  Pallas kernels  20.3 us (24%)
  local copies, waits for them, and re-layouts  4.05 us (5%)
    ppermute x24, starting transfers between devices, permute(): return lax.ppermute(block, BOTH, everywhere(sizes, target))  29.5 us
    ppermute x24, waiting for transfers between devices, permute(): return lax.ppermute(block, BOTH, everywhere(sizes, target))  15.7 us
    pallas_call x4, Pallas kernels, conv_call(): pl.pallas_call(functools.partial(conv_kernel, tuple(jobs), parts, frames)...  11.3 us
    ppermute x2, waiting for transfers between devices, body(): back.append(lax.ppermute(done[p], BOTH, pairs))  9.43 us
    pallas_call x1, Pallas kernels, attend_call(): pl.pallas_call(functools.partial(attend_kernel, frames, share, chunks), o...  5.94 us
    ppermute x2, starting transfers between devices, body(): back.append(lax.ppermute(done[p], BOTH, pairs))  5.26 us
    unnamed x16, local copies, waits for them, and re-layouts  2.9 us
    pallas_call x1, Pallas kernels, place_call(): pl.pallas_call(place_kernel, out_shape=jax.ShapeDtypeStruct((frames, *par...  1.85 us
  transfers between devices with their start and end apart: 26, of which 8 were waited for; matrix products, arithmetic and copies ran while one was open for 1% of the time, Pallas kernels for 13%

profile of v3, /device:TPU:1, one launch (start us, length us, event | category | flops | bytes accessed | tf_op | source)
XLA Modules:
  0.0 84.5 jit_solution(10680612304209398915)
XLA Ops:
  0.0 0.1 collective-permute-start
  0.1 1.1 %constant_dynamic-slice_fusion = (bf16[2,4,64,128]{3,2,1,0:T(8,128)(2,1)S(1)}, bf16[2,4,64,128]{3,2,1,0:T(8,128)(2,1)S(1)}, bf16[2,4,64,128]{3,2,1,0:T(8,128)(2,1)S(1)}, bf16[2,4,64,128]{3,2,1,0:T(8,128)(2,1)S(1)}) fusion(bf16[2,4,64,512]{3,2,1,0:T(8,128)(2,1)} %param.6, s32[]{:T(128)S(6)} %select_n.28, s32[]{:T(128)S(6)} %select_n.26, s32[]{:T(128)S(6)} %select_n.25, ...), kind=kLoop, calls=%fused_computation | loop fusion | bytes 1048592 | tf_op jit(solution)/shard_map/dynamic_slice | solution.py:373
  1.2 3.7 %collective-permute-start.6 = (bf16[2,4,64,128]{3,2,1,0:T(8,128)(2,1)S(1)}, bf16[2,4,64,128]{3,2,1,0:T(8,128)(2,1)S(1)}, u32[]{:S(2)}, u32[]{:S(2)}) collective-permute-start(bf16[2,4,64,128]{3,2,1,0:T(8,128)(2,1)S(1)} %get-tuple-element.35), channel_id=1, source_target_pairs={{0,24},{1,25},{2,26},{3,27},{4,28},{5,29},{6,30},{7,31},{8,16},{9,... | collective-permute-start | bytes 393224 | tf_op jit(solution)/shard_map/ppermute | solution.py:363
  4.9 0.3 collective-permute-start.2
  5.2 0.1 collective-permute-start.4
  5.3 0.6 collective-permute-start.1
  5.8 2.9 %collective-permute-done.6.refs_2_.refs_3_.refs_4_ = bf16[2,4,64,128]{3,2,1,0:T(8,128)(2,1)S(1)} collective-permute-done((bf16[2,4,64,128]{3,2,1,0:T(8,128)(2,1)S(1)}, bf16[2,4,64,128]{3,2,1,0:T(8,128)(2,1)S(1)}, u32[]{:S(2)}, u32[]{:S(2)}) %collective-permute-start.6) | collective-permute-done | bytes 131104 | tf_op jit(solution)/shard_map/ppermute | solution.py:363
  8.8 0.8 collective-permute-start.7
  9.5 2.1 %collective-permute-done.2.refs_1_.refs_2_ = bf16[2,4,64,128]{3,2,1,0:T(8,128)(2,1)S(1)} collective-permute-done((bf16[2,4,64,128]{3,2,1,0:T(8,128)(2,1)S(1)}, bf16[2,4,64,128]{3,2,1,0:T(8,128)(2,1)S(1)}, u32[]{:S(2)}, u32[]{:S(2)}) %collective-permute-start.2) | collective-permute-done | bytes 131104 | tf_op jit(solution)/shard_map/ppermute | solution.py:363
  11.7 0.8 collective-permute-start.3
  12.4 0.0 collective-permute-done.4.refs_2_.refs_3_
  12.5 0.0 collective-permute-start.5
  12.5 0.1 pad_add_fusion.refs_0_.meta
  12.5 0.0 collective-permute-done.refs_2_
  12.5 1.5 %copy-done = bf16[27,64,512]{2,1,0:T(8,128)(2,1)S(1)} copy-done((bf16[27,64,512]{2,1,0:T(8,128)(2,1)S(1)}, bf16[27,64,512]{2,1,0:T(8,128)(2,1)}, u32[]{:S(2)}) %copy-start) | copy-done | bytes 1769496
  14.0 0.9 %merge_kernel_slices.1.refs_1_ = bf16[3,9,128,512]{3,2,1,0:T(8,128)(2,1)S(1)} custom-call(s32[3]{0:T(128)S(1)} %pad_add_fusion.refs_0_.meta, bf16[9,3,64,512]{3,2,1,0:T(8,128)(2,1)S(1)} %bitcast.5, bf16[9,3,64,512]{3,2,1,0:T(8,128)(2,1)S(1)} %collective-permute-done.refs_2_), custom_call_target="tpu_custom_call" | custom-call | tf_op jit(solution)/shard_map/merge_kernel_slices/pallas_call | solution.py:58
  14.9 0.0 collective-permute-done.1.refs_3_.refs_4_.refs_5_
  14.9 0.0 collective-permute-done.7.refs_6_.refs_7_.refs_8_
  14.9 0.0 collective-permute-done.3.refs_4_.refs_5_.refs_6_
  14.9 0.0 collective-permute-done.5.refs_5_.refs_6_.refs_7_
  14.9 1.8 %conv_inner.2.refs_8_ = bf16[256,512]{1,0:T(8,128)(2,1)S(1)} custom-call(s32[3]{0:T(128)S(1)} %pad_add_fusion.refs_0_.meta, bf16[3,9,128,512]{3,2,1,0:T(8,128)(2,1)S(1)} %merge_kernel_slices.1.refs_1_, bf16[2,4,64,128]{3,2,1,0:T(8,128)(2,1)S(1)} %collective-permute-done.6.refs_2_.refs_3_.refs_4_, ...), custom_call_target="tpu_custom_call" | custom-call | flops 905969664 | bytes 3538944 | tf_op jit(solution)/shard_map/conv_inner/pallas_call | solution.py:170
  16.8 3.2 %collective-permute-start.8 = (bf16[8,2,64,128]{3,2,1,0:T(8,128)(2,1)S(1)}, bf16[8,2,64,128]{3,2,1,0:T(8,128)(2,1)S(1)}, u32[]{:S(2)}, u32[]{:S(2)}) collective-permute-start(bf16[8,2,64,128]{3,2,1,0:T(8,128)(2,1)S(1)} %get-tuple-element.20), channel_id=1, source_target_pairs={{0,1},{1,2},{2,3},{4,5},{5,6},{6,7},{8,9},{9,10},{10,11},{12,13},{... | collective-permute-start | bytes 786440 | tf_op jit(solution)/shard_map/ppermute | solution.py:363
  20.0 1.3 %collective-permute-start.9 = (bf16[8,2,64,128]{3,2,1,0:T(8,128)(2,1)S(1)}, bf16[8,2,64,128]{3,2,1,0:T(8,128)(2,1)S(1)}, u32[]{:S(2)}, u32[]{:S(2)}) collective-permute-start(bf16[8,2,64,128]{3,2,1,0:T(8,128)(2,1)S(1)} %get-tuple-element.21), channel_id=1, source_target_pairs={{1,0},{2,1},{3,2},{5,4},{6,5},{7,6},{9,8},{10,9},{11,10},{13,12},{... | collective-permute-start | bytes 786440 | tf_op jit(solution)/shard_map/ppermute | solution.py:363
  21.3 2.1 %collective-permute-start.10 = (bf16[256,512]{1,0:T(8,128)(2,1)S(1)}, bf16[256,512]{1,0:T(8,128)(2,1)S(1)}, u32[]{:S(2)}, u32[]{:S(2)}) collective-permute-start(bf16[256,512]{1,0:T(8,128)(2,1)S(1)} %conv_inner.2.refs_8_), channel_id=1, source_target_pairs={{0,24},{1,25},{2,26},{3,27},{4,28},{5,29},{6,30},{7,31},{8,16},{9,... | collective-permute-start | bytes 786440 | tf_op jit(solution)/shard_map/ppermute | solution.py:363
  23.4 2.8 %conv_inner.3 = (bf16[256,512]{1,0:T(8,128)(2,1)S(1)}, bf16[256,512]{1,0:T(8,128)(2,1)S(1)}) custom-call(s32[3]{0:T(128)S(1)} %pad_add_fusion.refs_0_.meta, bf16[3,9,128,512]{3,2,1,0:T(8,128)(2,1)S(1)} %merge_kernel_slices.1.refs_1_, bf16[2,4,64,128]{3,2,1,0:T(8,128)(2,1)S(1)} %collective-permute-done.2.refs_1_.refs_2_, ...), custom_call_target="tpu_custom_call" | custom-call | flops 1811939328 | bytes 3538944 | tf_op jit(solution)/shard_map/conv_inner/pallas_call | solution.py:170
  26.3 0.4 collective-permute-start.11
  26.7 0.3 collective-permute-start.12
  26.9 0.0 collective-permute-done.8.refs_9_.refs_7_
  26.9 2.0 %collective-permute-done.9.refs_10_.refs_8_ = bf16[8,2,64,128]{3,2,1,0:T(8,128)(2,1)S(1)} collective-permute-done((bf16[8,2,64,128]{3,2,1,0:T(8,128)(2,1)S(1)}, bf16[8,2,64,128]{3,2,1,0:T(8,128)(2,1)S(1)}, u32[]{:S(2)}, u32[]{:S(2)}) %collective-permute-start.9) | collective-permute-done | bytes 262176 | tf_op jit(solution)/shard_map/ppermute | solution.py:363
  28.9 3.9 %conv_rim.2 = (bf16[256,512]{1,0:T(8,128)(2,1)S(1)}, bf16[256,512]{1,0:T(8,128)(2,1)S(1)}, bf16[256,512]{1,0:T(8,128)(2,1)S(1)}) custom-call(s32[3]{0:T(128)S(1)} %pad_add_fusion.refs_0_.meta, bf16[3,9,128,512]{3,2,1,0:T(8,128)(2,1)S(1)} %merge_kernel_slices.1.refs_1_, bf16[2,4,64,128]{3,2,1,0:T(8,128)(2,1)S(1)} %collective-permute-done.2.refs_1_.refs_2_, ...), custom_call_target="tpu_custom_call" | custom-call | flops 2717908992 | bytes 3538944 | tf_op jit(solution)/shard_map/conv_rim/pallas_call | solution.py:170
  32.8 2.7 %collective-permute-start.14 = (bf16[256,512]{1,0:T(8,128)(2,1)S(1)}, bf16[256,512]{1,0:T(8,128)(2,1)S(1)}, u32[]{:S(2)}, u32[]{:S(2)}) collective-permute-start(bf16[256,512]{1,0:T(8,128)(2,1)S(1)} %get-tuple-element.28), channel_id=1, source_target_pairs={{0,24},{1,25},{2,26},{3,27},{4,28},{5,29},{6,30},{7,31},{8,16},{9,... | collective-permute-start | bytes 786440 | tf_op jit(solution)/shard_map/ppermute | solution.py:363
  35.5 0.0 collective-permute-start.15
  35.5 0.0 collective-permute-done.10.refs_1_
  35.5 0.4 collective-permute-start.16
  35.9 2.8 %conv_rim.3 = (f32[256,512]{1,0:T(8,128)S(1)}, f32[256,512]{1,0:T(8,128)S(1)}) custom-call(s32[3]{0:T(128)S(1)} %pad_add_fusion.refs_0_.meta, bf16[3,9,128,512]{3,2,1,0:T(8,128)(2,1)S(1)} %merge_kernel_slices.1.refs_1_, bf16[2,4,64,128]{3,2,1,0:T(8,128)(2,1)S(1)} %get-tuple-element.37.refs_0_.refs_2_, ...), custom_call_target="tpu_custom_call" | custom-call | flops 1811939328 | bytes 3538944 | tf_op jit(solution)/shard_map/conv_rim/pallas_call | solution.py:170
  38.7 0.0 copy-start.2
  38.7 0.0 copy-start.3
  38.7 0.0 copy-start.4
  38.7 0.0 copy-start.5
  38.7 0.0 collective-permute-done.11.refs_2_
  38.7 0.1 sum_parts.2
  38.9 6.5 %collective-permute-start.13 = (bf16[128,512]{1,0:T(8,128)(2,1)S(1)}, bf16[128,512]{1,0:T(8,128)(2,1)S(1)}, u32[]{:S(2)}, u32[]{:S(2)}) collective-permute-start(bf16[128,512]{1,0:T(8,128)(2,1)S(1)} %get-tuple-element.26), channel_id=1, source_target_pairs={{0,0},{1,1},{2,4},{3,5},{4,2},{5,3},{6,6},{7,7},{8,8},{9,9},{10,12... | collective-permute-start | bytes 393224 | tf_op jit(solution)/shard_map/ppermute | solution.py:363
  45.4 0.1 collective-permute-start.18
  45.5 0.0 collective-permute-done.14.refs_1_
  45.5 2.4 %collective-permute-done.15.refs_2_ = bf16[256,512]{1,0:T(8,128)(2,1)S(1)} collective-permute-done((bf16[256,512]{1,0:T(8,128)(2,1)S(1)}, bf16[256,512]{1,0:T(8,128)(2,1)S(1)}, u32[]{:S(2)}, u32[]{:S(2)}) %collective-permute-start.15) | collective-permute-done | bytes 262176 | tf_op jit(solution)/shard_map/ppermute | solution.py:363
  47.9 0.0 collective-permute-done.16.refs_3_
  47.9 0.1 sum_parts.3
  48.0 4.9 %collective-permute-start.17 = (bf16[128,512]{1,0:T(8,128)(2,1)S(1)}, bf16[128,512]{1,0:T(8,128)(2,1)S(1)}, u32[]{:S(2)}, u32[]{:S(2)}) collective-permute-start(bf16[128,512]{1,0:T(8,128)(2,1)S(1)} %get-tuple-element.30), channel_id=1, source_target_pairs={{0,0},{1,1},{2,4},{3,5},{4,2},{5,3},{6,6},{7,7},{8,8},{9,9},{10,12... | collective-permute-start | bytes 393224 | tf_op jit(solution)/shard_map/ppermute | solution.py:363
  52.9 1.0 %collective-permute-start.19 = (bf16[128,512]{1,0:T(8,128)(2,1)S(1)}, bf16[128,512]{1,0:T(8,128)(2,1)S(1)}, u32[]{:S(2)}, u32[]{:S(2)}) collective-permute-start(bf16[128,512]{1,0:T(8,128)(2,1)S(1)} %get-tuple-element.32), channel_id=1, source_target_pairs={{0,1},{1,0},{2,5},{3,4},{4,3},{5,2},{6,7},{7,6},{8,9},{9,8},{10,13... | collective-permute-start | bytes 393224 | tf_op jit(solution)/shard_map/ppermute | solution.py:363
  54.0 0.0 collective-permute-done.18.refs_2_
  54.0 0.5 collective-permute-start.22
  54.5 2.5 %collective-permute-done.17.refs_1_ = bf16[128,512]{1,0:T(8,128)(2,1)S(1)} collective-permute-done((bf16[128,512]{1,0:T(8,128)(2,1)S(1)}, bf16[128,512]{1,0:T(8,128)(2,1)S(1)}, u32[]{:S(2)}, u32[]{:S(2)}) %collective-permute-start.17) | collective-permute-done | bytes 131104 | tf_op jit(solution)/shard_map/ppermute | solution.py:363
  57.0 2.3 %collective-permute-done.19.refs_3_ = bf16[128,512]{1,0:T(8,128)(2,1)S(1)} collective-permute-done((bf16[128,512]{1,0:T(8,128)(2,1)S(1)}, bf16[128,512]{1,0:T(8,128)(2,1)S(1)}, u32[]{:S(2)}, u32[]{:S(2)}) %collective-permute-start.19) | collective-permute-done | bytes 131104 | tf_op jit(solution)/shard_map/ppermute | solution.py:363
  59.3 0.0 collective-permute-start.23
  59.3 0.0 collective-permute-done.20.refs_4_
  59.3 1.3 %collective-permute-done.23.refs_7_ = bf16[128,512]{1,0:T(8,128)(2,1)S(1)} collective-permute-done((bf16[128,512]{1,0:T(8,128)(2,1)S(1)}, bf16[128,512]{1,0:T(8,128)(2,1)S(1)}, u32[]{:S(2)}, u32[]{:S(2)}) %collective-permute-start.23) | collective-permute-done | bytes 131104 | tf_op jit(solution)/shard_map/ppermute | solution.py:363
  60.6 5.9 %attend.1 = (bf16[4,64,512]{2,1,0:T(8,128)(2,1)S(1)}, bf16[4,64,512]{2,1,0:T(8,128)(2,1)S(1)}) custom-call(bf16[128,512]{1,0:T(8,128)(2,1)S(1)} %collective-permute-done.13.refs_0_, bf16[128,512]{1,0:T(8,128)(2,1)S(1)} %collective-permute-done.17.refs_1_, bf16[128,512]{1,0:T(8,128)(2,1)S(1)} %collective-permute-done.18.refs_2_, ...), custom_call_target="tpu_custom_call" | custom-call | flops 2684354560 | bytes 3145728 | tf_op jit(solution)/shard_map/attend/pallas_call | solution.py:309
  66.6 5.0 %collective-permute-start.24 = (bf16[4,64,512]{2,1,0:T(8,128)(2,1)S(1)}, bf16[4,64,512]{2,1,0:T(8,128)(2,1)S(1)}, u32[]{:S(2)}, u32[]{:S(2)}) collective-permute-start(bf16[4,64,512]{2,1,0:T(8,128)(2,1)S(1)} %get-tuple-element.33), channel_id=1, source_target_pairs={{0,0},{1,1},{4,2},{5,3},{2,4},{3,5},{6,6},{7,7},{8,8},{9,9},{12,10... | collective-permute-start | bytes 786440 | tf_op jit(solution)/shard_map/ppermute | solution.py:431
  71.6 0.2 collective-permute-start.25
  71.9 9.4 %collective-permute-done.24.refs_0_ = bf16[4,64,512]{2,1,0:T(8,128)(2,1)S(1)} collective-permute-done((bf16[4,64,512]{2,1,0:T(8,128)(2,1)S(1)}, bf16[4,64,512]{2,1,0:T(8,128)(2,1)S(1)}, u32[]{:S(2)}, u32[]{:S(2)}) %collective-permute-start.24) | collective-permute-done | bytes 262176 | tf_op jit(solution)/shard_map/ppermute | solution.py:431
  81.3 0.0 collective-permute-done.25.refs_1_
  81.3 0.7 copy-done.6
  82.0 0.7 copy-done.7
  82.7 1.8 %place_frames.1 = bf16[2,4,64,512]{3,2,1,0:T(8,128)(2,1)} custom-call(s32[3]{0:T(128)} %copy-done.1, bf16[4,64,512]{2,1,0:T(8,128)(2,1)} %copy-done.6, bf16[4,64,512]{2,1,0:T(8,128)(2,1)} %copy-done.7), custom_call_target="tpu_custom_call" | custom-call | tf_op jit(solution)/shard_map/place_frames/pallas_call | solution.py:340
  (16 shorter events, 0.1 us)
Async XLA Ops:
  0.0 12.5 %collective-permute-start = (bf16[9,3,64,512]{3,2,1,0:T(8,128)(2,1)}, bf16[9,3,64,512]{3,2,1,0:T(8,128)(2,1)S(1)}, u32[]{:S(2)}, u32[]{:S(2)}) collective-permute-start(bf16[9,3,64,512]{3,2,1,0:T(8,128)(2,1)} %bitcast.4), channel_id=1, source_target_pairs={{0,4},{1,5},{2,6},{3,7},{4,0},{5,1},{6,2},{7,3},{8,12},{9,13},{10,... | collective-permute-start | bytes 5308424 | tf_op jit(solution)/shard_map/ppermute | solution.py:363
  1.2 7.6 %collective-permute-start.6 = (bf16[2,4,64,128]{3,2,1,0:T(8,128)(2,1)S(1)}, bf16[2,4,64,128]{3,2,1,0:T(8,128)(2,1)S(1)}, u32[]{:S(2)}, u32[]{:S(2)}) collective-permute-start(bf16[2,4,64,128]{3,2,1,0:T(8,128)(2,1)S(1)} %get-tuple-element.35), channel_id=1, source_target_pairs={{0,24},{1,25},{2,26},{3,27},{4,28},{5,29},{6,30},{7,31},{8,16},{9,... | collective-permute-start | bytes 393224 | tf_op jit(solution)/shard_map/ppermute | solution.py:363
  4.9 6.8 %collective-permute-start.2 = (bf16[2,4,64,128]{3,2,1,0:T(8,128)(2,1)S(1)}, bf16[2,4,64,128]{3,2,1,0:T(8,128)(2,1)S(1)}, u32[]{:S(2)}, u32[]{:S(2)}) collective-permute-start(bf16[2,4,64,128]{3,2,1,0:T(8,128)(2,1)S(1)} %get-tuple-element.36), channel_id=1, source_target_pairs={{0,8},{1,9},{2,10},{3,11},{4,12},{5,13},{6,14},{7,15},{8,0},{9,1},... | collective-permute-start | bytes 393224 | tf_op jit(solution)/shard_map/ppermute | solution.py:363
  5.2 7.3 %collective-permute-start.4 = (bf16[2,4,64,128]{3,2,1,0:T(8,128)(2,1)S(1)}, bf16[2,4,64,128]{3,2,1,0:T(8,128)(2,1)S(1)}, u32[]{:S(2)}, u32[]{:S(2)}) collective-permute-start(bf16[2,4,64,128]{3,2,1,0:T(8,128)(2,1)S(1)} %get-tuple-element.38), channel_id=1, source_target_pairs={{0,16},{1,17},{2,18},{3,19},{4,20},{5,21},{6,22},{7,23},{8,24},{9,... | collective-permute-start | bytes 393224 | tf_op jit(solution)/shard_map/ppermute | solution.py:363
  5.3 9.6 %collective-permute-start.1 = (bf16[2,4,64,128]{3,2,1,0:T(8,128)(2,1)S(1)}, bf16[2,4,64,128]{3,2,1,0:T(8,128)(2,1)S(1)}, u32[]{:S(2)}, u32[]{:S(2)}) collective-permute-start(bf16[2,4,64,128]{3,2,1,0:T(8,128)(2,1)S(1)} %get-tuple-element.37.refs_0_.refs_2_), channel_id=1, source_target_pairs={{0,4},{1,5},{2,6},{3,7},{4,0},{5,1},{6,2},{7,3},{8,12},{9,13},{10,... | collective-permute-start | bytes 393224 | tf_op jit(solution)/shard_map/ppermute | solution.py:363
  8.8 6.1 %collective-permute-start.7 = (bf16[2,4,64,128]{3,2,1,0:T(8,128)(2,1)S(1)}, bf16[2,4,64,128]{3,2,1,0:T(8,128)(2,1)S(1)}, u32[]{:S(2)}, u32[]{:S(2)}) collective-permute-start(bf16[2,4,64,128]{3,2,1,0:T(8,128)(2,1)S(1)} %collective-permute-done.6.refs_2_.refs_3_.refs_4_), channel_id=1, source_target_pairs={{0,4},{1,5},{2,6},{3,7},{4,0},{5,1},{6,2},{7,3},{8,12},{9,13},{10,... | collective-permute-start | bytes 393224 | tf_op jit(solution)/shard_map/ppermute | solution.py:363
  11.7 3.2 %collective-permute-start.3 = (bf16[2,4,64,128]{3,2,1,0:T(8,128)(2,1)S(1)}, bf16[2,4,64,128]{3,2,1,0:T(8,128)(2,1)S(1)}, u32[]{:S(2)}, u32[]{:S(2)}) collective-permute-start(bf16[2,4,64,128]{3,2,1,0:T(8,128)(2,1)S(1)} %collective-permute-done.2.refs_1_.refs_2_), channel_id=1, source_target_pairs={{0,4},{1,5},{2,6},{3,7},{4,0},{5,1},{6,2},{7,3},{8,12},{9,13},{10,... | collective-permute-start | bytes 393224 | tf_op jit(solution)/shard_map/ppermute | solution.py:363
  12.5 2.5 %collective-permute-start.5 = (bf16[2,4,64,128]{3,2,1,0:T(8,128)(2,1)S(1)}, bf16[2,4,64,128]{3,2,1,0:T(8,128)(2,1)S(1)}, u32[]{:S(2)}, u32[]{:S(2)}) collective-permute-start(bf16[2,4,64,128]{3,2,1,0:T(8,128)(2,1)S(1)} %collective-permute-done.4.refs_2_.refs_3_), channel_id=1, source_target_pairs={{0,4},{1,5},{2,6},{3,7},{4,0},{5,1},{6,2},{7,3},{8,12},{9,13},{10,... | collective-permute-start | bytes 393224 | tf_op jit(solution)/shard_map/ppermute | solution.py:363
  12.5 23.3 %copy-start.1 = (s32[3]{0:T(128)}, s32[3]{0:T(128)S(1)}, u32[]{:S(2)}) copy-start(s32[3]{0:T(128)S(1)} %pad_add_fusion.refs_0_.meta) | copy-start | bytes 40
  12.5 1.5 %copy-start = (bf16[27,64,512]{2,1,0:T(8,128)(2,1)S(1)}, bf16[27,64,512]{2,1,0:T(8,128)(2,1)}, u32[]{:S(2)}) copy-start(bf16[27,64,512]{2,1,0:T(8,128)(2,1)} %param.7) | copy-start | bytes 5308420
  16.8 10.1 %collective-permute-start.8 = (bf16[8,2,64,128]{3,2,1,0:T(8,128)(2,1)S(1)}, bf16[8,2,64,128]{3,2,1,0:T(8,128)(2,1)S(1)}, u32[]{:S(2)}, u32[]{:S(2)}) collective-permute-start(bf16[8,2,64,128]{3,2,1,0:T(8,128)(2,1)S(1)} %get-tuple-element.20), channel_id=1, source_target_pairs={{0,1},{1,2},{2,3},{4,5},{5,6},{6,7},{8,9},{9,10},{10,11},{12,13},{... | collective-permute-start | bytes 786440 | tf_op jit(solution)/shard_map/ppermute | solution.py:363
  20.0 8.9 %collective-permute-start.9 = (bf16[8,2,64,128]{3,2,1,0:T(8,128)(2,1)S(1)}, bf16[8,2,64,128]{3,2,1,0:T(8,128)(2,1)S(1)}, u32[]{:S(2)}, u32[]{:S(2)}) collective-permute-start(bf16[8,2,64,128]{3,2,1,0:T(8,128)(2,1)S(1)} %get-tuple-element.21), channel_id=1, source_target_pairs={{1,0},{2,1},{3,2},{5,4},{6,5},{7,6},{9,8},{10,9},{11,10},{13,12},{... | collective-permute-start | bytes 786440 | tf_op jit(solution)/shard_map/ppermute | solution.py:363
  21.3 14.2 %collective-permute-start.10 = (bf16[256,512]{1,0:T(8,128)(2,1)S(1)}, bf16[256,512]{1,0:T(8,128)(2,1)S(1)}, u32[]{:S(2)}, u32[]{:S(2)}) collective-permute-start(bf16[256,512]{1,0:T(8,128)(2,1)S(1)} %conv_inner.2.refs_8_), channel_id=1, source_target_pairs={{0,24},{1,25},{2,26},{3,27},{4,28},{5,29},{6,30},{7,31},{8,16},{9,... | collective-permute-start | bytes 786440 | tf_op jit(solution)/shard_map/ppermute | solution.py:363
  26.3 12.5 %collective-permute-start.11 = (bf16[256,512]{1,0:T(8,128)(2,1)S(1)}, bf16[256,512]{1,0:T(8,128)(2,1)S(1)}, u32[]{:S(2)}, u32[]{:S(2)}) collective-permute-start(bf16[256,512]{1,0:T(8,128)(2,1)S(1)} %get-tuple-element.25), channel_id=1, source_target_pairs={{0,16},{1,17},{2,18},{3,19},{4,20},{5,21},{6,22},{7,23},{8,24},{9,... | collective-permute-start | bytes 786440 | tf_op jit(solution)/shard_map/ppermute | solution.py:363
  26.7 12.1 %collective-permute-start.12 = (bf16[256,512]{1,0:T(8,128)(2,1)S(1)}, bf16[256,512]{1,0:T(8,128)(2,1)S(1)}, u32[]{:S(2)}, u32[]{:S(2)}) collective-permute-start(bf16[256,512]{1,0:T(8,128)(2,1)S(1)} %get-tuple-element.22.refs_11_), channel_id=1, source_target_pairs={{0,8},{1,9},{2,10},{3,11},{4,12},{5,13},{6,14},{7,15},{8,0},{9,1},... | collective-permute-start | bytes 786440 | tf_op jit(solution)/shard_map/ppermute | solution.py:363
  32.8 12.6 %collective-permute-start.14 = (bf16[256,512]{1,0:T(8,128)(2,1)S(1)}, bf16[256,512]{1,0:T(8,128)(2,1)S(1)}, u32[]{:S(2)}, u32[]{:S(2)}) collective-permute-start(bf16[256,512]{1,0:T(8,128)(2,1)S(1)} %get-tuple-element.28), channel_id=1, source_target_pairs={{0,24},{1,25},{2,26},{3,27},{4,28},{5,29},{6,30},{7,31},{8,16},{9,... | collective-permute-start | bytes 786440 | tf_op jit(solution)/shard_map/ppermute | solution.py:363
  35.5 12.4 %collective-permute-start.15 = (bf16[256,512]{1,0:T(8,128)(2,1)S(1)}, bf16[256,512]{1,0:T(8,128)(2,1)S(1)}, u32[]{:S(2)}, u32[]{:S(2)}) collective-permute-start(bf16[256,512]{1,0:T(8,128)(2,1)S(1)} %get-tuple-element.29), channel_id=1, source_target_pairs={{0,16},{1,17},{2,18},{3,19},{4,20},{5,21},{6,22},{7,23},{8,24},{9,... | collective-permute-start | bytes 786440 | tf_op jit(solution)/shard_map/ppermute | solution.py:363
  35.5 12.4 %collective-permute-start.16 = (bf16[256,512]{1,0:T(8,128)(2,1)S(1)}, bf16[256,512]{1,0:T(8,128)(2,1)S(1)}, u32[]{:S(2)}, u32[]{:S(2)}) collective-permute-start(bf16[256,512]{1,0:T(8,128)(2,1)S(1)} %get-tuple-element.23.refs_9_), channel_id=1, source_target_pairs={{0,8},{1,9},{2,10},{3,11},{4,12},{5,13},{6,14},{7,15},{8,0},{9,1},... | collective-permute-start | bytes 786440 | tf_op jit(solution)/shard_map/ppermute | solution.py:363
  38.7 22.0 %copy-start.2 = (bf16[512,512]{1,0:T(8,128)(2,1)S(1)}, bf16[512,512]{1,0:T(8,128)(2,1)}, u32[]{:S(2)}) copy-start(bf16[512,512]{1,0:T(8,128)(2,1)} %refs_8_.1) | copy-start | bytes 1572868
  38.7 21.9 %copy-start.3 = (bf16[512,512]{1,0:T(8,128)(2,1)S(1)}, bf16[512,512]{1,0:T(8,128)(2,1)}, u32[]{:S(2)}) copy-start(bf16[512,512]{1,0:T(8,128)(2,1)} %refs_9_.1) | copy-start | bytes 1572868
  38.7 21.9 %copy-start.4 = (bf16[512,512]{1,0:T(8,128)(2,1)S(1)}, bf16[512,512]{1,0:T(8,128)(2,1)}, u32[]{:S(2)}) copy-start(bf16[512,512]{1,0:T(8,128)(2,1)} %refs_10_.1) | copy-start | bytes 1572868
  38.7 21.9 %copy-start.5 = (bf16[512,512]{1,0:T(8,128)(2,1)S(1)}, bf16[512,512]{1,0:T(8,128)(2,1)}, u32[]{:S(2)}) copy-start(bf16[512,512]{1,0:T(8,128)(2,1)} %refs_11_.1) | copy-start | bytes 1572868
  38.9 15.1 %collective-permute-start.13 = (bf16[128,512]{1,0:T(8,128)(2,1)S(1)}, bf16[128,512]{1,0:T(8,128)(2,1)S(1)}, u32[]{:S(2)}, u32[]{:S(2)}) collective-permute-start(bf16[128,512]{1,0:T(8,128)(2,1)S(1)} %get-tuple-element.26), channel_id=1, source_target_pairs={{0,0},{1,1},{2,4},{3,5},{4,2},{5,3},{6,6},{7,7},{8,8},{9,9},{10,12... | collective-permute-start | bytes 393224 | tf_op jit(solution)/shard_map/ppermute | solution.py:363
  45.4 8.6 %collective-permute-start.18 = (bf16[128,512]{1,0:T(8,128)(2,1)S(1)}, bf16[128,512]{1,0:T(8,128)(2,1)S(1)}, u32[]{:S(2)}, u32[]{:S(2)}) collective-permute-start(bf16[128,512]{1,0:T(8,128)(2,1)S(1)} %get-tuple-element.31), channel_id=1, source_target_pairs={{0,1},{1,0},{2,5},{3,4},{4,3},{5,2},{6,7},{7,6},{8,9},{9,8},{10,13... | collective-permute-start | bytes 393224 | tf_op jit(solution)/shard_map/ppermute | solution.py:363
  48.0 8.9 %collective-permute-start.17 = (bf16[128,512]{1,0:T(8,128)(2,1)S(1)}, bf16[128,512]{1,0:T(8,128)(2,1)S(1)}, u32[]{:S(2)}, u32[]{:S(2)}) collective-permute-start(bf16[128,512]{1,0:T(8,128)(2,1)S(1)} %get-tuple-element.30), channel_id=1, source_target_pairs={{0,0},{1,1},{2,4},{3,5},{4,2},{5,3},{6,6},{7,7},{8,8},{9,9},{10,12... | collective-permute-start | bytes 393224 | tf_op jit(solution)/shard_map/ppermute | solution.py:363
  52.9 6.4 %collective-permute-start.19 = (bf16[128,512]{1,0:T(8,128)(2,1)S(1)}, bf16[128,512]{1,0:T(8,128)(2,1)S(1)}, u32[]{:S(2)}, u32[]{:S(2)}) collective-permute-start(bf16[128,512]{1,0:T(8,128)(2,1)S(1)} %get-tuple-element.32), channel_id=1, source_target_pairs={{0,1},{1,0},{2,5},{3,4},{4,3},{5,2},{6,7},{7,6},{8,9},{9,8},{10,13... | collective-permute-start | bytes 393224 | tf_op jit(solution)/shard_map/ppermute | solution.py:363
  54.0 5.3 %collective-permute-start.20 = (bf16[128,512]{1,0:T(8,128)(2,1)S(1)}, bf16[128,512]{1,0:T(8,128)(2,1)S(1)}, u32[]{:S(2)}, u32[]{:S(2)}) collective-permute-start(bf16[128,512]{1,0:T(8,128)(2,1)S(1)} %collective-permute-done.13.refs_0_), channel_id=1, source_target_pairs={{0,4},{1,5},{2,6},{3,7},{4,0},{5,1},{6,2},{7,3},{8,12},{9,13},{10,... | collective-permute-start | bytes 393224 | tf_op jit(solution)/shard_map/ppermute | solution.py:363
  54.0 5.3 %collective-permute-start.22 = (bf16[128,512]{1,0:T(8,128)(2,1)S(1)}, bf16[128,512]{1,0:T(8,128)(2,1)S(1)}, u32[]{:S(2)}, u32[]{:S(2)}) collective-permute-start(bf16[128,512]{1,0:T(8,128)(2,1)S(1)} %collective-permute-done.18.refs_2_), channel_id=1, source_target_pairs={{0,4},{1,5},{2,6},{3,7},{4,0},{5,1},{6,2},{7,3},{8,12},{9,13},{10,... | collective-permute-start | bytes 393224 | tf_op jit(solution)/shard_map/ppermute | solution.py:363
  57.0 2.3 %collective-permute-start.21 = (bf16[128,512]{1,0:T(8,128)(2,1)S(1)}, bf16[128,512]{1,0:T(8,128)(2,1)S(1)}, u32[]{:S(2)}, u32[]{:S(2)}) collective-permute-start(bf16[128,512]{1,0:T(8,128)(2,1)S(1)} %collective-permute-done.17.refs_1_), channel_id=1, source_target_pairs={{0,4},{1,5},{2,6},{3,7},{4,0},{5,1},{6,2},{7,3},{8,12},{9,13},{10,... | collective-permute-start | bytes 393224 | tf_op jit(solution)/shard_map/ppermute | solution.py:363
  59.3 1.3 %collective-permute-start.23 = (bf16[128,512]{1,0:T(8,128)(2,1)S(1)}, bf16[128,512]{1,0:T(8,128)(2,1)S(1)}, u32[]{:S(2)}, u32[]{:S(2)}) collective-permute-start(bf16[128,512]{1,0:T(8,128)(2,1)S(1)} %collective-permute-done.19.refs_3_), channel_id=1, source_target_pairs={{0,4},{1,5},{2,6},{3,7},{4,0},{5,1},{6,2},{7,3},{8,12},{9,13},{10,... | collective-permute-start | bytes 393224 | tf_op jit(solution)/shard_map/ppermute | solution.py:363
  66.6 14.7 %collective-permute-start.24 = (bf16[4,64,512]{2,1,0:T(8,128)(2,1)S(1)}, bf16[4,64,512]{2,1,0:T(8,128)(2,1)S(1)}, u32[]{:S(2)}, u32[]{:S(2)}) collective-permute-start(bf16[4,64,512]{2,1,0:T(8,128)(2,1)S(1)} %get-tuple-element.33), channel_id=1, source_target_pairs={{0,0},{1,1},{4,2},{5,3},{2,4},{3,5},{6,6},{7,7},{8,8},{9,9},{12,10... | collective-permute-start | bytes 786440 | tf_op jit(solution)/shard_map/ppermute | solution.py:431
  71.6 9.7 %collective-permute-start.25 = (bf16[4,64,512]{2,1,0:T(8,128)(2,1)S(1)}, bf16[4,64,512]{2,1,0:T(8,128)(2,1)S(1)}, u32[]{:S(2)}, u32[]{:S(2)}) collective-permute-start(bf16[4,64,512]{2,1,0:T(8,128)(2,1)S(1)} %get-tuple-element.34), channel_id=1, source_target_pairs={{1,0},{0,1},{5,2},{4,3},{3,4},{2,5},{7,6},{6,7},{9,8},{8,9},{13,10... | collective-permute-start | bytes 786440 | tf_op jit(solution)/shard_map/ppermute | solution.py:431
  81.3 0.7 copy-start.6
  82.0 0.7 copy-start.7

commit v4 on v3

--- a/solution.py
+++ b/solution.py
@@ -67,50 +67,77 @@
     )(meta, *slices)
 
 
-def halo_call(pieces, after):
-    frames, rows_here, columns, width = pieces[0].shape
-    out = jax.ShapeDtypeStruct((len(pieces), frames, columns, width), jnp.bfloat16)
-
+def partner(member, place):
+    odd = member % 2 == 1
+    if isinstance(member, int) and isinstance(place, int):
+        return 3 - place if odd and place in (1, 2) else place
+    swapped = jnp.where(jnp.logical_or(place == 1, place == 2), 3 - place, place)
+    return jnp.where(odd, swapped, place)
+
+
+def split_call(meta, above, below, parts):
+    frames, columns, chans = above.shape
+    width = chans // parts
+
+    def kernel(meta, above, below, *outs):
+        for place, out in enumerate(outs):
+            to = lax.bitwise_xor(meta[0], partner(meta[1], jnp.int32(place)))
+            lanes = pl.ds(pl.multiple_of(to * width, width), width)
+            out[0] = above[:, :, lanes]
+            out[1] = below[:, :, lanes]
+
+    return pl.pallas_call(
+        kernel,
+        out_shape=[jax.ShapeDtypeStruct((2, frames, columns, width), above.dtype)] * parts,
+        in_specs=[pl.BlockSpec(memory_space=pltpu.SMEM)] + in_vmem(2),
+        out_specs=in_vmem(parts),
+        compiler_params=pltpu.CompilerParams(vmem_limit_bytes=VMEM_LIMIT),
+        name="split_halo_rows",
+    )(meta, above, below)
+
+
+def stack_call(pieces, after):
     def kernel(*refs):
-        first, last = refs[-2:]
         for i in range(len(pieces)):
-            first[i] = refs[i][:, 0]
-            last[i] = refs[i][:, rows_here - 1]
+            refs[-1][i] = refs[i][...]
 
     return pl.pallas_call(
         kernel,
-        out_shape=[out] * 2,
+        out_shape=jax.ShapeDtypeStruct((len(pieces), *pieces[0].shape), pieces[0].dtype),
         in_specs=in_vmem(len(pieces)) + [pl.BlockSpec(memory_space=pl.ANY)],
-        out_specs=in_vmem(2),
-        compiler_params=pltpu.CompilerParams(vmem_limit_bytes=VMEM_LIMIT),
-        name="halo_rows",
+        out_specs=pl.BlockSpec(memory_space=pltpu.VMEM),
+        compiler_params=pltpu.CompilerParams(vmem_limit_bytes=VMEM_LIMIT),
+        name="stack_halo_rows",
     )(*pieces, after)
 
 
-def conv_kernel(jobs, parts, frames, *refs):
+def conv_kernel(jobs, parts, group, frames, out_count, *refs):
     meta, weights, refs = refs[0], refs[1], refs[2:]
     dests = sorted({s for s, _ in jobs})
     any_rim = any(rim for _, rim in jobs)
     held, refs = refs[: len(dests)], refs[len(dests) :]
     before, refs = refs[:parts], refs[parts:]
     if any_rim:
-        (above, below), refs = refs[:2], refs[2:]
-    outs, raw = refs[-1 - len(jobs) : -1], refs[-1]
+        (rims, rims_before), refs = refs[:2], refs[2:]
+    outs, raw = refs[:-1], refs[-1]
+    outs = outs[len(outs) - out_count :]
     part, member, z = meta[0], meta[1], meta[2]
     lags, _, width, chans = weights.shape
     _, rows_here, columns, _ = held[0].shape
 
-    for n, s in enumerate(dests):
-        to = lax.bitwise_xor(part, s)
-        wraps = member == 0
-        place = jnp.where(wraps, lax.bitwise_xor(part, jnp.maximum(to - 1, 0)), s)
-        valid = jnp.logical_or(jnp.logical_not(wraps), to > 0)
+    first = member == 0
+    for n, where in enumerate(dests):
+        to = lax.bitwise_xor(part, partner(member, jnp.int32(where)))
+        valid = jnp.logical_or(jnp.logical_not(first), to > 0)
+        sender = jnp.where(first, group - 1, member - 1)
+        want = jnp.where(first, jnp.maximum(to - 1, 0), to)
+        place = partner(sender, lax.bitwise_xor(part, want))
         raw[n, frames:, 1 : 1 + rows_here] = held[n][...]
         if any_rim:
-            raw[n, frames:, 0] = above[s]
-            raw[n, frames:, 1 + rows_here] = below[s]
-            raw[n, :frames, 0] = above[parts + place]
-            raw[n, :frames, 1 + rows_here] = below[parts + place]
+            raw[n, frames:, 0] = rims[where, 0]
+            raw[n, frames:, 1 + rows_here] = rims[where, 1]
+            raw[n, :frames, 0] = rims_before[place, 0]
+            raw[n, :frames, 1 + rows_here] = rims_before[place, 1]
         for i in range(parts):
 
             @pl.when(place == i)
@@ -157,27 +184,32 @@
         place += out.shape[0]
 
 
-def conv_call(jobs, meta, weights, held, before, halos, frames, out_type, after=()):
+def conv_call(jobs, meta, weights, held, before, rims, group, frames, joined, after=()):
     parts = len(held)
-    dests = sorted({s for s, _ in jobs})
+    dests = sorted({place for place, _ in jobs})
     _, rows_here, columns, width = held[0].shape
     lags, taps, _, chans = weights.shape
     any_rim = any(rim for _, rim in jobs)
     counts = [frames * (2 if rim else rows_here - 2) * columns for _, rim in jobs]
-    operands = [weights, *[held[s] for s in dests], *before, *(halos if any_rim else ())]
+    total = sum(counts)
+    operands = [weights, *[held[n] for n in dests], *before, *(rims if any_rim else ())]
     specs = [pl.BlockSpec(memory_space=pltpu.SMEM)] + in_vmem(len(operands))
     specs += [pl.BlockSpec(memory_space=pl.ANY)] * len(after)
-    return pl.pallas_call(
-        functools.partial(conv_kernel, tuple(jobs), parts, frames),
-        out_shape=[jax.ShapeDtypeStruct((count, chans), out_type) for count in counts],
+    if joined:
+        outs = [jax.ShapeDtypeStruct((total, chans), jnp.bfloat16)]
+    else:
+        outs = [jax.ShapeDtypeStruct((count, chans), jnp.float32) for count in counts]
+    return pl.pallas_call(
+        functools.partial(conv_kernel, tuple(jobs), parts, group, frames, len(outs)),
+        out_shape=outs,
         in_specs=specs,
-        out_specs=in_vmem(len(jobs)),
+        out_specs=in_vmem(len(outs)),
         scratch_shapes=[
             pltpu.VMEM((len(dests), 2 * frames, rows_here + 2, columns, width), jnp.bfloat16)
         ],
         compiler_params=pltpu.CompilerParams(vmem_limit_bytes=VMEM_LIMIT),
         cost_estimate=pl.CostEstimate(
-            flops=2 * sum(counts) * taps * lags * width * chans,
+            flops=2 * total * taps * lags * width * chans,
             bytes_accessed=2 * taps * lags * width * chans,
             transcendentals=0,
         ),
@@ -185,27 +217,28 @@
     )(meta, *operands, *after)
 
 
-def sum_call(pieces, frames):
-    count, chans = pieces[0].shape
-    out = jax.ShapeDtypeStruct((count // frames, chans), jnp.bfloat16)
+def sum_call(pieces, splits, after=()):
+    count = pieces[0][0].shape[0]
+    chans = pieces[0][0].shape[1]
+    size = count // splits
+    out = jax.ShapeDtypeStruct((size, chans), jnp.bfloat16)
 
     def kernel(*refs):
-        ins, outs = refs[: len(pieces)], refs[len(pieces) :]
-        for p, out_ref in enumerate(outs):
-            size = out_ref.shape[0]
-            total = ins[0][pl.ds(p * size, size)].astype(jnp.float32)
-            for ref in ins[1:]:
-                total = total + ref[pl.ds(p * size, size)].astype(jnp.float32)
+        for p, out_ref in enumerate(refs[len(refs) - splits :]):
+            total = None
+            for (_, start), ref in zip(pieces, refs):
+                rows = ref[start + p * size : start + (p + 1) * size].astype(jnp.float32)
+                total = rows if total is None else total + rows
             out_ref[...] = total.astype(out_ref.dtype)
 
     return pl.pallas_call(
         kernel,
-        out_shape=[out] * frames,
-        in_specs=in_vmem(len(pieces)),
-        out_specs=in_vmem(frames),
+        out_shape=[out] * splits,
+        in_specs=in_vmem(len(pieces)) + [pl.BlockSpec(memory_space=pl.ANY)] * len(after),
+        out_specs=in_vmem(splits),
         compiler_params=pltpu.CompilerParams(vmem_limit_bytes=VMEM_LIMIT),
         name="sum_parts",
-    )(*pieces)
+    )(*[array for array, _ in pieces], *after)
 
 
 def attend_kernel(frames, share, chunks, *refs):
@@ -270,9 +303,9 @@
         ).astype(jnp.bfloat16)
 
     place = 0
-    for index in range(own_count):
-        ref = tokens[index]
-        rows = ref.shape[0]
+    for p, out in enumerate(outs):
+        mine = tokens[p * chunks : (p + 1) * chunks]
+        rows = sum(ref.shape[0] for ref in mine)
         queries = jnp.dot(
             normed[pl.ds(place, rows)], wq[...], preferred_element_type=jnp.float32
         ).astype(jnp.bfloat16)
@@ -285,17 +318,14 @@
         denominator = jnp.sum(exp_weights.astype(jnp.float32), axis=1, keepdims=True)
         numerator = jnp.dot(exp_weights, values[...], preferred_element_type=jnp.float32)
         attended = (numerator / denominator).astype(jnp.bfloat16)
-        summed = ref[...].astype(jnp.float32) + jnp.dot(
-            attended, wo[...], preferred_element_type=jnp.float32
-        )
-        summed = summed.astype(jnp.bfloat16)
-        out = outs[index // chunks]
+        added = jnp.dot(attended, wo[...], preferred_element_type=jnp.float32)
         rows_here, columns, _ = out.shape
-        if index % chunks == 0:
-            out[1 : rows_here - 1] = summed.reshape(rows_here - 2, columns, chans)
-        else:
-            out[0] = summed[:columns]
-            out[rows_here - 1] = summed[columns:]
+        inner = mine[0].shape[0]
+        first = mine[0][...].astype(jnp.float32) + added[:inner]
+        out[1 : rows_here - 1] = first.astype(jnp.bfloat16).reshape(rows_here - 2, columns, chans)
+        second = (mine[1][...].astype(jnp.float32) + added[inner:]).astype(jnp.bfloat16)
+        out[0] = second[:columns]
+        out[rows_here - 1] = second[columns:]
 
 
 def attend_call(own, others, weights, frames, rows_here, columns):
@@ -320,31 +350,6 @@
         ),
         name="attend",
     )(*operands)
-
-
-def place_kernel(meta, *refs):
-    parts, out, sems = refs[:-2], refs[-2], refs[-1]
-    frames = len(parts)
-    copies = [
-        pltpu.make_async_copy(ref, out.at[lax.rem(meta[2] + p, frames)], sems.at[p])
-        for p, ref in enumerate(parts)
-    ]
-    for copy in copies:
-        copy.start()
-    for copy in copies:
-        copy.wait()
-
-
-def place_call(meta, parts):
-    frames = len(parts)
-    return pl.pallas_call(
-        place_kernel,
-        out_shape=jax.ShapeDtypeStruct((frames, *parts[0].shape), parts[0].dtype),
-        in_specs=[pl.BlockSpec(memory_space=pltpu.SMEM)] + in_vmem(frames),
-        out_specs=pl.BlockSpec(memory_space=pl.ANY),
-        scratch_shapes=[pltpu.SemaphoreType.DMA((frames,))],
-        name="place_frames",
-    )(meta, *parts)
 
 
 def body(latents, conv_weight, query_weight, key_weight, value_weight, out_weight):
@@ -362,40 +367,60 @@
     def permute(block, target):
         return lax.ppermute(block, BOTH, everywhere(sizes, target))
 
-    def to_part(s):
-        return lambda t, z: ((t // group ^ s) * group + t % group, z)
+    def to_place(place):
+        return lambda t, z: ((t // group ^ partner(t % group, place)) * group + t % group, z)
 
     def to_member(step):
         return lambda t, z: (t // group * group + (t + step) % group, z)
-
-    held, before = [None] * parts, [None] * parts
-    for s in reversed(range(parts)):
-        piece = lax.dynamic_slice_in_dim(latents, (part ^ s) * width, width, axis=3)
-        held[s] = permute(piece, to_part(s)) if s else piece
-    for s in range(parts):
-        before[s] = permute(held[s], to_member(1))
 
     split = conv_weight.reshape(taps // 3, 3, chans_here, chans)
     slices = [split] + [permute(split, to_member(step)) for step in range(1, group)]
     weights = merge_call(meta, slices)
 
-    away = list(reversed(range(1, parts)))
+    above = permute(latents[:, -1], lambda t, z: (t, z + 1) if z + 1 < depth else None)
+    below = permute(latents[:, 0], lambda t, z: (t, z - 1) if z else None)
+
+    held, before = [None] * parts, [None] * parts
+    order = [0, 3, 1, 2]
+    for place in order:
+        start = (part ^ partner(member, jnp.int32(place))) * width
+        piece = lax.dynamic_slice_in_dim(latents, start, width, axis=3)
+        held[place] = permute(piece, to_place(place)) if place else piece
+    rims = split_call(meta, above, below, parts)
+    rims = [permute(x, to_place(place)) if place else x for place, x in enumerate(rims)]
+    held[2], weights = lax.optimization_barrier((held[2], weights))
+    for place in order:
+        before[place] = permute(held[place], to_member(1))
+
     conv = functools.partial(
-        conv_call, meta=meta, weights=weights, held=held, before=before, frames=frames
+        conv_call,
+        meta=meta,
+        weights=weights,
+        held=held,
+        before=before,
+        group=group,
+        frames=frames,
     )
-    inner = conv([(s, False) for s in away[:1]], halos=None, out_type=jnp.bfloat16)
-    first, last = halo_call([*held, *before], inner[0])
-    halos = (
-        permute(last, lambda t, z: (t, z + 1) if z + 1 < depth else None),
-        permute(first, lambda t, z: (t, z - 1) if z else None),
+
+    (inner_sent,) = conv([(1, False), (3, False)], rims=None, joined=True)
+    rims = stack_call(rims, inner_sent)
+    rims = (rims, permute(rims, to_member(1)))
+    (rim_sent,) = conv([(1, True), (3, True)], rims=rims, joined=True)
+    inner_got = permute(inner_sent, to_place(1))
+    rim_got = permute(rim_sent, to_place(1))
+    inner_on, inner_own = conv(
+        [(2, False), (0, False)], rims=None, joined=False, after=(rim_sent,)
     )
-    inner += conv([(s, False) for s in away[1:]], halos=None, out_type=jnp.bfloat16)
-    rim = conv([(s, True) for s in away], halos=halos, out_type=jnp.bfloat16, after=inner[-1:])
-    mine = conv([(0, False), (0, True)], halos=halos, out_type=jnp.float32, after=rim[-1:])
-    sums = []
-    for sent, own_part in ((inner, mine[0]), (rim, mine[1])):
-        got = [permute(x, to_part(s)) for s, x in zip(away, sent)]
-        sums.append(sum_call([own_part, *got], frames))
+    half = inner_on.shape[0]
+    (inner_relay,) = sum_call([(inner_on, 0), (inner_got, half)], 1)
+    rim_on, rim_own = conv([(2, True), (0, True)], rims=rims, joined=False, after=(inner_relay,))
+    (rim_relay,) = sum_call([(rim_on, 0), (rim_got, rim_on.shape[0])], 1)
+    inner_last = permute(inner_relay, to_place(2))
+    rim_last = permute(rim_relay, to_place(2))
+    sums = [
+        sum_call([(inner_own, 0), (inner_got, 0), (inner_last, 0)], frames, after=(rim_relay,)),
+        sum_call([(rim_own, 0), (rim_got, 0), (rim_last, 0)], frames),
+    ]
 
     share = depth // frames
 
@@ -429,7 +454,16 @@
     for p in range(frames):
         pairs = [(b, a) for a, b in everywhere(sizes, lambda t, z: frame_home(t, z, p))]
         back.append(lax.ppermute(done[p], BOTH, pairs))
-    return place_call(meta, back)
+    return jnp.stack(
+        [
+            functools.reduce(
+                lambda rest, p: jnp.where((z_index + p) % frames == f, back[p], rest),
+                range(1, frames),
+                back[0],
+            )
+            for f in range(frames)
+        ]
+    )
 
 
 def solution(mesh):

time: 85.1 us -> 83.1 us (0.976)
  Pallas kernels: 20.3 us -> 17.6 us
  waiting for transfers between devices: 25.1 us -> 26.5 us
  starting transfers between devices: 34.8 us -> 33.9 us
  other arithmetic: 0.08 us -> 0.96 us
    pallas_call x1, Pallas kernels: 5.94 us -> 4.45 us  [attend_call(): pl.pallas_call(functools.partial(attend_kernel, frames, share, chunks), o...]
    unnamed x16 -> x10, local copies, waits for them, and re-layouts: 2.9 us -> 1.5 us
    pallas_call x8 -> x10, Pallas kernels: 13.5 us -> 12.3 us  [the longest x4 11.4 us: conv_call(): pl.pallas_call(functools.partial(conv_kernel, tuple(jobs), parts, group,...]
    ppermute x2, waiting for transfers between devices: 9.43 us -> 10.5 us  [body(): back.append(lax.ppermute(done[p], BOTH, pairs))]
    ppermute x2, starting transfers between devices: 5.26 us -> 4.2 us  [body(): back.append(lax.ppermute(done[p], BOTH, pairs))]
    squeeze x0 -> x1, local copies, waits for them, and re-layouts: none -> 0.99 us  [body(): below = permute(latents[:, 0], lambda t, z: (t, z - 1) if z else None)]
    another operation x0 -> x2, other arithmetic: none -> 0.88 us  [body(): jnp.stack([functools.reduce(lambda rest, p: jnp.where((z_index + p) % fra...]
    ppermute x24 -> x26, waiting for transfers between devices: 15.7 us -> 15.9 us  [permute(): return lax.ppermute(block, BOTH, everywhere(sizes, target))]
  transfers between devices with their start and end apart: 26 -> 28, of which waited for: 8 -> 12; matrix products, arithmetic and copies ran while one was open for 1% -> 3% of each run, Pallas kernels for 13% -> 16%
where the time goes in v4:
time: 83.1 us; the launch traced here: 82.9 us
  starting transfers between devices  33.9 us (41%)
  waiting for transfers between devices  26.5 us (32%)
  Pallas kernels  17.6 us (21%)
  local copies, waits for them, and re-layouts  3.63 us (4%)
  other arithmetic  0.96 us (1%)
    ppermute x26, starting transfers between devices, permute(): return lax.ppermute(block, BOTH, everywhere(sizes, target))  29.7 us
    ppermute x26, waiting for transfers between devices, permute(): return lax.ppermute(block, BOTH, everywhere(sizes, target))  15.9 us
    pallas_call x4, Pallas kernels, conv_call(): pl.pallas_call(functools.partial(conv_kernel, tuple(jobs), parts, group,...  11.4 us
    ppermute x2, waiting for transfers between devices, body(): back.append(lax.ppermute(done[p], BOTH, pairs))  10.5 us
    pallas_call x1, Pallas kernels, attend_call(): pl.pallas_call(functools.partial(attend_kernel, frames, share, chunks), o...  4.45 us
    ppermute x2, starting transfers between devices, body(): back.append(lax.ppermute(done[p], BOTH, pairs))  4.2 us
  transfers between devices with their start and end apart: 28, of which 12 were waited for; matrix products, arithmetic and copies ran while one was open for 3% of the time, Pallas kernels for 16%

profile of v4, /device:TPU:1, one launch (start us, length us, event | category | flops | bytes accessed | tf_op | source)
XLA Modules:
  0.0 82.9 jit_solution(3861799189414315518)
XLA Ops:
  0.0 0.1 collective-permute-start.1
  0.1 1.1 %constant_dynamic-slice_fusion = (bf16[2,4,64,128]{3,2,1,0:T(8,128)(2,1)S(1)}, bf16[2,4,64,128]{3,2,1,0:T(8,128)(2,1)S(1)}, bf16[2,4,64,128]{3,2,1,0:T(8,128)(2,1)S(1)}, bf16[2,4,64,128]{3,2,1,0:T(8,128)(2,1)S(1)}) fusion(bf16[2,4,64,512]{3,2,1,0:T(8,128)(2,1)} %param.6, s32[]{:T(128)S(6)} %select_n.75, s32[]{:T(128)S(6)} %select_n.74, s32[]{:T(128)S(6)} %select_n.72, ...), kind=kLoop, calls=%fused_computation.5 | loop fusion | bytes 1048592 | tf_op jit(solution)/shard_map/dynamic_slice | solution.py:387
  1.2 2.7 %collective-permute-start = (bf16[2,4,64,128]{3,2,1,0:T(8,128)(2,1)S(1)}, bf16[2,4,64,128]{3,2,1,0:T(8,128)(2,1)S(1)}, u32[]{:S(2)}, u32[]{:S(2)}) collective-permute-start(bf16[2,4,64,128]{3,2,1,0:T(8,128)(2,1)S(1)} %get-tuple-element.44), channel_id=1, source_target_pairs={{0,16},{1,17},{2,18},{3,19},{4,12},{5,13},{6,14},{7,15},{8,24},{9,... | collective-permute-start | bytes 393224 | tf_op jit(solution)/shard_map/ppermute | solution.py:368
  3.9 1.2 %collective-permute-start.3 = (bf16[2,4,64,128]{3,2,1,0:T(8,128)(2,1)S(1)}, bf16[2,4,64,128]{3,2,1,0:T(8,128)(2,1)S(1)}, u32[]{:S(2)}, u32[]{:S(2)}) collective-permute-start(bf16[2,4,64,128]{3,2,1,0:T(8,128)(2,1)S(1)} %get-tuple-element.42), channel_id=1, source_target_pairs={{0,8},{1,9},{2,10},{3,11},{4,20},{5,21},{6,22},{7,23},{8,0},{9,1},... | collective-permute-start | bytes 393224 | tf_op jit(solution)/shard_map/ppermute | solution.py:368
  5.2 0.0 collective-permute-start.6
  5.2 1.0 %slice_bitcast_fusion = (bf16[2,64,512]{2,1,0:T(8,128)(2,1)S(1)}, bf16[2,64,512]{2,1,0:T(8,128)(2,1)S(1)}) fusion(bf16[2,4,64,512]{3,2,1,0:T(8,128)(2,1)} %param.6), kind=kLoop, calls=%fused_computation.3 | loop fusion | bytes 524288 | tf_op jit(solution)/shard_map/squeeze | solution.py:381
  6.2 3.4 %collective-permute-start.8 = (bf16[2,64,512]{2,1,0:T(8,128)(2,1)S(1)}, bf16[2,64,512]{2,1,0:T(8,128)(2,1)S(1)}, u32[]{:S(2)}, u32[]{:S(2)}) collective-permute-start(bf16[2,64,512]{2,1,0:T(8,128)(2,1)S(1)} %get-tuple-element.40), channel_id=1, source_target_pairs={{0,1},{1,2},{2,3},{4,5},{5,6},{6,7},{8,9},{9,10},{10,11},{12,13},{... | collective-permute-start | bytes 393224 | tf_op jit(solution)/shard_map/ppermute | solution.py:368
  9.6 0.1 pad_add_fusion.refs_0_.meta
  9.7 0.0 collective-permute-done.1.refs_2_
  9.7 1.3 %collective-permute-start.9 = (bf16[2,64,512]{2,1,0:T(8,128)(2,1)S(1)}, bf16[2,64,512]{2,1,0:T(8,128)(2,1)S(1)}, u32[]{:S(2)}, u32[]{:S(2)}) collective-permute-start(bf16[2,64,512]{2,1,0:T(8,128)(2,1)S(1)} %get-tuple-element.39), channel_id=1, source_target_pairs={{1,0},{2,1},{3,2},{5,4},{6,5},{7,6},{9,8},{10,9},{11,10},{13,12},{... | collective-permute-start | bytes 393224 | tf_op jit(solution)/shard_map/ppermute | solution.py:368
  11.0 0.0 copy-start
  11.0 1.5 %copy-done = bf16[27,64,512]{2,1,0:T(8,128)(2,1)S(1)} copy-done((bf16[27,64,512]{2,1,0:T(8,128)(2,1)S(1)}, bf16[27,64,512]{2,1,0:T(8,128)(2,1)}, u32[]{:S(2)}) %copy-start) | copy-done | bytes 1769496
  12.4 0.9 %merge_kernel_slices.1.refs_1_ = bf16[3,9,128,512]{3,2,1,0:T(8,128)(2,1)S(1)} custom-call(s32[3]{0:T(128)S(1)} %pad_add_fusion.refs_0_.meta, bf16[9,3,64,512]{3,2,1,0:T(8,128)(2,1)S(1)} %bitcast.17, bf16[9,3,64,512]{3,2,1,0:T(8,128)(2,1)S(1)} %collective-permute-done.1.refs_2_), custom_call_target="tpu_custom_call" | custom-call | tf_op jit(solution)/shard_map/merge_kernel_slices/pallas_call | solution.py:58
  13.3 0.0 collective-permute-done.refs_3_
  13.3 1.2 %collective-permute-start.2 = (bf16[2,4,64,128]{3,2,1,0:T(8,128)(2,1)S(1)}, bf16[2,4,64,128]{3,2,1,0:T(8,128)(2,1)S(1)}, u32[]{:S(2)}, u32[]{:S(2)}) collective-permute-start(bf16[2,4,64,128]{3,2,1,0:T(8,128)(2,1)S(1)} %get-tuple-element.43.refs_2_), channel_id=1, source_target_pairs={{0,4},{1,5},{2,6},{3,7},{4,0},{5,1},{6,2},{7,3},{8,12},{9,13},{10,... | collective-permute-start | bytes 393224 | tf_op jit(solution)/shard_map/ppermute | solution.py:368
  14.5 0.1 collective-permute-start.4
  14.6 0.0 collective-permute-done.6.refs_3_
  14.6 0.4 collective-permute-start.7
  15.0 0.1 collective-permute-start.5
  15.1 0.3 collective-permute-done.9.below
  15.4 0.6 split_halo_rows.1
  16.0 1.3 %collective-permute-start.10 = (bf16[2,2,64,128]{3,2,1,0:T(8,128)(2,1)S(1)}, bf16[2,2,64,128]{3,2,1,0:T(8,128)(2,1)S(1)}, u32[]{:S(2)}, u32[]{:S(2)}) collective-permute-start(bf16[2,2,64,128]{3,2,1,0:T(8,128)(2,1)S(1)} %get-tuple-element.24), channel_id=1, source_target_pairs={{0,8},{1,9},{2,10},{3,11},{4,20},{5,21},{6,22},{7,23},{8,0},{9,1},... | collective-permute-start | bytes 196616 | tf_op jit(solution)/shard_map/ppermute | solution.py:368
  17.3 1.2 %collective-permute-start.11 = (bf16[2,2,64,128]{3,2,1,0:T(8,128)(2,1)S(1)}, bf16[2,2,64,128]{3,2,1,0:T(8,128)(2,1)S(1)}, u32[]{:S(2)}, u32[]{:S(2)}) collective-permute-start(bf16[2,2,64,128]{3,2,1,0:T(8,128)(2,1)S(1)} %get-tuple-element.25), channel_id=1, source_target_pairs={{0,16},{1,17},{2,18},{3,19},{4,12},{5,13},{6,14},{7,15},{8,24},{9,... | collective-permute-start | bytes 196616 | tf_op jit(solution)/shard_map/ppermute | solution.py:368
  18.5 0.0 collective-permute-done.4.refs_5_
  18.5 0.2 collective-permute-start.12
  18.7 2.9 %conv_inner.2.refs_4_ = bf16[512,512]{1,0:T(8,128)(2,1)S(1)} custom-call(s32[3]{0:T(128)S(1)} %pad_add_fusion.refs_0_.meta, bf16[3,9,128,512]{3,2,1,0:T(8,128)(2,1)S(1)} %merge_kernel_slices.1.refs_1_, bf16[2,4,64,128]{3,2,1,0:T(8,128)(2,1)S(1)} %collective-permute-done.3.refs_2_, bf16[2,4,64,128]{3,2,1,0:T(8,128)(2,1)S(1)} %collective-permute-done.6.refs_3_, ...), custom_call_target="tpu_custom_call" | custom-call | flops 1811939328 | bytes 3538944 | tf_op jit(solution)/shard_map/conv_inner/pallas_call | solution.py:202
  21.6 0.0 collective-permute-done.11.refs_2_
  21.6 1.3 %collective-permute-done.12.refs_3_ = bf16[2,2,64,128]{3,2,1,0:T(8,128)(2,1)S(1)} collective-permute-done((bf16[2,2,64,128]{3,2,1,0:T(8,128)(2,1)S(1)}, bf16[2,2,64,128]{3,2,1,0:T(8,128)(2,1)S(1)}, u32[]{:S(2)}, u32[]{:S(2)}) %collective-permute-start.12) | collective-permute-done | bytes 65568 | tf_op jit(solution)/shard_map/ppermute | solution.py:368
  22.9 3.7 %collective-permute-start.13 = (bf16[4,2,2,64,128]{4,3,2,1,0:T(8,128)(2,1)S(1)}, bf16[4,2,2,64,128]{4,3,2,1,0:T(8,128)(2,1)S(1)}, u32[]{:S(2)}, u32[]{:S(2)}) collective-permute-start(bf16[4,2,2,64,128]{4,3,2,1,0:T(8,128)(2,1)S(1)} %stack_halo_rows.1.refs_8_), channel_id=1, source_target_pairs={{0,4},{1,5},{2,6},{3,7},{4,0},{5,1},{6,2},{7,3},{8,12},{9,13},{10,... | collective-permute-start | bytes 786440 | tf_op jit(solution)/shard_map/ppermute | solution.py:368
  26.6 0.2 collective-permute-start.14
  26.8 0.9 %collective-permute-done.13.refs_9_ = bf16[4,2,2,64,128]{4,3,2,1,0:T(8,128)(2,1)S(1)} collective-permute-done((bf16[4,2,2,64,128]{4,3,2,1,0:T(8,128)(2,1)S(1)}, bf16[4,2,2,64,128]{4,3,2,1,0:T(8,128)(2,1)S(1)}, u32[]{:S(2)}, u32[]{:S(2)}) %collective-permute-start.13) | collective-permute-done | bytes 262176 | tf_op jit(solution)/shard_map/ppermute | solution.py:368
  27.7 2.9 %conv_rim.2.refs_8_ = bf16[512,512]{1,0:T(8,128)(2,1)S(1)} custom-call(s32[3]{0:T(128)S(1)} %pad_add_fusion.refs_0_.meta, bf16[3,9,128,512]{3,2,1,0:T(8,128)(2,1)S(1)} %merge_kernel_slices.1.refs_1_, bf16[2,4,64,128]{3,2,1,0:T(8,128)(2,1)S(1)} %collective-permute-done.3.refs_2_, bf16[2,4,64,128]{3,2,1,0:T(8,128)(2,1)S(1)} %collective-permute-done.6.refs_3_, ...), custom_call_target="tpu_custom_call" | custom-call | flops 1811939328 | bytes 3538944 | tf_op jit(solution)/shard_map/conv_rim/pallas_call | solution.py:202
  30.6 0.4 collective-permute-start.16
  31.0 2.8 %conv_inner.3 = (f32[256,512]{1,0:T(8,128)S(1)}, f32[256,512]{1,0:T(8,128)S(1)}) custom-call(s32[3]{0:T(128)S(1)} %pad_add_fusion.refs_0_.meta, bf16[3,9,128,512]{3,2,1,0:T(8,128)(2,1)S(1)} %merge_kernel_slices.1.refs_1_, bf16[2,4,64,128]{3,2,1,0:T(8,128)(2,1)S(1)} %get-tuple-element.43.refs_2_, bf16[2,4,64,128]{3,2,1,0:T(8,128)(2,1)S(1)} %collective-permute-done.refs_3_, ...), custom_call_target="tpu_custom_call" | custom-call | flops 1811939328 | bytes 3538944 | tf_op jit(solution)/shard_map/conv_inner/pallas_call | solution.py:202
  33.8 1.1 %collective-permute-done.14.refs_1_ = bf16[512,512]{1,0:T(8,128)(2,1)S(1)} collective-permute-done((bf16[512,512]{1,0:T(8,128)(2,1)S(1)}, bf16[512,512]{1,0:T(8,128)(2,1)S(1)}, u32[]{:S(2)}, u32[]{:S(2)}) %collective-permute-start.14) | collective-permute-done | bytes 524320 | tf_op jit(solution)/shard_map/ppermute | solution.py:368
  35.0 0.3 collective-permute-start.15
  35.3 2.9 %conv_rim.3 = (f32[256,512]{1,0:T(8,128)S(1)}, f32[256,512]{1,0:T(8,128)S(1)}) custom-call(s32[3]{0:T(128)S(1)} %pad_add_fusion.refs_0_.meta, bf16[3,9,128,512]{3,2,1,0:T(8,128)(2,1)S(1)} %merge_kernel_slices.1.refs_1_, bf16[2,4,64,128]{3,2,1,0:T(8,128)(2,1)S(1)} %get-tuple-element.43.refs_2_, bf16[2,4,64,128]{3,2,1,0:T(8,128)(2,1)S(1)} %collective-permute-done.refs_3_, ...), custom_call_target="tpu_custom_call" | custom-call | flops 1811939328 | bytes 3538944 | tf_op jit(solution)/shard_map/conv_rim/pallas_call | solution.py:202
  38.1 3.7 %collective-permute-done.16.refs_1_ = bf16[512,512]{1,0:T(8,128)(2,1)S(1)} collective-permute-done((bf16[512,512]{1,0:T(8,128)(2,1)S(1)}, bf16[512,512]{1,0:T(8,128)(2,1)S(1)}, u32[]{:S(2)}, u32[]{:S(2)}) %collective-permute-start.16) | collective-permute-done | bytes 524320 | tf_op jit(solution)/shard_map/ppermute | solution.py:368
  41.9 0.1 sum_parts.5.refs_3_
  41.9 0.0 copy-start.1
  41.9 0.0 copy-start.2
  41.9 0.0 copy-start.3
  42.0 0.0 copy-start.4
  42.0 0.3 collective-permute-start.18
  42.3 1.1 %collective-permute-done.15.refs_2_ = bf16[256,512]{1,0:T(8,128)(2,1)S(1)} collective-permute-done((bf16[256,512]{1,0:T(8,128)(2,1)S(1)}, bf16[256,512]{1,0:T(8,128)(2,1)S(1)}, u32[]{:S(2)}, u32[]{:S(2)}) %collective-permute-start.15) | collective-permute-done | bytes 262176 | tf_op jit(solution)/shard_map/ppermute | solution.py:368
  43.4 0.1 sum_parts.6
  43.5 5.6 %collective-permute-start.17 = (bf16[128,512]{1,0:T(8,128)(2,1)S(1)}, bf16[128,512]{1,0:T(8,128)(2,1)S(1)}, u32[]{:S(2)}, u32[]{:S(2)}) collective-permute-start(bf16[128,512]{1,0:T(8,128)(2,1)S(1)} %get-tuple-element.30), channel_id=1, source_target_pairs={{0,0},{1,1},{2,4},{3,5},{4,2},{5,3},{6,6},{7,7},{8,8},{9,9},{10,12... | collective-permute-start | bytes 393224 | tf_op jit(solution)/shard_map/ppermute | solution.py:368
  49.2 0.1 collective-permute-start.20
  49.2 0.0 collective-permute-done.18.refs_2_
  49.3 0.1 sum_parts.7
  49.3 5.7 %collective-permute-start.19 = (bf16[128,512]{1,0:T(8,128)(2,1)S(1)}, bf16[128,512]{1,0:T(8,128)(2,1)S(1)}, u32[]{:S(2)}, u32[]{:S(2)}) collective-permute-start(bf16[128,512]{1,0:T(8,128)(2,1)S(1)} %get-tuple-element.32), channel_id=1, source_target_pairs={{0,0},{1,1},{2,4},{3,5},{4,2},{5,3},{6,6},{7,7},{8,8},{9,9},{10,12... | collective-permute-start | bytes 393224 | tf_op jit(solution)/shard_map/ppermute | solution.py:368
  55.0 0.1 collective-permute-start.21
  55.1 0.1 collective-permute-start.22
  55.2 0.4 collective-permute-done.20.refs_2_
  55.6 0.1 collective-permute-start.24
  55.7 3.3 %collective-permute-done.19.refs_1_ = bf16[128,512]{1,0:T(8,128)(2,1)S(1)} collective-permute-done((bf16[128,512]{1,0:T(8,128)(2,1)S(1)}, bf16[128,512]{1,0:T(8,128)(2,1)S(1)}, u32[]{:S(2)}, u32[]{:S(2)}) %collective-permute-start.19) | collective-permute-done | bytes 131104 | tf_op jit(solution)/shard_map/ppermute | solution.py:368
  59.0 2.3 %collective-permute-done.21.refs_3_ = bf16[128,512]{1,0:T(8,128)(2,1)S(1)} collective-permute-done((bf16[128,512]{1,0:T(8,128)(2,1)S(1)}, bf16[128,512]{1,0:T(8,128)(2,1)S(1)}, u32[]{:S(2)}, u32[]{:S(2)}) %collective-permute-start.21) | collective-permute-done | bytes 131104 | tf_op jit(solution)/shard_map/ppermute | solution.py:368
  61.4 1.3 %collective-permute-done.25.refs_7_ = bf16[128,512]{1,0:T(8,128)(2,1)S(1)} collective-permute-done((bf16[128,512]{1,0:T(8,128)(2,1)S(1)}, bf16[128,512]{1,0:T(8,128)(2,1)S(1)}, u32[]{:S(2)}, u32[]{:S(2)}) %collective-permute-start.25) | collective-permute-done | bytes 131104 | tf_op jit(solution)/shard_map/ppermute | solution.py:368
  62.7 4.5 %attend.1 = (bf16[4,64,512]{2,1,0:T(8,128)(2,1)S(1)}, bf16[4,64,512]{2,1,0:T(8,128)(2,1)S(1)}) custom-call(bf16[128,512]{1,0:T(8,128)(2,1)S(1)} %collective-permute-done.17.refs_0_, bf16[128,512]{1,0:T(8,128)(2,1)S(1)} %collective-permute-done.19.refs_1_, bf16[128,512]{1,0:T(8,128)(2,1)S(1)} %collective-permute-done.20.refs_2_, ...), custom_call_target="tpu_custom_call" | custom-call | flops 2684354560 | bytes 3145728 | tf_op jit(solution)/shard_map/attend/pallas_call | solution.py:339
  67.2 1.9 %collective-permute-start.26 = (bf16[4,64,512]{2,1,0:T(8,128)(2,1)S(1)}, bf16[4,64,512]{2,1,0:T(8,128)(2,1)S(1)}, u32[]{:S(2)}, u32[]{:S(2)}) collective-permute-start(bf16[4,64,512]{2,1,0:T(8,128)(2,1)S(1)} %get-tuple-element.35), channel_id=1, source_target_pairs={{1,0},{0,1},{5,2},{4,3},{3,4},{2,5},{7,6},{6,7},{9,8},{8,9},{13,10... | collective-permute-start | bytes 786440 | tf_op jit(solution)/shard_map/ppermute | solution.py:456
  69.2 2.3 %collective-permute-start.27 = (bf16[4,64,512]{2,1,0:T(8,128)(2,1)S(1)}, bf16[4,64,512]{2,1,0:T(8,128)(2,1)S(1)}, u32[]{:S(2)}, u32[]{:S(2)}) collective-permute-start(bf16[4,64,512]{2,1,0:T(8,128)(2,1)S(1)} %get-tuple-element.36), channel_id=1, source_target_pairs={{0,0},{1,1},{4,2},{5,3},{2,4},{3,5},{6,6},{7,7},{8,8},{9,9},{12,10... | collective-permute-start | bytes 786440 | tf_op jit(solution)/shard_map/ppermute | solution.py:456
  71.4 5.5 %collective-permute-done.26 = bf16[4,64,512]{2,1,0:T(8,128)(2,1)S(1)} collective-permute-done((bf16[4,64,512]{2,1,0:T(8,128)(2,1)S(1)}, bf16[4,64,512]{2,1,0:T(8,128)(2,1)S(1)}, u32[]{:S(2)}, u32[]{:S(2)}) %collective-permute-start.26) | collective-permute-done | bytes 262176 | tf_op jit(solution)/shard_map/ppermute | solution.py:456
  77.0 5.0 %collective-permute-done.27 = bf16[4,64,512]{2,1,0:T(8,128)(2,1)S(1)} collective-permute-done((bf16[4,64,512]{2,1,0:T(8,128)(2,1)S(1)}, bf16[4,64,512]{2,1,0:T(8,128)(2,1)S(1)}, u32[]{:S(2)}, u32[]{:S(2)}) %collective-permute-start.27) | collective-permute-done | bytes 262176 | tf_op jit(solution)/shard_map/ppermute | solution.py:456
  82.0 0.8 %pad_maximum_fusion = bf16[2,4,64,512]{3,2,1,0:T(8,128)(2,1)} fusion(bf16[1,4,64,512]{3,2,1,0:T(8,128)(2,1)S(1)} %get-tuple-element.38, bf16[1,4,64,512]{3,2,1,0:T(8,128)(2,1)S(1)} %get-tuple-element.37), kind=kLoop, calls=%fused_computation | loop fusion | flops 262144 | bytes 1048576 | tf_op jit(solution)/shard_map/stack | solution.py:457
  (19 shorter events, 0.1 us)
Async XLA Ops:
  0.0 9.7 %collective-permute-start.1 = (bf16[9,3,64,512]{3,2,1,0:T(8,128)(2,1)}, bf16[9,3,64,512]{3,2,1,0:T(8,128)(2,1)S(1)}, u32[]{:S(2)}, u32[]{:S(2)}) collective-permute-start(bf16[9,3,64,512]{3,2,1,0:T(8,128)(2,1)} %bitcast.16), channel_id=1, source_target_pairs={{0,4},{1,5},{2,6},{3,7},{4,0},{5,1},{6,2},{7,3},{8,12},{9,13},{10,... | collective-permute-start | bytes 5308424 | tf_op jit(solution)/shard_map/ppermute | solution.py:368
  1.2 12.1 %collective-permute-start = (bf16[2,4,64,128]{3,2,1,0:T(8,128)(2,1)S(1)}, bf16[2,4,64,128]{3,2,1,0:T(8,128)(2,1)S(1)}, u32[]{:S(2)}, u32[]{:S(2)}) collective-permute-start(bf16[2,4,64,128]{3,2,1,0:T(8,128)(2,1)S(1)} %get-tuple-element.44), channel_id=1, source_target_pairs={{0,16},{1,17},{2,18},{3,19},{4,12},{5,13},{6,14},{7,15},{8,24},{9,... | collective-permute-start | bytes 393224 | tf_op jit(solution)/shard_map/ppermute | solution.py:368
  3.9 10.6 %collective-permute-start.3 = (bf16[2,4,64,128]{3,2,1,0:T(8,128)(2,1)S(1)}, bf16[2,4,64,128]{3,2,1,0:T(8,128)(2,1)S(1)}, u32[]{:S(2)}, u32[]{:S(2)}) collective-permute-start(bf16[2,4,64,128]{3,2,1,0:T(8,128)(2,1)S(1)} %get-tuple-element.42), channel_id=1, source_target_pairs={{0,8},{1,9},{2,10},{3,11},{4,20},{5,21},{6,22},{7,23},{8,0},{9,1},... | collective-permute-start | bytes 393224 | tf_op jit(solution)/shard_map/ppermute | solution.py:368
  5.2 9.4 %collective-permute-start.6 = (bf16[2,4,64,128]{3,2,1,0:T(8,128)(2,1)S(1)}, bf16[2,4,64,128]{3,2,1,0:T(8,128)(2,1)S(1)}, u32[]{:S(2)}, u32[]{:S(2)}) collective-permute-start(bf16[2,4,64,128]{3,2,1,0:T(8,128)(2,1)S(1)} %get-tuple-element.41), channel_id=1, source_target_pairs={{0,24},{1,25},{2,26},{3,27},{4,28},{5,29},{6,30},{7,31},{8,16},{9,... | collective-permute-start | bytes 393224 | tf_op jit(solution)/shard_map/ppermute | solution.py:368
  6.2 8.8 %collective-permute-start.8 = (bf16[2,64,512]{2,1,0:T(8,128)(2,1)S(1)}, bf16[2,64,512]{2,1,0:T(8,128)(2,1)S(1)}, u32[]{:S(2)}, u32[]{:S(2)}) collective-permute-start(bf16[2,64,512]{2,1,0:T(8,128)(2,1)S(1)} %get-tuple-element.40), channel_id=1, source_target_pairs={{0,1},{1,2},{2,3},{4,5},{5,6},{6,7},{8,9},{9,10},{10,11},{12,13},{... | collective-permute-start | bytes 393224 | tf_op jit(solution)/shard_map/ppermute | solution.py:368
  9.7 5.7 %collective-permute-start.9 = (bf16[2,64,512]{2,1,0:T(8,128)(2,1)S(1)}, bf16[2,64,512]{2,1,0:T(8,128)(2,1)S(1)}, u32[]{:S(2)}, u32[]{:S(2)}) collective-permute-start(bf16[2,64,512]{2,1,0:T(8,128)(2,1)S(1)} %get-tuple-element.39), channel_id=1, source_target_pairs={{1,0},{2,1},{3,2},{5,4},{6,5},{7,6},{9,8},{10,9},{11,10},{13,12},{... | collective-permute-start | bytes 393224 | tf_op jit(solution)/shard_map/ppermute | solution.py:368
  11.0 1.5 %copy-start = (bf16[27,64,512]{2,1,0:T(8,128)(2,1)S(1)}, bf16[27,64,512]{2,1,0:T(8,128)(2,1)}, u32[]{:S(2)}) copy-start(bf16[27,64,512]{2,1,0:T(8,128)(2,1)} %param.7) | copy-start | bytes 5308420
  13.3 4.0 %collective-permute-start.2 = (bf16[2,4,64,128]{3,2,1,0:T(8,128)(2,1)S(1)}, bf16[2,4,64,128]{3,2,1,0:T(8,128)(2,1)S(1)}, u32[]{:S(2)}, u32[]{:S(2)}) collective-permute-start(bf16[2,4,64,128]{3,2,1,0:T(8,128)(2,1)S(1)} %get-tuple-element.43.refs_2_), channel_id=1, source_target_pairs={{0,4},{1,5},{2,6},{3,7},{4,0},{5,1},{6,2},{7,3},{8,12},{9,13},{10,... | collective-permute-start | bytes 393224 | tf_op jit(solution)/shard_map/ppermute | solution.py:368
  14.5 4.0 %collective-permute-start.4 = (bf16[2,4,64,128]{3,2,1,0:T(8,128)(2,1)S(1)}, bf16[2,4,64,128]{3,2,1,0:T(8,128)(2,1)S(1)}, u32[]{:S(2)}, u32[]{:S(2)}) collective-permute-start(bf16[2,4,64,128]{3,2,1,0:T(8,128)(2,1)S(1)} %collective-permute-done.3.refs_2_), channel_id=1, source_target_pairs={{0,4},{1,5},{2,6},{3,7},{4,0},{5,1},{6,2},{7,3},{8,12},{9,13},{10,... | collective-permute-start | bytes 393224 | tf_op jit(solution)/shard_map/ppermute | solution.py:368
  14.6 4.1 %collective-permute-start.7 = (bf16[2,4,64,128]{3,2,1,0:T(8,128)(2,1)S(1)}, bf16[2,4,64,128]{3,2,1,0:T(8,128)(2,1)S(1)}, u32[]{:S(2)}, u32[]{:S(2)}) collective-permute-start(bf16[2,4,64,128]{3,2,1,0:T(8,128)(2,1)S(1)} %collective-permute-done.6.refs_3_), channel_id=1, source_target_pairs={{0,4},{1,5},{2,6},{3,7},{4,0},{5,1},{6,2},{7,3},{8,12},{9,13},{10,... | collective-permute-start | bytes 393224 | tf_op jit(solution)/shard_map/ppermute | solution.py:368
  15.0 3.7 %collective-permute-start.5 = (bf16[2,4,64,128]{3,2,1,0:T(8,128)(2,1)S(1)}, bf16[2,4,64,128]{3,2,1,0:T(8,128)(2,1)S(1)}, u32[]{:S(2)}, u32[]{:S(2)}) collective-permute-start(bf16[2,4,64,128]{3,2,1,0:T(8,128)(2,1)S(1)} %collective-permute-done.refs_3_), channel_id=1, source_target_pairs={{0,4},{1,5},{2,6},{3,7},{4,0},{5,1},{6,2},{7,3},{8,12},{9,13},{10,... | collective-permute-start | bytes 393224 | tf_op jit(solution)/shard_map/ppermute | solution.py:368
  16.0 5.6 %collective-permute-start.10 = (bf16[2,2,64,128]{3,2,1,0:T(8,128)(2,1)S(1)}, bf16[2,2,64,128]{3,2,1,0:T(8,128)(2,1)S(1)}, u32[]{:S(2)}, u32[]{:S(2)}) collective-permute-start(bf16[2,2,64,128]{3,2,1,0:T(8,128)(2,1)S(1)} %get-tuple-element.24), channel_id=1, source_target_pairs={{0,8},{1,9},{2,10},{3,11},{4,20},{5,21},{6,22},{7,23},{8,0},{9,1},... | collective-permute-start | bytes 196616 | tf_op jit(solution)/shard_map/ppermute | solution.py:368
  17.3 4.3 %collective-permute-start.11 = (bf16[2,2,64,128]{3,2,1,0:T(8,128)(2,1)S(1)}, bf16[2,2,64,128]{3,2,1,0:T(8,128)(2,1)S(1)}, u32[]{:S(2)}, u32[]{:S(2)}) collective-permute-start(bf16[2,2,64,128]{3,2,1,0:T(8,128)(2,1)S(1)} %get-tuple-element.25), channel_id=1, source_target_pairs={{0,16},{1,17},{2,18},{3,19},{4,12},{5,13},{6,14},{7,15},{8,24},{9,... | collective-permute-start | bytes 196616 | tf_op jit(solution)/shard_map/ppermute | solution.py:368
  18.5 4.4 %collective-permute-start.12 = (bf16[2,2,64,128]{3,2,1,0:T(8,128)(2,1)S(1)}, bf16[2,2,64,128]{3,2,1,0:T(8,128)(2,1)S(1)}, u32[]{:S(2)}, u32[]{:S(2)}) collective-permute-start(bf16[2,2,64,128]{3,2,1,0:T(8,128)(2,1)S(1)} %get-tuple-element.26), channel_id=1, source_target_pairs={{0,24},{1,25},{2,26},{3,27},{4,28},{5,29},{6,30},{7,31},{8,16},{9,... | collective-permute-start | bytes 196616 | tf_op jit(solution)/shard_map/ppermute | solution.py:368
  22.9 4.8 %collective-permute-start.13 = (bf16[4,2,2,64,128]{4,3,2,1,0:T(8,128)(2,1)S(1)}, bf16[4,2,2,64,128]{4,3,2,1,0:T(8,128)(2,1)S(1)}, u32[]{:S(2)}, u32[]{:S(2)}) collective-permute-start(bf16[4,2,2,64,128]{4,3,2,1,0:T(8,128)(2,1)S(1)} %stack_halo_rows.1.refs_8_), channel_id=1, source_target_pairs={{0,4},{1,5},{2,6},{3,7},{4,0},{5,1},{6,2},{7,3},{8,12},{9,13},{10,... | collective-permute-start | bytes 786440 | tf_op jit(solution)/shard_map/ppermute | solution.py:368
  26.6 8.3 %collective-permute-start.14 = (bf16[512,512]{1,0:T(8,128)(2,1)S(1)}, bf16[512,512]{1,0:T(8,128)(2,1)S(1)}, u32[]{:S(2)}, u32[]{:S(2)}) collective-permute-start(bf16[512,512]{1,0:T(8,128)(2,1)S(1)} %conv_inner.2.refs_4_), channel_id=1, source_target_pairs={{0,8},{1,9},{2,10},{3,11},{4,20},{5,21},{6,22},{7,23},{8,0},{9,1},... | collective-permute-start | bytes 1572872 | tf_op jit(solution)/shard_map/ppermute | solution.py:368
  30.6 11.3 %collective-permute-start.16 = (bf16[512,512]{1,0:T(8,128)(2,1)S(1)}, bf16[512,512]{1,0:T(8,128)(2,1)S(1)}, u32[]{:S(2)}, u32[]{:S(2)}) collective-permute-start(bf16[512,512]{1,0:T(8,128)(2,1)S(1)} %conv_rim.2.refs_8_), channel_id=1, source_target_pairs={{0,8},{1,9},{2,10},{3,11},{4,20},{5,21},{6,22},{7,23},{8,0},{9,1},... | collective-permute-start | bytes 1572872 | tf_op jit(solution)/shard_map/ppermute | solution.py:368
  35.0 8.5 %collective-permute-start.15 = (bf16[256,512]{1,0:T(8,128)(2,1)S(1)}, bf16[256,512]{1,0:T(8,128)(2,1)S(1)}, u32[]{:S(2)}, u32[]{:S(2)}) collective-permute-start(bf16[256,512]{1,0:T(8,128)(2,1)S(1)} %sum_parts.4.refs_10_), channel_id=1, source_target_pairs={{0,16},{1,17},{2,18},{3,19},{4,12},{5,13},{6,14},{7,15},{8,24},{9,... | collective-permute-start | bytes 786440 | tf_op jit(solution)/shard_map/ppermute | solution.py:368
  41.9 20.8 %copy-start.1 = (bf16[512,512]{1,0:T(8,128)(2,1)S(1)}, bf16[512,512]{1,0:T(8,128)(2,1)}, u32[]{:S(2)}) copy-start(bf16[512,512]{1,0:T(8,128)(2,1)} %refs_8_.1) | copy-start | bytes 1572868
  41.9 20.8 %copy-start.2 = (bf16[512,512]{1,0:T(8,128)(2,1)S(1)}, bf16[512,512]{1,0:T(8,128)(2,1)}, u32[]{:S(2)}) copy-start(bf16[512,512]{1,0:T(8,128)(2,1)} %refs_9_.1) | copy-start | bytes 1572868
  41.9 20.8 %copy-start.3 = (bf16[512,512]{1,0:T(8,128)(2,1)S(1)}, bf16[512,512]{1,0:T(8,128)(2,1)}, u32[]{:S(2)}) copy-start(bf16[512,512]{1,0:T(8,128)(2,1)} %refs_10_.1) | copy-start | bytes 1572868
  42.0 20.8 %copy-start.4 = (bf16[512,512]{1,0:T(8,128)(2,1)S(1)}, bf16[512,512]{1,0:T(8,128)(2,1)}, u32[]{:S(2)}) copy-start(bf16[512,512]{1,0:T(8,128)(2,1)} %refs_11_.1) | copy-start | bytes 1572868
  42.0 7.3 %collective-permute-start.18 = (bf16[256,512]{1,0:T(8,128)(2,1)S(1)}, bf16[256,512]{1,0:T(8,128)(2,1)S(1)}, u32[]{:S(2)}, u32[]{:S(2)}) collective-permute-start(bf16[256,512]{1,0:T(8,128)(2,1)S(1)} %sum_parts.5.refs_3_), channel_id=1, source_target_pairs={{0,16},{1,17},{2,18},{3,19},{4,12},{5,13},{6,14},{7,15},{8,24},{9,... | collective-permute-start | bytes 786440 | tf_op jit(solution)/shard_map/ppermute | solution.py:368
  43.5 11.6 %collective-permute-start.17 = (bf16[128,512]{1,0:T(8,128)(2,1)S(1)}, bf16[128,512]{1,0:T(8,128)(2,1)S(1)}, u32[]{:S(2)}, u32[]{:S(2)}) collective-permute-start(bf16[128,512]{1,0:T(8,128)(2,1)S(1)} %get-tuple-element.30), channel_id=1, source_target_pairs={{0,0},{1,1},{2,4},{3,5},{4,2},{5,3},{6,6},{7,7},{8,8},{9,9},{10,12... | collective-permute-start | bytes 393224 | tf_op jit(solution)/shard_map/ppermute | solution.py:368
  49.2 6.5 %collective-permute-start.20 = (bf16[128,512]{1,0:T(8,128)(2,1)S(1)}, bf16[128,512]{1,0:T(8,128)(2,1)S(1)}, u32[]{:S(2)}, u32[]{:S(2)}) collective-permute-start(bf16[128,512]{1,0:T(8,128)(2,1)S(1)} %get-tuple-element.33), channel_id=1, source_target_pairs={{0,1},{1,0},{2,5},{3,4},{4,3},{5,2},{6,7},{7,6},{8,9},{9,8},{10,13... | collective-permute-start | bytes 393224 | tf_op jit(solution)/shard_map/ppermute | solution.py:368
  49.3 9.7 %collective-permute-start.19 = (bf16[128,512]{1,0:T(8,128)(2,1)S(1)}, bf16[128,512]{1,0:T(8,128)(2,1)S(1)}, u32[]{:S(2)}, u32[]{:S(2)}) collective-permute-start(bf16[128,512]{1,0:T(8,128)(2,1)S(1)} %get-tuple-element.32), channel_id=1, source_target_pairs={{0,0},{1,1},{2,4},{3,5},{4,2},{5,3},{6,6},{7,7},{8,8},{9,9},{10,12... | collective-permute-start | bytes 393224 | tf_op jit(solution)/shard_map/ppermute | solution.py:368
  55.0 6.4 %collective-permute-start.21 = (bf16[128,512]{1,0:T(8,128)(2,1)S(1)}, bf16[128,512]{1,0:T(8,128)(2,1)S(1)}, u32[]{:S(2)}, u32[]{:S(2)}) collective-permute-start(bf16[128,512]{1,0:T(8,128)(2,1)S(1)} %get-tuple-element.34), channel_id=1, source_target_pairs={{0,1},{1,0},{2,5},{3,4},{4,3},{5,2},{6,7},{7,6},{8,9},{9,8},{10,13... | collective-permute-start | bytes 393224 | tf_op jit(solution)/shard_map/ppermute | solution.py:368
  55.1 6.3 %collective-permute-start.22 = (bf16[128,512]{1,0:T(8,128)(2,1)S(1)}, bf16[128,512]{1,0:T(8,128)(2,1)S(1)}, u32[]{:S(2)}, u32[]{:S(2)}) collective-permute-start(bf16[128,512]{1,0:T(8,128)(2,1)S(1)} %collective-permute-done.17.refs_0_), channel_id=1, source_target_pairs={{0,4},{1,5},{2,6},{3,7},{4,0},{5,1},{6,2},{7,3},{8,12},{9,13},{10,... | collective-permute-start | bytes 393224 | tf_op jit(solution)/shard_map/ppermute | solution.py:368
  55.6 5.8 %collective-permute-start.24 = (bf16[128,512]{1,0:T(8,128)(2,1)S(1)}, bf16[128,512]{1,0:T(8,128)(2,1)S(1)}, u32[]{:S(2)}, u32[]{:S(2)}) collective-permute-start(bf16[128,512]{1,0:T(8,128)(2,1)S(1)} %collective-permute-done.20.refs_2_), channel_id=1, source_target_pairs={{0,4},{1,5},{2,6},{3,7},{4,0},{5,1},{6,2},{7,3},{8,12},{9,13},{10,... | collective-permute-start | bytes 393224 | tf_op jit(solution)/shard_map/ppermute | solution.py:368
  59.0 2.4 %collective-permute-start.23 = (bf16[128,512]{1,0:T(8,128)(2,1)S(1)}, bf16[128,512]{1,0:T(8,128)(2,1)S(1)}, u32[]{:S(2)}, u32[]{:S(2)}) collective-permute-start(bf16[128,512]{1,0:T(8,128)(2,1)S(1)} %collective-permute-done.19.refs_1_), channel_id=1, source_target_pairs={{0,4},{1,5},{2,6},{3,7},{4,0},{5,1},{6,2},{7,3},{8,12},{9,13},{10,... | collective-permute-start | bytes 393224 | tf_op jit(solution)/shard_map/ppermute | solution.py:368
  61.4 1.3 %collective-permute-start.25 = (bf16[128,512]{1,0:T(8,128)(2,1)S(1)}, bf16[128,512]{1,0:T(8,128)(2,1)S(1)}, u32[]{:S(2)}, u32[]{:S(2)}) collective-permute-start(bf16[128,512]{1,0:T(8,128)(2,1)S(1)} %collective-permute-done.21.refs_3_), channel_id=1, source_target_pairs={{0,4},{1,5},{2,6},{3,7},{4,0},{5,1},{6,2},{7,3},{8,12},{9,13},{10,... | collective-permute-start | bytes 393224 | tf_op jit(solution)/shard_map/ppermute | solution.py:368
  67.2 9.8 %collective-permute-start.26 = (bf16[4,64,512]{2,1,0:T(8,128)(2,1)S(1)}, bf16[4,64,512]{2,1,0:T(8,128)(2,1)S(1)}, u32[]{:S(2)}, u32[]{:S(2)}) collective-permute-start(bf16[4,64,512]{2,1,0:T(8,128)(2,1)S(1)} %get-tuple-element.35), channel_id=1, source_target_pairs={{1,0},{0,1},{5,2},{4,3},{3,4},{2,5},{7,6},{6,7},{9,8},{8,9},{13,10... | collective-permute-start | bytes 786440 | tf_op jit(solution)/shard_map/ppermute | solution.py:456
  69.2 12.8 %collective-permute-start.27 = (bf16[4,64,512]{2,1,0:T(8,128)(2,1)S(1)}, bf16[4,64,512]{2,1,0:T(8,128)(2,1)S(1)}, u32[]{:S(2)}, u32[]{:S(2)}) collective-permute-start(bf16[4,64,512]{2,1,0:T(8,128)(2,1)S(1)} %get-tuple-element.36), channel_id=1, source_target_pairs={{0,0},{1,1},{4,2},{5,3},{2,4},{3,5},{6,6},{7,7},{8,8},{9,9},{12,10... | collective-permute-start | bytes 786440 | tf_op jit(solution)/shard_map/ppermute | solution.py:456

commit v5 on v4

--- a/solution.py
+++ b/solution.py
@@ -59,7 +59,8 @@
         functools.partial(merge_kernel, group),
         out_shape=jax.ShapeDtypeStruct((lags, taps, group * chans_here, chans), jnp.bfloat16),
         in_specs=[pl.BlockSpec(memory_space=pltpu.SMEM)]
-        + [pl.BlockSpec(memory_space=pl.ANY)] * group,
+        + [pl.BlockSpec(memory_space=pltpu.HBM)]
+        + [pl.BlockSpec(memory_space=pl.ANY)] * (group - 1),
         out_specs=pl.BlockSpec(memory_space=pltpu.VMEM),
         scratch_shapes=[pltpu.SemaphoreType.DMA((lags, group))],
         compiler_params=pltpu.CompilerParams(vmem_limit_bytes=VMEM_LIMIT),
@@ -104,7 +105,7 @@
     return pl.pallas_call(
         kernel,
         out_shape=jax.ShapeDtypeStruct((len(pieces), *pieces[0].shape), pieces[0].dtype),
-        in_specs=in_vmem(len(pieces)) + [pl.BlockSpec(memory_space=pl.ANY)],
+        in_specs=in_vmem(len(pieces) + 1),
         out_specs=pl.BlockSpec(memory_space=pltpu.VMEM),
         compiler_params=pltpu.CompilerParams(vmem_limit_bytes=VMEM_LIMIT),
         name="stack_halo_rows",
@@ -184,7 +185,7 @@
         place += out.shape[0]
 
 
-def conv_call(jobs, meta, weights, held, before, rims, group, frames, joined, after=()):
+def conv_call(jobs, meta, weights, held, before, rims, group, frames, out_type, after=()):
     parts = len(held)
     dests = sorted({place for place, _ in jobs})
     _, rows_here, columns, width = held[0].shape
@@ -194,11 +195,8 @@
     total = sum(counts)
     operands = [weights, *[held[n] for n in dests], *before, *(rims if any_rim else ())]
     specs = [pl.BlockSpec(memory_space=pltpu.SMEM)] + in_vmem(len(operands))
-    specs += [pl.BlockSpec(memory_space=pl.ANY)] * len(after)
-    if joined:
-        outs = [jax.ShapeDtypeStruct((total, chans), jnp.bfloat16)]
-    else:
-        outs = [jax.ShapeDtypeStruct((count, chans), jnp.float32) for count in counts]
+    specs += in_vmem(len(after))
+    outs = [jax.ShapeDtypeStruct((count, chans), out_type) for count in counts]
     return pl.pallas_call(
         functools.partial(conv_kernel, tuple(jobs), parts, group, frames, len(outs)),
         out_shape=outs,
@@ -208,37 +206,31 @@
             pltpu.VMEM((len(dests), 2 * frames, rows_here + 2, columns, width), jnp.bfloat16)
         ],
         compiler_params=pltpu.CompilerParams(vmem_limit_bytes=VMEM_LIMIT),
-        cost_estimate=pl.CostEstimate(
-            flops=2 * total * taps * lags * width * chans,
-            bytes_accessed=2 * taps * lags * width * chans,
-            transcendentals=0,
-        ),
+        cost_estimate=pl.CostEstimate(flops=10**11, bytes_accessed=1000, transcendentals=0),
         name="conv_rim" if any_rim else "conv_inner",
     )(meta, *operands, *after)
 
 
 def sum_call(pieces, splits, after=()):
-    count = pieces[0][0].shape[0]
-    chans = pieces[0][0].shape[1]
+    count, chans = pieces[0].shape
     size = count // splits
-    out = jax.ShapeDtypeStruct((size, chans), jnp.bfloat16)
 
     def kernel(*refs):
         for p, out_ref in enumerate(refs[len(refs) - splits :]):
             total = None
-            for (_, start), ref in zip(pieces, refs):
-                rows = ref[start + p * size : start + (p + 1) * size].astype(jnp.float32)
+            for ref in refs[: len(pieces)]:
+                rows = ref[p * size : (p + 1) * size].astype(jnp.float32)
                 total = rows if total is None else total + rows
             out_ref[...] = total.astype(out_ref.dtype)
 
     return pl.pallas_call(
         kernel,
-        out_shape=[out] * splits,
-        in_specs=in_vmem(len(pieces)) + [pl.BlockSpec(memory_space=pl.ANY)] * len(after),
+        out_shape=[jax.ShapeDtypeStruct((size, chans), jnp.bfloat16)] * splits,
+        in_specs=in_vmem(len(pieces) + len(after)),
         out_specs=in_vmem(splits),
         compiler_params=pltpu.CompilerParams(vmem_limit_bytes=VMEM_LIMIT),
         name="sum_parts",
-    )(*[array for array, _ in pieces], *after)
+    )(*pieces, *after)
 
 
 def attend_kernel(frames, share, chunks, *refs):
@@ -386,8 +378,6 @@
         start = (part ^ partner(member, jnp.int32(place))) * width
         piece = lax.dynamic_slice_in_dim(latents, start, width, axis=3)
         held[place] = permute(piece, to_place(place)) if place else piece
-    rims = split_call(meta, above, below, parts)
-    rims = [permute(x, to_place(place)) if place else x for place, x in enumerate(rims)]
     held[2], weights = lax.optimization_barrier((held[2], weights))
     for place in order:
         before[place] = permute(held[place], to_member(1))
@@ -402,24 +392,35 @@
         frames=frames,
     )
 
-    (inner_sent,) = conv([(1, False), (3, False)], rims=None, joined=True)
-    rims = stack_call(rims, inner_sent)
+    def hop(pieces):
+        return [permute(x, to_place(1)) for x in pieces]
+
+    rims = split_call(meta, above, below, parts)
+    inner_sent = conv(
+        [(3, False), (1, False)], rims=None, out_type=jnp.bfloat16, after=rims[:1]
+    )
+    inner_got = hop(inner_sent)
+    inner_on, inner_own = conv(
+        [(2, False), (0, False)], rims=None, out_type=jnp.float32, after=inner_sent[:1]
+    )
+    rims, _ = lax.optimization_barrier((rims, inner_sent[0]))
+    rims = [permute(x, to_place(place)) if place else x for place, x in enumerate(rims)]
+    rims = stack_call(rims, inner_on)
     rims = (rims, permute(rims, to_member(1)))
-    (rim_sent,) = conv([(1, True), (3, True)], rims=rims, joined=True)
-    inner_got = permute(inner_sent, to_place(1))
-    rim_got = permute(rim_sent, to_place(1))
-    inner_on, inner_own = conv(
-        [(2, False), (0, False)], rims=None, joined=False, after=(rim_sent,)
-    )
-    half = inner_on.shape[0]
-    (inner_relay,) = sum_call([(inner_on, 0), (inner_got, half)], 1)
-    rim_on, rim_own = conv([(2, True), (0, True)], rims=rims, joined=False, after=(inner_relay,))
-    (rim_relay,) = sum_call([(rim_on, 0), (rim_got, rim_on.shape[0])], 1)
+    (inner_relay,) = sum_call([inner_on, inner_got[0]], 1, after=inner_got[1:])
+    rim_sent = conv(
+        [(3, True), (1, True)], rims=rims, out_type=jnp.bfloat16, after=(inner_relay,)
+    )
+    rim_got = hop(rim_sent)
     inner_last = permute(inner_relay, to_place(2))
+    rim_on, rim_own = conv(
+        [(2, True), (0, True)], rims=rims, out_type=jnp.float32, after=rim_sent[:1]
+    )
+    (rim_relay,) = sum_call([rim_on, rim_got[0]], 1, after=rim_got[1:])
     rim_last = permute(rim_relay, to_place(2))
     sums = [
-        sum_call([(inner_own, 0), (inner_got, 0), (inner_last, 0)], frames, after=(rim_relay,)),
-        sum_call([(rim_own, 0), (rim_got, 0), (rim_last, 0)], frames),
+        sum_call([inner_own, inner_got[1], inner_last], frames),
+        sum_call([rim_own, rim_got[1], rim_last], frames),
     ]
 
     share = depth // frames

time: 83.1 us -> 86.9 us (1.046)
  starting transfers between devices: 33.9 us -> 38.8 us
  waiting for transfers between devices: 26.5 us -> 23.3 us
  Pallas kernels: 17.6 us -> 19.7 us
    ppermute x26 -> x28, starting transfers between devices: 29.7 us -> 33.9 us  [permute(): return lax.ppermute(block, BOTH, everywhere(sizes, target))]
    ppermute x26 -> x28, waiting for transfers between devices: 15.9 us -> 12.7 us  [permute(): return lax.ppermute(block, BOTH, everywhere(sizes, target))]
    pallas_call x4, Pallas kernels: 0.3 us -> 1.97 us  [sum_call(): pl.pallas_call(kernel, out_shape=[jax.ShapeDtypeStruct((size, chans), jnp...]
  transfers between devices with their start and end apart: 28 -> 30, of which waited for: 12 -> 14; matrix products, arithmetic and copies ran while one was open for 3% -> 3% of each run, Pallas kernels for 16% -> 14%
where the time goes in v5:
time: 86.9 us; the launch traced here: 86.6 us
  starting transfers between devices  38.8 us (45%)
  waiting for transfers between devices  23.3 us (27%)
  Pallas kernels  19.7 us (23%)
  local copies, waits for them, and re-layouts  3.64 us (4%)
  other arithmetic  0.96 us (1%)
    ppermute x28, starting transfers between devices, permute(): return lax.ppermute(block, BOTH, everywhere(sizes, target))  33.9 us
    ppermute x28, waiting for transfers between devices, permute(): return lax.ppermute(block, BOTH, everywhere(sizes, target))  12.7 us
    pallas_call x4, Pallas kernels, conv_call(): pl.pallas_call(functools.partial(conv_kernel, tuple(jobs), parts, group,...  11.9 us
    ppermute x2, waiting for transfers between devices, body(): back.append(lax.ppermute(done[p], BOTH, pairs))  10.5 us
    ppermute x2, starting transfers between devices, body(): back.append(lax.ppermute(done[p], BOTH, pairs))  4.9 us
    pallas_call x1, Pallas kernels, attend_call(): pl.pallas_call(functools.partial(attend_kernel, frames, share, chunks), o...  4.4 us
    pallas_call x4, Pallas kernels, sum_call(): pl.pallas_call(kernel, out_shape=[jax.ShapeDtypeStruct((size, chans), jnp...  1.97 us
  transfers between devices with their start and end apart: 30, of which 14 were waited for; matrix products, arithmetic and copies ran while one was open for 3% of the time, Pallas kernels for 14%

profile of v5, /device:TPU:1, one launch (start us, length us, event | category | flops | bytes accessed | tf_op | source)
XLA Modules:
  0.0 86.6 jit_solution(1645825769988296564)
XLA Ops:
  0.0 0.1 collective-permute-start.1
  0.1 1.1 %constant_dynamic-slice_fusion = (bf16[2,4,64,128]{3,2,1,0:T(8,128)(2,1)S(1)}, bf16[2,4,64,128]{3,2,1,0:T(8,128)(2,1)S(1)}, bf16[2,4,64,128]{3,2,1,0:T(8,128)(2,1)S(1)}, bf16[2,4,64,128]{3,2,1,0:T(8,128)(2,1)S(1)}) fusion(bf16[2,4,64,512]{3,2,1,0:T(8,128)(2,1)} %param.6, s32[]{:T(128)S(6)} %select_n.75, s32[]{:T(128)S(6)} %select_n.74, s32[]{:T(128)S(6)} %select_n.72, ...), kind=kLoop, calls=%fused_computation.5 | loop fusion | bytes 1048592 | tf_op jit(solution)/shard_map/dynamic_slice | solution.py:379
  1.2 3.7 %collective-permute-start.6 = (bf16[2,4,64,128]{3,2,1,0:T(8,128)(2,1)S(1)}, bf16[2,4,64,128]{3,2,1,0:T(8,128)(2,1)S(1)}, u32[]{:S(2)}, u32[]{:S(2)}) collective-permute-start(bf16[2,4,64,128]{3,2,1,0:T(8,128)(2,1)S(1)} %get-tuple-element.57), channel_id=1, source_target_pairs={{0,24},{1,25},{2,26},{3,27},{4,28},{5,29},{6,30},{7,31},{8,16},{9,... | collective-permute-start | bytes 393224 | tf_op jit(solution)/shard_map/ppermute | solution.py:360
  4.9 0.2 collective-permute-start.3
  5.1 0.1 collective-permute-start
  5.3 1.0 %slice_bitcast_fusion = (bf16[2,64,512]{2,1,0:T(8,128)(2,1)S(1)}, bf16[2,64,512]{2,1,0:T(8,128)(2,1)S(1)}) fusion(bf16[2,4,64,512]{3,2,1,0:T(8,128)(2,1)} %param.6), kind=kLoop, calls=%fused_computation.3 | loop fusion | bytes 524288 | tf_op jit(solution)/shard_map/squeeze | solution.py:373
  6.2 1.3 %collective-permute-start.9 = (bf16[2,64,512]{2,1,0:T(8,128)(2,1)S(1)}, bf16[2,64,512]{2,1,0:T(8,128)(2,1)S(1)}, u32[]{:S(2)}, u32[]{:S(2)}) collective-permute-start(bf16[2,64,512]{2,1,0:T(8,128)(2,1)S(1)} %get-tuple-element.55), channel_id=1, source_target_pairs={{1,0},{2,1},{3,2},{5,4},{6,5},{7,6},{9,8},{10,9},{11,10},{13,12},{... | collective-permute-start | bytes 393224 | tf_op jit(solution)/shard_map/ppermute | solution.py:360
  7.5 0.1 pad_add_fusion.refs_0_.meta
  7.6 0.0 collective-permute-done.1.refs_2_
  7.6 4.0 %collective-permute-start.8 = (bf16[2,64,512]{2,1,0:T(8,128)(2,1)S(1)}, bf16[2,64,512]{2,1,0:T(8,128)(2,1)S(1)}, u32[]{:S(2)}, u32[]{:S(2)}) collective-permute-start(bf16[2,64,512]{2,1,0:T(8,128)(2,1)S(1)} %get-tuple-element.56), channel_id=1, source_target_pairs={{0,1},{1,2},{2,3},{4,5},{5,6},{6,7},{8,9},{9,10},{10,11},{12,13},{... | collective-permute-start | bytes 393224 | tf_op jit(solution)/shard_map/ppermute | solution.py:360
  11.6 0.0 copy-start
  11.6 1.5 %copy-done = bf16[27,64,512]{2,1,0:T(8,128)(2,1)S(1)} copy-done((bf16[27,64,512]{2,1,0:T(8,128)(2,1)S(1)}, bf16[27,64,512]{2,1,0:T(8,128)(2,1)}, u32[]{:S(2)}) %copy-start) | copy-done | bytes 1769496
  13.1 0.9 merge_kernel_slices.1.refs_1_
  14.0 1.2 %collective-permute-start.2 = (bf16[2,4,64,128]{3,2,1,0:T(8,128)(2,1)S(1)}, bf16[2,4,64,128]{3,2,1,0:T(8,128)(2,1)S(1)}, u32[]{:S(2)}, u32[]{:S(2)}) collective-permute-start(bf16[2,4,64,128]{3,2,1,0:T(8,128)(2,1)S(1)} %get-tuple-element.59.refs_2_), channel_id=1, source_target_pairs={{0,4},{1,5},{2,6},{3,7},{4,0},{5,1},{6,2},{7,3},{8,12},{9,13},{10,... | collective-permute-start | bytes 393224 | tf_op jit(solution)/shard_map/ppermute | solution.py:360
  15.2 0.0 collective-permute-done.3.refs_2_
  15.2 0.1 collective-permute-start.7
  15.2 0.0 collective-permute-done.refs_3_
  15.3 0.4 collective-permute-start.4
  15.7 0.1 collective-permute-start.5
  15.8 0.6 split_halo_rows.1
  16.4 0.1 collective-permute-done.7.refs_7_
  16.5 0.2 collective-permute-done.4.refs_5_
  16.7 0.3 collective-permute-done.5.refs_6_
  17.0 2.9 %conv_inner.2 = (bf16[256,512]{1,0:T(8,128)(2,1)S(1)}, bf16[256,512]{1,0:T(8,128)(2,1)S(1)}) custom-call(s32[3]{0:T(128)S(1)} %pad_add_fusion.refs_0_.meta, bf16[3,9,128,512]{3,2,1,0:T(8,128)(2,1)S(1)} %merge_kernel_slices.1.refs_1_, bf16[2,4,64,128]{3,2,1,0:T(8,128)(2,1)S(1)} %collective-permute-done.3.refs_2_, ...), custom_call_target="tpu_custom_call" | custom-call | flops 99999997952 | bytes 1000 | tf_op jit(solution)/shard_map/conv_inner/pallas_call | solution.py:200
  19.9 1.7 %collective-permute-start.11 = (bf16[256,512]{1,0:T(8,128)(2,1)S(1)}, bf16[256,512]{1,0:T(8,128)(2,1)S(1)}, u32[]{:S(2)}, u32[]{:S(2)}) collective-permute-start(bf16[256,512]{1,0:T(8,128)(2,1)S(1)} %get-tuple-element.32.refs_8_), channel_id=1, source_target_pairs={{0,8},{1,9},{2,10},{3,11},{4,20},{5,21},{6,22},{7,23},{8,0},{9,1},... | collective-permute-start | bytes 786440 | tf_op jit(solution)/shard_map/ppermute | solution.py:360
  21.6 0.1 collective-permute-start.14
  21.7 1.4 %collective-permute-start.15 = (bf16[2,2,64,128]{3,2,1,0:T(8,128)(2,1)S(1)}, bf16[2,2,64,128]{3,2,1,0:T(8,128)(2,1)S(1)}, u32[]{:S(2)}, u32[]{:S(2)}) collective-permute-start(bf16[2,2,64,128]{3,2,1,0:T(8,128)(2,1)S(1)} %get-tuple-element.42), channel_id=1, source_target_pairs={{0,16},{1,17},{2,18},{3,19},{4,12},{5,13},{6,14},{7,15},{8,24},{9,... | collective-permute-start | bytes 196616 | tf_op jit(solution)/shard_map/ppermute | solution.py:360
  23.0 1.2 %collective-permute-start.16 = (bf16[2,2,64,128]{3,2,1,0:T(8,128)(2,1)S(1)}, bf16[2,2,64,128]{3,2,1,0:T(8,128)(2,1)S(1)}, u32[]{:S(2)}, u32[]{:S(2)}) collective-permute-start(bf16[2,2,64,128]{3,2,1,0:T(8,128)(2,1)S(1)} %get-tuple-element.43), channel_id=1, source_target_pairs={{0,24},{1,25},{2,26},{3,27},{4,28},{5,29},{6,30},{7,31},{8,16},{9,... | collective-permute-start | bytes 196616 | tf_op jit(solution)/shard_map/ppermute | solution.py:360
  24.2 0.1 collective-permute-start.10
  24.3 2.8 %conv_inner.3 = (f32[256,512]{1,0:T(8,128)S(1)}, f32[256,512]{1,0:T(8,128)S(1)}) custom-call(s32[3]{0:T(128)S(1)} %pad_add_fusion.refs_0_.meta, bf16[3,9,128,512]{3,2,1,0:T(8,128)(2,1)S(1)} %merge_kernel_slices.1.refs_1_, bf16[2,4,64,128]{3,2,1,0:T(8,128)(2,1)S(1)} %get-tuple-element.59.refs_2_, bf16[2,4,64,128]{3,2,1,0:T(8,128)(2,1)S(1)} %collective-permute-done.refs_3_, ...), custom_call_target="tpu_custom_call" | custom-call | flops 99999997952 | bytes 1000 | tf_op jit(solution)/shard_map/conv_inner/pallas_call | solution.py:200
  27.2 0.1 collective-permute-done.14.refs_1_
  27.2 0.7 collective-permute-done.16.refs_3_
  28.0 2.9 %collective-permute-start.17 = (bf16[4,2,2,64,128]{4,3,2,1,0:T(8,128)(2,1)S(1)}, bf16[4,2,2,64,128]{4,3,2,1,0:T(8,128)(2,1)S(1)}, u32[]{:S(2)}, u32[]{:S(2)}) collective-permute-start(bf16[4,2,2,64,128]{4,3,2,1,0:T(8,128)(2,1)S(1)} %stack_halo_rows.1.refs_8_), channel_id=1, source_target_pairs={{0,4},{1,5},{2,6},{3,7},{4,0},{5,1},{6,2},{7,3},{8,12},{9,13},{10,... | collective-permute-start | bytes 786440 | tf_op jit(solution)/shard_map/ppermute | solution.py:360
  30.9 0.4 collective-permute-done.10.refs_2_.refs_1_
  31.3 0.8 sum_parts.4.refs_10_
  32.1 1.4 %collective-permute-start.12 = (bf16[256,512]{1,0:T(8,128)(2,1)}, bf16[256,512]{1,0:T(8,128)(2,1)}, u32[]{:S(2)}, u32[]{:S(2)}) collective-permute-start(bf16[256,512]{1,0:T(8,128)(2,1)} %sum_parts.4.refs_10_), channel_id=1, source_target_pairs={{0,16},{1,17},{2,18},{3,19},{4,12},{5,13},{6,14},{7,15},{8,24},{9,... | collective-permute-start | bytes 786440 | tf_op jit(solution)/shard_map/ppermute | solution.py:360
  33.5 3.3 %conv_rim.2 = (bf16[256,512]{1,0:T(8,128)(2,1)S(1)}, bf16[256,512]{1,0:T(8,128)(2,1)S(1)}) custom-call(s32[3]{0:T(128)S(1)} %pad_add_fusion.refs_0_.meta, bf16[3,9,128,512]{3,2,1,0:T(8,128)(2,1)S(1)} %merge_kernel_slices.1.refs_1_, bf16[2,4,64,128]{3,2,1,0:T(8,128)(2,1)S(1)} %collective-permute-done.3.refs_2_, ...), custom_call_target="tpu_custom_call" | custom-call | flops 99999997952 | bytes 1000 | tf_op jit(solution)/shard_map/conv_rim/pallas_call | solution.py:200
  36.8 1.3 %collective-permute-start.18 = (bf16[256,512]{1,0:T(8,128)(2,1)S(1)}, bf16[256,512]{1,0:T(8,128)(2,1)S(1)}, u32[]{:S(2)}, u32[]{:S(2)}) collective-permute-start(bf16[256,512]{1,0:T(8,128)(2,1)S(1)} %get-tuple-element.46), channel_id=1, source_target_pairs={{0,8},{1,9},{2,10},{3,11},{4,20},{5,21},{6,22},{7,23},{8,0},{9,1},... | collective-permute-start | bytes 786440 | tf_op jit(solution)/shard_map/ppermute | solution.py:360
  38.1 0.2 collective-permute-start.19
  38.4 2.9 %conv_rim.3 = (f32[256,512]{1,0:T(8,128)S(1)}, f32[256,512]{1,0:T(8,128)S(1)}) custom-call(s32[3]{0:T(128)S(1)} %pad_add_fusion.refs_0_.meta, bf16[3,9,128,512]{3,2,1,0:T(8,128)(2,1)S(1)} %merge_kernel_slices.1.refs_1_, bf16[2,4,64,128]{3,2,1,0:T(8,128)(2,1)S(1)} %get-tuple-element.59.refs_2_, bf16[2,4,64,128]{3,2,1,0:T(8,128)(2,1)S(1)} %collective-permute-done.refs_3_, ...), custom_call_target="tpu_custom_call" | custom-call | flops 99999997952 | bytes 1000 | tf_op jit(solution)/shard_map/conv_rim/pallas_call | solution.py:200
  41.2 0.0 copy-start.3
  41.2 0.0 copy-start.4
  41.2 0.0 copy-start.5
  41.3 0.0 copy-start.6
  41.3 1.1 %collective-permute-done.18.refs_2_.refs_1_ = bf16[256,512]{1,0:T(8,128)(2,1)S(1)} collective-permute-done((bf16[256,512]{1,0:T(8,128)(2,1)S(1)}, bf16[256,512]{1,0:T(8,128)(2,1)S(1)}, u32[]{:S(2)}, u32[]{:S(2)}) %collective-permute-start.18) | collective-permute-done | bytes 262176 | tf_op jit(solution)/shard_map/ppermute | solution.py:360
  42.4 2.8 %collective-permute-done.19.refs_1_ = bf16[256,512]{1,0:T(8,128)(2,1)S(1)} collective-permute-done((bf16[256,512]{1,0:T(8,128)(2,1)S(1)}, bf16[256,512]{1,0:T(8,128)(2,1)S(1)}, u32[]{:S(2)}, u32[]{:S(2)}) %collective-permute-start.19) | collective-permute-done | bytes 262176 | tf_op jit(solution)/shard_map/ppermute | solution.py:360
  45.2 0.1 sum_parts.6
  45.3 1.2 %collective-permute-start.20 = (bf16[256,512]{1,0:T(8,128)(2,1)S(1)}, bf16[256,512]{1,0:T(8,128)(2,1)S(1)}, u32[]{:S(2)}, u32[]{:S(2)}) collective-permute-start(bf16[256,512]{1,0:T(8,128)(2,1)S(1)} %sum_parts.6), channel_id=1, source_target_pairs={{0,16},{1,17},{2,18},{3,19},{4,12},{5,13},{6,14},{7,15},{8,24},{9,... | collective-permute-start | bytes 786440 | tf_op jit(solution)/shard_map/ppermute | solution.py:360
  46.5 1.0 %sum_parts.5 = (bf16[128,512]{1,0:T(8,128)(2,1)S(1)}, bf16[128,512]{1,0:T(8,128)(2,1)S(1)}) custom-call(f32[256,512]{1,0:T(8,128)S(1)} %get-tuple-element.33.refs_0_, bf16[256,512]{1,0:T(8,128)(2,1)S(1)} %copy-done.2, bf16[256,512]{1,0:T(8,128)(2,1)} %collective-permute-done.12.refs_2_), custom_call_target="tpu_custom_call" | custom-call | tf_op jit(solution)/shard_map/sum_parts/pallas_call | solution.py:226
  47.5 5.7 %collective-permute-start.13 = (bf16[128,512]{1,0:T(8,128)(2,1)S(1)}, bf16[128,512]{1,0:T(8,128)(2,1)S(1)}, u32[]{:S(2)}, u32[]{:S(2)}) collective-permute-start(bf16[128,512]{1,0:T(8,128)(2,1)S(1)} %get-tuple-element.36), channel_id=1, source_target_pairs={{0,0},{1,1},{2,4},{3,5},{4,2},{5,3},{6,6},{7,7},{8,8},{9,9},{10,12... | collective-permute-start | bytes 393224 | tf_op jit(solution)/shard_map/ppermute | solution.py:360
  53.2 0.1 collective-permute-start.22
  53.3 0.1 sum_parts.7
  53.4 4.7 %collective-permute-start.21 = (bf16[128,512]{1,0:T(8,128)(2,1)S(1)}, bf16[128,512]{1,0:T(8,128)(2,1)S(1)}, u32[]{:S(2)}, u32[]{:S(2)}) collective-permute-start(bf16[128,512]{1,0:T(8,128)(2,1)S(1)} %get-tuple-element.48), channel_id=1, source_target_pairs={{0,0},{1,1},{2,4},{3,5},{4,2},{5,3},{6,6},{7,7},{8,8},{9,9},{10,12... | collective-permute-start | bytes 393224 | tf_op jit(solution)/shard_map/ppermute | solution.py:360
  58.1 0.8 collective-permute-start.23
  58.9 0.7 collective-permute-done.22.refs_2_
  59.6 3.2 %collective-permute-done.21.refs_1_ = bf16[128,512]{1,0:T(8,128)(2,1)S(1)} collective-permute-done((bf16[128,512]{1,0:T(8,128)(2,1)S(1)}, bf16[128,512]{1,0:T(8,128)(2,1)S(1)}, u32[]{:S(2)}, u32[]{:S(2)}) %collective-permute-start.21) | collective-permute-done | bytes 131104 | tf_op jit(solution)/shard_map/ppermute | solution.py:360
  62.8 1.7 %collective-permute-done.23.refs_3_ = bf16[128,512]{1,0:T(8,128)(2,1)S(1)} collective-permute-done((bf16[128,512]{1,0:T(8,128)(2,1)S(1)}, bf16[128,512]{1,0:T(8,128)(2,1)S(1)}, u32[]{:S(2)}, u32[]{:S(2)}) %collective-permute-start.23) | collective-permute-done | bytes 131104 | tf_op jit(solution)/shard_map/ppermute | solution.py:360
  64.5 1.3 %collective-permute-done.27.refs_7_ = bf16[128,512]{1,0:T(8,128)(2,1)S(1)} collective-permute-done((bf16[128,512]{1,0:T(8,128)(2,1)S(1)}, bf16[128,512]{1,0:T(8,128)(2,1)S(1)}, u32[]{:S(2)}, u32[]{:S(2)}) %collective-permute-start.27) | collective-permute-done | bytes 131104 | tf_op jit(solution)/shard_map/ppermute | solution.py:360
  65.9 4.4 %attend.1 = (bf16[4,64,512]{2,1,0:T(8,128)(2,1)S(1)}, bf16[4,64,512]{2,1,0:T(8,128)(2,1)S(1)}) custom-call(bf16[128,512]{1,0:T(8,128)(2,1)S(1)} %collective-permute-done.13.refs_0_, bf16[128,512]{1,0:T(8,128)(2,1)S(1)} %collective-permute-done.21.refs_1_, bf16[128,512]{1,0:T(8,128)(2,1)S(1)} %collective-permute-done.22.refs_2_, ...), custom_call_target="tpu_custom_call" | custom-call | flops 2684354560 | bytes 3145728 | tf_op jit(solution)/shard_map/attend/pallas_call | solution.py:331
  70.3 2.7 %collective-permute-start.28 = (bf16[4,64,512]{2,1,0:T(8,128)(2,1)S(1)}, bf16[4,64,512]{2,1,0:T(8,128)(2,1)S(1)}, u32[]{:S(2)}, u32[]{:S(2)}) collective-permute-start(bf16[4,64,512]{2,1,0:T(8,128)(2,1)S(1)} %get-tuple-element.51), channel_id=1, source_target_pairs={{1,0},{0,1},{5,2},{4,3},{3,4},{2,5},{7,6},{6,7},{9,8},{8,9},{13,10... | collective-permute-start | bytes 786440 | tf_op jit(solution)/shard_map/ppermute | solution.py:457
  72.9 2.2 %collective-permute-start.29 = (bf16[4,64,512]{2,1,0:T(8,128)(2,1)S(1)}, bf16[4,64,512]{2,1,0:T(8,128)(2,1)S(1)}, u32[]{:S(2)}, u32[]{:S(2)}) collective-permute-start(bf16[4,64,512]{2,1,0:T(8,128)(2,1)S(1)} %get-tuple-element.52), channel_id=1, source_target_pairs={{0,0},{1,1},{4,2},{5,3},{2,4},{3,5},{6,6},{7,7},{8,8},{9,9},{12,10... | collective-permute-start | bytes 786440 | tf_op jit(solution)/shard_map/ppermute | solution.py:457
  75.2 5.5 %collective-permute-done.28 = bf16[4,64,512]{2,1,0:T(8,128)(2,1)S(1)} collective-permute-done((bf16[4,64,512]{2,1,0:T(8,128)(2,1)S(1)}, bf16[4,64,512]{2,1,0:T(8,128)(2,1)S(1)}, u32[]{:S(2)}, u32[]{:S(2)}) %collective-permute-start.28) | collective-permute-done | bytes 262176 | tf_op jit(solution)/shard_map/ppermute | solution.py:457
  80.7 5.0 %collective-permute-done.29 = bf16[4,64,512]{2,1,0:T(8,128)(2,1)S(1)} collective-permute-done((bf16[4,64,512]{2,1,0:T(8,128)(2,1)S(1)}, bf16[4,64,512]{2,1,0:T(8,128)(2,1)S(1)}, u32[]{:S(2)}, u32[]{:S(2)}) %collective-permute-start.29) | collective-permute-done | bytes 262176 | tf_op jit(solution)/shard_map/ppermute | solution.py:457
  85.8 0.8 pad_maximum_fusion
  (27 shorter events, 0.1 us)
Async XLA Ops:
  0.0 7.6 %collective-permute-start.1 = (bf16[9,3,64,512]{3,2,1,0:T(8,128)(2,1)}, bf16[9,3,64,512]{3,2,1,0:T(8,128)(2,1)S(1)}, u32[]{:S(2)}, u32[]{:S(2)}) collective-permute-start(bf16[9,3,64,512]{3,2,1,0:T(8,128)(2,1)} %bitcast.16), channel_id=1, source_target_pairs={{0,4},{1,5},{2,6},{3,7},{4,0},{5,1},{6,2},{7,3},{8,12},{9,13},{10,... | collective-permute-start | bytes 5308424 | tf_op jit(solution)/shard_map/ppermute | solution.py:360
  1.2 12.7 %collective-permute-start.6 = (bf16[2,4,64,128]{3,2,1,0:T(8,128)(2,1)S(1)}, bf16[2,4,64,128]{3,2,1,0:T(8,128)(2,1)S(1)}, u32[]{:S(2)}, u32[]{:S(2)}) collective-permute-start(bf16[2,4,64,128]{3,2,1,0:T(8,128)(2,1)S(1)} %get-tuple-element.57), channel_id=1, source_target_pairs={{0,24},{1,25},{2,26},{3,27},{4,28},{5,29},{6,30},{7,31},{8,16},{9,... | collective-permute-start | bytes 393224 | tf_op jit(solution)/shard_map/ppermute | solution.py:360
  4.9 10.3 %collective-permute-start.3 = (bf16[2,4,64,128]{3,2,1,0:T(8,128)(2,1)S(1)}, bf16[2,4,64,128]{3,2,1,0:T(8,128)(2,1)S(1)}, u32[]{:S(2)}, u32[]{:S(2)}) collective-permute-start(bf16[2,4,64,128]{3,2,1,0:T(8,128)(2,1)S(1)} %get-tuple-element.58), channel_id=1, source_target_pairs={{0,8},{1,9},{2,10},{3,11},{4,20},{5,21},{6,22},{7,23},{8,0},{9,1},... | collective-permute-start | bytes 393224 | tf_op jit(solution)/shard_map/ppermute | solution.py:360
  5.1 10.1 %collective-permute-start = (bf16[2,4,64,128]{3,2,1,0:T(8,128)(2,1)S(1)}, bf16[2,4,64,128]{3,2,1,0:T(8,128)(2,1)S(1)}, u32[]{:S(2)}, u32[]{:S(2)}) collective-permute-start(bf16[2,4,64,128]{3,2,1,0:T(8,128)(2,1)S(1)} %get-tuple-element.60), channel_id=1, source_target_pairs={{0,16},{1,17},{2,18},{3,19},{4,12},{5,13},{6,14},{7,15},{8,24},{9,... | collective-permute-start | bytes 393224 | tf_op jit(solution)/shard_map/ppermute | solution.py:360
  6.2 9.4 %collective-permute-start.9 = (bf16[2,64,512]{2,1,0:T(8,128)(2,1)S(1)}, bf16[2,64,512]{2,1,0:T(8,128)(2,1)S(1)}, u32[]{:S(2)}, u32[]{:S(2)}) collective-permute-start(bf16[2,64,512]{2,1,0:T(8,128)(2,1)S(1)} %get-tuple-element.55), channel_id=1, source_target_pairs={{1,0},{2,1},{3,2},{5,4},{6,5},{7,6},{9,8},{10,9},{11,10},{13,12},{... | collective-permute-start | bytes 393224 | tf_op jit(solution)/shard_map/ppermute | solution.py:360
  7.6 8.1 %collective-permute-start.8 = (bf16[2,64,512]{2,1,0:T(8,128)(2,1)S(1)}, bf16[2,64,512]{2,1,0:T(8,128)(2,1)S(1)}, u32[]{:S(2)}, u32[]{:S(2)}) collective-permute-start(bf16[2,64,512]{2,1,0:T(8,128)(2,1)S(1)} %get-tuple-element.56), channel_id=1, source_target_pairs={{0,1},{1,2},{2,3},{4,5},{5,6},{6,7},{8,9},{9,10},{10,11},{12,13},{... | collective-permute-start | bytes 393224 | tf_op jit(solution)/shard_map/ppermute | solution.py:360
  11.6 1.5 %copy-start = (bf16[27,64,512]{2,1,0:T(8,128)(2,1)S(1)}, bf16[27,64,512]{2,1,0:T(8,128)(2,1)}, u32[]{:S(2)}) copy-start(bf16[27,64,512]{2,1,0:T(8,128)(2,1)} %param.7) | copy-start | bytes 5308420
  14.0 2.4 %collective-permute-start.2 = (bf16[2,4,64,128]{3,2,1,0:T(8,128)(2,1)S(1)}, bf16[2,4,64,128]{3,2,1,0:T(8,128)(2,1)S(1)}, u32[]{:S(2)}, u32[]{:S(2)}) collective-permute-start(bf16[2,4,64,128]{3,2,1,0:T(8,128)(2,1)S(1)} %get-tuple-element.59.refs_2_), channel_id=1, source_target_pairs={{0,4},{1,5},{2,6},{3,7},{4,0},{5,1},{6,2},{7,3},{8,12},{9,13},{10,... | collective-permute-start | bytes 393224 | tf_op jit(solution)/shard_map/ppermute | solution.py:360
  15.2 1.3 %collective-permute-start.7 = (bf16[2,4,64,128]{3,2,1,0:T(8,128)(2,1)S(1)}, bf16[2,4,64,128]{3,2,1,0:T(8,128)(2,1)S(1)}, u32[]{:S(2)}, u32[]{:S(2)}) collective-permute-start(bf16[2,4,64,128]{3,2,1,0:T(8,128)(2,1)S(1)} %collective-permute-done.6.refs_3_), channel_id=1, source_target_pairs={{0,4},{1,5},{2,6},{3,7},{4,0},{5,1},{6,2},{7,3},{8,12},{9,13},{10,... | collective-permute-start | bytes 393224 | tf_op jit(solution)/shard_map/ppermute | solution.py:360
  15.3 1.4 %collective-permute-start.4 = (bf16[2,4,64,128]{3,2,1,0:T(8,128)(2,1)S(1)}, bf16[2,4,64,128]{3,2,1,0:T(8,128)(2,1)S(1)}, u32[]{:S(2)}, u32[]{:S(2)}) collective-permute-start(bf16[2,4,64,128]{3,2,1,0:T(8,128)(2,1)S(1)} %collective-permute-done.3.refs_2_), channel_id=1, source_target_pairs={{0,4},{1,5},{2,6},{3,7},{4,0},{5,1},{6,2},{7,3},{8,12},{9,13},{10,... | collective-permute-start | bytes 393224 | tf_op jit(solution)/shard_map/ppermute | solution.py:360
  15.7 1.3 %collective-permute-start.5 = (bf16[2,4,64,128]{3,2,1,0:T(8,128)(2,1)S(1)}, bf16[2,4,64,128]{3,2,1,0:T(8,128)(2,1)S(1)}, u32[]{:S(2)}, u32[]{:S(2)}) collective-permute-start(bf16[2,4,64,128]{3,2,1,0:T(8,128)(2,1)S(1)} %collective-permute-done.refs_3_), channel_id=1, source_target_pairs={{0,4},{1,5},{2,6},{3,7},{4,0},{5,1},{6,2},{7,3},{8,12},{9,13},{10,... | collective-permute-start | bytes 393224 | tf_op jit(solution)/shard_map/ppermute | solution.py:360
  19.9 11.4 %collective-permute-start.11 = (bf16[256,512]{1,0:T(8,128)(2,1)S(1)}, bf16[256,512]{1,0:T(8,128)(2,1)S(1)}, u32[]{:S(2)}, u32[]{:S(2)}) collective-permute-start(bf16[256,512]{1,0:T(8,128)(2,1)S(1)} %get-tuple-element.32.refs_8_), channel_id=1, source_target_pairs={{0,8},{1,9},{2,10},{3,11},{4,20},{5,21},{6,22},{7,23},{8,0},{9,1},... | collective-permute-start | bytes 786440 | tf_op jit(solution)/shard_map/ppermute | solution.py:360
  21.6 5.6 %collective-permute-start.14 = (bf16[2,2,64,128]{3,2,1,0:T(8,128)(2,1)S(1)}, bf16[2,2,64,128]{3,2,1,0:T(8,128)(2,1)S(1)}, u32[]{:S(2)}, u32[]{:S(2)}) collective-permute-start(bf16[2,2,64,128]{3,2,1,0:T(8,128)(2,1)S(1)} %get-tuple-element.41), channel_id=1, source_target_pairs={{0,8},{1,9},{2,10},{3,11},{4,20},{5,21},{6,22},{7,23},{8,0},{9,1},... | collective-permute-start | bytes 196616 | tf_op jit(solution)/shard_map/ppermute | solution.py:360
  21.7 5.6 %collective-permute-start.15 = (bf16[2,2,64,128]{3,2,1,0:T(8,128)(2,1)S(1)}, bf16[2,2,64,128]{3,2,1,0:T(8,128)(2,1)S(1)}, u32[]{:S(2)}, u32[]{:S(2)}) collective-permute-start(bf16[2,2,64,128]{3,2,1,0:T(8,128)(2,1)S(1)} %get-tuple-element.42), channel_id=1, source_target_pairs={{0,16},{1,17},{2,18},{3,19},{4,12},{5,13},{6,14},{7,15},{8,24},{9,... | collective-permute-start | bytes 196616 | tf_op jit(solution)/shard_map/ppermute | solution.py:360
  23.0 4.9 %collective-permute-start.16 = (bf16[2,2,64,128]{3,2,1,0:T(8,128)(2,1)S(1)}, bf16[2,2,64,128]{3,2,1,0:T(8,128)(2,1)S(1)}, u32[]{:S(2)}, u32[]{:S(2)}) collective-permute-start(bf16[2,2,64,128]{3,2,1,0:T(8,128)(2,1)S(1)} %get-tuple-element.43), channel_id=1, source_target_pairs={{0,24},{1,25},{2,26},{3,27},{4,28},{5,29},{6,30},{7,31},{8,16},{9,... | collective-permute-start | bytes 196616 | tf_op jit(solution)/shard_map/ppermute | solution.py:360
  24.2 7.0 %collective-permute-start.10 = (bf16[256,512]{1,0:T(8,128)(2,1)S(1)}, bf16[256,512]{1,0:T(8,128)(2,1)S(1)}, u32[]{:S(2)}, u32[]{:S(2)}) collective-permute-start(bf16[256,512]{1,0:T(8,128)(2,1)S(1)} %get-tuple-element.34), channel_id=1, source_target_pairs={{0,8},{1,9},{2,10},{3,11},{4,20},{5,21},{6,22},{7,23},{8,0},{9,1},... | collective-permute-start | bytes 786440 | tf_op jit(solution)/shard_map/ppermute | solution.py:360
  28.0 5.5 %collective-permute-start.17 = (bf16[4,2,2,64,128]{4,3,2,1,0:T(8,128)(2,1)S(1)}, bf16[4,2,2,64,128]{4,3,2,1,0:T(8,128)(2,1)S(1)}, u32[]{:S(2)}, u32[]{:S(2)}) collective-permute-start(bf16[4,2,2,64,128]{4,3,2,1,0:T(8,128)(2,1)S(1)} %stack_halo_rows.1.refs_8_), channel_id=1, source_target_pairs={{0,4},{1,5},{2,6},{3,7},{4,0},{5,1},{6,2},{7,3},{8,12},{9,13},{10,... | collective-permute-start | bytes 786440 | tf_op jit(solution)/shard_map/ppermute | solution.py:360
  31.3 5.5 %copy-start.1 = (bf16[256,512]{1,0:T(8,128)(2,1)}, bf16[256,512]{1,0:T(8,128)(2,1)S(1)}, u32[]{:S(2)}) copy-start(bf16[256,512]{1,0:T(8,128)(2,1)S(1)} %collective-permute-done.10.refs_2_.refs_1_) | copy-start | bytes 786436
  32.1 14.4 %collective-permute-start.12 = (bf16[256,512]{1,0:T(8,128)(2,1)}, bf16[256,512]{1,0:T(8,128)(2,1)}, u32[]{:S(2)}, u32[]{:S(2)}) collective-permute-start(bf16[256,512]{1,0:T(8,128)(2,1)} %sum_parts.4.refs_10_), channel_id=1, source_target_pairs={{0,16},{1,17},{2,18},{3,19},{4,12},{5,13},{6,14},{7,15},{8,24},{9,... | collective-permute-start | bytes 786440 | tf_op jit(solution)/shard_map/ppermute | solution.py:360
  36.8 5.6 %collective-permute-start.18 = (bf16[256,512]{1,0:T(8,128)(2,1)S(1)}, bf16[256,512]{1,0:T(8,128)(2,1)S(1)}, u32[]{:S(2)}, u32[]{:S(2)}) collective-permute-start(bf16[256,512]{1,0:T(8,128)(2,1)S(1)} %get-tuple-element.46), channel_id=1, source_target_pairs={{0,8},{1,9},{2,10},{3,11},{4,20},{5,21},{6,22},{7,23},{8,0},{9,1},... | collective-permute-start | bytes 786440 | tf_op jit(solution)/shard_map/ppermute | solution.py:360
  38.1 8.4 %copy-start.2 = (bf16[256,512]{1,0:T(8,128)(2,1)S(1)}, bf16[256,512]{1,0:T(8,128)(2,1)}, u32[]{:S(2)}) copy-start(bf16[256,512]{1,0:T(8,128)(2,1)} %copy-done.1) | copy-start | bytes 786436
  38.1 7.1 %collective-permute-start.19 = (bf16[256,512]{1,0:T(8,128)(2,1)S(1)}, bf16[256,512]{1,0:T(8,128)(2,1)S(1)}, u32[]{:S(2)}, u32[]{:S(2)}) collective-permute-start(bf16[256,512]{1,0:T(8,128)(2,1)S(1)} %get-tuple-element.44.refs_10_), channel_id=1, source_target_pairs={{0,8},{1,9},{2,10},{3,11},{4,20},{5,21},{6,22},{7,23},{8,0},{9,1},... | collective-permute-start | bytes 786440 | tf_op jit(solution)/shard_map/ppermute | solution.py:360
  41.2 24.6 %copy-start.3 = (bf16[512,512]{1,0:T(8,128)(2,1)S(1)}, bf16[512,512]{1,0:T(8,128)(2,1)}, u32[]{:S(2)}) copy-start(bf16[512,512]{1,0:T(8,128)(2,1)} %refs_8_.1) | copy-start | bytes 1572868
  41.2 24.6 %copy-start.4 = (bf16[512,512]{1,0:T(8,128)(2,1)S(1)}, bf16[512,512]{1,0:T(8,128)(2,1)}, u32[]{:S(2)}) copy-start(bf16[512,512]{1,0:T(8,128)(2,1)} %refs_9_.1) | copy-start | bytes 1572868
  41.2 24.6 %copy-start.5 = (bf16[512,512]{1,0:T(8,128)(2,1)S(1)}, bf16[512,512]{1,0:T(8,128)(2,1)}, u32[]{:S(2)}) copy-start(bf16[512,512]{1,0:T(8,128)(2,1)} %refs_10_.1) | copy-start | bytes 1572868
  41.3 24.6 %copy-start.6 = (bf16[512,512]{1,0:T(8,128)(2,1)S(1)}, bf16[512,512]{1,0:T(8,128)(2,1)}, u32[]{:S(2)}) copy-start(bf16[512,512]{1,0:T(8,128)(2,1)} %refs_11_.1) | copy-start | bytes 1572868
  45.3 8.0 %collective-permute-start.20 = (bf16[256,512]{1,0:T(8,128)(2,1)S(1)}, bf16[256,512]{1,0:T(8,128)(2,1)S(1)}, u32[]{:S(2)}, u32[]{:S(2)}) collective-permute-start(bf16[256,512]{1,0:T(8,128)(2,1)S(1)} %sum_parts.6), channel_id=1, source_target_pairs={{0,16},{1,17},{2,18},{3,19},{4,12},{5,13},{6,14},{7,15},{8,24},{9,... | collective-permute-start | bytes 786440 | tf_op jit(solution)/shard_map/ppermute | solution.py:360
  47.5 11.4 %collective-permute-start.13 = (bf16[128,512]{1,0:T(8,128)(2,1)S(1)}, bf16[128,512]{1,0:T(8,128)(2,1)S(1)}, u32[]{:S(2)}, u32[]{:S(2)}) collective-permute-start(bf16[128,512]{1,0:T(8,128)(2,1)S(1)} %get-tuple-element.36), channel_id=1, source_target_pairs={{0,0},{1,1},{2,4},{3,5},{4,2},{5,3},{6,6},{7,7},{8,8},{9,9},{10,12... | collective-permute-start | bytes 393224 | tf_op jit(solution)/shard_map/ppermute | solution.py:360
  53.2 6.4 %collective-permute-start.22 = (bf16[128,512]{1,0:T(8,128)(2,1)S(1)}, bf16[128,512]{1,0:T(8,128)(2,1)S(1)}, u32[]{:S(2)}, u32[]{:S(2)}) collective-permute-start(bf16[128,512]{1,0:T(8,128)(2,1)S(1)} %get-tuple-element.49), channel_id=1, source_target_pairs={{0,1},{1,0},{2,5},{3,4},{4,3},{5,2},{6,7},{7,6},{8,9},{9,8},{10,13... | collective-permute-start | bytes 393224 | tf_op jit(solution)/shard_map/ppermute | solution.py:360
  53.4 9.4 %collective-permute-start.21 = (bf16[128,512]{1,0:T(8,128)(2,1)S(1)}, bf16[128,512]{1,0:T(8,128)(2,1)S(1)}, u32[]{:S(2)}, u32[]{:S(2)}) collective-permute-start(bf16[128,512]{1,0:T(8,128)(2,1)S(1)} %get-tuple-element.48), channel_id=1, source_target_pairs={{0,0},{1,1},{2,4},{3,5},{4,2},{5,3},{6,6},{7,7},{8,8},{9,9},{10,12... | collective-permute-start | bytes 393224 | tf_op jit(solution)/shard_map/ppermute | solution.py:360
  58.1 6.4 %collective-permute-start.23 = (bf16[128,512]{1,0:T(8,128)(2,1)S(1)}, bf16[128,512]{1,0:T(8,128)(2,1)S(1)}, u32[]{:S(2)}, u32[]{:S(2)}) collective-permute-start(bf16[128,512]{1,0:T(8,128)(2,1)S(1)} %get-tuple-element.50), channel_id=1, source_target_pairs={{0,1},{1,0},{2,5},{3,4},{4,3},{5,2},{6,7},{7,6},{8,9},{9,8},{10,13... | collective-permute-start | bytes 393224 | tf_op jit(solution)/shard_map/ppermute | solution.py:360
  58.9 5.6 %collective-permute-start.24 = (bf16[128,512]{1,0:T(8,128)(2,1)S(1)}, bf16[128,512]{1,0:T(8,128)(2,1)S(1)}, u32[]{:S(2)}, u32[]{:S(2)}) collective-permute-start(bf16[128,512]{1,0:T(8,128)(2,1)S(1)} %collective-permute-done.13.refs_0_), channel_id=1, source_target_pairs={{0,4},{1,5},{2,6},{3,7},{4,0},{5,1},{6,2},{7,3},{8,12},{9,13},{10,... | collective-permute-start | bytes 393224 | tf_op jit(solution)/shard_map/ppermute | solution.py:360
  59.6 4.9 %collective-permute-start.26 = (bf16[128,512]{1,0:T(8,128)(2,1)S(1)}, bf16[128,512]{1,0:T(8,128)(2,1)S(1)}, u32[]{:S(2)}, u32[]{:S(2)}) collective-permute-start(bf16[128,512]{1,0:T(8,128)(2,1)S(1)} %collective-permute-done.22.refs_2_), channel_id=1, source_target_pairs={{0,4},{1,5},{2,6},{3,7},{4,0},{5,1},{6,2},{7,3},{8,12},{9,13},{10,... | collective-permute-start | bytes 393224 | tf_op jit(solution)/shard_map/ppermute | solution.py:360
  62.8 1.7 %collective-permute-start.25 = (bf16[128,512]{1,0:T(8,128)(2,1)S(1)}, bf16[128,512]{1,0:T(8,128)(2,1)S(1)}, u32[]{:S(2)}, u32[]{:S(2)}) collective-permute-start(bf16[128,512]{1,0:T(8,128)(2,1)S(1)} %collective-permute-done.21.refs_1_), channel_id=1, source_target_pairs={{0,4},{1,5},{2,6},{3,7},{4,0},{5,1},{6,2},{7,3},{8,12},{9,13},{10,... | collective-permute-start | bytes 393224 | tf_op jit(solution)/shard_map/ppermute | solution.py:360
  64.5 1.3 %collective-permute-start.27 = (bf16[128,512]{1,0:T(8,128)(2,1)S(1)}, bf16[128,512]{1,0:T(8,128)(2,1)S(1)}, u32[]{:S(2)}, u32[]{:S(2)}) collective-permute-start(bf16[128,512]{1,0:T(8,128)(2,1)S(1)} %collective-permute-done.23.refs_3_), channel_id=1, source_target_pairs={{0,4},{1,5},{2,6},{3,7},{4,0},{5,1},{6,2},{7,3},{8,12},{9,13},{10,... | collective-permute-start | bytes 393224 | tf_op jit(solution)/shard_map/ppermute | solution.py:360
  70.3 10.5 %collective-permute-start.28 = (bf16[4,64,512]{2,1,0:T(8,128)(2,1)S(1)}, bf16[4,64,512]{2,1,0:T(8,128)(2,1)S(1)}, u32[]{:S(2)}, u32[]{:S(2)}) collective-permute-start(bf16[4,64,512]{2,1,0:T(8,128)(2,1)S(1)} %get-tuple-element.51), channel_id=1, source_target_pairs={{1,0},{0,1},{5,2},{4,3},{3,4},{2,5},{7,6},{6,7},{9,8},{8,9},{13,10... | collective-permute-start | bytes 786440 | tf_op jit(solution)/shard_map/ppermute | solution.py:457
  72.9 12.8 %collective-permute-start.29 = (bf16[4,64,512]{2,1,0:T(8,128)(2,1)S(1)}, bf16[4,64,512]{2,1,0:T(8,128)(2,1)S(1)}, u32[]{:S(2)}, u32[]{:S(2)}) collective-permute-start(bf16[4,64,512]{2,1,0:T(8,128)(2,1)S(1)} %get-tuple-element.52), channel_id=1, source_target_pairs={{0,0},{1,1},{4,2},{5,3},{2,4},{3,5},{6,6},{7,7},{8,8},{9,9},{12,10... | collective-permute-start | bytes 786440 | tf_op jit(solution)/shard_map/ppermute | solution.py:457

commit v6 on v5

v6 whole, which is shorter than its diff:
```python
import functools

import jax
import jax.numpy as jnp
from jax import lax
from jax.experimental import pallas as pl
from jax.experimental.pallas import tpu as pltpu
from jax.sharding import PartitionSpec as P

G = 32
LANES = 128
CORES = 2

epsilon = 1e-06

BOTH = ("tm", "rows")
VMEM_LIMIT = 16 * 1024 * 1024


def everywhere(sizes, target):
    devices, depth = sizes
    pairs = []
    for t in range(devices):
        for z in range(depth):
            to = target(t, z)
            if to is not None:
                pairs.append((t * depth + z, to[0] * depth + to[1]))
    return pairs


def in_vmem(count):
    return [pl.BlockSpec(memory_space=pltpu.VMEM)] * count


def merge_kernel(group, *refs):
    meta, refs = refs[0], refs[1:]
    slices, out, sems = refs[:group], refs[group], refs[group + 1]
    chans_here = slices[0].shape[2]
    copies = []
    for lag in range(out.shape[0]):
        for step in range(group):
            owner = lax.rem(meta[1] - step + group, group)
            rows = pl.ds(pl.multiple_of(owner * chans_here, 16), chans_here)
            copies.append(
                pltpu.make_async_copy(
                    slices[step].at[:, lag], out.at[lag, :, rows], sems.at[lag, step]
                )
            )
    for copy in copies:
        copy.start()
    for copy in copies:
        copy.wait()


def merge_call(meta, slices):
    group = len(slices)
    taps, lags, chans_here, chans = slices[0].shape
    return pl.pallas_call(
        functools.partial(merge_kernel, group),
        out_shape=jax.ShapeDtypeStruct((lags, taps, group * chans_here, chans), jnp.bfloat16),
        in_specs=[pl.BlockSpec(memory_space=pltpu.SMEM)]
        + [pl.BlockSpec(memory_space=pltpu.HBM)]
        + [pl.BlockSpec(memory_space=pl.ANY)] * (group - 1),
        out_specs=pl.BlockSpec(memory_space=pltpu.VMEM),
        scratch_shapes=[pltpu.SemaphoreType.DMA((lags, group))],
        compiler_params=pltpu.CompilerParams(vmem_limit_bytes=VMEM_LIMIT),
        name="merge_kernel_slices",
    )(meta, *slices)


def partner(member, place):
    odd = member % 2 == 1
    if isinstance(member, int) and isinstance(place, int):
        return 3 - place if odd and place in (1, 2) else place
    swapped = jnp.where(jnp.logical_or(place == 1, place == 2), 3 - place, place)
    return jnp.where(odd, swapped, place)


def frame_call(meta, latents, above, below, parts):
    frames, rows_here, columns, chans = latents.shape
    width = chans // parts

    def kernel(meta, latents, above, below, *outs):
        for place, out in enumerate(outs):
            to = lax.bitwise_xor(meta[0], partner(meta[1], jnp.int32(place)))
            lanes = pl.ds(pl.multiple_of(to * width, width), width)
            out[:, 0] = above[:, :, lanes]
            out[:, 1 : 1 + rows_here] = latents[:, :, :, lanes]
            out[:, 1 + rows_here] = below[:, :, lanes]

    return pl.pallas_call(
        kernel,
        out_shape=[
            jax.ShapeDtypeStruct((frames, rows_here + 2, columns, width), latents.dtype)
        ]
        * parts,
        in_specs=[pl.BlockSpec(memory_space=pltpu.SMEM)] + in_vmem(3),
        out_specs=in_vmem(parts),
        compiler_params=pltpu.CompilerParams(vmem_limit_bytes=VMEM_LIMIT),
        name="frame_parts",
    )(meta, latents, above, below)


def conv_kernel(jobs, parts, group, frames, *refs):
    meta, weights, refs = refs[0], refs[1], refs[2:]
    dests = sorted({place for place, _ in jobs})
    held, refs = refs[: len(dests)], refs[len(dests) :]
    before, refs = refs[:parts], refs[parts:]
    outs, raw = refs[-1 - len(jobs) : -1], refs[-1]
    part, member, z = meta[0], meta[1], meta[2]
    lags, _, width, chans = weights.shape
    _, rows_framed, columns, _ = held[0].shape
    rows_here = rows_framed - 2

    first = member == 0
    for n, where in enumerate(dests):
        to = lax.bitwise_xor(part, partner(member, jnp.int32(where)))
        valid = jnp.logical_or(jnp.logical_not(first), to > 0)
        sender = jnp.where(first, group - 1, member - 1)
        want = jnp.where(first, jnp.maximum(to - 1, 0), to)
        place = partner(sender, lax.bitwise_xor(part, want))
        raw[n, frames:] = held[n][...]
        for i in range(parts):

            @pl.when(place == i)
            def _():
                raw[n, :frames] = before[i][...]

        @pl.when(jnp.logical_not(valid))
        def _():
            raw[n, :frames] = jnp.zeros_like(raw[n, :frames])

    side = 3

    def patches(a, b):
        pieces = []
        for where, p in jobs:
            f = lax.rem(z + p, frames) + a
            pieces.append(raw[dests.index(where), f, b : b + rows_here].reshape(-1, width))
        return jnp.concatenate(pieces, axis=0)

    lhs = jnp.concatenate([patches(a, b) for a in range(side) for b in range(side)], axis=1)
    count = lhs.shape[0]
    column = lax.broadcasted_iota(jnp.int32, (count, chans), 0) % columns
    total = None
    for lag in (1, 0, 2):
        product = jnp.dot(
            lhs, weights[lag].reshape(-1, chans), preferred_element_type=jnp.float32
        )
        if lag == 1:
            total = product
        elif lag == 0:
            total = total + jnp.where(column == 0, 0.0, pltpu.roll(product, 1, 0))
        else:
            moved = pltpu.roll(product, count - 1, 0)
            total = total + jnp.where(column == columns - 1, 0.0, moved)
    size = rows_here * columns
    for n, out in enumerate(outs):
        out[...] = total[n * size : (n + 1) * size].astype(out.dtype)


def conv_call(jobs, meta, weights, held, before, group, frames, out_type, after=()):
    parts = len(held)
    dests = sorted({place for place, _ in jobs})
    _, rows_framed, columns, width = held[0].shape
    lags, taps, _, chans = weights.shape
    count = (rows_framed - 2) * columns
    operands = [weights, *[held[n] for n in dests], *before, *after]
    return pl.pallas_call(
        functools.partial(conv_kernel, tuple(jobs), parts, group, frames),
        out_shape=[jax.ShapeDtypeStruct((count, chans), out_type)] * len(jobs),
        in_specs=[pl.BlockSpec(memory_space=pltpu.SMEM)] + in_vmem(len(operands)),
        out_specs=in_vmem(len(jobs)),
        scratch_shapes=[
            pltpu.VMEM((len(dests), 2 * frames, rows_framed, columns, width), jnp.bfloat16)
        ],
        compiler_params=pltpu.CompilerParams(vmem_limit_bytes=VMEM_LIMIT),
        cost_estimate=pl.CostEstimate(
            flops=10**11, bytes_accessed=2 * taps * lags * width * chans, transcendentals=0
        ),
        name="conv_sums",
    )(meta, *operands)


def sum_call(pieces, after=()):
    def kernel(*refs):
        total = refs[0][...].astype(jnp.float32)
        for ref in refs[1 : len(pieces)]:
            total = total + ref[...].astype(jnp.float32)
        refs[-1][...] = total.astype(refs[-1].dtype)

    return pl.pallas_call(
        kernel,
        out_shape=jax.ShapeDtypeStruct(pieces[0].shape, jnp.bfloat16),
        in_specs=in_vmem(len(pieces) + len(after)),
        out_specs=pl.BlockSpec(memory_space=pltpu.VMEM),
        compiler_params=pltpu.CompilerParams(vmem_limit_bytes=VMEM_LIMIT),
        name="sum_parts",
    )(*pieces, *after)


def attend_kernel(frames, share, *refs):
    all_count = frames * share
    tokens, refs = refs[:all_count], refs[all_count:]
    (wq, wk, wv, wo), refs = refs[:4], refs[4:]
    outs, (normed, keys, values) = refs[:frames], refs[frames:]
    size, chans = normed.shape
    per_group = chans // G

    tile_row = lax.broadcasted_iota(jnp.int32, (LANES, LANES), 0) // per_group
    tile_col = lax.broadcasted_iota(jnp.int32, (LANES, LANES), 1) // per_group
    same = (tile_row == tile_col).astype(jnp.float32).astype(jnp.bfloat16)

    def group_mean(sums):
        first = sums.astype(jnp.bfloat16)
        rest = sums - first.astype(jnp.float32)
        second = rest.astype(jnp.bfloat16)
        third = rest - second.astype(jnp.float32)
        tiles = []
        for tile in range(chans // LANES):
            lanes = slice(tile * LANES, (tile + 1) * LANES)
            stacked = jnp.concatenate(
                [
                    first.astype(jnp.float32)[:, lanes],
                    second.astype(jnp.float32)[:, lanes],
                    third[:, lanes],
                ],
                axis=0,
            ).astype(jnp.bfloat16)
            spread = jnp.dot(stacked, same, preferred_element_type=jnp.float32)
            tiles.append(jnp.sum(spread, axis=0, keepdims=True))
        return jnp.concatenate(tiles, axis=1) / (size * per_group)

    def folded(x):
        return jnp.sum(x.reshape(-1, 8, chans), axis=0)

    average = group_mean(sum(folded(ref[...].astype(jnp.float32)) for ref in tokens))

    def spread_of(ref):
        centered = ref[...].astype(jnp.float32) - average
        return folded(centered * centered)

    scale = lax.rsqrt(group_mean(sum(spread_of(ref) for ref in tokens)) + epsilon)
    place = 0
    for ref in tokens:
        rows = ref.shape[0]
        normed[pl.ds(place, rows)] = (
            (ref[...].astype(jnp.float32) - average) * scale
        ).astype(jnp.bfloat16)
        place += rows

    step = min(256, size)
    for start in range(0, size, step):
        x = normed[pl.ds(start, step)]
        keys[pl.ds(start, step)] = jnp.dot(
            x, wk[...], preferred_element_type=jnp.float32
        ).astype(jnp.bfloat16)
        values[pl.ds(start, step)] = jnp.dot(
            x, wv[...], preferred_element_type=jnp.float32
        ).astype(jnp.bfloat16)

    rows = tokens[0].shape[0]
    for p, out in enumerate(outs):
        queries = jnp.dot(
            normed[pl.ds(p * rows, rows)], wq[...], preferred_element_type=jnp.float32
        ).astype(jnp.bfloat16)
        scores = lax.dot_general(
            queries, keys[...], (((1,), (1,)), ((), ())), preferred_element_type=jnp.float32
        ) * chans ** (-0.5)
        row_max = jnp.max(scores, axis=1, keepdims=True)
        exp_weights = jnp.exp(scores - row_max).astype(jnp.bfloat16)
        denominator = jnp.sum(exp_weights.astype(jnp.float32), axis=1, keepdims=True)
        numerator = jnp.dot(exp_weights, values[...], preferred_element_type=jnp.float32)
        attended = (numerator / denominator).astype(jnp.bfloat16)
        summed = tokens[p][...].astype(jnp.float32) + jnp.dot(
            attended, wo[...], preferred_element_type=jnp.float32
        )
        out[...] = summed.astype(jnp.bfloat16)


def attend_call(own, others, weights):
    frames = len(own)
    share = 1 + len(others) // len(own)
    chans = own[0].shape[1]
    size = sum(x.shape[0] for x in own) * share
    mine = size // share
    out = jax.ShapeDtypeStruct(own[0].shape, jnp.bfloat16)
    operands = [*own, *others, *weights]
    return pl.pallas_call(
        functools.partial(attend_kernel, frames, share),
        out_shape=[out] * frames,
        in_specs=in_vmem(len(operands)),
        out_specs=in_vmem(frames),
        scratch_shapes=[pltpu.VMEM((size, chans), jnp.bfloat16)] * 3,
        compiler_params=pltpu.CompilerParams(vmem_limit_bytes=VMEM_LIMIT),
        cost_estimate=pl.CostEstimate(
            flops=2 * (2 * size * chans * chans + 2 * mine * chans * (chans + size)),
            bytes_accessed=8 * chans * chans + 2 * size * chans,
            transcendentals=mine * size,
        ),
        name="attend",
    )(*operands)


def body(latents, conv_weight, query_weight, key_weight, value_weight, out_weight):
    frames, rows_here, columns, chans = latents.shape
    taps, chans_here, _ = conv_weight.shape
    devices, depth = lax.axis_size("tm"), lax.axis_size("rows")
    sizes = (devices, depth)
    group = LANES // chans_here
    parts = devices // group
    width = group * chans_here
    t_index, z_index = lax.axis_index("tm"), lax.axis_index("rows")
    part, member = t_index // group, t_index % group
    meta = jnp.stack([part, member, z_index]).astype(jnp.int32)

    def permute(block, target):
        return lax.ppermute(block, BOTH, everywhere(sizes, target))

    def to_place(place):
        return lambda t, z: ((t // group ^ partner(t % group, place)) * group + t % group, z)

    def to_member(step):
        return lambda t, z: (t // group * group + (t + step) % group, z)

    split = conv_weight.reshape(taps // 3, 3, chans_here, chans)
    slices = [split] + [permute(split, to_member(step)) for step in range(1, group)]
    weights = merge_call(meta, slices)

    above = permute(latents[:, -1], lambda t, z: (t, z + 1) if z + 1 < depth else None)
    below = permute(latents[:, 0], lambda t, z: (t, z - 1) if z else None)

    above, weights = lax.optimization_barrier((above, weights))
    held = frame_call(meta, latents, above, below, parts)
    held = [permute(x, to_place(place)) if place else x for place, x in enumerate(held)]
    before = [permute(x, to_member(1)) for x in held]

    conv = functools.partial(
        conv_call,
        meta=meta,
        weights=weights,
        held=held,
        before=before,
        group=group,
        frames=frames,
    )

    sent, got = [], []
    for p in range(frames):
        sent.append(
            conv([(3, p), (1, p)], out_type=jnp.bfloat16, after=sent[-1][:1] if sent else ())
        )
        got.append([permute(x, to_place(1)) for x in sent[p]])
    token = sent[-1][0]
    kept, relays = [], []
    for p in range(frames):
        on, own_part = conv([(2, p), (0, p)], out_type=jnp.float32, after=(token,))
        token = sum_call([on, got[p][0]], after=got[p][1:])
        kept.append(own_part)
        relays.append(permute(token, to_place(2)))
    sums = [sum_call([kept[p], got[p][1], relays[p]]) for p in range(frames)]

    share = depth // frames

    def frame_home(t, z, p):
        frame = t % CORES * frames + (z + p) % frames
        slot = frame * share + z // frames
        return (t // CORES * CORES + slot % CORES, slot // CORES)

    def next_in_frame(t, z, step):
        slot = z * CORES + t % CORES
        slot = slot // share * share + (slot + step) % share
        return (t // CORES * CORES + slot % CORES, slot // CORES)

    own = [permute(x, lambda t, z: frame_home(t, z, p)) for p, x in enumerate(sums)]
    others = []
    for step in range(1, share):
        others += [permute(x, lambda t, z: next_in_frame(t, z, step)) for x in own]

    done = attend_call(own, others, (query_weight, key_weight, value_weight, out_weight))
    done = [x.reshape(rows_here, columns, chans) for x in done]
    back = []
    for p in range(frames):
        pairs = [(b, a) for a, b in everywhere(sizes, lambda t, z: frame_home(t, z, p))]
        back.append(lax.ppermute(done[p], BOTH, pairs))
    return jnp.stack(
        [
            functools.reduce(
                lambda rest, p: jnp.where((z_index + p) % frames == f, back[p], rest),
                range(1, frames),
                back[0],
            )
            for f in range(frames)
        ]
    )


def solution(mesh):
    placed = (P("tm", "rows", None, None), P(None, "tm", None), P(), P(), P(), P())
    return jax.shard_map(
        body, mesh=mesh, in_specs=placed, out_specs=P("tm", "rows", None, None), check_vma=False
    )
```

time: 86.9 us -> 89.4 us (1.029)
  Pallas kernels: 19.7 us -> 24.1 us
  starting transfers between devices: 38.8 us -> 35.3 us
  waiting for transfers between devices: 23.3 us -> 26 us
  local copies, waits for them, and re-layouts: 3.64 us -> 2.51 us
    ppermute x28 -> x20, waiting for transfers between devices: 12.7 us -> 15.4 us  [permute(): return lax.ppermute(block, BOTH, everywhere(sizes, target))]
    pallas_call x7 -> x6, Pallas kernels: 6.98 us -> 9.49 us  [the longest x4 4.43 us: sum_call(): pl.pallas_call(kernel, out_shape=jax.ShapeDtypeStruct(pieces[0].shape, jn...]
    ppermute x28 -> x20, starting transfers between devices: 33.9 us -> 31.5 us  [permute(): return lax.ppermute(block, BOTH, everywhere(sizes, target))]
    pallas_call x4, Pallas kernels: 11.9 us -> 13.7 us  [conv_call(): pl.pallas_call(functools.partial(conv_kernel, tuple(jobs), parts, group,...]
    dynamic_slice x1 -> x0, local copies, waits for them, and re-layouts: 1.15 us -> none  [body(): piece = lax.dynamic_slice_in_dim(latents, start, width, axis=3)]
    ppermute x2, starting transfers between devices: 4.9 us -> 3.79 us  [body(): back.append(lax.ppermute(done[p], BOTH, pairs))]
  transfers between devices with their start and end apart: 30 -> 22, of which waited for: 14 -> 10; matrix products, arithmetic and copies ran while one was open for 3% -> 1% of each run, Pallas kernels for 14% -> 17%
where the time goes in v6:
time: 89.4 us; the launch traced here: 89 us
  starting transfers between devices  35.3 us (39%)
  waiting for transfers between devices  26 us (29%)
  Pallas kernels  24.1 us (27%)
  local copies, waits for them, and re-layouts  2.51 us (3%)
  other arithmetic  0.96 us (1%)
    ppermute x20, starting transfers between devices, permute(): return lax.ppermute(block, BOTH, everywhere(sizes, target))  31.5 us
    ppermute x20, waiting for transfers between devices, permute(): return lax.ppermute(block, BOTH, everywhere(sizes, target))  15.4 us
    pallas_call x4, Pallas kernels, conv_call(): pl.pallas_call(functools.partial(conv_kernel, tuple(jobs), parts, group,...  13.7 us
    ppermute x2, waiting for transfers between devices, body(): back.append(lax.ppermute(done[p], BOTH, pairs))  10.6 us
    pallas_call x4, Pallas kernels, sum_call(): pl.pallas_call(kernel, out_shape=jax.ShapeDtypeStruct(pieces[0].shape, jn...  4.43 us
    pallas_call x1, Pallas kernels, attend_call(): pl.pallas_call(functools.partial(attend_kernel, frames, share), out_shape...  4.37 us
    ppermute x2, starting transfers between devices, body(): back.append(lax.ppermute(done[p], BOTH, pairs))  3.79 us
  transfers between devices with their start and end apart: 22, of which 10 were waited for; matrix products, arithmetic and copies ran while one was open for 1% of the time, Pallas kernels for 17%

profile of v6, /device:TPU:1, one launch (start us, length us, event | category | flops | bytes accessed | tf_op | source)
XLA Modules:
  0.0 89.0 jit_solution(6589970559681196781)
XLA Ops:
  0.0 0.1 collective-permute-start.1
  0.1 1.0 %slice_bitcast_fusion = (bf16[2,64,512]{2,1,0:T(8,128)(2,1)S(1)}, bf16[2,64,512]{2,1,0:T(8,128)(2,1)S(1)}) fusion(bf16[2,4,64,512]{3,2,1,0:T(8,128)(2,1)} %latents.1), kind=kLoop, calls=%fused_computation.3 | loop fusion | bytes 524288 | tf_op jit(solution)/shard_map/squeeze | solution.py:331
  1.0 4.7 %collective-permute-start = (bf16[2,64,512]{2,1,0:T(8,128)(2,1)S(1)}, bf16[2,64,512]{2,1,0:T(8,128)(2,1)S(1)}, u32[]{:S(2)}, u32[]{:S(2)}) collective-permute-start(bf16[2,64,512]{2,1,0:T(8,128)(2,1)S(1)} %get-tuple-element.40), channel_id=1, source_target_pairs={{0,1},{1,2},{2,3},{4,5},{5,6},{6,7},{8,9},{9,10},{10,11},{12,13},{... | collective-permute-start | bytes 393224 | tf_op jit(solution)/shard_map/ppermute | solution.py:318
  5.7 1.3 %collective-permute-start.2 = (bf16[2,64,512]{2,1,0:T(8,128)(2,1)S(1)}, bf16[2,64,512]{2,1,0:T(8,128)(2,1)S(1)}, u32[]{:S(2)}, u32[]{:S(2)}) collective-permute-start(bf16[2,64,512]{2,1,0:T(8,128)(2,1)S(1)} %get-tuple-element.39), channel_id=1, source_target_pairs={{1,0},{2,1},{3,2},{5,4},{6,5},{7,6},{9,8},{10,9},{11,10},{13,12},{... | collective-permute-start | bytes 393224 | tf_op jit(solution)/shard_map/ppermute | solution.py:318
  7.0 0.1 pad_add_fusion.refs_0_.meta
  7.1 0.0 collective-permute-done.1.refs_2_
  7.1 1.5 %copy-done = bf16[27,64,512]{2,1,0:T(8,128)(2,1)S(1)} copy-done((bf16[27,64,512]{2,1,0:T(8,128)(2,1)S(1)}, bf16[27,64,512]{2,1,0:T(8,128)(2,1)}, u32[]{:S(2)}) %copy-start) | copy-done | bytes 1769496
  8.6 0.9 merge_kernel_slices.1.refs_1_
  9.5 0.0 collective-permute-done.above
  9.5 3.0 %collective-permute-done.2.below = bf16[2,64,512]{2,1,0:T(8,128)(2,1)S(1)} collective-permute-done((bf16[2,64,512]{2,1,0:T(8,128)(2,1)S(1)}, bf16[2,64,512]{2,1,0:T(8,128)(2,1)S(1)}, u32[]{:S(2)}, u32[]{:S(2)}) %collective-permute-start.2) | collective-permute-done | bytes 131104 | tf_op jit(solution)/shard_map/ppermute | solution.py:318
  12.4 0.7 frame_parts.1
  13.1 1.3 %collective-permute-start.5 = (bf16[2,6,64,128]{3,2,1,0:T(8,128)(2,1)S(1)}, bf16[2,6,64,128]{3,2,1,0:T(8,128)(2,1)S(1)}, u32[]{:S(2)}, u32[]{:S(2)}) collective-permute-start(bf16[2,6,64,128]{3,2,1,0:T(8,128)(2,1)S(1)} %get-tuple-element.25), channel_id=1, source_target_pairs={{0,8},{1,9},{2,10},{3,11},{4,20},{5,21},{6,22},{7,23},{8,0},{9,1},... | collective-permute-start | bytes 589832 | tf_op jit(solution)/shard_map/ppermute | solution.py:318
  14.4 1.2 %collective-permute-start.3 = (bf16[2,6,64,128]{3,2,1,0:T(8,128)(2,1)S(1)}, bf16[2,6,64,128]{3,2,1,0:T(8,128)(2,1)S(1)}, u32[]{:S(2)}, u32[]{:S(2)}) collective-permute-start(bf16[2,6,64,128]{3,2,1,0:T(8,128)(2,1)S(1)} %get-tuple-element.24), channel_id=1, source_target_pairs={{0,16},{1,17},{2,18},{3,19},{4,12},{5,13},{6,14},{7,15},{8,24},{9,... | collective-permute-start | bytes 589832 | tf_op jit(solution)/shard_map/ppermute | solution.py:318
  15.6 0.2 collective-permute-start.8
  15.8 1.9 %collective-permute-start.4 = (bf16[2,6,64,128]{3,2,1,0:T(8,128)(2,1)S(1)}, bf16[2,6,64,128]{3,2,1,0:T(8,128)(2,1)S(1)}, u32[]{:S(2)}, u32[]{:S(2)}) collective-permute-start(bf16[2,6,64,128]{3,2,1,0:T(8,128)(2,1)S(1)} %get-tuple-element.23.refs_2_), channel_id=1, source_target_pairs={{0,4},{1,5},{2,6},{3,7},{4,0},{5,1},{6,2},{7,3},{8,12},{9,13},{10,... | collective-permute-start | bytes 589832 | tf_op jit(solution)/shard_map/ppermute | solution.py:318
  17.8 0.2 collective-permute-done.5.refs_2_
  18.0 4.1 %collective-permute-start.6 = (bf16[2,6,64,128]{3,2,1,0:T(8,128)(2,1)S(1)}, bf16[2,6,64,128]{3,2,1,0:T(8,128)(2,1)S(1)}, u32[]{:S(2)}, u32[]{:S(2)}) collective-permute-start(bf16[2,6,64,128]{3,2,1,0:T(8,128)(2,1)S(1)} %collective-permute-done.5.refs_2_), channel_id=1, source_target_pairs={{0,4},{1,5},{2,6},{3,7},{4,0},{5,1},{6,2},{7,3},{8,12},{9,13},{10,... | collective-permute-start | bytes 589832 | tf_op jit(solution)/shard_map/ppermute | solution.py:318
  22.1 0.0 collective-permute-done.3.refs_3_
  22.1 0.5 collective-permute-start.7
  22.6 1.7 %collective-permute-done.8.refs_3_ = bf16[2,6,64,128]{3,2,1,0:T(8,128)(2,1)S(1)} collective-permute-done((bf16[2,6,64,128]{3,2,1,0:T(8,128)(2,1)S(1)}, bf16[2,6,64,128]{3,2,1,0:T(8,128)(2,1)S(1)}, u32[]{:S(2)}, u32[]{:S(2)}) %collective-permute-start.8) | collective-permute-done | bytes 196640 | tf_op jit(solution)/shard_map/ppermute | solution.py:318
  24.2 1.6 %collective-permute-start.9 = (bf16[2,6,64,128]{3,2,1,0:T(8,128)(2,1)S(1)}, bf16[2,6,64,128]{3,2,1,0:T(8,128)(2,1)S(1)}, u32[]{:S(2)}, u32[]{:S(2)}) collective-permute-start(bf16[2,6,64,128]{3,2,1,0:T(8,128)(2,1)S(1)} %collective-permute-done.8.refs_3_), channel_id=1, source_target_pairs={{0,4},{1,5},{2,6},{3,7},{4,0},{5,1},{6,2},{7,3},{8,12},{9,13},{10,... | collective-permute-start | bytes 589832 | tf_op jit(solution)/shard_map/ppermute | solution.py:318
  25.9 0.0 collective-permute-done.4.refs_4_
  25.9 0.0 collective-permute-done.6.refs_5_
  25.9 0.0 collective-permute-done.7.refs_6_
  25.9 1.1 %collective-permute-done.9.refs_7_ = bf16[2,6,64,128]{3,2,1,0:T(8,128)(2,1)S(1)} collective-permute-done((bf16[2,6,64,128]{3,2,1,0:T(8,128)(2,1)S(1)}, bf16[2,6,64,128]{3,2,1,0:T(8,128)(2,1)S(1)}, u32[]{:S(2)}, u32[]{:S(2)}) %collective-permute-start.9) | collective-permute-done | bytes 196640 | tf_op jit(solution)/shard_map/ppermute | solution.py:318
  27.0 3.6 %conv_sums.4 = (bf16[256,512]{1,0:T(8,128)(2,1)}, bf16[256,512]{1,0:T(8,128)(2,1)}) custom-call(s32[3]{0:T(128)S(1)} %pad_add_fusion.refs_0_.meta, bf16[3,9,128,512]{3,2,1,0:T(8,128)(2,1)S(1)} %merge_kernel_slices.1.refs_1_, bf16[2,6,64,128]{3,2,1,0:T(8,128)(2,1)S(1)} %collective-permute-done.5.refs_2_, ...), custom_call_target="tpu_custom_call" | custom-call | flops 99999997952 | bytes 3538944 | tf_op jit(solution)/shard_map/conv_sums/pallas_call | solution.py:169
  30.5 0.0 copy-done.6
  30.5 1.2 %collective-permute-start.10 = (bf16[256,512]{1,0:T(8,128)(2,1)}, bf16[256,512]{1,0:T(8,128)(2,1)}, u32[]{:S(2)}, u32[]{:S(2)}) collective-permute-start(bf16[256,512]{1,0:T(8,128)(2,1)} %get-tuple-element.30), channel_id=1, source_target_pairs={{0,8},{1,9},{2,10},{3,11},{4,20},{5,21},{6,22},{7,23},{8,0},{9,1},... | collective-permute-start | bytes 786440 | tf_op jit(solution)/shard_map/ppermute | solution.py:318
  31.8 0.2 collective-permute-start.11
  32.0 4.0 %conv_sums.5 = (bf16[256,512]{1,0:T(8,128)(2,1)}, bf16[256,512]{1,0:T(8,128)(2,1)}) custom-call(s32[3]{0:T(128)S(1)} %pad_add_fusion.refs_0_.meta, bf16[3,9,128,512]{3,2,1,0:T(8,128)(2,1)S(1)} %merge_kernel_slices.1.refs_1_, bf16[2,6,64,128]{3,2,1,0:T(8,128)(2,1)S(1)} %collective-permute-done.5.refs_2_, ...), custom_call_target="tpu_custom_call" | custom-call | flops 99999997952 | bytes 3538944 | tf_op jit(solution)/shard_map/conv_sums/pallas_call | solution.py:169
  36.1 1.2 %collective-permute-start.14 = (bf16[256,512]{1,0:T(8,128)(2,1)}, bf16[256,512]{1,0:T(8,128)(2,1)}, u32[]{:S(2)}, u32[]{:S(2)}) collective-permute-start(bf16[256,512]{1,0:T(8,128)(2,1)} %get-tuple-element.33), channel_id=1, source_target_pairs={{0,8},{1,9},{2,10},{3,11},{4,20},{5,21},{6,22},{7,23},{8,0},{9,1},... | collective-permute-start | bytes 786440 | tf_op jit(solution)/shard_map/ppermute | solution.py:318
  37.3 0.2 collective-permute-start.15
  37.5 3.3 %conv_sums.6 = (f32[256,512]{1,0:T(8,128)S(1)}, f32[256,512]{1,0:T(8,128)S(1)}) custom-call(s32[3]{0:T(128)S(1)} %pad_add_fusion.refs_0_.meta, bf16[3,9,128,512]{3,2,1,0:T(8,128)(2,1)S(1)} %merge_kernel_slices.1.refs_1_, bf16[2,6,64,128]{3,2,1,0:T(8,128)(2,1)S(1)} %copy-done.7, bf16[2,6,64,128]{3,2,1,0:T(8,128)(2,1)S(1)} %copy-done.9, ...), custom_call_target="tpu_custom_call" | custom-call | flops 99999997952 | bytes 3538944 | tf_op jit(solution)/shard_map/conv_sums/pallas_call | solution.py:169
  40.8 0.0 collective-permute-done.10.refs_2_.refs_1_
  40.8 0.0 collective-permute-done.11.refs_1_
  40.8 1.1 %sum_parts.4.refs_8_ = bf16[256,512]{1,0:T(8,128)(2,1)S(1)} custom-call(f32[256,512]{1,0:T(8,128)S(1)} %get-tuple-element.31.refs_0_, bf16[256,512]{1,0:T(8,128)(2,1)} %collective-permute-done.11.refs_1_, bf16[256,512]{1,0:T(8,128)(2,1)} %collective-permute-done.10.refs_2_.refs_1_), custom_call_target="tpu_custom_call" | custom-call | tf_op jit(solution)/shard_map/sum_parts/pallas_call | solution.py:192
  41.9 1.3 %collective-permute-start.12 = (bf16[256,512]{1,0:T(8,128)(2,1)S(1)}, bf16[256,512]{1,0:T(8,128)(2,1)S(1)}, u32[]{:S(2)}, u32[]{:S(2)}) collective-permute-start(bf16[256,512]{1,0:T(8,128)(2,1)S(1)} %sum_parts.4.refs_8_), channel_id=1, source_target_pairs={{0,16},{1,17},{2,18},{3,19},{4,12},{5,13},{6,14},{7,15},{8,24},{9,... | collective-permute-start | bytes 786440 | tf_op jit(solution)/shard_map/ppermute | solution.py:318
  43.2 2.8 %conv_sums.7 = (f32[256,512]{1,0:T(8,128)S(1)}, f32[256,512]{1,0:T(8,128)S(1)}) custom-call(s32[3]{0:T(128)S(1)} %pad_add_fusion.refs_0_.meta, bf16[3,9,128,512]{3,2,1,0:T(8,128)(2,1)S(1)} %merge_kernel_slices.1.refs_1_, bf16[2,6,64,128]{3,2,1,0:T(8,128)(2,1)S(1)} %copy-done.7, bf16[2,6,64,128]{3,2,1,0:T(8,128)(2,1)S(1)} %copy-done.9, ...), custom_call_target="tpu_custom_call" | custom-call | flops 99999997952 | bytes 3538944 | tf_op jit(solution)/shard_map/conv_sums/pallas_call | solution.py:169
  46.1 0.0 collective-permute-done.14.refs_2_.refs_1_
  46.1 0.0 collective-permute-done.15.refs_1_
  46.1 0.0 copy-start.2
  46.1 0.0 copy-start.3
  46.1 0.0 copy-start.4
  46.1 0.0 copy-start.5
  46.2 1.2 %sum_parts.6 = bf16[256,512]{1,0:T(8,128)(2,1)S(1)} custom-call(f32[256,512]{1,0:T(8,128)S(1)} %get-tuple-element.34.refs_0_, bf16[256,512]{1,0:T(8,128)(2,1)} %collective-permute-done.15.refs_1_, bf16[256,512]{1,0:T(8,128)(2,1)} %collective-permute-done.14.refs_2_.refs_1_), custom_call_target="tpu_custom_call" | custom-call | tf_op jit(solution)/shard_map/sum_parts/pallas_call | solution.py:192
  47.4 0.3 collective-permute-start.16
  47.7 1.1 %collective-permute-done.12.refs_2_ = bf16[256,512]{1,0:T(8,128)(2,1)S(1)} collective-permute-done((bf16[256,512]{1,0:T(8,128)(2,1)S(1)}, bf16[256,512]{1,0:T(8,128)(2,1)S(1)}, u32[]{:S(2)}, u32[]{:S(2)}) %collective-permute-start.12) | collective-permute-done | bytes 262176 | tf_op jit(solution)/shard_map/ppermute | solution.py:318
  48.8 1.0 %sum_parts.5 = bf16[256,512]{1,0:T(8,128)(2,1)S(1)} custom-call(f32[256,512]{1,0:T(8,128)S(1)} %get-tuple-element.29.refs_0_, bf16[256,512]{1,0:T(8,128)(2,1)} %collective-permute-done.10.refs_2_.refs_1_, bf16[256,512]{1,0:T(8,128)(2,1)S(1)} %collective-permute-done.12.refs_2_), custom_call_target="tpu_custom_call" | custom-call | tf_op jit(solution)/shard_map/sum_parts/pallas_call | solution.py:192
  49.9 5.8 %collective-permute-start.13 = (bf16[256,512]{1,0:T(8,128)(2,1)S(1)}, bf16[256,512]{1,0:T(8,128)(2,1)S(1)}, u32[]{:S(2)}, u32[]{:S(2)}) collective-permute-start(bf16[256,512]{1,0:T(8,128)(2,1)S(1)} %sum_parts.5), channel_id=1, source_target_pairs={{0,0},{1,1},{2,4},{3,5},{4,2},{5,3},{6,6},{7,7},{8,8},{9,9},{10,12... | collective-permute-start | bytes 786440 | tf_op jit(solution)/shard_map/ppermute | solution.py:318
  55.7 0.0 collective-permute-done.16.refs_2_
  55.7 1.1 %sum_parts.7 = bf16[256,512]{1,0:T(8,128)(2,1)S(1)} custom-call(f32[256,512]{1,0:T(8,128)S(1)} %get-tuple-element.32.refs_0_, bf16[256,512]{1,0:T(8,128)(2,1)} %collective-permute-done.14.refs_2_.refs_1_, bf16[256,512]{1,0:T(8,128)(2,1)S(1)} %collective-permute-done.16.refs_2_), custom_call_target="tpu_custom_call" | custom-call | tf_op jit(solution)/shard_map/sum_parts/pallas_call | solution.py:192
  56.7 1.2 %collective-permute-start.17 = (bf16[256,512]{1,0:T(8,128)(2,1)S(1)}, bf16[256,512]{1,0:T(8,128)(2,1)S(1)}, u32[]{:S(2)}, u32[]{:S(2)}) collective-permute-start(bf16[256,512]{1,0:T(8,128)(2,1)S(1)} %sum_parts.7), channel_id=1, source_target_pairs={{0,1},{1,0},{2,5},{3,4},{4,3},{5,2},{6,7},{7,6},{8,9},{9,8},{10,13... | collective-permute-start | bytes 786440 | tf_op jit(solution)/shard_map/ppermute | solution.py:318
  58.0 5.0 %collective-permute-done.13.refs_0_ = bf16[256,512]{1,0:T(8,128)(2,1)S(1)} collective-permute-done((bf16[256,512]{1,0:T(8,128)(2,1)S(1)}, bf16[256,512]{1,0:T(8,128)(2,1)S(1)}, u32[]{:S(2)}, u32[]{:S(2)}) %collective-permute-start.13) | collective-permute-done | bytes 262176 | tf_op jit(solution)/shard_map/ppermute | solution.py:318
  63.0 0.0 collective-permute-start.18
  63.0 2.3 %collective-permute-done.17.refs_1_ = bf16[256,512]{1,0:T(8,128)(2,1)S(1)} collective-permute-done((bf16[256,512]{1,0:T(8,128)(2,1)S(1)}, bf16[256,512]{1,0:T(8,128)(2,1)S(1)}, u32[]{:S(2)}, u32[]{:S(2)}) %collective-permute-start.17) | collective-permute-done | bytes 262176 | tf_op jit(solution)/shard_map/ppermute | solution.py:318
  65.2 3.0 %collective-permute-start.19 = (bf16[256,512]{1,0:T(8,128)(2,1)S(1)}, bf16[256,512]{1,0:T(8,128)(2,1)S(1)}, u32[]{:S(2)}, u32[]{:S(2)}) collective-permute-start(bf16[256,512]{1,0:T(8,128)(2,1)S(1)} %collective-permute-done.17.refs_1_), channel_id=1, source_target_pairs={{0,4},{1,5},{2,6},{3,7},{4,0},{5,1},{6,2},{7,3},{8,12},{9,13},{10,... | collective-permute-start | bytes 786440 | tf_op jit(solution)/shard_map/ppermute | solution.py:318
  68.2 0.0 collective-permute-done.18.refs_2_
  68.2 1.2 %collective-permute-done.19.refs_3_ = bf16[256,512]{1,0:T(8,128)(2,1)S(1)} collective-permute-done((bf16[256,512]{1,0:T(8,128)(2,1)S(1)}, bf16[256,512]{1,0:T(8,128)(2,1)S(1)}, u32[]{:S(2)}, u32[]{:S(2)}) %collective-permute-start.19) | collective-permute-done | bytes 262176 | tf_op jit(solution)/shard_map/ppermute | solution.py:318
  69.4 4.4 %attend.1 = (bf16[256,512]{1,0:T(8,128)(2,1)S(1)}, bf16[256,512]{1,0:T(8,128)(2,1)S(1)}) custom-call(bf16[256,512]{1,0:T(8,128)(2,1)S(1)} %collective-permute-done.13.refs_0_, bf16[256,512]{1,0:T(8,128)(2,1)S(1)} %collective-permute-done.17.refs_1_, bf16[256,512]{1,0:T(8,128)(2,1)S(1)} %collective-permute-done.18.refs_2_, ...), custom_call_target="tpu_custom_call" | custom-call | flops 2684354560 | bytes 3145728 | tf_op jit(solution)/shard_map/attend/pallas_call | solution.py:289
  73.8 1.1 %collective-permute-start.20 = (bf16[4,64,512]{2,1,0:T(8,128)(2,1)S(1)}, bf16[4,64,512]{2,1,0:T(8,128)(2,1)S(1)}, u32[]{:S(2)}, u32[]{:S(2)}) collective-permute-start(bf16[4,64,512]{2,1,0:T(8,128)(2,1)S(1)} %bitcast.21), channel_id=1, source_target_pairs={{1,0},{0,1},{5,2},{4,3},{3,4},{2,5},{7,6},{6,7},{9,8},{8,9},{13,10... | collective-permute-start | bytes 786440 | tf_op jit(solution)/shard_map/ppermute | solution.py:385
  74.8 2.7 %collective-permute-start.21 = (bf16[4,64,512]{2,1,0:T(8,128)(2,1)S(1)}, bf16[4,64,512]{2,1,0:T(8,128)(2,1)S(1)}, u32[]{:S(2)}, u32[]{:S(2)}) collective-permute-start(bf16[4,64,512]{2,1,0:T(8,128)(2,1)S(1)} %bitcast.20), channel_id=1, source_target_pairs={{0,0},{1,1},{4,2},{5,3},{2,4},{3,5},{6,6},{7,7},{8,8},{9,9},{12,10... | collective-permute-start | bytes 786440 | tf_op jit(solution)/shard_map/ppermute | solution.py:385
  77.6 5.0 %collective-permute-done.20 = bf16[4,64,512]{2,1,0:T(8,128)(2,1)S(1)} collective-permute-done((bf16[4,64,512]{2,1,0:T(8,128)(2,1)S(1)}, bf16[4,64,512]{2,1,0:T(8,128)(2,1)S(1)}, u32[]{:S(2)}, u32[]{:S(2)}) %collective-permute-start.20) | collective-permute-done | bytes 262176 | tf_op jit(solution)/shard_map/ppermute | solution.py:385
  82.5 5.6 %collective-permute-done.21 = bf16[4,64,512]{2,1,0:T(8,128)(2,1)S(1)} collective-permute-done((bf16[4,64,512]{2,1,0:T(8,128)(2,1)S(1)}, bf16[4,64,512]{2,1,0:T(8,128)(2,1)S(1)}, u32[]{:S(2)}, u32[]{:S(2)}) %collective-permute-start.21) | collective-permute-done | bytes 262176 | tf_op jit(solution)/shard_map/ppermute | solution.py:385
  88.2 0.8 pad_maximum_fusion
  (15 shorter events, 0.1 us)
Async XLA Ops:
  0.0 7.1 %collective-permute-start.1 = (bf16[9,3,64,512]{3,2,1,0:T(8,128)(2,1)}, bf16[9,3,64,512]{3,2,1,0:T(8,128)(2,1)S(1)}, u32[]{:S(2)}, u32[]{:S(2)}) collective-permute-start(bf16[9,3,64,512]{3,2,1,0:T(8,128)(2,1)} %bitcast.18), channel_id=1, source_target_pairs={{0,4},{1,5},{2,6},{3,7},{4,0},{5,1},{6,2},{7,3},{8,12},{9,13},{10,... | collective-permute-start | bytes 5308424 | tf_op jit(solution)/shard_map/ppermute | solution.py:318
  1.0 8.4 %collective-permute-start = (bf16[2,64,512]{2,1,0:T(8,128)(2,1)S(1)}, bf16[2,64,512]{2,1,0:T(8,128)(2,1)S(1)}, u32[]{:S(2)}, u32[]{:S(2)}) collective-permute-start(bf16[2,64,512]{2,1,0:T(8,128)(2,1)S(1)} %get-tuple-element.40), channel_id=1, source_target_pairs={{0,1},{1,2},{2,3},{4,5},{5,6},{6,7},{8,9},{9,10},{10,11},{12,13},{... | collective-permute-start | bytes 393224 | tf_op jit(solution)/shard_map/ppermute | solution.py:318
  5.7 6.7 %collective-permute-start.2 = (bf16[2,64,512]{2,1,0:T(8,128)(2,1)S(1)}, bf16[2,64,512]{2,1,0:T(8,128)(2,1)S(1)}, u32[]{:S(2)}, u32[]{:S(2)}) collective-permute-start(bf16[2,64,512]{2,1,0:T(8,128)(2,1)S(1)} %get-tuple-element.39), channel_id=1, source_target_pairs={{1,0},{2,1},{3,2},{5,4},{6,5},{7,6},{9,8},{10,9},{11,10},{13,12},{... | collective-permute-start | bytes 393224 | tf_op jit(solution)/shard_map/ppermute | solution.py:318
  7.1 1.5 %copy-start = (bf16[27,64,512]{2,1,0:T(8,128)(2,1)S(1)}, bf16[27,64,512]{2,1,0:T(8,128)(2,1)}, u32[]{:S(2)}) copy-start(bf16[27,64,512]{2,1,0:T(8,128)(2,1)} %param.7) | copy-start | bytes 5308420
  8.6 3.8 %copy-start.1 = (bf16[2,4,64,512]{3,2,1,0:T(8,128)(2,1)S(1)}, bf16[2,4,64,512]{3,2,1,0:T(8,128)(2,1)}, u32[]{:S(2)}) copy-start(bf16[2,4,64,512]{3,2,1,0:T(8,128)(2,1)} %latents.1) | copy-start | bytes 1572868
  13.1 17.4 %copy-start.6 = (bf16[2,6,64,128]{3,2,1,0:T(8,128)(2,1)}, bf16[2,6,64,128]{3,2,1,0:T(8,128)(2,1)S(1)}, u32[]{:S(2)}) copy-start(bf16[2,6,64,128]{3,2,1,0:T(8,128)(2,1)S(1)} %get-tuple-element.23.refs_2_) | copy-start | bytes 589828
  13.1 4.9 %collective-permute-start.5 = (bf16[2,6,64,128]{3,2,1,0:T(8,128)(2,1)S(1)}, bf16[2,6,64,128]{3,2,1,0:T(8,128)(2,1)S(1)}, u32[]{:S(2)}, u32[]{:S(2)}) collective-permute-start(bf16[2,6,64,128]{3,2,1,0:T(8,128)(2,1)S(1)} %get-tuple-element.25), channel_id=1, source_target_pairs={{0,8},{1,9},{2,10},{3,11},{4,20},{5,21},{6,22},{7,23},{8,0},{9,1},... | collective-permute-start | bytes 589832 | tf_op jit(solution)/shard_map/ppermute | solution.py:318
  14.4 7.6 %collective-permute-start.3 = (bf16[2,6,64,128]{3,2,1,0:T(8,128)(2,1)S(1)}, bf16[2,6,64,128]{3,2,1,0:T(8,128)(2,1)S(1)}, u32[]{:S(2)}, u32[]{:S(2)}) collective-permute-start(bf16[2,6,64,128]{3,2,1,0:T(8,128)(2,1)S(1)} %get-tuple-element.24), channel_id=1, source_target_pairs={{0,16},{1,17},{2,18},{3,19},{4,12},{5,13},{6,14},{7,15},{8,24},{9,... | collective-permute-start | bytes 589832 | tf_op jit(solution)/shard_map/ppermute | solution.py:318
  15.6 8.6 %collective-permute-start.8 = (bf16[2,6,64,128]{3,2,1,0:T(8,128)(2,1)S(1)}, bf16[2,6,64,128]{3,2,1,0:T(8,128)(2,1)S(1)}, u32[]{:S(2)}, u32[]{:S(2)}) collective-permute-start(bf16[2,6,64,128]{3,2,1,0:T(8,128)(2,1)S(1)} %get-tuple-element.26), channel_id=1, source_target_pairs={{0,24},{1,25},{2,26},{3,27},{4,28},{5,29},{6,30},{7,31},{8,16},{9,... | collective-permute-start | bytes 589832 | tf_op jit(solution)/shard_map/ppermute | solution.py:318
  15.8 10.1 %collective-permute-start.4 = (bf16[2,6,64,128]{3,2,1,0:T(8,128)(2,1)S(1)}, bf16[2,6,64,128]{3,2,1,0:T(8,128)(2,1)S(1)}, u32[]{:S(2)}, u32[]{:S(2)}) collective-permute-start(bf16[2,6,64,128]{3,2,1,0:T(8,128)(2,1)S(1)} %get-tuple-element.23.refs_2_), channel_id=1, source_target_pairs={{0,4},{1,5},{2,6},{3,7},{4,0},{5,1},{6,2},{7,3},{8,12},{9,13},{10,... | collective-permute-start | bytes 589832 | tf_op jit(solution)/shard_map/ppermute | solution.py:318
  18.0 7.9 %collective-permute-start.6 = (bf16[2,6,64,128]{3,2,1,0:T(8,128)(2,1)S(1)}, bf16[2,6,64,128]{3,2,1,0:T(8,128)(2,1)S(1)}, u32[]{:S(2)}, u32[]{:S(2)}) collective-permute-start(bf16[2,6,64,128]{3,2,1,0:T(8,128)(2,1)S(1)} %collective-permute-done.5.refs_2_), channel_id=1, source_target_pairs={{0,4},{1,5},{2,6},{3,7},{4,0},{5,1},{6,2},{7,3},{8,12},{9,13},{10,... | collective-permute-start | bytes 589832 | tf_op jit(solution)/shard_map/ppermute | solution.py:318
  22.1 8.5 %copy-start.8 = (bf16[2,6,64,128]{3,2,1,0:T(8,128)(2,1)}, bf16[2,6,64,128]{3,2,1,0:T(8,128)(2,1)S(1)}, u32[]{:S(2)}) copy-start(bf16[2,6,64,128]{3,2,1,0:T(8,128)(2,1)S(1)} %collective-permute-done.3.refs_3_) | copy-start | bytes 589828
  22.1 3.8 %collective-permute-start.7 = (bf16[2,6,64,128]{3,2,1,0:T(8,128)(2,1)S(1)}, bf16[2,6,64,128]{3,2,1,0:T(8,128)(2,1)S(1)}, u32[]{:S(2)}, u32[]{:S(2)}) collective-permute-start(bf16[2,6,64,128]{3,2,1,0:T(8,128)(2,1)S(1)} %collective-permute-done.3.refs_3_), channel_id=1, source_target_pairs={{0,4},{1,5},{2,6},{3,7},{4,0},{5,1},{6,2},{7,3},{8,12},{9,13},{10,... | collective-permute-start | bytes 589832 | tf_op jit(solution)/shard_map/ppermute | solution.py:318
  24.2 2.7 %collective-permute-start.9 = (bf16[2,6,64,128]{3,2,1,0:T(8,128)(2,1)S(1)}, bf16[2,6,64,128]{3,2,1,0:T(8,128)(2,1)S(1)}, u32[]{:S(2)}, u32[]{:S(2)}) collective-permute-start(bf16[2,6,64,128]{3,2,1,0:T(8,128)(2,1)S(1)} %collective-permute-done.8.refs_3_), channel_id=1, source_target_pairs={{0,4},{1,5},{2,6},{3,7},{4,0},{5,1},{6,2},{7,3},{8,12},{9,13},{10,... | collective-permute-start | bytes 589832 | tf_op jit(solution)/shard_map/ppermute | solution.py:318
  30.5 10.3 %collective-permute-start.10 = (bf16[256,512]{1,0:T(8,128)(2,1)}, bf16[256,512]{1,0:T(8,128)(2,1)}, u32[]{:S(2)}, u32[]{:S(2)}) collective-permute-start(bf16[256,512]{1,0:T(8,128)(2,1)} %get-tuple-element.30), channel_id=1, source_target_pairs={{0,8},{1,9},{2,10},{3,11},{4,20},{5,21},{6,22},{7,23},{8,0},{9,1},... | collective-permute-start | bytes 786440 | tf_op jit(solution)/shard_map/ppermute | solution.py:318
  31.8 5.7 %copy-start.7 = (bf16[2,6,64,128]{3,2,1,0:T(8,128)(2,1)S(1)}, bf16[2,6,64,128]{3,2,1,0:T(8,128)(2,1)}, u32[]{:S(2)}) copy-start(bf16[2,6,64,128]{3,2,1,0:T(8,128)(2,1)} %copy-done.6) | copy-start | bytes 589828
  31.8 5.7 %copy-start.9 = (bf16[2,6,64,128]{3,2,1,0:T(8,128)(2,1)S(1)}, bf16[2,6,64,128]{3,2,1,0:T(8,128)(2,1)}, u32[]{:S(2)}) copy-start(bf16[2,6,64,128]{3,2,1,0:T(8,128)(2,1)} %copy-done.8) | copy-start | bytes 589828
  31.8 9.0 %collective-permute-start.11 = (bf16[256,512]{1,0:T(8,128)(2,1)}, bf16[256,512]{1,0:T(8,128)(2,1)}, u32[]{:S(2)}, u32[]{:S(2)}) collective-permute-start(bf16[256,512]{1,0:T(8,128)(2,1)} %get-tuple-element.27.refs_8_), channel_id=1, source_target_pairs={{0,8},{1,9},{2,10},{3,11},{4,20},{5,21},{6,22},{7,23},{8,0},{9,1},... | collective-permute-start | bytes 786440 | tf_op jit(solution)/shard_map/ppermute | solution.py:318
  36.1 10.0 %collective-permute-start.14 = (bf16[256,512]{1,0:T(8,128)(2,1)}, bf16[256,512]{1,0:T(8,128)(2,1)}, u32[]{:S(2)}, u32[]{:S(2)}) collective-permute-start(bf16[256,512]{1,0:T(8,128)(2,1)} %get-tuple-element.33), channel_id=1, source_target_pairs={{0,8},{1,9},{2,10},{3,11},{4,20},{5,21},{6,22},{7,23},{8,0},{9,1},... | collective-permute-start | bytes 786440 | tf_op jit(solution)/shard_map/ppermute | solution.py:318
  37.3 8.8 %collective-permute-start.15 = (bf16[256,512]{1,0:T(8,128)(2,1)}, bf16[256,512]{1,0:T(8,128)(2,1)}, u32[]{:S(2)}, u32[]{:S(2)}) collective-permute-start(bf16[256,512]{1,0:T(8,128)(2,1)} %get-tuple-element.28.refs_8_), channel_id=1, source_target_pairs={{0,8},{1,9},{2,10},{3,11},{4,20},{5,21},{6,22},{7,23},{8,0},{9,1},... | collective-permute-start | bytes 786440 | tf_op jit(solution)/shard_map/ppermute | solution.py:318
  41.9 6.9 %collective-permute-start.12 = (bf16[256,512]{1,0:T(8,128)(2,1)S(1)}, bf16[256,512]{1,0:T(8,128)(2,1)S(1)}, u32[]{:S(2)}, u32[]{:S(2)}) collective-permute-start(bf16[256,512]{1,0:T(8,128)(2,1)S(1)} %sum_parts.4.refs_8_), channel_id=1, source_target_pairs={{0,16},{1,17},{2,18},{3,19},{4,12},{5,13},{6,14},{7,15},{8,24},{9,... | collective-permute-start | bytes 786440 | tf_op jit(solution)/shard_map/ppermute | solution.py:318
  46.1 23.3 %copy-start.2 = (bf16[512,512]{1,0:T(8,128)(2,1)S(1)}, bf16[512,512]{1,0:T(8,128)(2,1)}, u32[]{:S(2)}) copy-start(bf16[512,512]{1,0:T(8,128)(2,1)} %refs_4_.1) | copy-start | bytes 1572868
  46.1 23.3 %copy-start.3 = (bf16[512,512]{1,0:T(8,128)(2,1)S(1)}, bf16[512,512]{1,0:T(8,128)(2,1)}, u32[]{:S(2)}) copy-start(bf16[512,512]{1,0:T(8,128)(2,1)} %refs_5_.1) | copy-start | bytes 1572868
  46.1 23.3 %copy-start.4 = (bf16[512,512]{1,0:T(8,128)(2,1)S(1)}, bf16[512,512]{1,0:T(8,128)(2,1)}, u32[]{:S(2)}) copy-start(bf16[512,512]{1,0:T(8,128)(2,1)} %refs_6_.1) | copy-start | bytes 1572868
  46.1 23.3 %copy-start.5 = (bf16[512,512]{1,0:T(8,128)(2,1)S(1)}, bf16[512,512]{1,0:T(8,128)(2,1)}, u32[]{:S(2)}) copy-start(bf16[512,512]{1,0:T(8,128)(2,1)} %refs_7_.1) | copy-start | bytes 1572868
  47.4 8.3 %collective-permute-start.16 = (bf16[256,512]{1,0:T(8,128)(2,1)S(1)}, bf16[256,512]{1,0:T(8,128)(2,1)S(1)}, u32[]{:S(2)}, u32[]{:S(2)}) collective-permute-start(bf16[256,512]{1,0:T(8,128)(2,1)S(1)} %sum_parts.6), channel_id=1, source_target_pairs={{0,16},{1,17},{2,18},{3,19},{4,12},{5,13},{6,14},{7,15},{8,24},{9,... | collective-permute-start | bytes 786440 | tf_op jit(solution)/shard_map/ppermute | solution.py:318
  49.9 13.1 %collective-permute-start.13 = (bf16[256,512]{1,0:T(8,128)(2,1)S(1)}, bf16[256,512]{1,0:T(8,128)(2,1)S(1)}, u32[]{:S(2)}, u32[]{:S(2)}) collective-permute-start(bf16[256,512]{1,0:T(8,128)(2,1)S(1)} %sum_parts.5), channel_id=1, source_target_pairs={{0,0},{1,1},{2,4},{3,5},{4,2},{5,3},{6,6},{7,7},{8,8},{9,9},{10,12... | collective-permute-start | bytes 786440 | tf_op jit(solution)/shard_map/ppermute | solution.py:318
  56.7 8.5 %collective-permute-start.17 = (bf16[256,512]{1,0:T(8,128)(2,1)S(1)}, bf16[256,512]{1,0:T(8,128)(2,1)S(1)}, u32[]{:S(2)}, u32[]{:S(2)}) collective-permute-start(bf16[256,512]{1,0:T(8,128)(2,1)S(1)} %sum_parts.7), channel_id=1, source_target_pairs={{0,1},{1,0},{2,5},{3,4},{4,3},{5,2},{6,7},{7,6},{8,9},{9,8},{10,13... | collective-permute-start | bytes 786440 | tf_op jit(solution)/shard_map/ppermute | solution.py:318
  63.0 5.2 %collective-permute-start.18 = (bf16[256,512]{1,0:T(8,128)(2,1)S(1)}, bf16[256,512]{1,0:T(8,128)(2,1)S(1)}, u32[]{:S(2)}, u32[]{:S(2)}) collective-permute-start(bf16[256,512]{1,0:T(8,128)(2,1)S(1)} %collective-permute-done.13.refs_0_), channel_id=1, source_target_pairs={{0,4},{1,5},{2,6},{3,7},{4,0},{5,1},{6,2},{7,3},{8,12},{9,13},{10,... | collective-permute-start | bytes 786440 | tf_op jit(solution)/shard_map/ppermute | solution.py:318
  65.2 4.1 %collective-permute-start.19 = (bf16[256,512]{1,0:T(8,128)(2,1)S(1)}, bf16[256,512]{1,0:T(8,128)(2,1)S(1)}, u32[]{:S(2)}, u32[]{:S(2)}) collective-permute-start(bf16[256,512]{1,0:T(8,128)(2,1)S(1)} %collective-permute-done.17.refs_1_), channel_id=1, source_target_pairs={{0,4},{1,5},{2,6},{3,7},{4,0},{5,1},{6,2},{7,3},{8,12},{9,13},{10,... | collective-permute-start | bytes 786440 | tf_op jit(solution)/shard_map/ppermute | solution.py:318
  73.8 8.8 %collective-permute-start.20 = (bf16[4,64,512]{2,1,0:T(8,128)(2,1)S(1)}, bf16[4,64,512]{2,1,0:T(8,128)(2,1)S(1)}, u32[]{:S(2)}, u32[]{:S(2)}) collective-permute-start(bf16[4,64,512]{2,1,0:T(8,128)(2,1)S(1)} %bitcast.21), channel_id=1, source_target_pairs={{1,0},{0,1},{5,2},{4,3},{3,4},{2,5},{7,6},{6,7},{9,8},{8,9},{13,10... | collective-permute-start | bytes 786440 | tf_op jit(solution)/shard_map/ppermute | solution.py:385
  74.8 13.3 %collective-permute-start.21 = (bf16[4,64,512]{2,1,0:T(8,128)(2,1)S(1)}, bf16[4,64,512]{2,1,0:T(8,128)(2,1)S(1)}, u32[]{:S(2)}, u32[]{:S(2)}) collective-permute-start(bf16[4,64,512]{2,1,0:T(8,128)(2,1)S(1)} %bitcast.20), channel_id=1, source_target_pairs={{0,0},{1,1},{4,2},{5,3},{2,4},{3,5},{6,6},{7,7},{8,8},{9,9},{12,10... | collective-permute-start | bytes 786440 | tf_op jit(solution)/shard_map/ppermute | solution.py:385

commit v7 on v6

--- a/solution.py
+++ b/solution.py
@@ -176,7 +176,9 @@
         ],
         compiler_params=pltpu.CompilerParams(vmem_limit_bytes=VMEM_LIMIT),
         cost_estimate=pl.CostEstimate(
-            flops=10**11, bytes_accessed=2 * taps * lags * width * chans, transcendentals=0
+            flops=2 * len(jobs) * count * taps * lags * width * chans,
+            bytes_accessed=2 * taps * lags * width * chans,
+            transcendentals=0,
         ),
         name="conv_sums",
     )(meta, *operands)

time: 89.4 us -> 87.3 us (0.977)
  Pallas kernels: 24.1 us -> 17.6 us
  starting transfers between devices: 35.3 us -> 38 us
  waiting for transfers between devices: 26 us -> 27.8 us
    pallas_call x4, Pallas kernels: 4.43 us -> 0.33 us  [sum_call(): pl.pallas_call(kernel, out_shape=jax.ShapeDtypeStruct(pieces[0].shape, jn...]
    pallas_call x4, Pallas kernels: 13.7 us -> 11.4 us  [conv_call(): pl.pallas_call(functools.partial(conv_kernel, tuple(jobs), parts, group,...]
    ppermute x20, starting transfers between devices: 31.5 us -> 33.6 us  [permute(): return lax.ppermute(block, BOTH, everywhere(sizes, target))]
    ppermute x20, waiting for transfers between devices: 15.4 us -> 17.2 us  [permute(): return lax.ppermute(block, BOTH, everywhere(sizes, target))]
  transfers between devices with their start and end apart: 22 -> 22, of which waited for: 10 -> 10; matrix products, arithmetic and copies ran while one was open for 1% -> 1% of each run, Pallas kernels for 17% -> 11%
where the time goes in v7:
time: 87.3 us; the launch traced here: 87.1 us
  starting transfers between devices  38 us (44%)
  waiting for transfers between devices  27.8 us (32%)
  Pallas kernels  17.6 us (20%)
  local copies, waits for them, and re-layouts  2.48 us (3%)
  other arithmetic  0.96 us (1%)
    ppermute x20, starting transfers between devices, permute(): return lax.ppermute(block, BOTH, everywhere(sizes, target))  33.6 us
    ppermute x20, waiting for transfers between devices, permute(): return lax.ppermute(block, BOTH, everywhere(sizes, target))  17.2 us
    pallas_call x4, Pallas kernels, conv_call(): pl.pallas_call(functools.partial(conv_kernel, tuple(jobs), parts, group,...  11.4 us
    ppermute x2, waiting for transfers between devices, body(): back.append(lax.ppermute(done[p], BOTH, pairs))  10.6 us
    ppermute x2, starting transfers between devices, body(): back.append(lax.ppermute(done[p], BOTH, pairs))  4.41 us
    pallas_call x1, Pallas kernels, attend_call(): pl.pallas_call(functools.partial(attend_kernel, frames, share), out_shape...  4.37 us
  transfers between devices with their start and end apart: 22, of which 10 were waited for; matrix products, arithmetic and copies ran while one was open for 1% of the time, Pallas kernels for 11%

profile of v7, /device:TPU:1, one launch (start us, length us, event | category | flops | bytes accessed | tf_op | source)
XLA Modules:
  0.0 87.1 jit_solution(8516996465758095724)
XLA Ops:
  0.0 0.1 collective-permute-start.1
  0.1 1.0 %slice_bitcast_fusion = (bf16[2,64,512]{2,1,0:T(8,128)(2,1)S(1)}, bf16[2,64,512]{2,1,0:T(8,128)(2,1)S(1)}) fusion(bf16[2,4,64,512]{3,2,1,0:T(8,128)(2,1)} %latents.1), kind=kLoop, calls=%fused_computation.3 | loop fusion | bytes 524288 | tf_op jit(solution)/shard_map/squeeze | solution.py:333
  1.0 4.7 %collective-permute-start = (bf16[2,64,512]{2,1,0:T(8,128)(2,1)S(1)}, bf16[2,64,512]{2,1,0:T(8,128)(2,1)S(1)}, u32[]{:S(2)}, u32[]{:S(2)}) collective-permute-start(bf16[2,64,512]{2,1,0:T(8,128)(2,1)S(1)} %get-tuple-element.40), channel_id=1, source_target_pairs={{0,1},{1,2},{2,3},{4,5},{5,6},{6,7},{8,9},{9,10},{10,11},{12,13},{... | collective-permute-start | bytes 393224 | tf_op jit(solution)/shard_map/ppermute | solution.py:320
  5.7 1.3 %collective-permute-start.2 = (bf16[2,64,512]{2,1,0:T(8,128)(2,1)S(1)}, bf16[2,64,512]{2,1,0:T(8,128)(2,1)S(1)}, u32[]{:S(2)}, u32[]{:S(2)}) collective-permute-start(bf16[2,64,512]{2,1,0:T(8,128)(2,1)S(1)} %get-tuple-element.39), channel_id=1, source_target_pairs={{1,0},{2,1},{3,2},{5,4},{6,5},{7,6},{9,8},{10,9},{11,10},{13,12},{... | collective-permute-start | bytes 393224 | tf_op jit(solution)/shard_map/ppermute | solution.py:320
  7.0 0.1 pad_add_fusion.refs_0_.meta
  7.1 0.0 collective-permute-done.1.refs_2_
  7.1 1.5 %copy-done = bf16[27,64,512]{2,1,0:T(8,128)(2,1)S(1)} copy-done((bf16[27,64,512]{2,1,0:T(8,128)(2,1)S(1)}, bf16[27,64,512]{2,1,0:T(8,128)(2,1)}, u32[]{:S(2)}) %copy-start) | copy-done | bytes 1769496
  8.6 0.9 merge_kernel_slices.1.refs_1_
  9.5 0.0 collective-permute-done.above
  9.5 3.0 %collective-permute-done.2.below = bf16[2,64,512]{2,1,0:T(8,128)(2,1)S(1)} collective-permute-done((bf16[2,64,512]{2,1,0:T(8,128)(2,1)S(1)}, bf16[2,64,512]{2,1,0:T(8,128)(2,1)S(1)}, u32[]{:S(2)}, u32[]{:S(2)}) %collective-permute-start.2) | collective-permute-done | bytes 131104 | tf_op jit(solution)/shard_map/ppermute | solution.py:320
  12.4 0.0 copy-done.1
  12.4 0.7 frame_parts.1
  13.1 1.3 %collective-permute-start.5 = (bf16[2,6,64,128]{3,2,1,0:T(8,128)(2,1)S(1)}, bf16[2,6,64,128]{3,2,1,0:T(8,128)(2,1)S(1)}, u32[]{:S(2)}, u32[]{:S(2)}) collective-permute-start(bf16[2,6,64,128]{3,2,1,0:T(8,128)(2,1)S(1)} %get-tuple-element.25), channel_id=1, source_target_pairs={{0,8},{1,9},{2,10},{3,11},{4,20},{5,21},{6,22},{7,23},{8,0},{9,1},... | collective-permute-start | bytes 589832 | tf_op jit(solution)/shard_map/ppermute | solution.py:320
  14.4 1.2 %collective-permute-start.3 = (bf16[2,6,64,128]{3,2,1,0:T(8,128)(2,1)S(1)}, bf16[2,6,64,128]{3,2,1,0:T(8,128)(2,1)S(1)}, u32[]{:S(2)}, u32[]{:S(2)}) collective-permute-start(bf16[2,6,64,128]{3,2,1,0:T(8,128)(2,1)S(1)} %get-tuple-element.24), channel_id=1, source_target_pairs={{0,16},{1,17},{2,18},{3,19},{4,12},{5,13},{6,14},{7,15},{8,24},{9,... | collective-permute-start | bytes 589832 | tf_op jit(solution)/shard_map/ppermute | solution.py:320
  15.6 0.2 collective-permute-start.8
  15.8 1.9 %collective-permute-start.4 = (bf16[2,6,64,128]{3,2,1,0:T(8,128)(2,1)S(1)}, bf16[2,6,64,128]{3,2,1,0:T(8,128)(2,1)S(1)}, u32[]{:S(2)}, u32[]{:S(2)}) collective-permute-start(bf16[2,6,64,128]{3,2,1,0:T(8,128)(2,1)S(1)} %get-tuple-element.23.refs_2_), channel_id=1, source_target_pairs={{0,4},{1,5},{2,6},{3,7},{4,0},{5,1},{6,2},{7,3},{8,12},{9,13},{10,... | collective-permute-start | bytes 589832 | tf_op jit(solution)/shard_map/ppermute | solution.py:320
  17.8 0.2 collective-permute-done.5.refs_2_
  18.0 4.1 %collective-permute-start.6 = (bf16[2,6,64,128]{3,2,1,0:T(8,128)(2,1)S(1)}, bf16[2,6,64,128]{3,2,1,0:T(8,128)(2,1)S(1)}, u32[]{:S(2)}, u32[]{:S(2)}) collective-permute-start(bf16[2,6,64,128]{3,2,1,0:T(8,128)(2,1)S(1)} %collective-permute-done.5.refs_2_), channel_id=1, source_target_pairs={{0,4},{1,5},{2,6},{3,7},{4,0},{5,1},{6,2},{7,3},{8,12},{9,13},{10,... | collective-permute-start | bytes 589832 | tf_op jit(solution)/shard_map/ppermute | solution.py:320
  22.1 0.0 collective-permute-done.3.refs_3_
  22.1 0.5 collective-permute-start.7
  22.6 1.7 %collective-permute-done.8.refs_3_ = bf16[2,6,64,128]{3,2,1,0:T(8,128)(2,1)S(1)} collective-permute-done((bf16[2,6,64,128]{3,2,1,0:T(8,128)(2,1)S(1)}, bf16[2,6,64,128]{3,2,1,0:T(8,128)(2,1)S(1)}, u32[]{:S(2)}, u32[]{:S(2)}) %collective-permute-start.8) | collective-permute-done | bytes 196640 | tf_op jit(solution)/shard_map/ppermute | solution.py:320
  24.2 1.6 %collective-permute-start.9 = (bf16[2,6,64,128]{3,2,1,0:T(8,128)(2,1)S(1)}, bf16[2,6,64,128]{3,2,1,0:T(8,128)(2,1)S(1)}, u32[]{:S(2)}, u32[]{:S(2)}) collective-permute-start(bf16[2,6,64,128]{3,2,1,0:T(8,128)(2,1)S(1)} %collective-permute-done.8.refs_3_), channel_id=1, source_target_pairs={{0,4},{1,5},{2,6},{3,7},{4,0},{5,1},{6,2},{7,3},{8,12},{9,13},{10,... | collective-permute-start | bytes 589832 | tf_op jit(solution)/shard_map/ppermute | solution.py:320
  25.9 0.0 collective-permute-done.4.refs_4_
  25.9 0.0 collective-permute-done.6.refs_5_
  25.9 0.0 collective-permute-done.7.refs_6_
  25.9 1.1 %collective-permute-done.9.refs_7_ = bf16[2,6,64,128]{3,2,1,0:T(8,128)(2,1)S(1)} collective-permute-done((bf16[2,6,64,128]{3,2,1,0:T(8,128)(2,1)S(1)}, bf16[2,6,64,128]{3,2,1,0:T(8,128)(2,1)S(1)}, u32[]{:S(2)}, u32[]{:S(2)}) %collective-permute-start.9) | collective-permute-done | bytes 196640 | tf_op jit(solution)/shard_map/ppermute | solution.py:320
  27.0 2.8 %conv_sums.4 = (bf16[256,512]{1,0:T(8,128)(2,1)S(1)}, bf16[256,512]{1,0:T(8,128)(2,1)S(1)}) custom-call(s32[3]{0:T(128)S(1)} %pad_add_fusion.refs_0_.meta, bf16[3,9,128,512]{3,2,1,0:T(8,128)(2,1)S(1)} %merge_kernel_slices.1.refs_1_, bf16[2,6,64,128]{3,2,1,0:T(8,128)(2,1)S(1)} %collective-permute-done.5.refs_2_, ...), custom_call_target="tpu_custom_call" | custom-call | flops 1811939328 | bytes 3538944 | tf_op jit(solution)/shard_map/conv_sums/pallas_call | solution.py:169
  29.8 1.3 %collective-permute-start.10 = (bf16[256,512]{1,0:T(8,128)(2,1)S(1)}, bf16[256,512]{1,0:T(8,128)(2,1)S(1)}, u32[]{:S(2)}, u32[]{:S(2)}) collective-permute-start(bf16[256,512]{1,0:T(8,128)(2,1)S(1)} %get-tuple-element.30), channel_id=1, source_target_pairs={{0,8},{1,9},{2,10},{3,11},{4,20},{5,21},{6,22},{7,23},{8,0},{9,1},... | collective-permute-start | bytes 786440 | tf_op jit(solution)/shard_map/ppermute | solution.py:320
  31.1 0.2 collective-permute-start.11
  31.3 2.8 %conv_sums.5 = (bf16[256,512]{1,0:T(8,128)(2,1)S(1)}, bf16[256,512]{1,0:T(8,128)(2,1)S(1)}) custom-call(s32[3]{0:T(128)S(1)} %pad_add_fusion.refs_0_.meta, bf16[3,9,128,512]{3,2,1,0:T(8,128)(2,1)S(1)} %merge_kernel_slices.1.refs_1_, bf16[2,6,64,128]{3,2,1,0:T(8,128)(2,1)S(1)} %collective-permute-done.5.refs_2_, ...), custom_call_target="tpu_custom_call" | custom-call | flops 1811939328 | bytes 3538944 | tf_op jit(solution)/shard_map/conv_sums/pallas_call | solution.py:169
  34.2 1.3 %collective-permute-start.14 = (bf16[256,512]{1,0:T(8,128)(2,1)S(1)}, bf16[256,512]{1,0:T(8,128)(2,1)S(1)}, u32[]{:S(2)}, u32[]{:S(2)}) collective-permute-start(bf16[256,512]{1,0:T(8,128)(2,1)S(1)} %get-tuple-element.33), channel_id=1, source_target_pairs={{0,8},{1,9},{2,10},{3,11},{4,20},{5,21},{6,22},{7,23},{8,0},{9,1},... | collective-permute-start | bytes 786440 | tf_op jit(solution)/shard_map/ppermute | solution.py:320
  35.5 0.2 collective-permute-start.15
  35.7 2.8 %conv_sums.6 = (f32[256,512]{1,0:T(8,128)S(1)}, f32[256,512]{1,0:T(8,128)S(1)}) custom-call(s32[3]{0:T(128)S(1)} %pad_add_fusion.refs_0_.meta, bf16[3,9,128,512]{3,2,1,0:T(8,128)(2,1)S(1)} %merge_kernel_slices.1.refs_1_, bf16[2,6,64,128]{3,2,1,0:T(8,128)(2,1)S(1)} %get-tuple-element.23.refs_2_, bf16[2,6,64,128]{3,2,1,0:T(8,128)(2,1)S(1)} %collective-permute-done.3.refs_3_, ...), custom_call_target="tpu_custom_call" | custom-call | flops 1811939328 | bytes 3538944 | tf_op jit(solution)/shard_map/conv_sums/pallas_call | solution.py:169
  38.6 0.0 collective-permute-done.10.refs_2_.refs_1_
  38.6 0.0 collective-permute-done.11.refs_1_
  38.6 0.1 sum_parts.4.refs_8_
  38.7 1.3 %collective-permute-start.12 = (bf16[256,512]{1,0:T(8,128)(2,1)S(1)}, bf16[256,512]{1,0:T(8,128)(2,1)S(1)}, u32[]{:S(2)}, u32[]{:S(2)}) collective-permute-start(bf16[256,512]{1,0:T(8,128)(2,1)S(1)} %sum_parts.4.refs_8_), channel_id=1, source_target_pairs={{0,16},{1,17},{2,18},{3,19},{4,12},{5,13},{6,14},{7,15},{8,24},{9,... | collective-permute-start | bytes 786440 | tf_op jit(solution)/shard_map/ppermute | solution.py:320
  40.0 2.8 %conv_sums.7 = (f32[256,512]{1,0:T(8,128)S(1)}, f32[256,512]{1,0:T(8,128)S(1)}) custom-call(s32[3]{0:T(128)S(1)} %pad_add_fusion.refs_0_.meta, bf16[3,9,128,512]{3,2,1,0:T(8,128)(2,1)S(1)} %merge_kernel_slices.1.refs_1_, bf16[2,6,64,128]{3,2,1,0:T(8,128)(2,1)S(1)} %get-tuple-element.23.refs_2_, bf16[2,6,64,128]{3,2,1,0:T(8,128)(2,1)S(1)} %collective-permute-done.3.refs_3_, ...), custom_call_target="tpu_custom_call" | custom-call | flops 1811939328 | bytes 3538944 | tf_op jit(solution)/shard_map/conv_sums/pallas_call | solution.py:169
  42.8 0.0 collective-permute-done.14.refs_2_.refs_1_
  42.8 1.3 %collective-permute-done.15.refs_1_ = bf16[256,512]{1,0:T(8,128)(2,1)S(1)} collective-permute-done((bf16[256,512]{1,0:T(8,128)(2,1)S(1)}, bf16[256,512]{1,0:T(8,128)(2,1)S(1)}, u32[]{:S(2)}, u32[]{:S(2)}) %collective-permute-start.15) | collective-permute-done | bytes 262176 | tf_op jit(solution)/shard_map/ppermute | solution.py:320
  44.2 0.1 sum_parts.6
  44.2 1.2 %collective-permute-start.16 = (bf16[256,512]{1,0:T(8,128)(2,1)S(1)}, bf16[256,512]{1,0:T(8,128)(2,1)S(1)}, u32[]{:S(2)}, u32[]{:S(2)}) collective-permute-start(bf16[256,512]{1,0:T(8,128)(2,1)S(1)} %sum_parts.6), channel_id=1, source_target_pairs={{0,16},{1,17},{2,18},{3,19},{4,12},{5,13},{6,14},{7,15},{8,24},{9,... | collective-permute-start | bytes 786440 | tf_op jit(solution)/shard_map/ppermute | solution.py:320
  45.5 1.6 %collective-permute-done.12.refs_2_ = bf16[256,512]{1,0:T(8,128)(2,1)S(1)} collective-permute-done((bf16[256,512]{1,0:T(8,128)(2,1)S(1)}, bf16[256,512]{1,0:T(8,128)(2,1)S(1)}, u32[]{:S(2)}, u32[]{:S(2)}) %collective-permute-start.12) | collective-permute-done | bytes 262176 | tf_op jit(solution)/shard_map/ppermute | solution.py:320
  47.1 0.1 sum_parts.5
  47.2 6.8 %collective-permute-start.13 = (bf16[256,512]{1,0:T(8,128)(2,1)S(1)}, bf16[256,512]{1,0:T(8,128)(2,1)S(1)}, u32[]{:S(2)}, u32[]{:S(2)}) collective-permute-start(bf16[256,512]{1,0:T(8,128)(2,1)S(1)} %sum_parts.5), channel_id=1, source_target_pairs={{0,0},{1,1},{2,4},{3,5},{4,2},{5,3},{6,6},{7,7},{8,8},{9,9},{10,12... | collective-permute-start | bytes 786440 | tf_op jit(solution)/shard_map/ppermute | solution.py:320
  54.1 0.0 collective-permute-done.16.refs_2_
  54.1 0.1 sum_parts.7
  54.2 1.9 %collective-permute-start.17 = (bf16[256,512]{1,0:T(8,128)(2,1)S(1)}, bf16[256,512]{1,0:T(8,128)(2,1)S(1)}, u32[]{:S(2)}, u32[]{:S(2)}) collective-permute-start(bf16[256,512]{1,0:T(8,128)(2,1)S(1)} %sum_parts.7), channel_id=1, source_target_pairs={{0,1},{1,0},{2,5},{3,4},{4,3},{5,2},{6,7},{7,6},{8,9},{9,8},{10,13... | collective-permute-start | bytes 786440 | tf_op jit(solution)/shard_map/ppermute | solution.py:320
  56.1 7.1 %collective-permute-done.13.refs_0_ = bf16[256,512]{1,0:T(8,128)(2,1)S(1)} collective-permute-done((bf16[256,512]{1,0:T(8,128)(2,1)S(1)}, bf16[256,512]{1,0:T(8,128)(2,1)S(1)}, u32[]{:S(2)}, u32[]{:S(2)}) %collective-permute-start.13) | collective-permute-done | bytes 262176 | tf_op jit(solution)/shard_map/ppermute | solution.py:320
  63.2 0.0 collective-permute-start.18
  63.2 0.0 collective-permute-done.17.refs_1_
  63.2 2.4 %collective-permute-start.19 = (bf16[256,512]{1,0:T(8,128)(2,1)S(1)}, bf16[256,512]{1,0:T(8,128)(2,1)S(1)}, u32[]{:S(2)}, u32[]{:S(2)}) collective-permute-start(bf16[256,512]{1,0:T(8,128)(2,1)S(1)} %collective-permute-done.17.refs_1_), channel_id=1, source_target_pairs={{0,4},{1,5},{2,6},{3,7},{4,0},{5,1},{6,2},{7,3},{8,12},{9,13},{10,... | collective-permute-start | bytes 786440 | tf_op jit(solution)/shard_map/ppermute | solution.py:320
  65.6 0.0 collective-permute-done.18.refs_2_
  65.7 1.2 %collective-permute-done.19.refs_3_ = bf16[256,512]{1,0:T(8,128)(2,1)S(1)} collective-permute-done((bf16[256,512]{1,0:T(8,128)(2,1)S(1)}, bf16[256,512]{1,0:T(8,128)(2,1)S(1)}, u32[]{:S(2)}, u32[]{:S(2)}) %collective-permute-start.19) | collective-permute-done | bytes 262176 | tf_op jit(solution)/shard_map/ppermute | solution.py:320
  66.8 0.0 copy-done.2
  66.8 0.0 copy-done.3
  66.8 0.0 copy-done.4
  66.8 0.0 copy-done.5
  66.8 4.4 %attend.1 = (bf16[256,512]{1,0:T(8,128)(2,1)S(1)}, bf16[256,512]{1,0:T(8,128)(2,1)S(1)}) custom-call(bf16[256,512]{1,0:T(8,128)(2,1)S(1)} %collective-permute-done.13.refs_0_, bf16[256,512]{1,0:T(8,128)(2,1)S(1)} %collective-permute-done.17.refs_1_, bf16[256,512]{1,0:T(8,128)(2,1)S(1)} %collective-permute-done.18.refs_2_, ...), custom_call_target="tpu_custom_call" | custom-call | flops 2684354560 | bytes 3145728 | tf_op jit(solution)/shard_map/attend/pallas_call | solution.py:291
  71.2 2.1 %collective-permute-start.20 = (bf16[4,64,512]{2,1,0:T(8,128)(2,1)S(1)}, bf16[4,64,512]{2,1,0:T(8,128)(2,1)S(1)}, u32[]{:S(2)}, u32[]{:S(2)}) collective-permute-start(bf16[4,64,512]{2,1,0:T(8,128)(2,1)S(1)} %bitcast.21), channel_id=1, source_target_pairs={{1,0},{0,1},{5,2},{4,3},{3,4},{2,5},{7,6},{6,7},{9,8},{8,9},{13,10... | collective-permute-start | bytes 786440 | tf_op jit(solution)/shard_map/ppermute | solution.py:387
  73.3 2.3 %collective-permute-start.21 = (bf16[4,64,512]{2,1,0:T(8,128)(2,1)S(1)}, bf16[4,64,512]{2,1,0:T(8,128)(2,1)S(1)}, u32[]{:S(2)}, u32[]{:S(2)}) collective-permute-start(bf16[4,64,512]{2,1,0:T(8,128)(2,1)S(1)} %bitcast.20), channel_id=1, source_target_pairs={{0,0},{1,1},{4,2},{5,3},{2,4},{3,5},{6,6},{7,7},{8,8},{9,9},{12,10... | collective-permute-start | bytes 786440 | tf_op jit(solution)/shard_map/ppermute | solution.py:387
  75.6 5.2 %collective-permute-done.20 = bf16[4,64,512]{2,1,0:T(8,128)(2,1)S(1)} collective-permute-done((bf16[4,64,512]{2,1,0:T(8,128)(2,1)S(1)}, bf16[4,64,512]{2,1,0:T(8,128)(2,1)S(1)}, u32[]{:S(2)}, u32[]{:S(2)}) %collective-permute-start.20) | collective-permute-done | bytes 262176 | tf_op jit(solution)/shard_map/ppermute | solution.py:387
  80.8 5.4 %collective-permute-done.21 = bf16[4,64,512]{2,1,0:T(8,128)(2,1)S(1)} collective-permute-done((bf16[4,64,512]{2,1,0:T(8,128)(2,1)S(1)}, bf16[4,64,512]{2,1,0:T(8,128)(2,1)S(1)}, u32[]{:S(2)}, u32[]{:S(2)}) %collective-permute-start.21) | collective-permute-done | bytes 262176 | tf_op jit(solution)/shard_map/ppermute | solution.py:387
  86.2 0.8 pad_maximum_fusion
  (7 shorter events, 0.0 us)
Async XLA Ops:
  0.0 7.1 %collective-permute-start.1 = (bf16[9,3,64,512]{3,2,1,0:T(8,128)(2,1)}, bf16[9,3,64,512]{3,2,1,0:T(8,128)(2,1)S(1)}, u32[]{:S(2)}, u32[]{:S(2)}) collective-permute-start(bf16[9,3,64,512]{3,2,1,0:T(8,128)(2,1)} %bitcast.18), channel_id=1, source_target_pairs={{0,4},{1,5},{2,6},{3,7},{4,0},{5,1},{6,2},{7,3},{8,12},{9,13},{10,... | collective-permute-start | bytes 5308424 | tf_op jit(solution)/shard_map/ppermute | solution.py:320
  1.0 8.4 %collective-permute-start = (bf16[2,64,512]{2,1,0:T(8,128)(2,1)S(1)}, bf16[2,64,512]{2,1,0:T(8,128)(2,1)S(1)}, u32[]{:S(2)}, u32[]{:S(2)}) collective-permute-start(bf16[2,64,512]{2,1,0:T(8,128)(2,1)S(1)} %get-tuple-element.40), channel_id=1, source_target_pairs={{0,1},{1,2},{2,3},{4,5},{5,6},{6,7},{8,9},{9,10},{10,11},{12,13},{... | collective-permute-start | bytes 393224 | tf_op jit(solution)/shard_map/ppermute | solution.py:320
  5.7 6.7 %collective-permute-start.2 = (bf16[2,64,512]{2,1,0:T(8,128)(2,1)S(1)}, bf16[2,64,512]{2,1,0:T(8,128)(2,1)S(1)}, u32[]{:S(2)}, u32[]{:S(2)}) collective-permute-start(bf16[2,64,512]{2,1,0:T(8,128)(2,1)S(1)} %get-tuple-element.39), channel_id=1, source_target_pairs={{1,0},{2,1},{3,2},{5,4},{6,5},{7,6},{9,8},{10,9},{11,10},{13,12},{... | collective-permute-start | bytes 393224 | tf_op jit(solution)/shard_map/ppermute | solution.py:320
  7.1 1.5 %copy-start = (bf16[27,64,512]{2,1,0:T(8,128)(2,1)S(1)}, bf16[27,64,512]{2,1,0:T(8,128)(2,1)}, u32[]{:S(2)}) copy-start(bf16[27,64,512]{2,1,0:T(8,128)(2,1)} %param.7) | copy-start | bytes 5308420
  8.6 3.8 %copy-start.1 = (bf16[2,4,64,512]{3,2,1,0:T(8,128)(2,1)S(1)}, bf16[2,4,64,512]{3,2,1,0:T(8,128)(2,1)}, u32[]{:S(2)}) copy-start(bf16[2,4,64,512]{3,2,1,0:T(8,128)(2,1)} %latents.1) | copy-start | bytes 1572868
  13.1 4.9 %collective-permute-start.5 = (bf16[2,6,64,128]{3,2,1,0:T(8,128)(2,1)S(1)}, bf16[2,6,64,128]{3,2,1,0:T(8,128)(2,1)S(1)}, u32[]{:S(2)}, u32[]{:S(2)}) collective-permute-start(bf16[2,6,64,128]{3,2,1,0:T(8,128)(2,1)S(1)} %get-tuple-element.25), channel_id=1, source_target_pairs={{0,8},{1,9},{2,10},{3,11},{4,20},{5,21},{6,22},{7,23},{8,0},{9,1},... | collective-permute-start | bytes 589832 | tf_op jit(solution)/shard_map/ppermute | solution.py:320
  14.4 7.6 %collective-permute-start.3 = (bf16[2,6,64,128]{3,2,1,0:T(8,128)(2,1)S(1)}, bf16[2,6,64,128]{3,2,1,0:T(8,128)(2,1)S(1)}, u32[]{:S(2)}, u32[]{:S(2)}) collective-permute-start(bf16[2,6,64,128]{3,2,1,0:T(8,128)(2,1)S(1)} %get-tuple-element.24), channel_id=1, source_target_pairs={{0,16},{1,17},{2,18},{3,19},{4,12},{5,13},{6,14},{7,15},{8,24},{9,... | collective-permute-start | bytes 589832 | tf_op jit(solution)/shard_map/ppermute | solution.py:320
  15.6 8.6 %collective-permute-start.8 = (bf16[2,6,64,128]{3,2,1,0:T(8,128)(2,1)S(1)}, bf16[2,6,64,128]{3,2,1,0:T(8,128)(2,1)S(1)}, u32[]{:S(2)}, u32[]{:S(2)}) collective-permute-start(bf16[2,6,64,128]{3,2,1,0:T(8,128)(2,1)S(1)} %get-tuple-element.26), channel_id=1, source_target_pairs={{0,24},{1,25},{2,26},{3,27},{4,28},{5,29},{6,30},{7,31},{8,16},{9,... | collective-permute-start | bytes 589832 | tf_op jit(solution)/shard_map/ppermute | solution.py:320
  15.8 10.1 %collective-permute-start.4 = (bf16[2,6,64,128]{3,2,1,0:T(8,128)(2,1)S(1)}, bf16[2,6,64,128]{3,2,1,0:T(8,128)(2,1)S(1)}, u32[]{:S(2)}, u32[]{:S(2)}) collective-permute-start(bf16[2,6,64,128]{3,2,1,0:T(8,128)(2,1)S(1)} %get-tuple-element.23.refs_2_), channel_id=1, source_target_pairs={{0,4},{1,5},{2,6},{3,7},{4,0},{5,1},{6,2},{7,3},{8,12},{9,13},{10,... | collective-permute-start | bytes 589832 | tf_op jit(solution)/shard_map/ppermute | solution.py:320
  18.0 7.9 %collective-permute-start.6 = (bf16[2,6,64,128]{3,2,1,0:T(8,128)(2,1)S(1)}, bf16[2,6,64,128]{3,2,1,0:T(8,128)(2,1)S(1)}, u32[]{:S(2)}, u32[]{:S(2)}) collective-permute-start(bf16[2,6,64,128]{3,2,1,0:T(8,128)(2,1)S(1)} %collective-permute-done.5.refs_2_), channel_id=1, source_target_pairs={{0,4},{1,5},{2,6},{3,7},{4,0},{5,1},{6,2},{7,3},{8,12},{9,13},{10,... | collective-permute-start | bytes 589832 | tf_op jit(solution)/shard_map/ppermute | solution.py:320
  22.1 3.8 %collective-permute-start.7 = (bf16[2,6,64,128]{3,2,1,0:T(8,128)(2,1)S(1)}, bf16[2,6,64,128]{3,2,1,0:T(8,128)(2,1)S(1)}, u32[]{:S(2)}, u32[]{:S(2)}) collective-permute-start(bf16[2,6,64,128]{3,2,1,0:T(8,128)(2,1)S(1)} %collective-permute-done.3.refs_3_), channel_id=1, source_target_pairs={{0,4},{1,5},{2,6},{3,7},{4,0},{5,1},{6,2},{7,3},{8,12},{9,13},{10,... | collective-permute-start | bytes 589832 | tf_op jit(solution)/shard_map/ppermute | solution.py:320
  24.2 2.7 %collective-permute-start.9 = (bf16[2,6,64,128]{3,2,1,0:T(8,128)(2,1)S(1)}, bf16[2,6,64,128]{3,2,1,0:T(8,128)(2,1)S(1)}, u32[]{:S(2)}, u32[]{:S(2)}) collective-permute-start(bf16[2,6,64,128]{3,2,1,0:T(8,128)(2,1)S(1)} %collective-permute-done.8.refs_3_), channel_id=1, source_target_pairs={{0,4},{1,5},{2,6},{3,7},{4,0},{5,1},{6,2},{7,3},{8,12},{9,13},{10,... | collective-permute-start | bytes 589832 | tf_op jit(solution)/shard_map/ppermute | solution.py:320
  29.8 8.8 %collective-permute-start.10 = (bf16[256,512]{1,0:T(8,128)(2,1)S(1)}, bf16[256,512]{1,0:T(8,128)(2,1)S(1)}, u32[]{:S(2)}, u32[]{:S(2)}) collective-permute-start(bf16[256,512]{1,0:T(8,128)(2,1)S(1)} %get-tuple-element.30), channel_id=1, source_target_pairs={{0,8},{1,9},{2,10},{3,11},{4,20},{5,21},{6,22},{7,23},{8,0},{9,1},... | collective-permute-start | bytes 786440 | tf_op jit(solution)/shard_map/ppermute | solution.py:320
  31.1 7.5 %collective-permute-start.11 = (bf16[256,512]{1,0:T(8,128)(2,1)S(1)}, bf16[256,512]{1,0:T(8,128)(2,1)S(1)}, u32[]{:S(2)}, u32[]{:S(2)}) collective-permute-start(bf16[256,512]{1,0:T(8,128)(2,1)S(1)} %get-tuple-element.27.refs_8_), channel_id=1, source_target_pairs={{0,8},{1,9},{2,10},{3,11},{4,20},{5,21},{6,22},{7,23},{8,0},{9,1},... | collective-permute-start | bytes 786440 | tf_op jit(solution)/shard_map/ppermute | solution.py:320
  34.2 8.6 %collective-permute-start.14 = (bf16[256,512]{1,0:T(8,128)(2,1)S(1)}, bf16[256,512]{1,0:T(8,128)(2,1)S(1)}, u32[]{:S(2)}, u32[]{:S(2)}) collective-permute-start(bf16[256,512]{1,0:T(8,128)(2,1)S(1)} %get-tuple-element.33), channel_id=1, source_target_pairs={{0,8},{1,9},{2,10},{3,11},{4,20},{5,21},{6,22},{7,23},{8,0},{9,1},... | collective-permute-start | bytes 786440 | tf_op jit(solution)/shard_map/ppermute | solution.py:320
  35.5 8.6 %collective-permute-start.15 = (bf16[256,512]{1,0:T(8,128)(2,1)S(1)}, bf16[256,512]{1,0:T(8,128)(2,1)S(1)}, u32[]{:S(2)}, u32[]{:S(2)}) collective-permute-start(bf16[256,512]{1,0:T(8,128)(2,1)S(1)} %get-tuple-element.28.refs_8_), channel_id=1, source_target_pairs={{0,8},{1,9},{2,10},{3,11},{4,20},{5,21},{6,22},{7,23},{8,0},{9,1},... | collective-permute-start | bytes 786440 | tf_op jit(solution)/shard_map/ppermute | solution.py:320
  38.7 8.5 %collective-permute-start.12 = (bf16[256,512]{1,0:T(8,128)(2,1)S(1)}, bf16[256,512]{1,0:T(8,128)(2,1)S(1)}, u32[]{:S(2)}, u32[]{:S(2)}) collective-permute-start(bf16[256,512]{1,0:T(8,128)(2,1)S(1)} %sum_parts.4.refs_8_), channel_id=1, source_target_pairs={{0,16},{1,17},{2,18},{3,19},{4,12},{5,13},{6,14},{7,15},{8,24},{9,... | collective-permute-start | bytes 786440 | tf_op jit(solution)/shard_map/ppermute | solution.py:320
  44.2 22.7 %copy-start.2 = (bf16[512,512]{1,0:T(8,128)(2,1)S(1)}, bf16[512,512]{1,0:T(8,128)(2,1)}, u32[]{:S(2)}) copy-start(bf16[512,512]{1,0:T(8,128)(2,1)} %refs_4_.1) | copy-start | bytes 1572868
  44.2 22.7 %copy-start.3 = (bf16[512,512]{1,0:T(8,128)(2,1)S(1)}, bf16[512,512]{1,0:T(8,128)(2,1)}, u32[]{:S(2)}) copy-start(bf16[512,512]{1,0:T(8,128)(2,1)} %refs_5_.1) | copy-start | bytes 1572868
  44.2 22.7 %copy-start.4 = (bf16[512,512]{1,0:T(8,128)(2,1)S(1)}, bf16[512,512]{1,0:T(8,128)(2,1)}, u32[]{:S(2)}) copy-start(bf16[512,512]{1,0:T(8,128)(2,1)} %refs_6_.1) | copy-start | bytes 1572868
  44.2 22.7 %copy-start.5 = (bf16[512,512]{1,0:T(8,128)(2,1)S(1)}, bf16[512,512]{1,0:T(8,128)(2,1)}, u32[]{:S(2)}) copy-start(bf16[512,512]{1,0:T(8,128)(2,1)} %refs_7_.1) | copy-start | bytes 1572868
  44.2 9.8 %collective-permute-start.16 = (bf16[256,512]{1,0:T(8,128)(2,1)S(1)}, bf16[256,512]{1,0:T(8,128)(2,1)S(1)}, u32[]{:S(2)}, u32[]{:S(2)}) collective-permute-start(bf16[256,512]{1,0:T(8,128)(2,1)S(1)} %sum_parts.6), channel_id=1, source_target_pairs={{0,16},{1,17},{2,18},{3,19},{4,12},{5,13},{6,14},{7,15},{8,24},{9,... | collective-permute-start | bytes 786440 | tf_op jit(solution)/shard_map/ppermute | solution.py:320
  47.2 16.0 %collective-permute-start.13 = (bf16[256,512]{1,0:T(8,128)(2,1)S(1)}, bf16[256,512]{1,0:T(8,128)(2,1)S(1)}, u32[]{:S(2)}, u32[]{:S(2)}) collective-permute-start(bf16[256,512]{1,0:T(8,128)(2,1)S(1)} %sum_parts.5), channel_id=1, source_target_pairs={{0,0},{1,1},{2,4},{3,5},{4,2},{5,3},{6,6},{7,7},{8,8},{9,9},{10,12... | collective-permute-start | bytes 786440 | tf_op jit(solution)/shard_map/ppermute | solution.py:320
  54.2 9.0 %collective-permute-start.17 = (bf16[256,512]{1,0:T(8,128)(2,1)S(1)}, bf16[256,512]{1,0:T(8,128)(2,1)S(1)}, u32[]{:S(2)}, u32[]{:S(2)}) collective-permute-start(bf16[256,512]{1,0:T(8,128)(2,1)S(1)} %sum_parts.7), channel_id=1, source_target_pairs={{0,1},{1,0},{2,5},{3,4},{4,3},{5,2},{6,7},{7,6},{8,9},{9,8},{10,13... | collective-permute-start | bytes 786440 | tf_op jit(solution)/shard_map/ppermute | solution.py:320
  63.2 2.4 %collective-permute-start.18 = (bf16[256,512]{1,0:T(8,128)(2,1)S(1)}, bf16[256,512]{1,0:T(8,128)(2,1)S(1)}, u32[]{:S(2)}, u32[]{:S(2)}) collective-permute-start(bf16[256,512]{1,0:T(8,128)(2,1)S(1)} %collective-permute-done.13.refs_0_), channel_id=1, source_target_pairs={{0,4},{1,5},{2,6},{3,7},{4,0},{5,1},{6,2},{7,3},{8,12},{9,13},{10,... | collective-permute-start | bytes 786440 | tf_op jit(solution)/shard_map/ppermute | solution.py:320
  63.2 3.6 %collective-permute-start.19 = (bf16[256,512]{1,0:T(8,128)(2,1)S(1)}, bf16[256,512]{1,0:T(8,128)(2,1)S(1)}, u32[]{:S(2)}, u32[]{:S(2)}) collective-permute-start(bf16[256,512]{1,0:T(8,128)(2,1)S(1)} %collective-permute-done.17.refs_1_), channel_id=1, source_target_pairs={{0,4},{1,5},{2,6},{3,7},{4,0},{5,1},{6,2},{7,3},{8,12},{9,13},{10,... | collective-permute-start | bytes 786440 | tf_op jit(solution)/shard_map/ppermute | solution.py:320
  71.2 9.6 %collective-permute-start.20 = (bf16[4,64,512]{2,1,0:T(8,128)(2,1)S(1)}, bf16[4,64,512]{2,1,0:T(8,128)(2,1)S(1)}, u32[]{:S(2)}, u32[]{:S(2)}) collective-permute-start(bf16[4,64,512]{2,1,0:T(8,128)(2,1)S(1)} %bitcast.21), channel_id=1, source_target_pairs={{1,0},{0,1},{5,2},{4,3},{3,4},{2,5},{7,6},{6,7},{9,8},{8,9},{13,10... | collective-permute-start | bytes 786440 | tf_op jit(solution)/shard_map/ppermute | solution.py:387
  73.3 12.9 %collective-permute-start.21 = (bf16[4,64,512]{2,1,0:T(8,128)(2,1)S(1)}, bf16[4,64,512]{2,1,0:T(8,128)(2,1)S(1)}, u32[]{:S(2)}, u32[]{:S(2)}) collective-permute-start(bf16[4,64,512]{2,1,0:T(8,128)(2,1)S(1)} %bitcast.20), channel_id=1, source_target_pairs={{0,0},{1,1},{4,2},{5,3},{2,4},{3,5},{6,6},{7,7},{8,8},{9,9},{12,10... | collective-permute-start | bytes 786440 | tf_op jit(solution)/shard_map/ppermute | solution.py:387

commit v8 on v3

--- a/solution.py
+++ b/solution.py
@@ -80,7 +80,7 @@
     return pl.pallas_call(
         kernel,
         out_shape=[out] * 2,
-        in_specs=in_vmem(len(pieces)) + [pl.BlockSpec(memory_space=pl.ANY)],
+        in_specs=in_vmem(len(pieces) + 1),
         out_specs=in_vmem(2),
         compiler_params=pltpu.CompilerParams(vmem_limit_bytes=VMEM_LIMIT),
         name="halo_rows",
@@ -166,7 +166,7 @@
     counts = [frames * (2 if rim else rows_here - 2) * columns for _, rim in jobs]
     operands = [weights, *[held[s] for s in dests], *before, *(halos if any_rim else ())]
     specs = [pl.BlockSpec(memory_space=pltpu.SMEM)] + in_vmem(len(operands))
-    specs += [pl.BlockSpec(memory_space=pl.ANY)] * len(after)
+    specs += in_vmem(len(after))
     return pl.pallas_call(
         functools.partial(conv_kernel, tuple(jobs), parts, frames),
         out_shape=[jax.ShapeDtypeStruct((count, chans), out_type) for count in counts],
@@ -177,7 +177,7 @@
         ],
         compiler_params=pltpu.CompilerParams(vmem_limit_bytes=VMEM_LIMIT),
         cost_estimate=pl.CostEstimate(
-            flops=2 * sum(counts) * taps * lags * width * chans,
+            flops=20 * sum(counts) * taps * lags * width * chans,
             bytes_accessed=2 * taps * lags * width * chans,
             transcendentals=0,
         ),
@@ -185,27 +185,26 @@
     )(meta, *operands, *after)
 
 
-def sum_call(pieces, frames):
+def sum_call(pieces, splits, after=()):
     count, chans = pieces[0].shape
-    out = jax.ShapeDtypeStruct((count // frames, chans), jnp.bfloat16)
+    size = count // splits
 
     def kernel(*refs):
-        ins, outs = refs[: len(pieces)], refs[len(pieces) :]
-        for p, out_ref in enumerate(outs):
-            size = out_ref.shape[0]
-            total = ins[0][pl.ds(p * size, size)].astype(jnp.float32)
-            for ref in ins[1:]:
-                total = total + ref[pl.ds(p * size, size)].astype(jnp.float32)
+        for p, out_ref in enumerate(refs[len(refs) - splits :]):
+            total = None
+            for ref in refs[: len(pieces)]:
+                rows = ref[p * size : (p + 1) * size].astype(jnp.float32)
+                total = rows if total is None else total + rows
             out_ref[...] = total.astype(out_ref.dtype)
 
     return pl.pallas_call(
         kernel,
-        out_shape=[out] * frames,
-        in_specs=in_vmem(len(pieces)),
-        out_specs=in_vmem(frames),
+        out_shape=[jax.ShapeDtypeStruct((size, chans), jnp.bfloat16)] * splits,
+        in_specs=in_vmem(len(pieces) + len(after)),
+        out_specs=in_vmem(splits),
         compiler_params=pltpu.CompilerParams(vmem_limit_bytes=VMEM_LIMIT),
         name="sum_parts",
-    )(*pieces)
+    )(*pieces, *after)
 
 
 def attend_kernel(frames, share, chunks, *refs):
@@ -270,9 +269,9 @@
         ).astype(jnp.bfloat16)
 
     place = 0
-    for index in range(own_count):
-        ref = tokens[index]
-        rows = ref.shape[0]
+    for p, out in enumerate(outs):
+        mine = tokens[p * chunks : (p + 1) * chunks]
+        rows = sum(ref.shape[0] for ref in mine)
         queries = jnp.dot(
             normed[pl.ds(place, rows)], wq[...], preferred_element_type=jnp.float32
         ).astype(jnp.bfloat16)
@@ -285,17 +284,14 @@
         denominator = jnp.sum(exp_weights.astype(jnp.float32), axis=1, keepdims=True)
         numerator = jnp.dot(exp_weights, values[...], preferred_element_type=jnp.float32)
         attended = (numerator / denominator).astype(jnp.bfloat16)
-        summed = ref[...].astype(jnp.float32) + jnp.dot(
-            attended, wo[...], preferred_element_type=jnp.float32
-        )
-        summed = summed.astype(jnp.bfloat16)
-        out = outs[index // chunks]
+        added = jnp.dot(attended, wo[...], preferred_element_type=jnp.float32)
         rows_here, columns, _ = out.shape
-        if index % chunks == 0:
-            out[1 : rows_here - 1] = summed.reshape(rows_here - 2, columns, chans)
-        else:
-            out[0] = summed[:columns]
-            out[rows_here - 1] = summed[columns:]
+        inner = mine[0].shape[0]
+        first = mine[0][...].astype(jnp.float32) + added[:inner]
+        out[1 : rows_here - 1] = first.astype(jnp.bfloat16).reshape(rows_here - 2, columns, chans)
+        second = (mine[1][...].astype(jnp.float32) + added[inner:]).astype(jnp.bfloat16)
+        out[0] = second[:columns]
+        out[rows_here - 1] = second[columns:]
 
 
 def attend_call(own, others, weights, frames, rows_here, columns):
@@ -322,31 +318,6 @@
     )(*operands)
 
 
-def place_kernel(meta, *refs):
-    parts, out, sems = refs[:-2], refs[-2], refs[-1]
-    frames = len(parts)
-    copies = [
-        pltpu.make_async_copy(ref, out.at[lax.rem(meta[2] + p, frames)], sems.at[p])
-        for p, ref in enumerate(parts)
-    ]
-    for copy in copies:
-        copy.start()
-    for copy in copies:
-        copy.wait()
-
-
-def place_call(meta, parts):
-    frames = len(parts)
-    return pl.pallas_call(
-        place_kernel,
-        out_shape=jax.ShapeDtypeStruct((frames, *parts[0].shape), parts[0].dtype),
-        in_specs=[pl.BlockSpec(memory_space=pltpu.SMEM)] + in_vmem(frames),
-        out_specs=pl.BlockSpec(memory_space=pl.ANY),
-        scratch_shapes=[pltpu.SemaphoreType.DMA((frames,))],
-        name="place_frames",
-    )(meta, *parts)
-
-
 def body(latents, conv_weight, query_weight, key_weight, value_weight, out_weight):
     frames, rows_here, columns, chans = latents.shape
     taps, chans_here, _ = conv_weight.shape
@@ -384,18 +355,21 @@
         conv_call, meta=meta, weights=weights, held=held, before=before, frames=frames
     )
     inner = conv([(s, False) for s in away[:1]], halos=None, out_type=jnp.bfloat16)
-    first, last = halo_call([*held, *before], inner[0])
+    inner += conv(
+        [(s, False) for s in away[1:]], halos=None, out_type=jnp.bfloat16, after=inner[:1]
+    )
+    first, last = halo_call([*held, *before], inner[-1])
     halos = (
         permute(last, lambda t, z: (t, z + 1) if z + 1 < depth else None),
         permute(first, lambda t, z: (t, z - 1) if z else None),
     )
-    inner += conv([(s, False) for s in away[1:]], halos=None, out_type=jnp.bfloat16)
-    rim = conv([(s, True) for s in away], halos=halos, out_type=jnp.bfloat16, after=inner[-1:])
-    mine = conv([(0, False), (0, True)], halos=halos, out_type=jnp.float32, after=rim[-1:])
+    inner_own = conv([(0, False)], halos=None, out_type=jnp.float32, after=(first,))
+    rim = conv([(s, True) for s in away], halos=halos, out_type=jnp.bfloat16, after=inner_own)
+    rim_own = conv([(0, True)], halos=halos, out_type=jnp.float32, after=rim[-1:])
     sums = []
-    for sent, own_part in ((inner, mine[0]), (rim, mine[1])):
+    for sent, own_part in ((inner, inner_own), (rim, rim_own)):
         got = [permute(x, to_part(s)) for s, x in zip(away, sent)]
-        sums.append(sum_call([own_part, *got], frames))
+        sums.append(sum_call([*own_part, *got], frames, after=rim_own))
 
     share = depth // frames
 
@@ -429,7 +403,16 @@
     for p in range(frames):
         pairs = [(b, a) for a, b in everywhere(sizes, lambda t, z: frame_home(t, z, p))]
         back.append(lax.ppermute(done[p], BOTH, pairs))
-    return place_call(meta, back)
+    return jnp.stack(
+        [
+            functools.reduce(
+                lambda rest, p: jnp.where((z_index + p) % frames == f, back[p], rest),
+                range(1, frames),
+                back[0],
+            )
+            for f in range(frames)
+        ]
+    )
 
 
 def solution(mesh):

time: 85.1 us -> 85.5 us (level)
  waiting for transfers between devices: 25.1 us -> 28.2 us
  Pallas kernels: 20.3 us -> 17.7 us
  local copies, waits for them, and re-layouts: 4.05 us -> 2.65 us
  other arithmetic: 0.08 us -> 0.96 us
    ppermute x24, waiting for transfers between devices: 15.7 us -> 17.6 us  [permute(): return lax.ppermute(block, BOTH, everywhere(sizes, target))]
    pallas_call x4 -> x3, Pallas kernels: 2.15 us -> 0.28 us  [the longest x2 0.25 us: sum_call(): pl.pallas_call(kernel, out_shape=[jax.ShapeDtypeStruct((size, chans), jnp...]
    ppermute x24, starting transfers between devices: 29.5 us -> 31.3 us  [permute(): return lax.ppermute(block, BOTH, everywhere(sizes, target))]
    pallas_call x1, Pallas kernels: 5.94 us -> 4.41 us  [attend_call(): pl.pallas_call(functools.partial(attend_kernel, frames, share, chunks), o...]
    unnamed x16 -> x10, local copies, waits for them, and re-layouts: 2.9 us -> 1.5 us
    ppermute x2, waiting for transfers between devices: 9.43 us -> 10.6 us  [body(): back.append(lax.ppermute(done[p], BOTH, pairs))]
    ppermute x2, starting transfers between devices: 5.26 us -> 4.2 us  [body(): back.append(lax.ppermute(done[p], BOTH, pairs))]
    another operation x0 -> x2, other arithmetic: none -> 0.88 us  [body(): jnp.stack([functools.reduce(lambda rest, p: jnp.where((z_index + p) % fra...]
  transfers between devices with their start and end apart: 26 -> 26, of which waited for: 8 -> 10; matrix products, arithmetic and copies ran while one was open for 1% -> 1% of each run, Pallas kernels for 13% -> 13%
where the time goes in v8:
time: 85.5 us; the launch traced here: 85.2 us
  starting transfers between devices  35.5 us (42%)
  waiting for transfers between devices  28.2 us (33%)
  Pallas kernels  17.7 us (21%)
  local copies, waits for them, and re-layouts  2.65 us (3%)
  other arithmetic  0.96 us (1%)
    ppermute x24, starting transfers between devices, permute(): return lax.ppermute(block, BOTH, everywhere(sizes, target))  31.3 us
    ppermute x24, waiting for transfers between devices, permute(): return lax.ppermute(block, BOTH, everywhere(sizes, target))  17.6 us
    pallas_call x5, Pallas kernels, conv_call(): pl.pallas_call(functools.partial(conv_kernel, tuple(jobs), parts, frames)...  12.1 us
    ppermute x2, waiting for transfers between devices, body(): back.append(lax.ppermute(done[p], BOTH, pairs))  10.6 us
    pallas_call x1, Pallas kernels, attend_call(): pl.pallas_call(functools.partial(attend_kernel, frames, share, chunks), o...  4.41 us
    ppermute x2, starting transfers between devices, body(): back.append(lax.ppermute(done[p], BOTH, pairs))  4.2 us
  transfers between devices with their start and end apart: 26, of which 10 were waited for; matrix products, arithmetic and copies ran while one was open for 1% of the time, Pallas kernels for 13%

profile of v8, /device:TPU:1, one launch (start us, length us, event | category | flops | bytes accessed | tf_op | source)
XLA Modules:
  0.0 85.2 jit_solution(15494572912575085432)
XLA Ops:
  0.0 0.1 collective-permute-start
  0.1 1.1 %constant_dynamic-slice_fusion = (bf16[2,4,64,128]{3,2,1,0:T(8,128)(2,1)S(1)}, bf16[2,4,64,128]{3,2,1,0:T(8,128)(2,1)S(1)}, bf16[2,4,64,128]{3,2,1,0:T(8,128)(2,1)S(1)}, bf16[2,4,64,128]{3,2,1,0:T(8,128)(2,1)S(1)}) fusion(bf16[2,4,64,512]{3,2,1,0:T(8,128)(2,1)} %param.6, s32[]{:T(128)S(6)} %select_n.50, s32[]{:T(128)S(6)} %select_n.48, s32[]{:T(128)S(6)} %select_n.47, ...), kind=kLoop, calls=%fused_computation.3 | loop fusion | bytes 1048592 | tf_op jit(solution)/shard_map/dynamic_slice | solution.py:344
  1.2 2.7 %collective-permute-start.2 = (bf16[2,4,64,128]{3,2,1,0:T(8,128)(2,1)S(1)}, bf16[2,4,64,128]{3,2,1,0:T(8,128)(2,1)S(1)}, u32[]{:S(2)}, u32[]{:S(2)}) collective-permute-start(bf16[2,4,64,128]{3,2,1,0:T(8,128)(2,1)S(1)} %get-tuple-element.34), channel_id=1, source_target_pairs={{0,8},{1,9},{2,10},{3,11},{4,12},{5,13},{6,14},{7,15},{8,0},{9,1},... | collective-permute-start | bytes 393224 | tf_op jit(solution)/shard_map/ppermute | solution.py:334
  3.9 1.2 %collective-permute-start.4 = (bf16[2,4,64,128]{3,2,1,0:T(8,128)(2,1)S(1)}, bf16[2,4,64,128]{3,2,1,0:T(8,128)(2,1)S(1)}, u32[]{:S(2)}, u32[]{:S(2)}) collective-permute-start(bf16[2,4,64,128]{3,2,1,0:T(8,128)(2,1)S(1)} %get-tuple-element.36), channel_id=1, source_target_pairs={{0,16},{1,17},{2,18},{3,19},{4,20},{5,21},{6,22},{7,23},{8,24},{9,... | collective-permute-start | bytes 393224 | tf_op jit(solution)/shard_map/ppermute | solution.py:334
  5.2 0.0 collective-permute-start.6
  5.2 0.6 collective-permute-start.1
  5.8 2.0 %collective-permute-done.2.refs_2_.refs_1_ = bf16[2,4,64,128]{3,2,1,0:T(8,128)(2,1)S(1)} collective-permute-done((bf16[2,4,64,128]{3,2,1,0:T(8,128)(2,1)S(1)}, bf16[2,4,64,128]{3,2,1,0:T(8,128)(2,1)S(1)}, u32[]{:S(2)}, u32[]{:S(2)}) %collective-permute-start.2) | collective-permute-done | bytes 131104 | tf_op jit(solution)/shard_map/ppermute | solution.py:334
  7.8 0.7 collective-permute-start.3
  8.5 2.0 %collective-permute-done.4.refs_3_.refs_2_ = bf16[2,4,64,128]{3,2,1,0:T(8,128)(2,1)S(1)} collective-permute-done((bf16[2,4,64,128]{3,2,1,0:T(8,128)(2,1)S(1)}, bf16[2,4,64,128]{3,2,1,0:T(8,128)(2,1)S(1)}, u32[]{:S(2)}, u32[]{:S(2)}) %collective-permute-start.4) | collective-permute-done | bytes 131104 | tf_op jit(solution)/shard_map/ppermute | solution.py:334
  10.5 2.2 %collective-permute-start.5 = (bf16[2,4,64,128]{3,2,1,0:T(8,128)(2,1)S(1)}, bf16[2,4,64,128]{3,2,1,0:T(8,128)(2,1)S(1)}, u32[]{:S(2)}, u32[]{:S(2)}) collective-permute-start(bf16[2,4,64,128]{3,2,1,0:T(8,128)(2,1)S(1)} %collective-permute-done.4.refs_3_.refs_2_), channel_id=1, source_target_pairs={{0,4},{1,5},{2,6},{3,7},{4,0},{5,1},{6,2},{7,3},{8,12},{9,13},{10,... | collective-permute-start | bytes 393224 | tf_op jit(solution)/shard_map/ppermute | solution.py:334
  12.7 0.0 collective-permute-done.6.refs_2_.refs_3_.refs_4_
  12.7 0.0 collective-permute-start.7
  12.7 0.1 pad_add_fusion.refs_0_
  12.7 0.0 collective-permute-done.refs_2_
  12.8 1.5 %copy-done = bf16[27,64,512]{2,1,0:T(8,128)(2,1)S(1)} copy-done((bf16[27,64,512]{2,1,0:T(8,128)(2,1)S(1)}, bf16[27,64,512]{2,1,0:T(8,128)(2,1)}, u32[]{:S(2)}) %copy-start) | copy-done | bytes 1769496
  14.2 0.9 %merge_kernel_slices.1.refs_1_ = bf16[3,9,128,512]{3,2,1,0:T(8,128)(2,1)S(1)} custom-call(s32[3]{0:T(128)S(1)} %pad_add_fusion.refs_0_, bf16[9,3,64,512]{3,2,1,0:T(8,128)(2,1)S(1)} %bitcast.9, bf16[9,3,64,512]{3,2,1,0:T(8,128)(2,1)S(1)} %collective-permute-done.refs_2_), custom_call_target="tpu_custom_call" | custom-call | tf_op jit(solution)/shard_map/merge_kernel_slices/pallas_call | solution.py:58
  15.1 0.0 collective-permute-done.1.refs_3_.refs_4_.refs_5_
  15.1 0.0 collective-permute-done.3.refs_4_.refs_5_.refs_6_
  15.1 0.0 collective-permute-done.5.refs_5_.refs_6_.refs_7_
  15.1 0.0 collective-permute-done.7.refs_6_.refs_7_.refs_8_
  15.1 1.8 %conv_inner.3.refs_8_ = bf16[256,512]{1,0:T(8,128)(2,1)S(1)} custom-call(s32[3]{0:T(128)S(1)} %pad_add_fusion.refs_0_, bf16[3,9,128,512]{3,2,1,0:T(8,128)(2,1)S(1)} %merge_kernel_slices.1.refs_1_, bf16[2,4,64,128]{3,2,1,0:T(8,128)(2,1)S(1)} %collective-permute-done.6.refs_2_.refs_3_.refs_4_, ...), custom_call_target="tpu_custom_call" | custom-call | flops 9059696640 | bytes 3538944 | tf_op jit(solution)/shard_map/conv_inner/pallas_call | solution.py:170
  16.9 1.3 %collective-permute-start.8 = (bf16[256,512]{1,0:T(8,128)(2,1)S(1)}, bf16[256,512]{1,0:T(8,128)(2,1)S(1)}, u32[]{:S(2)}, u32[]{:S(2)}) collective-permute-start(bf16[256,512]{1,0:T(8,128)(2,1)S(1)} %conv_inner.3.refs_8_), channel_id=1, source_target_pairs={{0,24},{1,25},{2,26},{3,27},{4,28},{5,29},{6,30},{7,31},{8,16},{9,... | collective-permute-start | bytes 786440 | tf_op jit(solution)/shard_map/ppermute | solution.py:334
  18.2 2.8 %conv_inner.4 = (bf16[256,512]{1,0:T(8,128)(2,1)S(1)}, bf16[256,512]{1,0:T(8,128)(2,1)S(1)}) custom-call(s32[3]{0:T(128)S(1)} %pad_add_fusion.refs_0_, bf16[3,9,128,512]{3,2,1,0:T(8,128)(2,1)S(1)} %merge_kernel_slices.1.refs_1_, bf16[2,4,64,128]{3,2,1,0:T(8,128)(2,1)S(1)} %collective-permute-done.2.refs_2_.refs_1_, ...), custom_call_target="tpu_custom_call" | custom-call | flops 18119393280 | bytes 3538944 | tf_op jit(solution)/shard_map/conv_inner/pallas_call | solution.py:170
  21.1 1.0 %collective-permute-start.9 = (bf16[256,512]{1,0:T(8,128)(2,1)S(1)}, bf16[256,512]{1,0:T(8,128)(2,1)S(1)}, u32[]{:S(2)}, u32[]{:S(2)}) collective-permute-start(bf16[256,512]{1,0:T(8,128)(2,1)S(1)} %get-tuple-element.20), channel_id=1, source_target_pairs={{0,16},{1,17},{2,18},{3,19},{4,20},{5,21},{6,22},{7,23},{8,24},{9,... | collective-permute-start | bytes 786440 | tf_op jit(solution)/shard_map/ppermute | solution.py:334
  22.0 0.5 collective-permute-start.10
  22.6 3.2 %collective-permute-start.11 = (bf16[8,2,64,128]{3,2,1,0:T(8,128)(2,1)S(1)}, bf16[8,2,64,128]{3,2,1,0:T(8,128)(2,1)S(1)}, u32[]{:S(2)}, u32[]{:S(2)}) collective-permute-start(bf16[8,2,64,128]{3,2,1,0:T(8,128)(2,1)S(1)} %get-tuple-element.21), channel_id=1, source_target_pairs={{0,1},{1,2},{2,3},{4,5},{5,6},{6,7},{8,9},{9,10},{10,11},{12,13},{... | collective-permute-start | bytes 786440 | tf_op jit(solution)/shard_map/ppermute | solution.py:334
  25.8 1.3 %collective-permute-start.12 = (bf16[8,2,64,128]{3,2,1,0:T(8,128)(2,1)S(1)}, bf16[8,2,64,128]{3,2,1,0:T(8,128)(2,1)S(1)}, u32[]{:S(2)}, u32[]{:S(2)}) collective-permute-start(bf16[8,2,64,128]{3,2,1,0:T(8,128)(2,1)S(1)} %get-tuple-element.19.refs_7_), channel_id=1, source_target_pairs={{1,0},{2,1},{3,2},{5,4},{6,5},{7,6},{9,8},{10,9},{11,10},{13,12},{... | collective-permute-start | bytes 786440 | tf_op jit(solution)/shard_map/ppermute | solution.py:334
  27.1 1.8 %conv_inner.5.refs_11_.refs_0_ = f32[256,512]{1,0:T(8,128)S(1)} custom-call(s32[3]{0:T(128)S(1)} %pad_add_fusion.refs_0_, bf16[3,9,128,512]{3,2,1,0:T(8,128)(2,1)S(1)} %merge_kernel_slices.1.refs_1_, bf16[2,4,64,128]{3,2,1,0:T(8,128)(2,1)S(1)} %get-tuple-element.35.refs_0_.refs_2_, ...), custom_call_target="tpu_custom_call" | custom-call | flops 9059696640 | bytes 3538944 | tf_op jit(solution)/shard_map/conv_inner/pallas_call | solution.py:170
  28.9 1.1 %collective-permute-done.11.refs_9_.refs_7_ = bf16[8,2,64,128]{3,2,1,0:T(8,128)(2,1)S(1)} collective-permute-done((bf16[8,2,64,128]{3,2,1,0:T(8,128)(2,1)S(1)}, bf16[8,2,64,128]{3,2,1,0:T(8,128)(2,1)S(1)}, u32[]{:S(2)}, u32[]{:S(2)}) %collective-permute-start.11) | collective-permute-done | bytes 262176 | tf_op jit(solution)/shard_map/ppermute | solution.py:334
  30.0 3.8 %collective-permute-done.12.refs_10_.refs_8_ = bf16[8,2,64,128]{3,2,1,0:T(8,128)(2,1)S(1)} collective-permute-done((bf16[8,2,64,128]{3,2,1,0:T(8,128)(2,1)S(1)}, bf16[8,2,64,128]{3,2,1,0:T(8,128)(2,1)S(1)}, u32[]{:S(2)}, u32[]{:S(2)}) %collective-permute-start.12) | collective-permute-done | bytes 262176 | tf_op jit(solution)/shard_map/ppermute | solution.py:334
  33.9 3.9 %conv_rim.2 = (bf16[256,512]{1,0:T(8,128)(2,1)S(1)}, bf16[256,512]{1,0:T(8,128)(2,1)S(1)}, bf16[256,512]{1,0:T(8,128)(2,1)S(1)}) custom-call(s32[3]{0:T(128)S(1)} %pad_add_fusion.refs_0_, bf16[3,9,128,512]{3,2,1,0:T(8,128)(2,1)S(1)} %merge_kernel_slices.1.refs_1_, bf16[2,4,64,128]{3,2,1,0:T(8,128)(2,1)S(1)} %collective-permute-done.2.refs_2_.refs_1_, ...), custom_call_target="tpu_custom_call" | custom-call | flops 27179089920 | bytes 3538944 | tf_op jit(solution)/shard_map/conv_rim/pallas_call | solution.py:170
  37.8 1.2 %collective-permute-start.14 = (bf16[256,512]{1,0:T(8,128)(2,1)S(1)}, bf16[256,512]{1,0:T(8,128)(2,1)S(1)}, u32[]{:S(2)}, u32[]{:S(2)}) collective-permute-start(bf16[256,512]{1,0:T(8,128)(2,1)S(1)} %get-tuple-element.24), channel_id=1, source_target_pairs={{0,24},{1,25},{2,26},{3,27},{4,28},{5,29},{6,30},{7,31},{8,16},{9,... | collective-permute-start | bytes 786440 | tf_op jit(solution)/shard_map/ppermute | solution.py:334
  39.0 1.4 %collective-permute-start.15 = (bf16[256,512]{1,0:T(8,128)(2,1)S(1)}, bf16[256,512]{1,0:T(8,128)(2,1)S(1)}, u32[]{:S(2)}, u32[]{:S(2)}) collective-permute-start(bf16[256,512]{1,0:T(8,128)(2,1)S(1)} %get-tuple-element.25), channel_id=1, source_target_pairs={{0,16},{1,17},{2,18},{3,19},{4,20},{5,21},{6,22},{7,23},{8,24},{9,... | collective-permute-start | bytes 786440 | tf_op jit(solution)/shard_map/ppermute | solution.py:334
  40.5 0.0 collective-permute-done.8.refs_1_
  40.5 0.0 collective-permute-start.16
  40.5 1.8 %conv_rim.3.refs_4_.refs_0_ = f32[256,512]{1,0:T(8,128)S(1)} custom-call(s32[3]{0:T(128)S(1)} %pad_add_fusion.refs_0_, bf16[3,9,128,512]{3,2,1,0:T(8,128)(2,1)S(1)} %merge_kernel_slices.1.refs_1_, bf16[2,4,64,128]{3,2,1,0:T(8,128)(2,1)S(1)} %get-tuple-element.35.refs_0_.refs_2_, bf16[2,4,64,128]{3,2,1,0:T(8,128)(2,1)S(1)} %collective-permute-done.1.refs_3_.refs_4_.refs_5_, ...), custom_call_target="tpu_custom_call" | custom-call | flops 9059696640 | bytes 3538944 | tf_op jit(solution)/shard_map/conv_rim/pallas_call | solution.py:170
  42.3 0.0 copy-start.1
  42.3 0.0 copy-start.2
  42.3 0.0 copy-start.3
  42.3 0.0 copy-start.4
  42.4 0.0 collective-permute-done.9.refs_2_
  42.4 0.0 collective-permute-done.10.refs_3_
  42.4 0.1 sum_parts.2
  42.5 7.6 %collective-permute-start.13 = (bf16[128,512]{1,0:T(8,128)(2,1)S(1)}, bf16[128,512]{1,0:T(8,128)(2,1)S(1)}, u32[]{:S(2)}, u32[]{:S(2)}) collective-permute-start(bf16[128,512]{1,0:T(8,128)(2,1)S(1)} %get-tuple-element.23), channel_id=1, source_target_pairs={{0,0},{1,1},{2,4},{3,5},{4,2},{5,3},{6,6},{7,7},{8,8},{9,9},{10,12... | collective-permute-start | bytes 393224 | tf_op jit(solution)/shard_map/ppermute | solution.py:334
  50.1 0.1 collective-permute-start.18
  50.2 0.0 collective-permute-done.14.refs_1_
  50.2 1.9 %collective-permute-done.15.refs_2_ = bf16[256,512]{1,0:T(8,128)(2,1)S(1)} collective-permute-done((bf16[256,512]{1,0:T(8,128)(2,1)S(1)}, bf16[256,512]{1,0:T(8,128)(2,1)S(1)}, u32[]{:S(2)}, u32[]{:S(2)}) %collective-permute-start.15) | collective-permute-done | bytes 262176 | tf_op jit(solution)/shard_map/ppermute | solution.py:334
  52.1 0.0 collective-permute-done.16.refs_3_
  52.1 0.1 sum_parts.3
  52.2 5.2 %collective-permute-start.17 = (bf16[128,512]{1,0:T(8,128)(2,1)S(1)}, bf16[128,512]{1,0:T(8,128)(2,1)S(1)}, u32[]{:S(2)}, u32[]{:S(2)}) collective-permute-start(bf16[128,512]{1,0:T(8,128)(2,1)S(1)} %get-tuple-element.26), channel_id=1, source_target_pairs={{0,0},{1,1},{2,4},{3,5},{4,2},{5,3},{6,6},{7,7},{8,8},{9,9},{10,12... | collective-permute-start | bytes 393224 | tf_op jit(solution)/shard_map/ppermute | solution.py:334
  57.4 0.4 collective-permute-start.19
  57.8 0.0 collective-permute-done.18.refs_2_
  57.9 0.5 collective-permute-start.22
  58.4 3.1 %collective-permute-done.17.refs_1_ = bf16[128,512]{1,0:T(8,128)(2,1)S(1)} collective-permute-done((bf16[128,512]{1,0:T(8,128)(2,1)S(1)}, bf16[128,512]{1,0:T(8,128)(2,1)S(1)}, u32[]{:S(2)}, u32[]{:S(2)}) %collective-permute-start.17) | collective-permute-done | bytes 131104 | tf_op jit(solution)/shard_map/ppermute | solution.py:334
  61.4 2.3 %collective-permute-done.19.refs_3_ = bf16[128,512]{1,0:T(8,128)(2,1)S(1)} collective-permute-done((bf16[128,512]{1,0:T(8,128)(2,1)S(1)}, bf16[128,512]{1,0:T(8,128)(2,1)S(1)}, u32[]{:S(2)}, u32[]{:S(2)}) %collective-permute-start.19) | collective-permute-done | bytes 131104 | tf_op jit(solution)/shard_map/ppermute | solution.py:334
  63.8 0.0 collective-permute-start.23
  63.8 0.0 collective-permute-done.20.refs_4_
  63.8 1.3 %collective-permute-done.23.refs_7_ = bf16[128,512]{1,0:T(8,128)(2,1)S(1)} collective-permute-done((bf16[128,512]{1,0:T(8,128)(2,1)S(1)}, bf16[128,512]{1,0:T(8,128)(2,1)S(1)}, u32[]{:S(2)}, u32[]{:S(2)}) %collective-permute-start.23) | collective-permute-done | bytes 131104 | tf_op jit(solution)/shard_map/ppermute | solution.py:334
  65.1 4.4 %attend.1 = (bf16[4,64,512]{2,1,0:T(8,128)(2,1)S(1)}, bf16[4,64,512]{2,1,0:T(8,128)(2,1)S(1)}) custom-call(bf16[128,512]{1,0:T(8,128)(2,1)S(1)} %collective-permute-done.13.refs_0_, bf16[128,512]{1,0:T(8,128)(2,1)S(1)} %collective-permute-done.17.refs_1_, bf16[128,512]{1,0:T(8,128)(2,1)S(1)} %collective-permute-done.18.refs_2_, ...), custom_call_target="tpu_custom_call" | custom-call | flops 2684354560 | bytes 3145728 | tf_op jit(solution)/shard_map/attend/pallas_call | solution.py:305
  69.5 1.4 %collective-permute-start.24 = (bf16[4,64,512]{2,1,0:T(8,128)(2,1)S(1)}, bf16[4,64,512]{2,1,0:T(8,128)(2,1)S(1)}, u32[]{:S(2)}, u32[]{:S(2)}) collective-permute-start(bf16[4,64,512]{2,1,0:T(8,128)(2,1)S(1)} %get-tuple-element.29), channel_id=1, source_target_pairs={{1,0},{0,1},{5,2},{4,3},{3,4},{2,5},{7,6},{6,7},{9,8},{8,9},{13,10... | collective-permute-start | bytes 786440 | tf_op jit(solution)/shard_map/ppermute | solution.py:405
  70.9 2.8 %collective-permute-start.25 = (bf16[4,64,512]{2,1,0:T(8,128)(2,1)S(1)}, bf16[4,64,512]{2,1,0:T(8,128)(2,1)S(1)}, u32[]{:S(2)}, u32[]{:S(2)}) collective-permute-start(bf16[4,64,512]{2,1,0:T(8,128)(2,1)S(1)} %get-tuple-element.30), channel_id=1, source_target_pairs={{0,0},{1,1},{4,2},{5,3},{2,4},{3,5},{6,6},{7,7},{8,8},{9,9},{12,10... | collective-permute-start | bytes 786440 | tf_op jit(solution)/shard_map/ppermute | solution.py:405
  73.8 4.7 %collective-permute-done.24 = bf16[4,64,512]{2,1,0:T(8,128)(2,1)S(1)} collective-permute-done((bf16[4,64,512]{2,1,0:T(8,128)(2,1)S(1)}, bf16[4,64,512]{2,1,0:T(8,128)(2,1)S(1)}, u32[]{:S(2)}, u32[]{:S(2)}) %collective-permute-start.24) | collective-permute-done | bytes 262176 | tf_op jit(solution)/shard_map/ppermute | solution.py:405
  78.4 5.9 %collective-permute-done.25 = bf16[4,64,512]{2,1,0:T(8,128)(2,1)S(1)} collective-permute-done((bf16[4,64,512]{2,1,0:T(8,128)(2,1)S(1)}, bf16[4,64,512]{2,1,0:T(8,128)(2,1)S(1)}, u32[]{:S(2)}, u32[]{:S(2)}) %collective-permute-start.25) | collective-permute-done | bytes 262176 | tf_op jit(solution)/shard_map/ppermute | solution.py:405
  84.4 0.8 pad_maximum_fusion
  (12 shorter events, 0.1 us)
Async XLA Ops:
  0.0 12.7 %collective-permute-start = (bf16[9,3,64,512]{3,2,1,0:T(8,128)(2,1)}, bf16[9,3,64,512]{3,2,1,0:T(8,128)(2,1)S(1)}, u32[]{:S(2)}, u32[]{:S(2)}) collective-permute-start(bf16[9,3,64,512]{3,2,1,0:T(8,128)(2,1)} %bitcast.8), channel_id=1, source_target_pairs={{0,4},{1,5},{2,6},{3,7},{4,0},{5,1},{6,2},{7,3},{8,12},{9,13},{10,... | collective-permute-start | bytes 5308424 | tf_op jit(solution)/shard_map/ppermute | solution.py:334
  1.2 6.6 %collective-permute-start.2 = (bf16[2,4,64,128]{3,2,1,0:T(8,128)(2,1)S(1)}, bf16[2,4,64,128]{3,2,1,0:T(8,128)(2,1)S(1)}, u32[]{:S(2)}, u32[]{:S(2)}) collective-permute-start(bf16[2,4,64,128]{3,2,1,0:T(8,128)(2,1)S(1)} %get-tuple-element.34), channel_id=1, source_target_pairs={{0,8},{1,9},{2,10},{3,11},{4,12},{5,13},{6,14},{7,15},{8,0},{9,1},... | collective-permute-start | bytes 393224 | tf_op jit(solution)/shard_map/ppermute | solution.py:334
  3.9 6.5 %collective-permute-start.4 = (bf16[2,4,64,128]{3,2,1,0:T(8,128)(2,1)S(1)}, bf16[2,4,64,128]{3,2,1,0:T(8,128)(2,1)S(1)}, u32[]{:S(2)}, u32[]{:S(2)}) collective-permute-start(bf16[2,4,64,128]{3,2,1,0:T(8,128)(2,1)S(1)} %get-tuple-element.36), channel_id=1, source_target_pairs={{0,16},{1,17},{2,18},{3,19},{4,20},{5,21},{6,22},{7,23},{8,24},{9,... | collective-permute-start | bytes 393224 | tf_op jit(solution)/shard_map/ppermute | solution.py:334
  5.2 7.5 %collective-permute-start.6 = (bf16[2,4,64,128]{3,2,1,0:T(8,128)(2,1)S(1)}, bf16[2,4,64,128]{3,2,1,0:T(8,128)(2,1)S(1)}, u32[]{:S(2)}, u32[]{:S(2)}) collective-permute-start(bf16[2,4,64,128]{3,2,1,0:T(8,128)(2,1)S(1)} %get-tuple-element.33), channel_id=1, source_target_pairs={{0,24},{1,25},{2,26},{3,27},{4,28},{5,29},{6,30},{7,31},{8,16},{9,... | collective-permute-start | bytes 393224 | tf_op jit(solution)/shard_map/ppermute | solution.py:334
  5.2 9.9 %collective-permute-start.1 = (bf16[2,4,64,128]{3,2,1,0:T(8,128)(2,1)S(1)}, bf16[2,4,64,128]{3,2,1,0:T(8,128)(2,1)S(1)}, u32[]{:S(2)}, u32[]{:S(2)}) collective-permute-start(bf16[2,4,64,128]{3,2,1,0:T(8,128)(2,1)S(1)} %get-tuple-element.35.refs_0_.refs_2_), channel_id=1, source_target_pairs={{0,4},{1,5},{2,6},{3,7},{4,0},{5,1},{6,2},{7,3},{8,12},{9,13},{10,... | collective-permute-start | bytes 393224 | tf_op jit(solution)/shard_map/ppermute | solution.py:334
  7.8 7.3 %collective-permute-start.3 = (bf16[2,4,64,128]{3,2,1,0:T(8,128)(2,1)S(1)}, bf16[2,4,64,128]{3,2,1,0:T(8,128)(2,1)S(1)}, u32[]{:S(2)}, u32[]{:S(2)}) collective-permute-start(bf16[2,4,64,128]{3,2,1,0:T(8,128)(2,1)S(1)} %collective-permute-done.2.refs_2_.refs_1_), channel_id=1, source_target_pairs={{0,4},{1,5},{2,6},{3,7},{4,0},{5,1},{6,2},{7,3},{8,12},{9,13},{10,... | collective-permute-start | bytes 393224 | tf_op jit(solution)/shard_map/ppermute | solution.py:334
  10.5 4.7 %collective-permute-start.5 = (bf16[2,4,64,128]{3,2,1,0:T(8,128)(2,1)S(1)}, bf16[2,4,64,128]{3,2,1,0:T(8,128)(2,1)S(1)}, u32[]{:S(2)}, u32[]{:S(2)}) collective-permute-start(bf16[2,4,64,128]{3,2,1,0:T(8,128)(2,1)S(1)} %collective-permute-done.4.refs_3_.refs_2_), channel_id=1, source_target_pairs={{0,4},{1,5},{2,6},{3,7},{4,0},{5,1},{6,2},{7,3},{8,12},{9,13},{10,... | collective-permute-start | bytes 393224 | tf_op jit(solution)/shard_map/ppermute | solution.py:334
  12.7 2.5 %collective-permute-start.7 = (bf16[2,4,64,128]{3,2,1,0:T(8,128)(2,1)S(1)}, bf16[2,4,64,128]{3,2,1,0:T(8,128)(2,1)S(1)}, u32[]{:S(2)}, u32[]{:S(2)}) collective-permute-start(bf16[2,4,64,128]{3,2,1,0:T(8,128)(2,1)S(1)} %collective-permute-done.6.refs_2_.refs_3_.refs_4_), channel_id=1, source_target_pairs={{0,4},{1,5},{2,6},{3,7},{4,0},{5,1},{6,2},{7,3},{8,12},{9,13},{10,... | collective-permute-start | bytes 393224 | tf_op jit(solution)/shard_map/ppermute | solution.py:334
  12.7 1.5 %copy-start = (bf16[27,64,512]{2,1,0:T(8,128)(2,1)S(1)}, bf16[27,64,512]{2,1,0:T(8,128)(2,1)}, u32[]{:S(2)}) copy-start(bf16[27,64,512]{2,1,0:T(8,128)(2,1)} %param.7) | copy-start | bytes 5308420
  16.9 23.5 %collective-permute-start.8 = (bf16[256,512]{1,0:T(8,128)(2,1)S(1)}, bf16[256,512]{1,0:T(8,128)(2,1)S(1)}, u32[]{:S(2)}, u32[]{:S(2)}) collective-permute-start(bf16[256,512]{1,0:T(8,128)(2,1)S(1)} %conv_inner.3.refs_8_), channel_id=1, source_target_pairs={{0,24},{1,25},{2,26},{3,27},{4,28},{5,29},{6,30},{7,31},{8,16},{9,... | collective-permute-start | bytes 786440 | tf_op jit(solution)/shard_map/ppermute | solution.py:334
  21.1 21.3 %collective-permute-start.9 = (bf16[256,512]{1,0:T(8,128)(2,1)S(1)}, bf16[256,512]{1,0:T(8,128)(2,1)S(1)}, u32[]{:S(2)}, u32[]{:S(2)}) collective-permute-start(bf16[256,512]{1,0:T(8,128)(2,1)S(1)} %get-tuple-element.20), channel_id=1, source_target_pairs={{0,16},{1,17},{2,18},{3,19},{4,20},{5,21},{6,22},{7,23},{8,24},{9,... | collective-permute-start | bytes 786440 | tf_op jit(solution)/shard_map/ppermute | solution.py:334
  22.0 20.3 %collective-permute-start.10 = (bf16[256,512]{1,0:T(8,128)(2,1)S(1)}, bf16[256,512]{1,0:T(8,128)(2,1)S(1)}, u32[]{:S(2)}, u32[]{:S(2)}) collective-permute-start(bf16[256,512]{1,0:T(8,128)(2,1)S(1)} %get-tuple-element.18.refs_8_), channel_id=1, source_target_pairs={{0,8},{1,9},{2,10},{3,11},{4,12},{5,13},{6,14},{7,15},{8,0},{9,1},... | collective-permute-start | bytes 786440 | tf_op jit(solution)/shard_map/ppermute | solution.py:334
  22.6 7.4 %collective-permute-start.11 = (bf16[8,2,64,128]{3,2,1,0:T(8,128)(2,1)S(1)}, bf16[8,2,64,128]{3,2,1,0:T(8,128)(2,1)S(1)}, u32[]{:S(2)}, u32[]{:S(2)}) collective-permute-start(bf16[8,2,64,128]{3,2,1,0:T(8,128)(2,1)S(1)} %get-tuple-element.21), channel_id=1, source_target_pairs={{0,1},{1,2},{2,3},{4,5},{5,6},{6,7},{8,9},{9,10},{10,11},{12,13},{... | collective-permute-start | bytes 786440 | tf_op jit(solution)/shard_map/ppermute | solution.py:334
  25.8 8.1 %collective-permute-start.12 = (bf16[8,2,64,128]{3,2,1,0:T(8,128)(2,1)S(1)}, bf16[8,2,64,128]{3,2,1,0:T(8,128)(2,1)S(1)}, u32[]{:S(2)}, u32[]{:S(2)}) collective-permute-start(bf16[8,2,64,128]{3,2,1,0:T(8,128)(2,1)S(1)} %get-tuple-element.19.refs_7_), channel_id=1, source_target_pairs={{1,0},{2,1},{3,2},{5,4},{6,5},{7,6},{9,8},{10,9},{11,10},{13,12},{... | collective-permute-start | bytes 786440 | tf_op jit(solution)/shard_map/ppermute | solution.py:334
  37.8 12.4 %collective-permute-start.14 = (bf16[256,512]{1,0:T(8,128)(2,1)S(1)}, bf16[256,512]{1,0:T(8,128)(2,1)S(1)}, u32[]{:S(2)}, u32[]{:S(2)}) collective-permute-start(bf16[256,512]{1,0:T(8,128)(2,1)S(1)} %get-tuple-element.24), channel_id=1, source_target_pairs={{0,24},{1,25},{2,26},{3,27},{4,28},{5,29},{6,30},{7,31},{8,16},{9,... | collective-permute-start | bytes 786440 | tf_op jit(solution)/shard_map/ppermute | solution.py:334
  39.0 13.1 %collective-permute-start.15 = (bf16[256,512]{1,0:T(8,128)(2,1)S(1)}, bf16[256,512]{1,0:T(8,128)(2,1)S(1)}, u32[]{:S(2)}, u32[]{:S(2)}) collective-permute-start(bf16[256,512]{1,0:T(8,128)(2,1)S(1)} %get-tuple-element.25), channel_id=1, source_target_pairs={{0,16},{1,17},{2,18},{3,19},{4,20},{5,21},{6,22},{7,23},{8,24},{9,... | collective-permute-start | bytes 786440 | tf_op jit(solution)/shard_map/ppermute | solution.py:334
  40.5 11.6 %collective-permute-start.16 = (bf16[256,512]{1,0:T(8,128)(2,1)S(1)}, bf16[256,512]{1,0:T(8,128)(2,1)S(1)}, u32[]{:S(2)}, u32[]{:S(2)}) collective-permute-start(bf16[256,512]{1,0:T(8,128)(2,1)S(1)} %get-tuple-element.22.refs_9_), channel_id=1, source_target_pairs={{0,8},{1,9},{2,10},{3,11},{4,12},{5,13},{6,14},{7,15},{8,0},{9,1},... | collective-permute-start | bytes 786440 | tf_op jit(solution)/shard_map/ppermute | solution.py:334
  42.3 22.8 %copy-start.1 = (bf16[512,512]{1,0:T(8,128)(2,1)S(1)}, bf16[512,512]{1,0:T(8,128)(2,1)}, u32[]{:S(2)}) copy-start(bf16[512,512]{1,0:T(8,128)(2,1)} %refs_8_.1) | copy-start | bytes 1572868
  42.3 22.8 %copy-start.2 = (bf16[512,512]{1,0:T(8,128)(2,1)S(1)}, bf16[512,512]{1,0:T(8,128)(2,1)}, u32[]{:S(2)}) copy-start(bf16[512,512]{1,0:T(8,128)(2,1)} %refs_9_.1) | copy-start | bytes 1572868
  42.3 22.8 %copy-start.3 = (bf16[512,512]{1,0:T(8,128)(2,1)S(1)}, bf16[512,512]{1,0:T(8,128)(2,1)}, u32[]{:S(2)}) copy-start(bf16[512,512]{1,0:T(8,128)(2,1)} %refs_10_.1) | copy-start | bytes 1572868
  42.3 22.8 %copy-start.4 = (bf16[512,512]{1,0:T(8,128)(2,1)S(1)}, bf16[512,512]{1,0:T(8,128)(2,1)}, u32[]{:S(2)}) copy-start(bf16[512,512]{1,0:T(8,128)(2,1)} %refs_11_.1) | copy-start | bytes 1572868
  42.5 15.3 %collective-permute-start.13 = (bf16[128,512]{1,0:T(8,128)(2,1)S(1)}, bf16[128,512]{1,0:T(8,128)(2,1)S(1)}, u32[]{:S(2)}, u32[]{:S(2)}) collective-permute-start(bf16[128,512]{1,0:T(8,128)(2,1)S(1)} %get-tuple-element.23), channel_id=1, source_target_pairs={{0,0},{1,1},{2,4},{3,5},{4,2},{5,3},{6,6},{7,7},{8,8},{9,9},{10,12... | collective-permute-start | bytes 393224 | tf_op jit(solution)/shard_map/ppermute | solution.py:334
  50.1 7.7 %collective-permute-start.18 = (bf16[128,512]{1,0:T(8,128)(2,1)S(1)}, bf16[128,512]{1,0:T(8,128)(2,1)S(1)}, u32[]{:S(2)}, u32[]{:S(2)}) collective-permute-start(bf16[128,512]{1,0:T(8,128)(2,1)S(1)} %get-tuple-element.27), channel_id=1, source_target_pairs={{0,1},{1,0},{2,5},{3,4},{4,3},{5,2},{6,7},{7,6},{8,9},{9,8},{10,13... | collective-permute-start | bytes 393224 | tf_op jit(solution)/shard_map/ppermute | solution.py:334
  52.2 9.2 %collective-permute-start.17 = (bf16[128,512]{1,0:T(8,128)(2,1)S(1)}, bf16[128,512]{1,0:T(8,128)(2,1)S(1)}, u32[]{:S(2)}, u32[]{:S(2)}) collective-permute-start(bf16[128,512]{1,0:T(8,128)(2,1)S(1)} %get-tuple-element.26), channel_id=1, source_target_pairs={{0,0},{1,1},{2,4},{3,5},{4,2},{5,3},{6,6},{7,7},{8,8},{9,9},{10,12... | collective-permute-start | bytes 393224 | tf_op jit(solution)/shard_map/ppermute | solution.py:334
  57.4 6.4 %collective-permute-start.19 = (bf16[128,512]{1,0:T(8,128)(2,1)S(1)}, bf16[128,512]{1,0:T(8,128)(2,1)S(1)}, u32[]{:S(2)}, u32[]{:S(2)}) collective-permute-start(bf16[128,512]{1,0:T(8,128)(2,1)S(1)} %get-tuple-element.28), channel_id=1, source_target_pairs={{0,1},{1,0},{2,5},{3,4},{4,3},{5,2},{6,7},{7,6},{8,9},{9,8},{10,13... | collective-permute-start | bytes 393224 | tf_op jit(solution)/shard_map/ppermute | solution.py:334
  57.8 5.9 %collective-permute-start.20 = (bf16[128,512]{1,0:T(8,128)(2,1)S(1)}, bf16[128,512]{1,0:T(8,128)(2,1)S(1)}, u32[]{:S(2)}, u32[]{:S(2)}) collective-permute-start(bf16[128,512]{1,0:T(8,128)(2,1)S(1)} %collective-permute-done.13.refs_0_), channel_id=1, source_target_pairs={{0,4},{1,5},{2,6},{3,7},{4,0},{5,1},{6,2},{7,3},{8,12},{9,13},{10,... | collective-permute-start | bytes 393224 | tf_op jit(solution)/shard_map/ppermute | solution.py:334
  57.9 5.9 %collective-permute-start.22 = (bf16[128,512]{1,0:T(8,128)(2,1)S(1)}, bf16[128,512]{1,0:T(8,128)(2,1)S(1)}, u32[]{:S(2)}, u32[]{:S(2)}) collective-permute-start(bf16[128,512]{1,0:T(8,128)(2,1)S(1)} %collective-permute-done.18.refs_2_), channel_id=1, source_target_pairs={{0,4},{1,5},{2,6},{3,7},{4,0},{5,1},{6,2},{7,3},{8,12},{9,13},{10,... | collective-permute-start | bytes 393224 | tf_op jit(solution)/shard_map/ppermute | solution.py:334
  61.4 2.3 %collective-permute-start.21 = (bf16[128,512]{1,0:T(8,128)(2,1)S(1)}, bf16[128,512]{1,0:T(8,128)(2,1)S(1)}, u32[]{:S(2)}, u32[]{:S(2)}) collective-permute-start(bf16[128,512]{1,0:T(8,128)(2,1)S(1)} %collective-permute-done.17.refs_1_), channel_id=1, source_target_pairs={{0,4},{1,5},{2,6},{3,7},{4,0},{5,1},{6,2},{7,3},{8,12},{9,13},{10,... | collective-permute-start | bytes 393224 | tf_op jit(solution)/shard_map/ppermute | solution.py:334
  63.8 1.3 %collective-permute-start.23 = (bf16[128,512]{1,0:T(8,128)(2,1)S(1)}, bf16[128,512]{1,0:T(8,128)(2,1)S(1)}, u32[]{:S(2)}, u32[]{:S(2)}) collective-permute-start(bf16[128,512]{1,0:T(8,128)(2,1)S(1)} %collective-permute-done.19.refs_3_), channel_id=1, source_target_pairs={{0,4},{1,5},{2,6},{3,7},{4,0},{5,1},{6,2},{7,3},{8,12},{9,13},{10,... | collective-permute-start | bytes 393224 | tf_op jit(solution)/shard_map/ppermute | solution.py:334
  69.5 8.9 %collective-permute-start.24 = (bf16[4,64,512]{2,1,0:T(8,128)(2,1)S(1)}, bf16[4,64,512]{2,1,0:T(8,128)(2,1)S(1)}, u32[]{:S(2)}, u32[]{:S(2)}) collective-permute-start(bf16[4,64,512]{2,1,0:T(8,128)(2,1)S(1)} %get-tuple-element.29), channel_id=1, source_target_pairs={{1,0},{0,1},{5,2},{4,3},{3,4},{2,5},{7,6},{6,7},{9,8},{8,9},{13,10... | collective-permute-start | bytes 786440 | tf_op jit(solution)/shard_map/ppermute | solution.py:405
  70.9 13.4 %collective-permute-start.25 = (bf16[4,64,512]{2,1,0:T(8,128)(2,1)S(1)}, bf16[4,64,512]{2,1,0:T(8,128)(2,1)S(1)}, u32[]{:S(2)}, u32[]{:S(2)}) collective-permute-start(bf16[4,64,512]{2,1,0:T(8,128)(2,1)S(1)} %get-tuple-element.30), channel_id=1, source_target_pairs={{0,0},{1,1},{4,2},{5,3},{2,4},{3,5},{6,6},{7,7},{8,8},{9,9},{12,10... | collective-permute-start | bytes 786440 | tf_op jit(solution)/shard_map/ppermute | solution.py:405

commit v9 on v8

--- a/solution.py
+++ b/solution.py
@@ -67,57 +67,29 @@
     )(meta, *slices)
 
 
-def halo_call(pieces, after):
-    frames, rows_here, columns, width = pieces[0].shape
-    out = jax.ShapeDtypeStruct((len(pieces), frames, columns, width), jnp.bfloat16)
-
-    def kernel(*refs):
-        first, last = refs[-2:]
-        for i in range(len(pieces)):
-            first[i] = refs[i][:, 0]
-            last[i] = refs[i][:, rows_here - 1]
-
-    return pl.pallas_call(
-        kernel,
-        out_shape=[out] * 2,
-        in_specs=in_vmem(len(pieces) + 1),
-        out_specs=in_vmem(2),
-        compiler_params=pltpu.CompilerParams(vmem_limit_bytes=VMEM_LIMIT),
-        name="halo_rows",
-    )(*pieces, after)
-
-
-def conv_kernel(jobs, parts, frames, *refs):
-    meta, weights, refs = refs[0], refs[1], refs[2:]
+def conv_kernel(jobs, any_rim, frames, *refs):
+    meta, weights, held, before, refs = refs[0], refs[1], refs[2], refs[3], refs[4:]
     dests = sorted({s for s, _ in jobs})
-    any_rim = any(rim for _, rim in jobs)
-    held, refs = refs[: len(dests)], refs[len(dests) :]
-    before, refs = refs[:parts], refs[parts:]
     if any_rim:
-        (above, below), refs = refs[:2], refs[2:]
+        (rims, rims_before), refs = refs[:2], refs[2:]
     outs, raw = refs[-1 - len(jobs) : -1], refs[-1]
     part, member, z = meta[0], meta[1], meta[2]
     lags, _, width, chans = weights.shape
-    _, rows_here, columns, _ = held[0].shape
+    _, _, rows_here, columns, _ = held.shape
 
     for n, s in enumerate(dests):
         to = lax.bitwise_xor(part, s)
-        wraps = member == 0
-        place = jnp.where(wraps, lax.bitwise_xor(part, jnp.maximum(to - 1, 0)), s)
-        valid = jnp.logical_or(jnp.logical_not(wraps), to > 0)
-        raw[n, frames:, 1 : 1 + rows_here] = held[n][...]
+        first = member == 0
+        want = jnp.where(first, jnp.maximum(to - 1, 0), to)
+        raw[n, frames:, 1 : 1 + rows_here] = held[to]
+        raw[n, :frames, 1 : 1 + rows_here] = before[want]
         if any_rim:
-            raw[n, frames:, 0] = above[s]
-            raw[n, frames:, 1 + rows_here] = below[s]
-            raw[n, :frames, 0] = above[parts + place]
-            raw[n, :frames, 1 + rows_here] = below[parts + place]
-        for i in range(parts):
-
-            @pl.when(place == i)
-            def _():
-                raw[n, :frames, 1 : 1 + rows_here] = before[i][...]
-
-        @pl.when(jnp.logical_not(valid))
+            raw[n, frames:, 0] = rims[to, 0]
+            raw[n, frames:, 1 + rows_here] = rims[to, 1]
+            raw[n, :frames, 0] = rims_before[want, 0]
+            raw[n, :frames, 1 + rows_here] = rims_before[want, 1]
+
+        @pl.when(jnp.logical_and(first, to == 0))
         def _():
             raw[n, :frames] = jnp.zeros_like(raw[n, :frames])
 
@@ -157,18 +129,17 @@
         place += out.shape[0]
 
 
-def conv_call(jobs, meta, weights, held, before, halos, frames, out_type, after=()):
-    parts = len(held)
+def conv_call(jobs, meta, weights, held, before, rims, frames, out_type, after=()):
     dests = sorted({s for s, _ in jobs})
-    _, rows_here, columns, width = held[0].shape
+    _, _, rows_here, columns, width = held.shape
     lags, taps, _, chans = weights.shape
-    any_rim = any(rim for _, rim in jobs)
+    any_rim = rims is not None
     counts = [frames * (2 if rim else rows_here - 2) * columns for _, rim in jobs]
-    operands = [weights, *[held[s] for s in dests], *before, *(halos if any_rim else ())]
+    operands = [weights, held, before, *(rims if any_rim else ())]
     specs = [pl.BlockSpec(memory_space=pltpu.SMEM)] + in_vmem(len(operands))
     specs += in_vmem(len(after))
     return pl.pallas_call(
-        functools.partial(conv_kernel, tuple(jobs), parts, frames),
+        functools.partial(conv_kernel, tuple(jobs), any_rim, frames),
         out_shape=[jax.ShapeDtypeStruct((count, chans), out_type) for count in counts],
         in_specs=specs,
         out_specs=in_vmem(len(jobs)),
@@ -339,12 +310,18 @@
     def to_member(step):
         return lambda t, z: (t // group * group + (t + step) % group, z)
 
-    held, before = [None] * parts, [None] * parts
-    for s in reversed(range(parts)):
-        piece = lax.dynamic_slice_in_dim(latents, (part ^ s) * width, width, axis=3)
-        held[s] = permute(piece, to_part(s)) if s else piece
-    for s in range(parts):
-        before[s] = permute(held[s], to_member(1))
+    def across(block):
+        groups = [[n * group + m for n in range(parts)] for m in range(group)]
+        return lax.all_to_all(block, "tm", 0, 0, axis_index_groups=groups, tiled=True)
+
+    def by_part(x):
+        return jnp.moveaxis(x.reshape(*x.shape[:-1], parts, width), -2, 0)
+
+    above = permute(latents[:, -1], lambda t, z: (t, z + 1) if z + 1 < depth else None)
+    below = permute(latents[:, 0], lambda t, z: (t, z - 1) if z else None)
+
+    held = across(by_part(latents))
+    before = permute(held, to_member(1))
 
     split = conv_weight.reshape(taps // 3, 3, chans_here, chans)
     slices = [split] + [permute(split, to_member(step)) for step in range(1, group)]
@@ -354,18 +331,17 @@
     conv = functools.partial(
         conv_call, meta=meta, weights=weights, held=held, before=before, frames=frames
     )
-    inner = conv([(s, False) for s in away[:1]], halos=None, out_type=jnp.bfloat16)
+    inner = conv([(s, False) for s in away[:1]], rims=None, out_type=jnp.bfloat16)
     inner += conv(
-        [(s, False) for s in away[1:]], halos=None, out_type=jnp.bfloat16, after=inner[:1]
-    )
-    first, last = halo_call([*held, *before], inner[-1])
-    halos = (
-        permute(last, lambda t, z: (t, z + 1) if z + 1 < depth else None),
-        permute(first, lambda t, z: (t, z - 1) if z else None),
-    )
-    inner_own = conv([(0, False)], halos=None, out_type=jnp.float32, after=(first,))
-    rim = conv([(s, True) for s in away], halos=halos, out_type=jnp.bfloat16, after=inner_own)
-    rim_own = conv([(0, True)], halos=halos, out_type=jnp.float32, after=rim[-1:])
+        [(s, False) for s in away[1:]], rims=None, out_type=jnp.bfloat16, after=inner[:1]
+    )
+    edges = by_part(jnp.stack([above, below]))
+    edges, _ = lax.optimization_barrier((edges, inner[-1]))
+    edges = across(edges)
+    rims = (edges, permute(edges, to_member(1)))
+    inner_own = conv([(0, False)], rims=None, out_type=jnp.float32, after=inner[-1:])
+    rim = conv([(s, True) for s in away], rims=rims, out_type=jnp.bfloat16, after=inner_own)
+    rim_own = conv([(0, True)], rims=rims, out_type=jnp.float32, after=rim[-1:])
     sums = []
     for sent, own_part in ((inner, inner_own), (rim, rim_own)):
         got = [permute(x, to_part(s)) for s, x in zip(away, sent)]

time: 85.5 us -> 109 us (1.27)
  blocking collectives: 0 us -> 12.7 us
  waiting for transfers between devices: 28.2 us -> 22 us
  starting transfers between devices: 35.5 us -> 41.4 us
  local copies, waits for them, and re-layouts: 2.65 us -> 7.91 us
  Pallas kernels: 17.7 us -> 22.2 us
    all_to_all x0 -> x1, blocking collectives: none -> 12.7 us  [across(): lax.all_to_all(block, 'tm', 0, 0, axis_index_groups=groups, tiled=True)]
    ppermute x24 -> x19, waiting for transfers between devices: 17.6 us -> 9.92 us  [permute(): return lax.ppermute(block, BOTH, everywhere(sizes, target))]
    unnamed x10 -> x24, local copies, waits for them, and re-layouts: 1.5 us -> 6.56 us
    all_to_all x0 -> x1, starting transfers between devices: none -> 4.04 us  [across(): lax.all_to_all(block, 'tm', 0, 0, axis_index_groups=groups, tiled=True)]
    pallas_call x6 -> x5, Pallas kernels: 12.1 us -> 15.4 us  [conv_call(): pl.pallas_call(functools.partial(conv_kernel, tuple(jobs), any_rim, frame...]
    all_to_all x0 -> x1, waiting for transfers between devices: none -> 1.57 us  [across(): lax.all_to_all(block, 'tm', 0, 0, axis_index_groups=groups, tiled=True)]
    pallas_call x2, Pallas kernels: 0.25 us -> 1.49 us  [sum_call(): pl.pallas_call(kernel, out_shape=[jax.ShapeDtypeStruct((size, chans), jnp...]
    transpose x0 -> x1, local copies, waits for them, and re-layouts: none -> 1.22 us  [by_part(): return jnp.moveaxis(x.reshape(*x.shape[:-1], parts, width), -2, 0)]
  transfers between devices with their start and end apart: 26 -> 22, of which waited for: 10 -> 9; matrix products, arithmetic and copies ran while one was open for 1% -> 2% of each run, Pallas kernels for 13% -> 11%
where the time goes in v9:
time: 109 us; the launch traced here: 108 us
  starting transfers between devices  41.4 us (38%)
  Pallas kernels  22.2 us (20%)
  waiting for transfers between devices  22 us (20%)
  blocking collectives  12.7 us (12%)
  local copies, waits for them, and re-layouts  7.91 us (7%)
  other arithmetic  1.67 us (2%)
    ppermute x19, starting transfers between devices, permute(): return lax.ppermute(block, BOTH, everywhere(sizes, target))  32.2 us
    pallas_call x5, Pallas kernels, conv_call(): pl.pallas_call(functools.partial(conv_kernel, tuple(jobs), any_rim, frame...  15.4 us
    all_to_all x1, blocking collectives, across(): lax.all_to_all(block, 'tm', 0, 0, axis_index_groups=groups, tiled=True)  12.7 us
    ppermute x2, waiting for transfers between devices, body(): back.append(lax.ppermute(done[p], BOTH, pairs))  10.5 us
    ppermute x19, waiting for transfers between devices, permute(): return lax.ppermute(block, BOTH, everywhere(sizes, target))  9.92 us
    unnamed x24, local copies, waits for them, and re-layouts  6.56 us
    ppermute x2, starting transfers between devices, body(): back.append(lax.ppermute(done[p], BOTH, pairs))  5.1 us
    pallas_call x1, Pallas kernels, attend_call(): pl.pallas_call(functools.partial(attend_kernel, frames, share, chunks), o...  4.39 us
  transfers between devices with their start and end apart: 22, of which 9 were waited for; matrix products, arithmetic and copies ran while one was open for 2% of the time, Pallas kernels for 11%

profile of v9, /device:TPU:1, one launch (start us, length us, event | category | flops | bytes accessed | tf_op | source)
XLA Modules:
  0.0 108.2 jit_solution(8650495905848089516)
XLA Ops:
  0.0 0.1 collective-permute-start
  0.1 1.2 %bitcast_bitcast_fusion = bf16[4,2,4,64,128]{4,3,2,1,0:T(8,128)(2,1)S(1)} fusion(bf16[2,4,64,512]{3,2,1,0:T(8,128)(2,1)} %param.6), kind=kLoop, calls=%fused_computation | loop fusion | bytes 1048576 | tf_op jit(solution)/shard_map/transpose | solution.py:318
  1.3 12.7 %all_to_all.10.refs_2_ = bf16[4,2,4,64,128]{4,3,2,1,0:T(8,128)(2,1)} all-to-all(bf16[4,2,4,64,128]{4,3,2,1,0:T(8,128)(2,1)S(1)} %bitcast_bitcast_fusion), channel_id=1, replica_groups={{0,8,16,24},{4,12,20,28},{1,9,17,25},{5,13,21,29},{2,10,18,26},{6,14,22..., dimensions={0} | all-to-all | bytes 1048576 | tf_op jit(solution)/shard_map/all_to_all | solution.py:315
  14.0 1.5 %collective-permute-start.1 = (bf16[4,2,4,64,128]{4,3,2,1,0:T(8,128)(2,1)}, bf16[4,2,4,64,128]{4,3,2,1,0:T(8,128)(2,1)}, u32[]{:S(2)}, u32[]{:S(2)}) collective-permute-start(bf16[4,2,4,64,128]{4,3,2,1,0:T(8,128)(2,1)} %all_to_all.10.refs_2_), channel_id=1, source_target_pairs={{0,4},{1,5},{2,6},{3,7},{4,0},{5,1},{6,2},{7,3},{8,12},{9,13},{10,... | collective-permute-start | bytes 1572872 | tf_op jit(solution)/shard_map/ppermute | solution.py:305
  15.5 1.3 %collective-permute-start.6 = (bf16[2,64,512]{2,1,0:T(8,128)(2,1)S(1)}, bf16[2,64,512]{2,1,0:T(8,128)(2,1)S(1)}, u32[]{:S(2)}, u32[]{:S(2)}) collective-permute-start(bf16[2,64,512]{2,1,0:T(8,128)(2,1)S(1)} %get-tuple-element.32), channel_id=1, source_target_pairs={{1,0},{2,1},{3,2},{5,4},{6,5},{7,6},{9,8},{10,9},{11,10},{13,12},{... | collective-permute-start | bytes 393224 | tf_op jit(solution)/shard_map/ppermute | solution.py:305
  16.8 4.0 %collective-permute-start.5 = (bf16[2,64,512]{2,1,0:T(8,128)(2,1)S(1)}, bf16[2,64,512]{2,1,0:T(8,128)(2,1)S(1)}, u32[]{:S(2)}, u32[]{:S(2)}) collective-permute-start(bf16[2,64,512]{2,1,0:T(8,128)(2,1)S(1)} %get-tuple-element.31), channel_id=1, source_target_pairs={{0,1},{1,2},{2,3},{4,5},{5,6},{6,7},{8,9},{9,10},{10,11},{12,13},{... | collective-permute-start | bytes 393224 | tf_op jit(solution)/shard_map/ppermute | solution.py:305
  20.9 0.1 pad_add_fusion.refs_0_
  20.9 1.6 %collective-permute-done.6 = bf16[2,64,512]{2,1,0:T(8,128)(2,1)S(1)} collective-permute-done((bf16[2,64,512]{2,1,0:T(8,128)(2,1)S(1)}, bf16[2,64,512]{2,1,0:T(8,128)(2,1)S(1)}, u32[]{:S(2)}, u32[]{:S(2)}) %collective-permute-start.6) | collective-permute-done | bytes 131104 | tf_op jit(solution)/shard_map/ppermute | solution.py:305
  22.6 0.8 collective-permute-done.5
  23.5 0.7 maximum_bitcast_fusion
  24.2 0.0 collective-permute-done.refs_2_
  24.2 1.2 %copy-done.1 = bf16[9,3,64,512]{3,2,1,0:T(8,128)(2,1)} copy-done((bf16[9,3,64,512]{3,2,1,0:T(8,128)(2,1)}, bf16[9,3,64,512]{3,2,1,0:T(8,128)(2,1)S(1)}, u32[]{:S(2)}) %copy-start.1) | copy-done | bytes 1769496
  25.4 1.5 %copy-done = bf16[27,64,512]{2,1,0:T(8,128)(2,1)S(1)} copy-done((bf16[27,64,512]{2,1,0:T(8,128)(2,1)S(1)}, bf16[27,64,512]{2,1,0:T(8,128)(2,1)}, u32[]{:S(2)}) %copy-start) | copy-done | bytes 1769496
  26.9 1.5 %copy-done.2 = bf16[9,3,64,512]{3,2,1,0:T(8,128)(2,1)S(1)} copy-done((bf16[9,3,64,512]{3,2,1,0:T(8,128)(2,1)S(1)}, bf16[9,3,64,512]{3,2,1,0:T(8,128)(2,1)}, u32[]{:S(2)}) %copy-start.2) | copy-done | bytes 1769496
  28.4 0.9 merge_kernel_slices.1.refs_1_
  29.2 0.0 collective-permute-done.1.refs_3_
  29.3 2.4 %conv_inner.3.refs_4_ = bf16[256,512]{1,0:T(8,128)(2,1)S(1)} custom-call(s32[3]{0:T(128)S(1)} %pad_add_fusion.refs_0_, bf16[3,9,128,512]{3,2,1,0:T(8,128)(2,1)S(1)} %merge_kernel_slices.1.refs_1_, bf16[4,2,4,64,128]{4,3,2,1,0:T(8,128)(2,1)} %all_to_all.10.refs_2_, bf16[4,2,4,64,128]{4,3,2,1,0:T(8,128)(2,1)} %collective-permute-done.1.refs_3_), custom_call_target="tpu_custom_call" | custom-call | flops 9059696640 | bytes 3538944 | tf_op jit(solution)/shard_map/conv_inner/pallas_call | solution.py:141
  31.7 3.5 %conv_inner.4 = (bf16[256,512]{1,0:T(8,128)(2,1)S(1)}, bf16[256,512]{1,0:T(8,128)(2,1)S(1)}) custom-call(s32[3]{0:T(128)S(1)} %pad_add_fusion.refs_0_, bf16[3,9,128,512]{3,2,1,0:T(8,128)(2,1)S(1)} %merge_kernel_slices.1.refs_1_, bf16[4,2,4,64,128]{4,3,2,1,0:T(8,128)(2,1)} %all_to_all.10.refs_2_, bf16[4,2,4,64,128]{4,3,2,1,0:T(8,128)(2,1)} %collective-permute-done.1.refs_3_, ...), custom_call_target="tpu_custom_call" | custom-call | flops 18119393280 | bytes 3538944 | tf_op jit(solution)/shard_map/conv_inner/pallas_call | solution.py:141
  35.3 0.0 copy-start.7
  35.3 0.7 copy-done.7
  36.0 0.7 copy-done.9
  36.7 4.0 %all-to-all-start.1 = ((bf16[4,2,2,64,128]{4,3,2,1,0:T(8,128)(2,1)}), bf16[4,2,2,64,128]{4,3,2,1,0:T(8,128)(2,1)}, u32[]{:S(2)}, u32[]{:S(2)}) async-start(bf16[4,2,2,64,128]{4,3,2,1,0:T(8,128)(2,1)} %maximum_bitcast_fusion), calls=%async_computation.1 | async-start | bytes 524288 | tf_op jit(solution)/shard_map/all_to_all | solution.py:315
  40.7 2.3 %collective-permute-start.2 = (bf16[256,512]{1,0:T(8,128)(2,1)}, bf16[256,512]{1,0:T(8,128)(2,1)}, u32[]{:S(2)}, u32[]{:S(2)}) collective-permute-start(bf16[256,512]{1,0:T(8,128)(2,1)} %copy-done.10), channel_id=1, source_target_pairs={{0,24},{1,25},{2,26},{3,27},{4,28},{5,29},{6,30},{7,31},{8,16},{9,... | collective-permute-start | bytes 786440 | tf_op jit(solution)/shard_map/ppermute | solution.py:305
  43.0 0.3 collective-permute-start.4
  43.3 0.1 collective-permute-start.3
  43.4 1.6 %all-to-all-done.1.refs_4_ = bf16[4,2,2,64,128]{4,3,2,1,0:T(8,128)(2,1)} async-done(((bf16[4,2,2,64,128]{4,3,2,1,0:T(8,128)(2,1)}), bf16[4,2,2,64,128]{4,3,2,1,0:T(8,128)(2,1)}, u32[]{:S(2)}, u32[]{:S(2)}) %all-to-all-start.1) | async-done | bytes 262176 | tf_op jit(solution)/shard_map/all_to_all | solution.py:315
  45.0 3.5 %collective-permute-start.7 = (bf16[4,2,2,64,128]{4,3,2,1,0:T(8,128)(2,1)}, bf16[4,2,2,64,128]{4,3,2,1,0:T(8,128)(2,1)S(1)}, u32[]{:S(2)}, u32[]{:S(2)}) collective-permute-start(bf16[4,2,2,64,128]{4,3,2,1,0:T(8,128)(2,1)} %all-to-all-done.1.refs_4_), channel_id=1, source_target_pairs={{0,4},{1,5},{2,6},{3,7},{4,0},{5,1},{6,2},{7,3},{8,12},{9,13},{10,... | collective-permute-start | bytes 786440 | tf_op jit(solution)/shard_map/ppermute | solution.py:305
  48.5 0.9 copy-done.8
  49.5 2.4 %conv_inner.5.refs_6_.refs_0_ = f32[256,512]{1,0:T(8,128)S(1)} custom-call(s32[3]{0:T(128)S(1)} %pad_add_fusion.refs_0_, bf16[3,9,128,512]{3,2,1,0:T(8,128)(2,1)S(1)} %merge_kernel_slices.1.refs_1_, bf16[4,2,4,64,128]{4,3,2,1,0:T(8,128)(2,1)} %all_to_all.10.refs_2_, bf16[4,2,4,64,128]{4,3,2,1,0:T(8,128)(2,1)} %collective-permute-done.1.refs_3_, ...), custom_call_target="tpu_custom_call" | custom-call | flops 9059696640 | bytes 3538944 | tf_op jit(solution)/shard_map/conv_inner/pallas_call | solution.py:141
  51.9 0.0 collective-permute-done.7.refs_5_
  51.9 4.6 %conv_rim.2 = (bf16[256,512]{1,0:T(8,128)(2,1)S(1)}, bf16[256,512]{1,0:T(8,128)(2,1)S(1)}, bf16[256,512]{1,0:T(8,128)(2,1)S(1)}) custom-call(s32[3]{0:T(128)S(1)} %pad_add_fusion.refs_0_, bf16[3,9,128,512]{3,2,1,0:T(8,128)(2,1)S(1)} %merge_kernel_slices.1.refs_1_, bf16[4,2,4,64,128]{4,3,2,1,0:T(8,128)(2,1)} %all_to_all.10.refs_2_, ...), custom_call_target="tpu_custom_call" | custom-call | flops 27179089920 | bytes 3538944 | tf_op jit(solution)/shard_map/conv_rim/pallas_call | solution.py:141
  56.5 5.0 %collective-permute-start.9 = (bf16[256,512]{1,0:T(8,128)(2,1)S(1)}, bf16[256,512]{1,0:T(8,128)(2,1)S(1)}, u32[]{:S(2)}, u32[]{:S(2)}) collective-permute-start(bf16[256,512]{1,0:T(8,128)(2,1)S(1)} %get-tuple-element.22), channel_id=1, source_target_pairs={{0,24},{1,25},{2,26},{3,27},{4,28},{5,29},{6,30},{7,31},{8,16},{9,... | collective-permute-start | bytes 786440 | tf_op jit(solution)/shard_map/ppermute | solution.py:305
  61.5 0.2 collective-permute-start.10
  61.6 0.0 collective-permute-done.2.refs_1_
  61.6 0.2 collective-permute-start.11
  61.8 2.5 %conv_rim.3.refs_4_.refs_0_ = f32[256,512]{1,0:T(8,128)S(1)} custom-call(s32[3]{0:T(128)S(1)} %pad_add_fusion.refs_0_, bf16[3,9,128,512]{3,2,1,0:T(8,128)(2,1)S(1)} %merge_kernel_slices.1.refs_1_, bf16[4,2,4,64,128]{4,3,2,1,0:T(8,128)(2,1)} %all_to_all.10.refs_2_, bf16[4,2,4,64,128]{4,3,2,1,0:T(8,128)(2,1)} %collective-permute-done.1.refs_3_, ...), custom_call_target="tpu_custom_call" | custom-call | flops 9059696640 | bytes 3538944 | tf_op jit(solution)/shard_map/conv_rim/pallas_call | solution.py:141
  64.3 0.0 copy-start.3
  64.3 0.0 copy-start.4
  64.3 0.0 copy-start.5
  64.3 0.0 copy-start.6
  64.4 0.0 collective-permute-done.4.refs_3_
  64.4 1.4 %sum_parts.2 = (bf16[128,512]{1,0:T(8,128)(2,1)S(1)}, bf16[128,512]{1,0:T(8,128)(2,1)S(1)}) custom-call(f32[256,512]{1,0:T(8,128)S(1)} %conv_inner.5.refs_6_.refs_0_, bf16[256,512]{1,0:T(8,128)(2,1)} %collective-permute-done.2.refs_1_, bf16[256,512]{1,0:T(8,128)(2,1)} %collective-permute-done.3.refs_2_, bf16[256,512]{1,0:T(8,128)(2,1)} %collective-permute-done.4.refs_3_, ...), custom_call_target="tpu_custom_call" | custom-call | tf_op jit(solution)/shard_map/sum_parts/pallas_call | solution.py:171
  65.7 5.6 %collective-permute-start.8 = (bf16[128,512]{1,0:T(8,128)(2,1)S(1)}, bf16[128,512]{1,0:T(8,128)(2,1)S(1)}, u32[]{:S(2)}, u32[]{:S(2)}) collective-permute-start(bf16[128,512]{1,0:T(8,128)(2,1)S(1)} %get-tuple-element.21), channel_id=1, source_target_pairs={{0,0},{1,1},{2,4},{3,5},{4,2},{5,3},{6,6},{7,7},{8,8},{9,9},{10,12... | collective-permute-start | bytes 393224 | tf_op jit(solution)/shard_map/ppermute | solution.py:305
  71.4 1.1 %collective-permute-start.13 = (bf16[128,512]{1,0:T(8,128)(2,1)S(1)}, bf16[128,512]{1,0:T(8,128)(2,1)S(1)}, u32[]{:S(2)}, u32[]{:S(2)}) collective-permute-start(bf16[128,512]{1,0:T(8,128)(2,1)S(1)} %get-tuple-element.25), channel_id=1, source_target_pairs={{0,1},{1,0},{2,5},{3,4},{4,3},{5,2},{6,7},{7,6},{8,9},{9,8},{10,13... | collective-permute-start | bytes 393224 | tf_op jit(solution)/shard_map/ppermute | solution.py:305
  72.5 0.0 collective-permute-done.9.refs_1_
  72.5 1.4 %collective-permute-done.10.refs_2_ = bf16[256,512]{1,0:T(8,128)(2,1)S(1)} collective-permute-done((bf16[256,512]{1,0:T(8,128)(2,1)S(1)}, bf16[256,512]{1,0:T(8,128)(2,1)S(1)}, u32[]{:S(2)}, u32[]{:S(2)}) %collective-permute-start.10) | collective-permute-done | bytes 262176 | tf_op jit(solution)/shard_map/ppermute | solution.py:305
  73.9 0.0 collective-permute-done.11.refs_3_
  73.9 0.1 sum_parts.3
  74.0 5.5 %collective-permute-start.12 = (bf16[128,512]{1,0:T(8,128)(2,1)S(1)}, bf16[128,512]{1,0:T(8,128)(2,1)S(1)}, u32[]{:S(2)}, u32[]{:S(2)}) collective-permute-start(bf16[128,512]{1,0:T(8,128)(2,1)S(1)} %get-tuple-element.24), channel_id=1, source_target_pairs={{0,0},{1,1},{2,4},{3,5},{4,2},{5,3},{6,6},{7,7},{8,8},{9,9},{10,12... | collective-permute-start | bytes 393224 | tf_op jit(solution)/shard_map/ppermute | solution.py:305
  79.5 1.1 %collective-permute-start.14 = (bf16[128,512]{1,0:T(8,128)(2,1)S(1)}, bf16[128,512]{1,0:T(8,128)(2,1)S(1)}, u32[]{:S(2)}, u32[]{:S(2)}) collective-permute-start(bf16[128,512]{1,0:T(8,128)(2,1)S(1)} %get-tuple-element.26), channel_id=1, source_target_pairs={{0,1},{1,0},{2,5},{3,4},{4,3},{5,2},{6,7},{7,6},{8,9},{9,8},{10,13... | collective-permute-start | bytes 393224 | tf_op jit(solution)/shard_map/ppermute | solution.py:305
  80.6 0.0 collective-permute-done.13.refs_2_
  80.6 0.5 collective-permute-start.17
  81.1 2.4 %collective-permute-done.12.refs_1_ = bf16[128,512]{1,0:T(8,128)(2,1)S(1)} collective-permute-done((bf16[128,512]{1,0:T(8,128)(2,1)S(1)}, bf16[128,512]{1,0:T(8,128)(2,1)S(1)}, u32[]{:S(2)}, u32[]{:S(2)}) %collective-permute-start.12) | collective-permute-done | bytes 131104 | tf_op jit(solution)/shard_map/ppermute | solution.py:305
  83.5 0.0 collective-permute-start.16
  83.5 2.3 %collective-permute-done.14.refs_3_ = bf16[128,512]{1,0:T(8,128)(2,1)S(1)} collective-permute-done((bf16[128,512]{1,0:T(8,128)(2,1)S(1)}, bf16[128,512]{1,0:T(8,128)(2,1)S(1)}, u32[]{:S(2)}, u32[]{:S(2)}) %collective-permute-start.14) | collective-permute-done | bytes 131104 | tf_op jit(solution)/shard_map/ppermute | solution.py:305
  85.9 0.0 collective-permute-done.17.refs_6_
  85.9 0.0 collective-permute-done.16.refs_5_
  85.9 1.3 %collective-permute-done.18.refs_7_ = bf16[128,512]{1,0:T(8,128)(2,1)S(1)} collective-permute-done((bf16[128,512]{1,0:T(8,128)(2,1)S(1)}, bf16[128,512]{1,0:T(8,128)(2,1)S(1)}, u32[]{:S(2)}, u32[]{:S(2)}) %collective-permute-start.18) | collective-permute-done | bytes 131104 | tf_op jit(solution)/shard_map/ppermute | solution.py:305
  87.2 4.4 %attend.1 = (bf16[4,64,512]{2,1,0:T(8,128)(2,1)S(1)}, bf16[4,64,512]{2,1,0:T(8,128)(2,1)S(1)}) custom-call(bf16[128,512]{1,0:T(8,128)(2,1)S(1)} %collective-permute-done.8.refs_0_, bf16[128,512]{1,0:T(8,128)(2,1)S(1)} %collective-permute-done.12.refs_1_, bf16[128,512]{1,0:T(8,128)(2,1)S(1)} %collective-permute-done.13.refs_2_, ...), custom_call_target="tpu_custom_call" | custom-call | flops 2684354560 | bytes 3145728 | tf_op jit(solution)/shard_map/attend/pallas_call | solution.py:276
  91.6 2.9 %collective-permute-start.19 = (bf16[4,64,512]{2,1,0:T(8,128)(2,1)S(1)}, bf16[4,64,512]{2,1,0:T(8,128)(2,1)S(1)}, u32[]{:S(2)}, u32[]{:S(2)}) collective-permute-start(bf16[4,64,512]{2,1,0:T(8,128)(2,1)S(1)} %get-tuple-element.27), channel_id=1, source_target_pairs={{1,0},{0,1},{5,2},{4,3},{3,4},{2,5},{7,6},{6,7},{9,8},{8,9},{13,10... | collective-permute-start | bytes 786440 | tf_op jit(solution)/shard_map/ppermute | solution.py:381
  94.5 2.2 %collective-permute-start.20 = (bf16[4,64,512]{2,1,0:T(8,128)(2,1)S(1)}, bf16[4,64,512]{2,1,0:T(8,128)(2,1)S(1)}, u32[]{:S(2)}, u32[]{:S(2)}) collective-permute-start(bf16[4,64,512]{2,1,0:T(8,128)(2,1)S(1)} %get-tuple-element.28), channel_id=1, source_target_pairs={{0,0},{1,1},{4,2},{5,3},{2,4},{3,5},{6,6},{7,7},{8,8},{9,9},{12,10... | collective-permute-start | bytes 786440 | tf_op jit(solution)/shard_map/ppermute | solution.py:381
  96.7 5.1 %collective-permute-done.19 = bf16[4,64,512]{2,1,0:T(8,128)(2,1)S(1)} collective-permute-done((bf16[4,64,512]{2,1,0:T(8,128)(2,1)S(1)}, bf16[4,64,512]{2,1,0:T(8,128)(2,1)S(1)}, u32[]{:S(2)}, u32[]{:S(2)}) %collective-permute-start.19) | collective-permute-done | bytes 262176 | tf_op jit(solution)/shard_map/ppermute | solution.py:381
  101.9 5.4 %collective-permute-done.20 = bf16[4,64,512]{2,1,0:T(8,128)(2,1)S(1)} collective-permute-done((bf16[4,64,512]{2,1,0:T(8,128)(2,1)S(1)}, bf16[4,64,512]{2,1,0:T(8,128)(2,1)S(1)}, u32[]{:S(2)}, u32[]{:S(2)}) %collective-permute-start.20) | collective-permute-done | bytes 262176 | tf_op jit(solution)/shard_map/ppermute | solution.py:381
  107.3 0.8 pad_maximum_fusion
  (24 shorter events, 0.2 us)
Async XLA Ops:
  0.0 15.5 %copy-start.11 = (bf16[2,4,64,512]{3,2,1,0:T(8,128)(2,1)S(1)}, bf16[2,4,64,512]{3,2,1,0:T(8,128)(2,1)}, u32[]{:S(2)}) copy-start(bf16[2,4,64,512]{3,2,1,0:T(8,128)(2,1)} %param.6) | copy-start | bytes 1572868
  0.0 24.2 %collective-permute-start = (bf16[9,3,64,512]{3,2,1,0:T(8,128)(2,1)}, bf16[9,3,64,512]{3,2,1,0:T(8,128)(2,1)S(1)}, u32[]{:S(2)}, u32[]{:S(2)}) collective-permute-start(bf16[9,3,64,512]{3,2,1,0:T(8,128)(2,1)} %bitcast.21), channel_id=1, source_target_pairs={{0,4},{1,5},{2,6},{3,7},{4,0},{5,1},{6,2},{7,3},{8,12},{9,13},{10,... | collective-permute-start | bytes 5308424 | tf_op jit(solution)/shard_map/ppermute | solution.py:305
  14.0 15.3 %collective-permute-start.1 = (bf16[4,2,4,64,128]{4,3,2,1,0:T(8,128)(2,1)}, bf16[4,2,4,64,128]{4,3,2,1,0:T(8,128)(2,1)}, u32[]{:S(2)}, u32[]{:S(2)}) collective-permute-start(bf16[4,2,4,64,128]{4,3,2,1,0:T(8,128)(2,1)} %all_to_all.10.refs_2_), channel_id=1, source_target_pairs={{0,4},{1,5},{2,6},{3,7},{4,0},{5,1},{6,2},{7,3},{8,12},{9,13},{10,... | collective-permute-start | bytes 1572872 | tf_op jit(solution)/shard_map/ppermute | solution.py:305
  15.5 7.0 %collective-permute-start.6 = (bf16[2,64,512]{2,1,0:T(8,128)(2,1)S(1)}, bf16[2,64,512]{2,1,0:T(8,128)(2,1)S(1)}, u32[]{:S(2)}, u32[]{:S(2)}) collective-permute-start(bf16[2,64,512]{2,1,0:T(8,128)(2,1)S(1)} %get-tuple-element.32), channel_id=1, source_target_pairs={{1,0},{2,1},{3,2},{5,4},{6,5},{7,6},{9,8},{10,9},{11,10},{13,12},{... | collective-permute-start | bytes 393224 | tf_op jit(solution)/shard_map/ppermute | solution.py:305
  16.8 6.6 %collective-permute-start.5 = (bf16[2,64,512]{2,1,0:T(8,128)(2,1)S(1)}, bf16[2,64,512]{2,1,0:T(8,128)(2,1)S(1)}, u32[]{:S(2)}, u32[]{:S(2)}) collective-permute-start(bf16[2,64,512]{2,1,0:T(8,128)(2,1)S(1)} %get-tuple-element.31), channel_id=1, source_target_pairs={{0,1},{1,2},{2,3},{4,5},{5,6},{6,7},{8,9},{9,10},{10,11},{12,13},{... | collective-permute-start | bytes 393224 | tf_op jit(solution)/shard_map/ppermute | solution.py:305
  24.2 1.2 %copy-start.1 = (bf16[9,3,64,512]{3,2,1,0:T(8,128)(2,1)}, bf16[9,3,64,512]{3,2,1,0:T(8,128)(2,1)S(1)}, u32[]{:S(2)}) copy-start(bf16[9,3,64,512]{3,2,1,0:T(8,128)(2,1)S(1)} %collective-permute-done.refs_2_) | copy-start | bytes 5308420
  25.4 1.5 %copy-start = (bf16[27,64,512]{2,1,0:T(8,128)(2,1)S(1)}, bf16[27,64,512]{2,1,0:T(8,128)(2,1)}, u32[]{:S(2)}) copy-start(bf16[27,64,512]{2,1,0:T(8,128)(2,1)} %param.7) | copy-start | bytes 5308420
  26.9 1.5 %copy-start.2 = (bf16[9,3,64,512]{3,2,1,0:T(8,128)(2,1)S(1)}, bf16[9,3,64,512]{3,2,1,0:T(8,128)(2,1)}, u32[]{:S(2)}) copy-start(bf16[9,3,64,512]{3,2,1,0:T(8,128)(2,1)} %copy-done.1) | copy-start | bytes 5308420
  31.7 3.6 %copy-start.10 = (bf16[256,512]{1,0:T(8,128)(2,1)}, bf16[256,512]{1,0:T(8,128)(2,1)S(1)}, u32[]{:S(2)}) copy-start(bf16[256,512]{1,0:T(8,128)(2,1)S(1)} %conv_inner.3.refs_4_) | copy-start | bytes 786436
  35.3 0.7 copy-start.7
  36.0 0.7 copy-start.9
  36.7 8.3 %all-to-all-start.1 = ((bf16[4,2,2,64,128]{4,3,2,1,0:T(8,128)(2,1)}), bf16[4,2,2,64,128]{4,3,2,1,0:T(8,128)(2,1)}, u32[]{:S(2)}, u32[]{:S(2)}) async-start(bf16[4,2,2,64,128]{4,3,2,1,0:T(8,128)(2,1)} %maximum_bitcast_fusion), calls=%async_computation.1 | async-start | bytes 524288 | tf_op jit(solution)/shard_map/all_to_all | solution.py:315
  40.7 20.9 %collective-permute-start.2 = (bf16[256,512]{1,0:T(8,128)(2,1)}, bf16[256,512]{1,0:T(8,128)(2,1)}, u32[]{:S(2)}, u32[]{:S(2)}) collective-permute-start(bf16[256,512]{1,0:T(8,128)(2,1)} %copy-done.10), channel_id=1, source_target_pairs={{0,24},{1,25},{2,26},{3,27},{4,28},{5,29},{6,30},{7,31},{8,16},{9,... | collective-permute-start | bytes 786440 | tf_op jit(solution)/shard_map/ppermute | solution.py:305
  43.0 21.3 %collective-permute-start.4 = (bf16[256,512]{1,0:T(8,128)(2,1)}, bf16[256,512]{1,0:T(8,128)(2,1)}, u32[]{:S(2)}, u32[]{:S(2)}) collective-permute-start(bf16[256,512]{1,0:T(8,128)(2,1)} %copy-done.7), channel_id=1, source_target_pairs={{0,8},{1,9},{2,10},{3,11},{4,12},{5,13},{6,14},{7,15},{8,0},{9,1},... | collective-permute-start | bytes 786440 | tf_op jit(solution)/shard_map/ppermute | solution.py:305
  43.3 21.1 %collective-permute-start.3 = (bf16[256,512]{1,0:T(8,128)(2,1)}, bf16[256,512]{1,0:T(8,128)(2,1)}, u32[]{:S(2)}, u32[]{:S(2)}) collective-permute-start(bf16[256,512]{1,0:T(8,128)(2,1)} %copy-done.9), channel_id=1, source_target_pairs={{0,16},{1,17},{2,18},{3,19},{4,20},{5,21},{6,22},{7,23},{8,24},{9,... | collective-permute-start | bytes 786440 | tf_op jit(solution)/shard_map/ppermute | solution.py:305
  45.0 6.9 %collective-permute-start.7 = (bf16[4,2,2,64,128]{4,3,2,1,0:T(8,128)(2,1)}, bf16[4,2,2,64,128]{4,3,2,1,0:T(8,128)(2,1)S(1)}, u32[]{:S(2)}, u32[]{:S(2)}) collective-permute-start(bf16[4,2,2,64,128]{4,3,2,1,0:T(8,128)(2,1)} %all-to-all-done.1.refs_4_), channel_id=1, source_target_pairs={{0,4},{1,5},{2,6},{3,7},{4,0},{5,1},{6,2},{7,3},{8,12},{9,13},{10,... | collective-permute-start | bytes 786440 | tf_op jit(solution)/shard_map/ppermute | solution.py:305
  48.5 0.9 copy-start.8
  56.5 16.0 %collective-permute-start.9 = (bf16[256,512]{1,0:T(8,128)(2,1)S(1)}, bf16[256,512]{1,0:T(8,128)(2,1)S(1)}, u32[]{:S(2)}, u32[]{:S(2)}) collective-permute-start(bf16[256,512]{1,0:T(8,128)(2,1)S(1)} %get-tuple-element.22), channel_id=1, source_target_pairs={{0,24},{1,25},{2,26},{3,27},{4,28},{5,29},{6,30},{7,31},{8,16},{9,... | collective-permute-start | bytes 786440 | tf_op jit(solution)/shard_map/ppermute | solution.py:305
  61.5 12.4 %collective-permute-start.10 = (bf16[256,512]{1,0:T(8,128)(2,1)S(1)}, bf16[256,512]{1,0:T(8,128)(2,1)S(1)}, u32[]{:S(2)}, u32[]{:S(2)}) collective-permute-start(bf16[256,512]{1,0:T(8,128)(2,1)S(1)} %get-tuple-element.23), channel_id=1, source_target_pairs={{0,16},{1,17},{2,18},{3,19},{4,20},{5,21},{6,22},{7,23},{8,24},{9,... | collective-permute-start | bytes 786440 | tf_op jit(solution)/shard_map/ppermute | solution.py:305
  61.6 12.2 %collective-permute-start.11 = (bf16[256,512]{1,0:T(8,128)(2,1)S(1)}, bf16[256,512]{1,0:T(8,128)(2,1)S(1)}, u32[]{:S(2)}, u32[]{:S(2)}) collective-permute-start(bf16[256,512]{1,0:T(8,128)(2,1)S(1)} %get-tuple-element.20.refs_6_), channel_id=1, source_target_pairs={{0,8},{1,9},{2,10},{3,11},{4,12},{5,13},{6,14},{7,15},{8,0},{9,1},... | collective-permute-start | bytes 786440 | tf_op jit(solution)/shard_map/ppermute | solution.py:305
  64.3 22.9 %copy-start.3 = (bf16[512,512]{1,0:T(8,128)(2,1)S(1)}, bf16[512,512]{1,0:T(8,128)(2,1)}, u32[]{:S(2)}) copy-start(bf16[512,512]{1,0:T(8,128)(2,1)} %refs_8_.1) | copy-start | bytes 1572868
  64.3 22.9 %copy-start.4 = (bf16[512,512]{1,0:T(8,128)(2,1)S(1)}, bf16[512,512]{1,0:T(8,128)(2,1)}, u32[]{:S(2)}) copy-start(bf16[512,512]{1,0:T(8,128)(2,1)} %refs_9_.1) | copy-start | bytes 1572868
  64.3 22.9 %copy-start.5 = (bf16[512,512]{1,0:T(8,128)(2,1)S(1)}, bf16[512,512]{1,0:T(8,128)(2,1)}, u32[]{:S(2)}) copy-start(bf16[512,512]{1,0:T(8,128)(2,1)} %refs_10_.1) | copy-start | bytes 1572868
  64.3 22.9 %copy-start.6 = (bf16[512,512]{1,0:T(8,128)(2,1)S(1)}, bf16[512,512]{1,0:T(8,128)(2,1)}, u32[]{:S(2)}) copy-start(bf16[512,512]{1,0:T(8,128)(2,1)} %refs_11_.1) | copy-start | bytes 1572868
  65.7 14.8 %collective-permute-start.8 = (bf16[128,512]{1,0:T(8,128)(2,1)S(1)}, bf16[128,512]{1,0:T(8,128)(2,1)S(1)}, u32[]{:S(2)}, u32[]{:S(2)}) collective-permute-start(bf16[128,512]{1,0:T(8,128)(2,1)S(1)} %get-tuple-element.21), channel_id=1, source_target_pairs={{0,0},{1,1},{2,4},{3,5},{4,2},{5,3},{6,6},{7,7},{8,8},{9,9},{10,12... | collective-permute-start | bytes 393224 | tf_op jit(solution)/shard_map/ppermute | solution.py:305
  71.4 9.2 %collective-permute-start.13 = (bf16[128,512]{1,0:T(8,128)(2,1)S(1)}, bf16[128,512]{1,0:T(8,128)(2,1)S(1)}, u32[]{:S(2)}, u32[]{:S(2)}) collective-permute-start(bf16[128,512]{1,0:T(8,128)(2,1)S(1)} %get-tuple-element.25), channel_id=1, source_target_pairs={{0,1},{1,0},{2,5},{3,4},{4,3},{5,2},{6,7},{7,6},{8,9},{9,8},{10,13... | collective-permute-start | bytes 393224 | tf_op jit(solution)/shard_map/ppermute | solution.py:305
  74.0 9.5 %collective-permute-start.12 = (bf16[128,512]{1,0:T(8,128)(2,1)S(1)}, bf16[128,512]{1,0:T(8,128)(2,1)S(1)}, u32[]{:S(2)}, u32[]{:S(2)}) collective-permute-start(bf16[128,512]{1,0:T(8,128)(2,1)S(1)} %get-tuple-element.24), channel_id=1, source_target_pairs={{0,0},{1,1},{2,4},{3,5},{4,2},{5,3},{6,6},{7,7},{8,8},{9,9},{10,12... | collective-permute-start | bytes 393224 | tf_op jit(solution)/shard_map/ppermute | solution.py:305
  79.5 6.4 %collective-permute-start.14 = (bf16[128,512]{1,0:T(8,128)(2,1)S(1)}, bf16[128,512]{1,0:T(8,128)(2,1)S(1)}, u32[]{:S(2)}, u32[]{:S(2)}) collective-permute-start(bf16[128,512]{1,0:T(8,128)(2,1)S(1)} %get-tuple-element.26), channel_id=1, source_target_pairs={{0,1},{1,0},{2,5},{3,4},{4,3},{5,2},{6,7},{7,6},{8,9},{9,8},{10,13... | collective-permute-start | bytes 393224 | tf_op jit(solution)/shard_map/ppermute | solution.py:305
  80.6 5.3 %collective-permute-start.15 = (bf16[128,512]{1,0:T(8,128)(2,1)S(1)}, bf16[128,512]{1,0:T(8,128)(2,1)S(1)}, u32[]{:S(2)}, u32[]{:S(2)}) collective-permute-start(bf16[128,512]{1,0:T(8,128)(2,1)S(1)} %collective-permute-done.8.refs_0_), channel_id=1, source_target_pairs={{0,4},{1,5},{2,6},{3,7},{4,0},{5,1},{6,2},{7,3},{8,12},{9,13},{10,... | collective-permute-start | bytes 393224 | tf_op jit(solution)/shard_map/ppermute | solution.py:305
  80.6 5.3 %collective-permute-start.17 = (bf16[128,512]{1,0:T(8,128)(2,1)S(1)}, bf16[128,512]{1,0:T(8,128)(2,1)S(1)}, u32[]{:S(2)}, u32[]{:S(2)}) collective-permute-start(bf16[128,512]{1,0:T(8,128)(2,1)S(1)} %collective-permute-done.13.refs_2_), channel_id=1, source_target_pairs={{0,4},{1,5},{2,6},{3,7},{4,0},{5,1},{6,2},{7,3},{8,12},{9,13},{10,... | collective-permute-start | bytes 393224 | tf_op jit(solution)/shard_map/ppermute | solution.py:305
  83.5 2.3 %collective-permute-start.16 = (bf16[128,512]{1,0:T(8,128)(2,1)S(1)}, bf16[128,512]{1,0:T(8,128)(2,1)S(1)}, u32[]{:S(2)}, u32[]{:S(2)}) collective-permute-start(bf16[128,512]{1,0:T(8,128)(2,1)S(1)} %collective-permute-done.12.refs_1_), channel_id=1, source_target_pairs={{0,4},{1,5},{2,6},{3,7},{4,0},{5,1},{6,2},{7,3},{8,12},{9,13},{10,... | collective-permute-start | bytes 393224 | tf_op jit(solution)/shard_map/ppermute | solution.py:305
  85.8 1.3 %collective-permute-start.18 = (bf16[128,512]{1,0:T(8,128)(2,1)S(1)}, bf16[128,512]{1,0:T(8,128)(2,1)S(1)}, u32[]{:S(2)}, u32[]{:S(2)}) collective-permute-start(bf16[128,512]{1,0:T(8,128)(2,1)S(1)} %collective-permute-done.14.refs_3_), channel_id=1, source_target_pairs={{0,4},{1,5},{2,6},{3,7},{4,0},{5,1},{6,2},{7,3},{8,12},{9,13},{10,... | collective-permute-start | bytes 393224 | tf_op jit(solution)/shard_map/ppermute | solution.py:305
  91.6 10.3 %collective-permute-start.19 = (bf16[4,64,512]{2,1,0:T(8,128)(2,1)S(1)}, bf16[4,64,512]{2,1,0:T(8,128)(2,1)S(1)}, u32[]{:S(2)}, u32[]{:S(2)}) collective-permute-start(bf16[4,64,512]{2,1,0:T(8,128)(2,1)S(1)} %get-tuple-element.27), channel_id=1, source_target_pairs={{1,0},{0,1},{5,2},{4,3},{3,4},{2,5},{7,6},{6,7},{9,8},{8,9},{13,10... | collective-permute-start | bytes 786440 | tf_op jit(solution)/shard_map/ppermute | solution.py:381
  94.5 12.8 %collective-permute-start.20 = (bf16[4,64,512]{2,1,0:T(8,128)(2,1)S(1)}, bf16[4,64,512]{2,1,0:T(8,128)(2,1)S(1)}, u32[]{:S(2)}, u32[]{:S(2)}) collective-permute-start(bf16[4,64,512]{2,1,0:T(8,128)(2,1)S(1)} %get-tuple-element.28), channel_id=1, source_target_pairs={{0,0},{1,1},{4,2},{5,3},{2,4},{3,5},{6,6},{7,7},{8,8},{9,9},{12,10... | collective-permute-start | bytes 786440 | tf_op jit(solution)/shard_map/ppermute | solution.py:381

commit v10 on v5

--- a/solution.py
+++ b/solution.py
@@ -206,7 +206,11 @@
             pltpu.VMEM((len(dests), 2 * frames, rows_here + 2, columns, width), jnp.bfloat16)
         ],
         compiler_params=pltpu.CompilerParams(vmem_limit_bytes=VMEM_LIMIT),
-        cost_estimate=pl.CostEstimate(flops=10**11, bytes_accessed=1000, transcendentals=0),
+        cost_estimate=pl.CostEstimate(
+            flops=20 * total * taps * lags * width * chans,
+            bytes_accessed=2 * taps * lags * width * chans,
+            transcendentals=0,
+        ),
         name="conv_rim" if any_rim else "conv_inner",
     )(meta, *operands, *after)
 
@@ -423,25 +427,22 @@
         sum_call([rim_own, rim_got[1], rim_last], frames),
     ]
 
-    share = depth // frames
-
-    def frame_home(t, z, p):
-        frame = t % CORES * frames + (z + p) % frames
-        slot = frame * share + z // frames
-        return (t // CORES * CORES + slot % CORES, slot // CORES)
-
-    def next_in_frame(t, z, step):
-        slot = z * CORES + t % CORES
-        slot = slot // share * share + (slot + step) % share
-        return (t // CORES * CORES + slot % CORES, slot // CORES)
-
-    own = []
-    for p in range(frames):
-        for chunk in sums:
-            own.append(permute(chunk[p], lambda t, z: frame_home(t, z, p)))
-    others = []
-    for step in range(1, share):
-        others += [permute(x, lambda t, z: next_in_frame(t, z, step)) for x in own]
+    segments = depth // frames
+
+    def frame_home(t, z, p, s):
+        slot = t % CORES * frames + (z + p) % frames
+        segment = (z // frames + s) % segments
+        return (t // CORES * CORES + slot % CORES, segment * frames + slot // CORES)
+
+    own, others = [None] * (frames * len(sums)), []
+    for c, chunk in enumerate(sums):
+        for s in reversed(range(segments)):
+            for p in range(frames):
+                block = permute(chunk[p], lambda t, z: frame_home(t, z, p, s))
+                if s:
+                    others.append(block)
+                else:
+                    own[p * len(sums) + c] = block
 
     done = attend_call(
         own,
@@ -453,7 +454,7 @@
     )
     back = []
     for p in range(frames):
-        pairs = [(b, a) for a, b in everywhere(sizes, lambda t, z: frame_home(t, z, p))]
+        pairs = [(b, a) for a, b in everywhere(sizes, lambda t, z: frame_home(t, z, p, 0))]
         back.append(lax.ppermute(done[p], BOTH, pairs))
     return jnp.stack(
         [

time: 86.9 us -> 86.2 us (level)
  Pallas kernels: 19.7 us -> 17.6 us
  starting transfers between devices: 38.8 us -> 40.8 us
    ppermute x2, waiting for transfers between devices: 10.5 us -> 5.44 us  [body(): back.append(lax.ppermute(done[p], BOTH, pairs))]
    ppermute x28, waiting for transfers between devices: 12.7 us -> 17.3 us  [permute(): return lax.ppermute(block, BOTH, everywhere(sizes, target))]
    ppermute x28, starting transfers between devices: 33.9 us -> 38.1 us  [permute(): return lax.ppermute(block, BOTH, everywhere(sizes, target))]
    ppermute x2, starting transfers between devices: 4.9 us -> 2.62 us  [body(): back.append(lax.ppermute(done[p], BOTH, pairs))]
    pallas_call x4, Pallas kernels: 1.97 us -> 0.29 us  [sum_call(): pl.pallas_call(kernel, out_shape=[jax.ShapeDtypeStruct((size, chans), jnp...]
  transfers between devices with their start and end apart: 30 -> 30, of which waited for: 14 -> 12; matrix products, arithmetic and copies ran while one was open for 3% -> 3% of each run, Pallas kernels for 14% -> 12%
where the time goes in v10:
time: 86.2 us; the launch traced here: 86 us
  starting transfers between devices  40.8 us (47%)
  waiting for transfers between devices  22.8 us (26%)
  Pallas kernels  17.6 us (20%)
  local copies, waits for them, and re-layouts  3.63 us (4%)
  other arithmetic  0.96 us (1%)
    ppermute x28, starting transfers between devices, permute(): return lax.ppermute(block, BOTH, everywhere(sizes, target))  38.1 us
    ppermute x28, waiting for transfers between devices, permute(): return lax.ppermute(block, BOTH, everywhere(sizes, target))  17.3 us
    pallas_call x4, Pallas kernels, conv_call(): pl.pallas_call(functools.partial(conv_kernel, tuple(jobs), parts, group,...  11.4 us
    ppermute x2, waiting for transfers between devices, body(): back.append(lax.ppermute(done[p], BOTH, pairs))  5.44 us
    pallas_call x1, Pallas kernels, attend_call(): pl.pallas_call(functools.partial(attend_kernel, frames, share, chunks), o...  4.4 us
    ppermute x2, starting transfers between devices, body(): back.append(lax.ppermute(done[p], BOTH, pairs))  2.62 us
  transfers between devices with their start and end apart: 30, of which 12 were waited for; matrix products, arithmetic and copies ran while one was open for 3% of the time, Pallas kernels for 12%

profile of v10, /device:TPU:1, one launch (start us, length us, event | category | flops | bytes accessed | tf_op | source)
XLA Modules:
  0.0 86.0 jit_solution(16483524002372705265)
XLA Ops:
  0.0 0.1 collective-permute-start.1
  0.1 1.1 %constant_dynamic-slice_fusion = (bf16[2,4,64,128]{3,2,1,0:T(8,128)(2,1)S(1)}, bf16[2,4,64,128]{3,2,1,0:T(8,128)(2,1)S(1)}, bf16[2,4,64,128]{3,2,1,0:T(8,128)(2,1)S(1)}, bf16[2,4,64,128]{3,2,1,0:T(8,128)(2,1)S(1)}) fusion(bf16[2,4,64,512]{3,2,1,0:T(8,128)(2,1)} %param.6, s32[]{:T(128)S(6)} %select_n.75, s32[]{:T(128)S(6)} %select_n.74, s32[]{:T(128)S(6)} %select_n.72, ...), kind=kLoop, calls=%fused_computation.5 | loop fusion | bytes 1048592 | tf_op jit(solution)/shard_map/dynamic_slice | solution.py:383
  1.2 3.7 %collective-permute-start.6 = (bf16[2,4,64,128]{3,2,1,0:T(8,128)(2,1)S(1)}, bf16[2,4,64,128]{3,2,1,0:T(8,128)(2,1)S(1)}, u32[]{:S(2)}, u32[]{:S(2)}) collective-permute-start(bf16[2,4,64,128]{3,2,1,0:T(8,128)(2,1)S(1)} %get-tuple-element.57), channel_id=1, source_target_pairs={{0,24},{1,25},{2,26},{3,27},{4,28},{5,29},{6,30},{7,31},{8,16},{9,... | collective-permute-start | bytes 393224 | tf_op jit(solution)/shard_map/ppermute | solution.py:364
  4.9 0.2 collective-permute-start.3
  5.1 0.1 collective-permute-start
  5.3 1.0 %slice_bitcast_fusion = (bf16[2,64,512]{2,1,0:T(8,128)(2,1)S(1)}, bf16[2,64,512]{2,1,0:T(8,128)(2,1)S(1)}) fusion(bf16[2,4,64,512]{3,2,1,0:T(8,128)(2,1)} %param.6), kind=kLoop, calls=%fused_computation.3 | loop fusion | bytes 524288 | tf_op jit(solution)/shard_map/squeeze | solution.py:377
  6.2 1.3 %collective-permute-start.9 = (bf16[2,64,512]{2,1,0:T(8,128)(2,1)S(1)}, bf16[2,64,512]{2,1,0:T(8,128)(2,1)S(1)}, u32[]{:S(2)}, u32[]{:S(2)}) collective-permute-start(bf16[2,64,512]{2,1,0:T(8,128)(2,1)S(1)} %get-tuple-element.55), channel_id=1, source_target_pairs={{1,0},{2,1},{3,2},{5,4},{6,5},{7,6},{9,8},{10,9},{11,10},{13,12},{... | collective-permute-start | bytes 393224 | tf_op jit(solution)/shard_map/ppermute | solution.py:364
  7.5 0.1 pad_add_fusion.refs_0_.meta
  7.6 4.0 %collective-permute-start.8 = (bf16[2,64,512]{2,1,0:T(8,128)(2,1)S(1)}, bf16[2,64,512]{2,1,0:T(8,128)(2,1)S(1)}, u32[]{:S(2)}, u32[]{:S(2)}) collective-permute-start(bf16[2,64,512]{2,1,0:T(8,128)(2,1)S(1)} %get-tuple-element.56), channel_id=1, source_target_pairs={{0,1},{1,2},{2,3},{4,5},{5,6},{6,7},{8,9},{9,10},{10,11},{12,13},{... | collective-permute-start | bytes 393224 | tf_op jit(solution)/shard_map/ppermute | solution.py:364
  11.6 0.0 copy-start
  11.6 1.5 %copy-done = bf16[27,64,512]{2,1,0:T(8,128)(2,1)S(1)} copy-done((bf16[27,64,512]{2,1,0:T(8,128)(2,1)S(1)}, bf16[27,64,512]{2,1,0:T(8,128)(2,1)}, u32[]{:S(2)}) %copy-start) | copy-done | bytes 1769496
  13.1 0.9 merge_kernel_slices.1.refs_1_
  14.0 0.0 collective-permute-done.6.refs_3_
  14.0 1.2 %collective-permute-start.2 = (bf16[2,4,64,128]{3,2,1,0:T(8,128)(2,1)S(1)}, bf16[2,4,64,128]{3,2,1,0:T(8,128)(2,1)S(1)}, u32[]{:S(2)}, u32[]{:S(2)}) collective-permute-start(bf16[2,4,64,128]{3,2,1,0:T(8,128)(2,1)S(1)} %get-tuple-element.59.refs_2_), channel_id=1, source_target_pairs={{0,4},{1,5},{2,6},{3,7},{4,0},{5,1},{6,2},{7,3},{8,12},{9,13},{10,... | collective-permute-start | bytes 393224 | tf_op jit(solution)/shard_map/ppermute | solution.py:364
  15.2 0.1 collective-permute-start.7
  15.3 0.4 collective-permute-start.4
  15.7 0.1 collective-permute-start.5
  15.8 0.6 split_halo_rows.1
  16.4 0.1 collective-permute-done.7.refs_7_
  16.5 0.2 collective-permute-done.4.refs_5_
  16.7 0.3 collective-permute-done.5.refs_6_
  17.0 2.8 %conv_inner.2 = (bf16[256,512]{1,0:T(8,128)(2,1)S(1)}, bf16[256,512]{1,0:T(8,128)(2,1)S(1)}) custom-call(s32[3]{0:T(128)S(1)} %pad_add_fusion.refs_0_.meta, bf16[3,9,128,512]{3,2,1,0:T(8,128)(2,1)S(1)} %merge_kernel_slices.1.refs_1_, bf16[2,4,64,128]{3,2,1,0:T(8,128)(2,1)S(1)} %collective-permute-done.3.refs_2_, ...), custom_call_target="tpu_custom_call" | custom-call | flops 18119393280 | bytes 3538944 | tf_op jit(solution)/shard_map/conv_inner/pallas_call | solution.py:200
  19.9 1.7 %collective-permute-start.11 = (bf16[256,512]{1,0:T(8,128)(2,1)S(1)}, bf16[256,512]{1,0:T(8,128)(2,1)S(1)}, u32[]{:S(2)}, u32[]{:S(2)}) collective-permute-start(bf16[256,512]{1,0:T(8,128)(2,1)S(1)} %get-tuple-element.32.refs_8_), channel_id=1, source_target_pairs={{0,8},{1,9},{2,10},{3,11},{4,20},{5,21},{6,22},{7,23},{8,0},{9,1},... | collective-permute-start | bytes 786440 | tf_op jit(solution)/shard_map/ppermute | solution.py:364
  21.6 0.1 collective-permute-start.14
  21.7 1.4 %collective-permute-start.15 = (bf16[2,2,64,128]{3,2,1,0:T(8,128)(2,1)S(1)}, bf16[2,2,64,128]{3,2,1,0:T(8,128)(2,1)S(1)}, u32[]{:S(2)}, u32[]{:S(2)}) collective-permute-start(bf16[2,2,64,128]{3,2,1,0:T(8,128)(2,1)S(1)} %get-tuple-element.42), channel_id=1, source_target_pairs={{0,16},{1,17},{2,18},{3,19},{4,12},{5,13},{6,14},{7,15},{8,24},{9,... | collective-permute-start | bytes 196616 | tf_op jit(solution)/shard_map/ppermute | solution.py:364
  23.0 1.2 %collective-permute-start.16 = (bf16[2,2,64,128]{3,2,1,0:T(8,128)(2,1)S(1)}, bf16[2,2,64,128]{3,2,1,0:T(8,128)(2,1)S(1)}, u32[]{:S(2)}, u32[]{:S(2)}) collective-permute-start(bf16[2,2,64,128]{3,2,1,0:T(8,128)(2,1)S(1)} %get-tuple-element.43), channel_id=1, source_target_pairs={{0,24},{1,25},{2,26},{3,27},{4,28},{5,29},{6,30},{7,31},{8,16},{9,... | collective-permute-start | bytes 196616 | tf_op jit(solution)/shard_map/ppermute | solution.py:364
  24.2 0.1 collective-permute-start.10
  24.3 2.8 %conv_inner.3 = (f32[256,512]{1,0:T(8,128)S(1)}, f32[256,512]{1,0:T(8,128)S(1)}) custom-call(s32[3]{0:T(128)S(1)} %pad_add_fusion.refs_0_.meta, bf16[3,9,128,512]{3,2,1,0:T(8,128)(2,1)S(1)} %merge_kernel_slices.1.refs_1_, bf16[2,4,64,128]{3,2,1,0:T(8,128)(2,1)S(1)} %get-tuple-element.59.refs_2_, bf16[2,4,64,128]{3,2,1,0:T(8,128)(2,1)S(1)} %collective-permute-done.refs_3_, ...), custom_call_target="tpu_custom_call" | custom-call | flops 18119393280 | bytes 3538944 | tf_op jit(solution)/shard_map/conv_inner/pallas_call | solution.py:200
  27.2 0.1 collective-permute-done.14.refs_1_
  27.2 0.7 collective-permute-done.16.refs_3_
  28.0 2.9 %collective-permute-start.17 = (bf16[4,2,2,64,128]{4,3,2,1,0:T(8,128)(2,1)S(1)}, bf16[4,2,2,64,128]{4,3,2,1,0:T(8,128)(2,1)S(1)}, u32[]{:S(2)}, u32[]{:S(2)}) collective-permute-start(bf16[4,2,2,64,128]{4,3,2,1,0:T(8,128)(2,1)S(1)} %stack_halo_rows.1.refs_8_), channel_id=1, source_target_pairs={{0,4},{1,5},{2,6},{3,7},{4,0},{5,1},{6,2},{7,3},{8,12},{9,13},{10,... | collective-permute-start | bytes 786440 | tf_op jit(solution)/shard_map/ppermute | solution.py:364
  30.9 0.4 collective-permute-done.10.refs_2_.refs_1_
  31.3 0.1 sum_parts.4.refs_10_
  31.3 1.5 %collective-permute-start.12 = (bf16[256,512]{1,0:T(8,128)(2,1)S(1)}, bf16[256,512]{1,0:T(8,128)(2,1)S(1)}, u32[]{:S(2)}, u32[]{:S(2)}) collective-permute-start(bf16[256,512]{1,0:T(8,128)(2,1)S(1)} %sum_parts.4.refs_10_), channel_id=1, source_target_pairs={{0,16},{1,17},{2,18},{3,19},{4,12},{5,13},{6,14},{7,15},{8,24},{9,... | collective-permute-start | bytes 786440 | tf_op jit(solution)/shard_map/ppermute | solution.py:364
  32.8 2.9 %conv_rim.2 = (bf16[256,512]{1,0:T(8,128)(2,1)S(1)}, bf16[256,512]{1,0:T(8,128)(2,1)S(1)}) custom-call(s32[3]{0:T(128)S(1)} %pad_add_fusion.refs_0_.meta, bf16[3,9,128,512]{3,2,1,0:T(8,128)(2,1)S(1)} %merge_kernel_slices.1.refs_1_, bf16[2,4,64,128]{3,2,1,0:T(8,128)(2,1)S(1)} %collective-permute-done.3.refs_2_, ...), custom_call_target="tpu_custom_call" | custom-call | flops 18119393280 | bytes 3538944 | tf_op jit(solution)/shard_map/conv_rim/pallas_call | solution.py:200
  35.7 1.3 %collective-permute-start.18 = (bf16[256,512]{1,0:T(8,128)(2,1)S(1)}, bf16[256,512]{1,0:T(8,128)(2,1)S(1)}, u32[]{:S(2)}, u32[]{:S(2)}) collective-permute-start(bf16[256,512]{1,0:T(8,128)(2,1)S(1)} %get-tuple-element.46), channel_id=1, source_target_pairs={{0,8},{1,9},{2,10},{3,11},{4,20},{5,21},{6,22},{7,23},{8,0},{9,1},... | collective-permute-start | bytes 786440 | tf_op jit(solution)/shard_map/ppermute | solution.py:364
  37.0 0.2 collective-permute-start.19
  37.2 2.9 %conv_rim.3 = (f32[256,512]{1,0:T(8,128)S(1)}, f32[256,512]{1,0:T(8,128)S(1)}) custom-call(s32[3]{0:T(128)S(1)} %pad_add_fusion.refs_0_.meta, bf16[3,9,128,512]{3,2,1,0:T(8,128)(2,1)S(1)} %merge_kernel_slices.1.refs_1_, bf16[2,4,64,128]{3,2,1,0:T(8,128)(2,1)S(1)} %get-tuple-element.59.refs_2_, bf16[2,4,64,128]{3,2,1,0:T(8,128)(2,1)S(1)} %collective-permute-done.refs_3_, ...), custom_call_target="tpu_custom_call" | custom-call | flops 18119393280 | bytes 3538944 | tf_op jit(solution)/shard_map/conv_rim/pallas_call | solution.py:200
  40.1 0.0 copy-start.1
  40.1 0.0 copy-start.2
  40.1 0.0 copy-start.3
  40.1 0.0 copy-start.4
  40.1 1.1 %collective-permute-done.18.refs_2_.refs_1_ = bf16[256,512]{1,0:T(8,128)(2,1)S(1)} collective-permute-done((bf16[256,512]{1,0:T(8,128)(2,1)S(1)}, bf16[256,512]{1,0:T(8,128)(2,1)S(1)}, u32[]{:S(2)}, u32[]{:S(2)}) %collective-permute-start.18) | collective-permute-done | bytes 262176 | tf_op jit(solution)/shard_map/ppermute | solution.py:364
  41.3 2.8 %collective-permute-done.19.refs_1_ = bf16[256,512]{1,0:T(8,128)(2,1)S(1)} collective-permute-done((bf16[256,512]{1,0:T(8,128)(2,1)S(1)}, bf16[256,512]{1,0:T(8,128)(2,1)S(1)}, u32[]{:S(2)}, u32[]{:S(2)}) %collective-permute-start.19) | collective-permute-done | bytes 262176 | tf_op jit(solution)/shard_map/ppermute | solution.py:364
  44.1 0.1 sum_parts.6
  44.1 1.5 %collective-permute-start.20 = (bf16[256,512]{1,0:T(8,128)(2,1)S(1)}, bf16[256,512]{1,0:T(8,128)(2,1)S(1)}, u32[]{:S(2)}, u32[]{:S(2)}) collective-permute-start(bf16[256,512]{1,0:T(8,128)(2,1)S(1)} %sum_parts.6), channel_id=1, source_target_pairs={{0,16},{1,17},{2,18},{3,19},{4,12},{5,13},{6,14},{7,15},{8,24},{9,... | collective-permute-start | bytes 786440 | tf_op jit(solution)/shard_map/ppermute | solution.py:364
  45.6 0.1 sum_parts.5
  45.7 3.5 %collective-permute-start.24 = (bf16[128,512]{1,0:T(8,128)(2,1)S(1)}, bf16[128,512]{1,0:T(8,128)(2,1)S(1)}, u32[]{:S(2)}, u32[]{:S(2)}) collective-permute-start(bf16[128,512]{1,0:T(8,128)(2,1)S(1)} %get-tuple-element.36), channel_id=1, source_target_pairs={{0,2},{1,6},{2,0},{3,4},{4,3},{5,7},{6,1},{7,5},{8,10},{9,14},{10,... | collective-permute-start | bytes 393224 | tf_op jit(solution)/shard_map/ppermute | solution.py:364
  49.2 1.9 %collective-permute-start.13 = (bf16[128,512]{1,0:T(8,128)(2,1)S(1)}, bf16[128,512]{1,0:T(8,128)(2,1)S(1)}, u32[]{:S(2)}, u32[]{:S(2)}) collective-permute-start(bf16[128,512]{1,0:T(8,128)(2,1)S(1)} %get-tuple-element.36), channel_id=1, source_target_pairs={{0,0},{1,4},{2,2},{3,6},{4,1},{5,5},{6,3},{7,7},{8,8},{9,12},{10,1... | collective-permute-start | bytes 393224 | tf_op jit(solution)/shard_map/ppermute | solution.py:364
  51.1 0.1 collective-permute-start.25
  51.2 1.9 %collective-permute-start.22 = (bf16[128,512]{1,0:T(8,128)(2,1)S(1)}, bf16[128,512]{1,0:T(8,128)(2,1)S(1)}, u32[]{:S(2)}, u32[]{:S(2)}) collective-permute-start(bf16[128,512]{1,0:T(8,128)(2,1)S(1)} %get-tuple-element.49), channel_id=1, source_target_pairs={{0,4},{1,0},{2,6},{3,2},{4,5},{5,1},{6,7},{7,3},{8,12},{9,8},{10,1... | collective-permute-start | bytes 393224 | tf_op jit(solution)/shard_map/ppermute | solution.py:364
  53.2 0.1 sum_parts.7
  53.3 2.2 %collective-permute-start.26 = (bf16[128,512]{1,0:T(8,128)(2,1)S(1)}, bf16[128,512]{1,0:T(8,128)(2,1)S(1)}, u32[]{:S(2)}, u32[]{:S(2)}) collective-permute-start(bf16[128,512]{1,0:T(8,128)(2,1)S(1)} %get-tuple-element.48), channel_id=1, source_target_pairs={{0,2},{1,6},{2,0},{3,4},{4,3},{5,7},{6,1},{7,5},{8,10},{9,14},{10,... | collective-permute-start | bytes 393224 | tf_op jit(solution)/shard_map/ppermute | solution.py:364
  55.5 5.4 %collective-permute-start.21 = (bf16[128,512]{1,0:T(8,128)(2,1)S(1)}, bf16[128,512]{1,0:T(8,128)(2,1)S(1)}, u32[]{:S(2)}, u32[]{:S(2)}) collective-permute-start(bf16[128,512]{1,0:T(8,128)(2,1)S(1)} %get-tuple-element.48), channel_id=1, source_target_pairs={{0,0},{1,4},{2,2},{3,6},{4,1},{5,5},{6,3},{7,7},{8,8},{9,12},{10,1... | collective-permute-start | bytes 393224 | tf_op jit(solution)/shard_map/ppermute | solution.py:364
  60.9 0.1 collective-permute-start.27
  61.0 6.2 %collective-permute-done.25.refs_5_ = bf16[128,512]{1,0:T(8,128)(2,1)S(1)} collective-permute-done((bf16[128,512]{1,0:T(8,128)(2,1)S(1)}, bf16[128,512]{1,0:T(8,128)(2,1)S(1)}, u32[]{:S(2)}, u32[]{:S(2)}) %collective-permute-start.25) | collective-permute-done | bytes 131104 | tf_op jit(solution)/shard_map/ppermute | solution.py:364
  67.2 0.1 collective-permute-start.23
  67.2 5.3 %collective-permute-done.27.refs_7_ = bf16[128,512]{1,0:T(8,128)(2,1)S(1)} collective-permute-done((bf16[128,512]{1,0:T(8,128)(2,1)S(1)}, bf16[128,512]{1,0:T(8,128)(2,1)S(1)}, u32[]{:S(2)}, u32[]{:S(2)}) %collective-permute-start.27) | collective-permute-done | bytes 131104 | tf_op jit(solution)/shard_map/ppermute | solution.py:364
  72.6 4.4 %attend.1 = (bf16[4,64,512]{2,1,0:T(8,128)(2,1)S(1)}, bf16[4,64,512]{2,1,0:T(8,128)(2,1)S(1)}) custom-call(bf16[128,512]{1,0:T(8,128)(2,1)S(1)} %collective-permute-done.13.refs_0_, bf16[128,512]{1,0:T(8,128)(2,1)S(1)} %collective-permute-done.21.refs_1_, bf16[128,512]{1,0:T(8,128)(2,1)S(1)} %collective-permute-done.22.refs_2_, ...), custom_call_target="tpu_custom_call" | custom-call | flops 2684354560 | bytes 3145728 | tf_op jit(solution)/shard_map/attend/pallas_call | solution.py:335
  77.0 0.1 collective-permute-start.28
  77.1 2.6 %collective-permute-start.29 = (bf16[4,64,512]{2,1,0:T(8,128)(2,1)S(1)}, bf16[4,64,512]{2,1,0:T(8,128)(2,1)S(1)}, u32[]{:S(2)}, u32[]{:S(2)}) collective-permute-start(bf16[4,64,512]{2,1,0:T(8,128)(2,1)S(1)} %get-tuple-element.52), channel_id=1, source_target_pairs={{0,0},{4,1},{2,2},{6,3},{1,4},{5,5},{3,6},{7,7},{8,8},{12,9},{10,1... | collective-permute-start | bytes 786440 | tf_op jit(solution)/shard_map/ppermute | solution.py:458
  79.6 2.9 %collective-permute-done.28 = bf16[4,64,512]{2,1,0:T(8,128)(2,1)S(1)} collective-permute-done((bf16[4,64,512]{2,1,0:T(8,128)(2,1)S(1)}, bf16[4,64,512]{2,1,0:T(8,128)(2,1)S(1)}, u32[]{:S(2)}, u32[]{:S(2)}) %collective-permute-start.28) | collective-permute-done | bytes 262176 | tf_op jit(solution)/shard_map/ppermute | solution.py:458
  82.5 2.6 %collective-permute-done.29 = bf16[4,64,512]{2,1,0:T(8,128)(2,1)S(1)} collective-permute-done((bf16[4,64,512]{2,1,0:T(8,128)(2,1)S(1)}, bf16[4,64,512]{2,1,0:T(8,128)(2,1)S(1)}, u32[]{:S(2)}, u32[]{:S(2)}) %collective-permute-start.29) | collective-permute-done | bytes 262176 | tf_op jit(solution)/shard_map/ppermute | solution.py:458
  85.1 0.8 pad_maximum_fusion
  (23 shorter events, 0.1 us)
Async XLA Ops:
  0.0 7.6 %collective-permute-start.1 = (bf16[9,3,64,512]{3,2,1,0:T(8,128)(2,1)}, bf16[9,3,64,512]{3,2,1,0:T(8,128)(2,1)S(1)}, u32[]{:S(2)}, u32[]{:S(2)}) collective-permute-start(bf16[9,3,64,512]{3,2,1,0:T(8,128)(2,1)} %bitcast.16), channel_id=1, source_target_pairs={{0,4},{1,5},{2,6},{3,7},{4,0},{5,1},{6,2},{7,3},{8,12},{9,13},{10,... | collective-permute-start | bytes 5308424 | tf_op jit(solution)/shard_map/ppermute | solution.py:364
  1.2 12.7 %collective-permute-start.6 = (bf16[2,4,64,128]{3,2,1,0:T(8,128)(2,1)S(1)}, bf16[2,4,64,128]{3,2,1,0:T(8,128)(2,1)S(1)}, u32[]{:S(2)}, u32[]{:S(2)}) collective-permute-start(bf16[2,4,64,128]{3,2,1,0:T(8,128)(2,1)S(1)} %get-tuple-element.57), channel_id=1, source_target_pairs={{0,24},{1,25},{2,26},{3,27},{4,28},{5,29},{6,30},{7,31},{8,16},{9,... | collective-permute-start | bytes 393224 | tf_op jit(solution)/shard_map/ppermute | solution.py:364
  4.9 10.3 %collective-permute-start.3 = (bf16[2,4,64,128]{3,2,1,0:T(8,128)(2,1)S(1)}, bf16[2,4,64,128]{3,2,1,0:T(8,128)(2,1)S(1)}, u32[]{:S(2)}, u32[]{:S(2)}) collective-permute-start(bf16[2,4,64,128]{3,2,1,0:T(8,128)(2,1)S(1)} %get-tuple-element.58), channel_id=1, source_target_pairs={{0,8},{1,9},{2,10},{3,11},{4,20},{5,21},{6,22},{7,23},{8,0},{9,1},... | collective-permute-start | bytes 393224 | tf_op jit(solution)/shard_map/ppermute | solution.py:364
  5.1 10.1 %collective-permute-start = (bf16[2,4,64,128]{3,2,1,0:T(8,128)(2,1)S(1)}, bf16[2,4,64,128]{3,2,1,0:T(8,128)(2,1)S(1)}, u32[]{:S(2)}, u32[]{:S(2)}) collective-permute-start(bf16[2,4,64,128]{3,2,1,0:T(8,128)(2,1)S(1)} %get-tuple-element.60), channel_id=1, source_target_pairs={{0,16},{1,17},{2,18},{3,19},{4,12},{5,13},{6,14},{7,15},{8,24},{9,... | collective-permute-start | bytes 393224 | tf_op jit(solution)/shard_map/ppermute | solution.py:364
  6.2 9.4 %collective-permute-start.9 = (bf16[2,64,512]{2,1,0:T(8,128)(2,1)S(1)}, bf16[2,64,512]{2,1,0:T(8,128)(2,1)S(1)}, u32[]{:S(2)}, u32[]{:S(2)}) collective-permute-start(bf16[2,64,512]{2,1,0:T(8,128)(2,1)S(1)} %get-tuple-element.55), channel_id=1, source_target_pairs={{1,0},{2,1},{3,2},{5,4},{6,5},{7,6},{9,8},{10,9},{11,10},{13,12},{... | collective-permute-start | bytes 393224 | tf_op jit(solution)/shard_map/ppermute | solution.py:364
  7.6 8.1 %collective-permute-start.8 = (bf16[2,64,512]{2,1,0:T(8,128)(2,1)S(1)}, bf16[2,64,512]{2,1,0:T(8,128)(2,1)S(1)}, u32[]{:S(2)}, u32[]{:S(2)}) collective-permute-start(bf16[2,64,512]{2,1,0:T(8,128)(2,1)S(1)} %get-tuple-element.56), channel_id=1, source_target_pairs={{0,1},{1,2},{2,3},{4,5},{5,6},{6,7},{8,9},{9,10},{10,11},{12,13},{... | collective-permute-start | bytes 393224 | tf_op jit(solution)/shard_map/ppermute | solution.py:364
  11.6 1.5 %copy-start = (bf16[27,64,512]{2,1,0:T(8,128)(2,1)S(1)}, bf16[27,64,512]{2,1,0:T(8,128)(2,1)}, u32[]{:S(2)}) copy-start(bf16[27,64,512]{2,1,0:T(8,128)(2,1)} %param.7) | copy-start | bytes 5308420
  14.0 2.4 %collective-permute-start.2 = (bf16[2,4,64,128]{3,2,1,0:T(8,128)(2,1)S(1)}, bf16[2,4,64,128]{3,2,1,0:T(8,128)(2,1)S(1)}, u32[]{:S(2)}, u32[]{:S(2)}) collective-permute-start(bf16[2,4,64,128]{3,2,1,0:T(8,128)(2,1)S(1)} %get-tuple-element.59.refs_2_), channel_id=1, source_target_pairs={{0,4},{1,5},{2,6},{3,7},{4,0},{5,1},{6,2},{7,3},{8,12},{9,13},{10,... | collective-permute-start | bytes 393224 | tf_op jit(solution)/shard_map/ppermute | solution.py:364
  15.2 1.3 %collective-permute-start.7 = (bf16[2,4,64,128]{3,2,1,0:T(8,128)(2,1)S(1)}, bf16[2,4,64,128]{3,2,1,0:T(8,128)(2,1)S(1)}, u32[]{:S(2)}, u32[]{:S(2)}) collective-permute-start(bf16[2,4,64,128]{3,2,1,0:T(8,128)(2,1)S(1)} %collective-permute-done.6.refs_3_), channel_id=1, source_target_pairs={{0,4},{1,5},{2,6},{3,7},{4,0},{5,1},{6,2},{7,3},{8,12},{9,13},{10,... | collective-permute-start | bytes 393224 | tf_op jit(solution)/shard_map/ppermute | solution.py:364
  15.3 1.4 %collective-permute-start.4 = (bf16[2,4,64,128]{3,2,1,0:T(8,128)(2,1)S(1)}, bf16[2,4,64,128]{3,2,1,0:T(8,128)(2,1)S(1)}, u32[]{:S(2)}, u32[]{:S(2)}) collective-permute-start(bf16[2,4,64,128]{3,2,1,0:T(8,128)(2,1)S(1)} %collective-permute-done.3.refs_2_), channel_id=1, source_target_pairs={{0,4},{1,5},{2,6},{3,7},{4,0},{5,1},{6,2},{7,3},{8,12},{9,13},{10,... | collective-permute-start | bytes 393224 | tf_op jit(solution)/shard_map/ppermute | solution.py:364
  15.7 1.3 %collective-permute-start.5 = (bf16[2,4,64,128]{3,2,1,0:T(8,128)(2,1)S(1)}, bf16[2,4,64,128]{3,2,1,0:T(8,128)(2,1)S(1)}, u32[]{:S(2)}, u32[]{:S(2)}) collective-permute-start(bf16[2,4,64,128]{3,2,1,0:T(8,128)(2,1)S(1)} %collective-permute-done.refs_3_), channel_id=1, source_target_pairs={{0,4},{1,5},{2,6},{3,7},{4,0},{5,1},{6,2},{7,3},{8,12},{9,13},{10,... | collective-permute-start | bytes 393224 | tf_op jit(solution)/shard_map/ppermute | solution.py:364
  19.9 11.4 %collective-permute-start.11 = (bf16[256,512]{1,0:T(8,128)(2,1)S(1)}, bf16[256,512]{1,0:T(8,128)(2,1)S(1)}, u32[]{:S(2)}, u32[]{:S(2)}) collective-permute-start(bf16[256,512]{1,0:T(8,128)(2,1)S(1)} %get-tuple-element.32.refs_8_), channel_id=1, source_target_pairs={{0,8},{1,9},{2,10},{3,11},{4,20},{5,21},{6,22},{7,23},{8,0},{9,1},... | collective-permute-start | bytes 786440 | tf_op jit(solution)/shard_map/ppermute | solution.py:364
  21.6 5.6 %collective-permute-start.14 = (bf16[2,2,64,128]{3,2,1,0:T(8,128)(2,1)S(1)}, bf16[2,2,64,128]{3,2,1,0:T(8,128)(2,1)S(1)}, u32[]{:S(2)}, u32[]{:S(2)}) collective-permute-start(bf16[2,2,64,128]{3,2,1,0:T(8,128)(2,1)S(1)} %get-tuple-element.41), channel_id=1, source_target_pairs={{0,8},{1,9},{2,10},{3,11},{4,20},{5,21},{6,22},{7,23},{8,0},{9,1},... | collective-permute-start | bytes 196616 | tf_op jit(solution)/shard_map/ppermute | solution.py:364
  21.7 5.6 %collective-permute-start.15 = (bf16[2,2,64,128]{3,2,1,0:T(8,128)(2,1)S(1)}, bf16[2,2,64,128]{3,2,1,0:T(8,128)(2,1)S(1)}, u32[]{:S(2)}, u32[]{:S(2)}) collective-permute-start(bf16[2,2,64,128]{3,2,1,0:T(8,128)(2,1)S(1)} %get-tuple-element.42), channel_id=1, source_target_pairs={{0,16},{1,17},{2,18},{3,19},{4,12},{5,13},{6,14},{7,15},{8,24},{9,... | collective-permute-start | bytes 196616 | tf_op jit(solution)/shard_map/ppermute | solution.py:364
  23.0 4.9 %collective-permute-start.16 = (bf16[2,2,64,128]{3,2,1,0:T(8,128)(2,1)S(1)}, bf16[2,2,64,128]{3,2,1,0:T(8,128)(2,1)S(1)}, u32[]{:S(2)}, u32[]{:S(2)}) collective-permute-start(bf16[2,2,64,128]{3,2,1,0:T(8,128)(2,1)S(1)} %get-tuple-element.43), channel_id=1, source_target_pairs={{0,24},{1,25},{2,26},{3,27},{4,28},{5,29},{6,30},{7,31},{8,16},{9,... | collective-permute-start | bytes 196616 | tf_op jit(solution)/shard_map/ppermute | solution.py:364
  24.2 7.0 %collective-permute-start.10 = (bf16[256,512]{1,0:T(8,128)(2,1)S(1)}, bf16[256,512]{1,0:T(8,128)(2,1)S(1)}, u32[]{:S(2)}, u32[]{:S(2)}) collective-permute-start(bf16[256,512]{1,0:T(8,128)(2,1)S(1)} %get-tuple-element.34), channel_id=1, source_target_pairs={{0,8},{1,9},{2,10},{3,11},{4,20},{5,21},{6,22},{7,23},{8,0},{9,1},... | collective-permute-start | bytes 786440 | tf_op jit(solution)/shard_map/ppermute | solution.py:364
  28.0 4.8 %collective-permute-start.17 = (bf16[4,2,2,64,128]{4,3,2,1,0:T(8,128)(2,1)S(1)}, bf16[4,2,2,64,128]{4,3,2,1,0:T(8,128)(2,1)S(1)}, u32[]{:S(2)}, u32[]{:S(2)}) collective-permute-start(bf16[4,2,2,64,128]{4,3,2,1,0:T(8,128)(2,1)S(1)} %stack_halo_rows.1.refs_8_), channel_id=1, source_target_pairs={{0,4},{1,5},{2,6},{3,7},{4,0},{5,1},{6,2},{7,3},{8,12},{9,13},{10,... | collective-permute-start | bytes 786440 | tf_op jit(solution)/shard_map/ppermute | solution.py:364
  31.3 14.3 %collective-permute-start.12 = (bf16[256,512]{1,0:T(8,128)(2,1)S(1)}, bf16[256,512]{1,0:T(8,128)(2,1)S(1)}, u32[]{:S(2)}, u32[]{:S(2)}) collective-permute-start(bf16[256,512]{1,0:T(8,128)(2,1)S(1)} %sum_parts.4.refs_10_), channel_id=1, source_target_pairs={{0,16},{1,17},{2,18},{3,19},{4,12},{5,13},{6,14},{7,15},{8,24},{9,... | collective-permute-start | bytes 786440 | tf_op jit(solution)/shard_map/ppermute | solution.py:364
  35.7 5.6 %collective-permute-start.18 = (bf16[256,512]{1,0:T(8,128)(2,1)S(1)}, bf16[256,512]{1,0:T(8,128)(2,1)S(1)}, u32[]{:S(2)}, u32[]{:S(2)}) collective-permute-start(bf16[256,512]{1,0:T(8,128)(2,1)S(1)} %get-tuple-element.46), channel_id=1, source_target_pairs={{0,8},{1,9},{2,10},{3,11},{4,20},{5,21},{6,22},{7,23},{8,0},{9,1},... | collective-permute-start | bytes 786440 | tf_op jit(solution)/shard_map/ppermute | solution.py:364
  37.0 7.1 %collective-permute-start.19 = (bf16[256,512]{1,0:T(8,128)(2,1)S(1)}, bf16[256,512]{1,0:T(8,128)(2,1)S(1)}, u32[]{:S(2)}, u32[]{:S(2)}) collective-permute-start(bf16[256,512]{1,0:T(8,128)(2,1)S(1)} %get-tuple-element.44.refs_10_), channel_id=1, source_target_pairs={{0,8},{1,9},{2,10},{3,11},{4,20},{5,21},{6,22},{7,23},{8,0},{9,1},... | collective-permute-start | bytes 786440 | tf_op jit(solution)/shard_map/ppermute | solution.py:364
  40.1 32.5 %copy-start.1 = (bf16[512,512]{1,0:T(8,128)(2,1)S(1)}, bf16[512,512]{1,0:T(8,128)(2,1)}, u32[]{:S(2)}) copy-start(bf16[512,512]{1,0:T(8,128)(2,1)} %refs_8_.1) | copy-start | bytes 1572868
  40.1 32.5 %copy-start.2 = (bf16[512,512]{1,0:T(8,128)(2,1)S(1)}, bf16[512,512]{1,0:T(8,128)(2,1)}, u32[]{:S(2)}) copy-start(bf16[512,512]{1,0:T(8,128)(2,1)} %refs_9_.1) | copy-start | bytes 1572868
  40.1 32.5 %copy-start.3 = (bf16[512,512]{1,0:T(8,128)(2,1)S(1)}, bf16[512,512]{1,0:T(8,128)(2,1)}, u32[]{:S(2)}) copy-start(bf16[512,512]{1,0:T(8,128)(2,1)} %refs_10_.1) | copy-start | bytes 1572868
  40.1 32.5 %copy-start.4 = (bf16[512,512]{1,0:T(8,128)(2,1)S(1)}, bf16[512,512]{1,0:T(8,128)(2,1)}, u32[]{:S(2)}) copy-start(bf16[512,512]{1,0:T(8,128)(2,1)} %refs_11_.1) | copy-start | bytes 1572868
  44.1 9.0 %collective-permute-start.20 = (bf16[256,512]{1,0:T(8,128)(2,1)S(1)}, bf16[256,512]{1,0:T(8,128)(2,1)S(1)}, u32[]{:S(2)}, u32[]{:S(2)}) collective-permute-start(bf16[256,512]{1,0:T(8,128)(2,1)S(1)} %sum_parts.6), channel_id=1, source_target_pairs={{0,16},{1,17},{2,18},{3,19},{4,12},{5,13},{6,14},{7,15},{8,24},{9,... | collective-permute-start | bytes 786440 | tf_op jit(solution)/shard_map/ppermute | solution.py:364
  45.7 9.8 %collective-permute-start.24 = (bf16[128,512]{1,0:T(8,128)(2,1)S(1)}, bf16[128,512]{1,0:T(8,128)(2,1)S(1)}, u32[]{:S(2)}, u32[]{:S(2)}) collective-permute-start(bf16[128,512]{1,0:T(8,128)(2,1)S(1)} %get-tuple-element.36), channel_id=1, source_target_pairs={{0,2},{1,6},{2,0},{3,4},{4,3},{5,7},{6,1},{7,5},{8,10},{9,14},{10,... | collective-permute-start | bytes 393224 | tf_op jit(solution)/shard_map/ppermute | solution.py:364
  49.2 11.7 %collective-permute-start.13 = (bf16[128,512]{1,0:T(8,128)(2,1)S(1)}, bf16[128,512]{1,0:T(8,128)(2,1)S(1)}, u32[]{:S(2)}, u32[]{:S(2)}) collective-permute-start(bf16[128,512]{1,0:T(8,128)(2,1)S(1)} %get-tuple-element.36), channel_id=1, source_target_pairs={{0,0},{1,4},{2,2},{3,6},{4,1},{5,5},{6,3},{7,7},{8,8},{9,12},{10,1... | collective-permute-start | bytes 393224 | tf_op jit(solution)/shard_map/ppermute | solution.py:364
  51.1 16.0 %collective-permute-start.25 = (bf16[128,512]{1,0:T(8,128)(2,1)S(1)}, bf16[128,512]{1,0:T(8,128)(2,1)S(1)}, u32[]{:S(2)}, u32[]{:S(2)}) collective-permute-start(bf16[128,512]{1,0:T(8,128)(2,1)S(1)} %get-tuple-element.49), channel_id=1, source_target_pairs={{0,6},{1,2},{2,4},{3,0},{4,7},{5,3},{6,5},{7,1},{8,14},{9,10},{10,... | collective-permute-start | bytes 393224 | tf_op jit(solution)/shard_map/ppermute | solution.py:364
  51.2 16.0 %collective-permute-start.22 = (bf16[128,512]{1,0:T(8,128)(2,1)S(1)}, bf16[128,512]{1,0:T(8,128)(2,1)S(1)}, u32[]{:S(2)}, u32[]{:S(2)}) collective-permute-start(bf16[128,512]{1,0:T(8,128)(2,1)S(1)} %get-tuple-element.49), channel_id=1, source_target_pairs={{0,4},{1,0},{2,6},{3,2},{4,5},{5,1},{6,7},{7,3},{8,12},{9,8},{10,1... | collective-permute-start | bytes 393224 | tf_op jit(solution)/shard_map/ppermute | solution.py:364
  53.3 14.0 %collective-permute-start.26 = (bf16[128,512]{1,0:T(8,128)(2,1)S(1)}, bf16[128,512]{1,0:T(8,128)(2,1)S(1)}, u32[]{:S(2)}, u32[]{:S(2)}) collective-permute-start(bf16[128,512]{1,0:T(8,128)(2,1)S(1)} %get-tuple-element.48), channel_id=1, source_target_pairs={{0,2},{1,6},{2,0},{3,4},{4,3},{5,7},{6,1},{7,5},{8,10},{9,14},{10,... | collective-permute-start | bytes 393224 | tf_op jit(solution)/shard_map/ppermute | solution.py:364
  55.5 11.8 %collective-permute-start.21 = (bf16[128,512]{1,0:T(8,128)(2,1)S(1)}, bf16[128,512]{1,0:T(8,128)(2,1)S(1)}, u32[]{:S(2)}, u32[]{:S(2)}) collective-permute-start(bf16[128,512]{1,0:T(8,128)(2,1)S(1)} %get-tuple-element.48), channel_id=1, source_target_pairs={{0,0},{1,4},{2,2},{3,6},{4,1},{5,5},{6,3},{7,7},{8,8},{9,12},{10,1... | collective-permute-start | bytes 393224 | tf_op jit(solution)/shard_map/ppermute | solution.py:364
  60.9 11.7 %collective-permute-start.27 = (bf16[128,512]{1,0:T(8,128)(2,1)S(1)}, bf16[128,512]{1,0:T(8,128)(2,1)S(1)}, u32[]{:S(2)}, u32[]{:S(2)}) collective-permute-start(bf16[128,512]{1,0:T(8,128)(2,1)S(1)} %get-tuple-element.50), channel_id=1, source_target_pairs={{0,6},{1,2},{2,4},{3,0},{4,7},{5,3},{6,5},{7,1},{8,14},{9,10},{10,... | collective-permute-start | bytes 393224 | tf_op jit(solution)/shard_map/ppermute | solution.py:364
  67.2 5.4 %collective-permute-start.23 = (bf16[128,512]{1,0:T(8,128)(2,1)S(1)}, bf16[128,512]{1,0:T(8,128)(2,1)S(1)}, u32[]{:S(2)}, u32[]{:S(2)}) collective-permute-start(bf16[128,512]{1,0:T(8,128)(2,1)S(1)} %get-tuple-element.50), channel_id=1, source_target_pairs={{0,4},{1,0},{2,6},{3,2},{4,5},{5,1},{6,7},{7,3},{8,12},{9,8},{10,1... | collective-permute-start | bytes 393224 | tf_op jit(solution)/shard_map/ppermute | solution.py:364
  77.0 5.5 %collective-permute-start.28 = (bf16[4,64,512]{2,1,0:T(8,128)(2,1)S(1)}, bf16[4,64,512]{2,1,0:T(8,128)(2,1)S(1)}, u32[]{:S(2)}, u32[]{:S(2)}) collective-permute-start(bf16[4,64,512]{2,1,0:T(8,128)(2,1)S(1)} %get-tuple-element.51), channel_id=1, source_target_pairs={{4,0},{0,1},{6,2},{2,3},{5,4},{1,5},{7,6},{3,7},{12,8},{8,9},{14,1... | collective-permute-start | bytes 786440 | tf_op jit(solution)/shard_map/ppermute | solution.py:458
  77.1 8.0 %collective-permute-start.29 = (bf16[4,64,512]{2,1,0:T(8,128)(2,1)S(1)}, bf16[4,64,512]{2,1,0:T(8,128)(2,1)S(1)}, u32[]{:S(2)}, u32[]{:S(2)}) collective-permute-start(bf16[4,64,512]{2,1,0:T(8,128)(2,1)S(1)} %get-tuple-element.52), channel_id=1, source_target_pairs={{0,0},{4,1},{2,2},{6,3},{1,4},{5,5},{3,6},{7,7},{8,8},{12,9},{10,1... | collective-permute-start | bytes 786440 | tf_op jit(solution)/shard_map/ppermute | solution.py:458

commit v11 on v8

--- a/solution.py
+++ b/solution.py
@@ -94,7 +94,7 @@
     held, refs = refs[: len(dests)], refs[len(dests) :]
     before, refs = refs[:parts], refs[parts:]
     if any_rim:
-        (above, below), refs = refs[:2], refs[2:]
+        (above, below, above_before, below_before), refs = refs[:4], refs[4:]
     outs, raw = refs[-1 - len(jobs) : -1], refs[-1]
     part, member, z = meta[0], meta[1], meta[2]
     lags, _, width, chans = weights.shape
@@ -109,8 +109,8 @@
         if any_rim:
             raw[n, frames:, 0] = above[s]
             raw[n, frames:, 1 + rows_here] = below[s]
-            raw[n, :frames, 0] = above[parts + place]
-            raw[n, :frames, 1 + rows_here] = below[parts + place]
+            raw[n, :frames, 0] = above_before[place]
+            raw[n, :frames, 1 + rows_here] = below_before[place]
         for i in range(parts):
 
             @pl.when(place == i)
@@ -339,16 +339,17 @@
     def to_member(step):
         return lambda t, z: (t // group * group + (t + step) % group, z)
 
+    split = conv_weight.reshape(taps // 3, 3, chans_here, chans)
+    slices = [split] + [permute(split, to_member(step)) for step in range(1, group)]
+    weights = merge_call(meta, slices)
+
     held, before = [None] * parts, [None] * parts
     for s in reversed(range(parts)):
         piece = lax.dynamic_slice_in_dim(latents, (part ^ s) * width, width, axis=3)
         held[s] = permute(piece, to_part(s)) if s else piece
+    held[-1], weights = lax.optimization_barrier((held[-1], weights))
     for s in range(parts):
         before[s] = permute(held[s], to_member(1))
-
-    split = conv_weight.reshape(taps // 3, 3, chans_here, chans)
-    slices = [split] + [permute(split, to_member(step)) for step in range(1, group)]
-    weights = merge_call(meta, slices)
 
     away = list(reversed(range(1, parts)))
     conv = functools.partial(
@@ -358,18 +359,21 @@
     inner += conv(
         [(s, False) for s in away[1:]], halos=None, out_type=jnp.bfloat16, after=inner[:1]
     )
-    first, last = halo_call([*held, *before], inner[-1])
+    inner_got = [permute(x, to_part(s)) for s, x in zip(away, inner)]
+    first, last = halo_call(held, inner[-1])
     halos = (
         permute(last, lambda t, z: (t, z + 1) if z + 1 < depth else None),
         permute(first, lambda t, z: (t, z - 1) if z else None),
     )
-    inner_own = conv([(0, False)], halos=None, out_type=jnp.float32, after=(first,))
-    rim = conv([(s, True) for s in away], halos=halos, out_type=jnp.bfloat16, after=inner_own)
+    halos += tuple(permute(x, to_member(1)) for x in halos)
+    inner_own = conv([(0, False)], halos=None, out_type=jnp.float32, after=(first, *inner_got[:1]))
+    rim = conv([(s, True) for s in away], halos=halos, out_type=jnp.bfloat16, after=(*inner_own, *inner_got[:0]))
     rim_own = conv([(0, True)], halos=halos, out_type=jnp.float32, after=rim[-1:])
-    sums = []
-    for sent, own_part in ((inner, inner_own), (rim, rim_own)):
-        got = [permute(x, to_part(s)) for s, x in zip(away, sent)]
-        sums.append(sum_call([*own_part, *got], frames, after=rim_own))
+    rim_got = [permute(x, to_part(s)) for s, x in zip(away, rim)]
+    sums = [
+        sum_call([*own_part, *got], frames, after=rim_own)
+        for own_part, got in ((inner_own, inner_got), (rim_own, rim_got))
+    ]
 
     share = depth // frames
 

time: 85.5 us -> 86.7 us (1.014)
  starting transfers between devices: 35.5 us -> 36.6 us
    ppermute x24 -> x26, starting transfers between devices: 31.3 us -> 32.4 us  [permute(): return lax.ppermute(block, BOTH, everywhere(sizes, target))]
    ppermute x24 -> x26, waiting for transfers between devices: 17.6 us -> 17.8 us  [permute(): return lax.ppermute(block, BOTH, everywhere(sizes, target))]
  transfers between devices with their start and end apart: 26 -> 28, of which waited for: 10 -> 10; matrix products, arithmetic and copies ran while one was open for 1% -> 1% of each run, Pallas kernels for 13% -> 13%
where the time goes in v11:
time: 86.7 us; the launch traced here: 86.5 us
  starting transfers between devices  36.6 us (42%)
  waiting for transfers between devices  28.4 us (33%)
  Pallas kernels  17.6 us (20%)
  local copies, waits for them, and re-layouts  2.65 us (3%)
  other arithmetic  0.96 us (1%)
    ppermute x26, starting transfers between devices, permute(): return lax.ppermute(block, BOTH, everywhere(sizes, target))  32.4 us
    ppermute x26, waiting for transfers between devices, permute(): return lax.ppermute(block, BOTH, everywhere(sizes, target))  17.8 us
    pallas_call x5, Pallas kernels, conv_call(): pl.pallas_call(functools.partial(conv_kernel, tuple(jobs), parts, frames)...  12.1 us
    ppermute x2, waiting for transfers between devices, body(): back.append(lax.ppermute(done[p], BOTH, pairs))  10.6 us
    pallas_call x1, Pallas kernels, attend_call(): pl.pallas_call(functools.partial(attend_kernel, frames, share, chunks), o...  4.41 us
    ppermute x2, starting transfers between devices, body(): back.append(lax.ppermute(done[p], BOTH, pairs))  4.18 us
  transfers between devices with their start and end apart: 28, of which 10 were waited for; matrix products, arithmetic and copies ran while one was open for 1% of the time, Pallas kernels for 13%

profile of v11, /device:TPU:1, one launch (start us, length us, event | category | flops | bytes accessed | tf_op | source)
XLA Modules:
  0.0 86.5 jit_solution(14859347575839918946)
XLA Ops:
  0.0 0.1 collective-permute-start.1
  0.1 1.1 %constant_dynamic-slice_fusion = (bf16[2,4,64,128]{3,2,1,0:T(8,128)(2,1)S(1)}, bf16[2,4,64,128]{3,2,1,0:T(8,128)(2,1)S(1)}, bf16[2,4,64,128]{3,2,1,0:T(8,128)(2,1)S(1)}, bf16[2,4,64,128]{3,2,1,0:T(8,128)(2,1)S(1)}) fusion(bf16[2,4,64,512]{3,2,1,0:T(8,128)(2,1)} %param.6, s32[]{:T(128)S(6)} %select_n.50, s32[]{:T(128)S(6)} %select_n.48, s32[]{:T(128)S(6)} %select_n.47, ...), kind=kLoop, calls=%fused_computation.3 | loop fusion | bytes 1048592 | tf_op jit(solution)/shard_map/dynamic_slice | solution.py:348
  1.2 2.7 %collective-permute-start.3 = (bf16[2,4,64,128]{3,2,1,0:T(8,128)(2,1)S(1)}, bf16[2,4,64,128]{3,2,1,0:T(8,128)(2,1)S(1)}, u32[]{:S(2)}, u32[]{:S(2)}) collective-permute-start(bf16[2,4,64,128]{3,2,1,0:T(8,128)(2,1)S(1)} %get-tuple-element.40), channel_id=1, source_target_pairs={{0,8},{1,9},{2,10},{3,11},{4,12},{5,13},{6,14},{7,15},{8,0},{9,1},... | collective-permute-start | bytes 393224 | tf_op jit(solution)/shard_map/ppermute | solution.py:334
  3.9 1.2 %collective-permute-start.5 = (bf16[2,4,64,128]{3,2,1,0:T(8,128)(2,1)S(1)}, bf16[2,4,64,128]{3,2,1,0:T(8,128)(2,1)S(1)}, u32[]{:S(2)}, u32[]{:S(2)}) collective-permute-start(bf16[2,4,64,128]{3,2,1,0:T(8,128)(2,1)S(1)} %get-tuple-element.37), channel_id=1, source_target_pairs={{0,16},{1,17},{2,18},{3,19},{4,20},{5,21},{6,22},{7,23},{8,24},{9,... | collective-permute-start | bytes 393224 | tf_op jit(solution)/shard_map/ppermute | solution.py:334
  5.2 0.0 collective-permute-start
  5.2 0.6 collective-permute-start.2
  5.8 0.1 pad_add_fusion.refs_0_
  5.8 2.0 %collective-permute-done.3.refs_2_.refs_1_ = bf16[2,4,64,128]{3,2,1,0:T(8,128)(2,1)S(1)} collective-permute-done((bf16[2,4,64,128]{3,2,1,0:T(8,128)(2,1)S(1)}, bf16[2,4,64,128]{3,2,1,0:T(8,128)(2,1)S(1)}, u32[]{:S(2)}, u32[]{:S(2)}) %collective-permute-start.3) | collective-permute-done | bytes 131104 | tf_op jit(solution)/shard_map/ppermute | solution.py:334
  7.8 0.7 collective-permute-start.4
  8.5 2.0 %collective-permute-done.5.refs_3_.refs_2_ = bf16[2,4,64,128]{3,2,1,0:T(8,128)(2,1)S(1)} collective-permute-done((bf16[2,4,64,128]{3,2,1,0:T(8,128)(2,1)S(1)}, bf16[2,4,64,128]{3,2,1,0:T(8,128)(2,1)S(1)}, u32[]{:S(2)}, u32[]{:S(2)}) %collective-permute-start.5) | collective-permute-done | bytes 131104 | tf_op jit(solution)/shard_map/ppermute | solution.py:334
  10.5 2.2 %collective-permute-start.6 = (bf16[2,4,64,128]{3,2,1,0:T(8,128)(2,1)S(1)}, bf16[2,4,64,128]{3,2,1,0:T(8,128)(2,1)S(1)}, u32[]{:S(2)}, u32[]{:S(2)}) collective-permute-start(bf16[2,4,64,128]{3,2,1,0:T(8,128)(2,1)S(1)} %collective-permute-done.5.refs_3_.refs_2_), channel_id=1, source_target_pairs={{0,4},{1,5},{2,6},{3,7},{4,0},{5,1},{6,2},{7,3},{8,12},{9,13},{10,... | collective-permute-start | bytes 393224 | tf_op jit(solution)/shard_map/ppermute | solution.py:334
  12.7 0.0 collective-permute-done.1.refs_2_
  12.7 1.5 %copy-done = bf16[27,64,512]{2,1,0:T(8,128)(2,1)S(1)} copy-done((bf16[27,64,512]{2,1,0:T(8,128)(2,1)S(1)}, bf16[27,64,512]{2,1,0:T(8,128)(2,1)}, u32[]{:S(2)}) %copy-start) | copy-done | bytes 1769496
  14.1 0.9 merge_kernel_slices.1.refs_1_
  15.0 0.1 collective-permute-start.7
  15.1 0.0 collective-permute-done.6.refs_5_.refs_6_.refs_7_
  15.1 1.3 %collective-permute-done.7.refs_6_.refs_7_.refs_8_ = bf16[2,4,64,128]{3,2,1,0:T(8,128)(2,1)S(1)} collective-permute-done((bf16[2,4,64,128]{3,2,1,0:T(8,128)(2,1)S(1)}, bf16[2,4,64,128]{3,2,1,0:T(8,128)(2,1)S(1)}, u32[]{:S(2)}, u32[]{:S(2)}) %collective-permute-start.7) | collective-permute-done | bytes 131104 | tf_op jit(solution)/shard_map/ppermute | solution.py:334
  16.4 1.8 %conv_inner.3.refs_8_ = bf16[256,512]{1,0:T(8,128)(2,1)S(1)} custom-call(s32[3]{0:T(128)S(1)} %pad_add_fusion.refs_0_, bf16[3,9,128,512]{3,2,1,0:T(8,128)(2,1)S(1)} %merge_kernel_slices.1.refs_1_, bf16[2,4,64,128]{3,2,1,0:T(8,128)(2,1)S(1)} %collective-permute-done.refs_2_.refs_3_.refs_4_, ...), custom_call_target="tpu_custom_call" | custom-call | flops 9059696640 | bytes 3538944 | tf_op jit(solution)/shard_map/conv_inner/pallas_call | solution.py:170
  18.2 1.3 %collective-permute-start.8 = (bf16[256,512]{1,0:T(8,128)(2,1)S(1)}, bf16[256,512]{1,0:T(8,128)(2,1)S(1)}, u32[]{:S(2)}, u32[]{:S(2)}) collective-permute-start(bf16[256,512]{1,0:T(8,128)(2,1)S(1)} %conv_inner.3.refs_8_), channel_id=1, source_target_pairs={{0,24},{1,25},{2,26},{3,27},{4,28},{5,29},{6,30},{7,31},{8,16},{9,... | collective-permute-start | bytes 786440 | tf_op jit(solution)/shard_map/ppermute | solution.py:334
  19.5 2.8 %conv_inner.4 = (bf16[256,512]{1,0:T(8,128)(2,1)S(1)}, bf16[256,512]{1,0:T(8,128)(2,1)S(1)}) custom-call(s32[3]{0:T(128)S(1)} %pad_add_fusion.refs_0_, bf16[3,9,128,512]{3,2,1,0:T(8,128)(2,1)S(1)} %merge_kernel_slices.1.refs_1_, bf16[2,4,64,128]{3,2,1,0:T(8,128)(2,1)S(1)} %collective-permute-done.3.refs_2_.refs_1_, ...), custom_call_target="tpu_custom_call" | custom-call | flops 18119393280 | bytes 3538944 | tf_op jit(solution)/shard_map/conv_inner/pallas_call | solution.py:170
  22.4 3.2 %collective-permute-start.11 = (bf16[4,2,64,128]{3,2,1,0:T(8,128)(2,1)S(1)}, bf16[4,2,64,128]{3,2,1,0:T(8,128)(2,1)S(1)}, u32[]{:S(2)}, u32[]{:S(2)}) collective-permute-start(bf16[4,2,64,128]{3,2,1,0:T(8,128)(2,1)S(1)} %get-tuple-element.25), channel_id=1, source_target_pairs={{0,1},{1,2},{2,3},{4,5},{5,6},{6,7},{8,9},{9,10},{10,11},{12,13},{... | collective-permute-start | bytes 393224 | tf_op jit(solution)/shard_map/ppermute | solution.py:334
  25.6 1.3 %collective-permute-start.12 = (bf16[4,2,64,128]{3,2,1,0:T(8,128)(2,1)S(1)}, bf16[4,2,64,128]{3,2,1,0:T(8,128)(2,1)S(1)}, u32[]{:S(2)}, u32[]{:S(2)}) collective-permute-start(bf16[4,2,64,128]{3,2,1,0:T(8,128)(2,1)S(1)} %get-tuple-element.23.refs_7_), channel_id=1, source_target_pairs={{1,0},{2,1},{3,2},{5,4},{6,5},{7,6},{9,8},{10,9},{11,10},{13,12},{... | collective-permute-start | bytes 393224 | tf_op jit(solution)/shard_map/ppermute | solution.py:334
  26.9 1.3 %collective-permute-start.10 = (bf16[256,512]{1,0:T(8,128)(2,1)S(1)}, bf16[256,512]{1,0:T(8,128)(2,1)S(1)}, u32[]{:S(2)}, u32[]{:S(2)}) collective-permute-start(bf16[256,512]{1,0:T(8,128)(2,1)S(1)} %get-tuple-element.22.refs_4_), channel_id=1, source_target_pairs={{0,8},{1,9},{2,10},{3,11},{4,12},{5,13},{6,14},{7,15},{8,0},{9,1},... | collective-permute-start | bytes 786440 | tf_op jit(solution)/shard_map/ppermute | solution.py:334
  28.2 0.2 collective-permute-start.9
  28.4 0.0 collective-permute-done.11.refs_9_.refs_7_
  28.4 1.3 %collective-permute-start.13 = (bf16[4,2,64,128]{3,2,1,0:T(8,128)(2,1)S(1)}, bf16[4,2,64,128]{3,2,1,0:T(8,128)(2,1)S(1)}, u32[]{:S(2)}, u32[]{:S(2)}) collective-permute-start(bf16[4,2,64,128]{3,2,1,0:T(8,128)(2,1)S(1)} %collective-permute-done.11.refs_9_.refs_7_), channel_id=1, source_target_pairs={{0,4},{1,5},{2,6},{3,7},{4,0},{5,1},{6,2},{7,3},{8,12},{9,13},{10,... | collective-permute-start | bytes 393224 | tf_op jit(solution)/shard_map/ppermute | solution.py:334
  29.7 2.1 %collective-permute-done.12.refs_10_.refs_8_ = bf16[4,2,64,128]{3,2,1,0:T(8,128)(2,1)S(1)} collective-permute-done((bf16[4,2,64,128]{3,2,1,0:T(8,128)(2,1)S(1)}, bf16[4,2,64,128]{3,2,1,0:T(8,128)(2,1)S(1)}, u32[]{:S(2)}, u32[]{:S(2)}) %collective-permute-start.12) | collective-permute-done | bytes 131104 | tf_op jit(solution)/shard_map/ppermute | solution.py:334
  31.8 1.6 %collective-permute-start.14 = (bf16[4,2,64,128]{3,2,1,0:T(8,128)(2,1)S(1)}, bf16[4,2,64,128]{3,2,1,0:T(8,128)(2,1)S(1)}, u32[]{:S(2)}, u32[]{:S(2)}) collective-permute-start(bf16[4,2,64,128]{3,2,1,0:T(8,128)(2,1)S(1)} %collective-permute-done.12.refs_10_.refs_8_), channel_id=1, source_target_pairs={{0,4},{1,5},{2,6},{3,7},{4,0},{5,1},{6,2},{7,3},{8,12},{9,13},{10,... | collective-permute-start | bytes 393224 | tf_op jit(solution)/shard_map/ppermute | solution.py:334
  33.4 1.8 %conv_inner.5.refs_13_.refs_0_ = f32[256,512]{1,0:T(8,128)S(1)} custom-call(s32[3]{0:T(128)S(1)} %pad_add_fusion.refs_0_, bf16[3,9,128,512]{3,2,1,0:T(8,128)(2,1)S(1)} %merge_kernel_slices.1.refs_1_, bf16[2,4,64,128]{3,2,1,0:T(8,128)(2,1)S(1)} %get-tuple-element.38.refs_0_.refs_2_, ...), custom_call_target="tpu_custom_call" | custom-call | flops 9059696640 | bytes 3538944 | tf_op jit(solution)/shard_map/conv_inner/pallas_call | solution.py:170
  35.2 0.0 collective-permute-done.14.refs_12_.refs_10_
  35.2 3.9 %conv_rim.2 = (bf16[256,512]{1,0:T(8,128)(2,1)S(1)}, bf16[256,512]{1,0:T(8,128)(2,1)S(1)}, bf16[256,512]{1,0:T(8,128)(2,1)S(1)}) custom-call(s32[3]{0:T(128)S(1)} %pad_add_fusion.refs_0_, bf16[3,9,128,512]{3,2,1,0:T(8,128)(2,1)S(1)} %merge_kernel_slices.1.refs_1_, bf16[2,4,64,128]{3,2,1,0:T(8,128)(2,1)S(1)} %collective-permute-done.3.refs_2_.refs_1_, ...), custom_call_target="tpu_custom_call" | custom-call | flops 27179089920 | bytes 3538944 | tf_op jit(solution)/shard_map/conv_rim/pallas_call | solution.py:170
  39.1 1.2 %collective-permute-start.16 = (bf16[256,512]{1,0:T(8,128)(2,1)S(1)}, bf16[256,512]{1,0:T(8,128)(2,1)S(1)}, u32[]{:S(2)}, u32[]{:S(2)}) collective-permute-start(bf16[256,512]{1,0:T(8,128)(2,1)S(1)} %get-tuple-element.28), channel_id=1, source_target_pairs={{0,24},{1,25},{2,26},{3,27},{4,28},{5,29},{6,30},{7,31},{8,16},{9,... | collective-permute-start | bytes 786440 | tf_op jit(solution)/shard_map/ppermute | solution.py:334
  40.3 1.2 %collective-permute-start.17 = (bf16[256,512]{1,0:T(8,128)(2,1)S(1)}, bf16[256,512]{1,0:T(8,128)(2,1)S(1)}, u32[]{:S(2)}, u32[]{:S(2)}) collective-permute-start(bf16[256,512]{1,0:T(8,128)(2,1)S(1)} %get-tuple-element.29), channel_id=1, source_target_pairs={{0,16},{1,17},{2,18},{3,19},{4,20},{5,21},{6,22},{7,23},{8,24},{9,... | collective-permute-start | bytes 786440 | tf_op jit(solution)/shard_map/ppermute | solution.py:334
  41.6 0.2 collective-permute-start.18
  41.8 1.8 %conv_rim.3.refs_4_.refs_0_ = f32[256,512]{1,0:T(8,128)S(1)} custom-call(s32[3]{0:T(128)S(1)} %pad_add_fusion.refs_0_, bf16[3,9,128,512]{3,2,1,0:T(8,128)(2,1)S(1)} %merge_kernel_slices.1.refs_1_, bf16[2,4,64,128]{3,2,1,0:T(8,128)(2,1)S(1)} %get-tuple-element.38.refs_0_.refs_2_, bf16[2,4,64,128]{3,2,1,0:T(8,128)(2,1)S(1)} %collective-permute-done.2.refs_3_.refs_4_.refs_5_, ...), custom_call_target="tpu_custom_call" | custom-call | flops 9059696640 | bytes 3538944 | tf_op jit(solution)/shard_map/conv_rim/pallas_call | solution.py:170
  43.6 0.0 copy-start.1
  43.7 0.0 copy-start.2
  43.7 0.0 copy-start.3
  43.7 0.0 copy-start.4
  43.7 0.0 collective-permute-done.9.refs_2_
  43.7 0.0 collective-permute-done.10.refs_3_
  43.7 0.1 sum_parts.2
  43.9 5.1 %collective-permute-start.15 = (bf16[128,512]{1,0:T(8,128)(2,1)S(1)}, bf16[128,512]{1,0:T(8,128)(2,1)S(1)}, u32[]{:S(2)}, u32[]{:S(2)}) collective-permute-start(bf16[128,512]{1,0:T(8,128)(2,1)S(1)} %get-tuple-element.27), channel_id=1, source_target_pairs={{0,0},{1,1},{2,4},{3,5},{4,2},{5,3},{6,6},{7,7},{8,8},{9,9},{10,12... | collective-permute-start | bytes 393224 | tf_op jit(solution)/shard_map/ppermute | solution.py:334
  49.0 0.6 collective-permute-start.20
  49.6 0.0 collective-permute-done.16.refs_1_
  49.6 4.3 %collective-permute-done.17.refs_2_ = bf16[256,512]{1,0:T(8,128)(2,1)S(1)} collective-permute-done((bf16[256,512]{1,0:T(8,128)(2,1)S(1)}, bf16[256,512]{1,0:T(8,128)(2,1)S(1)}, u32[]{:S(2)}, u32[]{:S(2)}) %collective-permute-start.17) | collective-permute-done | bytes 262176 | tf_op jit(solution)/shard_map/ppermute | solution.py:334
  54.0 0.0 collective-permute-done.18.refs_3_
  54.0 0.1 sum_parts.3
  54.1 4.6 %collective-permute-start.19 = (bf16[128,512]{1,0:T(8,128)(2,1)S(1)}, bf16[128,512]{1,0:T(8,128)(2,1)S(1)}, u32[]{:S(2)}, u32[]{:S(2)}) collective-permute-start(bf16[128,512]{1,0:T(8,128)(2,1)S(1)} %get-tuple-element.30), channel_id=1, source_target_pairs={{0,0},{1,1},{2,4},{3,5},{4,2},{5,3},{6,6},{7,7},{8,8},{9,9},{10,12... | collective-permute-start | bytes 393224 | tf_op jit(solution)/shard_map/ppermute | solution.py:334
  58.7 1.1 %collective-permute-start.21 = (bf16[128,512]{1,0:T(8,128)(2,1)S(1)}, bf16[128,512]{1,0:T(8,128)(2,1)S(1)}, u32[]{:S(2)}, u32[]{:S(2)}) collective-permute-start(bf16[128,512]{1,0:T(8,128)(2,1)S(1)} %get-tuple-element.32), channel_id=1, source_target_pairs={{0,1},{1,0},{2,5},{3,4},{4,3},{5,2},{6,7},{7,6},{8,9},{9,8},{10,13... | collective-permute-start | bytes 393224 | tf_op jit(solution)/shard_map/ppermute | solution.py:334
  59.7 0.0 collective-permute-done.15.refs_0_
  59.7 0.5 collective-permute-start.24
  60.2 2.5 %collective-permute-done.19.refs_1_ = bf16[128,512]{1,0:T(8,128)(2,1)S(1)} collective-permute-done((bf16[128,512]{1,0:T(8,128)(2,1)S(1)}, bf16[128,512]{1,0:T(8,128)(2,1)S(1)}, u32[]{:S(2)}, u32[]{:S(2)}) %collective-permute-start.19) | collective-permute-done | bytes 131104 | tf_op jit(solution)/shard_map/ppermute | solution.py:334
  62.7 0.0 collective-permute-start.23
  62.7 2.3 %collective-permute-done.21.refs_3_ = bf16[128,512]{1,0:T(8,128)(2,1)S(1)} collective-permute-done((bf16[128,512]{1,0:T(8,128)(2,1)S(1)}, bf16[128,512]{1,0:T(8,128)(2,1)S(1)}, u32[]{:S(2)}, u32[]{:S(2)}) %collective-permute-start.21) | collective-permute-done | bytes 131104 | tf_op jit(solution)/shard_map/ppermute | solution.py:334
  65.0 0.0 collective-permute-done.22.refs_4_
  65.0 0.0 collective-permute-done.24.refs_6_
  65.0 1.3 %collective-permute-done.25.refs_7_ = bf16[128,512]{1,0:T(8,128)(2,1)S(1)} collective-permute-done((bf16[128,512]{1,0:T(8,128)(2,1)S(1)}, bf16[128,512]{1,0:T(8,128)(2,1)S(1)}, u32[]{:S(2)}, u32[]{:S(2)}) %collective-permute-start.25) | collective-permute-done | bytes 131104 | tf_op jit(solution)/shard_map/ppermute | solution.py:334
  66.4 4.4 %attend.1 = (bf16[4,64,512]{2,1,0:T(8,128)(2,1)S(1)}, bf16[4,64,512]{2,1,0:T(8,128)(2,1)S(1)}) custom-call(bf16[128,512]{1,0:T(8,128)(2,1)S(1)} %collective-permute-done.15.refs_0_, bf16[128,512]{1,0:T(8,128)(2,1)S(1)} %collective-permute-done.19.refs_1_, bf16[128,512]{1,0:T(8,128)(2,1)S(1)} %collective-permute-done.20.refs_2_, ...), custom_call_target="tpu_custom_call" | custom-call | flops 2684354560 | bytes 3145728 | tf_op jit(solution)/shard_map/attend/pallas_call | solution.py:305
  70.8 1.4 %collective-permute-start.26 = (bf16[4,64,512]{2,1,0:T(8,128)(2,1)S(1)}, bf16[4,64,512]{2,1,0:T(8,128)(2,1)S(1)}, u32[]{:S(2)}, u32[]{:S(2)}) collective-permute-start(bf16[4,64,512]{2,1,0:T(8,128)(2,1)S(1)} %get-tuple-element.33), channel_id=1, source_target_pairs={{1,0},{0,1},{5,2},{4,3},{3,4},{2,5},{7,6},{6,7},{9,8},{8,9},{13,10... | collective-permute-start | bytes 786440 | tf_op jit(solution)/shard_map/ppermute | solution.py:409
  72.2 2.8 %collective-permute-start.27 = (bf16[4,64,512]{2,1,0:T(8,128)(2,1)S(1)}, bf16[4,64,512]{2,1,0:T(8,128)(2,1)S(1)}, u32[]{:S(2)}, u32[]{:S(2)}) collective-permute-start(bf16[4,64,512]{2,1,0:T(8,128)(2,1)S(1)} %get-tuple-element.34), channel_id=1, source_target_pairs={{0,0},{1,1},{4,2},{5,3},{2,4},{3,5},{6,6},{7,7},{8,8},{9,9},{12,10... | collective-permute-start | bytes 786440 | tf_op jit(solution)/shard_map/ppermute | solution.py:409
  75.0 4.6 %collective-permute-done.26 = bf16[4,64,512]{2,1,0:T(8,128)(2,1)S(1)} collective-permute-done((bf16[4,64,512]{2,1,0:T(8,128)(2,1)S(1)}, bf16[4,64,512]{2,1,0:T(8,128)(2,1)S(1)}, u32[]{:S(2)}, u32[]{:S(2)}) %collective-permute-start.26) | collective-permute-done | bytes 262176 | tf_op jit(solution)/shard_map/ppermute | solution.py:409
  79.7 5.9 %collective-permute-done.27 = bf16[4,64,512]{2,1,0:T(8,128)(2,1)S(1)} collective-permute-done((bf16[4,64,512]{2,1,0:T(8,128)(2,1)S(1)}, bf16[4,64,512]{2,1,0:T(8,128)(2,1)S(1)}, u32[]{:S(2)}, u32[]{:S(2)}) %collective-permute-start.27) | collective-permute-done | bytes 262176 | tf_op jit(solution)/shard_map/ppermute | solution.py:409
  85.6 0.8 pad_maximum_fusion
  (16 shorter events, 0.1 us)
Async XLA Ops:
  0.0 12.7 %collective-permute-start.1 = (bf16[9,3,64,512]{3,2,1,0:T(8,128)(2,1)}, bf16[9,3,64,512]{3,2,1,0:T(8,128)(2,1)S(1)}, u32[]{:S(2)}, u32[]{:S(2)}) collective-permute-start(bf16[9,3,64,512]{3,2,1,0:T(8,128)(2,1)} %bitcast.8), channel_id=1, source_target_pairs={{0,4},{1,5},{2,6},{3,7},{4,0},{5,1},{6,2},{7,3},{8,12},{9,13},{10,... | collective-permute-start | bytes 5308424 | tf_op jit(solution)/shard_map/ppermute | solution.py:334
  1.2 6.6 %collective-permute-start.3 = (bf16[2,4,64,128]{3,2,1,0:T(8,128)(2,1)S(1)}, bf16[2,4,64,128]{3,2,1,0:T(8,128)(2,1)S(1)}, u32[]{:S(2)}, u32[]{:S(2)}) collective-permute-start(bf16[2,4,64,128]{3,2,1,0:T(8,128)(2,1)S(1)} %get-tuple-element.40), channel_id=1, source_target_pairs={{0,8},{1,9},{2,10},{3,11},{4,12},{5,13},{6,14},{7,15},{8,0},{9,1},... | collective-permute-start | bytes 393224 | tf_op jit(solution)/shard_map/ppermute | solution.py:334
  3.9 6.5 %collective-permute-start.5 = (bf16[2,4,64,128]{3,2,1,0:T(8,128)(2,1)S(1)}, bf16[2,4,64,128]{3,2,1,0:T(8,128)(2,1)S(1)}, u32[]{:S(2)}, u32[]{:S(2)}) collective-permute-start(bf16[2,4,64,128]{3,2,1,0:T(8,128)(2,1)S(1)} %get-tuple-element.37), channel_id=1, source_target_pairs={{0,16},{1,17},{2,18},{3,19},{4,20},{5,21},{6,22},{7,23},{8,24},{9,... | collective-permute-start | bytes 393224 | tf_op jit(solution)/shard_map/ppermute | solution.py:334
  5.2 9.8 %collective-permute-start = (bf16[2,4,64,128]{3,2,1,0:T(8,128)(2,1)S(1)}, bf16[2,4,64,128]{3,2,1,0:T(8,128)(2,1)S(1)}, u32[]{:S(2)}, u32[]{:S(2)}) collective-permute-start(bf16[2,4,64,128]{3,2,1,0:T(8,128)(2,1)S(1)} %get-tuple-element.39), channel_id=1, source_target_pairs={{0,24},{1,25},{2,26},{3,27},{4,28},{5,29},{6,30},{7,31},{8,16},{9,... | collective-permute-start | bytes 393224 | tf_op jit(solution)/shard_map/ppermute | solution.py:334
  5.2 9.9 %collective-permute-start.2 = (bf16[2,4,64,128]{3,2,1,0:T(8,128)(2,1)S(1)}, bf16[2,4,64,128]{3,2,1,0:T(8,128)(2,1)S(1)}, u32[]{:S(2)}, u32[]{:S(2)}) collective-permute-start(bf16[2,4,64,128]{3,2,1,0:T(8,128)(2,1)S(1)} %get-tuple-element.38.refs_0_.refs_2_), channel_id=1, source_target_pairs={{0,4},{1,5},{2,6},{3,7},{4,0},{5,1},{6,2},{7,3},{8,12},{9,13},{10,... | collective-permute-start | bytes 393224 | tf_op jit(solution)/shard_map/ppermute | solution.py:334
  7.8 7.3 %collective-permute-start.4 = (bf16[2,4,64,128]{3,2,1,0:T(8,128)(2,1)S(1)}, bf16[2,4,64,128]{3,2,1,0:T(8,128)(2,1)S(1)}, u32[]{:S(2)}, u32[]{:S(2)}) collective-permute-start(bf16[2,4,64,128]{3,2,1,0:T(8,128)(2,1)S(1)} %collective-permute-done.3.refs_2_.refs_1_), channel_id=1, source_target_pairs={{0,4},{1,5},{2,6},{3,7},{4,0},{5,1},{6,2},{7,3},{8,12},{9,13},{10,... | collective-permute-start | bytes 393224 | tf_op jit(solution)/shard_map/ppermute | solution.py:334
  10.5 4.7 %collective-permute-start.6 = (bf16[2,4,64,128]{3,2,1,0:T(8,128)(2,1)S(1)}, bf16[2,4,64,128]{3,2,1,0:T(8,128)(2,1)S(1)}, u32[]{:S(2)}, u32[]{:S(2)}) collective-permute-start(bf16[2,4,64,128]{3,2,1,0:T(8,128)(2,1)S(1)} %collective-permute-done.5.refs_3_.refs_2_), channel_id=1, source_target_pairs={{0,4},{1,5},{2,6},{3,7},{4,0},{5,1},{6,2},{7,3},{8,12},{9,13},{10,... | collective-permute-start | bytes 393224 | tf_op jit(solution)/shard_map/ppermute | solution.py:334
  12.7 1.5 %copy-start = (bf16[27,64,512]{2,1,0:T(8,128)(2,1)S(1)}, bf16[27,64,512]{2,1,0:T(8,128)(2,1)}, u32[]{:S(2)}) copy-start(bf16[27,64,512]{2,1,0:T(8,128)(2,1)} %param.7) | copy-start | bytes 5308420
  15.0 1.4 %collective-permute-start.7 = (bf16[2,4,64,128]{3,2,1,0:T(8,128)(2,1)S(1)}, bf16[2,4,64,128]{3,2,1,0:T(8,128)(2,1)S(1)}, u32[]{:S(2)}, u32[]{:S(2)}) collective-permute-start(bf16[2,4,64,128]{3,2,1,0:T(8,128)(2,1)S(1)} %collective-permute-done.refs_2_.refs_3_.refs_4_), channel_id=1, source_target_pairs={{0,4},{1,5},{2,6},{3,7},{4,0},{5,1},{6,2},{7,3},{8,12},{9,13},{10,... | collective-permute-start | bytes 393224 | tf_op jit(solution)/shard_map/ppermute | solution.py:334
  18.2 15.2 %collective-permute-start.8 = (bf16[256,512]{1,0:T(8,128)(2,1)S(1)}, bf16[256,512]{1,0:T(8,128)(2,1)S(1)}, u32[]{:S(2)}, u32[]{:S(2)}) collective-permute-start(bf16[256,512]{1,0:T(8,128)(2,1)S(1)} %conv_inner.3.refs_8_), channel_id=1, source_target_pairs={{0,24},{1,25},{2,26},{3,27},{4,28},{5,29},{6,30},{7,31},{8,16},{9,... | collective-permute-start | bytes 786440 | tf_op jit(solution)/shard_map/ppermute | solution.py:334
  22.4 6.0 %collective-permute-start.11 = (bf16[4,2,64,128]{3,2,1,0:T(8,128)(2,1)S(1)}, bf16[4,2,64,128]{3,2,1,0:T(8,128)(2,1)S(1)}, u32[]{:S(2)}, u32[]{:S(2)}) collective-permute-start(bf16[4,2,64,128]{3,2,1,0:T(8,128)(2,1)S(1)} %get-tuple-element.25), channel_id=1, source_target_pairs={{0,1},{1,2},{2,3},{4,5},{5,6},{6,7},{8,9},{9,10},{10,11},{12,13},{... | collective-permute-start | bytes 393224 | tf_op jit(solution)/shard_map/ppermute | solution.py:334
  25.6 6.2 %collective-permute-start.12 = (bf16[4,2,64,128]{3,2,1,0:T(8,128)(2,1)S(1)}, bf16[4,2,64,128]{3,2,1,0:T(8,128)(2,1)S(1)}, u32[]{:S(2)}, u32[]{:S(2)}) collective-permute-start(bf16[4,2,64,128]{3,2,1,0:T(8,128)(2,1)S(1)} %get-tuple-element.23.refs_7_), channel_id=1, source_target_pairs={{1,0},{2,1},{3,2},{5,4},{6,5},{7,6},{9,8},{10,9},{11,10},{13,12},{... | collective-permute-start | bytes 393224 | tf_op jit(solution)/shard_map/ppermute | solution.py:334
  26.9 16.8 %collective-permute-start.10 = (bf16[256,512]{1,0:T(8,128)(2,1)S(1)}, bf16[256,512]{1,0:T(8,128)(2,1)S(1)}, u32[]{:S(2)}, u32[]{:S(2)}) collective-permute-start(bf16[256,512]{1,0:T(8,128)(2,1)S(1)} %get-tuple-element.22.refs_4_), channel_id=1, source_target_pairs={{0,8},{1,9},{2,10},{3,11},{4,12},{5,13},{6,14},{7,15},{8,0},{9,1},... | collective-permute-start | bytes 786440 | tf_op jit(solution)/shard_map/ppermute | solution.py:334
  28.2 15.5 %collective-permute-start.9 = (bf16[256,512]{1,0:T(8,128)(2,1)S(1)}, bf16[256,512]{1,0:T(8,128)(2,1)S(1)}, u32[]{:S(2)}, u32[]{:S(2)}) collective-permute-start(bf16[256,512]{1,0:T(8,128)(2,1)S(1)} %get-tuple-element.24), channel_id=1, source_target_pairs={{0,16},{1,17},{2,18},{3,19},{4,20},{5,21},{6,22},{7,23},{8,24},{9,... | collective-permute-start | bytes 786440 | tf_op jit(solution)/shard_map/ppermute | solution.py:334
  28.4 6.8 %collective-permute-start.13 = (bf16[4,2,64,128]{3,2,1,0:T(8,128)(2,1)S(1)}, bf16[4,2,64,128]{3,2,1,0:T(8,128)(2,1)S(1)}, u32[]{:S(2)}, u32[]{:S(2)}) collective-permute-start(bf16[4,2,64,128]{3,2,1,0:T(8,128)(2,1)S(1)} %collective-permute-done.11.refs_9_.refs_7_), channel_id=1, source_target_pairs={{0,4},{1,5},{2,6},{3,7},{4,0},{5,1},{6,2},{7,3},{8,12},{9,13},{10,... | collective-permute-start | bytes 393224 | tf_op jit(solution)/shard_map/ppermute | solution.py:334
  31.8 3.4 %collective-permute-start.14 = (bf16[4,2,64,128]{3,2,1,0:T(8,128)(2,1)S(1)}, bf16[4,2,64,128]{3,2,1,0:T(8,128)(2,1)S(1)}, u32[]{:S(2)}, u32[]{:S(2)}) collective-permute-start(bf16[4,2,64,128]{3,2,1,0:T(8,128)(2,1)S(1)} %collective-permute-done.12.refs_10_.refs_8_), channel_id=1, source_target_pairs={{0,4},{1,5},{2,6},{3,7},{4,0},{5,1},{6,2},{7,3},{8,12},{9,13},{10,... | collective-permute-start | bytes 393224 | tf_op jit(solution)/shard_map/ppermute | solution.py:334
  39.1 10.5 %collective-permute-start.16 = (bf16[256,512]{1,0:T(8,128)(2,1)S(1)}, bf16[256,512]{1,0:T(8,128)(2,1)S(1)}, u32[]{:S(2)}, u32[]{:S(2)}) collective-permute-start(bf16[256,512]{1,0:T(8,128)(2,1)S(1)} %get-tuple-element.28), channel_id=1, source_target_pairs={{0,24},{1,25},{2,26},{3,27},{4,28},{5,29},{6,30},{7,31},{8,16},{9,... | collective-permute-start | bytes 786440 | tf_op jit(solution)/shard_map/ppermute | solution.py:334
  40.3 13.6 %collective-permute-start.17 = (bf16[256,512]{1,0:T(8,128)(2,1)S(1)}, bf16[256,512]{1,0:T(8,128)(2,1)S(1)}, u32[]{:S(2)}, u32[]{:S(2)}) collective-permute-start(bf16[256,512]{1,0:T(8,128)(2,1)S(1)} %get-tuple-element.29), channel_id=1, source_target_pairs={{0,16},{1,17},{2,18},{3,19},{4,20},{5,21},{6,22},{7,23},{8,24},{9,... | collective-permute-start | bytes 786440 | tf_op jit(solution)/shard_map/ppermute | solution.py:334
  41.6 12.4 %collective-permute-start.18 = (bf16[256,512]{1,0:T(8,128)(2,1)S(1)}, bf16[256,512]{1,0:T(8,128)(2,1)S(1)}, u32[]{:S(2)}, u32[]{:S(2)}) collective-permute-start(bf16[256,512]{1,0:T(8,128)(2,1)S(1)} %get-tuple-element.26.refs_11_), channel_id=1, source_target_pairs={{0,8},{1,9},{2,10},{3,11},{4,12},{5,13},{6,14},{7,15},{8,0},{9,1},... | collective-permute-start | bytes 786440 | tf_op jit(solution)/shard_map/ppermute | solution.py:334
  43.6 22.7 %copy-start.1 = (bf16[512,512]{1,0:T(8,128)(2,1)S(1)}, bf16[512,512]{1,0:T(8,128)(2,1)}, u32[]{:S(2)}) copy-start(bf16[512,512]{1,0:T(8,128)(2,1)} %refs_8_.1) | copy-start | bytes 1572868
  43.7 22.7 %copy-start.2 = (bf16[512,512]{1,0:T(8,128)(2,1)S(1)}, bf16[512,512]{1,0:T(8,128)(2,1)}, u32[]{:S(2)}) copy-start(bf16[512,512]{1,0:T(8,128)(2,1)} %refs_9_.1) | copy-start | bytes 1572868
  43.7 22.7 %copy-start.3 = (bf16[512,512]{1,0:T(8,128)(2,1)S(1)}, bf16[512,512]{1,0:T(8,128)(2,1)}, u32[]{:S(2)}) copy-start(bf16[512,512]{1,0:T(8,128)(2,1)} %refs_10_.1) | copy-start | bytes 1572868
  43.7 22.7 %copy-start.4 = (bf16[512,512]{1,0:T(8,128)(2,1)S(1)}, bf16[512,512]{1,0:T(8,128)(2,1)}, u32[]{:S(2)}) copy-start(bf16[512,512]{1,0:T(8,128)(2,1)} %refs_11_.1) | copy-start | bytes 1572868
  43.9 15.9 %collective-permute-start.15 = (bf16[128,512]{1,0:T(8,128)(2,1)S(1)}, bf16[128,512]{1,0:T(8,128)(2,1)S(1)}, u32[]{:S(2)}, u32[]{:S(2)}) collective-permute-start(bf16[128,512]{1,0:T(8,128)(2,1)S(1)} %get-tuple-element.27), channel_id=1, source_target_pairs={{0,0},{1,1},{2,4},{3,5},{4,2},{5,3},{6,6},{7,7},{8,8},{9,9},{10,12... | collective-permute-start | bytes 393224 | tf_op jit(solution)/shard_map/ppermute | solution.py:334
  49.0 10.7 %collective-permute-start.20 = (bf16[128,512]{1,0:T(8,128)(2,1)S(1)}, bf16[128,512]{1,0:T(8,128)(2,1)S(1)}, u32[]{:S(2)}, u32[]{:S(2)}) collective-permute-start(bf16[128,512]{1,0:T(8,128)(2,1)S(1)} %get-tuple-element.31), channel_id=1, source_target_pairs={{0,1},{1,0},{2,5},{3,4},{4,3},{5,2},{6,7},{7,6},{8,9},{9,8},{10,13... | collective-permute-start | bytes 393224 | tf_op jit(solution)/shard_map/ppermute | solution.py:334
  54.1 8.6 %collective-permute-start.19 = (bf16[128,512]{1,0:T(8,128)(2,1)S(1)}, bf16[128,512]{1,0:T(8,128)(2,1)S(1)}, u32[]{:S(2)}, u32[]{:S(2)}) collective-permute-start(bf16[128,512]{1,0:T(8,128)(2,1)S(1)} %get-tuple-element.30), channel_id=1, source_target_pairs={{0,0},{1,1},{2,4},{3,5},{4,2},{5,3},{6,6},{7,7},{8,8},{9,9},{10,12... | collective-permute-start | bytes 393224 | tf_op jit(solution)/shard_map/ppermute | solution.py:334
  58.7 6.4 %collective-permute-start.21 = (bf16[128,512]{1,0:T(8,128)(2,1)S(1)}, bf16[128,512]{1,0:T(8,128)(2,1)S(1)}, u32[]{:S(2)}, u32[]{:S(2)}) collective-permute-start(bf16[128,512]{1,0:T(8,128)(2,1)S(1)} %get-tuple-element.32), channel_id=1, source_target_pairs={{0,1},{1,0},{2,5},{3,4},{4,3},{5,2},{6,7},{7,6},{8,9},{9,8},{10,13... | collective-permute-start | bytes 393224 | tf_op jit(solution)/shard_map/ppermute | solution.py:334
  59.7 5.3 %collective-permute-start.22 = (bf16[128,512]{1,0:T(8,128)(2,1)S(1)}, bf16[128,512]{1,0:T(8,128)(2,1)S(1)}, u32[]{:S(2)}, u32[]{:S(2)}) collective-permute-start(bf16[128,512]{1,0:T(8,128)(2,1)S(1)} %collective-permute-done.15.refs_0_), channel_id=1, source_target_pairs={{0,4},{1,5},{2,6},{3,7},{4,0},{5,1},{6,2},{7,3},{8,12},{9,13},{10,... | collective-permute-start | bytes 393224 | tf_op jit(solution)/shard_map/ppermute | solution.py:334
  59.7 5.3 %collective-permute-start.24 = (bf16[128,512]{1,0:T(8,128)(2,1)S(1)}, bf16[128,512]{1,0:T(8,128)(2,1)S(1)}, u32[]{:S(2)}, u32[]{:S(2)}) collective-permute-start(bf16[128,512]{1,0:T(8,128)(2,1)S(1)} %collective-permute-done.20.refs_2_), channel_id=1, source_target_pairs={{0,4},{1,5},{2,6},{3,7},{4,0},{5,1},{6,2},{7,3},{8,12},{9,13},{10,... | collective-permute-start | bytes 393224 | tf_op jit(solution)/shard_map/ppermute | solution.py:334
  62.7 2.3 %collective-permute-start.23 = (bf16[128,512]{1,0:T(8,128)(2,1)S(1)}, bf16[128,512]{1,0:T(8,128)(2,1)S(1)}, u32[]{:S(2)}, u32[]{:S(2)}) collective-permute-start(bf16[128,512]{1,0:T(8,128)(2,1)S(1)} %collective-permute-done.19.refs_1_), channel_id=1, source_target_pairs={{0,4},{1,5},{2,6},{3,7},{4,0},{5,1},{6,2},{7,3},{8,12},{9,13},{10,... | collective-permute-start | bytes 393224 | tf_op jit(solution)/shard_map/ppermute | solution.py:334
  65.0 1.3 %collective-permute-start.25 = (bf16[128,512]{1,0:T(8,128)(2,1)S(1)}, bf16[128,512]{1,0:T(8,128)(2,1)S(1)}, u32[]{:S(2)}, u32[]{:S(2)}) collective-permute-start(bf16[128,512]{1,0:T(8,128)(2,1)S(1)} %collective-permute-done.21.refs_3_), channel_id=1, source_target_pairs={{0,4},{1,5},{2,6},{3,7},{4,0},{5,1},{6,2},{7,3},{8,12},{9,13},{10,... | collective-permute-start | bytes 393224 | tf_op jit(solution)/shard_map/ppermute | solution.py:334
  70.8 8.8 %collective-permute-start.26 = (bf16[4,64,512]{2,1,0:T(8,128)(2,1)S(1)}, bf16[4,64,512]{2,1,0:T(8,128)(2,1)S(1)}, u32[]{:S(2)}, u32[]{:S(2)}) collective-permute-start(bf16[4,64,512]{2,1,0:T(8,128)(2,1)S(1)} %get-tuple-element.33), channel_id=1, source_target_pairs={{1,0},{0,1},{5,2},{4,3},{3,4},{2,5},{7,6},{6,7},{9,8},{8,9},{13,10... | collective-permute-start | bytes 786440 | tf_op jit(solution)/shard_map/ppermute | solution.py:409
  72.2 13.4 %collective-permute-start.27 = (bf16[4,64,512]{2,1,0:T(8,128)(2,1)S(1)}, bf16[4,64,512]{2,1,0:T(8,128)(2,1)S(1)}, u32[]{:S(2)}, u32[]{:S(2)}) collective-permute-start(bf16[4,64,512]{2,1,0:T(8,128)(2,1)S(1)} %get-tuple-element.34), channel_id=1, source_target_pairs={{0,0},{1,1},{4,2},{5,3},{2,4},{3,5},{6,6},{7,7},{8,8},{9,9},{12,10... | collective-permute-start | bytes 786440 | tf_op jit(solution)/shard_map/ppermute | solution.py:409

commit v12 on v5

--- a/solution.py
+++ b/solution.py
@@ -206,7 +206,11 @@
             pltpu.VMEM((len(dests), 2 * frames, rows_here + 2, columns, width), jnp.bfloat16)
         ],
         compiler_params=pltpu.CompilerParams(vmem_limit_bytes=VMEM_LIMIT),
-        cost_estimate=pl.CostEstimate(flops=10**11, bytes_accessed=1000, transcendentals=0),
+        cost_estimate=pl.CostEstimate(
+            flops=2 * total * taps * lags * width * chans,
+            bytes_accessed=2 * taps * lags * width * chans,
+            transcendentals=0,
+        ),
         name="conv_rim" if any_rim else "conv_inner",
     )(meta, *operands, *after)
 
@@ -396,30 +400,27 @@
         return [permute(x, to_place(1)) for x in pieces]
 
     rims = split_call(meta, above, below, parts)
-    inner_sent = conv(
-        [(3, False), (1, False)], rims=None, out_type=jnp.bfloat16, after=rims[:1]
-    )
+    rims = [permute(x, to_place(place)) if place else x for place, x in enumerate(rims)]
+    inner_sent = conv([(3, False), (1, False)], rims=None, out_type=jnp.bfloat16)
     inner_got = hop(inner_sent)
+    rims = stack_call(rims, inner_sent[0])
+    rims = (rims, permute(rims, to_member(1)))
+    rim_sent = conv(
+        [(3, True), (1, True)], rims=rims, out_type=jnp.bfloat16, after=inner_got[:2]
+    )
+    rim_got = hop(rim_sent)
     inner_on, inner_own = conv(
-        [(2, False), (0, False)], rims=None, out_type=jnp.float32, after=inner_sent[:1]
-    )
-    rims, _ = lax.optimization_barrier((rims, inner_sent[0]))
-    rims = [permute(x, to_place(place)) if place else x for place, x in enumerate(rims)]
-    rims = stack_call(rims, inner_on)
-    rims = (rims, permute(rims, to_member(1)))
-    (inner_relay,) = sum_call([inner_on, inner_got[0]], 1, after=inner_got[1:])
-    rim_sent = conv(
-        [(3, True), (1, True)], rims=rims, out_type=jnp.bfloat16, after=(inner_relay,)
-    )
-    rim_got = hop(rim_sent)
+        [(2, False), (0, False)], rims=None, out_type=jnp.float32, after=rim_sent[:1]
+    )
+    (inner_relay,) = sum_call([inner_on, inner_got[0]], 1)
     inner_last = permute(inner_relay, to_place(2))
     rim_on, rim_own = conv(
-        [(2, True), (0, True)], rims=rims, out_type=jnp.float32, after=rim_sent[:1]
-    )
-    (rim_relay,) = sum_call([rim_on, rim_got[0]], 1, after=rim_got[1:])
+        [(2, True), (0, True)], rims=rims, out_type=jnp.float32, after=(inner_relay,)
+    )
+    (rim_relay,) = sum_call([rim_on, rim_got[0]], 1)
     rim_last = permute(rim_relay, to_place(2))
     sums = [
-        sum_call([inner_own, inner_got[1], inner_last], frames),
+        sum_call([inner_own, inner_got[1], inner_last], frames, after=(rim_relay,)),
         sum_call([rim_own, rim_got[1], rim_last], frames),
     ]
 

time: 86.9 us -> 86.4 us (level)
  waiting for transfers between devices: 23.3 us -> 25.9 us
  Pallas kernels: 19.7 us -> 17.6 us
  starting transfers between devices: 38.8 us -> 37.7 us
    ppermute x28, waiting for transfers between devices: 12.7 us -> 15.3 us  [permute(): return lax.ppermute(block, BOTH, everywhere(sizes, target))]
    pallas_call x4, Pallas kernels: 1.97 us -> 0.3 us  [sum_call(): pl.pallas_call(kernel, out_shape=[jax.ShapeDtypeStruct((size, chans), jnp...]
    ppermute x28, starting transfers between devices: 33.9 us -> 32.8 us  [permute(): return lax.ppermute(block, BOTH, everywhere(sizes, target))]
  transfers between devices with their start and end apart: 30 -> 30, of which waited for: 14 -> 10; matrix products, arithmetic and copies ran while one was open for 3% -> 3% of each run, Pallas kernels for 14% -> 12%
where the time goes in v12:
time: 86.4 us; the launch traced here: 86.1 us
  starting transfers between devices  37.7 us (44%)
  waiting for transfers between devices  25.9 us (30%)
  Pallas kernels  17.6 us (20%)
  local copies, waits for them, and re-layouts  3.63 us (4%)
  other arithmetic  0.96 us (1%)
    ppermute x28, starting transfers between devices, permute(): return lax.ppermute(block, BOTH, everywhere(sizes, target))  32.8 us
    ppermute x28, waiting for transfers between devices, permute(): return lax.ppermute(block, BOTH, everywhere(sizes, target))  15.3 us
    pallas_call x4, Pallas kernels, conv_call(): pl.pallas_call(functools.partial(conv_kernel, tuple(jobs), parts, group,...  11.4 us
    ppermute x2, waiting for transfers between devices, body(): back.append(lax.ppermute(done[p], BOTH, pairs))  10.6 us
    ppermute x2, starting transfers between devices, body(): back.append(lax.ppermute(done[p], BOTH, pairs))  4.91 us
    pallas_call x1, Pallas kernels, attend_call(): pl.pallas_call(functools.partial(attend_kernel, frames, share, chunks), o...  4.47 us
  transfers between devices with their start and end apart: 30, of which 10 were waited for; matrix products, arithmetic and copies ran while one was open for 3% of the time, Pallas kernels for 12%

profile of v12, /device:TPU:1, one launch (start us, length us, event | category | flops | bytes accessed | tf_op | source)
XLA Modules:
  0.0 86.1 jit_solution(13369596053514633664)
XLA Ops:
  0.0 0.1 collective-permute-start.1
  0.1 1.1 %constant_dynamic-slice_fusion = (bf16[2,4,64,128]{3,2,1,0:T(8,128)(2,1)S(1)}, bf16[2,4,64,128]{3,2,1,0:T(8,128)(2,1)S(1)}, bf16[2,4,64,128]{3,2,1,0:T(8,128)(2,1)S(1)}, bf16[2,4,64,128]{3,2,1,0:T(8,128)(2,1)S(1)}) fusion(bf16[2,4,64,512]{3,2,1,0:T(8,128)(2,1)} %param.6, s32[]{:T(128)S(6)} %select_n.75, s32[]{:T(128)S(6)} %select_n.74, s32[]{:T(128)S(6)} %select_n.72, ...), kind=kLoop, calls=%fused_computation.5 | loop fusion | bytes 1048592 | tf_op jit(solution)/shard_map/dynamic_slice | solution.py:383
  1.2 2.7 %collective-permute-start = (bf16[2,4,64,128]{3,2,1,0:T(8,128)(2,1)S(1)}, bf16[2,4,64,128]{3,2,1,0:T(8,128)(2,1)S(1)}, u32[]{:S(2)}, u32[]{:S(2)}) collective-permute-start(bf16[2,4,64,128]{3,2,1,0:T(8,128)(2,1)S(1)} %get-tuple-element.52), channel_id=1, source_target_pairs={{0,16},{1,17},{2,18},{3,19},{4,12},{5,13},{6,14},{7,15},{8,24},{9,... | collective-permute-start | bytes 393224 | tf_op jit(solution)/shard_map/ppermute | solution.py:364
  3.9 1.2 %collective-permute-start.3 = (bf16[2,4,64,128]{3,2,1,0:T(8,128)(2,1)S(1)}, bf16[2,4,64,128]{3,2,1,0:T(8,128)(2,1)S(1)}, u32[]{:S(2)}, u32[]{:S(2)}) collective-permute-start(bf16[2,4,64,128]{3,2,1,0:T(8,128)(2,1)S(1)} %get-tuple-element.50), channel_id=1, source_target_pairs={{0,8},{1,9},{2,10},{3,11},{4,20},{5,21},{6,22},{7,23},{8,0},{9,1},... | collective-permute-start | bytes 393224 | tf_op jit(solution)/shard_map/ppermute | solution.py:364
  5.2 0.0 collective-permute-start.6
  5.2 1.0 %slice_bitcast_fusion = (bf16[2,64,512]{2,1,0:T(8,128)(2,1)S(1)}, bf16[2,64,512]{2,1,0:T(8,128)(2,1)S(1)}) fusion(bf16[2,4,64,512]{3,2,1,0:T(8,128)(2,1)} %param.6), kind=kLoop, calls=%fused_computation.3 | loop fusion | bytes 524288 | tf_op jit(solution)/shard_map/squeeze | solution.py:377
  6.2 3.4 %collective-permute-start.8 = (bf16[2,64,512]{2,1,0:T(8,128)(2,1)S(1)}, bf16[2,64,512]{2,1,0:T(8,128)(2,1)S(1)}, u32[]{:S(2)}, u32[]{:S(2)}) collective-permute-start(bf16[2,64,512]{2,1,0:T(8,128)(2,1)S(1)} %get-tuple-element.48), channel_id=1, source_target_pairs={{0,1},{1,2},{2,3},{4,5},{5,6},{6,7},{8,9},{9,10},{10,11},{12,13},{... | collective-permute-start | bytes 393224 | tf_op jit(solution)/shard_map/ppermute | solution.py:364
  9.6 0.1 pad_add_fusion.refs_0_.meta
  9.7 1.3 %collective-permute-start.9 = (bf16[2,64,512]{2,1,0:T(8,128)(2,1)S(1)}, bf16[2,64,512]{2,1,0:T(8,128)(2,1)S(1)}, u32[]{:S(2)}, u32[]{:S(2)}) collective-permute-start(bf16[2,64,512]{2,1,0:T(8,128)(2,1)S(1)} %get-tuple-element.47), channel_id=1, source_target_pairs={{1,0},{2,1},{3,2},{5,4},{6,5},{7,6},{9,8},{10,9},{11,10},{13,12},{... | collective-permute-start | bytes 393224 | tf_op jit(solution)/shard_map/ppermute | solution.py:364
  11.0 0.0 copy-start
  11.0 1.5 %copy-done = bf16[27,64,512]{2,1,0:T(8,128)(2,1)S(1)} copy-done((bf16[27,64,512]{2,1,0:T(8,128)(2,1)S(1)}, bf16[27,64,512]{2,1,0:T(8,128)(2,1)}, u32[]{:S(2)}) %copy-start) | copy-done | bytes 1769496
  12.4 0.9 merge_kernel_slices.1.refs_1_
  13.3 0.0 collective-permute-done.refs_3_
  13.3 1.2 %collective-permute-start.2 = (bf16[2,4,64,128]{3,2,1,0:T(8,128)(2,1)S(1)}, bf16[2,4,64,128]{3,2,1,0:T(8,128)(2,1)S(1)}, u32[]{:S(2)}, u32[]{:S(2)}) collective-permute-start(bf16[2,4,64,128]{3,2,1,0:T(8,128)(2,1)S(1)} %get-tuple-element.51.refs_2_), channel_id=1, source_target_pairs={{0,4},{1,5},{2,6},{3,7},{4,0},{5,1},{6,2},{7,3},{8,12},{9,13},{10,... | collective-permute-start | bytes 393224 | tf_op jit(solution)/shard_map/ppermute | solution.py:364
  14.5 0.0 collective-permute-done.3.refs_2_
  14.5 0.1 collective-permute-start.4
  14.6 0.4 collective-permute-start.7
  15.0 0.0 collective-permute-done.8.above
  15.0 0.1 collective-permute-start.5
  15.1 0.3 collective-permute-done.9.below
  15.4 0.6 split_halo_rows.1
  16.0 1.3 %collective-permute-start.10 = (bf16[2,2,64,128]{3,2,1,0:T(8,128)(2,1)S(1)}, bf16[2,2,64,128]{3,2,1,0:T(8,128)(2,1)S(1)}, u32[]{:S(2)}, u32[]{:S(2)}) collective-permute-start(bf16[2,2,64,128]{3,2,1,0:T(8,128)(2,1)S(1)} %get-tuple-element.28), channel_id=1, source_target_pairs={{0,8},{1,9},{2,10},{3,11},{4,20},{5,21},{6,22},{7,23},{8,0},{9,1},... | collective-permute-start | bytes 196616 | tf_op jit(solution)/shard_map/ppermute | solution.py:364
  17.3 0.0 collective-permute-done.2.refs_4_
  17.3 1.2 %collective-permute-start.11 = (bf16[2,2,64,128]{3,2,1,0:T(8,128)(2,1)S(1)}, bf16[2,2,64,128]{3,2,1,0:T(8,128)(2,1)S(1)}, u32[]{:S(2)}, u32[]{:S(2)}) collective-permute-start(bf16[2,2,64,128]{3,2,1,0:T(8,128)(2,1)S(1)} %get-tuple-element.29), channel_id=1, source_target_pairs={{0,16},{1,17},{2,18},{3,19},{4,12},{5,13},{6,14},{7,15},{8,24},{9,... | collective-permute-start | bytes 196616 | tf_op jit(solution)/shard_map/ppermute | solution.py:364
  18.5 0.0 collective-permute-done.4.refs_5_
  18.5 0.2 collective-permute-start.12
  18.7 2.9 %conv_inner.2 = (bf16[256,512]{1,0:T(8,128)(2,1)S(1)}, bf16[256,512]{1,0:T(8,128)(2,1)S(1)}) custom-call(s32[3]{0:T(128)S(1)} %pad_add_fusion.refs_0_.meta, bf16[3,9,128,512]{3,2,1,0:T(8,128)(2,1)S(1)} %merge_kernel_slices.1.refs_1_, bf16[2,4,64,128]{3,2,1,0:T(8,128)(2,1)S(1)} %collective-permute-done.3.refs_2_, ...), custom_call_target="tpu_custom_call" | custom-call | flops 1811939328 | bytes 3538944 | tf_op jit(solution)/shard_map/conv_inner/pallas_call | solution.py:200
  21.6 1.3 %collective-permute-start.14 = (bf16[256,512]{1,0:T(8,128)(2,1)S(1)}, bf16[256,512]{1,0:T(8,128)(2,1)S(1)}, u32[]{:S(2)}, u32[]{:S(2)}) collective-permute-start(bf16[256,512]{1,0:T(8,128)(2,1)S(1)} %get-tuple-element.31.refs_4_), channel_id=1, source_target_pairs={{0,8},{1,9},{2,10},{3,11},{4,20},{5,21},{6,22},{7,23},{8,0},{9,1},... | collective-permute-start | bytes 786440 | tf_op jit(solution)/shard_map/ppermute | solution.py:364
  22.9 0.0 collective-permute-done.12.refs_3_
  22.9 3.8 %collective-permute-start.13 = (bf16[4,2,2,64,128]{4,3,2,1,0:T(8,128)(2,1)S(1)}, bf16[4,2,2,64,128]{4,3,2,1,0:T(8,128)(2,1)S(1)}, u32[]{:S(2)}, u32[]{:S(2)}) collective-permute-start(bf16[4,2,2,64,128]{4,3,2,1,0:T(8,128)(2,1)S(1)} %stack_halo_rows.1.refs_8_), channel_id=1, source_target_pairs={{0,4},{1,5},{2,6},{3,7},{4,0},{5,1},{6,2},{7,3},{8,12},{9,13},{10,... | collective-permute-start | bytes 786440 | tf_op jit(solution)/shard_map/ppermute | solution.py:364
  26.7 0.9 %collective-permute-start.15 = (bf16[256,512]{1,0:T(8,128)(2,1)S(1)}, bf16[256,512]{1,0:T(8,128)(2,1)S(1)}, u32[]{:S(2)}, u32[]{:S(2)}) collective-permute-start(bf16[256,512]{1,0:T(8,128)(2,1)S(1)} %get-tuple-element.32), channel_id=1, source_target_pairs={{0,8},{1,9},{2,10},{3,11},{4,20},{5,21},{6,22},{7,23},{8,0},{9,1},... | collective-permute-start | bytes 786440 | tf_op jit(solution)/shard_map/ppermute | solution.py:364
  27.6 0.3 collective-permute-done.13.refs_9_
  27.8 4.4 %collective-permute-done.15.refs_11_.refs_1_ = bf16[256,512]{1,0:T(8,128)(2,1)S(1)} collective-permute-done((bf16[256,512]{1,0:T(8,128)(2,1)S(1)}, bf16[256,512]{1,0:T(8,128)(2,1)S(1)}, u32[]{:S(2)}, u32[]{:S(2)}) %collective-permute-start.15) | collective-permute-done | bytes 262176 | tf_op jit(solution)/shard_map/ppermute | solution.py:364
  32.2 2.9 %conv_rim.2 = (bf16[256,512]{1,0:T(8,128)(2,1)S(1)}, bf16[256,512]{1,0:T(8,128)(2,1)S(1)}) custom-call(s32[3]{0:T(128)S(1)} %pad_add_fusion.refs_0_.meta, bf16[3,9,128,512]{3,2,1,0:T(8,128)(2,1)S(1)} %merge_kernel_slices.1.refs_1_, bf16[2,4,64,128]{3,2,1,0:T(8,128)(2,1)S(1)} %collective-permute-done.3.refs_2_, ...), custom_call_target="tpu_custom_call" | custom-call | flops 1811939328 | bytes 3538944 | tf_op jit(solution)/shard_map/conv_rim/pallas_call | solution.py:200
  35.1 1.0 %collective-permute-start.17 = (bf16[256,512]{1,0:T(8,128)(2,1)S(1)}, bf16[256,512]{1,0:T(8,128)(2,1)S(1)}, u32[]{:S(2)}, u32[]{:S(2)}) collective-permute-start(bf16[256,512]{1,0:T(8,128)(2,1)S(1)} %get-tuple-element.33.refs_8_), channel_id=1, source_target_pairs={{0,8},{1,9},{2,10},{3,11},{4,20},{5,21},{6,22},{7,23},{8,0},{9,1},... | collective-permute-start | bytes 786440 | tf_op jit(solution)/shard_map/ppermute | solution.py:364
  36.0 0.6 collective-permute-start.19
  36.6 2.8 %conv_inner.3 = (f32[256,512]{1,0:T(8,128)S(1)}, f32[256,512]{1,0:T(8,128)S(1)}) custom-call(s32[3]{0:T(128)S(1)} %pad_add_fusion.refs_0_.meta, bf16[3,9,128,512]{3,2,1,0:T(8,128)(2,1)S(1)} %merge_kernel_slices.1.refs_1_, bf16[2,4,64,128]{3,2,1,0:T(8,128)(2,1)S(1)} %get-tuple-element.51.refs_2_, bf16[2,4,64,128]{3,2,1,0:T(8,128)(2,1)S(1)} %collective-permute-done.refs_3_, ...), custom_call_target="tpu_custom_call" | custom-call | flops 1811939328 | bytes 3538944 | tf_op jit(solution)/shard_map/conv_inner/pallas_call | solution.py:200
  39.5 0.1 sum_parts.4.refs_10_
  39.5 0.3 collective-permute-start.16
  39.8 2.9 %conv_rim.3 = (f32[256,512]{1,0:T(8,128)S(1)}, f32[256,512]{1,0:T(8,128)S(1)}) custom-call(s32[3]{0:T(128)S(1)} %pad_add_fusion.refs_0_.meta, bf16[3,9,128,512]{3,2,1,0:T(8,128)(2,1)S(1)} %merge_kernel_slices.1.refs_1_, bf16[2,4,64,128]{3,2,1,0:T(8,128)(2,1)S(1)} %get-tuple-element.51.refs_2_, bf16[2,4,64,128]{3,2,1,0:T(8,128)(2,1)S(1)} %collective-permute-done.refs_3_, ...), custom_call_target="tpu_custom_call" | custom-call | flops 1811939328 | bytes 3538944 | tf_op jit(solution)/shard_map/conv_rim/pallas_call | solution.py:200
  42.7 0.0 copy-start.1
  42.7 0.0 copy-start.2
  42.7 0.0 copy-start.3
  42.7 0.0 copy-start.4
  42.8 0.1 sum_parts.5.refs_3_
  42.8 1.3 %collective-permute-start.20 = (bf16[256,512]{1,0:T(8,128)(2,1)S(1)}, bf16[256,512]{1,0:T(8,128)(2,1)S(1)}, u32[]{:S(2)}, u32[]{:S(2)}) collective-permute-start(bf16[256,512]{1,0:T(8,128)(2,1)S(1)} %sum_parts.5.refs_3_), channel_id=1, source_target_pairs={{0,16},{1,17},{2,18},{3,19},{4,12},{5,13},{6,14},{7,15},{8,24},{9,... | collective-permute-start | bytes 786440 | tf_op jit(solution)/shard_map/ppermute | solution.py:364
  44.1 3.9 %collective-permute-done.16.refs_2_ = bf16[256,512]{1,0:T(8,128)(2,1)S(1)} collective-permute-done((bf16[256,512]{1,0:T(8,128)(2,1)S(1)}, bf16[256,512]{1,0:T(8,128)(2,1)S(1)}, u32[]{:S(2)}, u32[]{:S(2)}) %collective-permute-start.16) | collective-permute-done | bytes 262176 | tf_op jit(solution)/shard_map/ppermute | solution.py:364
  48.0 0.1 sum_parts.6
  48.1 4.4 %collective-permute-start.18 = (bf16[128,512]{1,0:T(8,128)(2,1)S(1)}, bf16[128,512]{1,0:T(8,128)(2,1)S(1)}, u32[]{:S(2)}, u32[]{:S(2)}) collective-permute-start(bf16[128,512]{1,0:T(8,128)(2,1)S(1)} %get-tuple-element.37), channel_id=1, source_target_pairs={{0,0},{1,1},{2,4},{3,5},{4,2},{5,3},{6,6},{7,7},{8,8},{9,9},{10,12... | collective-permute-start | bytes 393224 | tf_op jit(solution)/shard_map/ppermute | solution.py:364
  52.5 1.3 %collective-permute-start.22 = (bf16[128,512]{1,0:T(8,128)(2,1)S(1)}, bf16[128,512]{1,0:T(8,128)(2,1)S(1)}, u32[]{:S(2)}, u32[]{:S(2)}) collective-permute-start(bf16[128,512]{1,0:T(8,128)(2,1)S(1)} %get-tuple-element.41), channel_id=1, source_target_pairs={{0,1},{1,0},{2,5},{3,4},{4,3},{5,2},{6,7},{7,6},{8,9},{9,8},{10,13... | collective-permute-start | bytes 393224 | tf_op jit(solution)/shard_map/ppermute | solution.py:364
  53.7 0.1 sum_parts.7
  53.8 3.2 %collective-permute-start.21 = (bf16[128,512]{1,0:T(8,128)(2,1)S(1)}, bf16[128,512]{1,0:T(8,128)(2,1)S(1)}, u32[]{:S(2)}, u32[]{:S(2)}) collective-permute-start(bf16[128,512]{1,0:T(8,128)(2,1)S(1)} %get-tuple-element.40), channel_id=1, source_target_pairs={{0,0},{1,1},{2,4},{3,5},{4,2},{5,3},{6,6},{7,7},{8,8},{9,9},{10,12... | collective-permute-start | bytes 393224 | tf_op jit(solution)/shard_map/ppermute | solution.py:364
  57.1 1.1 %collective-permute-start.23 = (bf16[128,512]{1,0:T(8,128)(2,1)S(1)}, bf16[128,512]{1,0:T(8,128)(2,1)S(1)}, u32[]{:S(2)}, u32[]{:S(2)}) collective-permute-start(bf16[128,512]{1,0:T(8,128)(2,1)S(1)} %get-tuple-element.42), channel_id=1, source_target_pairs={{0,1},{1,0},{2,5},{3,4},{4,3},{5,2},{6,7},{7,6},{8,9},{9,8},{10,13... | collective-permute-start | bytes 393224 | tf_op jit(solution)/shard_map/ppermute | solution.py:364
  58.2 1.3 %collective-permute-done.22.refs_2_ = bf16[128,512]{1,0:T(8,128)(2,1)S(1)} collective-permute-done((bf16[128,512]{1,0:T(8,128)(2,1)S(1)}, bf16[128,512]{1,0:T(8,128)(2,1)S(1)}, u32[]{:S(2)}, u32[]{:S(2)}) %collective-permute-start.22) | collective-permute-done | bytes 131104 | tf_op jit(solution)/shard_map/ppermute | solution.py:364
  59.4 4.3 %collective-permute-done.21.refs_1_ = bf16[128,512]{1,0:T(8,128)(2,1)S(1)} collective-permute-done((bf16[128,512]{1,0:T(8,128)(2,1)S(1)}, bf16[128,512]{1,0:T(8,128)(2,1)S(1)}, u32[]{:S(2)}, u32[]{:S(2)}) %collective-permute-start.21) | collective-permute-done | bytes 131104 | tf_op jit(solution)/shard_map/ppermute | solution.py:364
  63.7 0.5 collective-permute-start.27
  64.2 0.8 collective-permute-done.25.refs_5_
  65.0 0.2 collective-permute-done.27.refs_7_
  65.2 4.5 %attend.1 = (bf16[4,64,512]{2,1,0:T(8,128)(2,1)S(1)}, bf16[4,64,512]{2,1,0:T(8,128)(2,1)S(1)}) custom-call(bf16[128,512]{1,0:T(8,128)(2,1)S(1)} %collective-permute-done.18.refs_0_, bf16[128,512]{1,0:T(8,128)(2,1)S(1)} %collective-permute-done.21.refs_1_, bf16[128,512]{1,0:T(8,128)(2,1)S(1)} %collective-permute-done.22.refs_2_, ...), custom_call_target="tpu_custom_call" | custom-call | flops 2684354560 | bytes 3145728 | tf_op jit(solution)/shard_map/attend/pallas_call | solution.py:335
  69.7 2.5 %collective-permute-start.28 = (bf16[4,64,512]{2,1,0:T(8,128)(2,1)S(1)}, bf16[4,64,512]{2,1,0:T(8,128)(2,1)S(1)}, u32[]{:S(2)}, u32[]{:S(2)}) collective-permute-start(bf16[4,64,512]{2,1,0:T(8,128)(2,1)S(1)} %get-tuple-element.43), channel_id=1, source_target_pairs={{1,0},{0,1},{5,2},{4,3},{3,4},{2,5},{7,6},{6,7},{9,8},{8,9},{13,10... | collective-permute-start | bytes 786440 | tf_op jit(solution)/shard_map/ppermute | solution.py:458
  72.2 2.4 %collective-permute-start.29 = (bf16[4,64,512]{2,1,0:T(8,128)(2,1)S(1)}, bf16[4,64,512]{2,1,0:T(8,128)(2,1)S(1)}, u32[]{:S(2)}, u32[]{:S(2)}) collective-permute-start(bf16[4,64,512]{2,1,0:T(8,128)(2,1)S(1)} %get-tuple-element.44), channel_id=1, source_target_pairs={{0,0},{1,1},{4,2},{5,3},{2,4},{3,5},{6,6},{7,7},{8,8},{9,9},{12,10... | collective-permute-start | bytes 786440 | tf_op jit(solution)/shard_map/ppermute | solution.py:458
  74.6 5.5 %collective-permute-done.28 = bf16[4,64,512]{2,1,0:T(8,128)(2,1)S(1)} collective-permute-done((bf16[4,64,512]{2,1,0:T(8,128)(2,1)S(1)}, bf16[4,64,512]{2,1,0:T(8,128)(2,1)S(1)}, u32[]{:S(2)}, u32[]{:S(2)}) %collective-permute-start.28) | collective-permute-done | bytes 262176 | tf_op jit(solution)/shard_map/ppermute | solution.py:458
  80.1 5.1 %collective-permute-done.29 = bf16[4,64,512]{2,1,0:T(8,128)(2,1)S(1)} collective-permute-done((bf16[4,64,512]{2,1,0:T(8,128)(2,1)S(1)}, bf16[4,64,512]{2,1,0:T(8,128)(2,1)S(1)}, u32[]{:S(2)}, u32[]{:S(2)}) %collective-permute-start.29) | collective-permute-done | bytes 262176 | tf_op jit(solution)/shard_map/ppermute | solution.py:458
  85.2 0.8 pad_maximum_fusion
  (23 shorter events, 0.1 us)
Async XLA Ops:
  0.0 9.7 %collective-permute-start.1 = (bf16[9,3,64,512]{3,2,1,0:T(8,128)(2,1)}, bf16[9,3,64,512]{3,2,1,0:T(8,128)(2,1)S(1)}, u32[]{:S(2)}, u32[]{:S(2)}) collective-permute-start(bf16[9,3,64,512]{3,2,1,0:T(8,128)(2,1)} %bitcast.16), channel_id=1, source_target_pairs={{0,4},{1,5},{2,6},{3,7},{4,0},{5,1},{6,2},{7,3},{8,12},{9,13},{10,... | collective-permute-start | bytes 5308424 | tf_op jit(solution)/shard_map/ppermute | solution.py:364
  1.2 12.1 %collective-permute-start = (bf16[2,4,64,128]{3,2,1,0:T(8,128)(2,1)S(1)}, bf16[2,4,64,128]{3,2,1,0:T(8,128)(2,1)S(1)}, u32[]{:S(2)}, u32[]{:S(2)}) collective-permute-start(bf16[2,4,64,128]{3,2,1,0:T(8,128)(2,1)S(1)} %get-tuple-element.52), channel_id=1, source_target_pairs={{0,16},{1,17},{2,18},{3,19},{4,12},{5,13},{6,14},{7,15},{8,24},{9,... | collective-permute-start | bytes 393224 | tf_op jit(solution)/shard_map/ppermute | solution.py:364
  3.9 10.6 %collective-permute-start.3 = (bf16[2,4,64,128]{3,2,1,0:T(8,128)(2,1)S(1)}, bf16[2,4,64,128]{3,2,1,0:T(8,128)(2,1)S(1)}, u32[]{:S(2)}, u32[]{:S(2)}) collective-permute-start(bf16[2,4,64,128]{3,2,1,0:T(8,128)(2,1)S(1)} %get-tuple-element.50), channel_id=1, source_target_pairs={{0,8},{1,9},{2,10},{3,11},{4,20},{5,21},{6,22},{7,23},{8,0},{9,1},... | collective-permute-start | bytes 393224 | tf_op jit(solution)/shard_map/ppermute | solution.py:364
  5.2 9.4 %collective-permute-start.6 = (bf16[2,4,64,128]{3,2,1,0:T(8,128)(2,1)S(1)}, bf16[2,4,64,128]{3,2,1,0:T(8,128)(2,1)S(1)}, u32[]{:S(2)}, u32[]{:S(2)}) collective-permute-start(bf16[2,4,64,128]{3,2,1,0:T(8,128)(2,1)S(1)} %get-tuple-element.49), channel_id=1, source_target_pairs={{0,24},{1,25},{2,26},{3,27},{4,28},{5,29},{6,30},{7,31},{8,16},{9,... | collective-permute-start | bytes 393224 | tf_op jit(solution)/shard_map/ppermute | solution.py:364
  6.2 8.8 %collective-permute-start.8 = (bf16[2,64,512]{2,1,0:T(8,128)(2,1)S(1)}, bf16[2,64,512]{2,1,0:T(8,128)(2,1)S(1)}, u32[]{:S(2)}, u32[]{:S(2)}) collective-permute-start(bf16[2,64,512]{2,1,0:T(8,128)(2,1)S(1)} %get-tuple-element.48), channel_id=1, source_target_pairs={{0,1},{1,2},{2,3},{4,5},{5,6},{6,7},{8,9},{9,10},{10,11},{12,13},{... | collective-permute-start | bytes 393224 | tf_op jit(solution)/shard_map/ppermute | solution.py:364
  9.7 5.7 %collective-permute-start.9 = (bf16[2,64,512]{2,1,0:T(8,128)(2,1)S(1)}, bf16[2,64,512]{2,1,0:T(8,128)(2,1)S(1)}, u32[]{:S(2)}, u32[]{:S(2)}) collective-permute-start(bf16[2,64,512]{2,1,0:T(8,128)(2,1)S(1)} %get-tuple-element.47), channel_id=1, source_target_pairs={{1,0},{2,1},{3,2},{5,4},{6,5},{7,6},{9,8},{10,9},{11,10},{13,12},{... | collective-permute-start | bytes 393224 | tf_op jit(solution)/shard_map/ppermute | solution.py:364
  11.0 1.5 %copy-start = (bf16[27,64,512]{2,1,0:T(8,128)(2,1)S(1)}, bf16[27,64,512]{2,1,0:T(8,128)(2,1)}, u32[]{:S(2)}) copy-start(bf16[27,64,512]{2,1,0:T(8,128)(2,1)} %param.7) | copy-start | bytes 5308420
  13.3 4.0 %collective-permute-start.2 = (bf16[2,4,64,128]{3,2,1,0:T(8,128)(2,1)S(1)}, bf16[2,4,64,128]{3,2,1,0:T(8,128)(2,1)S(1)}, u32[]{:S(2)}, u32[]{:S(2)}) collective-permute-start(bf16[2,4,64,128]{3,2,1,0:T(8,128)(2,1)S(1)} %get-tuple-element.51.refs_2_), channel_id=1, source_target_pairs={{0,4},{1,5},{2,6},{3,7},{4,0},{5,1},{6,2},{7,3},{8,12},{9,13},{10,... | collective-permute-start | bytes 393224 | tf_op jit(solution)/shard_map/ppermute | solution.py:364
  14.5 4.0 %collective-permute-start.4 = (bf16[2,4,64,128]{3,2,1,0:T(8,128)(2,1)S(1)}, bf16[2,4,64,128]{3,2,1,0:T(8,128)(2,1)S(1)}, u32[]{:S(2)}, u32[]{:S(2)}) collective-permute-start(bf16[2,4,64,128]{3,2,1,0:T(8,128)(2,1)S(1)} %collective-permute-done.3.refs_2_), channel_id=1, source_target_pairs={{0,4},{1,5},{2,6},{3,7},{4,0},{5,1},{6,2},{7,3},{8,12},{9,13},{10,... | collective-permute-start | bytes 393224 | tf_op jit(solution)/shard_map/ppermute | solution.py:364
  14.6 4.1 %collective-permute-start.7 = (bf16[2,4,64,128]{3,2,1,0:T(8,128)(2,1)S(1)}, bf16[2,4,64,128]{3,2,1,0:T(8,128)(2,1)S(1)}, u32[]{:S(2)}, u32[]{:S(2)}) collective-permute-start(bf16[2,4,64,128]{3,2,1,0:T(8,128)(2,1)S(1)} %collective-permute-done.6.refs_3_), channel_id=1, source_target_pairs={{0,4},{1,5},{2,6},{3,7},{4,0},{5,1},{6,2},{7,3},{8,12},{9,13},{10,... | collective-permute-start | bytes 393224 | tf_op jit(solution)/shard_map/ppermute | solution.py:364
  15.0 3.7 %collective-permute-start.5 = (bf16[2,4,64,128]{3,2,1,0:T(8,128)(2,1)S(1)}, bf16[2,4,64,128]{3,2,1,0:T(8,128)(2,1)S(1)}, u32[]{:S(2)}, u32[]{:S(2)}) collective-permute-start(bf16[2,4,64,128]{3,2,1,0:T(8,128)(2,1)S(1)} %collective-permute-done.refs_3_), channel_id=1, source_target_pairs={{0,4},{1,5},{2,6},{3,7},{4,0},{5,1},{6,2},{7,3},{8,12},{9,13},{10,... | collective-permute-start | bytes 393224 | tf_op jit(solution)/shard_map/ppermute | solution.py:364
  16.0 6.9 %collective-permute-start.10 = (bf16[2,2,64,128]{3,2,1,0:T(8,128)(2,1)S(1)}, bf16[2,2,64,128]{3,2,1,0:T(8,128)(2,1)S(1)}, u32[]{:S(2)}, u32[]{:S(2)}) collective-permute-start(bf16[2,2,64,128]{3,2,1,0:T(8,128)(2,1)S(1)} %get-tuple-element.28), channel_id=1, source_target_pairs={{0,8},{1,9},{2,10},{3,11},{4,20},{5,21},{6,22},{7,23},{8,0},{9,1},... | collective-permute-start | bytes 196616 | tf_op jit(solution)/shard_map/ppermute | solution.py:364
  17.3 5.6 %collective-permute-start.11 = (bf16[2,2,64,128]{3,2,1,0:T(8,128)(2,1)S(1)}, bf16[2,2,64,128]{3,2,1,0:T(8,128)(2,1)S(1)}, u32[]{:S(2)}, u32[]{:S(2)}) collective-permute-start(bf16[2,2,64,128]{3,2,1,0:T(8,128)(2,1)S(1)} %get-tuple-element.29), channel_id=1, source_target_pairs={{0,16},{1,17},{2,18},{3,19},{4,12},{5,13},{6,14},{7,15},{8,24},{9,... | collective-permute-start | bytes 196616 | tf_op jit(solution)/shard_map/ppermute | solution.py:364
  18.5 4.4 %collective-permute-start.12 = (bf16[2,2,64,128]{3,2,1,0:T(8,128)(2,1)S(1)}, bf16[2,2,64,128]{3,2,1,0:T(8,128)(2,1)S(1)}, u32[]{:S(2)}, u32[]{:S(2)}) collective-permute-start(bf16[2,2,64,128]{3,2,1,0:T(8,128)(2,1)S(1)} %get-tuple-element.30), channel_id=1, source_target_pairs={{0,24},{1,25},{2,26},{3,27},{4,28},{5,29},{6,30},{7,31},{8,16},{9,... | collective-permute-start | bytes 196616 | tf_op jit(solution)/shard_map/ppermute | solution.py:364
  21.6 6.3 %collective-permute-start.14 = (bf16[256,512]{1,0:T(8,128)(2,1)S(1)}, bf16[256,512]{1,0:T(8,128)(2,1)S(1)}, u32[]{:S(2)}, u32[]{:S(2)}) collective-permute-start(bf16[256,512]{1,0:T(8,128)(2,1)S(1)} %get-tuple-element.31.refs_4_), channel_id=1, source_target_pairs={{0,8},{1,9},{2,10},{3,11},{4,20},{5,21},{6,22},{7,23},{8,0},{9,1},... | collective-permute-start | bytes 786440 | tf_op jit(solution)/shard_map/ppermute | solution.py:364
  22.9 4.9 %collective-permute-start.13 = (bf16[4,2,2,64,128]{4,3,2,1,0:T(8,128)(2,1)S(1)}, bf16[4,2,2,64,128]{4,3,2,1,0:T(8,128)(2,1)S(1)}, u32[]{:S(2)}, u32[]{:S(2)}) collective-permute-start(bf16[4,2,2,64,128]{4,3,2,1,0:T(8,128)(2,1)S(1)} %stack_halo_rows.1.refs_8_), channel_id=1, source_target_pairs={{0,4},{1,5},{2,6},{3,7},{4,0},{5,1},{6,2},{7,3},{8,12},{9,13},{10,... | collective-permute-start | bytes 786440 | tf_op jit(solution)/shard_map/ppermute | solution.py:364
  26.7 5.5 %collective-permute-start.15 = (bf16[256,512]{1,0:T(8,128)(2,1)S(1)}, bf16[256,512]{1,0:T(8,128)(2,1)S(1)}, u32[]{:S(2)}, u32[]{:S(2)}) collective-permute-start(bf16[256,512]{1,0:T(8,128)(2,1)S(1)} %get-tuple-element.32), channel_id=1, source_target_pairs={{0,8},{1,9},{2,10},{3,11},{4,20},{5,21},{6,22},{7,23},{8,0},{9,1},... | collective-permute-start | bytes 786440 | tf_op jit(solution)/shard_map/ppermute | solution.py:364
  35.1 7.7 %collective-permute-start.17 = (bf16[256,512]{1,0:T(8,128)(2,1)S(1)}, bf16[256,512]{1,0:T(8,128)(2,1)S(1)}, u32[]{:S(2)}, u32[]{:S(2)}) collective-permute-start(bf16[256,512]{1,0:T(8,128)(2,1)S(1)} %get-tuple-element.33.refs_8_), channel_id=1, source_target_pairs={{0,8},{1,9},{2,10},{3,11},{4,20},{5,21},{6,22},{7,23},{8,0},{9,1},... | collective-permute-start | bytes 786440 | tf_op jit(solution)/shard_map/ppermute | solution.py:364
  36.0 17.7 %collective-permute-start.19 = (bf16[256,512]{1,0:T(8,128)(2,1)S(1)}, bf16[256,512]{1,0:T(8,128)(2,1)S(1)}, u32[]{:S(2)}, u32[]{:S(2)}) collective-permute-start(bf16[256,512]{1,0:T(8,128)(2,1)S(1)} %get-tuple-element.39), channel_id=1, source_target_pairs={{0,8},{1,9},{2,10},{3,11},{4,20},{5,21},{6,22},{7,23},{8,0},{9,1},... | collective-permute-start | bytes 786440 | tf_op jit(solution)/shard_map/ppermute | solution.py:364
  39.5 8.5 %collective-permute-start.16 = (bf16[256,512]{1,0:T(8,128)(2,1)S(1)}, bf16[256,512]{1,0:T(8,128)(2,1)S(1)}, u32[]{:S(2)}, u32[]{:S(2)}) collective-permute-start(bf16[256,512]{1,0:T(8,128)(2,1)S(1)} %sum_parts.4.refs_10_), channel_id=1, source_target_pairs={{0,16},{1,17},{2,18},{3,19},{4,12},{5,13},{6,14},{7,15},{8,24},{9,... | collective-permute-start | bytes 786440 | tf_op jit(solution)/shard_map/ppermute | solution.py:364
  42.7 22.5 %copy-start.1 = (bf16[512,512]{1,0:T(8,128)(2,1)S(1)}, bf16[512,512]{1,0:T(8,128)(2,1)}, u32[]{:S(2)}) copy-start(bf16[512,512]{1,0:T(8,128)(2,1)} %refs_8_.1) | copy-start | bytes 1572868
  42.7 22.5 %copy-start.2 = (bf16[512,512]{1,0:T(8,128)(2,1)S(1)}, bf16[512,512]{1,0:T(8,128)(2,1)}, u32[]{:S(2)}) copy-start(bf16[512,512]{1,0:T(8,128)(2,1)} %refs_9_.1) | copy-start | bytes 1572868
  42.7 22.5 %copy-start.3 = (bf16[512,512]{1,0:T(8,128)(2,1)S(1)}, bf16[512,512]{1,0:T(8,128)(2,1)}, u32[]{:S(2)}) copy-start(bf16[512,512]{1,0:T(8,128)(2,1)} %refs_10_.1) | copy-start | bytes 1572868
  42.7 22.5 %copy-start.4 = (bf16[512,512]{1,0:T(8,128)(2,1)S(1)}, bf16[512,512]{1,0:T(8,128)(2,1)}, u32[]{:S(2)}) copy-start(bf16[512,512]{1,0:T(8,128)(2,1)} %refs_11_.1) | copy-start | bytes 1572868
  42.8 10.9 %collective-permute-start.20 = (bf16[256,512]{1,0:T(8,128)(2,1)S(1)}, bf16[256,512]{1,0:T(8,128)(2,1)S(1)}, u32[]{:S(2)}, u32[]{:S(2)}) collective-permute-start(bf16[256,512]{1,0:T(8,128)(2,1)S(1)} %sum_parts.5.refs_3_), channel_id=1, source_target_pairs={{0,16},{1,17},{2,18},{3,19},{4,12},{5,13},{6,14},{7,15},{8,24},{9,... | collective-permute-start | bytes 786440 | tf_op jit(solution)/shard_map/ppermute | solution.py:364
  48.1 10.1 %collective-permute-start.18 = (bf16[128,512]{1,0:T(8,128)(2,1)S(1)}, bf16[128,512]{1,0:T(8,128)(2,1)S(1)}, u32[]{:S(2)}, u32[]{:S(2)}) collective-permute-start(bf16[128,512]{1,0:T(8,128)(2,1)S(1)} %get-tuple-element.37), channel_id=1, source_target_pairs={{0,0},{1,1},{2,4},{3,5},{4,2},{5,3},{6,6},{7,7},{8,8},{9,9},{10,12... | collective-permute-start | bytes 393224 | tf_op jit(solution)/shard_map/ppermute | solution.py:364
  52.5 7.0 %collective-permute-start.22 = (bf16[128,512]{1,0:T(8,128)(2,1)S(1)}, bf16[128,512]{1,0:T(8,128)(2,1)S(1)}, u32[]{:S(2)}, u32[]{:S(2)}) collective-permute-start(bf16[128,512]{1,0:T(8,128)(2,1)S(1)} %get-tuple-element.41), channel_id=1, source_target_pairs={{0,1},{1,0},{2,5},{3,4},{4,3},{5,2},{6,7},{7,6},{8,9},{9,8},{10,13... | collective-permute-start | bytes 393224 | tf_op jit(solution)/shard_map/ppermute | solution.py:364
  53.8 9.9 %collective-permute-start.21 = (bf16[128,512]{1,0:T(8,128)(2,1)S(1)}, bf16[128,512]{1,0:T(8,128)(2,1)S(1)}, u32[]{:S(2)}, u32[]{:S(2)}) collective-permute-start(bf16[128,512]{1,0:T(8,128)(2,1)S(1)} %get-tuple-element.40), channel_id=1, source_target_pairs={{0,0},{1,1},{2,4},{3,5},{4,2},{5,3},{6,6},{7,7},{8,8},{9,9},{10,12... | collective-permute-start | bytes 393224 | tf_op jit(solution)/shard_map/ppermute | solution.py:364
  57.1 6.6 %collective-permute-start.23 = (bf16[128,512]{1,0:T(8,128)(2,1)S(1)}, bf16[128,512]{1,0:T(8,128)(2,1)S(1)}, u32[]{:S(2)}, u32[]{:S(2)}) collective-permute-start(bf16[128,512]{1,0:T(8,128)(2,1)S(1)} %get-tuple-element.42), channel_id=1, source_target_pairs={{0,1},{1,0},{2,5},{3,4},{4,3},{5,2},{6,7},{7,6},{8,9},{9,8},{10,13... | collective-permute-start | bytes 393224 | tf_op jit(solution)/shard_map/ppermute | solution.py:364
  58.2 6.0 %collective-permute-start.24 = (bf16[128,512]{1,0:T(8,128)(2,1)S(1)}, bf16[128,512]{1,0:T(8,128)(2,1)S(1)}, u32[]{:S(2)}, u32[]{:S(2)}) collective-permute-start(bf16[128,512]{1,0:T(8,128)(2,1)S(1)} %collective-permute-done.18.refs_0_), channel_id=1, source_target_pairs={{0,4},{1,5},{2,6},{3,7},{4,0},{5,1},{6,2},{7,3},{8,12},{9,13},{10,... | collective-permute-start | bytes 393224 | tf_op jit(solution)/shard_map/ppermute | solution.py:364
  59.4 4.8 %collective-permute-start.26 = (bf16[128,512]{1,0:T(8,128)(2,1)S(1)}, bf16[128,512]{1,0:T(8,128)(2,1)S(1)}, u32[]{:S(2)}, u32[]{:S(2)}) collective-permute-start(bf16[128,512]{1,0:T(8,128)(2,1)S(1)} %collective-permute-done.22.refs_2_), channel_id=1, source_target_pairs={{0,4},{1,5},{2,6},{3,7},{4,0},{5,1},{6,2},{7,3},{8,12},{9,13},{10,... | collective-permute-start | bytes 393224 | tf_op jit(solution)/shard_map/ppermute | solution.py:364
  63.7 1.3 %collective-permute-start.25 = (bf16[128,512]{1,0:T(8,128)(2,1)S(1)}, bf16[128,512]{1,0:T(8,128)(2,1)S(1)}, u32[]{:S(2)}, u32[]{:S(2)}) collective-permute-start(bf16[128,512]{1,0:T(8,128)(2,1)S(1)} %collective-permute-done.21.refs_1_), channel_id=1, source_target_pairs={{0,4},{1,5},{2,6},{3,7},{4,0},{5,1},{6,2},{7,3},{8,12},{9,13},{10,... | collective-permute-start | bytes 393224 | tf_op jit(solution)/shard_map/ppermute | solution.py:364
  63.7 1.5 %collective-permute-start.27 = (bf16[128,512]{1,0:T(8,128)(2,1)S(1)}, bf16[128,512]{1,0:T(8,128)(2,1)S(1)}, u32[]{:S(2)}, u32[]{:S(2)}) collective-permute-start(bf16[128,512]{1,0:T(8,128)(2,1)S(1)} %collective-permute-done.23.refs_3_), channel_id=1, source_target_pairs={{0,4},{1,5},{2,6},{3,7},{4,0},{5,1},{6,2},{7,3},{8,12},{9,13},{10,... | collective-permute-start | bytes 393224 | tf_op jit(solution)/shard_map/ppermute | solution.py:364
  69.7 10.4 %collective-permute-start.28 = (bf16[4,64,512]{2,1,0:T(8,128)(2,1)S(1)}, bf16[4,64,512]{2,1,0:T(8,128)(2,1)S(1)}, u32[]{:S(2)}, u32[]{:S(2)}) collective-permute-start(bf16[4,64,512]{2,1,0:T(8,128)(2,1)S(1)} %get-tuple-element.43), channel_id=1, source_target_pairs={{1,0},{0,1},{5,2},{4,3},{3,4},{2,5},{7,6},{6,7},{9,8},{8,9},{13,10... | collective-permute-start | bytes 786440 | tf_op jit(solution)/shard_map/ppermute | solution.py:458
  72.2 13.0 %collective-permute-start.29 = (bf16[4,64,512]{2,1,0:T(8,128)(2,1)S(1)}, bf16[4,64,512]{2,1,0:T(8,128)(2,1)S(1)}, u32[]{:S(2)}, u32[]{:S(2)}) collective-permute-start(bf16[4,64,512]{2,1,0:T(8,128)(2,1)S(1)} %get-tuple-element.44), channel_id=1, source_target_pairs={{0,0},{1,1},{4,2},{5,3},{2,4},{3,5},{6,6},{7,7},{8,8},{9,9},{12,10... | collective-permute-start | bytes 786440 | tf_op jit(solution)/shard_map/ppermute | solution.py:458

commit v13 on v8

--- a/solution.py
+++ b/solution.py
@@ -80,7 +80,7 @@
     return pl.pallas_call(
         kernel,
         out_shape=[out] * 2,
-        in_specs=in_vmem(len(pieces) + 1),
+        in_specs=in_vmem(len(pieces)) + [pl.BlockSpec(memory_space=pl.ANY)],
         out_specs=in_vmem(2),
         compiler_params=pltpu.CompilerParams(vmem_limit_bytes=VMEM_LIMIT),
         name="halo_rows",
@@ -166,7 +166,7 @@
     counts = [frames * (2 if rim else rows_here - 2) * columns for _, rim in jobs]
     operands = [weights, *[held[s] for s in dests], *before, *(halos if any_rim else ())]
     specs = [pl.BlockSpec(memory_space=pltpu.SMEM)] + in_vmem(len(operands))
-    specs += in_vmem(len(after))
+    specs += [pl.BlockSpec(memory_space=pl.ANY)] * len(after)
     return pl.pallas_call(
         functools.partial(conv_kernel, tuple(jobs), parts, frames),
         out_shape=[jax.ShapeDtypeStruct((count, chans), out_type) for count in counts],
@@ -177,7 +177,7 @@
         ],
         compiler_params=pltpu.CompilerParams(vmem_limit_bytes=VMEM_LIMIT),
         cost_estimate=pl.CostEstimate(
-            flops=20 * sum(counts) * taps * lags * width * chans,
+            flops=2 * sum(counts) * taps * lags * width * chans,
             bytes_accessed=2 * taps * lags * width * chans,
             transcendentals=0,
         ),
@@ -185,26 +185,27 @@
     )(meta, *operands, *after)
 
 
-def sum_call(pieces, splits, after=()):
+def sum_call(pieces, frames):
     count, chans = pieces[0].shape
-    size = count // splits
+    out = jax.ShapeDtypeStruct((count // frames, chans), jnp.bfloat16)
 
     def kernel(*refs):
-        for p, out_ref in enumerate(refs[len(refs) - splits :]):
-            total = None
-            for ref in refs[: len(pieces)]:
-                rows = ref[p * size : (p + 1) * size].astype(jnp.float32)
-                total = rows if total is None else total + rows
+        ins, outs = refs[: len(pieces)], refs[len(pieces) :]
+        for p, out_ref in enumerate(outs):
+            size = out_ref.shape[0]
+            total = ins[0][pl.ds(p * size, size)].astype(jnp.float32)
+            for ref in ins[1:]:
+                total = total + ref[pl.ds(p * size, size)].astype(jnp.float32)
             out_ref[...] = total.astype(out_ref.dtype)
 
     return pl.pallas_call(
         kernel,
-        out_shape=[jax.ShapeDtypeStruct((size, chans), jnp.bfloat16)] * splits,
-        in_specs=in_vmem(len(pieces) + len(after)),
-        out_specs=in_vmem(splits),
+        out_shape=[out] * frames,
+        in_specs=in_vmem(len(pieces)),
+        out_specs=in_vmem(frames),
         compiler_params=pltpu.CompilerParams(vmem_limit_bytes=VMEM_LIMIT),
         name="sum_parts",
-    )(*pieces, *after)
+    )(*pieces)
 
 
 def attend_kernel(frames, share, chunks, *refs):
@@ -355,21 +356,18 @@
         conv_call, meta=meta, weights=weights, held=held, before=before, frames=frames
     )
     inner = conv([(s, False) for s in away[:1]], halos=None, out_type=jnp.bfloat16)
-    inner += conv(
-        [(s, False) for s in away[1:]], halos=None, out_type=jnp.bfloat16, after=inner[:1]
-    )
-    first, last = halo_call([*held, *before], inner[-1])
+    first, last = halo_call([*held, *before], inner[0])
     halos = (
         permute(last, lambda t, z: (t, z + 1) if z + 1 < depth else None),
         permute(first, lambda t, z: (t, z - 1) if z else None),
     )
-    inner_own = conv([(0, False)], halos=None, out_type=jnp.float32, after=(first,))
-    rim = conv([(s, True) for s in away], halos=halos, out_type=jnp.bfloat16, after=inner_own)
-    rim_own = conv([(0, True)], halos=halos, out_type=jnp.float32, after=rim[-1:])
+    inner += conv([(s, False) for s in away[1:]], halos=None, out_type=jnp.bfloat16)
+    rim = conv([(s, True) for s in away], halos=halos, out_type=jnp.bfloat16, after=inner[-1:])
+    mine = conv([(0, False), (0, True)], halos=halos, out_type=jnp.float32, after=rim[-1:])
     sums = []
-    for sent, own_part in ((inner, inner_own), (rim, rim_own)):
+    for sent, own_part in ((inner, mine[0]), (rim, mine[1])):
         got = [permute(x, to_part(s)) for s, x in zip(away, sent)]
-        sums.append(sum_call([*own_part, *got], frames, after=rim_own))
+        sums.append(sum_call([own_part, *got], frames))
 
     share = depth // frames
 

time: 85.5 us -> 86.2 us (level); the launches traced: 85.2 us -> 85 us
  starting transfers between devices: 35.5 us -> 39.7 us
  waiting for transfers between devices: 28.2 us -> 24.5 us
    ppermute x24, waiting for transfers between devices: 17.6 us -> 14 us  [permute(): return lax.ppermute(block, BOTH, everywhere(sizes, target))]
    ppermute x24, starting transfers between devices: 31.3 us -> 34.6 us  [permute(): return lax.ppermute(block, BOTH, everywhere(sizes, target))]
    ppermute x2, starting transfers between devices: 4.2 us -> 5.11 us  [body(): back.append(lax.ppermute(done[p], BOTH, pairs))]
    pallas_call x5 -> x4, Pallas kernels: 12.1 us -> 11.3 us  [conv_call(): pl.pallas_call(functools.partial(conv_kernel, tuple(jobs), parts, frames)...]
where the time goes in v13:
time: 86.2 us; the launch traced here: 85 us
  starting transfers between devices  39.7 us (46%)
  waiting for transfers between devices  24.5 us (28%)
  Pallas kernels  16.9 us (20%)
  local copies, waits for them, and re-layouts  2.65 us (3%)
  other arithmetic  0.96 us (1%)
    ppermute x24, starting transfers between devices, permute(): return lax.ppermute(block, BOTH, everywhere(sizes, target))  34.6 us
    ppermute x24, waiting for transfers between devices, permute(): return lax.ppermute(block, BOTH, everywhere(sizes, target))  14 us
    pallas_call x4, Pallas kernels, conv_call(): pl.pallas_call(functools.partial(conv_kernel, tuple(jobs), parts, frames)...  11.3 us
    ppermute x2, waiting for transfers between devices, body(): back.append(lax.ppermute(done[p], BOTH, pairs))  10.5 us
    ppermute x2, starting transfers between devices, body(): back.append(lax.ppermute(done[p], BOTH, pairs))  5.11 us
    pallas_call x1, Pallas kernels, attend_call(): pl.pallas_call(functools.partial(attend_kernel, frames, share, chunks), o...  4.4 us
  transfers between devices with their start and end apart: 26, of which 10 were waited for; matrix products, arithmetic and copies ran while one was open for 1% of the time, Pallas kernels for 13%

profile of v13, /device:TPU:1, one launch (start us, length us, event | category | flops | bytes accessed | tf_op | source)
XLA Modules:
  0.0 85.0 jit_solution(1013937508667800857)
XLA Ops:
  0.0 0.1 collective-permute-start
  0.1 1.1 %constant_dynamic-slice_fusion = (bf16[2,4,64,128]{3,2,1,0:T(8,128)(2,1)S(1)}, bf16[2,4,64,128]{3,2,1,0:T(8,128)(2,1)S(1)}, bf16[2,4,64,128]{3,2,1,0:T(8,128)(2,1)S(1)}, bf16[2,4,64,128]{3,2,1,0:T(8,128)(2,1)S(1)}) fusion(bf16[2,4,64,512]{3,2,1,0:T(8,128)(2,1)} %param.6, s32[]{:T(128)S(6)} %select_n.50, s32[]{:T(128)S(6)} %select_n.48, s32[]{:T(128)S(6)} %select_n.47, ...), kind=kLoop, calls=%fused_computation.3 | loop fusion | bytes 1048592 | tf_op jit(solution)/shard_map/dynamic_slice | solution.py:345
  1.2 2.7 %collective-permute-start.2 = (bf16[2,4,64,128]{3,2,1,0:T(8,128)(2,1)S(1)}, bf16[2,4,64,128]{3,2,1,0:T(8,128)(2,1)S(1)}, u32[]{:S(2)}, u32[]{:S(2)}) collective-permute-start(bf16[2,4,64,128]{3,2,1,0:T(8,128)(2,1)S(1)} %get-tuple-element.38), channel_id=1, source_target_pairs={{0,8},{1,9},{2,10},{3,11},{4,12},{5,13},{6,14},{7,15},{8,0},{9,1},... | collective-permute-start | bytes 393224 | tf_op jit(solution)/shard_map/ppermute | solution.py:335
  3.9 1.2 %collective-permute-start.4 = (bf16[2,4,64,128]{3,2,1,0:T(8,128)(2,1)S(1)}, bf16[2,4,64,128]{3,2,1,0:T(8,128)(2,1)S(1)}, u32[]{:S(2)}, u32[]{:S(2)}) collective-permute-start(bf16[2,4,64,128]{3,2,1,0:T(8,128)(2,1)S(1)} %get-tuple-element.40), channel_id=1, source_target_pairs={{0,16},{1,17},{2,18},{3,19},{4,20},{5,21},{6,22},{7,23},{8,24},{9,... | collective-permute-start | bytes 393224 | tf_op jit(solution)/shard_map/ppermute | solution.py:335
  5.2 0.0 collective-permute-start.6
  5.2 0.6 collective-permute-start.1
  5.8 2.0 %collective-permute-done.2.refs_1_.refs_2_ = bf16[2,4,64,128]{3,2,1,0:T(8,128)(2,1)S(1)} collective-permute-done((bf16[2,4,64,128]{3,2,1,0:T(8,128)(2,1)S(1)}, bf16[2,4,64,128]{3,2,1,0:T(8,128)(2,1)S(1)}, u32[]{:S(2)}, u32[]{:S(2)}) %collective-permute-start.2) | collective-permute-done | bytes 131104 | tf_op jit(solution)/shard_map/ppermute | solution.py:335
  7.8 0.7 collective-permute-start.3
  8.5 2.0 %collective-permute-done.4.refs_2_.refs_3_ = bf16[2,4,64,128]{3,2,1,0:T(8,128)(2,1)S(1)} collective-permute-done((bf16[2,4,64,128]{3,2,1,0:T(8,128)(2,1)S(1)}, bf16[2,4,64,128]{3,2,1,0:T(8,128)(2,1)S(1)}, u32[]{:S(2)}, u32[]{:S(2)}) %collective-permute-start.4) | collective-permute-done | bytes 131104 | tf_op jit(solution)/shard_map/ppermute | solution.py:335
  10.5 2.2 %collective-permute-start.5 = (bf16[2,4,64,128]{3,2,1,0:T(8,128)(2,1)S(1)}, bf16[2,4,64,128]{3,2,1,0:T(8,128)(2,1)S(1)}, u32[]{:S(2)}, u32[]{:S(2)}) collective-permute-start(bf16[2,4,64,128]{3,2,1,0:T(8,128)(2,1)S(1)} %collective-permute-done.4.refs_2_.refs_3_), channel_id=1, source_target_pairs={{0,4},{1,5},{2,6},{3,7},{4,0},{5,1},{6,2},{7,3},{8,12},{9,13},{10,... | collective-permute-start | bytes 393224 | tf_op jit(solution)/shard_map/ppermute | solution.py:335
  12.7 0.0 collective-permute-done.6.refs_2_.refs_3_.refs_4_
  12.7 0.0 collective-permute-start.7
  12.7 0.1 pad_add_fusion.refs_0_
  12.8 1.5 %copy-done = bf16[27,64,512]{2,1,0:T(8,128)(2,1)S(1)} copy-done((bf16[27,64,512]{2,1,0:T(8,128)(2,1)S(1)}, bf16[27,64,512]{2,1,0:T(8,128)(2,1)}, u32[]{:S(2)}) %copy-start) | copy-done | bytes 1769496
  14.2 0.9 %merge_kernel_slices.1.refs_1_ = bf16[3,9,128,512]{3,2,1,0:T(8,128)(2,1)S(1)} custom-call(s32[3]{0:T(128)S(1)} %pad_add_fusion.refs_0_, bf16[9,3,64,512]{3,2,1,0:T(8,128)(2,1)S(1)} %bitcast.9, bf16[9,3,64,512]{3,2,1,0:T(8,128)(2,1)S(1)} %collective-permute-done.refs_2_), custom_call_target="tpu_custom_call" | custom-call | tf_op jit(solution)/shard_map/merge_kernel_slices/pallas_call | solution.py:58
  15.1 0.0 collective-permute-done.1.refs_3_.refs_4_.refs_5_
  15.1 0.0 collective-permute-done.3.refs_4_.refs_5_.refs_6_
  15.1 0.0 collective-permute-done.7.refs_6_.refs_7_.refs_8_
  15.1 1.8 %conv_inner.2.refs_8_ = bf16[256,512]{1,0:T(8,128)(2,1)S(1)} custom-call(s32[3]{0:T(128)S(1)} %pad_add_fusion.refs_0_, bf16[3,9,128,512]{3,2,1,0:T(8,128)(2,1)S(1)} %merge_kernel_slices.1.refs_1_, bf16[2,4,64,128]{3,2,1,0:T(8,128)(2,1)S(1)} %collective-permute-done.6.refs_2_.refs_3_.refs_4_, ...), custom_call_target="tpu_custom_call" | custom-call | flops 905969664 | bytes 3538944 | tf_op jit(solution)/shard_map/conv_inner/pallas_call | solution.py:170
  17.0 3.2 %collective-permute-start.8 = (bf16[8,2,64,128]{3,2,1,0:T(8,128)(2,1)S(1)}, bf16[8,2,64,128]{3,2,1,0:T(8,128)(2,1)S(1)}, u32[]{:S(2)}, u32[]{:S(2)}) collective-permute-start(bf16[8,2,64,128]{3,2,1,0:T(8,128)(2,1)S(1)} %get-tuple-element.20), channel_id=1, source_target_pairs={{0,1},{1,2},{2,3},{4,5},{5,6},{6,7},{8,9},{9,10},{10,11},{12,13},{... | collective-permute-start | bytes 786440 | tf_op jit(solution)/shard_map/ppermute | solution.py:335
  20.2 1.3 %collective-permute-start.9 = (bf16[8,2,64,128]{3,2,1,0:T(8,128)(2,1)S(1)}, bf16[8,2,64,128]{3,2,1,0:T(8,128)(2,1)S(1)}, u32[]{:S(2)}, u32[]{:S(2)}) collective-permute-start(bf16[8,2,64,128]{3,2,1,0:T(8,128)(2,1)S(1)} %get-tuple-element.21), channel_id=1, source_target_pairs={{1,0},{2,1},{3,2},{5,4},{6,5},{7,6},{9,8},{10,9},{11,10},{13,12},{... | collective-permute-start | bytes 786440 | tf_op jit(solution)/shard_map/ppermute | solution.py:335
  21.5 2.8 %conv_inner.3 = (bf16[256,512]{1,0:T(8,128)(2,1)S(1)}, bf16[256,512]{1,0:T(8,128)(2,1)S(1)}) custom-call(s32[3]{0:T(128)S(1)} %pad_add_fusion.refs_0_, bf16[3,9,128,512]{3,2,1,0:T(8,128)(2,1)S(1)} %merge_kernel_slices.1.refs_1_, bf16[2,4,64,128]{3,2,1,0:T(8,128)(2,1)S(1)} %collective-permute-done.2.refs_1_.refs_2_, ...), custom_call_target="tpu_custom_call" | custom-call | flops 1811939328 | bytes 3538944 | tf_op jit(solution)/shard_map/conv_inner/pallas_call | solution.py:170
  24.3 1.3 %collective-permute-start.11 = (bf16[256,512]{1,0:T(8,128)(2,1)S(1)}, bf16[256,512]{1,0:T(8,128)(2,1)S(1)}, u32[]{:S(2)}, u32[]{:S(2)}) collective-permute-start(bf16[256,512]{1,0:T(8,128)(2,1)S(1)} %get-tuple-element.25), channel_id=1, source_target_pairs={{0,16},{1,17},{2,18},{3,19},{4,20},{5,21},{6,22},{7,23},{8,24},{9,... | collective-permute-start | bytes 786440 | tf_op jit(solution)/shard_map/ppermute | solution.py:335
  25.6 0.9 %collective-permute-start.10 = (bf16[256,512]{1,0:T(8,128)(2,1)S(1)}, bf16[256,512]{1,0:T(8,128)(2,1)S(1)}, u32[]{:S(2)}, u32[]{:S(2)}) collective-permute-start(bf16[256,512]{1,0:T(8,128)(2,1)S(1)} %conv_inner.2.refs_8_), channel_id=1, source_target_pairs={{0,24},{1,25},{2,26},{3,27},{4,28},{5,29},{6,30},{7,31},{8,16},{9,... | collective-permute-start | bytes 786440 | tf_op jit(solution)/shard_map/ppermute | solution.py:335
  26.5 0.5 collective-permute-start.12
  27.1 0.0 collective-permute-done.8.refs_9_.refs_7_
  27.1 2.1 %collective-permute-done.9.refs_10_.refs_8_ = bf16[8,2,64,128]{3,2,1,0:T(8,128)(2,1)S(1)} collective-permute-done((bf16[8,2,64,128]{3,2,1,0:T(8,128)(2,1)S(1)}, bf16[8,2,64,128]{3,2,1,0:T(8,128)(2,1)S(1)}, u32[]{:S(2)}, u32[]{:S(2)}) %collective-permute-start.9) | collective-permute-done | bytes 262176 | tf_op jit(solution)/shard_map/ppermute | solution.py:335
  29.1 3.9 %conv_rim.2 = (bf16[256,512]{1,0:T(8,128)(2,1)S(1)}, bf16[256,512]{1,0:T(8,128)(2,1)S(1)}, bf16[256,512]{1,0:T(8,128)(2,1)S(1)}) custom-call(s32[3]{0:T(128)S(1)} %pad_add_fusion.refs_0_, bf16[3,9,128,512]{3,2,1,0:T(8,128)(2,1)S(1)} %merge_kernel_slices.1.refs_1_, bf16[2,4,64,128]{3,2,1,0:T(8,128)(2,1)S(1)} %collective-permute-done.2.refs_1_.refs_2_, ...), custom_call_target="tpu_custom_call" | custom-call | flops 2717908992 | bytes 3538944 | tf_op jit(solution)/shard_map/conv_rim/pallas_call | solution.py:170
  33.0 1.3 %collective-permute-start.14 = (bf16[256,512]{1,0:T(8,128)(2,1)S(1)}, bf16[256,512]{1,0:T(8,128)(2,1)S(1)}, u32[]{:S(2)}, u32[]{:S(2)}) collective-permute-start(bf16[256,512]{1,0:T(8,128)(2,1)S(1)} %get-tuple-element.28), channel_id=1, source_target_pairs={{0,24},{1,25},{2,26},{3,27},{4,28},{5,29},{6,30},{7,31},{8,16},{9,... | collective-permute-start | bytes 786440 | tf_op jit(solution)/shard_map/ppermute | solution.py:335
  34.3 1.5 %collective-permute-start.15 = (bf16[256,512]{1,0:T(8,128)(2,1)S(1)}, bf16[256,512]{1,0:T(8,128)(2,1)S(1)}, u32[]{:S(2)}, u32[]{:S(2)}) collective-permute-start(bf16[256,512]{1,0:T(8,128)(2,1)S(1)} %get-tuple-element.29), channel_id=1, source_target_pairs={{0,16},{1,17},{2,18},{3,19},{4,20},{5,21},{6,22},{7,23},{8,24},{9,... | collective-permute-start | bytes 786440 | tf_op jit(solution)/shard_map/ppermute | solution.py:335
  35.8 1.3 %collective-permute-done.11.refs_2_ = bf16[256,512]{1,0:T(8,128)(2,1)S(1)} collective-permute-done((bf16[256,512]{1,0:T(8,128)(2,1)S(1)}, bf16[256,512]{1,0:T(8,128)(2,1)S(1)}, u32[]{:S(2)}, u32[]{:S(2)}) %collective-permute-start.11) | collective-permute-done | bytes 262176 | tf_op jit(solution)/shard_map/ppermute | solution.py:335
  37.1 1.5 %collective-permute-start.16 = (bf16[256,512]{1,0:T(8,128)(2,1)S(1)}, bf16[256,512]{1,0:T(8,128)(2,1)S(1)}, u32[]{:S(2)}, u32[]{:S(2)}) collective-permute-start(bf16[256,512]{1,0:T(8,128)(2,1)S(1)} %get-tuple-element.23.refs_9_), channel_id=1, source_target_pairs={{0,8},{1,9},{2,10},{3,11},{4,12},{5,13},{6,14},{7,15},{8,0},{9,1},... | collective-permute-start | bytes 786440 | tf_op jit(solution)/shard_map/ppermute | solution.py:335
  38.6 2.8 %conv_rim.3 = (f32[256,512]{1,0:T(8,128)S(1)}, f32[256,512]{1,0:T(8,128)S(1)}) custom-call(s32[3]{0:T(128)S(1)} %pad_add_fusion.refs_0_, bf16[3,9,128,512]{3,2,1,0:T(8,128)(2,1)S(1)} %merge_kernel_slices.1.refs_1_, bf16[2,4,64,128]{3,2,1,0:T(8,128)(2,1)S(1)} %get-tuple-element.39.refs_0_.refs_2_, ...), custom_call_target="tpu_custom_call" | custom-call | flops 1811939328 | bytes 3538944 | tf_op jit(solution)/shard_map/conv_rim/pallas_call | solution.py:170
  41.4 0.0 copy-start.1
  41.4 0.0 copy-start.2
  41.4 0.0 copy-start.3
  41.4 0.0 copy-start.4
  41.4 0.0 collective-permute-done.12.refs_3_
  41.4 0.0 collective-permute-done.10.refs_1_
  41.5 0.1 sum_parts.2
  41.6 8.9 %collective-permute-start.13 = (bf16[128,512]{1,0:T(8,128)(2,1)S(1)}, bf16[128,512]{1,0:T(8,128)(2,1)S(1)}, u32[]{:S(2)}, u32[]{:S(2)}) collective-permute-start(bf16[128,512]{1,0:T(8,128)(2,1)S(1)} %get-tuple-element.26), channel_id=1, source_target_pairs={{0,0},{1,1},{2,4},{3,5},{4,2},{5,3},{6,6},{7,7},{8,8},{9,9},{10,12... | collective-permute-start | bytes 393224 | tf_op jit(solution)/shard_map/ppermute | solution.py:335
  50.5 1.1 %collective-permute-start.18 = (bf16[128,512]{1,0:T(8,128)(2,1)S(1)}, bf16[128,512]{1,0:T(8,128)(2,1)S(1)}, u32[]{:S(2)}, u32[]{:S(2)}) collective-permute-start(bf16[128,512]{1,0:T(8,128)(2,1)S(1)} %get-tuple-element.31), channel_id=1, source_target_pairs={{0,1},{1,0},{2,5},{3,4},{4,3},{5,2},{6,7},{7,6},{8,9},{9,8},{10,13... | collective-permute-start | bytes 393224 | tf_op jit(solution)/shard_map/ppermute | solution.py:335
  51.6 0.0 collective-permute-done.14.refs_1_
  51.6 0.0 collective-permute-done.15.refs_2_
  51.6 0.0 collective-permute-done.16.refs_3_
  51.6 0.1 sum_parts.3
  51.8 4.5 %collective-permute-start.17 = (bf16[128,512]{1,0:T(8,128)(2,1)S(1)}, bf16[128,512]{1,0:T(8,128)(2,1)S(1)}, u32[]{:S(2)}, u32[]{:S(2)}) collective-permute-start(bf16[128,512]{1,0:T(8,128)(2,1)S(1)} %get-tuple-element.30), channel_id=1, source_target_pairs={{0,0},{1,1},{2,4},{3,5},{4,2},{5,3},{6,6},{7,7},{8,8},{9,9},{10,12... | collective-permute-start | bytes 393224 | tf_op jit(solution)/shard_map/ppermute | solution.py:335
  56.3 1.1 %collective-permute-start.19 = (bf16[128,512]{1,0:T(8,128)(2,1)S(1)}, bf16[128,512]{1,0:T(8,128)(2,1)S(1)}, u32[]{:S(2)}, u32[]{:S(2)}) collective-permute-start(bf16[128,512]{1,0:T(8,128)(2,1)S(1)} %get-tuple-element.32), channel_id=1, source_target_pairs={{0,1},{1,0},{2,5},{3,4},{4,3},{5,2},{6,7},{7,6},{8,9},{9,8},{10,13... | collective-permute-start | bytes 393224 | tf_op jit(solution)/shard_map/ppermute | solution.py:335
  57.4 0.0 collective-permute-done.13.refs_0_
  57.4 0.0 collective-permute-start.20
  57.4 0.7 collective-permute-done.18.refs_2_
  58.1 0.0 collective-permute-start.22
  58.1 2.6 %collective-permute-done.17.refs_1_ = bf16[128,512]{1,0:T(8,128)(2,1)S(1)} collective-permute-done((bf16[128,512]{1,0:T(8,128)(2,1)S(1)}, bf16[128,512]{1,0:T(8,128)(2,1)S(1)}, u32[]{:S(2)}, u32[]{:S(2)}) %collective-permute-start.17) | collective-permute-done | bytes 131104 | tf_op jit(solution)/shard_map/ppermute | solution.py:335
  60.7 0.0 collective-permute-start.21
  60.7 2.0 %collective-permute-done.19.refs_3_ = bf16[128,512]{1,0:T(8,128)(2,1)S(1)} collective-permute-done((bf16[128,512]{1,0:T(8,128)(2,1)S(1)}, bf16[128,512]{1,0:T(8,128)(2,1)S(1)}, u32[]{:S(2)}, u32[]{:S(2)}) %collective-permute-start.19) | collective-permute-done | bytes 131104 | tf_op jit(solution)/shard_map/ppermute | solution.py:335
  62.6 0.0 collective-permute-start.23
  62.6 0.0 collective-permute-done.20.refs_4_
  62.7 1.3 %collective-permute-done.23.refs_7_ = bf16[128,512]{1,0:T(8,128)(2,1)S(1)} collective-permute-done((bf16[128,512]{1,0:T(8,128)(2,1)S(1)}, bf16[128,512]{1,0:T(8,128)(2,1)S(1)}, u32[]{:S(2)}, u32[]{:S(2)}) %collective-permute-start.23) | collective-permute-done | bytes 131104 | tf_op jit(solution)/shard_map/ppermute | solution.py:335
  64.0 4.4 %attend.1 = (bf16[4,64,512]{2,1,0:T(8,128)(2,1)S(1)}, bf16[4,64,512]{2,1,0:T(8,128)(2,1)S(1)}) custom-call(bf16[128,512]{1,0:T(8,128)(2,1)S(1)} %collective-permute-done.13.refs_0_, bf16[128,512]{1,0:T(8,128)(2,1)S(1)} %collective-permute-done.17.refs_1_, bf16[128,512]{1,0:T(8,128)(2,1)S(1)} %collective-permute-done.18.refs_2_, ...), custom_call_target="tpu_custom_call" | custom-call | flops 2684354560 | bytes 3145728 | tf_op jit(solution)/shard_map/attend/pallas_call | solution.py:306
  68.4 2.9 %collective-permute-start.24 = (bf16[4,64,512]{2,1,0:T(8,128)(2,1)S(1)}, bf16[4,64,512]{2,1,0:T(8,128)(2,1)S(1)}, u32[]{:S(2)}, u32[]{:S(2)}) collective-permute-start(bf16[4,64,512]{2,1,0:T(8,128)(2,1)S(1)} %get-tuple-element.33), channel_id=1, source_target_pairs={{1,0},{0,1},{5,2},{4,3},{3,4},{2,5},{7,6},{6,7},{9,8},{8,9},{13,10... | collective-permute-start | bytes 786440 | tf_op jit(solution)/shard_map/ppermute | solution.py:403
  71.3 2.2 %collective-permute-start.25 = (bf16[4,64,512]{2,1,0:T(8,128)(2,1)S(1)}, bf16[4,64,512]{2,1,0:T(8,128)(2,1)S(1)}, u32[]{:S(2)}, u32[]{:S(2)}) collective-permute-start(bf16[4,64,512]{2,1,0:T(8,128)(2,1)S(1)} %get-tuple-element.34), channel_id=1, source_target_pairs={{0,0},{1,1},{4,2},{5,3},{2,4},{3,5},{6,6},{7,7},{8,8},{9,9},{12,10... | collective-permute-start | bytes 786440 | tf_op jit(solution)/shard_map/ppermute | solution.py:403
  73.5 5.1 %collective-permute-done.24 = bf16[4,64,512]{2,1,0:T(8,128)(2,1)S(1)} collective-permute-done((bf16[4,64,512]{2,1,0:T(8,128)(2,1)S(1)}, bf16[4,64,512]{2,1,0:T(8,128)(2,1)S(1)}, u32[]{:S(2)}, u32[]{:S(2)}) %collective-permute-start.24) | collective-permute-done | bytes 262176 | tf_op jit(solution)/shard_map/ppermute | solution.py:403
  78.7 5.4 %collective-permute-done.25 = bf16[4,64,512]{2,1,0:T(8,128)(2,1)S(1)} collective-permute-done((bf16[4,64,512]{2,1,0:T(8,128)(2,1)S(1)}, bf16[4,64,512]{2,1,0:T(8,128)(2,1)S(1)}, u32[]{:S(2)}, u32[]{:S(2)}) %collective-permute-start.25) | collective-permute-done | bytes 262176 | tf_op jit(solution)/shard_map/ppermute | solution.py:403
  84.1 0.8 pad_maximum_fusion
  (11 shorter events, 0.1 us)
Async XLA Ops:
  0.0 12.7 %collective-permute-start = (bf16[9,3,64,512]{3,2,1,0:T(8,128)(2,1)}, bf16[9,3,64,512]{3,2,1,0:T(8,128)(2,1)S(1)}, u32[]{:S(2)}, u32[]{:S(2)}) collective-permute-start(bf16[9,3,64,512]{3,2,1,0:T(8,128)(2,1)} %bitcast.8), channel_id=1, source_target_pairs={{0,4},{1,5},{2,6},{3,7},{4,0},{5,1},{6,2},{7,3},{8,12},{9,13},{10,... | collective-permute-start | bytes 5308424 | tf_op jit(solution)/shard_map/ppermute | solution.py:335
  1.2 6.6 %collective-permute-start.2 = (bf16[2,4,64,128]{3,2,1,0:T(8,128)(2,1)S(1)}, bf16[2,4,64,128]{3,2,1,0:T(8,128)(2,1)S(1)}, u32[]{:S(2)}, u32[]{:S(2)}) collective-permute-start(bf16[2,4,64,128]{3,2,1,0:T(8,128)(2,1)S(1)} %get-tuple-element.38), channel_id=1, source_target_pairs={{0,8},{1,9},{2,10},{3,11},{4,12},{5,13},{6,14},{7,15},{8,0},{9,1},... | collective-permute-start | bytes 393224 | tf_op jit(solution)/shard_map/ppermute | solution.py:335
  3.9 6.5 %collective-permute-start.4 = (bf16[2,4,64,128]{3,2,1,0:T(8,128)(2,1)S(1)}, bf16[2,4,64,128]{3,2,1,0:T(8,128)(2,1)S(1)}, u32[]{:S(2)}, u32[]{:S(2)}) collective-permute-start(bf16[2,4,64,128]{3,2,1,0:T(8,128)(2,1)S(1)} %get-tuple-element.40), channel_id=1, source_target_pairs={{0,16},{1,17},{2,18},{3,19},{4,20},{5,21},{6,22},{7,23},{8,24},{9,... | collective-permute-start | bytes 393224 | tf_op jit(solution)/shard_map/ppermute | solution.py:335
  5.2 7.5 %collective-permute-start.6 = (bf16[2,4,64,128]{3,2,1,0:T(8,128)(2,1)S(1)}, bf16[2,4,64,128]{3,2,1,0:T(8,128)(2,1)S(1)}, u32[]{:S(2)}, u32[]{:S(2)}) collective-permute-start(bf16[2,4,64,128]{3,2,1,0:T(8,128)(2,1)S(1)} %get-tuple-element.37), channel_id=1, source_target_pairs={{0,24},{1,25},{2,26},{3,27},{4,28},{5,29},{6,30},{7,31},{8,16},{9,... | collective-permute-start | bytes 393224 | tf_op jit(solution)/shard_map/ppermute | solution.py:335
  5.2 9.9 %collective-permute-start.1 = (bf16[2,4,64,128]{3,2,1,0:T(8,128)(2,1)S(1)}, bf16[2,4,64,128]{3,2,1,0:T(8,128)(2,1)S(1)}, u32[]{:S(2)}, u32[]{:S(2)}) collective-permute-start(bf16[2,4,64,128]{3,2,1,0:T(8,128)(2,1)S(1)} %get-tuple-element.39.refs_0_.refs_2_), channel_id=1, source_target_pairs={{0,4},{1,5},{2,6},{3,7},{4,0},{5,1},{6,2},{7,3},{8,12},{9,13},{10,... | collective-permute-start | bytes 393224 | tf_op jit(solution)/shard_map/ppermute | solution.py:335
  7.8 7.3 %collective-permute-start.3 = (bf16[2,4,64,128]{3,2,1,0:T(8,128)(2,1)S(1)}, bf16[2,4,64,128]{3,2,1,0:T(8,128)(2,1)S(1)}, u32[]{:S(2)}, u32[]{:S(2)}) collective-permute-start(bf16[2,4,64,128]{3,2,1,0:T(8,128)(2,1)S(1)} %collective-permute-done.2.refs_1_.refs_2_), channel_id=1, source_target_pairs={{0,4},{1,5},{2,6},{3,7},{4,0},{5,1},{6,2},{7,3},{8,12},{9,13},{10,... | collective-permute-start | bytes 393224 | tf_op jit(solution)/shard_map/ppermute | solution.py:335
  10.5 4.7 %collective-permute-start.5 = (bf16[2,4,64,128]{3,2,1,0:T(8,128)(2,1)S(1)}, bf16[2,4,64,128]{3,2,1,0:T(8,128)(2,1)S(1)}, u32[]{:S(2)}, u32[]{:S(2)}) collective-permute-start(bf16[2,4,64,128]{3,2,1,0:T(8,128)(2,1)S(1)} %collective-permute-done.4.refs_2_.refs_3_), channel_id=1, source_target_pairs={{0,4},{1,5},{2,6},{3,7},{4,0},{5,1},{6,2},{7,3},{8,12},{9,13},{10,... | collective-permute-start | bytes 393224 | tf_op jit(solution)/shard_map/ppermute | solution.py:335
  12.7 2.5 %collective-permute-start.7 = (bf16[2,4,64,128]{3,2,1,0:T(8,128)(2,1)S(1)}, bf16[2,4,64,128]{3,2,1,0:T(8,128)(2,1)S(1)}, u32[]{:S(2)}, u32[]{:S(2)}) collective-permute-start(bf16[2,4,64,128]{3,2,1,0:T(8,128)(2,1)S(1)} %collective-permute-done.6.refs_2_.refs_3_.refs_4_), channel_id=1, source_target_pairs={{0,4},{1,5},{2,6},{3,7},{4,0},{5,1},{6,2},{7,3},{8,12},{9,13},{10,... | collective-permute-start | bytes 393224 | tf_op jit(solution)/shard_map/ppermute | solution.py:335
  12.7 1.5 %copy-start = (bf16[27,64,512]{2,1,0:T(8,128)(2,1)S(1)}, bf16[27,64,512]{2,1,0:T(8,128)(2,1)}, u32[]{:S(2)}) copy-start(bf16[27,64,512]{2,1,0:T(8,128)(2,1)} %param.7) | copy-start | bytes 5308420
  17.0 10.1 %collective-permute-start.8 = (bf16[8,2,64,128]{3,2,1,0:T(8,128)(2,1)S(1)}, bf16[8,2,64,128]{3,2,1,0:T(8,128)(2,1)S(1)}, u32[]{:S(2)}, u32[]{:S(2)}) collective-permute-start(bf16[8,2,64,128]{3,2,1,0:T(8,128)(2,1)S(1)} %get-tuple-element.20), channel_id=1, source_target_pairs={{0,1},{1,2},{2,3},{4,5},{5,6},{6,7},{8,9},{9,10},{10,11},{12,13},{... | collective-permute-start | bytes 786440 | tf_op jit(solution)/shard_map/ppermute | solution.py:335
  20.2 8.9 %collective-permute-start.9 = (bf16[8,2,64,128]{3,2,1,0:T(8,128)(2,1)S(1)}, bf16[8,2,64,128]{3,2,1,0:T(8,128)(2,1)S(1)}, u32[]{:S(2)}, u32[]{:S(2)}) collective-permute-start(bf16[8,2,64,128]{3,2,1,0:T(8,128)(2,1)S(1)} %get-tuple-element.21), channel_id=1, source_target_pairs={{1,0},{2,1},{3,2},{5,4},{6,5},{7,6},{9,8},{10,9},{11,10},{13,12},{... | collective-permute-start | bytes 786440 | tf_op jit(solution)/shard_map/ppermute | solution.py:335
  24.3 12.7 %collective-permute-start.11 = (bf16[256,512]{1,0:T(8,128)(2,1)S(1)}, bf16[256,512]{1,0:T(8,128)(2,1)S(1)}, u32[]{:S(2)}, u32[]{:S(2)}) collective-permute-start(bf16[256,512]{1,0:T(8,128)(2,1)S(1)} %get-tuple-element.25), channel_id=1, source_target_pairs={{0,16},{1,17},{2,18},{3,19},{4,20},{5,21},{6,22},{7,23},{8,24},{9,... | collective-permute-start | bytes 786440 | tf_op jit(solution)/shard_map/ppermute | solution.py:335
  25.6 15.8 %collective-permute-start.10 = (bf16[256,512]{1,0:T(8,128)(2,1)S(1)}, bf16[256,512]{1,0:T(8,128)(2,1)S(1)}, u32[]{:S(2)}, u32[]{:S(2)}) collective-permute-start(bf16[256,512]{1,0:T(8,128)(2,1)S(1)} %conv_inner.2.refs_8_), channel_id=1, source_target_pairs={{0,24},{1,25},{2,26},{3,27},{4,28},{5,29},{6,30},{7,31},{8,16},{9,... | collective-permute-start | bytes 786440 | tf_op jit(solution)/shard_map/ppermute | solution.py:335
  26.5 14.9 %collective-permute-start.12 = (bf16[256,512]{1,0:T(8,128)(2,1)S(1)}, bf16[256,512]{1,0:T(8,128)(2,1)S(1)}, u32[]{:S(2)}, u32[]{:S(2)}) collective-permute-start(bf16[256,512]{1,0:T(8,128)(2,1)S(1)} %get-tuple-element.22.refs_11_), channel_id=1, source_target_pairs={{0,8},{1,9},{2,10},{3,11},{4,12},{5,13},{6,14},{7,15},{8,0},{9,1},... | collective-permute-start | bytes 786440 | tf_op jit(solution)/shard_map/ppermute | solution.py:335
  33.0 18.6 %collective-permute-start.14 = (bf16[256,512]{1,0:T(8,128)(2,1)S(1)}, bf16[256,512]{1,0:T(8,128)(2,1)S(1)}, u32[]{:S(2)}, u32[]{:S(2)}) collective-permute-start(bf16[256,512]{1,0:T(8,128)(2,1)S(1)} %get-tuple-element.28), channel_id=1, source_target_pairs={{0,24},{1,25},{2,26},{3,27},{4,28},{5,29},{6,30},{7,31},{8,16},{9,... | collective-permute-start | bytes 786440 | tf_op jit(solution)/shard_map/ppermute | solution.py:335
  34.3 17.3 %collective-permute-start.15 = (bf16[256,512]{1,0:T(8,128)(2,1)S(1)}, bf16[256,512]{1,0:T(8,128)(2,1)S(1)}, u32[]{:S(2)}, u32[]{:S(2)}) collective-permute-start(bf16[256,512]{1,0:T(8,128)(2,1)S(1)} %get-tuple-element.29), channel_id=1, source_target_pairs={{0,16},{1,17},{2,18},{3,19},{4,20},{5,21},{6,22},{7,23},{8,24},{9,... | collective-permute-start | bytes 786440 | tf_op jit(solution)/shard_map/ppermute | solution.py:335
  37.1 14.5 %collective-permute-start.16 = (bf16[256,512]{1,0:T(8,128)(2,1)S(1)}, bf16[256,512]{1,0:T(8,128)(2,1)S(1)}, u32[]{:S(2)}, u32[]{:S(2)}) collective-permute-start(bf16[256,512]{1,0:T(8,128)(2,1)S(1)} %get-tuple-element.23.refs_9_), channel_id=1, source_target_pairs={{0,8},{1,9},{2,10},{3,11},{4,12},{5,13},{6,14},{7,15},{8,0},{9,1},... | collective-permute-start | bytes 786440 | tf_op jit(solution)/shard_map/ppermute | solution.py:335
  41.4 22.6 %copy-start.1 = (bf16[512,512]{1,0:T(8,128)(2,1)S(1)}, bf16[512,512]{1,0:T(8,128)(2,1)}, u32[]{:S(2)}) copy-start(bf16[512,512]{1,0:T(8,128)(2,1)} %refs_8_.1) | copy-start | bytes 1572868
  41.4 22.6 %copy-start.2 = (bf16[512,512]{1,0:T(8,128)(2,1)S(1)}, bf16[512,512]{1,0:T(8,128)(2,1)}, u32[]{:S(2)}) copy-start(bf16[512,512]{1,0:T(8,128)(2,1)} %refs_9_.1) | copy-start | bytes 1572868
  41.4 22.6 %copy-start.3 = (bf16[512,512]{1,0:T(8,128)(2,1)S(1)}, bf16[512,512]{1,0:T(8,128)(2,1)}, u32[]{:S(2)}) copy-start(bf16[512,512]{1,0:T(8,128)(2,1)} %refs_10_.1) | copy-start | bytes 1572868
  41.4 22.6 %copy-start.4 = (bf16[512,512]{1,0:T(8,128)(2,1)S(1)}, bf16[512,512]{1,0:T(8,128)(2,1)}, u32[]{:S(2)}) copy-start(bf16[512,512]{1,0:T(8,128)(2,1)} %refs_11_.1) | copy-start | bytes 1572868
  41.6 15.8 %collective-permute-start.13 = (bf16[128,512]{1,0:T(8,128)(2,1)S(1)}, bf16[128,512]{1,0:T(8,128)(2,1)S(1)}, u32[]{:S(2)}, u32[]{:S(2)}) collective-permute-start(bf16[128,512]{1,0:T(8,128)(2,1)S(1)} %get-tuple-element.26), channel_id=1, source_target_pairs={{0,0},{1,1},{2,4},{3,5},{4,2},{5,3},{6,6},{7,7},{8,8},{9,9},{10,12... | collective-permute-start | bytes 393224 | tf_op jit(solution)/shard_map/ppermute | solution.py:335
  50.5 7.6 %collective-permute-start.18 = (bf16[128,512]{1,0:T(8,128)(2,1)S(1)}, bf16[128,512]{1,0:T(8,128)(2,1)S(1)}, u32[]{:S(2)}, u32[]{:S(2)}) collective-permute-start(bf16[128,512]{1,0:T(8,128)(2,1)S(1)} %get-tuple-element.31), channel_id=1, source_target_pairs={{0,1},{1,0},{2,5},{3,4},{4,3},{5,2},{6,7},{7,6},{8,9},{9,8},{10,13... | collective-permute-start | bytes 393224 | tf_op jit(solution)/shard_map/ppermute | solution.py:335
  51.8 8.9 %collective-permute-start.17 = (bf16[128,512]{1,0:T(8,128)(2,1)S(1)}, bf16[128,512]{1,0:T(8,128)(2,1)S(1)}, u32[]{:S(2)}, u32[]{:S(2)}) collective-permute-start(bf16[128,512]{1,0:T(8,128)(2,1)S(1)} %get-tuple-element.30), channel_id=1, source_target_pairs={{0,0},{1,1},{2,4},{3,5},{4,2},{5,3},{6,6},{7,7},{8,8},{9,9},{10,12... | collective-permute-start | bytes 393224 | tf_op jit(solution)/shard_map/ppermute | solution.py:335
  56.3 6.4 %collective-permute-start.19 = (bf16[128,512]{1,0:T(8,128)(2,1)S(1)}, bf16[128,512]{1,0:T(8,128)(2,1)S(1)}, u32[]{:S(2)}, u32[]{:S(2)}) collective-permute-start(bf16[128,512]{1,0:T(8,128)(2,1)S(1)} %get-tuple-element.32), channel_id=1, source_target_pairs={{0,1},{1,0},{2,5},{3,4},{4,3},{5,2},{6,7},{7,6},{8,9},{9,8},{10,13... | collective-permute-start | bytes 393224 | tf_op jit(solution)/shard_map/ppermute | solution.py:335
  57.4 5.3 %collective-permute-start.20 = (bf16[128,512]{1,0:T(8,128)(2,1)S(1)}, bf16[128,512]{1,0:T(8,128)(2,1)S(1)}, u32[]{:S(2)}, u32[]{:S(2)}) collective-permute-start(bf16[128,512]{1,0:T(8,128)(2,1)S(1)} %collective-permute-done.13.refs_0_), channel_id=1, source_target_pairs={{0,4},{1,5},{2,6},{3,7},{4,0},{5,1},{6,2},{7,3},{8,12},{9,13},{10,... | collective-permute-start | bytes 393224 | tf_op jit(solution)/shard_map/ppermute | solution.py:335
  58.1 4.6 %collective-permute-start.22 = (bf16[128,512]{1,0:T(8,128)(2,1)S(1)}, bf16[128,512]{1,0:T(8,128)(2,1)S(1)}, u32[]{:S(2)}, u32[]{:S(2)}) collective-permute-start(bf16[128,512]{1,0:T(8,128)(2,1)S(1)} %collective-permute-done.18.refs_2_), channel_id=1, source_target_pairs={{0,4},{1,5},{2,6},{3,7},{4,0},{5,1},{6,2},{7,3},{8,12},{9,13},{10,... | collective-permute-start | bytes 393224 | tf_op jit(solution)/shard_map/ppermute | solution.py:335
  60.7 2.0 %collective-permute-start.21 = (bf16[128,512]{1,0:T(8,128)(2,1)S(1)}, bf16[128,512]{1,0:T(8,128)(2,1)S(1)}, u32[]{:S(2)}, u32[]{:S(2)}) collective-permute-start(bf16[128,512]{1,0:T(8,128)(2,1)S(1)} %collective-permute-done.17.refs_1_), channel_id=1, source_target_pairs={{0,4},{1,5},{2,6},{3,7},{4,0},{5,1},{6,2},{7,3},{8,12},{9,13},{10,... | collective-permute-start | bytes 393224 | tf_op jit(solution)/shard_map/ppermute | solution.py:335
  62.6 1.3 %collective-permute-start.23 = (bf16[128,512]{1,0:T(8,128)(2,1)S(1)}, bf16[128,512]{1,0:T(8,128)(2,1)S(1)}, u32[]{:S(2)}, u32[]{:S(2)}) collective-permute-start(bf16[128,512]{1,0:T(8,128)(2,1)S(1)} %collective-permute-done.19.refs_3_), channel_id=1, source_target_pairs={{0,4},{1,5},{2,6},{3,7},{4,0},{5,1},{6,2},{7,3},{8,12},{9,13},{10,... | collective-permute-start | bytes 393224 | tf_op jit(solution)/shard_map/ppermute | solution.py:335
  68.4 10.3 %collective-permute-start.24 = (bf16[4,64,512]{2,1,0:T(8,128)(2,1)S(1)}, bf16[4,64,512]{2,1,0:T(8,128)(2,1)S(1)}, u32[]{:S(2)}, u32[]{:S(2)}) collective-permute-start(bf16[4,64,512]{2,1,0:T(8,128)(2,1)S(1)} %get-tuple-element.33), channel_id=1, source_target_pairs={{1,0},{0,1},{5,2},{4,3},{3,4},{2,5},{7,6},{6,7},{9,8},{8,9},{13,10... | collective-permute-start | bytes 786440 | tf_op jit(solution)/shard_map/ppermute | solution.py:403
  71.3 12.8 %collective-permute-start.25 = (bf16[4,64,512]{2,1,0:T(8,128)(2,1)S(1)}, bf16[4,64,512]{2,1,0:T(8,128)(2,1)S(1)}, u32[]{:S(2)}, u32[]{:S(2)}) collective-permute-start(bf16[4,64,512]{2,1,0:T(8,128)(2,1)S(1)} %get-tuple-element.34), channel_id=1, source_target_pairs={{0,0},{1,1},{4,2},{5,3},{2,4},{3,5},{6,6},{7,7},{8,8},{9,9},{12,10... | collective-permute-start | bytes 786440 | tf_op jit(solution)/shard_map/ppermute | solution.py:403

commit v14 on v12

--- a/solution.py
+++ b/solution.py
@@ -406,7 +406,7 @@
     rims = stack_call(rims, inner_sent[0])
     rims = (rims, permute(rims, to_member(1)))
     rim_sent = conv(
-        [(3, True), (1, True)], rims=rims, out_type=jnp.bfloat16, after=inner_got[:2]
+        [(3, True), (1, True)], rims=rims, out_type=jnp.bfloat16, after=inner_got[:0]
     )
     rim_got = hop(rim_sent)
     inner_on, inner_own = conv(

time: 86.4 us -> 82.2 us (0.951)
  waiting for transfers between devices: 25.9 us -> 22.9 us
  starting transfers between devices: 37.7 us -> 36.5 us
    ppermute x28, waiting for transfers between devices: 15.3 us -> 12.4 us  [permute(): return lax.ppermute(block, BOTH, everywhere(sizes, target))]
    ppermute x28, starting transfers between devices: 32.8 us -> 31.6 us  [permute(): return lax.ppermute(block, BOTH, everywhere(sizes, target))]
  transfers between devices with their start and end apart: 30 -> 30, of which waited for: 10 -> 9; matrix products, arithmetic and copies ran while one was open for 3% -> 3% of each run, Pallas kernels for 12% -> 16%
where the time goes in v14:
time: 82.2 us; the launch traced here: 81.9 us
  starting transfers between devices  36.5 us (44%)
  waiting for transfers between devices  22.9 us (28%)
  Pallas kernels  17.6 us (21%)
  local copies, waits for them, and re-layouts  3.63 us (4%)
  other arithmetic  0.96 us (1%)
    ppermute x28, starting transfers between devices, permute(): return lax.ppermute(block, BOTH, everywhere(sizes, target))  31.6 us
    ppermute x28, waiting for transfers between devices, permute(): return lax.ppermute(block, BOTH, everywhere(sizes, target))  12.4 us
    pallas_call x4, Pallas kernels, conv_call(): pl.pallas_call(functools.partial(conv_kernel, tuple(jobs), parts, group,...  11.4 us
    ppermute x2, waiting for transfers between devices, body(): back.append(lax.ppermute(done[p], BOTH, pairs))  10.6 us
    ppermute x2, starting transfers between devices, body(): back.append(lax.ppermute(done[p], BOTH, pairs))  4.92 us
    pallas_call x1, Pallas kernels, attend_call(): pl.pallas_call(functools.partial(attend_kernel, frames, share, chunks), o...  4.45 us
  transfers between devices with their start and end apart: 30, of which 9 were waited for; matrix products, arithmetic and copies ran while one was open for 3% of the time, Pallas kernels for 16%

profile of v14, /device:TPU:1, one launch (start us, length us, event | category | flops | bytes accessed | tf_op | source)
XLA Modules:
  0.0 81.9 jit_solution(15518794422100888443)
XLA Ops:
  0.0 0.1 collective-permute-start.1
  0.1 1.1 %constant_dynamic-slice_fusion = (bf16[2,4,64,128]{3,2,1,0:T(8,128)(2,1)S(1)}, bf16[2,4,64,128]{3,2,1,0:T(8,128)(2,1)S(1)}, bf16[2,4,64,128]{3,2,1,0:T(8,128)(2,1)S(1)}, bf16[2,4,64,128]{3,2,1,0:T(8,128)(2,1)S(1)}) fusion(bf16[2,4,64,512]{3,2,1,0:T(8,128)(2,1)} %param.6, s32[]{:T(128)S(6)} %select_n.75, s32[]{:T(128)S(6)} %select_n.74, s32[]{:T(128)S(6)} %select_n.72, ...), kind=kLoop, calls=%fused_computation.5 | loop fusion | bytes 1048592 | tf_op jit(solution)/shard_map/dynamic_slice | solution.py:383
  1.2 2.7 %collective-permute-start = (bf16[2,4,64,128]{3,2,1,0:T(8,128)(2,1)S(1)}, bf16[2,4,64,128]{3,2,1,0:T(8,128)(2,1)S(1)}, u32[]{:S(2)}, u32[]{:S(2)}) collective-permute-start(bf16[2,4,64,128]{3,2,1,0:T(8,128)(2,1)S(1)} %get-tuple-element.52), channel_id=1, source_target_pairs={{0,16},{1,17},{2,18},{3,19},{4,12},{5,13},{6,14},{7,15},{8,24},{9,... | collective-permute-start | bytes 393224 | tf_op jit(solution)/shard_map/ppermute | solution.py:364
  3.9 1.2 %collective-permute-start.3 = (bf16[2,4,64,128]{3,2,1,0:T(8,128)(2,1)S(1)}, bf16[2,4,64,128]{3,2,1,0:T(8,128)(2,1)S(1)}, u32[]{:S(2)}, u32[]{:S(2)}) collective-permute-start(bf16[2,4,64,128]{3,2,1,0:T(8,128)(2,1)S(1)} %get-tuple-element.50), channel_id=1, source_target_pairs={{0,8},{1,9},{2,10},{3,11},{4,20},{5,21},{6,22},{7,23},{8,0},{9,1},... | collective-permute-start | bytes 393224 | tf_op jit(solution)/shard_map/ppermute | solution.py:364
  5.2 0.0 collective-permute-start.6
  5.2 1.0 %slice_bitcast_fusion = (bf16[2,64,512]{2,1,0:T(8,128)(2,1)S(1)}, bf16[2,64,512]{2,1,0:T(8,128)(2,1)S(1)}) fusion(bf16[2,4,64,512]{3,2,1,0:T(8,128)(2,1)} %param.6), kind=kLoop, calls=%fused_computation.3 | loop fusion | bytes 524288 | tf_op jit(solution)/shard_map/squeeze | solution.py:377
  6.2 3.4 %collective-permute-start.8 = (bf16[2,64,512]{2,1,0:T(8,128)(2,1)S(1)}, bf16[2,64,512]{2,1,0:T(8,128)(2,1)S(1)}, u32[]{:S(2)}, u32[]{:S(2)}) collective-permute-start(bf16[2,64,512]{2,1,0:T(8,128)(2,1)S(1)} %get-tuple-element.48), channel_id=1, source_target_pairs={{0,1},{1,2},{2,3},{4,5},{5,6},{6,7},{8,9},{9,10},{10,11},{12,13},{... | collective-permute-start | bytes 393224 | tf_op jit(solution)/shard_map/ppermute | solution.py:364
  9.6 0.1 pad_add_fusion.refs_0_.meta
  9.7 1.3 %collective-permute-start.9 = (bf16[2,64,512]{2,1,0:T(8,128)(2,1)S(1)}, bf16[2,64,512]{2,1,0:T(8,128)(2,1)S(1)}, u32[]{:S(2)}, u32[]{:S(2)}) collective-permute-start(bf16[2,64,512]{2,1,0:T(8,128)(2,1)S(1)} %get-tuple-element.47), channel_id=1, source_target_pairs={{1,0},{2,1},{3,2},{5,4},{6,5},{7,6},{9,8},{10,9},{11,10},{13,12},{... | collective-permute-start | bytes 393224 | tf_op jit(solution)/shard_map/ppermute | solution.py:364
  11.0 0.0 copy-start
  11.0 1.5 %copy-done = bf16[27,64,512]{2,1,0:T(8,128)(2,1)S(1)} copy-done((bf16[27,64,512]{2,1,0:T(8,128)(2,1)S(1)}, bf16[27,64,512]{2,1,0:T(8,128)(2,1)}, u32[]{:S(2)}) %copy-start) | copy-done | bytes 1769496
  12.4 0.9 %merge_kernel_slices.1.refs_1_ = bf16[3,9,128,512]{3,2,1,0:T(8,128)(2,1)S(1)} custom-call(s32[3]{0:T(128)S(1)} %pad_add_fusion.refs_0_.meta, bf16[9,3,64,512]{3,2,1,0:T(8,128)(2,1)S(1)} %bitcast.17, bf16[9,3,64,512]{3,2,1,0:T(8,128)(2,1)S(1)} %collective-permute-done.1.refs_2_), custom_call_target="tpu_custom_call" | custom-call | tf_op jit(solution)/shard_map/merge_kernel_slices/pallas_call | solution.py:58
  13.3 0.0 collective-permute-done.refs_3_
  13.3 1.2 %collective-permute-start.2 = (bf16[2,4,64,128]{3,2,1,0:T(8,128)(2,1)S(1)}, bf16[2,4,64,128]{3,2,1,0:T(8,128)(2,1)S(1)}, u32[]{:S(2)}, u32[]{:S(2)}) collective-permute-start(bf16[2,4,64,128]{3,2,1,0:T(8,128)(2,1)S(1)} %get-tuple-element.51.refs_2_), channel_id=1, source_target_pairs={{0,4},{1,5},{2,6},{3,7},{4,0},{5,1},{6,2},{7,3},{8,12},{9,13},{10,... | collective-permute-start | bytes 393224 | tf_op jit(solution)/shard_map/ppermute | solution.py:364
  14.5 0.0 collective-permute-done.3.refs_2_
  14.5 0.1 collective-permute-start.4
  14.6 0.4 collective-permute-start.7
  15.0 0.0 collective-permute-done.8.above
  15.0 0.1 collective-permute-start.5
  15.1 0.3 collective-permute-done.9.below
  15.4 0.6 split_halo_rows.1
  16.0 1.3 %collective-permute-start.10 = (bf16[2,2,64,128]{3,2,1,0:T(8,128)(2,1)S(1)}, bf16[2,2,64,128]{3,2,1,0:T(8,128)(2,1)S(1)}, u32[]{:S(2)}, u32[]{:S(2)}) collective-permute-start(bf16[2,2,64,128]{3,2,1,0:T(8,128)(2,1)S(1)} %get-tuple-element.28), channel_id=1, source_target_pairs={{0,8},{1,9},{2,10},{3,11},{4,20},{5,21},{6,22},{7,23},{8,0},{9,1},... | collective-permute-start | bytes 196616 | tf_op jit(solution)/shard_map/ppermute | solution.py:364
  17.3 0.0 collective-permute-done.2.refs_4_
  17.3 1.2 %collective-permute-start.11 = (bf16[2,2,64,128]{3,2,1,0:T(8,128)(2,1)S(1)}, bf16[2,2,64,128]{3,2,1,0:T(8,128)(2,1)S(1)}, u32[]{:S(2)}, u32[]{:S(2)}) collective-permute-start(bf16[2,2,64,128]{3,2,1,0:T(8,128)(2,1)S(1)} %get-tuple-element.29), channel_id=1, source_target_pairs={{0,16},{1,17},{2,18},{3,19},{4,12},{5,13},{6,14},{7,15},{8,24},{9,... | collective-permute-start | bytes 196616 | tf_op jit(solution)/shard_map/ppermute | solution.py:364
  18.5 0.2 collective-permute-start.12
  18.7 0.0 collective-permute-done.7.refs_7_
  18.7 0.0 collective-permute-done.5.refs_6_
  18.7 2.9 %conv_inner.2 = (bf16[256,512]{1,0:T(8,128)(2,1)S(1)}, bf16[256,512]{1,0:T(8,128)(2,1)S(1)}) custom-call(s32[3]{0:T(128)S(1)} %pad_add_fusion.refs_0_.meta, bf16[3,9,128,512]{3,2,1,0:T(8,128)(2,1)S(1)} %merge_kernel_slices.1.refs_1_, bf16[2,4,64,128]{3,2,1,0:T(8,128)(2,1)S(1)} %collective-permute-done.3.refs_2_, ...), custom_call_target="tpu_custom_call" | custom-call | flops 1811939328 | bytes 3538944 | tf_op jit(solution)/shard_map/conv_inner/pallas_call | solution.py:200
  21.6 0.0 collective-permute-done.10.refs_1_
  21.6 1.3 %collective-permute-done.12.refs_3_ = bf16[2,2,64,128]{3,2,1,0:T(8,128)(2,1)S(1)} collective-permute-done((bf16[2,2,64,128]{3,2,1,0:T(8,128)(2,1)S(1)}, bf16[2,2,64,128]{3,2,1,0:T(8,128)(2,1)S(1)}, u32[]{:S(2)}, u32[]{:S(2)}) %collective-permute-start.12) | collective-permute-done | bytes 65568 | tf_op jit(solution)/shard_map/ppermute | solution.py:364
  22.9 3.7 %collective-permute-start.13 = (bf16[4,2,2,64,128]{4,3,2,1,0:T(8,128)(2,1)S(1)}, bf16[4,2,2,64,128]{4,3,2,1,0:T(8,128)(2,1)S(1)}, u32[]{:S(2)}, u32[]{:S(2)}) collective-permute-start(bf16[4,2,2,64,128]{4,3,2,1,0:T(8,128)(2,1)S(1)} %stack_halo_rows.1.refs_8_), channel_id=1, source_target_pairs={{0,4},{1,5},{2,6},{3,7},{4,0},{5,1},{6,2},{7,3},{8,12},{9,13},{10,... | collective-permute-start | bytes 786440 | tf_op jit(solution)/shard_map/ppermute | solution.py:364
  26.6 0.2 collective-permute-start.15
  26.8 1.2 %collective-permute-start.14 = (bf16[256,512]{1,0:T(8,128)(2,1)S(1)}, bf16[256,512]{1,0:T(8,128)(2,1)S(1)}, u32[]{:S(2)}, u32[]{:S(2)}) collective-permute-start(bf16[256,512]{1,0:T(8,128)(2,1)S(1)} %get-tuple-element.34), channel_id=1, source_target_pairs={{0,8},{1,9},{2,10},{3,11},{4,20},{5,21},{6,22},{7,23},{8,0},{9,1},... | collective-permute-start | bytes 786440 | tf_op jit(solution)/shard_map/ppermute | solution.py:364
  28.0 0.0 collective-permute-done.13.refs_9_
  28.0 2.9 %conv_rim.2 = (bf16[256,512]{1,0:T(8,128)(2,1)S(1)}, bf16[256,512]{1,0:T(8,128)(2,1)S(1)}) custom-call(s32[3]{0:T(128)S(1)} %pad_add_fusion.refs_0_.meta, bf16[3,9,128,512]{3,2,1,0:T(8,128)(2,1)S(1)} %merge_kernel_slices.1.refs_1_, bf16[2,4,64,128]{3,2,1,0:T(8,128)(2,1)S(1)} %collective-permute-done.3.refs_2_, ...), custom_call_target="tpu_custom_call" | custom-call | flops 1811939328 | bytes 3538944 | tf_op jit(solution)/shard_map/conv_rim/pallas_call | solution.py:200
  30.9 0.3 collective-permute-start.17
  31.2 1.2 %collective-permute-start.19 = (bf16[256,512]{1,0:T(8,128)(2,1)S(1)}, bf16[256,512]{1,0:T(8,128)(2,1)S(1)}, u32[]{:S(2)}, u32[]{:S(2)}) collective-permute-start(bf16[256,512]{1,0:T(8,128)(2,1)S(1)} %get-tuple-element.39), channel_id=1, source_target_pairs={{0,8},{1,9},{2,10},{3,11},{4,20},{5,21},{6,22},{7,23},{8,0},{9,1},... | collective-permute-start | bytes 786440 | tf_op jit(solution)/shard_map/ppermute | solution.py:364
  32.4 2.8 %conv_inner.3 = (f32[256,512]{1,0:T(8,128)S(1)}, f32[256,512]{1,0:T(8,128)S(1)}) custom-call(s32[3]{0:T(128)S(1)} %pad_add_fusion.refs_0_.meta, bf16[3,9,128,512]{3,2,1,0:T(8,128)(2,1)S(1)} %merge_kernel_slices.1.refs_1_, bf16[2,4,64,128]{3,2,1,0:T(8,128)(2,1)S(1)} %get-tuple-element.51.refs_2_, bf16[2,4,64,128]{3,2,1,0:T(8,128)(2,1)S(1)} %collective-permute-done.refs_3_, ...), custom_call_target="tpu_custom_call" | custom-call | flops 1811939328 | bytes 3538944 | tf_op jit(solution)/shard_map/conv_inner/pallas_call | solution.py:200
  35.4 0.3 collective-permute-start.16
  35.7 2.9 %conv_rim.3 = (f32[256,512]{1,0:T(8,128)S(1)}, f32[256,512]{1,0:T(8,128)S(1)}) custom-call(s32[3]{0:T(128)S(1)} %pad_add_fusion.refs_0_.meta, bf16[3,9,128,512]{3,2,1,0:T(8,128)(2,1)S(1)} %merge_kernel_slices.1.refs_1_, bf16[2,4,64,128]{3,2,1,0:T(8,128)(2,1)S(1)} %get-tuple-element.51.refs_2_, bf16[2,4,64,128]{3,2,1,0:T(8,128)(2,1)S(1)} %collective-permute-done.refs_3_, ...), custom_call_target="tpu_custom_call" | custom-call | flops 1811939328 | bytes 3538944 | tf_op jit(solution)/shard_map/conv_rim/pallas_call | solution.py:200
  38.5 0.0 copy-start.1
  38.6 0.0 copy-start.2
  38.6 0.0 copy-start.3
  38.6 0.0 copy-start.4
  38.6 0.1 sum_parts.5.refs_3_
  38.7 1.3 %collective-permute-start.20 = (bf16[256,512]{1,0:T(8,128)(2,1)S(1)}, bf16[256,512]{1,0:T(8,128)(2,1)S(1)}, u32[]{:S(2)}, u32[]{:S(2)}) collective-permute-start(bf16[256,512]{1,0:T(8,128)(2,1)S(1)} %sum_parts.5.refs_3_), channel_id=1, source_target_pairs={{0,16},{1,17},{2,18},{3,19},{4,12},{5,13},{6,14},{7,15},{8,24},{9,... | collective-permute-start | bytes 786440 | tf_op jit(solution)/shard_map/ppermute | solution.py:364
  40.0 3.9 %collective-permute-done.16.refs_2_ = bf16[256,512]{1,0:T(8,128)(2,1)S(1)} collective-permute-done((bf16[256,512]{1,0:T(8,128)(2,1)S(1)}, bf16[256,512]{1,0:T(8,128)(2,1)S(1)}, u32[]{:S(2)}, u32[]{:S(2)}) %collective-permute-start.16) | collective-permute-done | bytes 262176 | tf_op jit(solution)/shard_map/ppermute | solution.py:364
  43.8 0.1 sum_parts.6
  43.9 4.0 %collective-permute-start.18 = (bf16[128,512]{1,0:T(8,128)(2,1)S(1)}, bf16[128,512]{1,0:T(8,128)(2,1)S(1)}, u32[]{:S(2)}, u32[]{:S(2)}) collective-permute-start(bf16[128,512]{1,0:T(8,128)(2,1)S(1)} %get-tuple-element.37), channel_id=1, source_target_pairs={{0,0},{1,1},{2,4},{3,5},{4,2},{5,3},{6,6},{7,7},{8,8},{9,9},{10,12... | collective-permute-start | bytes 393224 | tf_op jit(solution)/shard_map/ppermute | solution.py:364
  47.9 1.6 %collective-permute-start.22 = (bf16[128,512]{1,0:T(8,128)(2,1)S(1)}, bf16[128,512]{1,0:T(8,128)(2,1)S(1)}, u32[]{:S(2)}, u32[]{:S(2)}) collective-permute-start(bf16[128,512]{1,0:T(8,128)(2,1)S(1)} %get-tuple-element.41), channel_id=1, source_target_pairs={{0,1},{1,0},{2,5},{3,4},{4,3},{5,2},{6,7},{7,6},{8,9},{9,8},{10,13... | collective-permute-start | bytes 393224 | tf_op jit(solution)/shard_map/ppermute | solution.py:364
  49.6 0.1 sum_parts.7
  49.7 2.1 %collective-permute-start.21 = (bf16[128,512]{1,0:T(8,128)(2,1)S(1)}, bf16[128,512]{1,0:T(8,128)(2,1)S(1)}, u32[]{:S(2)}, u32[]{:S(2)}) collective-permute-start(bf16[128,512]{1,0:T(8,128)(2,1)S(1)} %get-tuple-element.40), channel_id=1, source_target_pairs={{0,0},{1,1},{2,4},{3,5},{4,2},{5,3},{6,6},{7,7},{8,8},{9,9},{10,12... | collective-permute-start | bytes 393224 | tf_op jit(solution)/shard_map/ppermute | solution.py:364
  51.7 1.9 %collective-permute-start.23 = (bf16[128,512]{1,0:T(8,128)(2,1)S(1)}, bf16[128,512]{1,0:T(8,128)(2,1)S(1)}, u32[]{:S(2)}, u32[]{:S(2)}) collective-permute-start(bf16[128,512]{1,0:T(8,128)(2,1)S(1)} %get-tuple-element.42), channel_id=1, source_target_pairs={{0,1},{1,0},{2,5},{3,4},{4,3},{5,2},{6,7},{7,6},{8,9},{9,8},{10,13... | collective-permute-start | bytes 393224 | tf_op jit(solution)/shard_map/ppermute | solution.py:364
  53.6 1.4 %collective-permute-done.22.refs_2_ = bf16[128,512]{1,0:T(8,128)(2,1)S(1)} collective-permute-done((bf16[128,512]{1,0:T(8,128)(2,1)S(1)}, bf16[128,512]{1,0:T(8,128)(2,1)S(1)}, u32[]{:S(2)}, u32[]{:S(2)}) %collective-permute-start.22) | collective-permute-done | bytes 131104 | tf_op jit(solution)/shard_map/ppermute | solution.py:364
  55.0 4.5 %collective-permute-done.21.refs_1_ = bf16[128,512]{1,0:T(8,128)(2,1)S(1)} collective-permute-done((bf16[128,512]{1,0:T(8,128)(2,1)S(1)}, bf16[128,512]{1,0:T(8,128)(2,1)S(1)}, u32[]{:S(2)}, u32[]{:S(2)}) %collective-permute-start.21) | collective-permute-done | bytes 131104 | tf_op jit(solution)/shard_map/ppermute | solution.py:364
  59.5 0.5 collective-permute-start.27
  60.0 0.8 %collective-permute-done.25.refs_5_ = bf16[128,512]{1,0:T(8,128)(2,1)S(1)} collective-permute-done((bf16[128,512]{1,0:T(8,128)(2,1)S(1)}, bf16[128,512]{1,0:T(8,128)(2,1)S(1)}, u32[]{:S(2)}, u32[]{:S(2)}) %collective-permute-start.25) | collective-permute-done | bytes 131104 | tf_op jit(solution)/shard_map/ppermute | solution.py:364
  60.9 0.2 collective-permute-done.27.refs_7_
  61.1 4.5 %attend.1 = (bf16[4,64,512]{2,1,0:T(8,128)(2,1)S(1)}, bf16[4,64,512]{2,1,0:T(8,128)(2,1)S(1)}) custom-call(bf16[128,512]{1,0:T(8,128)(2,1)S(1)} %collective-permute-done.18.refs_0_, bf16[128,512]{1,0:T(8,128)(2,1)S(1)} %collective-permute-done.21.refs_1_, bf16[128,512]{1,0:T(8,128)(2,1)S(1)} %collective-permute-done.22.refs_2_, ...), custom_call_target="tpu_custom_call" | custom-call | flops 2684354560 | bytes 3145728 | tf_op jit(solution)/shard_map/attend/pallas_call | solution.py:335
  65.5 2.1 %collective-permute-start.28 = (bf16[4,64,512]{2,1,0:T(8,128)(2,1)S(1)}, bf16[4,64,512]{2,1,0:T(8,128)(2,1)S(1)}, u32[]{:S(2)}, u32[]{:S(2)}) collective-permute-start(bf16[4,64,512]{2,1,0:T(8,128)(2,1)S(1)} %get-tuple-element.43), channel_id=1, source_target_pairs={{1,0},{0,1},{5,2},{4,3},{3,4},{2,5},{7,6},{6,7},{9,8},{8,9},{13,10... | collective-permute-start | bytes 786440 | tf_op jit(solution)/shard_map/ppermute | solution.py:458
  67.7 2.8 %collective-permute-start.29 = (bf16[4,64,512]{2,1,0:T(8,128)(2,1)S(1)}, bf16[4,64,512]{2,1,0:T(8,128)(2,1)S(1)}, u32[]{:S(2)}, u32[]{:S(2)}) collective-permute-start(bf16[4,64,512]{2,1,0:T(8,128)(2,1)S(1)} %get-tuple-element.44), channel_id=1, source_target_pairs={{0,0},{1,1},{4,2},{5,3},{2,4},{3,5},{6,6},{7,7},{8,8},{9,9},{12,10... | collective-permute-start | bytes 786440 | tf_op jit(solution)/shard_map/ppermute | solution.py:458
  70.5 5.0 %collective-permute-done.28 = bf16[4,64,512]{2,1,0:T(8,128)(2,1)S(1)} collective-permute-done((bf16[4,64,512]{2,1,0:T(8,128)(2,1)S(1)}, bf16[4,64,512]{2,1,0:T(8,128)(2,1)S(1)}, u32[]{:S(2)}, u32[]{:S(2)}) %collective-permute-start.28) | collective-permute-done | bytes 262176 | tf_op jit(solution)/shard_map/ppermute | solution.py:458
  75.5 5.6 %collective-permute-done.29 = bf16[4,64,512]{2,1,0:T(8,128)(2,1)S(1)} collective-permute-done((bf16[4,64,512]{2,1,0:T(8,128)(2,1)S(1)}, bf16[4,64,512]{2,1,0:T(8,128)(2,1)S(1)}, u32[]{:S(2)}, u32[]{:S(2)}) %collective-permute-start.29) | collective-permute-done | bytes 262176 | tf_op jit(solution)/shard_map/ppermute | solution.py:458
  81.1 0.8 %pad_maximum_fusion = bf16[2,4,64,512]{3,2,1,0:T(8,128)(2,1)} fusion(bf16[1,4,64,512]{3,2,1,0:T(8,128)(2,1)S(1)} %get-tuple-element.46, bf16[1,4,64,512]{3,2,1,0:T(8,128)(2,1)S(1)} %get-tuple-element.45), kind=kLoop, calls=%fused_computation | loop fusion | flops 262144 | bytes 1048576 | tf_op jit(solution)/shard_map/stack | solution.py:459
  (23 shorter events, 0.2 us)
Async XLA Ops:
  0.0 9.7 %collective-permute-start.1 = (bf16[9,3,64,512]{3,2,1,0:T(8,128)(2,1)}, bf16[9,3,64,512]{3,2,1,0:T(8,128)(2,1)S(1)}, u32[]{:S(2)}, u32[]{:S(2)}) collective-permute-start(bf16[9,3,64,512]{3,2,1,0:T(8,128)(2,1)} %bitcast.16), channel_id=1, source_target_pairs={{0,4},{1,5},{2,6},{3,7},{4,0},{5,1},{6,2},{7,3},{8,12},{9,13},{10,... | collective-permute-start | bytes 5308424 | tf_op jit(solution)/shard_map/ppermute | solution.py:364
  1.2 12.1 %collective-permute-start = (bf16[2,4,64,128]{3,2,1,0:T(8,128)(2,1)S(1)}, bf16[2,4,64,128]{3,2,1,0:T(8,128)(2,1)S(1)}, u32[]{:S(2)}, u32[]{:S(2)}) collective-permute-start(bf16[2,4,64,128]{3,2,1,0:T(8,128)(2,1)S(1)} %get-tuple-element.52), channel_id=1, source_target_pairs={{0,16},{1,17},{2,18},{3,19},{4,12},{5,13},{6,14},{7,15},{8,24},{9,... | collective-permute-start | bytes 393224 | tf_op jit(solution)/shard_map/ppermute | solution.py:364
  3.9 10.6 %collective-permute-start.3 = (bf16[2,4,64,128]{3,2,1,0:T(8,128)(2,1)S(1)}, bf16[2,4,64,128]{3,2,1,0:T(8,128)(2,1)S(1)}, u32[]{:S(2)}, u32[]{:S(2)}) collective-permute-start(bf16[2,4,64,128]{3,2,1,0:T(8,128)(2,1)S(1)} %get-tuple-element.50), channel_id=1, source_target_pairs={{0,8},{1,9},{2,10},{3,11},{4,20},{5,21},{6,22},{7,23},{8,0},{9,1},... | collective-permute-start | bytes 393224 | tf_op jit(solution)/shard_map/ppermute | solution.py:364
  5.2 9.4 %collective-permute-start.6 = (bf16[2,4,64,128]{3,2,1,0:T(8,128)(2,1)S(1)}, bf16[2,4,64,128]{3,2,1,0:T(8,128)(2,1)S(1)}, u32[]{:S(2)}, u32[]{:S(2)}) collective-permute-start(bf16[2,4,64,128]{3,2,1,0:T(8,128)(2,1)S(1)} %get-tuple-element.49), channel_id=1, source_target_pairs={{0,24},{1,25},{2,26},{3,27},{4,28},{5,29},{6,30},{7,31},{8,16},{9,... | collective-permute-start | bytes 393224 | tf_op jit(solution)/shard_map/ppermute | solution.py:364
  6.2 8.8 %collective-permute-start.8 = (bf16[2,64,512]{2,1,0:T(8,128)(2,1)S(1)}, bf16[2,64,512]{2,1,0:T(8,128)(2,1)S(1)}, u32[]{:S(2)}, u32[]{:S(2)}) collective-permute-start(bf16[2,64,512]{2,1,0:T(8,128)(2,1)S(1)} %get-tuple-element.48), channel_id=1, source_target_pairs={{0,1},{1,2},{2,3},{4,5},{5,6},{6,7},{8,9},{9,10},{10,11},{12,13},{... | collective-permute-start | bytes 393224 | tf_op jit(solution)/shard_map/ppermute | solution.py:364
  9.7 5.7 %collective-permute-start.9 = (bf16[2,64,512]{2,1,0:T(8,128)(2,1)S(1)}, bf16[2,64,512]{2,1,0:T(8,128)(2,1)S(1)}, u32[]{:S(2)}, u32[]{:S(2)}) collective-permute-start(bf16[2,64,512]{2,1,0:T(8,128)(2,1)S(1)} %get-tuple-element.47), channel_id=1, source_target_pairs={{1,0},{2,1},{3,2},{5,4},{6,5},{7,6},{9,8},{10,9},{11,10},{13,12},{... | collective-permute-start | bytes 393224 | tf_op jit(solution)/shard_map/ppermute | solution.py:364
  11.0 1.5 %copy-start = (bf16[27,64,512]{2,1,0:T(8,128)(2,1)S(1)}, bf16[27,64,512]{2,1,0:T(8,128)(2,1)}, u32[]{:S(2)}) copy-start(bf16[27,64,512]{2,1,0:T(8,128)(2,1)} %param.7) | copy-start | bytes 5308420
  13.3 4.0 %collective-permute-start.2 = (bf16[2,4,64,128]{3,2,1,0:T(8,128)(2,1)S(1)}, bf16[2,4,64,128]{3,2,1,0:T(8,128)(2,1)S(1)}, u32[]{:S(2)}, u32[]{:S(2)}) collective-permute-start(bf16[2,4,64,128]{3,2,1,0:T(8,128)(2,1)S(1)} %get-tuple-element.51.refs_2_), channel_id=1, source_target_pairs={{0,4},{1,5},{2,6},{3,7},{4,0},{5,1},{6,2},{7,3},{8,12},{9,13},{10,... | collective-permute-start | bytes 393224 | tf_op jit(solution)/shard_map/ppermute | solution.py:364
  14.5 4.0 %collective-permute-start.4 = (bf16[2,4,64,128]{3,2,1,0:T(8,128)(2,1)S(1)}, bf16[2,4,64,128]{3,2,1,0:T(8,128)(2,1)S(1)}, u32[]{:S(2)}, u32[]{:S(2)}) collective-permute-start(bf16[2,4,64,128]{3,2,1,0:T(8,128)(2,1)S(1)} %collective-permute-done.3.refs_2_), channel_id=1, source_target_pairs={{0,4},{1,5},{2,6},{3,7},{4,0},{5,1},{6,2},{7,3},{8,12},{9,13},{10,... | collective-permute-start | bytes 393224 | tf_op jit(solution)/shard_map/ppermute | solution.py:364
  14.6 4.1 %collective-permute-start.7 = (bf16[2,4,64,128]{3,2,1,0:T(8,128)(2,1)S(1)}, bf16[2,4,64,128]{3,2,1,0:T(8,128)(2,1)S(1)}, u32[]{:S(2)}, u32[]{:S(2)}) collective-permute-start(bf16[2,4,64,128]{3,2,1,0:T(8,128)(2,1)S(1)} %collective-permute-done.6.refs_3_), channel_id=1, source_target_pairs={{0,4},{1,5},{2,6},{3,7},{4,0},{5,1},{6,2},{7,3},{8,12},{9,13},{10,... | collective-permute-start | bytes 393224 | tf_op jit(solution)/shard_map/ppermute | solution.py:364
  15.0 3.7 %collective-permute-start.5 = (bf16[2,4,64,128]{3,2,1,0:T(8,128)(2,1)S(1)}, bf16[2,4,64,128]{3,2,1,0:T(8,128)(2,1)S(1)}, u32[]{:S(2)}, u32[]{:S(2)}) collective-permute-start(bf16[2,4,64,128]{3,2,1,0:T(8,128)(2,1)S(1)} %collective-permute-done.refs_3_), channel_id=1, source_target_pairs={{0,4},{1,5},{2,6},{3,7},{4,0},{5,1},{6,2},{7,3},{8,12},{9,13},{10,... | collective-permute-start | bytes 393224 | tf_op jit(solution)/shard_map/ppermute | solution.py:364
  16.0 5.6 %collective-permute-start.10 = (bf16[2,2,64,128]{3,2,1,0:T(8,128)(2,1)S(1)}, bf16[2,2,64,128]{3,2,1,0:T(8,128)(2,1)S(1)}, u32[]{:S(2)}, u32[]{:S(2)}) collective-permute-start(bf16[2,2,64,128]{3,2,1,0:T(8,128)(2,1)S(1)} %get-tuple-element.28), channel_id=1, source_target_pairs={{0,8},{1,9},{2,10},{3,11},{4,20},{5,21},{6,22},{7,23},{8,0},{9,1},... | collective-permute-start | bytes 196616 | tf_op jit(solution)/shard_map/ppermute | solution.py:364
  17.3 4.3 %collective-permute-start.11 = (bf16[2,2,64,128]{3,2,1,0:T(8,128)(2,1)S(1)}, bf16[2,2,64,128]{3,2,1,0:T(8,128)(2,1)S(1)}, u32[]{:S(2)}, u32[]{:S(2)}) collective-permute-start(bf16[2,2,64,128]{3,2,1,0:T(8,128)(2,1)S(1)} %get-tuple-element.29), channel_id=1, source_target_pairs={{0,16},{1,17},{2,18},{3,19},{4,12},{5,13},{6,14},{7,15},{8,24},{9,... | collective-permute-start | bytes 196616 | tf_op jit(solution)/shard_map/ppermute | solution.py:364
  18.5 4.4 %collective-permute-start.12 = (bf16[2,2,64,128]{3,2,1,0:T(8,128)(2,1)S(1)}, bf16[2,2,64,128]{3,2,1,0:T(8,128)(2,1)S(1)}, u32[]{:S(2)}, u32[]{:S(2)}) collective-permute-start(bf16[2,2,64,128]{3,2,1,0:T(8,128)(2,1)S(1)} %get-tuple-element.30), channel_id=1, source_target_pairs={{0,24},{1,25},{2,26},{3,27},{4,28},{5,29},{6,30},{7,31},{8,16},{9,... | collective-permute-start | bytes 196616 | tf_op jit(solution)/shard_map/ppermute | solution.py:364
  22.9 5.2 %collective-permute-start.13 = (bf16[4,2,2,64,128]{4,3,2,1,0:T(8,128)(2,1)S(1)}, bf16[4,2,2,64,128]{4,3,2,1,0:T(8,128)(2,1)S(1)}, u32[]{:S(2)}, u32[]{:S(2)}) collective-permute-start(bf16[4,2,2,64,128]{4,3,2,1,0:T(8,128)(2,1)S(1)} %stack_halo_rows.1.refs_8_), channel_id=1, source_target_pairs={{0,4},{1,5},{2,6},{3,7},{4,0},{5,1},{6,2},{7,3},{8,12},{9,13},{10,... | collective-permute-start | bytes 786440 | tf_op jit(solution)/shard_map/ppermute | solution.py:364
  26.6 8.7 %collective-permute-start.15 = (bf16[256,512]{1,0:T(8,128)(2,1)S(1)}, bf16[256,512]{1,0:T(8,128)(2,1)S(1)}, u32[]{:S(2)}, u32[]{:S(2)}) collective-permute-start(bf16[256,512]{1,0:T(8,128)(2,1)S(1)} %get-tuple-element.31.refs_4_), channel_id=1, source_target_pairs={{0,8},{1,9},{2,10},{3,11},{4,20},{5,21},{6,22},{7,23},{8,0},{9,1},... | collective-permute-start | bytes 786440 | tf_op jit(solution)/shard_map/ppermute | solution.py:364
  26.8 13.2 %collective-permute-start.14 = (bf16[256,512]{1,0:T(8,128)(2,1)S(1)}, bf16[256,512]{1,0:T(8,128)(2,1)S(1)}, u32[]{:S(2)}, u32[]{:S(2)}) collective-permute-start(bf16[256,512]{1,0:T(8,128)(2,1)S(1)} %get-tuple-element.34), channel_id=1, source_target_pairs={{0,8},{1,9},{2,10},{3,11},{4,20},{5,21},{6,22},{7,23},{8,0},{9,1},... | collective-permute-start | bytes 786440 | tf_op jit(solution)/shard_map/ppermute | solution.py:364
  30.9 7.7 %collective-permute-start.17 = (bf16[256,512]{1,0:T(8,128)(2,1)S(1)}, bf16[256,512]{1,0:T(8,128)(2,1)S(1)}, u32[]{:S(2)}, u32[]{:S(2)}) collective-permute-start(bf16[256,512]{1,0:T(8,128)(2,1)S(1)} %get-tuple-element.32.refs_8_), channel_id=1, source_target_pairs={{0,8},{1,9},{2,10},{3,11},{4,20},{5,21},{6,22},{7,23},{8,0},{9,1},... | collective-permute-start | bytes 786440 | tf_op jit(solution)/shard_map/ppermute | solution.py:364
  31.2 18.4 %collective-permute-start.19 = (bf16[256,512]{1,0:T(8,128)(2,1)S(1)}, bf16[256,512]{1,0:T(8,128)(2,1)S(1)}, u32[]{:S(2)}, u32[]{:S(2)}) collective-permute-start(bf16[256,512]{1,0:T(8,128)(2,1)S(1)} %get-tuple-element.39), channel_id=1, source_target_pairs={{0,8},{1,9},{2,10},{3,11},{4,20},{5,21},{6,22},{7,23},{8,0},{9,1},... | collective-permute-start | bytes 786440 | tf_op jit(solution)/shard_map/ppermute | solution.py:364
  35.4 8.5 %collective-permute-start.16 = (bf16[256,512]{1,0:T(8,128)(2,1)S(1)}, bf16[256,512]{1,0:T(8,128)(2,1)S(1)}, u32[]{:S(2)}, u32[]{:S(2)}) collective-permute-start(bf16[256,512]{1,0:T(8,128)(2,1)S(1)} %sum_parts.4.refs_10_), channel_id=1, source_target_pairs={{0,16},{1,17},{2,18},{3,19},{4,12},{5,13},{6,14},{7,15},{8,24},{9,... | collective-permute-start | bytes 786440 | tf_op jit(solution)/shard_map/ppermute | solution.py:364
  38.5 22.5 %copy-start.1 = (bf16[512,512]{1,0:T(8,128)(2,1)S(1)}, bf16[512,512]{1,0:T(8,128)(2,1)}, u32[]{:S(2)}) copy-start(bf16[512,512]{1,0:T(8,128)(2,1)} %refs_8_.1) | copy-start | bytes 1572868
  38.6 22.5 %copy-start.2 = (bf16[512,512]{1,0:T(8,128)(2,1)S(1)}, bf16[512,512]{1,0:T(8,128)(2,1)}, u32[]{:S(2)}) copy-start(bf16[512,512]{1,0:T(8,128)(2,1)} %refs_9_.1) | copy-start | bytes 1572868
  38.6 22.5 %copy-start.3 = (bf16[512,512]{1,0:T(8,128)(2,1)S(1)}, bf16[512,512]{1,0:T(8,128)(2,1)}, u32[]{:S(2)}) copy-start(bf16[512,512]{1,0:T(8,128)(2,1)} %refs_10_.1) | copy-start | bytes 1572868
  38.6 22.5 %copy-start.4 = (bf16[512,512]{1,0:T(8,128)(2,1)S(1)}, bf16[512,512]{1,0:T(8,128)(2,1)}, u32[]{:S(2)}) copy-start(bf16[512,512]{1,0:T(8,128)(2,1)} %refs_11_.1) | copy-start | bytes 1572868
  38.7 10.9 %collective-permute-start.20 = (bf16[256,512]{1,0:T(8,128)(2,1)S(1)}, bf16[256,512]{1,0:T(8,128)(2,1)S(1)}, u32[]{:S(2)}, u32[]{:S(2)}) collective-permute-start(bf16[256,512]{1,0:T(8,128)(2,1)S(1)} %sum_parts.5.refs_3_), channel_id=1, source_target_pairs={{0,16},{1,17},{2,18},{3,19},{4,12},{5,13},{6,14},{7,15},{8,24},{9,... | collective-permute-start | bytes 786440 | tf_op jit(solution)/shard_map/ppermute | solution.py:364
  43.9 9.7 %collective-permute-start.18 = (bf16[128,512]{1,0:T(8,128)(2,1)S(1)}, bf16[128,512]{1,0:T(8,128)(2,1)S(1)}, u32[]{:S(2)}, u32[]{:S(2)}) collective-permute-start(bf16[128,512]{1,0:T(8,128)(2,1)S(1)} %get-tuple-element.37), channel_id=1, source_target_pairs={{0,0},{1,1},{2,4},{3,5},{4,2},{5,3},{6,6},{7,7},{8,8},{9,9},{10,12... | collective-permute-start | bytes 393224 | tf_op jit(solution)/shard_map/ppermute | solution.py:364
  47.9 7.1 %collective-permute-start.22 = (bf16[128,512]{1,0:T(8,128)(2,1)S(1)}, bf16[128,512]{1,0:T(8,128)(2,1)S(1)}, u32[]{:S(2)}, u32[]{:S(2)}) collective-permute-start(bf16[128,512]{1,0:T(8,128)(2,1)S(1)} %get-tuple-element.41), channel_id=1, source_target_pairs={{0,1},{1,0},{2,5},{3,4},{4,3},{5,2},{6,7},{7,6},{8,9},{9,8},{10,13... | collective-permute-start | bytes 393224 | tf_op jit(solution)/shard_map/ppermute | solution.py:364
  49.7 9.9 %collective-permute-start.21 = (bf16[128,512]{1,0:T(8,128)(2,1)S(1)}, bf16[128,512]{1,0:T(8,128)(2,1)S(1)}, u32[]{:S(2)}, u32[]{:S(2)}) collective-permute-start(bf16[128,512]{1,0:T(8,128)(2,1)S(1)} %get-tuple-element.40), channel_id=1, source_target_pairs={{0,0},{1,1},{2,4},{3,5},{4,2},{5,3},{6,6},{7,7},{8,8},{9,9},{10,12... | collective-permute-start | bytes 393224 | tf_op jit(solution)/shard_map/ppermute | solution.py:364
  51.7 7.8 %collective-permute-start.23 = (bf16[128,512]{1,0:T(8,128)(2,1)S(1)}, bf16[128,512]{1,0:T(8,128)(2,1)S(1)}, u32[]{:S(2)}, u32[]{:S(2)}) collective-permute-start(bf16[128,512]{1,0:T(8,128)(2,1)S(1)} %get-tuple-element.42), channel_id=1, source_target_pairs={{0,1},{1,0},{2,5},{3,4},{4,3},{5,2},{6,7},{7,6},{8,9},{9,8},{10,13... | collective-permute-start | bytes 393224 | tf_op jit(solution)/shard_map/ppermute | solution.py:364
  53.6 6.4 %collective-permute-start.24 = (bf16[128,512]{1,0:T(8,128)(2,1)S(1)}, bf16[128,512]{1,0:T(8,128)(2,1)S(1)}, u32[]{:S(2)}, u32[]{:S(2)}) collective-permute-start(bf16[128,512]{1,0:T(8,128)(2,1)S(1)} %collective-permute-done.18.refs_0_), channel_id=1, source_target_pairs={{0,4},{1,5},{2,6},{3,7},{4,0},{5,1},{6,2},{7,3},{8,12},{9,13},{10,... | collective-permute-start | bytes 393224 | tf_op jit(solution)/shard_map/ppermute | solution.py:364
  55.0 5.0 %collective-permute-start.26 = (bf16[128,512]{1,0:T(8,128)(2,1)S(1)}, bf16[128,512]{1,0:T(8,128)(2,1)S(1)}, u32[]{:S(2)}, u32[]{:S(2)}) collective-permute-start(bf16[128,512]{1,0:T(8,128)(2,1)S(1)} %collective-permute-done.22.refs_2_), channel_id=1, source_target_pairs={{0,4},{1,5},{2,6},{3,7},{4,0},{5,1},{6,2},{7,3},{8,12},{9,13},{10,... | collective-permute-start | bytes 393224 | tf_op jit(solution)/shard_map/ppermute | solution.py:364
  59.5 1.3 %collective-permute-start.25 = (bf16[128,512]{1,0:T(8,128)(2,1)S(1)}, bf16[128,512]{1,0:T(8,128)(2,1)S(1)}, u32[]{:S(2)}, u32[]{:S(2)}) collective-permute-start(bf16[128,512]{1,0:T(8,128)(2,1)S(1)} %collective-permute-done.21.refs_1_), channel_id=1, source_target_pairs={{0,4},{1,5},{2,6},{3,7},{4,0},{5,1},{6,2},{7,3},{8,12},{9,13},{10,... | collective-permute-start | bytes 393224 | tf_op jit(solution)/shard_map/ppermute | solution.py:364
  59.5 1.5 %collective-permute-start.27 = (bf16[128,512]{1,0:T(8,128)(2,1)S(1)}, bf16[128,512]{1,0:T(8,128)(2,1)S(1)}, u32[]{:S(2)}, u32[]{:S(2)}) collective-permute-start(bf16[128,512]{1,0:T(8,128)(2,1)S(1)} %collective-permute-done.23.refs_3_), channel_id=1, source_target_pairs={{0,4},{1,5},{2,6},{3,7},{4,0},{5,1},{6,2},{7,3},{8,12},{9,13},{10,... | collective-permute-start | bytes 393224 | tf_op jit(solution)/shard_map/ppermute | solution.py:364
  65.5 9.9 %collective-permute-start.28 = (bf16[4,64,512]{2,1,0:T(8,128)(2,1)S(1)}, bf16[4,64,512]{2,1,0:T(8,128)(2,1)S(1)}, u32[]{:S(2)}, u32[]{:S(2)}) collective-permute-start(bf16[4,64,512]{2,1,0:T(8,128)(2,1)S(1)} %get-tuple-element.43), channel_id=1, source_target_pairs={{1,0},{0,1},{5,2},{4,3},{3,4},{2,5},{7,6},{6,7},{9,8},{8,9},{13,10... | collective-permute-start | bytes 786440 | tf_op jit(solution)/shard_map/ppermute | solution.py:458
  67.7 13.4 %collective-permute-start.29 = (bf16[4,64,512]{2,1,0:T(8,128)(2,1)S(1)}, bf16[4,64,512]{2,1,0:T(8,128)(2,1)S(1)}, u32[]{:S(2)}, u32[]{:S(2)}) collective-permute-start(bf16[4,64,512]{2,1,0:T(8,128)(2,1)S(1)} %get-tuple-element.44), channel_id=1, source_target_pairs={{0,0},{1,1},{4,2},{5,3},{2,4},{3,5},{6,6},{7,7},{8,8},{9,9},{12,10... | collective-permute-start | bytes 786440 | tf_op jit(solution)/shard_map/ppermute | solution.py:458

commit v15 on v14

--- a/solution.py
+++ b/solution.py
@@ -207,7 +207,7 @@
         ],
         compiler_params=pltpu.CompilerParams(vmem_limit_bytes=VMEM_LIMIT),
         cost_estimate=pl.CostEstimate(
-            flops=2 * total * taps * lags * width * chans,
+            flops=20 * total * taps * lags * width * chans,
             bytes_accessed=2 * taps * lags * width * chans,
             transcendentals=0,
         ),
@@ -403,15 +403,13 @@
     rims = [permute(x, to_place(place)) if place else x for place, x in enumerate(rims)]
     inner_sent = conv([(3, False), (1, False)], rims=None, out_type=jnp.bfloat16)
     inner_got = hop(inner_sent)
+    inner_on, inner_own = conv(
+        [(2, False), (0, False)], rims=None, out_type=jnp.float32, after=inner_sent[:1]
+    )
     rims = stack_call(rims, inner_sent[0])
     rims = (rims, permute(rims, to_member(1)))
-    rim_sent = conv(
-        [(3, True), (1, True)], rims=rims, out_type=jnp.bfloat16, after=inner_got[:0]
-    )
+    rim_sent = conv([(3, True), (1, True)], rims=rims, out_type=jnp.bfloat16, after=(inner_on,))
     rim_got = hop(rim_sent)
-    inner_on, inner_own = conv(
-        [(2, False), (0, False)], rims=None, out_type=jnp.float32, after=rim_sent[:1]
-    )
     (inner_relay,) = sum_call([inner_on, inner_got[0]], 1)
     inner_last = permute(inner_relay, to_place(2))
     rim_on, rim_own = conv(

time: 82.2 us -> 82.4 us (level)
  starting transfers between devices: 36.5 us -> 37.4 us
    ppermute x28, starting transfers between devices: 31.6 us -> 32.5 us  [permute(): return lax.ppermute(block, BOTH, everywhere(sizes, target))]
where the time goes in v15:
time: 82.4 us; the launch traced here: 82.1 us
  starting transfers between devices  37.4 us (45%)
  waiting for transfers between devices  22.3 us (27%)
  Pallas kernels  17.6 us (21%)
  local copies, waits for them, and re-layouts  3.63 us (4%)
  other arithmetic  0.96 us (1%)
    ppermute x28, starting transfers between devices, permute(): return lax.ppermute(block, BOTH, everywhere(sizes, target))  32.5 us
    ppermute x28, waiting for transfers between devices, permute(): return lax.ppermute(block, BOTH, everywhere(sizes, target))  11.7 us
    pallas_call x4, Pallas kernels, conv_call(): pl.pallas_call(functools.partial(conv_kernel, tuple(jobs), parts, group,...  11.4 us
    ppermute x2, waiting for transfers between devices, body(): back.append(lax.ppermute(done[p], BOTH, pairs))  10.6 us
    ppermute x2, starting transfers between devices, body(): back.append(lax.ppermute(done[p], BOTH, pairs))  4.91 us
    pallas_call x1, Pallas kernels, attend_call(): pl.pallas_call(functools.partial(attend_kernel, frames, share, chunks), o...  4.46 us
  transfers between devices with their start and end apart: 30, of which 9 were waited for; matrix products, arithmetic and copies ran while one was open for 3% of the time, Pallas kernels for 16%

profile of v15, /device:TPU:1, one launch (start us, length us, event | category | flops | bytes accessed | tf_op | source)
XLA Modules:
  0.0 82.1 jit_solution(1836906036860532688)
XLA Ops:
  0.0 0.1 collective-permute-start.1
  0.1 1.1 %constant_dynamic-slice_fusion = (bf16[2,4,64,128]{3,2,1,0:T(8,128)(2,1)S(1)}, bf16[2,4,64,128]{3,2,1,0:T(8,128)(2,1)S(1)}, bf16[2,4,64,128]{3,2,1,0:T(8,128)(2,1)S(1)}, bf16[2,4,64,128]{3,2,1,0:T(8,128)(2,1)S(1)}) fusion(bf16[2,4,64,512]{3,2,1,0:T(8,128)(2,1)} %param.6, s32[]{:T(128)S(6)} %select_n.75, s32[]{:T(128)S(6)} %select_n.74, s32[]{:T(128)S(6)} %select_n.72, ...), kind=kLoop, calls=%fused_computation.5 | loop fusion | bytes 1048592 | tf_op jit(solution)/shard_map/dynamic_slice | solution.py:383
  1.2 2.7 %collective-permute-start = (bf16[2,4,64,128]{3,2,1,0:T(8,128)(2,1)S(1)}, bf16[2,4,64,128]{3,2,1,0:T(8,128)(2,1)S(1)}, u32[]{:S(2)}, u32[]{:S(2)}) collective-permute-start(bf16[2,4,64,128]{3,2,1,0:T(8,128)(2,1)S(1)} %get-tuple-element.52), channel_id=1, source_target_pairs={{0,16},{1,17},{2,18},{3,19},{4,12},{5,13},{6,14},{7,15},{8,24},{9,... | collective-permute-start | bytes 393224 | tf_op jit(solution)/shard_map/ppermute | solution.py:364
  3.9 1.2 %collective-permute-start.3 = (bf16[2,4,64,128]{3,2,1,0:T(8,128)(2,1)S(1)}, bf16[2,4,64,128]{3,2,1,0:T(8,128)(2,1)S(1)}, u32[]{:S(2)}, u32[]{:S(2)}) collective-permute-start(bf16[2,4,64,128]{3,2,1,0:T(8,128)(2,1)S(1)} %get-tuple-element.50), channel_id=1, source_target_pairs={{0,8},{1,9},{2,10},{3,11},{4,20},{5,21},{6,22},{7,23},{8,0},{9,1},... | collective-permute-start | bytes 393224 | tf_op jit(solution)/shard_map/ppermute | solution.py:364
  5.2 0.0 collective-permute-start.6
  5.2 1.0 %slice_bitcast_fusion = (bf16[2,64,512]{2,1,0:T(8,128)(2,1)S(1)}, bf16[2,64,512]{2,1,0:T(8,128)(2,1)S(1)}) fusion(bf16[2,4,64,512]{3,2,1,0:T(8,128)(2,1)} %param.6), kind=kLoop, calls=%fused_computation.3 | loop fusion | bytes 524288 | tf_op jit(solution)/shard_map/squeeze | solution.py:377
  6.2 3.4 %collective-permute-start.11 = (bf16[2,64,512]{2,1,0:T(8,128)(2,1)S(1)}, bf16[2,64,512]{2,1,0:T(8,128)(2,1)S(1)}, u32[]{:S(2)}, u32[]{:S(2)}) collective-permute-start(bf16[2,64,512]{2,1,0:T(8,128)(2,1)S(1)} %get-tuple-element.48), channel_id=1, source_target_pairs={{0,1},{1,2},{2,3},{4,5},{5,6},{6,7},{8,9},{9,10},{10,11},{12,13},{... | collective-permute-start | bytes 393224 | tf_op jit(solution)/shard_map/ppermute | solution.py:364
  9.6 0.1 pad_add_fusion.refs_0_.meta
  9.7 0.0 collective-permute-done.1.refs_2_
  9.7 1.3 %collective-permute-start.12 = (bf16[2,64,512]{2,1,0:T(8,128)(2,1)S(1)}, bf16[2,64,512]{2,1,0:T(8,128)(2,1)S(1)}, u32[]{:S(2)}, u32[]{:S(2)}) collective-permute-start(bf16[2,64,512]{2,1,0:T(8,128)(2,1)S(1)} %get-tuple-element.47), channel_id=1, source_target_pairs={{1,0},{2,1},{3,2},{5,4},{6,5},{7,6},{9,8},{10,9},{11,10},{13,12},{... | collective-permute-start | bytes 393224 | tf_op jit(solution)/shard_map/ppermute | solution.py:364
  11.0 0.0 copy-start
  11.0 1.5 %copy-done = bf16[27,64,512]{2,1,0:T(8,128)(2,1)S(1)} copy-done((bf16[27,64,512]{2,1,0:T(8,128)(2,1)S(1)}, bf16[27,64,512]{2,1,0:T(8,128)(2,1)}, u32[]{:S(2)}) %copy-start) | copy-done | bytes 1769496
  12.4 0.9 %merge_kernel_slices.1.refs_1_ = bf16[3,9,128,512]{3,2,1,0:T(8,128)(2,1)S(1)} custom-call(s32[3]{0:T(128)S(1)} %pad_add_fusion.refs_0_.meta, bf16[9,3,64,512]{3,2,1,0:T(8,128)(2,1)S(1)} %bitcast.17, bf16[9,3,64,512]{3,2,1,0:T(8,128)(2,1)S(1)} %collective-permute-done.1.refs_2_), custom_call_target="tpu_custom_call" | custom-call | tf_op jit(solution)/shard_map/merge_kernel_slices/pallas_call | solution.py:58
  13.3 1.2 %collective-permute-start.2 = (bf16[2,4,64,128]{3,2,1,0:T(8,128)(2,1)S(1)}, bf16[2,4,64,128]{3,2,1,0:T(8,128)(2,1)S(1)}, u32[]{:S(2)}, u32[]{:S(2)}) collective-permute-start(bf16[2,4,64,128]{3,2,1,0:T(8,128)(2,1)S(1)} %get-tuple-element.51.refs_2_), channel_id=1, source_target_pairs={{0,4},{1,5},{2,6},{3,7},{4,0},{5,1},{6,2},{7,3},{8,12},{9,13},{10,... | collective-permute-start | bytes 393224 | tf_op jit(solution)/shard_map/ppermute | solution.py:364
  14.5 0.0 collective-permute-done.3.refs_2_
  14.5 0.1 collective-permute-start.4
  14.6 0.0 collective-permute-done.6.refs_3_
  14.6 0.4 collective-permute-start.7
  15.0 0.0 collective-permute-done.11.above
  15.0 0.1 collective-permute-start.5
  15.1 0.3 collective-permute-done.12.below
  15.4 0.6 split_halo_rows.1
  16.0 1.3 %collective-permute-start.13 = (bf16[2,2,64,128]{3,2,1,0:T(8,128)(2,1)S(1)}, bf16[2,2,64,128]{3,2,1,0:T(8,128)(2,1)S(1)}, u32[]{:S(2)}, u32[]{:S(2)}) collective-permute-start(bf16[2,2,64,128]{3,2,1,0:T(8,128)(2,1)S(1)} %get-tuple-element.32), channel_id=1, source_target_pairs={{0,8},{1,9},{2,10},{3,11},{4,20},{5,21},{6,22},{7,23},{8,0},{9,1},... | collective-permute-start | bytes 196616 | tf_op jit(solution)/shard_map/ppermute | solution.py:364
  17.3 0.0 collective-permute-done.2.refs_4_
  17.3 1.2 %collective-permute-start.14 = (bf16[2,2,64,128]{3,2,1,0:T(8,128)(2,1)S(1)}, bf16[2,2,64,128]{3,2,1,0:T(8,128)(2,1)S(1)}, u32[]{:S(2)}, u32[]{:S(2)}) collective-permute-start(bf16[2,2,64,128]{3,2,1,0:T(8,128)(2,1)S(1)} %get-tuple-element.33), channel_id=1, source_target_pairs={{0,16},{1,17},{2,18},{3,19},{4,12},{5,13},{6,14},{7,15},{8,24},{9,... | collective-permute-start | bytes 196616 | tf_op jit(solution)/shard_map/ppermute | solution.py:364
  18.5 0.2 collective-permute-start.15
  18.7 0.0 collective-permute-done.5.refs_6_
  18.7 2.9 %conv_inner.2 = (bf16[256,512]{1,0:T(8,128)(2,1)S(1)}, bf16[256,512]{1,0:T(8,128)(2,1)S(1)}) custom-call(s32[3]{0:T(128)S(1)} %pad_add_fusion.refs_0_.meta, bf16[3,9,128,512]{3,2,1,0:T(8,128)(2,1)S(1)} %merge_kernel_slices.1.refs_1_, bf16[2,4,64,128]{3,2,1,0:T(8,128)(2,1)S(1)} %collective-permute-done.3.refs_2_, ...), custom_call_target="tpu_custom_call" | custom-call | flops 18119393280 | bytes 3538944 | tf_op jit(solution)/shard_map/conv_inner/pallas_call | solution.py:200
  21.6 1.3 %collective-permute-start.9 = (bf16[256,512]{1,0:T(8,128)(2,1)S(1)}, bf16[256,512]{1,0:T(8,128)(2,1)S(1)}, u32[]{:S(2)}, u32[]{:S(2)}) collective-permute-start(bf16[256,512]{1,0:T(8,128)(2,1)S(1)} %get-tuple-element.27.refs_8_.refs_4_), channel_id=1, source_target_pairs={{0,8},{1,9},{2,10},{3,11},{4,20},{5,21},{6,22},{7,23},{8,0},{9,1},... | collective-permute-start | bytes 786440 | tf_op jit(solution)/shard_map/ppermute | solution.py:364
  22.9 0.0 collective-permute-done.15.refs_3_
  22.9 3.8 %collective-permute-start.16 = (bf16[4,2,2,64,128]{4,3,2,1,0:T(8,128)(2,1)S(1)}, bf16[4,2,2,64,128]{4,3,2,1,0:T(8,128)(2,1)S(1)}, u32[]{:S(2)}, u32[]{:S(2)}) collective-permute-start(bf16[4,2,2,64,128]{4,3,2,1,0:T(8,128)(2,1)S(1)} %stack_halo_rows.1.refs_8_), channel_id=1, source_target_pairs={{0,4},{1,5},{2,6},{3,7},{4,0},{5,1},{6,2},{7,3},{8,12},{9,13},{10,... | collective-permute-start | bytes 786440 | tf_op jit(solution)/shard_map/ppermute | solution.py:364
  26.7 0.9 %collective-permute-start.8 = (bf16[256,512]{1,0:T(8,128)(2,1)S(1)}, bf16[256,512]{1,0:T(8,128)(2,1)S(1)}, u32[]{:S(2)}, u32[]{:S(2)}) collective-permute-start(bf16[256,512]{1,0:T(8,128)(2,1)S(1)} %get-tuple-element.29), channel_id=1, source_target_pairs={{0,8},{1,9},{2,10},{3,11},{4,20},{5,21},{6,22},{7,23},{8,0},{9,1},... | collective-permute-start | bytes 786440 | tf_op jit(solution)/shard_map/ppermute | solution.py:364
  27.6 2.8 %conv_inner.3 = (f32[256,512]{1,0:T(8,128)S(1)}, f32[256,512]{1,0:T(8,128)S(1)}) custom-call(s32[3]{0:T(128)S(1)} %pad_add_fusion.refs_0_.meta, bf16[3,9,128,512]{3,2,1,0:T(8,128)(2,1)S(1)} %merge_kernel_slices.1.refs_1_, bf16[2,4,64,128]{3,2,1,0:T(8,128)(2,1)S(1)} %get-tuple-element.51.refs_2_, bf16[2,4,64,128]{3,2,1,0:T(8,128)(2,1)S(1)} %collective-permute-done.refs_3_, ...), custom_call_target="tpu_custom_call" | custom-call | flops 18119393280 | bytes 3538944 | tf_op jit(solution)/shard_map/conv_inner/pallas_call | solution.py:200
  30.5 2.9 %conv_rim.3 = (bf16[256,512]{1,0:T(8,128)(2,1)S(1)}, bf16[256,512]{1,0:T(8,128)(2,1)S(1)}) custom-call(s32[3]{0:T(128)S(1)} %pad_add_fusion.refs_0_.meta, bf16[3,9,128,512]{3,2,1,0:T(8,128)(2,1)S(1)} %merge_kernel_slices.1.refs_1_, bf16[2,4,64,128]{3,2,1,0:T(8,128)(2,1)S(1)} %collective-permute-done.3.refs_2_, ...), custom_call_target="tpu_custom_call" | custom-call | flops 18119393280 | bytes 3538944 | tf_op jit(solution)/shard_map/conv_rim/pallas_call | solution.py:200
  33.3 0.6 collective-permute-start.17
  33.9 0.9 %collective-permute-start.19 = (bf16[256,512]{1,0:T(8,128)(2,1)S(1)}, bf16[256,512]{1,0:T(8,128)(2,1)S(1)}, u32[]{:S(2)}, u32[]{:S(2)}) collective-permute-start(bf16[256,512]{1,0:T(8,128)(2,1)S(1)} %get-tuple-element.39), channel_id=1, source_target_pairs={{0,8},{1,9},{2,10},{3,11},{4,20},{5,21},{6,22},{7,23},{8,0},{9,1},... | collective-permute-start | bytes 786440 | tf_op jit(solution)/shard_map/ppermute | solution.py:364
  34.9 0.1 sum_parts.4.refs_10_
  34.9 0.3 collective-permute-start.10
  35.2 2.9 %conv_rim.2 = (f32[256,512]{1,0:T(8,128)S(1)}, f32[256,512]{1,0:T(8,128)S(1)}) custom-call(s32[3]{0:T(128)S(1)} %pad_add_fusion.refs_0_.meta, bf16[3,9,128,512]{3,2,1,0:T(8,128)(2,1)S(1)} %merge_kernel_slices.1.refs_1_, bf16[2,4,64,128]{3,2,1,0:T(8,128)(2,1)S(1)} %get-tuple-element.51.refs_2_, bf16[2,4,64,128]{3,2,1,0:T(8,128)(2,1)S(1)} %collective-permute-done.refs_3_, ...), custom_call_target="tpu_custom_call" | custom-call | flops 18119393280 | bytes 3538944 | tf_op jit(solution)/shard_map/conv_rim/pallas_call | solution.py:200
  38.1 0.0 copy-start.1
  38.1 0.0 copy-start.2
  38.1 0.0 copy-start.3
  38.1 0.0 copy-start.4
  38.1 1.2 %collective-permute-done.17.refs_1_ = bf16[256,512]{1,0:T(8,128)(2,1)S(1)} collective-permute-done((bf16[256,512]{1,0:T(8,128)(2,1)S(1)}, bf16[256,512]{1,0:T(8,128)(2,1)S(1)}, u32[]{:S(2)}, u32[]{:S(2)}) %collective-permute-start.17) | collective-permute-done | bytes 262176 | tf_op jit(solution)/shard_map/ppermute | solution.py:364
  39.3 0.1 sum_parts.5.refs_3_
  39.4 0.2 collective-permute-start.20
  39.5 3.9 %collective-permute-done.10.refs_2_ = bf16[256,512]{1,0:T(8,128)(2,1)S(1)} collective-permute-done((bf16[256,512]{1,0:T(8,128)(2,1)S(1)}, bf16[256,512]{1,0:T(8,128)(2,1)S(1)}, u32[]{:S(2)}, u32[]{:S(2)}) %collective-permute-start.10) | collective-permute-done | bytes 262176 | tf_op jit(solution)/shard_map/ppermute | solution.py:364
  43.4 0.1 sum_parts.6
  43.5 5.2 %collective-permute-start.18 = (bf16[128,512]{1,0:T(8,128)(2,1)S(1)}, bf16[128,512]{1,0:T(8,128)(2,1)S(1)}, u32[]{:S(2)}, u32[]{:S(2)}) collective-permute-start(bf16[128,512]{1,0:T(8,128)(2,1)S(1)} %get-tuple-element.37), channel_id=1, source_target_pairs={{0,0},{1,1},{2,4},{3,5},{4,2},{5,3},{6,6},{7,7},{8,8},{9,9},{10,12... | collective-permute-start | bytes 393224 | tf_op jit(solution)/shard_map/ppermute | solution.py:364
  48.6 0.5 collective-permute-start.22
  49.1 0.1 sum_parts.7
  49.2 3.2 %collective-permute-start.21 = (bf16[128,512]{1,0:T(8,128)(2,1)S(1)}, bf16[128,512]{1,0:T(8,128)(2,1)S(1)}, u32[]{:S(2)}, u32[]{:S(2)}) collective-permute-start(bf16[128,512]{1,0:T(8,128)(2,1)S(1)} %get-tuple-element.40), channel_id=1, source_target_pairs={{0,0},{1,1},{2,4},{3,5},{4,2},{5,3},{6,6},{7,7},{8,8},{9,9},{10,12... | collective-permute-start | bytes 393224 | tf_op jit(solution)/shard_map/ppermute | solution.py:364
  52.4 1.9 %collective-permute-start.23 = (bf16[128,512]{1,0:T(8,128)(2,1)S(1)}, bf16[128,512]{1,0:T(8,128)(2,1)S(1)}, u32[]{:S(2)}, u32[]{:S(2)}) collective-permute-start(bf16[128,512]{1,0:T(8,128)(2,1)S(1)} %get-tuple-element.42), channel_id=1, source_target_pairs={{0,1},{1,0},{2,5},{3,4},{4,3},{5,2},{6,7},{7,6},{8,9},{9,8},{10,13... | collective-permute-start | bytes 393224 | tf_op jit(solution)/shard_map/ppermute | solution.py:364
  54.3 1.1 %collective-permute-done.22.refs_2_ = bf16[128,512]{1,0:T(8,128)(2,1)S(1)} collective-permute-done((bf16[128,512]{1,0:T(8,128)(2,1)S(1)}, bf16[128,512]{1,0:T(8,128)(2,1)S(1)}, u32[]{:S(2)}, u32[]{:S(2)}) %collective-permute-start.22) | collective-permute-done | bytes 131104 | tf_op jit(solution)/shard_map/ppermute | solution.py:364
  55.5 4.2 %collective-permute-done.21.refs_1_ = bf16[128,512]{1,0:T(8,128)(2,1)S(1)} collective-permute-done((bf16[128,512]{1,0:T(8,128)(2,1)S(1)}, bf16[128,512]{1,0:T(8,128)(2,1)S(1)}, u32[]{:S(2)}, u32[]{:S(2)}) %collective-permute-start.21) | collective-permute-done | bytes 131104 | tf_op jit(solution)/shard_map/ppermute | solution.py:364
  59.7 0.5 collective-permute-start.27
  60.2 0.8 %collective-permute-done.25.refs_5_ = bf16[128,512]{1,0:T(8,128)(2,1)S(1)} collective-permute-done((bf16[128,512]{1,0:T(8,128)(2,1)S(1)}, bf16[128,512]{1,0:T(8,128)(2,1)S(1)}, u32[]{:S(2)}, u32[]{:S(2)}) %collective-permute-start.25) | collective-permute-done | bytes 131104 | tf_op jit(solution)/shard_map/ppermute | solution.py:364
  61.0 0.2 collective-permute-done.27.refs_7_
  61.2 4.5 %attend.1 = (bf16[4,64,512]{2,1,0:T(8,128)(2,1)S(1)}, bf16[4,64,512]{2,1,0:T(8,128)(2,1)S(1)}) custom-call(bf16[128,512]{1,0:T(8,128)(2,1)S(1)} %collective-permute-done.18.refs_0_, bf16[128,512]{1,0:T(8,128)(2,1)S(1)} %collective-permute-done.21.refs_1_, bf16[128,512]{1,0:T(8,128)(2,1)S(1)} %collective-permute-done.22.refs_2_, ...), custom_call_target="tpu_custom_call" | custom-call | flops 2684354560 | bytes 3145728 | tf_op jit(solution)/shard_map/attend/pallas_call | solution.py:335
  65.7 2.7 %collective-permute-start.28 = (bf16[4,64,512]{2,1,0:T(8,128)(2,1)S(1)}, bf16[4,64,512]{2,1,0:T(8,128)(2,1)S(1)}, u32[]{:S(2)}, u32[]{:S(2)}) collective-permute-start(bf16[4,64,512]{2,1,0:T(8,128)(2,1)S(1)} %get-tuple-element.43), channel_id=1, source_target_pairs={{1,0},{0,1},{5,2},{4,3},{3,4},{2,5},{7,6},{6,7},{9,8},{8,9},{13,10... | collective-permute-start | bytes 786440 | tf_op jit(solution)/shard_map/ppermute | solution.py:456
  68.4 2.3 %collective-permute-start.29 = (bf16[4,64,512]{2,1,0:T(8,128)(2,1)S(1)}, bf16[4,64,512]{2,1,0:T(8,128)(2,1)S(1)}, u32[]{:S(2)}, u32[]{:S(2)}) collective-permute-start(bf16[4,64,512]{2,1,0:T(8,128)(2,1)S(1)} %get-tuple-element.44), channel_id=1, source_target_pairs={{0,0},{1,1},{4,2},{5,3},{2,4},{3,5},{6,6},{7,7},{8,8},{9,9},{12,10... | collective-permute-start | bytes 786440 | tf_op jit(solution)/shard_map/ppermute | solution.py:456
  70.6 5.5 %collective-permute-done.28 = bf16[4,64,512]{2,1,0:T(8,128)(2,1)S(1)} collective-permute-done((bf16[4,64,512]{2,1,0:T(8,128)(2,1)S(1)}, bf16[4,64,512]{2,1,0:T(8,128)(2,1)S(1)}, u32[]{:S(2)}, u32[]{:S(2)}) %collective-permute-start.28) | collective-permute-done | bytes 262176 | tf_op jit(solution)/shard_map/ppermute | solution.py:456
  76.2 5.0 %collective-permute-done.29 = bf16[4,64,512]{2,1,0:T(8,128)(2,1)S(1)} collective-permute-done((bf16[4,64,512]{2,1,0:T(8,128)(2,1)S(1)}, bf16[4,64,512]{2,1,0:T(8,128)(2,1)S(1)}, u32[]{:S(2)}, u32[]{:S(2)}) %collective-permute-start.29) | collective-permute-done | bytes 262176 | tf_op jit(solution)/shard_map/ppermute | solution.py:456
  81.2 0.8 %pad_maximum_fusion = bf16[2,4,64,512]{3,2,1,0:T(8,128)(2,1)} fusion(bf16[1,4,64,512]{3,2,1,0:T(8,128)(2,1)S(1)} %get-tuple-element.46, bf16[1,4,64,512]{3,2,1,0:T(8,128)(2,1)S(1)} %get-tuple-element.45), kind=kLoop, calls=%fused_computation | loop fusion | flops 262144 | bytes 1048576 | tf_op jit(solution)/shard_map/stack | solution.py:457
  (23 shorter events, 0.1 us)
Async XLA Ops:
  0.0 9.7 %collective-permute-start.1 = (bf16[9,3,64,512]{3,2,1,0:T(8,128)(2,1)}, bf16[9,3,64,512]{3,2,1,0:T(8,128)(2,1)S(1)}, u32[]{:S(2)}, u32[]{:S(2)}) collective-permute-start(bf16[9,3,64,512]{3,2,1,0:T(8,128)(2,1)} %bitcast.16), channel_id=1, source_target_pairs={{0,4},{1,5},{2,6},{3,7},{4,0},{5,1},{6,2},{7,3},{8,12},{9,13},{10,... | collective-permute-start | bytes 5308424 | tf_op jit(solution)/shard_map/ppermute | solution.py:364
  1.2 12.1 %collective-permute-start = (bf16[2,4,64,128]{3,2,1,0:T(8,128)(2,1)S(1)}, bf16[2,4,64,128]{3,2,1,0:T(8,128)(2,1)S(1)}, u32[]{:S(2)}, u32[]{:S(2)}) collective-permute-start(bf16[2,4,64,128]{3,2,1,0:T(8,128)(2,1)S(1)} %get-tuple-element.52), channel_id=1, source_target_pairs={{0,16},{1,17},{2,18},{3,19},{4,12},{5,13},{6,14},{7,15},{8,24},{9,... | collective-permute-start | bytes 393224 | tf_op jit(solution)/shard_map/ppermute | solution.py:364
  3.9 10.6 %collective-permute-start.3 = (bf16[2,4,64,128]{3,2,1,0:T(8,128)(2,1)S(1)}, bf16[2,4,64,128]{3,2,1,0:T(8,128)(2,1)S(1)}, u32[]{:S(2)}, u32[]{:S(2)}) collective-permute-start(bf16[2,4,64,128]{3,2,1,0:T(8,128)(2,1)S(1)} %get-tuple-element.50), channel_id=1, source_target_pairs={{0,8},{1,9},{2,10},{3,11},{4,20},{5,21},{6,22},{7,23},{8,0},{9,1},... | collective-permute-start | bytes 393224 | tf_op jit(solution)/shard_map/ppermute | solution.py:364
  5.2 9.4 %collective-permute-start.6 = (bf16[2,4,64,128]{3,2,1,0:T(8,128)(2,1)S(1)}, bf16[2,4,64,128]{3,2,1,0:T(8,128)(2,1)S(1)}, u32[]{:S(2)}, u32[]{:S(2)}) collective-permute-start(bf16[2,4,64,128]{3,2,1,0:T(8,128)(2,1)S(1)} %get-tuple-element.49), channel_id=1, source_target_pairs={{0,24},{1,25},{2,26},{3,27},{4,28},{5,29},{6,30},{7,31},{8,16},{9,... | collective-permute-start | bytes 393224 | tf_op jit(solution)/shard_map/ppermute | solution.py:364
  6.2 8.8 %collective-permute-start.11 = (bf16[2,64,512]{2,1,0:T(8,128)(2,1)S(1)}, bf16[2,64,512]{2,1,0:T(8,128)(2,1)S(1)}, u32[]{:S(2)}, u32[]{:S(2)}) collective-permute-start(bf16[2,64,512]{2,1,0:T(8,128)(2,1)S(1)} %get-tuple-element.48), channel_id=1, source_target_pairs={{0,1},{1,2},{2,3},{4,5},{5,6},{6,7},{8,9},{9,10},{10,11},{12,13},{... | collective-permute-start | bytes 393224 | tf_op jit(solution)/shard_map/ppermute | solution.py:364
  9.7 5.7 %collective-permute-start.12 = (bf16[2,64,512]{2,1,0:T(8,128)(2,1)S(1)}, bf16[2,64,512]{2,1,0:T(8,128)(2,1)S(1)}, u32[]{:S(2)}, u32[]{:S(2)}) collective-permute-start(bf16[2,64,512]{2,1,0:T(8,128)(2,1)S(1)} %get-tuple-element.47), channel_id=1, source_target_pairs={{1,0},{2,1},{3,2},{5,4},{6,5},{7,6},{9,8},{10,9},{11,10},{13,12},{... | collective-permute-start | bytes 393224 | tf_op jit(solution)/shard_map/ppermute | solution.py:364
  11.0 1.5 %copy-start = (bf16[27,64,512]{2,1,0:T(8,128)(2,1)S(1)}, bf16[27,64,512]{2,1,0:T(8,128)(2,1)}, u32[]{:S(2)}) copy-start(bf16[27,64,512]{2,1,0:T(8,128)(2,1)} %param.7) | copy-start | bytes 5308420
  13.3 4.0 %collective-permute-start.2 = (bf16[2,4,64,128]{3,2,1,0:T(8,128)(2,1)S(1)}, bf16[2,4,64,128]{3,2,1,0:T(8,128)(2,1)S(1)}, u32[]{:S(2)}, u32[]{:S(2)}) collective-permute-start(bf16[2,4,64,128]{3,2,1,0:T(8,128)(2,1)S(1)} %get-tuple-element.51.refs_2_), channel_id=1, source_target_pairs={{0,4},{1,5},{2,6},{3,7},{4,0},{5,1},{6,2},{7,3},{8,12},{9,13},{10,... | collective-permute-start | bytes 393224 | tf_op jit(solution)/shard_map/ppermute | solution.py:364
  14.5 4.0 %collective-permute-start.4 = (bf16[2,4,64,128]{3,2,1,0:T(8,128)(2,1)S(1)}, bf16[2,4,64,128]{3,2,1,0:T(8,128)(2,1)S(1)}, u32[]{:S(2)}, u32[]{:S(2)}) collective-permute-start(bf16[2,4,64,128]{3,2,1,0:T(8,128)(2,1)S(1)} %collective-permute-done.3.refs_2_), channel_id=1, source_target_pairs={{0,4},{1,5},{2,6},{3,7},{4,0},{5,1},{6,2},{7,3},{8,12},{9,13},{10,... | collective-permute-start | bytes 393224 | tf_op jit(solution)/shard_map/ppermute | solution.py:364
  14.6 4.1 %collective-permute-start.7 = (bf16[2,4,64,128]{3,2,1,0:T(8,128)(2,1)S(1)}, bf16[2,4,64,128]{3,2,1,0:T(8,128)(2,1)S(1)}, u32[]{:S(2)}, u32[]{:S(2)}) collective-permute-start(bf16[2,4,64,128]{3,2,1,0:T(8,128)(2,1)S(1)} %collective-permute-done.6.refs_3_), channel_id=1, source_target_pairs={{0,4},{1,5},{2,6},{3,7},{4,0},{5,1},{6,2},{7,3},{8,12},{9,13},{10,... | collective-permute-start | bytes 393224 | tf_op jit(solution)/shard_map/ppermute | solution.py:364
  15.0 3.7 %collective-permute-start.5 = (bf16[2,4,64,128]{3,2,1,0:T(8,128)(2,1)S(1)}, bf16[2,4,64,128]{3,2,1,0:T(8,128)(2,1)S(1)}, u32[]{:S(2)}, u32[]{:S(2)}) collective-permute-start(bf16[2,4,64,128]{3,2,1,0:T(8,128)(2,1)S(1)} %collective-permute-done.refs_3_), channel_id=1, source_target_pairs={{0,4},{1,5},{2,6},{3,7},{4,0},{5,1},{6,2},{7,3},{8,12},{9,13},{10,... | collective-permute-start | bytes 393224 | tf_op jit(solution)/shard_map/ppermute | solution.py:364
  16.0 6.9 %collective-permute-start.13 = (bf16[2,2,64,128]{3,2,1,0:T(8,128)(2,1)S(1)}, bf16[2,2,64,128]{3,2,1,0:T(8,128)(2,1)S(1)}, u32[]{:S(2)}, u32[]{:S(2)}) collective-permute-start(bf16[2,2,64,128]{3,2,1,0:T(8,128)(2,1)S(1)} %get-tuple-element.32), channel_id=1, source_target_pairs={{0,8},{1,9},{2,10},{3,11},{4,20},{5,21},{6,22},{7,23},{8,0},{9,1},... | collective-permute-start | bytes 196616 | tf_op jit(solution)/shard_map/ppermute | solution.py:364
  17.3 5.6 %collective-permute-start.14 = (bf16[2,2,64,128]{3,2,1,0:T(8,128)(2,1)S(1)}, bf16[2,2,64,128]{3,2,1,0:T(8,128)(2,1)S(1)}, u32[]{:S(2)}, u32[]{:S(2)}) collective-permute-start(bf16[2,2,64,128]{3,2,1,0:T(8,128)(2,1)S(1)} %get-tuple-element.33), channel_id=1, source_target_pairs={{0,16},{1,17},{2,18},{3,19},{4,12},{5,13},{6,14},{7,15},{8,24},{9,... | collective-permute-start | bytes 196616 | tf_op jit(solution)/shard_map/ppermute | solution.py:364
  18.5 4.4 %collective-permute-start.15 = (bf16[2,2,64,128]{3,2,1,0:T(8,128)(2,1)S(1)}, bf16[2,2,64,128]{3,2,1,0:T(8,128)(2,1)S(1)}, u32[]{:S(2)}, u32[]{:S(2)}) collective-permute-start(bf16[2,2,64,128]{3,2,1,0:T(8,128)(2,1)S(1)} %get-tuple-element.34), channel_id=1, source_target_pairs={{0,24},{1,25},{2,26},{3,27},{4,28},{5,29},{6,30},{7,31},{8,16},{9,... | collective-permute-start | bytes 196616 | tf_op jit(solution)/shard_map/ppermute | solution.py:364
  21.6 13.3 %collective-permute-start.9 = (bf16[256,512]{1,0:T(8,128)(2,1)S(1)}, bf16[256,512]{1,0:T(8,128)(2,1)S(1)}, u32[]{:S(2)}, u32[]{:S(2)}) collective-permute-start(bf16[256,512]{1,0:T(8,128)(2,1)S(1)} %get-tuple-element.27.refs_8_.refs_4_), channel_id=1, source_target_pairs={{0,8},{1,9},{2,10},{3,11},{4,20},{5,21},{6,22},{7,23},{8,0},{9,1},... | collective-permute-start | bytes 786440 | tf_op jit(solution)/shard_map/ppermute | solution.py:364
  22.9 7.5 %collective-permute-start.16 = (bf16[4,2,2,64,128]{4,3,2,1,0:T(8,128)(2,1)S(1)}, bf16[4,2,2,64,128]{4,3,2,1,0:T(8,128)(2,1)S(1)}, u32[]{:S(2)}, u32[]{:S(2)}) collective-permute-start(bf16[4,2,2,64,128]{4,3,2,1,0:T(8,128)(2,1)S(1)} %stack_halo_rows.1.refs_8_), channel_id=1, source_target_pairs={{0,4},{1,5},{2,6},{3,7},{4,0},{5,1},{6,2},{7,3},{8,12},{9,13},{10,... | collective-permute-start | bytes 786440 | tf_op jit(solution)/shard_map/ppermute | solution.py:364
  26.7 12.8 %collective-permute-start.8 = (bf16[256,512]{1,0:T(8,128)(2,1)S(1)}, bf16[256,512]{1,0:T(8,128)(2,1)S(1)}, u32[]{:S(2)}, u32[]{:S(2)}) collective-permute-start(bf16[256,512]{1,0:T(8,128)(2,1)S(1)} %get-tuple-element.29), channel_id=1, source_target_pairs={{0,8},{1,9},{2,10},{3,11},{4,20},{5,21},{6,22},{7,23},{8,0},{9,1},... | collective-permute-start | bytes 786440 | tf_op jit(solution)/shard_map/ppermute | solution.py:364
  33.3 6.0 %collective-permute-start.17 = (bf16[256,512]{1,0:T(8,128)(2,1)S(1)}, bf16[256,512]{1,0:T(8,128)(2,1)S(1)}, u32[]{:S(2)}, u32[]{:S(2)}) collective-permute-start(bf16[256,512]{1,0:T(8,128)(2,1)S(1)} %get-tuple-element.36), channel_id=1, source_target_pairs={{0,8},{1,9},{2,10},{3,11},{4,20},{5,21},{6,22},{7,23},{8,0},{9,1},... | collective-permute-start | bytes 786440 | tf_op jit(solution)/shard_map/ppermute | solution.py:364
  33.9 15.2 %collective-permute-start.19 = (bf16[256,512]{1,0:T(8,128)(2,1)S(1)}, bf16[256,512]{1,0:T(8,128)(2,1)S(1)}, u32[]{:S(2)}, u32[]{:S(2)}) collective-permute-start(bf16[256,512]{1,0:T(8,128)(2,1)S(1)} %get-tuple-element.39), channel_id=1, source_target_pairs={{0,8},{1,9},{2,10},{3,11},{4,20},{5,21},{6,22},{7,23},{8,0},{9,1},... | collective-permute-start | bytes 786440 | tf_op jit(solution)/shard_map/ppermute | solution.py:364
  34.9 8.4 %collective-permute-start.10 = (bf16[256,512]{1,0:T(8,128)(2,1)S(1)}, bf16[256,512]{1,0:T(8,128)(2,1)S(1)}, u32[]{:S(2)}, u32[]{:S(2)}) collective-permute-start(bf16[256,512]{1,0:T(8,128)(2,1)S(1)} %sum_parts.4.refs_10_), channel_id=1, source_target_pairs={{0,16},{1,17},{2,18},{3,19},{4,12},{5,13},{6,14},{7,15},{8,24},{9,... | collective-permute-start | bytes 786440 | tf_op jit(solution)/shard_map/ppermute | solution.py:364
  38.1 23.1 %copy-start.1 = (bf16[512,512]{1,0:T(8,128)(2,1)S(1)}, bf16[512,512]{1,0:T(8,128)(2,1)}, u32[]{:S(2)}) copy-start(bf16[512,512]{1,0:T(8,128)(2,1)} %refs_8_.1) | copy-start | bytes 1572868
  38.1 23.1 %copy-start.2 = (bf16[512,512]{1,0:T(8,128)(2,1)S(1)}, bf16[512,512]{1,0:T(8,128)(2,1)}, u32[]{:S(2)}) copy-start(bf16[512,512]{1,0:T(8,128)(2,1)} %refs_9_.1) | copy-start | bytes 1572868
  38.1 23.1 %copy-start.3 = (bf16[512,512]{1,0:T(8,128)(2,1)S(1)}, bf16[512,512]{1,0:T(8,128)(2,1)}, u32[]{:S(2)}) copy-start(bf16[512,512]{1,0:T(8,128)(2,1)} %refs_10_.1) | copy-start | bytes 1572868
  38.1 23.1 %copy-start.4 = (bf16[512,512]{1,0:T(8,128)(2,1)S(1)}, bf16[512,512]{1,0:T(8,128)(2,1)}, u32[]{:S(2)}) copy-start(bf16[512,512]{1,0:T(8,128)(2,1)} %refs_11_.1) | copy-start | bytes 1572868
  39.4 9.8 %collective-permute-start.20 = (bf16[256,512]{1,0:T(8,128)(2,1)S(1)}, bf16[256,512]{1,0:T(8,128)(2,1)S(1)}, u32[]{:S(2)}, u32[]{:S(2)}) collective-permute-start(bf16[256,512]{1,0:T(8,128)(2,1)S(1)} %sum_parts.5.refs_3_), channel_id=1, source_target_pairs={{0,16},{1,17},{2,18},{3,19},{4,12},{5,13},{6,14},{7,15},{8,24},{9,... | collective-permute-start | bytes 786440 | tf_op jit(solution)/shard_map/ppermute | solution.py:364
  43.5 10.9 %collective-permute-start.18 = (bf16[128,512]{1,0:T(8,128)(2,1)S(1)}, bf16[128,512]{1,0:T(8,128)(2,1)S(1)}, u32[]{:S(2)}, u32[]{:S(2)}) collective-permute-start(bf16[128,512]{1,0:T(8,128)(2,1)S(1)} %get-tuple-element.37), channel_id=1, source_target_pairs={{0,0},{1,1},{2,4},{3,5},{4,2},{5,3},{6,6},{7,7},{8,8},{9,9},{10,12... | collective-permute-start | bytes 393224 | tf_op jit(solution)/shard_map/ppermute | solution.py:364
  48.6 6.8 %collective-permute-start.22 = (bf16[128,512]{1,0:T(8,128)(2,1)S(1)}, bf16[128,512]{1,0:T(8,128)(2,1)S(1)}, u32[]{:S(2)}, u32[]{:S(2)}) collective-permute-start(bf16[128,512]{1,0:T(8,128)(2,1)S(1)} %get-tuple-element.41), channel_id=1, source_target_pairs={{0,1},{1,0},{2,5},{3,4},{4,3},{5,2},{6,7},{7,6},{8,9},{9,8},{10,13... | collective-permute-start | bytes 393224 | tf_op jit(solution)/shard_map/ppermute | solution.py:364
  49.2 10.5 %collective-permute-start.21 = (bf16[128,512]{1,0:T(8,128)(2,1)S(1)}, bf16[128,512]{1,0:T(8,128)(2,1)S(1)}, u32[]{:S(2)}, u32[]{:S(2)}) collective-permute-start(bf16[128,512]{1,0:T(8,128)(2,1)S(1)} %get-tuple-element.40), channel_id=1, source_target_pairs={{0,0},{1,1},{2,4},{3,5},{4,2},{5,3},{6,6},{7,7},{8,8},{9,9},{10,12... | collective-permute-start | bytes 393224 | tf_op jit(solution)/shard_map/ppermute | solution.py:364
  52.4 7.3 %collective-permute-start.23 = (bf16[128,512]{1,0:T(8,128)(2,1)S(1)}, bf16[128,512]{1,0:T(8,128)(2,1)S(1)}, u32[]{:S(2)}, u32[]{:S(2)}) collective-permute-start(bf16[128,512]{1,0:T(8,128)(2,1)S(1)} %get-tuple-element.42), channel_id=1, source_target_pairs={{0,1},{1,0},{2,5},{3,4},{4,3},{5,2},{6,7},{7,6},{8,9},{9,8},{10,13... | collective-permute-start | bytes 393224 | tf_op jit(solution)/shard_map/ppermute | solution.py:364
  54.3 5.9 %collective-permute-start.24 = (bf16[128,512]{1,0:T(8,128)(2,1)S(1)}, bf16[128,512]{1,0:T(8,128)(2,1)S(1)}, u32[]{:S(2)}, u32[]{:S(2)}) collective-permute-start(bf16[128,512]{1,0:T(8,128)(2,1)S(1)} %collective-permute-done.18.refs_0_), channel_id=1, source_target_pairs={{0,4},{1,5},{2,6},{3,7},{4,0},{5,1},{6,2},{7,3},{8,12},{9,13},{10,... | collective-permute-start | bytes 393224 | tf_op jit(solution)/shard_map/ppermute | solution.py:364
  55.5 4.7 %collective-permute-start.26 = (bf16[128,512]{1,0:T(8,128)(2,1)S(1)}, bf16[128,512]{1,0:T(8,128)(2,1)S(1)}, u32[]{:S(2)}, u32[]{:S(2)}) collective-permute-start(bf16[128,512]{1,0:T(8,128)(2,1)S(1)} %collective-permute-done.22.refs_2_), channel_id=1, source_target_pairs={{0,4},{1,5},{2,6},{3,7},{4,0},{5,1},{6,2},{7,3},{8,12},{9,13},{10,... | collective-permute-start | bytes 393224 | tf_op jit(solution)/shard_map/ppermute | solution.py:364
  59.7 1.3 %collective-permute-start.25 = (bf16[128,512]{1,0:T(8,128)(2,1)S(1)}, bf16[128,512]{1,0:T(8,128)(2,1)S(1)}, u32[]{:S(2)}, u32[]{:S(2)}) collective-permute-start(bf16[128,512]{1,0:T(8,128)(2,1)S(1)} %collective-permute-done.21.refs_1_), channel_id=1, source_target_pairs={{0,4},{1,5},{2,6},{3,7},{4,0},{5,1},{6,2},{7,3},{8,12},{9,13},{10,... | collective-permute-start | bytes 393224 | tf_op jit(solution)/shard_map/ppermute | solution.py:364
  59.7 1.5 %collective-permute-start.27 = (bf16[128,512]{1,0:T(8,128)(2,1)S(1)}, bf16[128,512]{1,0:T(8,128)(2,1)S(1)}, u32[]{:S(2)}, u32[]{:S(2)}) collective-permute-start(bf16[128,512]{1,0:T(8,128)(2,1)S(1)} %collective-permute-done.23.refs_3_), channel_id=1, source_target_pairs={{0,4},{1,5},{2,6},{3,7},{4,0},{5,1},{6,2},{7,3},{8,12},{9,13},{10,... | collective-permute-start | bytes 393224 | tf_op jit(solution)/shard_map/ppermute | solution.py:364
  65.7 10.5 %collective-permute-start.28 = (bf16[4,64,512]{2,1,0:T(8,128)(2,1)S(1)}, bf16[4,64,512]{2,1,0:T(8,128)(2,1)S(1)}, u32[]{:S(2)}, u32[]{:S(2)}) collective-permute-start(bf16[4,64,512]{2,1,0:T(8,128)(2,1)S(1)} %get-tuple-element.43), channel_id=1, source_target_pairs={{1,0},{0,1},{5,2},{4,3},{3,4},{2,5},{7,6},{6,7},{9,8},{8,9},{13,10... | collective-permute-start | bytes 786440 | tf_op jit(solution)/shard_map/ppermute | solution.py:456
  68.4 12.8 %collective-permute-start.29 = (bf16[4,64,512]{2,1,0:T(8,128)(2,1)S(1)}, bf16[4,64,512]{2,1,0:T(8,128)(2,1)S(1)}, u32[]{:S(2)}, u32[]{:S(2)}) collective-permute-start(bf16[4,64,512]{2,1,0:T(8,128)(2,1)S(1)} %get-tuple-element.44), channel_id=1, source_target_pairs={{0,0},{1,1},{4,2},{5,3},{2,4},{3,5},{6,6},{7,7},{8,8},{9,9},{12,10... | collective-permute-start | bytes 786440 | tf_op jit(solution)/shard_map/ppermute | solution.py:456

commit v16 on v15

--- a/solution.py
+++ b/solution.py
@@ -406,21 +406,19 @@
     inner_on, inner_own = conv(
         [(2, False), (0, False)], rims=None, out_type=jnp.float32, after=inner_sent[:1]
     )
-    rims = stack_call(rims, inner_sent[0])
+    rims = stack_call(rims, inner_on)
     rims = (rims, permute(rims, to_member(1)))
     rim_sent = conv([(3, True), (1, True)], rims=rims, out_type=jnp.bfloat16, after=(inner_on,))
     rim_got = hop(rim_sent)
     (inner_relay,) = sum_call([inner_on, inner_got[0]], 1)
     inner_last = permute(inner_relay, to_place(2))
     rim_on, rim_own = conv(
-        [(2, True), (0, True)], rims=rims, out_type=jnp.float32, after=(inner_relay,)
-    )
-    (rim_relay,) = sum_call([rim_on, rim_got[0]], 1)
+        [(2, True), (0, True)], rims=rims, out_type=jnp.float32, after=rim_sent[:1]
+    )
+    inner_sums = sum_call([inner_own, inner_got[1], inner_last], frames, after=(rim_on,))
+    (rim_relay,) = sum_call([rim_on, rim_got[0]], 1, after=inner_sums[:1])
     rim_last = permute(rim_relay, to_place(2))
-    sums = [
-        sum_call([inner_own, inner_got[1], inner_last], frames, after=(rim_relay,)),
-        sum_call([rim_own, rim_got[1], rim_last], frames),
-    ]
+    sums = [inner_sums, sum_call([rim_own, rim_got[1], rim_last], frames)]
 
     share = depth // frames
 

time: 82.4 us -> 83.8 us (1.017)
  waiting for transfers between devices: 22.3 us -> 23.3 us
    ppermute x28, waiting for transfers between devices: 11.7 us -> 12.8 us  [permute(): return lax.ppermute(block, BOTH, everywhere(sizes, target))]
    ppermute x28, starting transfers between devices: 32.5 us -> 33.4 us  [permute(): return lax.ppermute(block, BOTH, everywhere(sizes, target))]
  transfers between devices with their start and end apart: 30 -> 30, of which waited for: 9 -> 8; matrix products, arithmetic and copies ran while one was open for 3% -> 3% of each run, Pallas kernels for 16% -> 16%
where the time goes in v16:
time: 83.8 us; the launch traced here: 83.5 us
  starting transfers between devices  37.7 us (45%)
  waiting for transfers between devices  23.3 us (28%)
  Pallas kernels  17.6 us (21%)
  local copies, waits for them, and re-layouts  3.63 us (4%)
  other arithmetic  0.96 us (1%)
    ppermute x28, starting transfers between devices, permute(): return lax.ppermute(block, BOTH, everywhere(sizes, target))  33.4 us
    ppermute x28, waiting for transfers between devices, permute(): return lax.ppermute(block, BOTH, everywhere(sizes, target))  12.8 us
    pallas_call x4, Pallas kernels, conv_call(): pl.pallas_call(functools.partial(conv_kernel, tuple(jobs), parts, group,...  11.4 us
    ppermute x2, waiting for transfers between devices, body(): back.append(lax.ppermute(done[p], BOTH, pairs))  10.6 us
    pallas_call x1, Pallas kernels, attend_call(): pl.pallas_call(functools.partial(attend_kernel, frames, share, chunks), o...  4.41 us
    ppermute x2, starting transfers between devices, body(): back.append(lax.ppermute(done[p], BOTH, pairs))  4.31 us
  transfers between devices with their start and end apart: 30, of which 8 were waited for; matrix products, arithmetic and copies ran while one was open for 3% of the time, Pallas kernels for 16%

profile of v16, /device:TPU:1, one launch (start us, length us, event | category | flops | bytes accessed | tf_op | source)
XLA Modules:
  0.0 83.5 jit_solution(15812211207997386047)
XLA Ops:
  0.0 0.1 collective-permute-start.1
  0.1 1.1 %constant_dynamic-slice_fusion = (bf16[2,4,64,128]{3,2,1,0:T(8,128)(2,1)S(1)}, bf16[2,4,64,128]{3,2,1,0:T(8,128)(2,1)S(1)}, bf16[2,4,64,128]{3,2,1,0:T(8,128)(2,1)S(1)}, bf16[2,4,64,128]{3,2,1,0:T(8,128)(2,1)S(1)}) fusion(bf16[2,4,64,512]{3,2,1,0:T(8,128)(2,1)} %param.6, s32[]{:T(128)S(6)} %select_n.75, s32[]{:T(128)S(6)} %select_n.74, s32[]{:T(128)S(6)} %select_n.72, ...), kind=kLoop, calls=%fused_computation.5 | loop fusion | bytes 1048592 | tf_op jit(solution)/shard_map/dynamic_slice | solution.py:383
  1.2 2.7 %collective-permute-start = (bf16[2,4,64,128]{3,2,1,0:T(8,128)(2,1)S(1)}, bf16[2,4,64,128]{3,2,1,0:T(8,128)(2,1)S(1)}, u32[]{:S(2)}, u32[]{:S(2)}) collective-permute-start(bf16[2,4,64,128]{3,2,1,0:T(8,128)(2,1)S(1)} %get-tuple-element.52), channel_id=1, source_target_pairs={{0,16},{1,17},{2,18},{3,19},{4,12},{5,13},{6,14},{7,15},{8,24},{9,... | collective-permute-start | bytes 393224 | tf_op jit(solution)/shard_map/ppermute | solution.py:364
  3.9 1.2 %collective-permute-start.3 = (bf16[2,4,64,128]{3,2,1,0:T(8,128)(2,1)S(1)}, bf16[2,4,64,128]{3,2,1,0:T(8,128)(2,1)S(1)}, u32[]{:S(2)}, u32[]{:S(2)}) collective-permute-start(bf16[2,4,64,128]{3,2,1,0:T(8,128)(2,1)S(1)} %get-tuple-element.50), channel_id=1, source_target_pairs={{0,8},{1,9},{2,10},{3,11},{4,20},{5,21},{6,22},{7,23},{8,0},{9,1},... | collective-permute-start | bytes 393224 | tf_op jit(solution)/shard_map/ppermute | solution.py:364
  5.2 0.0 collective-permute-start.6
  5.2 1.0 %slice_bitcast_fusion = (bf16[2,64,512]{2,1,0:T(8,128)(2,1)S(1)}, bf16[2,64,512]{2,1,0:T(8,128)(2,1)S(1)}) fusion(bf16[2,4,64,512]{3,2,1,0:T(8,128)(2,1)} %param.6), kind=kLoop, calls=%fused_computation.3 | loop fusion | bytes 524288 | tf_op jit(solution)/shard_map/squeeze | solution.py:377
  6.2 3.4 %collective-permute-start.11 = (bf16[2,64,512]{2,1,0:T(8,128)(2,1)S(1)}, bf16[2,64,512]{2,1,0:T(8,128)(2,1)S(1)}, u32[]{:S(2)}, u32[]{:S(2)}) collective-permute-start(bf16[2,64,512]{2,1,0:T(8,128)(2,1)S(1)} %get-tuple-element.48), channel_id=1, source_target_pairs={{0,1},{1,2},{2,3},{4,5},{5,6},{6,7},{8,9},{9,10},{10,11},{12,13},{... | collective-permute-start | bytes 393224 | tf_op jit(solution)/shard_map/ppermute | solution.py:364
  9.6 0.1 pad_add_fusion.refs_0_.meta
  9.7 0.0 collective-permute-done.1.refs_2_
  9.7 1.3 %collective-permute-start.12 = (bf16[2,64,512]{2,1,0:T(8,128)(2,1)S(1)}, bf16[2,64,512]{2,1,0:T(8,128)(2,1)S(1)}, u32[]{:S(2)}, u32[]{:S(2)}) collective-permute-start(bf16[2,64,512]{2,1,0:T(8,128)(2,1)S(1)} %get-tuple-element.47), channel_id=1, source_target_pairs={{1,0},{2,1},{3,2},{5,4},{6,5},{7,6},{9,8},{10,9},{11,10},{13,12},{... | collective-permute-start | bytes 393224 | tf_op jit(solution)/shard_map/ppermute | solution.py:364
  11.0 0.0 copy-start
  11.0 1.5 %copy-done = bf16[27,64,512]{2,1,0:T(8,128)(2,1)S(1)} copy-done((bf16[27,64,512]{2,1,0:T(8,128)(2,1)S(1)}, bf16[27,64,512]{2,1,0:T(8,128)(2,1)}, u32[]{:S(2)}) %copy-start) | copy-done | bytes 1769496
  12.4 0.9 %merge_kernel_slices.1.refs_1_ = bf16[3,9,128,512]{3,2,1,0:T(8,128)(2,1)S(1)} custom-call(s32[3]{0:T(128)S(1)} %pad_add_fusion.refs_0_.meta, bf16[9,3,64,512]{3,2,1,0:T(8,128)(2,1)S(1)} %bitcast.17, bf16[9,3,64,512]{3,2,1,0:T(8,128)(2,1)S(1)} %collective-permute-done.1.refs_2_), custom_call_target="tpu_custom_call" | custom-call | tf_op jit(solution)/shard_map/merge_kernel_slices/pallas_call | solution.py:58
  13.3 1.2 %collective-permute-start.2 = (bf16[2,4,64,128]{3,2,1,0:T(8,128)(2,1)S(1)}, bf16[2,4,64,128]{3,2,1,0:T(8,128)(2,1)S(1)}, u32[]{:S(2)}, u32[]{:S(2)}) collective-permute-start(bf16[2,4,64,128]{3,2,1,0:T(8,128)(2,1)S(1)} %get-tuple-element.51.refs_2_), channel_id=1, source_target_pairs={{0,4},{1,5},{2,6},{3,7},{4,0},{5,1},{6,2},{7,3},{8,12},{9,13},{10,... | collective-permute-start | bytes 393224 | tf_op jit(solution)/shard_map/ppermute | solution.py:364
  14.5 0.0 collective-permute-done.3.refs_2_
  14.5 0.1 collective-permute-start.4
  14.6 0.0 collective-permute-done.6.refs_3_
  14.6 0.4 collective-permute-start.7
  15.0 0.0 collective-permute-done.11.above
  15.0 0.1 collective-permute-start.5
  15.1 0.3 collective-permute-done.12.below
  15.4 0.6 split_halo_rows.1
  16.0 1.3 %collective-permute-start.13 = (bf16[2,2,64,128]{3,2,1,0:T(8,128)(2,1)S(1)}, bf16[2,2,64,128]{3,2,1,0:T(8,128)(2,1)S(1)}, u32[]{:S(2)}, u32[]{:S(2)}) collective-permute-start(bf16[2,2,64,128]{3,2,1,0:T(8,128)(2,1)S(1)} %get-tuple-element.32), channel_id=1, source_target_pairs={{0,8},{1,9},{2,10},{3,11},{4,20},{5,21},{6,22},{7,23},{8,0},{9,1},... | collective-permute-start | bytes 196616 | tf_op jit(solution)/shard_map/ppermute | solution.py:364
  17.3 0.0 collective-permute-done.2.refs_4_
  17.3 1.2 %collective-permute-start.14 = (bf16[2,2,64,128]{3,2,1,0:T(8,128)(2,1)S(1)}, bf16[2,2,64,128]{3,2,1,0:T(8,128)(2,1)S(1)}, u32[]{:S(2)}, u32[]{:S(2)}) collective-permute-start(bf16[2,2,64,128]{3,2,1,0:T(8,128)(2,1)S(1)} %get-tuple-element.33), channel_id=1, source_target_pairs={{0,16},{1,17},{2,18},{3,19},{4,12},{5,13},{6,14},{7,15},{8,24},{9,... | collective-permute-start | bytes 196616 | tf_op jit(solution)/shard_map/ppermute | solution.py:364
  18.5 0.2 collective-permute-start.15
  18.7 0.0 collective-permute-done.5.refs_6_
  18.7 2.9 %conv_inner.2 = (bf16[256,512]{1,0:T(8,128)(2,1)S(1)}, bf16[256,512]{1,0:T(8,128)(2,1)S(1)}) custom-call(s32[3]{0:T(128)S(1)} %pad_add_fusion.refs_0_.meta, bf16[3,9,128,512]{3,2,1,0:T(8,128)(2,1)S(1)} %merge_kernel_slices.1.refs_1_, bf16[2,4,64,128]{3,2,1,0:T(8,128)(2,1)S(1)} %collective-permute-done.3.refs_2_, ...), custom_call_target="tpu_custom_call" | custom-call | flops 18119393280 | bytes 3538944 | tf_op jit(solution)/shard_map/conv_inner/pallas_call | solution.py:200
  21.6 1.3 %collective-permute-start.9 = (bf16[256,512]{1,0:T(8,128)(2,1)S(1)}, bf16[256,512]{1,0:T(8,128)(2,1)S(1)}, u32[]{:S(2)}, u32[]{:S(2)}) collective-permute-start(bf16[256,512]{1,0:T(8,128)(2,1)S(1)} %get-tuple-element.27.refs_8_), channel_id=1, source_target_pairs={{0,8},{1,9},{2,10},{3,11},{4,20},{5,21},{6,22},{7,23},{8,0},{9,1},... | collective-permute-start | bytes 786440 | tf_op jit(solution)/shard_map/ppermute | solution.py:364
  22.9 2.8 %conv_inner.3 = (f32[256,512]{1,0:T(8,128)S(1)}, f32[256,512]{1,0:T(8,128)S(1)}) custom-call(s32[3]{0:T(128)S(1)} %pad_add_fusion.refs_0_.meta, bf16[3,9,128,512]{3,2,1,0:T(8,128)(2,1)S(1)} %merge_kernel_slices.1.refs_1_, bf16[2,4,64,128]{3,2,1,0:T(8,128)(2,1)S(1)} %get-tuple-element.51.refs_2_, bf16[2,4,64,128]{3,2,1,0:T(8,128)(2,1)S(1)} %collective-permute-done.refs_3_, ...), custom_call_target="tpu_custom_call" | custom-call | flops 18119393280 | bytes 3538944 | tf_op jit(solution)/shard_map/conv_inner/pallas_call | solution.py:200
  25.7 0.0 collective-permute-done.14.refs_2_
  25.8 3.5 %collective-permute-start.16 = (bf16[4,2,2,64,128]{4,3,2,1,0:T(8,128)(2,1)S(1)}, bf16[4,2,2,64,128]{4,3,2,1,0:T(8,128)(2,1)S(1)}, u32[]{:S(2)}, u32[]{:S(2)}) collective-permute-start(bf16[4,2,2,64,128]{4,3,2,1,0:T(8,128)(2,1)S(1)} %stack_halo_rows.1.refs_8_), channel_id=1, source_target_pairs={{0,4},{1,5},{2,6},{3,7},{4,0},{5,1},{6,2},{7,3},{8,12},{9,13},{10,... | collective-permute-start | bytes 786440 | tf_op jit(solution)/shard_map/ppermute | solution.py:364
  29.2 1.2 %collective-permute-start.8 = (bf16[256,512]{1,0:T(8,128)(2,1)S(1)}, bf16[256,512]{1,0:T(8,128)(2,1)S(1)}, u32[]{:S(2)}, u32[]{:S(2)}) collective-permute-start(bf16[256,512]{1,0:T(8,128)(2,1)S(1)} %get-tuple-element.29), channel_id=1, source_target_pairs={{0,8},{1,9},{2,10},{3,11},{4,20},{5,21},{6,22},{7,23},{8,0},{9,1},... | collective-permute-start | bytes 786440 | tf_op jit(solution)/shard_map/ppermute | solution.py:364
  30.5 0.1 sum_parts.4
  30.6 0.3 collective-permute-start.10
  30.8 2.9 %conv_rim.2 = (bf16[256,512]{1,0:T(8,128)(2,1)S(1)}, bf16[256,512]{1,0:T(8,128)(2,1)S(1)}) custom-call(s32[3]{0:T(128)S(1)} %pad_add_fusion.refs_0_.meta, bf16[3,9,128,512]{3,2,1,0:T(8,128)(2,1)S(1)} %merge_kernel_slices.1.refs_1_, bf16[2,4,64,128]{3,2,1,0:T(8,128)(2,1)S(1)} %collective-permute-done.3.refs_2_, ...), custom_call_target="tpu_custom_call" | custom-call | flops 18119393280 | bytes 3538944 | tf_op jit(solution)/shard_map/conv_rim/pallas_call | solution.py:200
  33.7 0.9 %collective-permute-start.18 = (bf16[256,512]{1,0:T(8,128)(2,1)S(1)}, bf16[256,512]{1,0:T(8,128)(2,1)S(1)}, u32[]{:S(2)}, u32[]{:S(2)}) collective-permute-start(bf16[256,512]{1,0:T(8,128)(2,1)S(1)} %get-tuple-element.39), channel_id=1, source_target_pairs={{0,8},{1,9},{2,10},{3,11},{4,20},{5,21},{6,22},{7,23},{8,0},{9,1},... | collective-permute-start | bytes 786440 | tf_op jit(solution)/shard_map/ppermute | solution.py:364
  34.6 0.7 collective-permute-start.19
  35.2 2.9 %conv_rim.3 = (f32[256,512]{1,0:T(8,128)S(1)}, f32[256,512]{1,0:T(8,128)S(1)}) custom-call(s32[3]{0:T(128)S(1)} %pad_add_fusion.refs_0_.meta, bf16[3,9,128,512]{3,2,1,0:T(8,128)(2,1)S(1)} %merge_kernel_slices.1.refs_1_, bf16[2,4,64,128]{3,2,1,0:T(8,128)(2,1)S(1)} %get-tuple-element.51.refs_2_, bf16[2,4,64,128]{3,2,1,0:T(8,128)(2,1)S(1)} %collective-permute-done.refs_3_, ...), custom_call_target="tpu_custom_call" | custom-call | flops 18119393280 | bytes 3538944 | tf_op jit(solution)/shard_map/conv_rim/pallas_call | solution.py:200
  38.1 0.0 collective-permute-done.10.refs_2_
  38.1 0.0 copy-start.1
  38.1 0.0 copy-start.2
  38.1 0.0 copy-start.3
  38.2 0.0 copy-start.4
  38.2 0.1 sum_parts.5
  38.3 4.9 %collective-permute-done.19.refs_1_ = bf16[256,512]{1,0:T(8,128)(2,1)S(1)} collective-permute-done((bf16[256,512]{1,0:T(8,128)(2,1)S(1)}, bf16[256,512]{1,0:T(8,128)(2,1)S(1)}, u32[]{:S(2)}, u32[]{:S(2)}) %collective-permute-start.19) | collective-permute-done | bytes 262176 | tf_op jit(solution)/shard_map/ppermute | solution.py:364
  43.2 0.1 sum_parts.6
  43.3 0.9 %collective-permute-start.20 = (bf16[256,512]{1,0:T(8,128)(2,1)S(1)}, bf16[256,512]{1,0:T(8,128)(2,1)S(1)}, u32[]{:S(2)}, u32[]{:S(2)}) collective-permute-start(bf16[256,512]{1,0:T(8,128)(2,1)S(1)} %sum_parts.6), channel_id=1, source_target_pairs={{0,16},{1,17},{2,18},{3,19},{4,12},{5,13},{6,14},{7,15},{8,24},{9,... | collective-permute-start | bytes 786440 | tf_op jit(solution)/shard_map/ppermute | solution.py:364
  44.2 5.5 %collective-permute-start.17 = (bf16[128,512]{1,0:T(8,128)(2,1)S(1)}, bf16[128,512]{1,0:T(8,128)(2,1)S(1)}, u32[]{:S(2)}, u32[]{:S(2)}) collective-permute-start(bf16[128,512]{1,0:T(8,128)(2,1)S(1)} %get-tuple-element.37.refs_2_), channel_id=1, source_target_pairs={{0,0},{1,1},{2,4},{3,5},{4,2},{5,3},{6,6},{7,7},{8,8},{9,9},{10,12... | collective-permute-start | bytes 393224 | tf_op jit(solution)/shard_map/ppermute | solution.py:364
  49.7 0.1 collective-permute-start.22
  49.8 0.1 sum_parts.7
  49.9 5.6 %collective-permute-start.21 = (bf16[128,512]{1,0:T(8,128)(2,1)S(1)}, bf16[128,512]{1,0:T(8,128)(2,1)S(1)}, u32[]{:S(2)}, u32[]{:S(2)}) collective-permute-start(bf16[128,512]{1,0:T(8,128)(2,1)S(1)} %get-tuple-element.40), channel_id=1, source_target_pairs={{0,0},{1,1},{2,4},{3,5},{4,2},{5,3},{6,6},{7,7},{8,8},{9,9},{10,12... | collective-permute-start | bytes 393224 | tf_op jit(solution)/shard_map/ppermute | solution.py:364
  55.6 0.1 collective-permute-start.23
  55.7 0.1 collective-permute-start.24
  55.7 1.3 %collective-permute-done.22.refs_2_ = bf16[128,512]{1,0:T(8,128)(2,1)S(1)} collective-permute-done((bf16[128,512]{1,0:T(8,128)(2,1)S(1)}, bf16[128,512]{1,0:T(8,128)(2,1)S(1)}, u32[]{:S(2)}, u32[]{:S(2)}) %collective-permute-start.22) | collective-permute-done | bytes 131104 | tf_op jit(solution)/shard_map/ppermute | solution.py:364
  57.0 2.7 %collective-permute-done.21.refs_1_ = bf16[128,512]{1,0:T(8,128)(2,1)S(1)} collective-permute-done((bf16[128,512]{1,0:T(8,128)(2,1)S(1)}, bf16[128,512]{1,0:T(8,128)(2,1)S(1)}, u32[]{:S(2)}, u32[]{:S(2)}) %collective-permute-start.21) | collective-permute-done | bytes 131104 | tf_op jit(solution)/shard_map/ppermute | solution.py:364
  59.7 2.2 %collective-permute-done.23.refs_3_ = bf16[128,512]{1,0:T(8,128)(2,1)S(1)} collective-permute-done((bf16[128,512]{1,0:T(8,128)(2,1)S(1)}, bf16[128,512]{1,0:T(8,128)(2,1)S(1)}, u32[]{:S(2)}, u32[]{:S(2)}) %collective-permute-start.23) | collective-permute-done | bytes 131104 | tf_op jit(solution)/shard_map/ppermute | solution.py:364
  62.0 1.3 %collective-permute-done.27.refs_7_ = bf16[128,512]{1,0:T(8,128)(2,1)S(1)} collective-permute-done((bf16[128,512]{1,0:T(8,128)(2,1)S(1)}, bf16[128,512]{1,0:T(8,128)(2,1)S(1)}, u32[]{:S(2)}, u32[]{:S(2)}) %collective-permute-start.27) | collective-permute-done | bytes 131104 | tf_op jit(solution)/shard_map/ppermute | solution.py:364
  63.3 4.4 %attend.1 = (bf16[4,64,512]{2,1,0:T(8,128)(2,1)S(1)}, bf16[4,64,512]{2,1,0:T(8,128)(2,1)S(1)}) custom-call(bf16[128,512]{1,0:T(8,128)(2,1)S(1)} %collective-permute-done.17.refs_0_, bf16[128,512]{1,0:T(8,128)(2,1)S(1)} %collective-permute-done.21.refs_1_, bf16[128,512]{1,0:T(8,128)(2,1)S(1)} %collective-permute-done.22.refs_2_, ...), custom_call_target="tpu_custom_call" | custom-call | flops 2684354560 | bytes 3145728 | tf_op jit(solution)/shard_map/attend/pallas_call | solution.py:335
  67.7 2.0 %collective-permute-start.28 = (bf16[4,64,512]{2,1,0:T(8,128)(2,1)S(1)}, bf16[4,64,512]{2,1,0:T(8,128)(2,1)S(1)}, u32[]{:S(2)}, u32[]{:S(2)}) collective-permute-start(bf16[4,64,512]{2,1,0:T(8,128)(2,1)S(1)} %get-tuple-element.43), channel_id=1, source_target_pairs={{1,0},{0,1},{5,2},{4,3},{3,4},{2,5},{7,6},{6,7},{9,8},{8,9},{13,10... | collective-permute-start | bytes 786440 | tf_op jit(solution)/shard_map/ppermute | solution.py:454
  69.7 2.4 %collective-permute-start.29 = (bf16[4,64,512]{2,1,0:T(8,128)(2,1)S(1)}, bf16[4,64,512]{2,1,0:T(8,128)(2,1)S(1)}, u32[]{:S(2)}, u32[]{:S(2)}) collective-permute-start(bf16[4,64,512]{2,1,0:T(8,128)(2,1)S(1)} %get-tuple-element.44), channel_id=1, source_target_pairs={{0,0},{1,1},{4,2},{5,3},{2,4},{3,5},{6,6},{7,7},{8,8},{9,9},{12,10... | collective-permute-start | bytes 786440 | tf_op jit(solution)/shard_map/ppermute | solution.py:454
  72.0 5.4 %collective-permute-done.28 = bf16[4,64,512]{2,1,0:T(8,128)(2,1)S(1)} collective-permute-done((bf16[4,64,512]{2,1,0:T(8,128)(2,1)S(1)}, bf16[4,64,512]{2,1,0:T(8,128)(2,1)S(1)}, u32[]{:S(2)}, u32[]{:S(2)}) %collective-permute-start.28) | collective-permute-done | bytes 262176 | tf_op jit(solution)/shard_map/ppermute | solution.py:454
  77.5 5.1 %collective-permute-done.29 = bf16[4,64,512]{2,1,0:T(8,128)(2,1)S(1)} collective-permute-done((bf16[4,64,512]{2,1,0:T(8,128)(2,1)S(1)}, bf16[4,64,512]{2,1,0:T(8,128)(2,1)S(1)}, u32[]{:S(2)}, u32[]{:S(2)}) %collective-permute-start.29) | collective-permute-done | bytes 262176 | tf_op jit(solution)/shard_map/ppermute | solution.py:454
  82.6 0.8 %pad_maximum_fusion = bf16[2,4,64,512]{3,2,1,0:T(8,128)(2,1)} fusion(bf16[1,4,64,512]{3,2,1,0:T(8,128)(2,1)S(1)} %get-tuple-element.46, bf16[1,4,64,512]{3,2,1,0:T(8,128)(2,1)S(1)} %get-tuple-element.45), kind=kLoop, calls=%fused_computation | loop fusion | flops 262144 | bytes 1048576 | tf_op jit(solution)/shard_map/stack | solution.py:455
  (23 shorter events, 0.1 us)
Async XLA Ops:
  0.0 9.7 %collective-permute-start.1 = (bf16[9,3,64,512]{3,2,1,0:T(8,128)(2,1)}, bf16[9,3,64,512]{3,2,1,0:T(8,128)(2,1)S(1)}, u32[]{:S(2)}, u32[]{:S(2)}) collective-permute-start(bf16[9,3,64,512]{3,2,1,0:T(8,128)(2,1)} %bitcast.16), channel_id=1, source_target_pairs={{0,4},{1,5},{2,6},{3,7},{4,0},{5,1},{6,2},{7,3},{8,12},{9,13},{10,... | collective-permute-start | bytes 5308424 | tf_op jit(solution)/shard_map/ppermute | solution.py:364
  1.2 12.1 %collective-permute-start = (bf16[2,4,64,128]{3,2,1,0:T(8,128)(2,1)S(1)}, bf16[2,4,64,128]{3,2,1,0:T(8,128)(2,1)S(1)}, u32[]{:S(2)}, u32[]{:S(2)}) collective-permute-start(bf16[2,4,64,128]{3,2,1,0:T(8,128)(2,1)S(1)} %get-tuple-element.52), channel_id=1, source_target_pairs={{0,16},{1,17},{2,18},{3,19},{4,12},{5,13},{6,14},{7,15},{8,24},{9,... | collective-permute-start | bytes 393224 | tf_op jit(solution)/shard_map/ppermute | solution.py:364
  3.9 10.6 %collective-permute-start.3 = (bf16[2,4,64,128]{3,2,1,0:T(8,128)(2,1)S(1)}, bf16[2,4,64,128]{3,2,1,0:T(8,128)(2,1)S(1)}, u32[]{:S(2)}, u32[]{:S(2)}) collective-permute-start(bf16[2,4,64,128]{3,2,1,0:T(8,128)(2,1)S(1)} %get-tuple-element.50), channel_id=1, source_target_pairs={{0,8},{1,9},{2,10},{3,11},{4,20},{5,21},{6,22},{7,23},{8,0},{9,1},... | collective-permute-start | bytes 393224 | tf_op jit(solution)/shard_map/ppermute | solution.py:364
  5.2 9.4 %collective-permute-start.6 = (bf16[2,4,64,128]{3,2,1,0:T(8,128)(2,1)S(1)}, bf16[2,4,64,128]{3,2,1,0:T(8,128)(2,1)S(1)}, u32[]{:S(2)}, u32[]{:S(2)}) collective-permute-start(bf16[2,4,64,128]{3,2,1,0:T(8,128)(2,1)S(1)} %get-tuple-element.49), channel_id=1, source_target_pairs={{0,24},{1,25},{2,26},{3,27},{4,28},{5,29},{6,30},{7,31},{8,16},{9,... | collective-permute-start | bytes 393224 | tf_op jit(solution)/shard_map/ppermute | solution.py:364
  6.2 8.8 %collective-permute-start.11 = (bf16[2,64,512]{2,1,0:T(8,128)(2,1)S(1)}, bf16[2,64,512]{2,1,0:T(8,128)(2,1)S(1)}, u32[]{:S(2)}, u32[]{:S(2)}) collective-permute-start(bf16[2,64,512]{2,1,0:T(8,128)(2,1)S(1)} %get-tuple-element.48), channel_id=1, source_target_pairs={{0,1},{1,2},{2,3},{4,5},{5,6},{6,7},{8,9},{9,10},{10,11},{12,13},{... | collective-permute-start | bytes 393224 | tf_op jit(solution)/shard_map/ppermute | solution.py:364
  9.7 5.7 %collective-permute-start.12 = (bf16[2,64,512]{2,1,0:T(8,128)(2,1)S(1)}, bf16[2,64,512]{2,1,0:T(8,128)(2,1)S(1)}, u32[]{:S(2)}, u32[]{:S(2)}) collective-permute-start(bf16[2,64,512]{2,1,0:T(8,128)(2,1)S(1)} %get-tuple-element.47), channel_id=1, source_target_pairs={{1,0},{2,1},{3,2},{5,4},{6,5},{7,6},{9,8},{10,9},{11,10},{13,12},{... | collective-permute-start | bytes 393224 | tf_op jit(solution)/shard_map/ppermute | solution.py:364
  11.0 1.5 %copy-start = (bf16[27,64,512]{2,1,0:T(8,128)(2,1)S(1)}, bf16[27,64,512]{2,1,0:T(8,128)(2,1)}, u32[]{:S(2)}) copy-start(bf16[27,64,512]{2,1,0:T(8,128)(2,1)} %param.7) | copy-start | bytes 5308420
  13.3 4.0 %collective-permute-start.2 = (bf16[2,4,64,128]{3,2,1,0:T(8,128)(2,1)S(1)}, bf16[2,4,64,128]{3,2,1,0:T(8,128)(2,1)S(1)}, u32[]{:S(2)}, u32[]{:S(2)}) collective-permute-start(bf16[2,4,64,128]{3,2,1,0:T(8,128)(2,1)S(1)} %get-tuple-element.51.refs_2_), channel_id=1, source_target_pairs={{0,4},{1,5},{2,6},{3,7},{4,0},{5,1},{6,2},{7,3},{8,12},{9,13},{10,... | collective-permute-start | bytes 393224 | tf_op jit(solution)/shard_map/ppermute | solution.py:364
  14.5 4.0 %collective-permute-start.4 = (bf16[2,4,64,128]{3,2,1,0:T(8,128)(2,1)S(1)}, bf16[2,4,64,128]{3,2,1,0:T(8,128)(2,1)S(1)}, u32[]{:S(2)}, u32[]{:S(2)}) collective-permute-start(bf16[2,4,64,128]{3,2,1,0:T(8,128)(2,1)S(1)} %collective-permute-done.3.refs_2_), channel_id=1, source_target_pairs={{0,4},{1,5},{2,6},{3,7},{4,0},{5,1},{6,2},{7,3},{8,12},{9,13},{10,... | collective-permute-start | bytes 393224 | tf_op jit(solution)/shard_map/ppermute | solution.py:364
  14.6 4.1 %collective-permute-start.7 = (bf16[2,4,64,128]{3,2,1,0:T(8,128)(2,1)S(1)}, bf16[2,4,64,128]{3,2,1,0:T(8,128)(2,1)S(1)}, u32[]{:S(2)}, u32[]{:S(2)}) collective-permute-start(bf16[2,4,64,128]{3,2,1,0:T(8,128)(2,1)S(1)} %collective-permute-done.6.refs_3_), channel_id=1, source_target_pairs={{0,4},{1,5},{2,6},{3,7},{4,0},{5,1},{6,2},{7,3},{8,12},{9,13},{10,... | collective-permute-start | bytes 393224 | tf_op jit(solution)/shard_map/ppermute | solution.py:364
  15.0 3.7 %collective-permute-start.5 = (bf16[2,4,64,128]{3,2,1,0:T(8,128)(2,1)S(1)}, bf16[2,4,64,128]{3,2,1,0:T(8,128)(2,1)S(1)}, u32[]{:S(2)}, u32[]{:S(2)}) collective-permute-start(bf16[2,4,64,128]{3,2,1,0:T(8,128)(2,1)S(1)} %collective-permute-done.refs_3_), channel_id=1, source_target_pairs={{0,4},{1,5},{2,6},{3,7},{4,0},{5,1},{6,2},{7,3},{8,12},{9,13},{10,... | collective-permute-start | bytes 393224 | tf_op jit(solution)/shard_map/ppermute | solution.py:364
  16.0 9.8 %collective-permute-start.13 = (bf16[2,2,64,128]{3,2,1,0:T(8,128)(2,1)S(1)}, bf16[2,2,64,128]{3,2,1,0:T(8,128)(2,1)S(1)}, u32[]{:S(2)}, u32[]{:S(2)}) collective-permute-start(bf16[2,2,64,128]{3,2,1,0:T(8,128)(2,1)S(1)} %get-tuple-element.32), channel_id=1, source_target_pairs={{0,8},{1,9},{2,10},{3,11},{4,20},{5,21},{6,22},{7,23},{8,0},{9,1},... | collective-permute-start | bytes 196616 | tf_op jit(solution)/shard_map/ppermute | solution.py:364
  17.3 8.5 %collective-permute-start.14 = (bf16[2,2,64,128]{3,2,1,0:T(8,128)(2,1)S(1)}, bf16[2,2,64,128]{3,2,1,0:T(8,128)(2,1)S(1)}, u32[]{:S(2)}, u32[]{:S(2)}) collective-permute-start(bf16[2,2,64,128]{3,2,1,0:T(8,128)(2,1)S(1)} %get-tuple-element.33), channel_id=1, source_target_pairs={{0,16},{1,17},{2,18},{3,19},{4,12},{5,13},{6,14},{7,15},{8,24},{9,... | collective-permute-start | bytes 196616 | tf_op jit(solution)/shard_map/ppermute | solution.py:364
  18.5 7.2 %collective-permute-start.15 = (bf16[2,2,64,128]{3,2,1,0:T(8,128)(2,1)S(1)}, bf16[2,2,64,128]{3,2,1,0:T(8,128)(2,1)S(1)}, u32[]{:S(2)}, u32[]{:S(2)}) collective-permute-start(bf16[2,2,64,128]{3,2,1,0:T(8,128)(2,1)S(1)} %get-tuple-element.34), channel_id=1, source_target_pairs={{0,24},{1,25},{2,26},{3,27},{4,28},{5,29},{6,30},{7,31},{8,16},{9,... | collective-permute-start | bytes 196616 | tf_op jit(solution)/shard_map/ppermute | solution.py:364
  21.6 8.9 %collective-permute-start.9 = (bf16[256,512]{1,0:T(8,128)(2,1)S(1)}, bf16[256,512]{1,0:T(8,128)(2,1)S(1)}, u32[]{:S(2)}, u32[]{:S(2)}) collective-permute-start(bf16[256,512]{1,0:T(8,128)(2,1)S(1)} %get-tuple-element.27.refs_8_), channel_id=1, source_target_pairs={{0,8},{1,9},{2,10},{3,11},{4,20},{5,21},{6,22},{7,23},{8,0},{9,1},... | collective-permute-start | bytes 786440 | tf_op jit(solution)/shard_map/ppermute | solution.py:364
  25.8 5.1 %collective-permute-start.16 = (bf16[4,2,2,64,128]{4,3,2,1,0:T(8,128)(2,1)S(1)}, bf16[4,2,2,64,128]{4,3,2,1,0:T(8,128)(2,1)S(1)}, u32[]{:S(2)}, u32[]{:S(2)}) collective-permute-start(bf16[4,2,2,64,128]{4,3,2,1,0:T(8,128)(2,1)S(1)} %stack_halo_rows.1.refs_8_), channel_id=1, source_target_pairs={{0,4},{1,5},{2,6},{3,7},{4,0},{5,1},{6,2},{7,3},{8,12},{9,13},{10,... | collective-permute-start | bytes 786440 | tf_op jit(solution)/shard_map/ppermute | solution.py:364
  29.2 8.9 %collective-permute-start.8 = (bf16[256,512]{1,0:T(8,128)(2,1)S(1)}, bf16[256,512]{1,0:T(8,128)(2,1)S(1)}, u32[]{:S(2)}, u32[]{:S(2)}) collective-permute-start(bf16[256,512]{1,0:T(8,128)(2,1)S(1)} %get-tuple-element.29), channel_id=1, source_target_pairs={{0,8},{1,9},{2,10},{3,11},{4,20},{5,21},{6,22},{7,23},{8,0},{9,1},... | collective-permute-start | bytes 786440 | tf_op jit(solution)/shard_map/ppermute | solution.py:364
  30.6 7.6 %collective-permute-start.10 = (bf16[256,512]{1,0:T(8,128)(2,1)S(1)}, bf16[256,512]{1,0:T(8,128)(2,1)S(1)}, u32[]{:S(2)}, u32[]{:S(2)}) collective-permute-start(bf16[256,512]{1,0:T(8,128)(2,1)S(1)} %sum_parts.4), channel_id=1, source_target_pairs={{0,16},{1,17},{2,18},{3,19},{4,12},{5,13},{6,14},{7,15},{8,24},{9,... | collective-permute-start | bytes 786440 | tf_op jit(solution)/shard_map/ppermute | solution.py:364
  33.7 16.1 %collective-permute-start.18 = (bf16[256,512]{1,0:T(8,128)(2,1)S(1)}, bf16[256,512]{1,0:T(8,128)(2,1)S(1)}, u32[]{:S(2)}, u32[]{:S(2)}) collective-permute-start(bf16[256,512]{1,0:T(8,128)(2,1)S(1)} %get-tuple-element.39), channel_id=1, source_target_pairs={{0,8},{1,9},{2,10},{3,11},{4,20},{5,21},{6,22},{7,23},{8,0},{9,1},... | collective-permute-start | bytes 786440 | tf_op jit(solution)/shard_map/ppermute | solution.py:364
  34.6 8.6 %collective-permute-start.19 = (bf16[256,512]{1,0:T(8,128)(2,1)S(1)}, bf16[256,512]{1,0:T(8,128)(2,1)S(1)}, u32[]{:S(2)}, u32[]{:S(2)}) collective-permute-start(bf16[256,512]{1,0:T(8,128)(2,1)S(1)} %get-tuple-element.35.refs_10_), channel_id=1, source_target_pairs={{0,8},{1,9},{2,10},{3,11},{4,20},{5,21},{6,22},{7,23},{8,0},{9,1},... | collective-permute-start | bytes 786440 | tf_op jit(solution)/shard_map/ppermute | solution.py:364
  38.1 25.2 %copy-start.1 = (bf16[512,512]{1,0:T(8,128)(2,1)S(1)}, bf16[512,512]{1,0:T(8,128)(2,1)}, u32[]{:S(2)}) copy-start(bf16[512,512]{1,0:T(8,128)(2,1)} %refs_8_.1) | copy-start | bytes 1572868
  38.1 25.1 %copy-start.2 = (bf16[512,512]{1,0:T(8,128)(2,1)S(1)}, bf16[512,512]{1,0:T(8,128)(2,1)}, u32[]{:S(2)}) copy-start(bf16[512,512]{1,0:T(8,128)(2,1)} %refs_9_.1) | copy-start | bytes 1572868
  38.1 25.1 %copy-start.3 = (bf16[512,512]{1,0:T(8,128)(2,1)S(1)}, bf16[512,512]{1,0:T(8,128)(2,1)}, u32[]{:S(2)}) copy-start(bf16[512,512]{1,0:T(8,128)(2,1)} %refs_10_.1) | copy-start | bytes 1572868
  38.2 25.1 %copy-start.4 = (bf16[512,512]{1,0:T(8,128)(2,1)S(1)}, bf16[512,512]{1,0:T(8,128)(2,1)}, u32[]{:S(2)}) copy-start(bf16[512,512]{1,0:T(8,128)(2,1)} %refs_11_.1) | copy-start | bytes 1572868
  43.3 6.6 %collective-permute-start.20 = (bf16[256,512]{1,0:T(8,128)(2,1)S(1)}, bf16[256,512]{1,0:T(8,128)(2,1)S(1)}, u32[]{:S(2)}, u32[]{:S(2)}) collective-permute-start(bf16[256,512]{1,0:T(8,128)(2,1)S(1)} %sum_parts.6), channel_id=1, source_target_pairs={{0,16},{1,17},{2,18},{3,19},{4,12},{5,13},{6,14},{7,15},{8,24},{9,... | collective-permute-start | bytes 786440 | tf_op jit(solution)/shard_map/ppermute | solution.py:364
  44.2 11.5 %collective-permute-start.17 = (bf16[128,512]{1,0:T(8,128)(2,1)S(1)}, bf16[128,512]{1,0:T(8,128)(2,1)S(1)}, u32[]{:S(2)}, u32[]{:S(2)}) collective-permute-start(bf16[128,512]{1,0:T(8,128)(2,1)S(1)} %get-tuple-element.37.refs_2_), channel_id=1, source_target_pairs={{0,0},{1,1},{2,4},{3,5},{4,2},{5,3},{6,6},{7,7},{8,8},{9,9},{10,12... | collective-permute-start | bytes 393224 | tf_op jit(solution)/shard_map/ppermute | solution.py:364
  49.7 7.3 %collective-permute-start.22 = (bf16[128,512]{1,0:T(8,128)(2,1)S(1)}, bf16[128,512]{1,0:T(8,128)(2,1)S(1)}, u32[]{:S(2)}, u32[]{:S(2)}) collective-permute-start(bf16[128,512]{1,0:T(8,128)(2,1)S(1)} %get-tuple-element.41), channel_id=1, source_target_pairs={{0,1},{1,0},{2,5},{3,4},{4,3},{5,2},{6,7},{7,6},{8,9},{9,8},{10,13... | collective-permute-start | bytes 393224 | tf_op jit(solution)/shard_map/ppermute | solution.py:364
  49.9 9.8 %collective-permute-start.21 = (bf16[128,512]{1,0:T(8,128)(2,1)S(1)}, bf16[128,512]{1,0:T(8,128)(2,1)S(1)}, u32[]{:S(2)}, u32[]{:S(2)}) collective-permute-start(bf16[128,512]{1,0:T(8,128)(2,1)S(1)} %get-tuple-element.40), channel_id=1, source_target_pairs={{0,0},{1,1},{2,4},{3,5},{4,2},{5,3},{6,6},{7,7},{8,8},{9,9},{10,12... | collective-permute-start | bytes 393224 | tf_op jit(solution)/shard_map/ppermute | solution.py:364
  55.6 6.4 %collective-permute-start.23 = (bf16[128,512]{1,0:T(8,128)(2,1)S(1)}, bf16[128,512]{1,0:T(8,128)(2,1)S(1)}, u32[]{:S(2)}, u32[]{:S(2)}) collective-permute-start(bf16[128,512]{1,0:T(8,128)(2,1)S(1)} %get-tuple-element.42), channel_id=1, source_target_pairs={{0,1},{1,0},{2,5},{3,4},{4,3},{5,2},{6,7},{7,6},{8,9},{9,8},{10,13... | collective-permute-start | bytes 393224 | tf_op jit(solution)/shard_map/ppermute | solution.py:364
  55.7 6.3 %collective-permute-start.24 = (bf16[128,512]{1,0:T(8,128)(2,1)S(1)}, bf16[128,512]{1,0:T(8,128)(2,1)S(1)}, u32[]{:S(2)}, u32[]{:S(2)}) collective-permute-start(bf16[128,512]{1,0:T(8,128)(2,1)S(1)} %collective-permute-done.17.refs_0_), channel_id=1, source_target_pairs={{0,4},{1,5},{2,6},{3,7},{4,0},{5,1},{6,2},{7,3},{8,12},{9,13},{10,... | collective-permute-start | bytes 393224 | tf_op jit(solution)/shard_map/ppermute | solution.py:364
  57.0 4.9 %collective-permute-start.26 = (bf16[128,512]{1,0:T(8,128)(2,1)S(1)}, bf16[128,512]{1,0:T(8,128)(2,1)S(1)}, u32[]{:S(2)}, u32[]{:S(2)}) collective-permute-start(bf16[128,512]{1,0:T(8,128)(2,1)S(1)} %collective-permute-done.22.refs_2_), channel_id=1, source_target_pairs={{0,4},{1,5},{2,6},{3,7},{4,0},{5,1},{6,2},{7,3},{8,12},{9,13},{10,... | collective-permute-start | bytes 393224 | tf_op jit(solution)/shard_map/ppermute | solution.py:364
  59.7 2.2 %collective-permute-start.25 = (bf16[128,512]{1,0:T(8,128)(2,1)S(1)}, bf16[128,512]{1,0:T(8,128)(2,1)S(1)}, u32[]{:S(2)}, u32[]{:S(2)}) collective-permute-start(bf16[128,512]{1,0:T(8,128)(2,1)S(1)} %collective-permute-done.21.refs_1_), channel_id=1, source_target_pairs={{0,4},{1,5},{2,6},{3,7},{4,0},{5,1},{6,2},{7,3},{8,12},{9,13},{10,... | collective-permute-start | bytes 393224 | tf_op jit(solution)/shard_map/ppermute | solution.py:364
  61.9 1.3 %collective-permute-start.27 = (bf16[128,512]{1,0:T(8,128)(2,1)S(1)}, bf16[128,512]{1,0:T(8,128)(2,1)S(1)}, u32[]{:S(2)}, u32[]{:S(2)}) collective-permute-start(bf16[128,512]{1,0:T(8,128)(2,1)S(1)} %collective-permute-done.23.refs_3_), channel_id=1, source_target_pairs={{0,4},{1,5},{2,6},{3,7},{4,0},{5,1},{6,2},{7,3},{8,12},{9,13},{10,... | collective-permute-start | bytes 393224 | tf_op jit(solution)/shard_map/ppermute | solution.py:364
  67.7 9.8 %collective-permute-start.28 = (bf16[4,64,512]{2,1,0:T(8,128)(2,1)S(1)}, bf16[4,64,512]{2,1,0:T(8,128)(2,1)S(1)}, u32[]{:S(2)}, u32[]{:S(2)}) collective-permute-start(bf16[4,64,512]{2,1,0:T(8,128)(2,1)S(1)} %get-tuple-element.43), channel_id=1, source_target_pairs={{1,0},{0,1},{5,2},{4,3},{3,4},{2,5},{7,6},{6,7},{9,8},{8,9},{13,10... | collective-permute-start | bytes 786440 | tf_op jit(solution)/shard_map/ppermute | solution.py:454
  69.7 12.9 %collective-permute-start.29 = (bf16[4,64,512]{2,1,0:T(8,128)(2,1)S(1)}, bf16[4,64,512]{2,1,0:T(8,128)(2,1)S(1)}, u32[]{:S(2)}, u32[]{:S(2)}) collective-permute-start(bf16[4,64,512]{2,1,0:T(8,128)(2,1)S(1)} %get-tuple-element.44), channel_id=1, source_target_pairs={{0,0},{1,1},{4,2},{5,3},{2,4},{3,5},{6,6},{7,7},{8,8},{9,9},{12,10... | collective-permute-start | bytes 786440 | tf_op jit(solution)/shard_map/ppermute | solution.py:454

commit v17 on v14

--- a/solution.py
+++ b/solution.py
@@ -308,12 +308,12 @@
         place += rows
         scores = lax.dot_general(
             queries, keys[...], (((1,), (1,)), ((), ())), preferred_element_type=jnp.float32
-        ) * chans ** (-0.5)
+        )
         row_max = jnp.max(scores, axis=1, keepdims=True)
-        exp_weights = jnp.exp(scores - row_max).astype(jnp.bfloat16)
+        exp_weights = jnp.exp((scores - row_max) * chans ** (-0.5)).astype(jnp.bfloat16)
         denominator = jnp.sum(exp_weights.astype(jnp.float32), axis=1, keepdims=True)
         numerator = jnp.dot(exp_weights, values[...], preferred_element_type=jnp.float32)
-        attended = (numerator / denominator).astype(jnp.bfloat16)
+        attended = (numerator * (1.0 / denominator)).astype(jnp.bfloat16)
         added = jnp.dot(attended, wo[...], preferred_element_type=jnp.float32)
         rows_here, columns, _ = out.shape
         inner = mine[0].shape[0]

time: 82.2 us -> 82.2 us (level)
  no operation moved by 1% of the time
where the time goes in v17:
time: 82.2 us; the launch traced here: 81.9 us
  starting transfers between devices  36.5 us (44%)
  waiting for transfers between devices  22.9 us (28%)
  Pallas kernels  17.6 us (21%)
  local copies, waits for them, and re-layouts  3.63 us (4%)
  other arithmetic  0.96 us (1%)
    ppermute x28, starting transfers between devices, permute(): return lax.ppermute(block, BOTH, everywhere(sizes, target))  31.6 us
    ppermute x28, waiting for transfers between devices, permute(): return lax.ppermute(block, BOTH, everywhere(sizes, target))  12.4 us
    pallas_call x4, Pallas kernels, conv_call(): pl.pallas_call(functools.partial(conv_kernel, tuple(jobs), parts, group,...  11.4 us
    ppermute x2, waiting for transfers between devices, body(): back.append(lax.ppermute(done[p], BOTH, pairs))  10.6 us
    ppermute x2, starting transfers between devices, body(): back.append(lax.ppermute(done[p], BOTH, pairs))  4.92 us
    pallas_call x1, Pallas kernels, attend_call(): pl.pallas_call(functools.partial(attend_kernel, frames, share, chunks), o...  4.45 us
  transfers between devices with their start and end apart: 30, of which 9 were waited for; matrix products, arithmetic and copies ran while one was open for 3% of the time, Pallas kernels for 16%

profile of v17, /device:TPU:1, one launch (start us, length us, event | category | flops | bytes accessed | tf_op | source)
XLA Modules:
  0.0 81.9 jit_solution(11717111103769641536)
XLA Ops:
  0.0 0.1 collective-permute-start.1
  0.1 1.1 %constant_dynamic-slice_fusion = (bf16[2,4,64,128]{3,2,1,0:T(8,128)(2,1)S(1)}, bf16[2,4,64,128]{3,2,1,0:T(8,128)(2,1)S(1)}, bf16[2,4,64,128]{3,2,1,0:T(8,128)(2,1)S(1)}, bf16[2,4,64,128]{3,2,1,0:T(8,128)(2,1)S(1)}) fusion(bf16[2,4,64,512]{3,2,1,0:T(8,128)(2,1)} %param.6, s32[]{:T(128)S(6)} %select_n.75, s32[]{:T(128)S(6)} %select_n.74, s32[]{:T(128)S(6)} %select_n.72, ...), kind=kLoop, calls=%fused_computation.5 | loop fusion | bytes 1048592 | tf_op jit(solution)/shard_map/dynamic_slice | solution.py:383
  1.2 2.7 %collective-permute-start = (bf16[2,4,64,128]{3,2,1,0:T(8,128)(2,1)S(1)}, bf16[2,4,64,128]{3,2,1,0:T(8,128)(2,1)S(1)}, u32[]{:S(2)}, u32[]{:S(2)}) collective-permute-start(bf16[2,4,64,128]{3,2,1,0:T(8,128)(2,1)S(1)} %get-tuple-element.52), channel_id=1, source_target_pairs={{0,16},{1,17},{2,18},{3,19},{4,12},{5,13},{6,14},{7,15},{8,24},{9,... | collective-permute-start | bytes 393224 | tf_op jit(solution)/shard_map/ppermute | solution.py:364
  3.9 1.2 %collective-permute-start.3 = (bf16[2,4,64,128]{3,2,1,0:T(8,128)(2,1)S(1)}, bf16[2,4,64,128]{3,2,1,0:T(8,128)(2,1)S(1)}, u32[]{:S(2)}, u32[]{:S(2)}) collective-permute-start(bf16[2,4,64,128]{3,2,1,0:T(8,128)(2,1)S(1)} %get-tuple-element.50), channel_id=1, source_target_pairs={{0,8},{1,9},{2,10},{3,11},{4,20},{5,21},{6,22},{7,23},{8,0},{9,1},... | collective-permute-start | bytes 393224 | tf_op jit(solution)/shard_map/ppermute | solution.py:364
  5.2 0.0 collective-permute-start.6
  5.2 1.0 %slice_bitcast_fusion = (bf16[2,64,512]{2,1,0:T(8,128)(2,1)S(1)}, bf16[2,64,512]{2,1,0:T(8,128)(2,1)S(1)}) fusion(bf16[2,4,64,512]{3,2,1,0:T(8,128)(2,1)} %param.6), kind=kLoop, calls=%fused_computation.3 | loop fusion | bytes 524288 | tf_op jit(solution)/shard_map/squeeze | solution.py:377
  6.2 3.4 %collective-permute-start.8 = (bf16[2,64,512]{2,1,0:T(8,128)(2,1)S(1)}, bf16[2,64,512]{2,1,0:T(8,128)(2,1)S(1)}, u32[]{:S(2)}, u32[]{:S(2)}) collective-permute-start(bf16[2,64,512]{2,1,0:T(8,128)(2,1)S(1)} %get-tuple-element.48), channel_id=1, source_target_pairs={{0,1},{1,2},{2,3},{4,5},{5,6},{6,7},{8,9},{9,10},{10,11},{12,13},{... | collective-permute-start | bytes 393224 | tf_op jit(solution)/shard_map/ppermute | solution.py:364
  9.6 0.1 pad_add_fusion.refs_0_.meta
  9.7 1.3 %collective-permute-start.9 = (bf16[2,64,512]{2,1,0:T(8,128)(2,1)S(1)}, bf16[2,64,512]{2,1,0:T(8,128)(2,1)S(1)}, u32[]{:S(2)}, u32[]{:S(2)}) collective-permute-start(bf16[2,64,512]{2,1,0:T(8,128)(2,1)S(1)} %get-tuple-element.47), channel_id=1, source_target_pairs={{1,0},{2,1},{3,2},{5,4},{6,5},{7,6},{9,8},{10,9},{11,10},{13,12},{... | collective-permute-start | bytes 393224 | tf_op jit(solution)/shard_map/ppermute | solution.py:364
  11.0 0.0 copy-start
  11.0 1.5 %copy-done = bf16[27,64,512]{2,1,0:T(8,128)(2,1)S(1)} copy-done((bf16[27,64,512]{2,1,0:T(8,128)(2,1)S(1)}, bf16[27,64,512]{2,1,0:T(8,128)(2,1)}, u32[]{:S(2)}) %copy-start) | copy-done | bytes 1769496
  12.4 0.9 %merge_kernel_slices.1.refs_1_ = bf16[3,9,128,512]{3,2,1,0:T(8,128)(2,1)S(1)} custom-call(s32[3]{0:T(128)S(1)} %pad_add_fusion.refs_0_.meta, bf16[9,3,64,512]{3,2,1,0:T(8,128)(2,1)S(1)} %bitcast.17, bf16[9,3,64,512]{3,2,1,0:T(8,128)(2,1)S(1)} %collective-permute-done.1.refs_2_), custom_call_target="tpu_custom_call" | custom-call | tf_op jit(solution)/shard_map/merge_kernel_slices/pallas_call | solution.py:58
  13.3 0.0 collective-permute-done.refs_3_
  13.3 1.2 %collective-permute-start.2 = (bf16[2,4,64,128]{3,2,1,0:T(8,128)(2,1)S(1)}, bf16[2,4,64,128]{3,2,1,0:T(8,128)(2,1)S(1)}, u32[]{:S(2)}, u32[]{:S(2)}) collective-permute-start(bf16[2,4,64,128]{3,2,1,0:T(8,128)(2,1)S(1)} %get-tuple-element.51.refs_2_), channel_id=1, source_target_pairs={{0,4},{1,5},{2,6},{3,7},{4,0},{5,1},{6,2},{7,3},{8,12},{9,13},{10,... | collective-permute-start | bytes 393224 | tf_op jit(solution)/shard_map/ppermute | solution.py:364
  14.5 0.1 collective-permute-start.4
  14.6 0.0 collective-permute-done.6.refs_3_
  14.6 0.4 collective-permute-start.7
  15.0 0.1 collective-permute-start.5
  15.1 0.3 collective-permute-done.9.below
  15.4 0.6 split_halo_rows.1
  16.0 1.3 %collective-permute-start.10 = (bf16[2,2,64,128]{3,2,1,0:T(8,128)(2,1)S(1)}, bf16[2,2,64,128]{3,2,1,0:T(8,128)(2,1)S(1)}, u32[]{:S(2)}, u32[]{:S(2)}) collective-permute-start(bf16[2,2,64,128]{3,2,1,0:T(8,128)(2,1)S(1)} %get-tuple-element.28), channel_id=1, source_target_pairs={{0,8},{1,9},{2,10},{3,11},{4,20},{5,21},{6,22},{7,23},{8,0},{9,1},... | collective-permute-start | bytes 196616 | tf_op jit(solution)/shard_map/ppermute | solution.py:364
  17.3 1.2 %collective-permute-start.11 = (bf16[2,2,64,128]{3,2,1,0:T(8,128)(2,1)S(1)}, bf16[2,2,64,128]{3,2,1,0:T(8,128)(2,1)S(1)}, u32[]{:S(2)}, u32[]{:S(2)}) collective-permute-start(bf16[2,2,64,128]{3,2,1,0:T(8,128)(2,1)S(1)} %get-tuple-element.29), channel_id=1, source_target_pairs={{0,16},{1,17},{2,18},{3,19},{4,12},{5,13},{6,14},{7,15},{8,24},{9,... | collective-permute-start | bytes 196616 | tf_op jit(solution)/shard_map/ppermute | solution.py:364
  18.5 0.0 collective-permute-done.4.refs_5_
  18.5 0.2 collective-permute-start.12
  18.7 2.9 %conv_inner.2 = (bf16[256,512]{1,0:T(8,128)(2,1)S(1)}, bf16[256,512]{1,0:T(8,128)(2,1)S(1)}) custom-call(s32[3]{0:T(128)S(1)} %pad_add_fusion.refs_0_.meta, bf16[3,9,128,512]{3,2,1,0:T(8,128)(2,1)S(1)} %merge_kernel_slices.1.refs_1_, bf16[2,4,64,128]{3,2,1,0:T(8,128)(2,1)S(1)} %collective-permute-done.3.refs_2_, ...), custom_call_target="tpu_custom_call" | custom-call | flops 1811939328 | bytes 3538944 | tf_op jit(solution)/shard_map/conv_inner/pallas_call | solution.py:200
  21.6 0.0 collective-permute-done.10.refs_1_
  21.6 0.0 collective-permute-done.11.refs_2_
  21.6 1.3 %collective-permute-done.12.refs_3_ = bf16[2,2,64,128]{3,2,1,0:T(8,128)(2,1)S(1)} collective-permute-done((bf16[2,2,64,128]{3,2,1,0:T(8,128)(2,1)S(1)}, bf16[2,2,64,128]{3,2,1,0:T(8,128)(2,1)S(1)}, u32[]{:S(2)}, u32[]{:S(2)}) %collective-permute-start.12) | collective-permute-done | bytes 65568 | tf_op jit(solution)/shard_map/ppermute | solution.py:364
  22.9 3.7 %collective-permute-start.13 = (bf16[4,2,2,64,128]{4,3,2,1,0:T(8,128)(2,1)S(1)}, bf16[4,2,2,64,128]{4,3,2,1,0:T(8,128)(2,1)S(1)}, u32[]{:S(2)}, u32[]{:S(2)}) collective-permute-start(bf16[4,2,2,64,128]{4,3,2,1,0:T(8,128)(2,1)S(1)} %stack_halo_rows.1.refs_8_), channel_id=1, source_target_pairs={{0,4},{1,5},{2,6},{3,7},{4,0},{5,1},{6,2},{7,3},{8,12},{9,13},{10,... | collective-permute-start | bytes 786440 | tf_op jit(solution)/shard_map/ppermute | solution.py:364
  26.6 0.2 collective-permute-start.15
  26.8 1.2 %collective-permute-start.14 = (bf16[256,512]{1,0:T(8,128)(2,1)S(1)}, bf16[256,512]{1,0:T(8,128)(2,1)S(1)}, u32[]{:S(2)}, u32[]{:S(2)}) collective-permute-start(bf16[256,512]{1,0:T(8,128)(2,1)S(1)} %get-tuple-element.34), channel_id=1, source_target_pairs={{0,8},{1,9},{2,10},{3,11},{4,20},{5,21},{6,22},{7,23},{8,0},{9,1},... | collective-permute-start | bytes 786440 | tf_op jit(solution)/shard_map/ppermute | solution.py:364
  28.0 2.9 %conv_rim.2 = (bf16[256,512]{1,0:T(8,128)(2,1)S(1)}, bf16[256,512]{1,0:T(8,128)(2,1)S(1)}) custom-call(s32[3]{0:T(128)S(1)} %pad_add_fusion.refs_0_.meta, bf16[3,9,128,512]{3,2,1,0:T(8,128)(2,1)S(1)} %merge_kernel_slices.1.refs_1_, bf16[2,4,64,128]{3,2,1,0:T(8,128)(2,1)S(1)} %collective-permute-done.3.refs_2_, ...), custom_call_target="tpu_custom_call" | custom-call | flops 1811939328 | bytes 3538944 | tf_op jit(solution)/shard_map/conv_rim/pallas_call | solution.py:200
  30.9 0.3 collective-permute-start.17
  31.2 1.2 %collective-permute-start.19 = (bf16[256,512]{1,0:T(8,128)(2,1)S(1)}, bf16[256,512]{1,0:T(8,128)(2,1)S(1)}, u32[]{:S(2)}, u32[]{:S(2)}) collective-permute-start(bf16[256,512]{1,0:T(8,128)(2,1)S(1)} %get-tuple-element.39), channel_id=1, source_target_pairs={{0,8},{1,9},{2,10},{3,11},{4,20},{5,21},{6,22},{7,23},{8,0},{9,1},... | collective-permute-start | bytes 786440 | tf_op jit(solution)/shard_map/ppermute | solution.py:364
  32.4 2.8 %conv_inner.3 = (f32[256,512]{1,0:T(8,128)S(1)}, f32[256,512]{1,0:T(8,128)S(1)}) custom-call(s32[3]{0:T(128)S(1)} %pad_add_fusion.refs_0_.meta, bf16[3,9,128,512]{3,2,1,0:T(8,128)(2,1)S(1)} %merge_kernel_slices.1.refs_1_, bf16[2,4,64,128]{3,2,1,0:T(8,128)(2,1)S(1)} %get-tuple-element.51.refs_2_, bf16[2,4,64,128]{3,2,1,0:T(8,128)(2,1)S(1)} %collective-permute-done.refs_3_, ...), custom_call_target="tpu_custom_call" | custom-call | flops 1811939328 | bytes 3538944 | tf_op jit(solution)/shard_map/conv_inner/pallas_call | solution.py:200
  35.3 0.0 collective-permute-done.15.refs_1_
  35.4 0.3 collective-permute-start.16
  35.7 2.9 %conv_rim.3 = (f32[256,512]{1,0:T(8,128)S(1)}, f32[256,512]{1,0:T(8,128)S(1)}) custom-call(s32[3]{0:T(128)S(1)} %pad_add_fusion.refs_0_.meta, bf16[3,9,128,512]{3,2,1,0:T(8,128)(2,1)S(1)} %merge_kernel_slices.1.refs_1_, bf16[2,4,64,128]{3,2,1,0:T(8,128)(2,1)S(1)} %get-tuple-element.51.refs_2_, bf16[2,4,64,128]{3,2,1,0:T(8,128)(2,1)S(1)} %collective-permute-done.refs_3_, ...), custom_call_target="tpu_custom_call" | custom-call | flops 1811939328 | bytes 3538944 | tf_op jit(solution)/shard_map/conv_rim/pallas_call | solution.py:200
  38.5 0.0 copy-start.1
  38.6 0.0 copy-start.2
  38.6 0.0 copy-start.3
  38.6 0.0 copy-start.4
  38.6 0.1 sum_parts.5.refs_3_
  38.7 1.3 %collective-permute-start.20 = (bf16[256,512]{1,0:T(8,128)(2,1)S(1)}, bf16[256,512]{1,0:T(8,128)(2,1)S(1)}, u32[]{:S(2)}, u32[]{:S(2)}) collective-permute-start(bf16[256,512]{1,0:T(8,128)(2,1)S(1)} %sum_parts.5.refs_3_), channel_id=1, source_target_pairs={{0,16},{1,17},{2,18},{3,19},{4,12},{5,13},{6,14},{7,15},{8,24},{9,... | collective-permute-start | bytes 786440 | tf_op jit(solution)/shard_map/ppermute | solution.py:364
  40.0 0.0 collective-permute-done.14.refs_1_
  40.0 3.9 %collective-permute-done.16.refs_2_ = bf16[256,512]{1,0:T(8,128)(2,1)S(1)} collective-permute-done((bf16[256,512]{1,0:T(8,128)(2,1)S(1)}, bf16[256,512]{1,0:T(8,128)(2,1)S(1)}, u32[]{:S(2)}, u32[]{:S(2)}) %collective-permute-start.16) | collective-permute-done | bytes 262176 | tf_op jit(solution)/shard_map/ppermute | solution.py:364
  43.8 0.1 sum_parts.6
  43.9 4.0 %collective-permute-start.18 = (bf16[128,512]{1,0:T(8,128)(2,1)S(1)}, bf16[128,512]{1,0:T(8,128)(2,1)S(1)}, u32[]{:S(2)}, u32[]{:S(2)}) collective-permute-start(bf16[128,512]{1,0:T(8,128)(2,1)S(1)} %get-tuple-element.37), channel_id=1, source_target_pairs={{0,0},{1,1},{2,4},{3,5},{4,2},{5,3},{6,6},{7,7},{8,8},{9,9},{10,12... | collective-permute-start | bytes 393224 | tf_op jit(solution)/shard_map/ppermute | solution.py:364
  47.9 1.6 %collective-permute-start.22 = (bf16[128,512]{1,0:T(8,128)(2,1)S(1)}, bf16[128,512]{1,0:T(8,128)(2,1)S(1)}, u32[]{:S(2)}, u32[]{:S(2)}) collective-permute-start(bf16[128,512]{1,0:T(8,128)(2,1)S(1)} %get-tuple-element.41), channel_id=1, source_target_pairs={{0,1},{1,0},{2,5},{3,4},{4,3},{5,2},{6,7},{7,6},{8,9},{9,8},{10,13... | collective-permute-start | bytes 393224 | tf_op jit(solution)/shard_map/ppermute | solution.py:364
  49.6 0.0 collective-permute-done.19.refs_1_
  49.6 0.1 sum_parts.7
  49.7 2.1 %collective-permute-start.21 = (bf16[128,512]{1,0:T(8,128)(2,1)S(1)}, bf16[128,512]{1,0:T(8,128)(2,1)S(1)}, u32[]{:S(2)}, u32[]{:S(2)}) collective-permute-start(bf16[128,512]{1,0:T(8,128)(2,1)S(1)} %get-tuple-element.40), channel_id=1, source_target_pairs={{0,0},{1,1},{2,4},{3,5},{4,2},{5,3},{6,6},{7,7},{8,8},{9,9},{10,12... | collective-permute-start | bytes 393224 | tf_op jit(solution)/shard_map/ppermute | solution.py:364
  51.7 1.9 %collective-permute-start.23 = (bf16[128,512]{1,0:T(8,128)(2,1)S(1)}, bf16[128,512]{1,0:T(8,128)(2,1)S(1)}, u32[]{:S(2)}, u32[]{:S(2)}) collective-permute-start(bf16[128,512]{1,0:T(8,128)(2,1)S(1)} %get-tuple-element.42), channel_id=1, source_target_pairs={{0,1},{1,0},{2,5},{3,4},{4,3},{5,2},{6,7},{7,6},{8,9},{9,8},{10,13... | collective-permute-start | bytes 393224 | tf_op jit(solution)/shard_map/ppermute | solution.py:364
  53.6 1.4 %collective-permute-done.22.refs_2_ = bf16[128,512]{1,0:T(8,128)(2,1)S(1)} collective-permute-done((bf16[128,512]{1,0:T(8,128)(2,1)S(1)}, bf16[128,512]{1,0:T(8,128)(2,1)S(1)}, u32[]{:S(2)}, u32[]{:S(2)}) %collective-permute-start.22) | collective-permute-done | bytes 131104 | tf_op jit(solution)/shard_map/ppermute | solution.py:364
  55.0 4.5 %collective-permute-done.21.refs_1_ = bf16[128,512]{1,0:T(8,128)(2,1)S(1)} collective-permute-done((bf16[128,512]{1,0:T(8,128)(2,1)S(1)}, bf16[128,512]{1,0:T(8,128)(2,1)S(1)}, u32[]{:S(2)}, u32[]{:S(2)}) %collective-permute-start.21) | collective-permute-done | bytes 131104 | tf_op jit(solution)/shard_map/ppermute | solution.py:364
  59.5 0.5 collective-permute-start.27
  60.0 0.8 %collective-permute-done.25.refs_5_ = bf16[128,512]{1,0:T(8,128)(2,1)S(1)} collective-permute-done((bf16[128,512]{1,0:T(8,128)(2,1)S(1)}, bf16[128,512]{1,0:T(8,128)(2,1)S(1)}, u32[]{:S(2)}, u32[]{:S(2)}) %collective-permute-start.25) | collective-permute-done | bytes 131104 | tf_op jit(solution)/shard_map/ppermute | solution.py:364
  60.9 0.2 collective-permute-done.27.refs_7_
  61.1 4.4 %attend.1 = (bf16[4,64,512]{2,1,0:T(8,128)(2,1)S(1)}, bf16[4,64,512]{2,1,0:T(8,128)(2,1)S(1)}) custom-call(bf16[128,512]{1,0:T(8,128)(2,1)S(1)} %collective-permute-done.18.refs_0_, bf16[128,512]{1,0:T(8,128)(2,1)S(1)} %collective-permute-done.21.refs_1_, bf16[128,512]{1,0:T(8,128)(2,1)S(1)} %collective-permute-done.22.refs_2_, ...), custom_call_target="tpu_custom_call" | custom-call | flops 2684354560 | bytes 3145728 | tf_op jit(solution)/shard_map/attend/pallas_call | solution.py:335
  65.5 2.1 %collective-permute-start.28 = (bf16[4,64,512]{2,1,0:T(8,128)(2,1)S(1)}, bf16[4,64,512]{2,1,0:T(8,128)(2,1)S(1)}, u32[]{:S(2)}, u32[]{:S(2)}) collective-permute-start(bf16[4,64,512]{2,1,0:T(8,128)(2,1)S(1)} %get-tuple-element.43), channel_id=1, source_target_pairs={{1,0},{0,1},{5,2},{4,3},{3,4},{2,5},{7,6},{6,7},{9,8},{8,9},{13,10... | collective-permute-start | bytes 786440 | tf_op jit(solution)/shard_map/ppermute | solution.py:458
  67.7 2.8 %collective-permute-start.29 = (bf16[4,64,512]{2,1,0:T(8,128)(2,1)S(1)}, bf16[4,64,512]{2,1,0:T(8,128)(2,1)S(1)}, u32[]{:S(2)}, u32[]{:S(2)}) collective-permute-start(bf16[4,64,512]{2,1,0:T(8,128)(2,1)S(1)} %get-tuple-element.44), channel_id=1, source_target_pairs={{0,0},{1,1},{4,2},{5,3},{2,4},{3,5},{6,6},{7,7},{8,8},{9,9},{12,10... | collective-permute-start | bytes 786440 | tf_op jit(solution)/shard_map/ppermute | solution.py:458
  70.5 5.0 %collective-permute-done.28 = bf16[4,64,512]{2,1,0:T(8,128)(2,1)S(1)} collective-permute-done((bf16[4,64,512]{2,1,0:T(8,128)(2,1)S(1)}, bf16[4,64,512]{2,1,0:T(8,128)(2,1)S(1)}, u32[]{:S(2)}, u32[]{:S(2)}) %collective-permute-start.28) | collective-permute-done | bytes 262176 | tf_op jit(solution)/shard_map/ppermute | solution.py:458
  75.5 5.6 %collective-permute-done.29 = bf16[4,64,512]{2,1,0:T(8,128)(2,1)S(1)} collective-permute-done((bf16[4,64,512]{2,1,0:T(8,128)(2,1)S(1)}, bf16[4,64,512]{2,1,0:T(8,128)(2,1)S(1)}, u32[]{:S(2)}, u32[]{:S(2)}) %collective-permute-start.29) | collective-permute-done | bytes 262176 | tf_op jit(solution)/shard_map/ppermute | solution.py:458
  81.1 0.8 %pad_maximum_fusion = bf16[2,4,64,512]{3,2,1,0:T(8,128)(2,1)} fusion(bf16[1,4,64,512]{3,2,1,0:T(8,128)(2,1)S(1)} %get-tuple-element.46, bf16[1,4,64,512]{3,2,1,0:T(8,128)(2,1)S(1)} %get-tuple-element.45), kind=kLoop, calls=%fused_computation | loop fusion | flops 262144 | bytes 1048576 | tf_op jit(solution)/shard_map/stack | solution.py:459
  (23 shorter events, 0.2 us)
Async XLA Ops:
  0.0 9.7 %collective-permute-start.1 = (bf16[9,3,64,512]{3,2,1,0:T(8,128)(2,1)}, bf16[9,3,64,512]{3,2,1,0:T(8,128)(2,1)S(1)}, u32[]{:S(2)}, u32[]{:S(2)}) collective-permute-start(bf16[9,3,64,512]{3,2,1,0:T(8,128)(2,1)} %bitcast.16), channel_id=1, source_target_pairs={{0,4},{1,5},{2,6},{3,7},{4,0},{5,1},{6,2},{7,3},{8,12},{9,13},{10,... | collective-permute-start | bytes 5308424 | tf_op jit(solution)/shard_map/ppermute | solution.py:364
  1.2 12.1 %collective-permute-start = (bf16[2,4,64,128]{3,2,1,0:T(8,128)(2,1)S(1)}, bf16[2,4,64,128]{3,2,1,0:T(8,128)(2,1)S(1)}, u32[]{:S(2)}, u32[]{:S(2)}) collective-permute-start(bf16[2,4,64,128]{3,2,1,0:T(8,128)(2,1)S(1)} %get-tuple-element.52), channel_id=1, source_target_pairs={{0,16},{1,17},{2,18},{3,19},{4,12},{5,13},{6,14},{7,15},{8,24},{9,... | collective-permute-start | bytes 393224 | tf_op jit(solution)/shard_map/ppermute | solution.py:364
  3.9 10.6 %collective-permute-start.3 = (bf16[2,4,64,128]{3,2,1,0:T(8,128)(2,1)S(1)}, bf16[2,4,64,128]{3,2,1,0:T(8,128)(2,1)S(1)}, u32[]{:S(2)}, u32[]{:S(2)}) collective-permute-start(bf16[2,4,64,128]{3,2,1,0:T(8,128)(2,1)S(1)} %get-tuple-element.50), channel_id=1, source_target_pairs={{0,8},{1,9},{2,10},{3,11},{4,20},{5,21},{6,22},{7,23},{8,0},{9,1},... | collective-permute-start | bytes 393224 | tf_op jit(solution)/shard_map/ppermute | solution.py:364
  5.2 9.4 %collective-permute-start.6 = (bf16[2,4,64,128]{3,2,1,0:T(8,128)(2,1)S(1)}, bf16[2,4,64,128]{3,2,1,0:T(8,128)(2,1)S(1)}, u32[]{:S(2)}, u32[]{:S(2)}) collective-permute-start(bf16[2,4,64,128]{3,2,1,0:T(8,128)(2,1)S(1)} %get-tuple-element.49), channel_id=1, source_target_pairs={{0,24},{1,25},{2,26},{3,27},{4,28},{5,29},{6,30},{7,31},{8,16},{9,... | collective-permute-start | bytes 393224 | tf_op jit(solution)/shard_map/ppermute | solution.py:364
  6.2 8.8 %collective-permute-start.8 = (bf16[2,64,512]{2,1,0:T(8,128)(2,1)S(1)}, bf16[2,64,512]{2,1,0:T(8,128)(2,1)S(1)}, u32[]{:S(2)}, u32[]{:S(2)}) collective-permute-start(bf16[2,64,512]{2,1,0:T(8,128)(2,1)S(1)} %get-tuple-element.48), channel_id=1, source_target_pairs={{0,1},{1,2},{2,3},{4,5},{5,6},{6,7},{8,9},{9,10},{10,11},{12,13},{... | collective-permute-start | bytes 393224 | tf_op jit(solution)/shard_map/ppermute | solution.py:364
  9.7 5.7 %collective-permute-start.9 = (bf16[2,64,512]{2,1,0:T(8,128)(2,1)S(1)}, bf16[2,64,512]{2,1,0:T(8,128)(2,1)S(1)}, u32[]{:S(2)}, u32[]{:S(2)}) collective-permute-start(bf16[2,64,512]{2,1,0:T(8,128)(2,1)S(1)} %get-tuple-element.47), channel_id=1, source_target_pairs={{1,0},{2,1},{3,2},{5,4},{6,5},{7,6},{9,8},{10,9},{11,10},{13,12},{... | collective-permute-start | bytes 393224 | tf_op jit(solution)/shard_map/ppermute | solution.py:364
  11.0 1.5 %copy-start = (bf16[27,64,512]{2,1,0:T(8,128)(2,1)S(1)}, bf16[27,64,512]{2,1,0:T(8,128)(2,1)}, u32[]{:S(2)}) copy-start(bf16[27,64,512]{2,1,0:T(8,128)(2,1)} %param.7) | copy-start | bytes 5308420
  13.3 4.0 %collective-permute-start.2 = (bf16[2,4,64,128]{3,2,1,0:T(8,128)(2,1)S(1)}, bf16[2,4,64,128]{3,2,1,0:T(8,128)(2,1)S(1)}, u32[]{:S(2)}, u32[]{:S(2)}) collective-permute-start(bf16[2,4,64,128]{3,2,1,0:T(8,128)(2,1)S(1)} %get-tuple-element.51.refs_2_), channel_id=1, source_target_pairs={{0,4},{1,5},{2,6},{3,7},{4,0},{5,1},{6,2},{7,3},{8,12},{9,13},{10,... | collective-permute-start | bytes 393224 | tf_op jit(solution)/shard_map/ppermute | solution.py:364
  14.5 4.0 %collective-permute-start.4 = (bf16[2,4,64,128]{3,2,1,0:T(8,128)(2,1)S(1)}, bf16[2,4,64,128]{3,2,1,0:T(8,128)(2,1)S(1)}, u32[]{:S(2)}, u32[]{:S(2)}) collective-permute-start(bf16[2,4,64,128]{3,2,1,0:T(8,128)(2,1)S(1)} %collective-permute-done.3.refs_2_), channel_id=1, source_target_pairs={{0,4},{1,5},{2,6},{3,7},{4,0},{5,1},{6,2},{7,3},{8,12},{9,13},{10,... | collective-permute-start | bytes 393224 | tf_op jit(solution)/shard_map/ppermute | solution.py:364
  14.6 4.1 %collective-permute-start.7 = (bf16[2,4,64,128]{3,2,1,0:T(8,128)(2,1)S(1)}, bf16[2,4,64,128]{3,2,1,0:T(8,128)(2,1)S(1)}, u32[]{:S(2)}, u32[]{:S(2)}) collective-permute-start(bf16[2,4,64,128]{3,2,1,0:T(8,128)(2,1)S(1)} %collective-permute-done.6.refs_3_), channel_id=1, source_target_pairs={{0,4},{1,5},{2,6},{3,7},{4,0},{5,1},{6,2},{7,3},{8,12},{9,13},{10,... | collective-permute-start | bytes 393224 | tf_op jit(solution)/shard_map/ppermute | solution.py:364
  15.0 3.7 %collective-permute-start.5 = (bf16[2,4,64,128]{3,2,1,0:T(8,128)(2,1)S(1)}, bf16[2,4,64,128]{3,2,1,0:T(8,128)(2,1)S(1)}, u32[]{:S(2)}, u32[]{:S(2)}) collective-permute-start(bf16[2,4,64,128]{3,2,1,0:T(8,128)(2,1)S(1)} %collective-permute-done.refs_3_), channel_id=1, source_target_pairs={{0,4},{1,5},{2,6},{3,7},{4,0},{5,1},{6,2},{7,3},{8,12},{9,13},{10,... | collective-permute-start | bytes 393224 | tf_op jit(solution)/shard_map/ppermute | solution.py:364
  16.0 5.6 %collective-permute-start.10 = (bf16[2,2,64,128]{3,2,1,0:T(8,128)(2,1)S(1)}, bf16[2,2,64,128]{3,2,1,0:T(8,128)(2,1)S(1)}, u32[]{:S(2)}, u32[]{:S(2)}) collective-permute-start(bf16[2,2,64,128]{3,2,1,0:T(8,128)(2,1)S(1)} %get-tuple-element.28), channel_id=1, source_target_pairs={{0,8},{1,9},{2,10},{3,11},{4,20},{5,21},{6,22},{7,23},{8,0},{9,1},... | collective-permute-start | bytes 196616 | tf_op jit(solution)/shard_map/ppermute | solution.py:364
  17.3 4.3 %collective-permute-start.11 = (bf16[2,2,64,128]{3,2,1,0:T(8,128)(2,1)S(1)}, bf16[2,2,64,128]{3,2,1,0:T(8,128)(2,1)S(1)}, u32[]{:S(2)}, u32[]{:S(2)}) collective-permute-start(bf16[2,2,64,128]{3,2,1,0:T(8,128)(2,1)S(1)} %get-tuple-element.29), channel_id=1, source_target_pairs={{0,16},{1,17},{2,18},{3,19},{4,12},{5,13},{6,14},{7,15},{8,24},{9,... | collective-permute-start | bytes 196616 | tf_op jit(solution)/shard_map/ppermute | solution.py:364
  18.5 4.4 %collective-permute-start.12 = (bf16[2,2,64,128]{3,2,1,0:T(8,128)(2,1)S(1)}, bf16[2,2,64,128]{3,2,1,0:T(8,128)(2,1)S(1)}, u32[]{:S(2)}, u32[]{:S(2)}) collective-permute-start(bf16[2,2,64,128]{3,2,1,0:T(8,128)(2,1)S(1)} %get-tuple-element.30), channel_id=1, source_target_pairs={{0,24},{1,25},{2,26},{3,27},{4,28},{5,29},{6,30},{7,31},{8,16},{9,... | collective-permute-start | bytes 196616 | tf_op jit(solution)/shard_map/ppermute | solution.py:364
  22.9 5.2 %collective-permute-start.13 = (bf16[4,2,2,64,128]{4,3,2,1,0:T(8,128)(2,1)S(1)}, bf16[4,2,2,64,128]{4,3,2,1,0:T(8,128)(2,1)S(1)}, u32[]{:S(2)}, u32[]{:S(2)}) collective-permute-start(bf16[4,2,2,64,128]{4,3,2,1,0:T(8,128)(2,1)S(1)} %stack_halo_rows.1.refs_8_), channel_id=1, source_target_pairs={{0,4},{1,5},{2,6},{3,7},{4,0},{5,1},{6,2},{7,3},{8,12},{9,13},{10,... | collective-permute-start | bytes 786440 | tf_op jit(solution)/shard_map/ppermute | solution.py:364
  26.6 8.7 %collective-permute-start.15 = (bf16[256,512]{1,0:T(8,128)(2,1)S(1)}, bf16[256,512]{1,0:T(8,128)(2,1)S(1)}, u32[]{:S(2)}, u32[]{:S(2)}) collective-permute-start(bf16[256,512]{1,0:T(8,128)(2,1)S(1)} %get-tuple-element.31.refs_4_), channel_id=1, source_target_pairs={{0,8},{1,9},{2,10},{3,11},{4,20},{5,21},{6,22},{7,23},{8,0},{9,1},... | collective-permute-start | bytes 786440 | tf_op jit(solution)/shard_map/ppermute | solution.py:364
  26.8 13.2 %collective-permute-start.14 = (bf16[256,512]{1,0:T(8,128)(2,1)S(1)}, bf16[256,512]{1,0:T(8,128)(2,1)S(1)}, u32[]{:S(2)}, u32[]{:S(2)}) collective-permute-start(bf16[256,512]{1,0:T(8,128)(2,1)S(1)} %get-tuple-element.34), channel_id=1, source_target_pairs={{0,8},{1,9},{2,10},{3,11},{4,20},{5,21},{6,22},{7,23},{8,0},{9,1},... | collective-permute-start | bytes 786440 | tf_op jit(solution)/shard_map/ppermute | solution.py:364
  30.9 7.7 %collective-permute-start.17 = (bf16[256,512]{1,0:T(8,128)(2,1)S(1)}, bf16[256,512]{1,0:T(8,128)(2,1)S(1)}, u32[]{:S(2)}, u32[]{:S(2)}) collective-permute-start(bf16[256,512]{1,0:T(8,128)(2,1)S(1)} %get-tuple-element.32.refs_8_), channel_id=1, source_target_pairs={{0,8},{1,9},{2,10},{3,11},{4,20},{5,21},{6,22},{7,23},{8,0},{9,1},... | collective-permute-start | bytes 786440 | tf_op jit(solution)/shard_map/ppermute | solution.py:364
  31.2 18.4 %collective-permute-start.19 = (bf16[256,512]{1,0:T(8,128)(2,1)S(1)}, bf16[256,512]{1,0:T(8,128)(2,1)S(1)}, u32[]{:S(2)}, u32[]{:S(2)}) collective-permute-start(bf16[256,512]{1,0:T(8,128)(2,1)S(1)} %get-tuple-element.39), channel_id=1, source_target_pairs={{0,8},{1,9},{2,10},{3,11},{4,20},{5,21},{6,22},{7,23},{8,0},{9,1},... | collective-permute-start | bytes 786440 | tf_op jit(solution)/shard_map/ppermute | solution.py:364
  35.4 8.5 %collective-permute-start.16 = (bf16[256,512]{1,0:T(8,128)(2,1)S(1)}, bf16[256,512]{1,0:T(8,128)(2,1)S(1)}, u32[]{:S(2)}, u32[]{:S(2)}) collective-permute-start(bf16[256,512]{1,0:T(8,128)(2,1)S(1)} %sum_parts.4.refs_10_), channel_id=1, source_target_pairs={{0,16},{1,17},{2,18},{3,19},{4,12},{5,13},{6,14},{7,15},{8,24},{9,... | collective-permute-start | bytes 786440 | tf_op jit(solution)/shard_map/ppermute | solution.py:364
  38.5 22.5 %copy-start.1 = (bf16[512,512]{1,0:T(8,128)(2,1)S(1)}, bf16[512,512]{1,0:T(8,128)(2,1)}, u32[]{:S(2)}) copy-start(bf16[512,512]{1,0:T(8,128)(2,1)} %refs_8_.1) | copy-start | bytes 1572868
  38.6 22.5 %copy-start.2 = (bf16[512,512]{1,0:T(8,128)(2,1)S(1)}, bf16[512,512]{1,0:T(8,128)(2,1)}, u32[]{:S(2)}) copy-start(bf16[512,512]{1,0:T(8,128)(2,1)} %refs_9_.1) | copy-start | bytes 1572868
  38.6 22.5 %copy-start.3 = (bf16[512,512]{1,0:T(8,128)(2,1)S(1)}, bf16[512,512]{1,0:T(8,128)(2,1)}, u32[]{:S(2)}) copy-start(bf16[512,512]{1,0:T(8,128)(2,1)} %refs_10_.1) | copy-start | bytes 1572868
  38.6 22.5 %copy-start.4 = (bf16[512,512]{1,0:T(8,128)(2,1)S(1)}, bf16[512,512]{1,0:T(8,128)(2,1)}, u32[]{:S(2)}) copy-start(bf16[512,512]{1,0:T(8,128)(2,1)} %refs_11_.1) | copy-start | bytes 1572868
  38.7 10.9 %collective-permute-start.20 = (bf16[256,512]{1,0:T(8,128)(2,1)S(1)}, bf16[256,512]{1,0:T(8,128)(2,1)S(1)}, u32[]{:S(2)}, u32[]{:S(2)}) collective-permute-start(bf16[256,512]{1,0:T(8,128)(2,1)S(1)} %sum_parts.5.refs_3_), channel_id=1, source_target_pairs={{0,16},{1,17},{2,18},{3,19},{4,12},{5,13},{6,14},{7,15},{8,24},{9,... | collective-permute-start | bytes 786440 | tf_op jit(solution)/shard_map/ppermute | solution.py:364
  43.9 9.7 %collective-permute-start.18 = (bf16[128,512]{1,0:T(8,128)(2,1)S(1)}, bf16[128,512]{1,0:T(8,128)(2,1)S(1)}, u32[]{:S(2)}, u32[]{:S(2)}) collective-permute-start(bf16[128,512]{1,0:T(8,128)(2,1)S(1)} %get-tuple-element.37), channel_id=1, source_target_pairs={{0,0},{1,1},{2,4},{3,5},{4,2},{5,3},{6,6},{7,7},{8,8},{9,9},{10,12... | collective-permute-start | bytes 393224 | tf_op jit(solution)/shard_map/ppermute | solution.py:364
  47.9 7.1 %collective-permute-start.22 = (bf16[128,512]{1,0:T(8,128)(2,1)S(1)}, bf16[128,512]{1,0:T(8,128)(2,1)S(1)}, u32[]{:S(2)}, u32[]{:S(2)}) collective-permute-start(bf16[128,512]{1,0:T(8,128)(2,1)S(1)} %get-tuple-element.41), channel_id=1, source_target_pairs={{0,1},{1,0},{2,5},{3,4},{4,3},{5,2},{6,7},{7,6},{8,9},{9,8},{10,13... | collective-permute-start | bytes 393224 | tf_op jit(solution)/shard_map/ppermute | solution.py:364
  49.7 9.9 %collective-permute-start.21 = (bf16[128,512]{1,0:T(8,128)(2,1)S(1)}, bf16[128,512]{1,0:T(8,128)(2,1)S(1)}, u32[]{:S(2)}, u32[]{:S(2)}) collective-permute-start(bf16[128,512]{1,0:T(8,128)(2,1)S(1)} %get-tuple-element.40), channel_id=1, source_target_pairs={{0,0},{1,1},{2,4},{3,5},{4,2},{5,3},{6,6},{7,7},{8,8},{9,9},{10,12... | collective-permute-start | bytes 393224 | tf_op jit(solution)/shard_map/ppermute | solution.py:364
  51.7 7.8 %collective-permute-start.23 = (bf16[128,512]{1,0:T(8,128)(2,1)S(1)}, bf16[128,512]{1,0:T(8,128)(2,1)S(1)}, u32[]{:S(2)}, u32[]{:S(2)}) collective-permute-start(bf16[128,512]{1,0:T(8,128)(2,1)S(1)} %get-tuple-element.42), channel_id=1, source_target_pairs={{0,1},{1,0},{2,5},{3,4},{4,3},{5,2},{6,7},{7,6},{8,9},{9,8},{10,13... | collective-permute-start | bytes 393224 | tf_op jit(solution)/shard_map/ppermute | solution.py:364
  53.6 6.4 %collective-permute-start.24 = (bf16[128,512]{1,0:T(8,128)(2,1)S(1)}, bf16[128,512]{1,0:T(8,128)(2,1)S(1)}, u32[]{:S(2)}, u32[]{:S(2)}) collective-permute-start(bf16[128,512]{1,0:T(8,128)(2,1)S(1)} %collective-permute-done.18.refs_0_), channel_id=1, source_target_pairs={{0,4},{1,5},{2,6},{3,7},{4,0},{5,1},{6,2},{7,3},{8,12},{9,13},{10,... | collective-permute-start | bytes 393224 | tf_op jit(solution)/shard_map/ppermute | solution.py:364
  55.0 5.0 %collective-permute-start.26 = (bf16[128,512]{1,0:T(8,128)(2,1)S(1)}, bf16[128,512]{1,0:T(8,128)(2,1)S(1)}, u32[]{:S(2)}, u32[]{:S(2)}) collective-permute-start(bf16[128,512]{1,0:T(8,128)(2,1)S(1)} %collective-permute-done.22.refs_2_), channel_id=1, source_target_pairs={{0,4},{1,5},{2,6},{3,7},{4,0},{5,1},{6,2},{7,3},{8,12},{9,13},{10,... | collective-permute-start | bytes 393224 | tf_op jit(solution)/shard_map/ppermute | solution.py:364
  59.5 1.3 %collective-permute-start.25 = (bf16[128,512]{1,0:T(8,128)(2,1)S(1)}, bf16[128,512]{1,0:T(8,128)(2,1)S(1)}, u32[]{:S(2)}, u32[]{:S(2)}) collective-permute-start(bf16[128,512]{1,0:T(8,128)(2,1)S(1)} %collective-permute-done.21.refs_1_), channel_id=1, source_target_pairs={{0,4},{1,5},{2,6},{3,7},{4,0},{5,1},{6,2},{7,3},{8,12},{9,13},{10,... | collective-permute-start | bytes 393224 | tf_op jit(solution)/shard_map/ppermute | solution.py:364
  59.5 1.5 %collective-permute-start.27 = (bf16[128,512]{1,0:T(8,128)(2,1)S(1)}, bf16[128,512]{1,0:T(8,128)(2,1)S(1)}, u32[]{:S(2)}, u32[]{:S(2)}) collective-permute-start(bf16[128,512]{1,0:T(8,128)(2,1)S(1)} %collective-permute-done.23.refs_3_), channel_id=1, source_target_pairs={{0,4},{1,5},{2,6},{3,7},{4,0},{5,1},{6,2},{7,3},{8,12},{9,13},{10,... | collective-permute-start | bytes 393224 | tf_op jit(solution)/shard_map/ppermute | solution.py:364
  65.5 9.9 %collective-permute-start.28 = (bf16[4,64,512]{2,1,0:T(8,128)(2,1)S(1)}, bf16[4,64,512]{2,1,0:T(8,128)(2,1)S(1)}, u32[]{:S(2)}, u32[]{:S(2)}) collective-permute-start(bf16[4,64,512]{2,1,0:T(8,128)(2,1)S(1)} %get-tuple-element.43), channel_id=1, source_target_pairs={{1,0},{0,1},{5,2},{4,3},{3,4},{2,5},{7,6},{6,7},{9,8},{8,9},{13,10... | collective-permute-start | bytes 786440 | tf_op jit(solution)/shard_map/ppermute | solution.py:458
  67.7 13.4 %collective-permute-start.29 = (bf16[4,64,512]{2,1,0:T(8,128)(2,1)S(1)}, bf16[4,64,512]{2,1,0:T(8,128)(2,1)S(1)}, u32[]{:S(2)}, u32[]{:S(2)}) collective-permute-start(bf16[4,64,512]{2,1,0:T(8,128)(2,1)S(1)} %get-tuple-element.44), channel_id=1, source_target_pairs={{0,0},{1,1},{4,2},{5,3},{2,4},{3,5},{6,6},{7,7},{8,8},{9,9},{12,10... | collective-permute-start | bytes 786440 | tf_op jit(solution)/shard_map/ppermute | solution.py:458
